TPU v7x, 32 devices: a whole 2x2x4 slice. The times are simulated.
32 devices in a mesh: ctx: 16 (over z, y, core), tp: 2 (over x).
Axes of the slice: x: 2, y: 2, z: 4, core: 2. Of those that a mesh axis runs over, the one named last changes fastest.
Arguments:
- hidden_in: bfloat16 [2, 3072, 5120], P(None, 'ctx', 'tp'), may hold values from -24 to 24
- w_q: bfloat16 [5120, 3072], P(None, 'tp'), may hold values from -0.078125 to 0.078125
- w_k: bfloat16 [5120, 3072], P(None, 'tp'), may hold values from -0.078125 to 0.078125
- w_v: bfloat16 [5120, 3072], P(None, 'tp'), may hold values from -0.078125 to 0.078125
- event_pos: int32 [2, 3072], P(None, 'ctx'), may hold values from 0 to 3071, as said below
Outputs:
- attention_out: bfloat16 [2, 3072, 3072], P(None, 'ctx', 'tp')
Inputs may be any that keep to these rules, and one draw needn't show every extreme that they name: `event_pos`: for each sequence the rows d * 2 * 96 to d * 2 * 96 + 2 * 96 - 1 hold span c_d in order and then span 3072 / 96 - 1 - c_d in order, where span c covers positions c * 96 to c * 96 + 95 and c_d runs over a permutation, drawn for each sequence, of the first 16 spans; every position occurs once.
All inputs are finite; a program needn't handle non-finite values.
Results may differ from a plain program's by a relative error of at most 0.0075.
The roundings to bfloat16 on the way count: a program that leaves them out, or rounds other values in their place, can miss the bound.
Values may be sent and summed in bfloat16 or wider, within the bound.
No kernel may reach another device: no remote copies, remote signals or barrier semaphores. Data moves between devices by JAX's collectives and lax.ppermute only.
A program may use at most 192 MiB of HBM per device.

v0:
```python
import math

import jax
import jax.numpy as jnp
from jax import lax
from jax.sharding import PartitionSpec as P

HD = 128


def on_device(hidden_in, w_q, w_k, w_v, event_pos):
    sequences = hidden_in.shape[0]
    block_rows = hidden_in.shape[1]
    features = w_q.shape[1]
    heads_here = features // HD
    row_total = sequences * block_rows
    empty = jnp.zeros((row_total, features), jnp.float32)
    totals = (empty, empty, empty)
    shard_piece = lax.all_gather(hidden_in, "tp", axis=2, tiled=True)
    width_here = shard_piece.shape[2]
    flat_rows = shard_piece.reshape(row_total, width_here)
    results = []
    for running, matrix in zip(totals, (w_q, w_k, w_v)):
        results.append(jnp.dot(flat_rows, matrix, preferred_element_type=jnp.float32))
    query_sum, key_sum, value_sum = tuple(results)
    queries = query_sum.astype(jnp.bfloat16).reshape(sequences, block_rows, features)
    keys = key_sum.astype(jnp.bfloat16).reshape(sequences, block_rows, features)
    values = value_sum.astype(jnp.bfloat16).reshape(sequences, block_rows, features)
    query_heads = queries.reshape(sequences, block_rows, heads_here, HD)
    score_scale = 1.0 / math.sqrt(HD)

    def update(state_now, shard_piece):
        run_max, run_sum, run_out = state_now
        key_part, value_part, pos_part = shard_piece
        key_count = key_part.shape[1]
        key_heads = key_part.reshape(sequences, key_count, heads_here, HD)
        value_heads = value_part.reshape(sequences, key_count, heads_here, HD)
        scores = (
            jnp.einsum(
                "sqhd,skhd->shqk", query_heads, key_heads, preferred_element_type=jnp.float32
            )
            * score_scale
        )
        visible = pos_part[:, None, None, :] <= event_pos[:, None, :, None]
        scores = jnp.where(visible, scores, -jnp.inf)
        new_max = jnp.maximum(run_max, jnp.max(scores, axis=3))
        shrink = jnp.exp(run_max - new_max)
        weights = jnp.exp(scores - new_max[..., None])
        new_sum = run_sum * shrink + jnp.sum(weights, axis=3)
        added = jnp.einsum(
            "shqk,skhd->shqd",
            weights.astype(jnp.bfloat16),
            value_heads,
            preferred_element_type=jnp.float32,
        )
        new_out = run_out * shrink[..., None] + added
        return (new_max, new_sum, new_out)

    initial = (
        jnp.full((sequences, heads_here, block_rows), -1e30, jnp.float32),
        jnp.zeros((sequences, heads_here, block_rows), jnp.float32),
        jnp.zeros((sequences, heads_here, block_rows, HD), jnp.float32),
    )
    everything = (
        lax.all_gather(keys, "ctx", axis=1, tiled=True),
        lax.all_gather(values, "ctx", axis=1, tiled=True),
        lax.all_gather(event_pos, "ctx", axis=1, tiled=True),
    )
    length = everything[0].shape[1]
    block_len = math.gcd(length, 512)

    def scan_step(state_now, block_index):
        offset = block_index * block_len
        shard_piece = tuple(
            (lax.dynamic_slice_in_dim(member, offset, block_len, 1) for member in everything)
        )
        return (update(state_now, shard_piece), None)

    final_state, leftover = lax.scan(
        scan_step, initial, jnp.arange(length // block_len, dtype=jnp.int32)
    )
    run_max, run_sum, run_out = final_state
    normed = run_out / run_sum[..., None]
    return (
        normed.transpose(0, 2, 1, 3).reshape(sequences, block_rows, features).astype(jnp.bfloat16)
    )


def solution(mesh):
    placed = (P(None, "ctx", "tp"), P(None, "tp"), P(None, "tp"), P(None, "tp"), P(None, "ctx"))
    return jax.shard_map(
        on_device, mesh=mesh, in_specs=placed, out_specs=P(None, "ctx", "tp"), check_vma=False
    )
```

profile of v0, /device:TPU:0, one launch (start us, length us, event | category | flops | bytes accessed | tf_op | source)
XLA Modules:
  0.0 513.4 jit_solution(10421865413234225308)
XLA Ops:
  7.3 58.1 %all-gather.5.cloned.1.call-done = bf16[2,192,5120]{2,1,0:T(8,128)(2,1)} async-done(((bf16[2,192,2560]{2,1,0:T(8,128)(2,1)}), bf16[2,192,5120]{2,1,0:T(8,128)(2,1)}) %all-gather.5.cloned.1.call-update) | async-done | bytes 3932176 | tf_op jit(solution)/shard_map/all_gather | solution.py:19
  65.4 10.8 %convolution_convert_fusion = bf16[384,1536]{1,0:T(8,128)(2,1)S(1)} fusion(bf16[384,5120]{1,0:T(8,128)(2,1)} %bitcast.62, bf16[5120,1536]{1,0:T(8,128)(2,1)} %param.10), kind=kOutput, calls=%fused_computation.22 | convolution fusion | flops 6040387584 | bytes 20840448 | tf_op jit(solution)/shard_map/dot_general | solution.py:24
  76.2 2.2 copy.28
  78.5 10.9 %convolution_convert_fusion.2 = bf16[384,1536]{1,0:T(8,128)(2,1)S(1)} fusion(bf16[384,5120]{1,0:T(8,128)(2,1)} %bitcast.63, bf16[5120,1536]{1,0:T(8,128)(2,1)} %param.9), kind=kOutput, calls=%fused_computation.24 | convolution fusion | flops 6040387584 | bytes 20840448 | tf_op jit(solution)/shard_map/dot_general | solution.py:24
  89.4 2.2 copy.27
  91.7 21.8 %all-gather = s32[16,192,2]{1,2,0:T(2,128)S(1)} all-gather(s32[1,192,2]{1,2,0:T(2,128)S(1)} %bitcast.61), channel_id=1, replica_groups=mesh['ctx'=16,'tp'=2] {'ctx'}, dimensions={0}, use_global_device_ids=true | all-gather | bytes 26112 | tf_op jit(solution)/shard_map/all_gather | solution.py:67
  113.6 11.0 %convolution_convert_fusion.1 = bf16[384,1536]{1,0:T(8,128)(2,1)S(1)} fusion(bf16[384,5120]{1,0:T(8,128)(2,1)} %bitcast.64, bf16[5120,1536]{1,0:T(8,128)(2,1)} %param.8), kind=kOutput, calls=%fused_computation.23 | convolution fusion | flops 6040387584 | bytes 20840448 | tf_op jit(solution)/shard_map/dot_general | solution.py:24
  126.9 50.8 %all-gather.9.cloned.1.call-done = bf16[2,3072,1536]{2,0,1:T(2,128)(2,1)} async-done(((bf16[2,192,1536]{2,0,1:T(2,128)(2,1)}), bf16[2,3072,1536]{2,0,1:T(2,128)(2,1)}) %all-gather.9.cloned.1.call-update) | async-done | bytes 18874384 | tf_op jit(solution)/shard_map/all_gather | solution.py:66
  177.7 100.8 %all-gather.7.cloned.1.call-done = bf16[2,3072,1536]{2,0,1:T(2,128)(2,1)} async-done(((bf16[2,192,1536]{2,0,1:T(2,128)(2,1)}), bf16[2,3072,1536]{2,0,1:T(2,128)(2,1)}) %all-gather.7.cloned.1.call-update) | async-done | bytes 18874384 | tf_op jit(solution)/shard_map/all_gather | solution.py:65
  278.5 225.5 %while.15 = (s32[]{:T(128)}, f32[2,12,192]{2,1,0:T(8,128)S(1)}, f32[2,12,192]{2,1,0:T(8,128)S(1)}, f32[2,12,192,128]{3,2,1,0:T(8,128)}, s32[6]{0:T(128)S(1)}, /*...) while((s32[]{:T(128)}, f32[2,12,192]{2,1,0:T(8,128)S(1)}, ...), condition=%wide.region_3.4_spmd.clone, body=%wide.region_0.3_spmd.clone.sunk | while | flops 1235900928 | bytes 98219824 | solution.py:79
  279.9 9.8 %constant_dynamic-slice_fusion.6 = (bf16[2,512,1536]{2,0,1:T(2,128)(2,1)}, bf16[2,512,1536]{2,0,1:T(2,128)(2,1)}) fusion(bf16[2,3072,1536]{2,0,1:T(2,128)(2,1)} %get-tuple-element.269, s32[]{:T(128)S(6)} %select_n.28, bf16[2,3072,1536]{2,0,1:T(2,128)(2,1)} %get-tuple-element.267), kind=kLoop, calls=%fused_computation.17.clone.1 | loop fusion | bytes 12582916 | tf_op jit(solution)/shard_map/while/body/eval_jaxpr/dynamic_slice | solution.py:75
  289.8 7.0 %copy.41 = bf16[2,512,1536]{1,2,0:T(8,128)(2,1)S(1)} copy(bf16[2,512,1536]{2,0,1:T(2,128)(2,1)} %get-tuple-element.226) | data formatting | bytes 6291456 | tf_op jit(solution)/shard_map/while/body/eval_jaxpr/dynamic_slice | solution.py:75
  296.8 8.6 %copy.42 = bf16[2,512,1536]{1,2,0:T(8,128)(2,1)} copy(bf16[2,512,1536]{2,0,1:T(2,128)(2,1)} %get-tuple-element.230) | data formatting | bytes 6291456 | tf_op jit(solution)/shard_map/while/body/eval_jaxpr/dynamic_slice | solution.py:75
  305.4 3.0 fusion.38
  308.4 3.0 fusion.39
  311.5 3.2 fusion.41
  314.7 1.4 copy-done.2
  317.5 9.8 %constant_dynamic-slice_fusion.6 = (bf16[2,512,1536]{2,0,1:T(2,128)(2,1)}, bf16[2,512,1536]{2,0,1:T(2,128)(2,1)}) fusion(bf16[2,3072,1536]{2,0,1:T(2,128)(2,1)} %get-tuple-element.269, s32[]{:T(128)S(6)} %select_n.28, bf16[2,3072,1536]{2,0,1:T(2,128)(2,1)} %get-tuple-element.267), kind=kLoop, calls=%fused_computation.17.clone.1 | loop fusion | bytes 12582916 | tf_op jit(solution)/shard_map/while/body/eval_jaxpr/dynamic_slice | solution.py:75
  327.3 7.0 %copy.41 = bf16[2,512,1536]{1,2,0:T(8,128)(2,1)S(1)} copy(bf16[2,512,1536]{2,0,1:T(2,128)(2,1)} %get-tuple-element.226) | data formatting | bytes 6291456 | tf_op jit(solution)/shard_map/while/body/eval_jaxpr/dynamic_slice | solution.py:75
  334.3 8.6 %copy.42 = bf16[2,512,1536]{1,2,0:T(8,128)(2,1)} copy(bf16[2,512,1536]{2,0,1:T(2,128)(2,1)} %get-tuple-element.230) | data formatting | bytes 6291456 | tf_op jit(solution)/shard_map/while/body/eval_jaxpr/dynamic_slice | solution.py:75
  342.9 3.0 fusion.38
  346.0 3.0 fusion.39
  349.1 3.2 fusion.41
  355.1 9.8 %constant_dynamic-slice_fusion.6 = (bf16[2,512,1536]{2,0,1:T(2,128)(2,1)}, bf16[2,512,1536]{2,0,1:T(2,128)(2,1)}) fusion(bf16[2,3072,1536]{2,0,1:T(2,128)(2,1)} %get-tuple-element.269, s32[]{:T(128)S(6)} %select_n.28, bf16[2,3072,1536]{2,0,1:T(2,128)(2,1)} %get-tuple-element.267), kind=kLoop, calls=%fused_computation.17.clone.1 | loop fusion | bytes 12582916 | tf_op jit(solution)/shard_map/while/body/eval_jaxpr/dynamic_slice | solution.py:75
  364.9 7.0 %copy.41 = bf16[2,512,1536]{1,2,0:T(8,128)(2,1)S(1)} copy(bf16[2,512,1536]{2,0,1:T(2,128)(2,1)} %get-tuple-element.226) | data formatting | bytes 6291456 | tf_op jit(solution)/shard_map/while/body/eval_jaxpr/dynamic_slice | solution.py:75
  371.9 8.6 %copy.42 = bf16[2,512,1536]{1,2,0:T(8,128)(2,1)} copy(bf16[2,512,1536]{2,0,1:T(2,128)(2,1)} %get-tuple-element.230) | data formatting | bytes 6291456 | tf_op jit(solution)/shard_map/while/body/eval_jaxpr/dynamic_slice | solution.py:75
  380.5 3.0 fusion.38
  383.5 3.0 fusion.39
  386.6 3.2 fusion.41
  392.7 9.8 %constant_dynamic-slice_fusion.6 = (bf16[2,512,1536]{2,0,1:T(2,128)(2,1)}, bf16[2,512,1536]{2,0,1:T(2,128)(2,1)}) fusion(bf16[2,3072,1536]{2,0,1:T(2,128)(2,1)} %get-tuple-element.269, s32[]{:T(128)S(6)} %select_n.28, bf16[2,3072,1536]{2,0,1:T(2,128)(2,1)} %get-tuple-element.267), kind=kLoop, calls=%fused_computation.17.clone.1 | loop fusion | bytes 12582916 | tf_op jit(solution)/shard_map/while/body/eval_jaxpr/dynamic_slice | solution.py:75
  402.5 7.0 %copy.41 = bf16[2,512,1536]{1,2,0:T(8,128)(2,1)S(1)} copy(bf16[2,512,1536]{2,0,1:T(2,128)(2,1)} %get-tuple-element.226) | data formatting | bytes 6291456 | tf_op jit(solution)/shard_map/while/body/eval_jaxpr/dynamic_slice | solution.py:75
  409.5 8.6 %copy.42 = bf16[2,512,1536]{1,2,0:T(8,128)(2,1)} copy(bf16[2,512,1536]{2,0,1:T(2,128)(2,1)} %get-tuple-element.230) | data formatting | bytes 6291456 | tf_op jit(solution)/shard_map/while/body/eval_jaxpr/dynamic_slice | solution.py:75
  418.1 3.0 fusion.38
  421.1 3.0 fusion.39
  424.2 3.2 fusion.41
  430.3 9.8 %constant_dynamic-slice_fusion.6 = (bf16[2,512,1536]{2,0,1:T(2,128)(2,1)}, bf16[2,512,1536]{2,0,1:T(2,128)(2,1)}) fusion(bf16[2,3072,1536]{2,0,1:T(2,128)(2,1)} %get-tuple-element.269, s32[]{:T(128)S(6)} %select_n.28, bf16[2,3072,1536]{2,0,1:T(2,128)(2,1)} %get-tuple-element.267), kind=kLoop, calls=%fused_computation.17.clone.1 | loop fusion | bytes 12582916 | tf_op jit(solution)/shard_map/while/body/eval_jaxpr/dynamic_slice | solution.py:75
  440.1 7.0 %copy.41 = bf16[2,512,1536]{1,2,0:T(8,128)(2,1)S(1)} copy(bf16[2,512,1536]{2,0,1:T(2,128)(2,1)} %get-tuple-element.226) | data formatting | bytes 6291456 | tf_op jit(solution)/shard_map/while/body/eval_jaxpr/dynamic_slice | solution.py:75
  447.1 8.6 %copy.42 = bf16[2,512,1536]{1,2,0:T(8,128)(2,1)} copy(bf16[2,512,1536]{2,0,1:T(2,128)(2,1)} %get-tuple-element.230) | data formatting | bytes 6291456 | tf_op jit(solution)/shard_map/while/body/eval_jaxpr/dynamic_slice | solution.py:75
  455.7 3.0 fusion.38
  458.7 3.0 fusion.39
  461.8 3.2 fusion.41
  467.9 9.8 %constant_dynamic-slice_fusion.6 = (bf16[2,512,1536]{2,0,1:T(2,128)(2,1)}, bf16[2,512,1536]{2,0,1:T(2,128)(2,1)}) fusion(bf16[2,3072,1536]{2,0,1:T(2,128)(2,1)} %get-tuple-element.269, s32[]{:T(128)S(6)} %select_n.28, bf16[2,3072,1536]{2,0,1:T(2,128)(2,1)} %get-tuple-element.267), kind=kLoop, calls=%fused_computation.17.clone.1 | loop fusion | bytes 12582916 | tf_op jit(solution)/shard_map/while/body/eval_jaxpr/dynamic_slice | solution.py:75
  477.7 7.0 %copy.41 = bf16[2,512,1536]{1,2,0:T(8,128)(2,1)S(1)} copy(bf16[2,512,1536]{2,0,1:T(2,128)(2,1)} %get-tuple-element.226) | data formatting | bytes 6291456 | tf_op jit(solution)/shard_map/while/body/eval_jaxpr/dynamic_slice | solution.py:75
  484.7 8.6 %copy.42 = bf16[2,512,1536]{1,2,0:T(8,128)(2,1)} copy(bf16[2,512,1536]{2,0,1:T(2,128)(2,1)} %get-tuple-element.230) | data formatting | bytes 6291456 | tf_op jit(solution)/shard_map/while/body/eval_jaxpr/dynamic_slice | solution.py:75
  493.3 3.0 fusion.38
  496.3 3.0 fusion.39
  499.4 3.2 fusion.41
  504.0 2.9 copy_bitcast_fusion
  (87 shorter events, 14.9 us)
Async XLA Ops:
  6.5 58.9 %all-gather.5.cloned.1.call-start = ((), (), s32[]{:S(2)}) async-start(), calls=%async_computation | async-start | bytes 5898240 | tf_op jit(solution)/shard_map/all_gather | solution.py:19
  7.3 170.5 %all-gather.9.cloned.1.call-start = ((), (), s32[]{:S(2)}) async-start(), calls=%async_computation.2 | async-start | bytes 20054016 | tf_op jit(solution)/shard_map/all_gather | solution.py:66
  78.5 200.0 %all-gather.7.cloned.1.call-start = ((), (), s32[]{:S(2)}) async-start(), calls=%async_computation.1 | async-start | bytes 20054016 | tf_op jit(solution)/shard_map/all_gather | solution.py:65
  89.4 2.3 copy-start.3
  308.4 3.1 copy-start
  308.4 3.1 copy-start.1
  314.7 1.4 copy-start.2
  345.9 3.1 copy-start
  345.9 3.1 copy-start.1
  352.3 1.4 copy-start.2
  383.5 3.1 copy-start
  383.5 3.1 copy-start.1
  389.9 1.4 copy-start.2
  421.1 3.1 copy-start
  421.1 3.1 copy-start.1
  427.4 1.4 copy-start.2
  458.7 3.1 copy-start
  458.7 3.1 copy-start.1
  465.0 1.4 copy-start.2
  496.3 3.1 copy-start
  496.3 3.1 copy-start.1
  502.6 1.4 copy-start.2
Sparse Core Ops, SparseCore 0:
  8.9 56.4 all-gather.4
  78.6 99.0 all-gather.8
  179.3 99.1 all-gather.6
where the time goes:
time: 516 us; the launch traced here: 513 us
  waiting for transfers between devices  210 us (41%)
  local copies, waits for them, and re-layouts  171 us (33%)
  matrix products  69.9 us (14%)
  other arithmetic  22.3 us (4%)
  blocking collectives  21.8 us (4%)
  between operations  13.2 us (3%)
    dynamic_slice x24, local copies, waits for them, and re-layouts, scan_step(): lax.dynamic_slice_in_dim(member, offset, block_len, 1)  153 us
    all_gather x1, waiting for transfers between devices, on_device(): lax.all_gather(keys, 'ctx', axis=1, tiled=True)  101 us
    all_gather x1, waiting for transfers between devices, on_device(): shard_piece = lax.all_gather(hidden_in, 'tp', axis=2, tiled=True)  58.1 us
    all_gather x1, waiting for transfers between devices, on_device(): lax.all_gather(values, 'ctx', axis=1, tiled=True)  50.8 us
    dot_general x3, matrix products, on_device(): jnp.dot(flat_rows, matrix, preferred_element_type=jnp.float32)  32.7 us
    all_gather x1, blocking collectives, on_device(): lax.all_gather(event_pos, 'ctx', axis=1, tiled=True)  21.8 us
    dot_general x6, matrix products, update(): jnp.einsum('shqk,skhd->shqd', weights.astype(jnp.bfloat16), value_heads,...  19.3 us
    reduce_sum x6, other arithmetic, update(): new_sum = run_sum * shrink + jnp.sum(weights, axis=3)  18.2 us
  transfers between devices with their start and end apart: 3, of which 3 were waited for; matrix products, arithmetic and copies ran while one was open for 5% of the time, Pallas kernels for 0%

commit v1 on v0

v1 whole, which is shorter than its diff:
```python
import functools
import math

import jax
import jax.numpy as jnp
from jax import lax
from jax.experimental import pallas as pl
from jax.experimental.pallas import tpu as pltpu
from jax.sharding import PartitionSpec as P

HD = 128
LOG2_E = 1.4426950408889634
HIDDEN = -1e30


def exchange(value, axis, size, bit):
    return lax.ppermute(value, axis, [(i, i ^ bit) for i in range(size)])


def project_body(steps, parts, sequences, place, *refs):
    inputs = refs[: sequences * parts]
    weights = refs[sequences * parts : -2]
    out_ref, total = refs[-2:]
    step = pl.program_id(0)

    @pl.when(step == 0)
    def _():
        total[...] = jnp.zeros_like(total)

    for part in range(parts):

        @pl.when(step // steps == part)
        def _():
            for s in range(sequences):
                rows = inputs[s * parts + part]
                rows = rows[0] if len(rows.shape) == 3 else rows[...]
                for n, weight in enumerate(weights):
                    wide = weight.shape[1]
                    total[s, :, n * wide : (n + 1) * wide] += jnp.dot(
                        rows, weight[...], preferred_element_type=jnp.float32
                    )

    @pl.when(step == steps * parts - 1)
    def _():
        out_ref[...] = total[...].astype(out_ref.dtype)


def project(hidden_in, received, chosen, weights, tp_me, group, wide):
    rows, feats = hidden_in.shape[1:]
    parts = 1 + len(received[0])
    steps = max(1, feats // 1280)
    depth = feats // steps
    sequences = len(chosen)

    def share_map(part, i, place):
        return (0, jnp.clip(i - part * steps, 0, steps - 1))

    def own_map(s, i, place):
        return (s, 0, jnp.clip(i, 0, steps - 1))

    def weight_map(i, place):
        return ((place[0] ^ (i // steps)) * steps + i % steps, place[1])

    in_specs = []
    operands = []
    for s in chosen:
        in_specs.append(pl.BlockSpec((1, rows, depth), functools.partial(own_map, s)))
        operands.append(hidden_in)
        for part in range(1, parts):
            in_specs.append(pl.BlockSpec((rows, depth), functools.partial(share_map, part)))
            operands.append(received[s][part - 1])
    for weight in weights:
        in_specs.append(pl.BlockSpec((depth, wide), weight_map))
        operands.append(weight)
    columns = wide * len(weights)
    return pl.pallas_call(
        functools.partial(project_body, steps, parts, sequences),
        out_shape=jax.ShapeDtypeStruct((sequences, rows, columns), jnp.bfloat16),
        grid_spec=pltpu.PrefetchScalarGridSpec(
            num_scalar_prefetch=1,
            grid=(steps * parts,),
            in_specs=in_specs,
            out_specs=pl.BlockSpec((sequences, rows, columns), lambda i, place: (0, 0, 0)),
            scratch_shapes=[pltpu.VMEM((sequences, rows, columns), jnp.float32)],
        ),
        compiler_params=pltpu.CompilerParams(vmem_limit_bytes=32 * 2**20),
        cost_estimate=pl.CostEstimate(
            flops=2 * sequences * rows * feats * parts * columns,
            bytes_accessed=2 * feats * parts * (columns + sequences * rows),
            transcendentals=0,
        ),
    )(jnp.stack([tp_me, group]).astype(jnp.int32), *operands)


def attend_body(seq, ways, blocks, spans, tile, table, place, *refs):
    query_refs = refs[:ways]
    block_refs = refs[ways : ways + blocks]
    out_refs = refs[ways + blocks : 2 * ways + blocks]
    ordered, scores, highest, sums, total, offsets, sems = refs[2 * ways + blocks :]
    rows, width = out_refs[0].shape
    half = rows // 2
    heads = width // HD
    rest = blocks // ways
    me = place[0]

    def span_of(slot):
        return table[(me ^ slot) * 2 + seq]

    copies = []
    for slot in range(blocks):
        low = span_of(slot)
        for part, span in ((0, low), (1, spans - 1 - low)):
            copies.append(
                pltpu.make_async_copy(
                    block_refs[slot].at[0, pl.ds(part * half, half)],
                    ordered.at[pl.ds(pl.multiple_of(span * half, 16), half)],
                    sems.at[2 * slot + part],
                )
            )
    for copy in copies:
        copy.start()
    for copy in copies:
        copy.wait()

    per_tile = tile // half
    slope = LOG2_E / math.sqrt(HD)
    row = lax.broadcasted_iota(jnp.int32, (rows, tile), 0)
    lane = lax.broadcasted_iota(jnp.int32, (rows, tile), 1)

    def score_step(first, query_ref, t, carry):
        start = pl.multiple_of(t * tile, 128)
        visible = offsets[first:] >= start
        for h in range(heads):
            part = lax.dot_general(
                query_ref[0, first:, h * HD : (h + 1) * HD],
                ordered[pl.ds(start, tile), h * HD : (h + 1) * HD],
                (((1,), (1,)), ((), ())),
                preferred_element_type=jnp.float32,
            )
            part = jnp.where(visible, part, HIDDEN)
            scores[h, first:, pl.ds(start, tile)] = part
            top = highest[h, first:]
            for j in range(tile // 128):
                top = jnp.maximum(top, part[:, j * 128 : (j + 1) * 128])
            highest[h, first:] = top
        return carry

    def value_step(first, tops, t, carry):
        start = pl.multiple_of(t * tile, 128)
        for h in range(heads):
            part = scores[h, first:, pl.ds(start, tile)]
            weight = jnp.exp2((part - tops[h][first:]) * slope)
            added = sums[h, first:]
            for j in range(tile // 128):
                added = added + weight[:, j * 128 : (j + 1) * 128]
            sums[h, first:] = added
            total[h, first:] += jnp.dot(
                weight.astype(jnp.bfloat16),
                ordered[pl.ds(start, tile), width + h * HD : width + (h + 1) * HD],
                preferred_element_type=jnp.float32,
            )
        return carry

    for a in range(ways):
        low = span_of(a * rest)
        high = spans - 1 - low
        query_ref = query_refs[a]
        offsets[...] = jnp.where(row < half, low * half + row, high * half + row - half) - lane
        highest[...] = jnp.full_like(highest, HIDDEN)
        sums[...] = jnp.zeros_like(sums)
        total[...] = jnp.zeros_like(total)
        both = (low + per_tile) // per_tile
        upto = (high + per_tile) // per_tile
        lax.fori_loop(0, both, functools.partial(score_step, 0, query_ref), 0)
        lax.fori_loop(both, upto, functools.partial(score_step, half, query_ref), 0)
        tops = [jnp.max(highest[h], axis=1, keepdims=True) for h in range(heads)]
        lax.fori_loop(0, both, functools.partial(value_step, 0, tops), 0)
        lax.fori_loop(both, upto, functools.partial(value_step, half, tops), 0)
        for h in range(heads):
            denom = jnp.sum(sums[h], axis=1, keepdims=True)
            out_refs[a][:, h * HD : (h + 1) * HD] = (total[h] / denom).astype(jnp.bfloat16)


def attend(seq, queries, blocks, table, me):
    rows, width = queries[0].shape[1:]
    ways, count = len(queries), len(blocks)
    spans = 2 * count
    half = rows // 2
    length = count * rows
    tile = 4 * half
    heads = width // HD
    smem = pl.BlockSpec(memory_space=pltpu.SMEM)
    one = pl.BlockSpec((1, rows, width), lambda i: (seq, 0, 0))
    flops = ways * heads * (spans + 3) * half * half * HD * 4
    return pl.pallas_call(
        functools.partial(attend_body, seq, ways, count, spans, tile),
        out_shape=[jax.ShapeDtypeStruct((rows, width), jnp.bfloat16)] * ways,
        grid=(1,),
        in_specs=[smem, smem] + [one] * ways + [pl.BlockSpec(memory_space=pl.ANY)] * count,
        out_specs=[pl.BlockSpec((rows, width), lambda i: (0, 0))] * ways,
        scratch_shapes=[
            pltpu.VMEM((length, 2 * width), jnp.bfloat16),
            pltpu.VMEM((heads, rows, length), jnp.float32),
            pltpu.VMEM((heads, rows, 128), jnp.float32),
            pltpu.VMEM((heads, rows, 128), jnp.float32),
            pltpu.VMEM((heads, rows, HD), jnp.float32),
            pltpu.VMEM((rows, tile), jnp.int32),
            pltpu.SemaphoreType.DMA((2 * count,)),
        ],
        compiler_params=pltpu.CompilerParams(vmem_limit_bytes=48 * 2**20),
        cost_estimate=pl.CostEstimate(
            flops=flops,
            bytes_accessed=4 * length * width + 4 * ways * rows * width,
            transcendentals=flops // (4 * HD),
        ),
    )(table, me, *queries, *blocks)


def assemble_body(ways, sequences, place, *refs):
    out_ref = refs[-1]
    for a in range(ways):

        @pl.when(pl.program_id(0) == a)
        def _():
            for s in range(sequences):
                out_ref[s] = refs[s * ways + a][...]


def assemble(pieces, group):
    sequences, ways = len(pieces), len(pieces[0])
    rows, width = pieces[0][0].shape
    return pl.pallas_call(
        functools.partial(assemble_body, ways, sequences),
        out_shape=jax.ShapeDtypeStruct((sequences, rows, ways * width), jnp.bfloat16),
        grid_spec=pltpu.PrefetchScalarGridSpec(
            num_scalar_prefetch=1,
            grid=(ways,),
            in_specs=[pl.BlockSpec((rows, width), lambda a, place: (0, 0))] * (sequences * ways),
            out_specs=pl.BlockSpec((sequences, rows, width), lambda a, place: (0, 0, place[0] ^ a)),
        ),
        compiler_params=pltpu.CompilerParams(vmem_limit_bytes=32 * 2**20),
    )(group.reshape(1), *[piece for row in pieces for piece in row])


def on_device(ctx_size, tp_size, hidden_in, w_q, w_k, w_v, event_pos):
    sequences, rows, _ = hidden_in.shape
    features = w_q.shape[1]
    ways = math.gcd(features // HD, ctx_size)
    rest = ctx_size // ways
    width = features // ways
    ctx_me = lax.axis_index("ctx").astype(jnp.int32)
    tp_me = lax.axis_index("tp").astype(jnp.int32)
    group = ctx_me // rest

    table = lax.all_gather(event_pos[:, 0] // (rows // 2), "ctx", axis=0, tiled=True)
    received = []
    for s in range(sequences):
        shares = [hidden_in[s]]
        bit = 1
        while bit < tp_size:
            shares += [exchange(share, "tp", tp_size, bit) for share in shares]
            bit *= 2
        received.append(shares[1:])

    order = list(range(ways - 1, -1, -1))

    def swap_groups(made):
        return {
            a: (exchange(made[a], "ctx", ctx_size, a * rest) if a else made[a]) for a in made
        }

    blocks = []
    for s in range(sequences):
        made = {
            a: project(hidden_in, received, [s], [w_k, w_v], tp_me, group ^ a, width)
            for a in order
        }
        blocks.append(swap_groups(made))
    made = {
        a: project(hidden_in, received, list(range(sequences)), [w_q], tp_me, group ^ a, width)
        for a in order
    }
    queries = swap_groups(made)
    pieces = []
    for s in range(sequences):
        held = {a * rest: blocks[s][a] for a in range(ways)}
        bit = rest // 2
        while bit:
            held.update({i | bit: exchange(held[i], "ctx", ctx_size, bit) for i in list(held)})
            bit //= 2
        outs = attend(
            s,
            [queries[a] for a in range(ways)],
            [held[i] for i in range(ctx_size)],
            table,
            ctx_me.reshape(1),
        )
        back = swap_groups({a: outs[a] for a in order})
        pieces.append([back[a] for a in range(ways)])
    return assemble(pieces, group)


def solution(mesh):
    sizes = dict(mesh.shape)
    placed = (P(None, "ctx", "tp"), P(None, "tp"), P(None, "tp"), P(None, "tp"), P(None, "ctx"))
    return jax.shard_map(
        functools.partial(on_device, sizes["ctx"], sizes["tp"]),
        mesh=mesh,
        in_specs=placed,
        out_specs=P(None, "ctx", "tp"),
        check_vma=False,
    )
```

time: 516 us -> 282 us (0.55)
  local copies, waits for them, and re-layouts: 171 us -> 33.3 us
  waiting for transfers between devices: 210 us -> 77.5 us
  Pallas kernels: 0 us -> 111 us
  matrix products: 69.9 us -> 0 us
  starting transfers between devices: 0.08 us -> 37.3 us
  other arithmetic: 22.3 us -> 0.65 us
  between operations: 13.2 us -> 1.06 us
    all_gather x3 -> x0, waiting for transfers between devices: 210 us -> none  [the longest x1 101 us: on_device(): lax.all_gather(keys, 'ctx', axis=1, tiled=True)]
    dynamic_slice x30 -> x0, local copies, waits for them, and re-layouts: 156 us -> none  [the longest x24 153 us: scan_step(): lax.dynamic_slice_in_dim(member, offset, block_len, 1)]
    pallas_call x0 -> x15, Pallas kernels: none -> 111 us  [the longest x12 67 us: project(): pl.pallas_call(functools.partial(project_body, steps, parts, sequences),...]
    ppermute x0 -> x41, waiting for transfers between devices: none -> 77.5 us  [exchange(): return lax.ppermute(value, axis, [(i, i ^ bit) for i in range(size)])]
    dot_general x15 -> x0, matrix products: 69.9 us -> none  [the longest x3 32.7 us: on_device(): jnp.dot(flat_rows, matrix, preferred_element_type=jnp.float32)]
    ppermute x0 -> x41, starting transfers between devices: none -> 37.3 us  [exchange(): return lax.ppermute(value, axis, [(i, i ^ bit) for i in range(size)])]
    unnamed x4 -> x72, local copies, waits for them, and re-layouts: 1.45 us -> 30.7 us
    all_gather x1 -> x0, blocking collectives: 21.8 us -> none  [on_device(): lax.all_gather(event_pos, 'ctx', axis=1, tiled=True)]
  transfers between devices with their start and end apart: 3 -> 41, of which waited for: 3 -> 12; matrix products, arithmetic and copies ran while one was open for 5% -> 0% of each run, Pallas kernels for 0% -> 39%
where the time goes in v1:
time: 282 us; the launch traced here: 280 us
  Pallas kernels  111 us (39%)
  waiting for transfers between devices  77.5 us (27%)
  starting transfers between devices  37.3 us (13%)
  local copies, waits for them, and re-layouts  33.3 us (12%)
  blocking collectives  19.7 us (7%)
    ppermute x41, waiting for transfers between devices, exchange(): return lax.ppermute(value, axis, [(i, i ^ bit) for i in range(size)])  77.5 us
    pallas_call x12, Pallas kernels, project(): pl.pallas_call(functools.partial(project_body, steps, parts, sequences),...  67 us
    pallas_call x2, Pallas kernels, attend(): pl.pallas_call(functools.partial(attend_body, seq, ways, count, spans, ti...  42.1 us
    ppermute x41, starting transfers between devices, exchange(): return lax.ppermute(value, axis, [(i, i ^ bit) for i in range(size)])  37.3 us
    unnamed x72, local copies, waits for them, and re-layouts  30.7 us
    unnamed x1, blocking collectives  19.7 us
  transfers between devices with their start and end apart: 41, of which 12 were waited for; matrix products, arithmetic and copies ran while one was open for 0% of the time, Pallas kernels for 39%

profile of v1, /device:TPU:0, one launch (start us, length us, event | category | flops | bytes accessed | tf_op | source)
XLA Modules:
  0.0 280.1 jit_solution(17687514896013092290)
XLA Ops:
  0.0 2.6 slice_bitcast_fusion
  2.6 2.9 %collective-permute-start.1 = (bf16[192,2560]{1,0:T(8,128)(2,1)S(1)}, bf16[192,2560]{1,0:T(8,128)(2,1)S(1)}, u32[]{:S(2)}, u32[]{:S(2)}) collective-permute-start(bf16[192,2560]{1,0:T(8,128)(2,1)S(1)} %get-tuple-element.21), channel_id=1, source_target_pairs={{0,1},{1,0},{2,3},{3,2},{4,5},{5,4},{6,7},{7,6},{8,9},{9,8},{10,11... | collective-permute-start | bytes 2949128 | tf_op jit(solution)/shard_map/ppermute | solution.py:17
  5.8 22.2 %collective-permute-done.1.refs_3_.refs_1_ = bf16[192,2560]{1,0:T(8,128)(2,1)S(1)} collective-permute-done((bf16[192,2560]{1,0:T(8,128)(2,1)S(1)}, bf16[192,2560]{1,0:T(8,128)(2,1)S(1)}, u32[]{:S(2)}, u32[]{:S(2)}) %collective-permute-start.1) | collective-permute-done | bytes 983072 | tf_op jit(solution)/shard_map/ppermute | solution.py:17
  28.1 5.5 %copy-done = bf16[5120,1536]{1,0:T(8,128)(2,1)S(1)} copy-done((bf16[5120,1536]{1,0:T(8,128)(2,1)S(1)}, bf16[5120,1536]{1,0:T(8,128)(2,1)}, u32[]{:S(2)}) %copy-start) | copy-done | bytes 15728664
  33.6 1.5 copy-done.2
  35.1 5.8 %shard_map.64.refs_4_ = bf16[1,192,768]{2,1,0:T(8,128)(2,1)S(1)} custom-call(s32[2]{0:T(128)S(1)} %pad_add_fusion.place, bf16[2,192,2560]{2,1,0:T(8,128)(2,1)S(1)} %copy-done.2, bf16[192,2560]{1,0:T(8,128)(2,1)S(1)} %collective-permute-done.1.refs_3_.refs_1_, bf16[5120,1536]{1,0:T(8,128)(2,1)S(1)} %copy-done, bf16[5120,1536]{1,0:T(8,128)(2,1)} %refs_3_.15), custom_call_target="tpu_custom_call" | custom-call | flops 1509949440 | bytes 9830400 | tf_op jit(solution)/shard_map/pallas_call | solution.py:76
  40.9 2.2 collective-permute-start.24
  43.0 5.4 %collective-permute-done.refs_1_ = bf16[192,2560]{1,0:T(8,128)(2,1)} collective-permute-done((bf16[192,2560]{1,0:T(8,128)(2,1)}, bf16[192,2560]{1,0:T(8,128)(2,1)}, u32[]{:S(2)}, u32[]{:S(2)}) %collective-permute-start) | collective-permute-done | bytes 983072 | tf_op jit(solution)/shard_map/ppermute | solution.py:17
  48.4 5.5 %copy-done.4 = bf16[5120,1536]{1,0:T(8,128)(2,1)S(1)} copy-done((bf16[5120,1536]{1,0:T(8,128)(2,1)S(1)}, bf16[5120,1536]{1,0:T(8,128)(2,1)}, u32[]{:S(2)}) %copy-start.4) | copy-done | bytes 15728664
  53.9 5.1 %shard_map.58 = bf16[2,192,384]{2,1,0:T(8,128)(2,1)S(1)} custom-call(s32[2]{0:T(128)S(1)} %pad_add_fusion.3.place, bf16[2,192,2560]{2,1,0:T(8,128)(2,1)S(1)} %copy-done.3, bf16[192,2560]{1,0:T(8,128)(2,1)} %collective-permute-done.refs_1_, bf16[2,192,2560]{2,1,0:T(8,128)(2,1)S(1)} %copy-done.3, bf16[192,2560]{1,0:T(8,128)(2,1)S(1)} %collective-permute-done.1.refs_3_.refs_1_, ...), custom_call_target="tpu_custom_call" | custom-call | flops 1509949440 | bytes 7864320 | tf_op jit(solution)/shard_map/pallas_call | solution.py:76
  59.0 3.9 %collective-permute-start.4 = (bf16[2,192,384]{2,1,0:T(8,128)(2,1)S(1)}, bf16[2,192,384]{2,1,0:T(8,128)(2,1)S(1)}, u32[]{:S(2)}, u32[]{:S(2)}) collective-permute-start(bf16[2,192,384]{2,1,0:T(8,128)(2,1)S(1)} %shard_map.58), channel_id=1, source_target_pairs={{0,24},{2,26},{4,28},{6,30},{8,16},{10,18},{12,20},{14,22},{16,8},... | collective-permute-start | bytes 884744 | tf_op jit(solution)/shard_map/ppermute | solution.py:17
  62.9 5.1 %shard_map.57 = bf16[2,192,384]{2,1,0:T(8,128)(2,1)S(1)} custom-call(s32[2]{0:T(128)S(1)} %pad_add_fusion.2.place, bf16[2,192,2560]{2,1,0:T(8,128)(2,1)S(1)} %copy-done.3, bf16[192,2560]{1,0:T(8,128)(2,1)} %collective-permute-done.refs_1_, bf16[2,192,2560]{2,1,0:T(8,128)(2,1)S(1)} %copy-done.3, bf16[192,2560]{1,0:T(8,128)(2,1)S(1)} %collective-permute-done.1.refs_3_.refs_1_, ...), custom_call_target="tpu_custom_call" | custom-call | flops 1509949440 | bytes 7864320 | tf_op jit(solution)/shard_map/pallas_call | solution.py:76
  68.0 5.1 %shard_map.56 = bf16[2,192,384]{2,1,0:T(8,128)(2,1)S(1)} custom-call(s32[2]{0:T(128)S(1)} %pad_add_fusion.1.place, bf16[2,192,2560]{2,1,0:T(8,128)(2,1)S(1)} %copy-done.3, bf16[192,2560]{1,0:T(8,128)(2,1)} %collective-permute-done.refs_1_, bf16[2,192,2560]{2,1,0:T(8,128)(2,1)S(1)} %copy-done.3, bf16[192,2560]{1,0:T(8,128)(2,1)S(1)} %collective-permute-done.1.refs_3_.refs_1_, ...), custom_call_target="tpu_custom_call" | custom-call | flops 1509949440 | bytes 7864320 | tf_op jit(solution)/shard_map/pallas_call | solution.py:76
  73.7 5.5 %copy-done.1 = bf16[5120,1536]{1,0:T(8,128)(2,1)S(1)} copy-done((bf16[5120,1536]{1,0:T(8,128)(2,1)S(1)}, bf16[5120,1536]{1,0:T(8,128)(2,1)}, u32[]{:S(2)}) %copy-start.1) | copy-done | bytes 15728664
  79.2 5.8 %shard_map.65 = bf16[1,192,768]{2,1,0:T(8,128)(2,1)S(1)} custom-call(s32[2]{0:T(128)S(1)} %pad_add_fusion.1.place, bf16[2,192,2560]{2,1,0:T(8,128)(2,1)S(1)} %copy-done.3, bf16[192,2560]{1,0:T(8,128)(2,1)S(1)} %collective-permute-done.1.refs_3_.refs_1_, bf16[5120,1536]{1,0:T(8,128)(2,1)S(1)} %copy-done.1, bf16[5120,1536]{1,0:T(8,128)(2,1)} %refs_3_.15), custom_call_target="tpu_custom_call" | custom-call | flops 1509949440 | bytes 9830400 | tf_op jit(solution)/shard_map/pallas_call | solution.py:76
  85.0 5.8 %shard_map.66 = bf16[1,192,768]{2,1,0:T(8,128)(2,1)S(1)} custom-call(s32[2]{0:T(128)S(1)} %pad_add_fusion.2.place, bf16[2,192,2560]{2,1,0:T(8,128)(2,1)S(1)} %copy-done.3, bf16[192,2560]{1,0:T(8,128)(2,1)S(1)} %collective-permute-done.1.refs_3_.refs_1_, bf16[5120,1536]{1,0:T(8,128)(2,1)S(1)} %copy-done.1, bf16[5120,1536]{1,0:T(8,128)(2,1)} %refs_3_.15), custom_call_target="tpu_custom_call" | custom-call | flops 1509949440 | bytes 9830400 | tf_op jit(solution)/shard_map/pallas_call | solution.py:76
  90.7 5.8 %shard_map.67 = bf16[1,192,768]{2,1,0:T(8,128)(2,1)S(1)} custom-call(s32[2]{0:T(128)S(1)} %pad_add_fusion.3.place, bf16[2,192,2560]{2,1,0:T(8,128)(2,1)S(1)} %copy-done.3, bf16[192,2560]{1,0:T(8,128)(2,1)S(1)} %collective-permute-done.1.refs_3_.refs_1_, bf16[5120,1536]{1,0:T(8,128)(2,1)S(1)} %copy-done.1, bf16[5120,1536]{1,0:T(8,128)(2,1)} %refs_3_.15), custom_call_target="tpu_custom_call" | custom-call | flops 1509949440 | bytes 9830400 | tf_op jit(solution)/shard_map/pallas_call | solution.py:76
  96.5 6.0 %shard_map.60 = bf16[1,192,768]{2,1,0:T(8,128)(2,1)S(1)} custom-call(s32[2]{0:T(128)S(1)} %pad_add_fusion.1.place, bf16[2,192,2560]{2,1,0:T(8,128)(2,1)S(1)} %copy-done.3, bf16[192,2560]{1,0:T(8,128)(2,1)} %collective-permute-done.refs_1_, bf16[5120,1536]{1,0:T(8,128)(2,1)S(1)} %copy-done.1, bf16[5120,1536]{1,0:T(8,128)(2,1)} %refs_3_.15), custom_call_target="tpu_custom_call" | custom-call | flops 1509949440 | bytes 9830400 | tf_op jit(solution)/shard_map/pallas_call | solution.py:76
  103.2 1.5 collective-permute-start.26
  105.4 2.9 %collective-permute-start.30 = (bf16[1,192,768]{2,1,0:T(8,128)(2,1)S(1)}, bf16[1,192,768]{2,1,0:T(8,128)(2,1)S(1)}, u32[]{:S(2)}, u32[]{:S(2)}) collective-permute-start(bf16[1,192,768]{2,1,0:T(8,128)(2,1)S(1)} %shard_map.66), channel_id=1, source_target_pairs={{0,16},{2,18},{4,20},{6,22},{8,24},{10,26},{12,28},{14,30},{16,0},... | collective-permute-start | bytes 884744 | tf_op jit(solution)/shard_map/ppermute | solution.py:17
  108.3 5.8 %shard_map.61 = bf16[1,192,768]{2,1,0:T(8,128)(2,1)S(1)} custom-call(s32[2]{0:T(128)S(1)} %pad_add_fusion.2.place, bf16[2,192,2560]{2,1,0:T(8,128)(2,1)S(1)} %copy-done.3, bf16[192,2560]{1,0:T(8,128)(2,1)} %collective-permute-done.refs_1_, bf16[5120,1536]{1,0:T(8,128)(2,1)S(1)} %copy-done.1, bf16[5120,1536]{1,0:T(8,128)(2,1)} %refs_3_.15), custom_call_target="tpu_custom_call" | custom-call | flops 1509949440 | bytes 9830400 | tf_op jit(solution)/shard_map/pallas_call | solution.py:76
  114.2 5.8 %shard_map.62 = bf16[1,192,768]{2,1,0:T(8,128)(2,1)S(1)} custom-call(s32[2]{0:T(128)S(1)} %pad_add_fusion.3.place, bf16[2,192,2560]{2,1,0:T(8,128)(2,1)S(1)} %copy-done.3, bf16[192,2560]{1,0:T(8,128)(2,1)} %collective-permute-done.refs_1_, bf16[5120,1536]{1,0:T(8,128)(2,1)S(1)} %copy-done.1, bf16[5120,1536]{1,0:T(8,128)(2,1)} %refs_3_.15), custom_call_target="tpu_custom_call" | custom-call | flops 1509949440 | bytes 9830400 | tf_op jit(solution)/shard_map/pallas_call | solution.py:76
  120.0 5.8 %shard_map.59.refs_4_ = bf16[1,192,768]{2,1,0:T(8,128)(2,1)S(1)} custom-call(s32[2]{0:T(128)S(1)} %pad_add_fusion.place, bf16[2,192,2560]{2,1,0:T(8,128)(2,1)S(1)} %copy-done.3, bf16[192,2560]{1,0:T(8,128)(2,1)} %collective-permute-done.refs_1_, bf16[5120,1536]{1,0:T(8,128)(2,1)S(1)} %copy-done.1, bf16[5120,1536]{1,0:T(8,128)(2,1)} %refs_3_.15), custom_call_target="tpu_custom_call" | custom-call | flops 1509949440 | bytes 9830400 | tf_op jit(solution)/shard_map/pallas_call | solution.py:76
  126.5 2.3 collective-permute-done.30.refs_12_
  128.8 1.5 collective-permute-start.12
  130.8 1.5 collective-permute-start.6
  133.0 2.6 collective-permute-done.8.refs_8_
  135.6 1.5 collective-permute-start.28
  137.1 17.1 %collective-permute-done.12.refs_12_ = bf16[1,192,768]{2,1,0:T(8,128)(2,1)} collective-permute-done((bf16[1,192,768]{2,1,0:T(8,128)(2,1)S(1)}, bf16[1,192,768]{2,1,0:T(8,128)(2,1)}, u32[]{:S(2)}, u32[]{:S(2)}) %collective-permute-start.12) | collective-permute-done | bytes 294944 | tf_op jit(solution)/shard_map/ppermute | solution.py:17
  154.2 1.5 collective-permute-start.32
  159.0 1.9 collective-permute-done.32.refs_14_
  160.9 3.2 %collective-permute-done.36.refs_18_ = bf16[1,192,768]{2,1,0:T(8,128)(2,1)S(1)} collective-permute-done((bf16[1,192,768]{2,1,0:T(8,128)(2,1)}, bf16[1,192,768]{2,1,0:T(8,128)(2,1)S(1)}, u32[]{:S(2)}, u32[]{:S(2)}) %collective-permute-start.36) | collective-permute-done | bytes 294944 | tf_op jit(solution)/shard_map/ppermute | solution.py:17
  164.1 1.5 collective-permute-start.10
  167.6 1.5 collective-permute-start.18
  171.0 3.3 %collective-permute-done.10.refs_10_ = bf16[1,192,768]{2,1,0:T(8,128)(2,1)} collective-permute-done((bf16[1,192,768]{2,1,0:T(8,128)(2,1)}, bf16[1,192,768]{2,1,0:T(8,128)(2,1)}, u32[]{:S(2)}, u32[]{:S(2)}) %collective-permute-start.10) | collective-permute-done | bytes 294944 | tf_op jit(solution)/shard_map/ppermute | solution.py:17
  174.3 5.8 %collective-permute-done.14.refs_14_ = bf16[1,192,768]{2,1,0:T(8,128)(2,1)} collective-permute-done((bf16[1,192,768]{2,1,0:T(8,128)(2,1)}, bf16[1,192,768]{2,1,0:T(8,128)(2,1)}, u32[]{:S(2)}, u32[]{:S(2)}) %collective-permute-start.14) | collective-permute-done | bytes 294944 | tf_op jit(solution)/shard_map/ppermute | solution.py:17
  180.2 3.2 %collective-permute-done.18.refs_18_ = bf16[1,192,768]{2,1,0:T(8,128)(2,1)} collective-permute-done((bf16[1,192,768]{2,1,0:T(8,128)(2,1)}, bf16[1,192,768]{2,1,0:T(8,128)(2,1)}, u32[]{:S(2)}, u32[]{:S(2)}) %collective-permute-start.18) | collective-permute-done | bytes 294944 | tf_op jit(solution)/shard_map/ppermute | solution.py:17
  183.5 19.7 %all-reduce.table = s32[32]{0:T(128)S(1)} all-reduce(s32[32]{0:T(128)S(1)} %fusion), channel_id=1, replica_groups=mesh['ctx'=16,'tp'=2] {'ctx'}, use_global_device_ids=true, to_apply=%add | all-reduce | flops 32 | bytes 256
  204.4 5.5 %copy-done.5 = bf16[5120,1536]{1,0:T(8,128)(2,1)S(1)} copy-done((bf16[5120,1536]{1,0:T(8,128)(2,1)S(1)}, bf16[5120,1536]{1,0:T(8,128)(2,1)}, u32[]{:S(2)}) %copy-start.5) | copy-done | bytes 15728664
  209.9 5.4 %shard_map.55.refs_0_ = bf16[2,192,384]{2,1,0:T(8,128)(2,1)S(1)} custom-call(s32[2]{0:T(128)S(1)} %pad_add_fusion.place, bf16[2,192,2560]{2,1,0:T(8,128)(2,1)S(1)} %copy-done.3, bf16[192,2560]{1,0:T(8,128)(2,1)} %collective-permute-done.refs_1_, bf16[2,192,2560]{2,1,0:T(8,128)(2,1)S(1)} %copy-done.3, ...), custom_call_target="tpu_custom_call" | custom-call | flops 1509949440 | bytes 7864320 | tf_op jit(solution)/shard_map/pallas_call | solution.py:76
  215.5 21.5 %shard_map.68 = (bf16[192,384]{1,0:T(8,128)(2,1)S(1)}, bf16[192,384]{1,0:T(8,128)(2,1)S(1)}, bf16[192,384]{1,0:T(8,128)(2,1)S(1)}, bf16[192,384]{1,0:T(8,128)(2,1)S(1)}) custom-call(s32[32]{0:T(128)S(1)} %all-reduce.table, s32[1]{0:T(128)} %bitcast.2.place, bf16[2,192,384]{2,1,0:T(8,128)(2,1)S(1)} %shard_map.55.refs_0_, bf16[2,192,384]{2,1,0:T(8,128)(2,1)S(1)} %copy-done.11, ...), custom_call_target="tpu_custom_call" | custom-call | flops 1981808640 | bytes 5898240 | tf_op jit(solution)/shard_map/pallas_call | solution.py:195
  237.0 2.8 %collective-permute-start.38 = (bf16[192,384]{1,0:T(8,128)(2,1)S(1)}, bf16[192,384]{1,0:T(8,128)(2,1)S(1)}, u32[]{:S(2)}, u32[]{:S(2)}) collective-permute-start(bf16[192,384]{1,0:T(8,128)(2,1)S(1)} %get-tuple-element.18), channel_id=1, source_target_pairs={{0,8},{2,10},{4,12},{6,14},{8,0},{10,2},{12,4},{14,6},{16,24},{18,... | collective-permute-start | bytes 442376 | tf_op jit(solution)/shard_map/ppermute | solution.py:17
  240.4 1.9 collective-permute-start.40
  243.0 20.6 %shard_map.63 = (bf16[192,384]{1,0:T(8,128)(2,1)S(1)}, bf16[192,384]{1,0:T(8,128)(2,1)S(1)}, bf16[192,384]{1,0:T(8,128)(2,1)S(1)}, bf16[192,384]{1,0:T(8,128)(2,1)S(1)}) custom-call(s32[32]{0:T(128)S(1)} %all-reduce.table, s32[1]{0:T(128)} %bitcast.2.place, bf16[2,192,384]{2,1,0:T(8,128)(2,1)S(1)} %shard_map.55.refs_0_, bf16[2,192,384]{2,1,0:T(8,128)(2,1)S(1)} %copy-done.11, ...), custom_call_target="tpu_custom_call" | custom-call | flops 1981808640 | bytes 5898240 | tf_op jit(solution)/shard_map/pallas_call | solution.py:195
  266.2 1.9 collective-permute-start.22
  268.1 3.8 %collective-permute-done.20.refs_1_ = bf16[192,384]{1,0:T(8,128)(2,1)S(1)} collective-permute-done((bf16[192,384]{1,0:T(8,128)(2,1)S(1)}, bf16[192,384]{1,0:T(8,128)(2,1)S(1)}, u32[]{:S(2)}, u32[]{:S(2)}) %collective-permute-start.20) | collective-permute-done | bytes 147488 | tf_op jit(solution)/shard_map/ppermute | solution.py:17
  271.9 6.7 %collective-permute-done.21.refs_2_ = bf16[192,384]{1,0:T(8,128)(2,1)S(1)} collective-permute-done((bf16[192,384]{1,0:T(8,128)(2,1)S(1)}, bf16[192,384]{1,0:T(8,128)(2,1)S(1)}, u32[]{:S(2)}, u32[]{:S(2)}) %collective-permute-start.21) | collective-permute-done | bytes 147488 | tf_op jit(solution)/shard_map/ppermute | solution.py:17
  278.5 1.6 shard_map.69
  (130 shorter events, 16.2 us)
Async XLA Ops:
  2.6 25.5 %collective-permute-start.1 = (bf16[192,2560]{1,0:T(8,128)(2,1)S(1)}, bf16[192,2560]{1,0:T(8,128)(2,1)S(1)}, u32[]{:S(2)}, u32[]{:S(2)}) collective-permute-start(bf16[192,2560]{1,0:T(8,128)(2,1)S(1)} %get-tuple-element.21), channel_id=1, source_target_pairs={{0,1},{1,0},{2,3},{3,2},{4,5},{5,4},{6,7},{7,6},{8,9},{9,8},{10,11... | collective-permute-start | bytes 2949128 | tf_op jit(solution)/shard_map/ppermute | solution.py:17
  5.5 42.9 %collective-permute-start = (bf16[192,2560]{1,0:T(8,128)(2,1)}, bf16[192,2560]{1,0:T(8,128)(2,1)}, u32[]{:S(2)}, u32[]{:S(2)}) collective-permute-start(bf16[192,2560]{1,0:T(8,128)(2,1)} %get-tuple-element.22), channel_id=1, source_target_pairs={{0,1},{1,0},{2,3},{3,2},{4,5},{5,4},{6,7},{7,6},{8,9},{9,8},{10,11... | collective-permute-start | bytes 2949128 | tf_op jit(solution)/shard_map/ppermute | solution.py:17
  35.1 13.3 %copy-start.3 = (bf16[2,192,2560]{2,1,0:T(8,128)(2,1)S(1)}, bf16[2,192,2560]{2,1,0:T(8,128)(2,1)}, u32[]{:S(2)}) copy-start(bf16[2,192,2560]{2,1,0:T(8,128)(2,1)} %refs_0_.23) | copy-start | bytes 5898244
  40.9 89.9 %collective-permute-start.24 = (bf16[1,192,768]{2,1,0:T(8,128)(2,1)S(1)}, bf16[1,192,768]{2,1,0:T(8,128)(2,1)}, u32[]{:S(2)}, u32[]{:S(2)}) collective-permute-start(bf16[1,192,768]{2,1,0:T(8,128)(2,1)S(1)} %shard_map.64.refs_4_), channel_id=1, source_target_pairs={{0,4},{2,6},{4,0},{6,2},{8,12},{10,14},{12,8},{14,10},{16,20},{18,... | collective-permute-start | bytes 884744 | tf_op jit(solution)/shard_map/ppermute | solution.py:17
  43.0 89.3 %collective-permute-start.23 = (bf16[1,192,768]{2,1,0:T(8,128)(2,1)S(1)}, bf16[1,192,768]{2,1,0:T(8,128)(2,1)S(1)}, u32[]{:S(2)}, u32[]{:S(2)}) collective-permute-start(bf16[1,192,768]{2,1,0:T(8,128)(2,1)S(1)} %shard_map.64.refs_4_), channel_id=1, source_target_pairs={{0,2},{2,0},{4,6},{6,4},{8,10},{10,8},{12,14},{14,12},{16,18},{18,... | collective-permute-start | bytes 884744 | tf_op jit(solution)/shard_map/ppermute | solution.py:17
  59.0 43.5 %collective-permute-start.4 = (bf16[2,192,384]{2,1,0:T(8,128)(2,1)S(1)}, bf16[2,192,384]{2,1,0:T(8,128)(2,1)S(1)}, u32[]{:S(2)}, u32[]{:S(2)}) collective-permute-start(bf16[2,192,384]{2,1,0:T(8,128)(2,1)S(1)} %shard_map.58), channel_id=1, source_target_pairs={{0,24},{2,26},{4,28},{6,30},{8,16},{10,18},{12,20},{14,22},{16,8},... | collective-permute-start | bytes 884744 | tf_op jit(solution)/shard_map/ppermute | solution.py:17
  68.0 36.7 %collective-permute-start.3 = (bf16[2,192,384]{2,1,0:T(8,128)(2,1)S(1)}, bf16[2,192,384]{2,1,0:T(8,128)(2,1)S(1)}, u32[]{:S(2)}, u32[]{:S(2)}) collective-permute-start(bf16[2,192,384]{2,1,0:T(8,128)(2,1)S(1)} %shard_map.57), channel_id=1, source_target_pairs={{0,16},{2,18},{4,20},{6,22},{8,24},{10,26},{12,28},{14,30},{16,0},... | collective-permute-start | bytes 884744 | tf_op jit(solution)/shard_map/ppermute | solution.py:17
  73.1 35.2 %collective-permute-start.2 = (bf16[2,192,384]{2,1,0:T(8,128)(2,1)S(1)}, bf16[2,192,384]{2,1,0:T(8,128)(2,1)S(1)}, u32[]{:S(2)}, u32[]{:S(2)}) collective-permute-start(bf16[2,192,384]{2,1,0:T(8,128)(2,1)S(1)} %shard_map.56), channel_id=1, source_target_pairs={{0,8},{2,10},{4,12},{6,14},{8,0},{10,2},{12,4},{14,6},{16,24},{18,... | collective-permute-start | bytes 884744 | tf_op jit(solution)/shard_map/ppermute | solution.py:17
  103.2 22.6 %collective-permute-start.26 = (bf16[1,192,768]{2,1,0:T(8,128)(2,1)S(1)}, bf16[1,192,768]{2,1,0:T(8,128)(2,1)S(1)}, u32[]{:S(2)}, u32[]{:S(2)}) collective-permute-start(bf16[1,192,768]{2,1,0:T(8,128)(2,1)S(1)} %shard_map.65), channel_id=1, source_target_pairs={{0,8},{2,10},{4,12},{6,14},{8,0},{10,2},{12,4},{14,6},{16,24},{18,... | collective-permute-start | bytes 884744 | tf_op jit(solution)/shard_map/ppermute | solution.py:17
  105.4 23.4 %collective-permute-start.30 = (bf16[1,192,768]{2,1,0:T(8,128)(2,1)S(1)}, bf16[1,192,768]{2,1,0:T(8,128)(2,1)S(1)}, u32[]{:S(2)}, u32[]{:S(2)}) collective-permute-start(bf16[1,192,768]{2,1,0:T(8,128)(2,1)S(1)} %shard_map.66), channel_id=1, source_target_pairs={{0,16},{2,18},{4,20},{6,22},{8,24},{10,26},{12,28},{14,30},{16,0},... | collective-permute-start | bytes 884744 | tf_op jit(solution)/shard_map/ppermute | solution.py:17
  108.3 21.9 %collective-permute-start.34 = (bf16[1,192,768]{2,1,0:T(8,128)(2,1)S(1)}, bf16[1,192,768]{2,1,0:T(8,128)(2,1)}, u32[]{:S(2)}, u32[]{:S(2)}) collective-permute-start(bf16[1,192,768]{2,1,0:T(8,128)(2,1)S(1)} %shard_map.67), channel_id=1, source_target_pairs={{0,24},{2,26},{4,28},{6,30},{8,16},{10,18},{12,20},{14,22},{16,8},... | collective-permute-start | bytes 884744 | tf_op jit(solution)/shard_map/ppermute | solution.py:17
  120.0 49.1 %copy-start.34 = (u32[32]{0:T(128)S(1)}, u32[32]{0:T(128)}, u32[]{:S(2)}) copy-start(u32[32]{0:T(128)} %constant.37) | copy-start | bytes 388
  120.0 50.3 %copy-start.33 = (s32[2,192]{1,0:T(2,128)S(1)}, s32[2,192]{1,0:T(2,128)}, u32[]{:S(2)}) copy-start(s32[2,192]{1,0:T(2,128)} %param.9) | copy-start | bytes 4612
  125.8 9.8 %collective-permute-start.8 = (bf16[1,192,768]{2,1,0:T(8,128)(2,1)S(1)}, bf16[1,192,768]{2,1,0:T(8,128)(2,1)}, u32[]{:S(2)}, u32[]{:S(2)}) collective-permute-start(bf16[1,192,768]{2,1,0:T(8,128)(2,1)S(1)} %shard_map.60), channel_id=1, source_target_pairs={{0,8},{2,10},{4,12},{6,14},{8,0},{10,2},{12,4},{14,6},{16,24},{18,... | collective-permute-start | bytes 884744 | tf_op jit(solution)/shard_map/ppermute | solution.py:17
  128.8 25.4 %collective-permute-start.12 = (bf16[1,192,768]{2,1,0:T(8,128)(2,1)S(1)}, bf16[1,192,768]{2,1,0:T(8,128)(2,1)}, u32[]{:S(2)}, u32[]{:S(2)}) collective-permute-start(bf16[1,192,768]{2,1,0:T(8,128)(2,1)S(1)} %shard_map.61), channel_id=1, source_target_pairs={{0,16},{2,18},{4,20},{6,22},{8,24},{10,26},{12,28},{14,30},{16,0},... | collective-permute-start | bytes 884744 | tf_op jit(solution)/shard_map/ppermute | solution.py:17
  130.3 25.4 %collective-permute-start.16 = (bf16[1,192,768]{2,1,0:T(8,128)(2,1)S(1)}, bf16[1,192,768]{2,1,0:T(8,128)(2,1)}, u32[]{:S(2)}, u32[]{:S(2)}) collective-permute-start(bf16[1,192,768]{2,1,0:T(8,128)(2,1)S(1)} %shard_map.62), channel_id=1, source_target_pairs={{0,24},{2,26},{4,28},{6,30},{8,16},{10,18},{12,20},{14,22},{16,8},... | collective-permute-start | bytes 884744 | tf_op jit(solution)/shard_map/ppermute | solution.py:17
  130.8 25.5 %collective-permute-start.6 = (bf16[1,192,768]{2,1,0:T(8,128)(2,1)S(1)}, bf16[1,192,768]{2,1,0:T(8,128)(2,1)S(1)}, u32[]{:S(2)}, u32[]{:S(2)}) collective-permute-start(bf16[1,192,768]{2,1,0:T(8,128)(2,1)S(1)} %shard_map.59.refs_4_), channel_id=1, source_target_pairs={{0,4},{2,6},{4,0},{6,2},{8,12},{10,14},{12,8},{14,10},{16,20},{18,... | collective-permute-start | bytes 884744 | tf_op jit(solution)/shard_map/ppermute | solution.py:17
  133.0 24.0 %collective-permute-start.5 = (bf16[1,192,768]{2,1,0:T(8,128)(2,1)S(1)}, bf16[1,192,768]{2,1,0:T(8,128)(2,1)S(1)}, u32[]{:S(2)}, u32[]{:S(2)}) collective-permute-start(bf16[1,192,768]{2,1,0:T(8,128)(2,1)S(1)} %shard_map.59.refs_4_), channel_id=1, source_target_pairs={{0,2},{2,0},{4,6},{6,4},{8,10},{10,8},{12,14},{14,12},{16,18},{18,... | collective-permute-start | bytes 884744 | tf_op jit(solution)/shard_map/ppermute | solution.py:17
  135.6 23.3 %collective-permute-start.28 = (bf16[1,192,768]{2,1,0:T(8,128)(2,1)S(1)}, bf16[1,192,768]{2,1,0:T(8,128)(2,1)S(1)}, u32[]{:S(2)}, u32[]{:S(2)}) collective-permute-start(bf16[1,192,768]{2,1,0:T(8,128)(2,1)S(1)} %collective-permute-done.26.refs_8_), channel_id=1, source_target_pairs={{0,4},{2,6},{4,0},{6,2},{8,12},{10,14},{12,8},{14,10},{16,20},{18,... | collective-permute-start | bytes 884744 | tf_op jit(solution)/shard_map/ppermute | solution.py:17
  154.2 6.7 %collective-permute-start.32 = (bf16[1,192,768]{2,1,0:T(8,128)(2,1)S(1)}, bf16[1,192,768]{2,1,0:T(8,128)(2,1)S(1)}, u32[]{:S(2)}, u32[]{:S(2)}) collective-permute-start(bf16[1,192,768]{2,1,0:T(8,128)(2,1)S(1)} %collective-permute-done.30.refs_12_), channel_id=1, source_target_pairs={{0,4},{2,6},{4,0},{6,2},{8,12},{10,14},{12,8},{14,10},{16,20},{18,... | collective-permute-start | bytes 884744 | tf_op jit(solution)/shard_map/ppermute | solution.py:17
  155.7 8.4 %collective-permute-start.36 = (bf16[1,192,768]{2,1,0:T(8,128)(2,1)}, bf16[1,192,768]{2,1,0:T(8,128)(2,1)S(1)}, u32[]{:S(2)}, u32[]{:S(2)}) collective-permute-start(bf16[1,192,768]{2,1,0:T(8,128)(2,1)} %collective-permute-done.34.refs_16_), channel_id=1, source_target_pairs={{0,4},{2,6},{4,0},{6,2},{8,12},{10,14},{12,8},{14,10},{16,20},{18,... | collective-permute-start | bytes 884744 | tf_op jit(solution)/shard_map/ppermute | solution.py:17
  156.2 9.4 %collective-permute-start.27 = (bf16[1,192,768]{2,1,0:T(8,128)(2,1)S(1)}, bf16[1,192,768]{2,1,0:T(8,128)(2,1)S(1)}, u32[]{:S(2)}, u32[]{:S(2)}) collective-permute-start(bf16[1,192,768]{2,1,0:T(8,128)(2,1)S(1)} %collective-permute-done.26.refs_8_), channel_id=1, source_target_pairs={{0,2},{2,0},{4,6},{6,4},{8,10},{10,8},{12,14},{14,12},{16,18},{18,... | collective-permute-start | bytes 884744 | tf_op jit(solution)/shard_map/ppermute | solution.py:17
  157.8 9.1 %collective-permute-start.31 = (bf16[1,192,768]{2,1,0:T(8,128)(2,1)S(1)}, bf16[1,192,768]{2,1,0:T(8,128)(2,1)S(1)}, u32[]{:S(2)}, u32[]{:S(2)}) collective-permute-start(bf16[1,192,768]{2,1,0:T(8,128)(2,1)S(1)} %collective-permute-done.30.refs_12_), channel_id=1, source_target_pairs={{0,2},{2,0},{4,6},{6,4},{8,10},{10,8},{12,14},{14,12},{16,18},{18,... | collective-permute-start | bytes 884744 | tf_op jit(solution)/shard_map/ppermute | solution.py:17
  158.9 7.9 %copy-start.22 = (bf16[1,192,768]{2,1,0:T(8,128)(2,1)}, bf16[1,192,768]{2,1,0:T(8,128)(2,1)S(1)}, u32[]{:S(2)}) copy-start(bf16[1,192,768]{2,1,0:T(8,128)(2,1)S(1)} %collective-permute-done.28.refs_10_) | copy-start | bytes 884740
  158.9 11.6 %collective-permute-start.35 = (bf16[1,192,768]{2,1,0:T(8,128)(2,1)}, bf16[1,192,768]{2,1,0:T(8,128)(2,1)}, u32[]{:S(2)}, u32[]{:S(2)}) collective-permute-start(bf16[1,192,768]{2,1,0:T(8,128)(2,1)} %collective-permute-done.34.refs_16_), channel_id=1, source_target_pairs={{0,2},{2,0},{4,6},{6,4},{8,10},{10,8},{12,14},{14,12},{16,18},{18,... | collective-permute-start | bytes 884744 | tf_op jit(solution)/shard_map/ppermute | solution.py:17
  160.9 8.2 %copy-start.24 = (bf16[1,192,768]{2,1,0:T(8,128)(2,1)}, bf16[1,192,768]{2,1,0:T(8,128)(2,1)S(1)}, u32[]{:S(2)}) copy-start(bf16[1,192,768]{2,1,0:T(8,128)(2,1)S(1)} %collective-permute-done.32.refs_14_) | copy-start | bytes 884740
  160.9 9.6 %collective-permute-start.25 = (bf16[1,192,768]{2,1,0:T(8,128)(2,1)}, bf16[1,192,768]{2,1,0:T(8,128)(2,1)}, u32[]{:S(2)}, u32[]{:S(2)}) collective-permute-start(bf16[1,192,768]{2,1,0:T(8,128)(2,1)} %collective-permute-done.24.refs_6_), channel_id=1, source_target_pairs={{0,2},{2,0},{4,6},{6,4},{8,10},{10,8},{12,14},{14,12},{16,18},{18,... | collective-permute-start | bytes 884744 | tf_op jit(solution)/shard_map/ppermute | solution.py:17
  164.1 10.3 %collective-permute-start.10 = (bf16[1,192,768]{2,1,0:T(8,128)(2,1)}, bf16[1,192,768]{2,1,0:T(8,128)(2,1)}, u32[]{:S(2)}, u32[]{:S(2)}) collective-permute-start(bf16[1,192,768]{2,1,0:T(8,128)(2,1)} %collective-permute-done.8.refs_8_), channel_id=1, source_target_pairs={{0,4},{2,6},{4,0},{6,2},{8,12},{10,14},{12,8},{14,10},{16,20},{18,... | collective-permute-start | bytes 884744 | tf_op jit(solution)/shard_map/ppermute | solution.py:17
  166.3 13.8 %collective-permute-start.14 = (bf16[1,192,768]{2,1,0:T(8,128)(2,1)}, bf16[1,192,768]{2,1,0:T(8,128)(2,1)}, u32[]{:S(2)}, u32[]{:S(2)}) collective-permute-start(bf16[1,192,768]{2,1,0:T(8,128)(2,1)} %collective-permute-done.12.refs_12_), channel_id=1, source_target_pairs={{0,4},{2,6},{4,0},{6,2},{8,12},{10,14},{12,8},{14,10},{16,20},{18,... | collective-permute-start | bytes 884744 | tf_op jit(solution)/shard_map/ppermute | solution.py:17
  167.6 15.7 %collective-permute-start.18 = (bf16[1,192,768]{2,1,0:T(8,128)(2,1)}, bf16[1,192,768]{2,1,0:T(8,128)(2,1)}, u32[]{:S(2)}, u32[]{:S(2)}) collective-permute-start(bf16[1,192,768]{2,1,0:T(8,128)(2,1)} %collective-permute-done.16.refs_16_), channel_id=1, source_target_pairs={{0,4},{2,6},{4,0},{6,2},{8,12},{10,14},{12,8},{14,10},{16,20},{18,... | collective-permute-start | bytes 884744 | tf_op jit(solution)/shard_map/ppermute | solution.py:17
  170.5 32.8 %collective-permute-start.13 = (bf16[1,192,768]{2,1,0:T(8,128)(2,1)}, bf16[1,192,768]{2,1,0:T(8,128)(2,1)}, u32[]{:S(2)}, u32[]{:S(2)}) collective-permute-start(bf16[1,192,768]{2,1,0:T(8,128)(2,1)} %collective-permute-done.12.refs_12_), channel_id=1, source_target_pairs={{0,2},{2,0},{4,6},{6,4},{8,10},{10,8},{12,14},{14,12},{16,18},{18,... | collective-permute-start | bytes 884744 | tf_op jit(solution)/shard_map/ppermute | solution.py:17
  170.6 32.7 %collective-permute-start.17 = (bf16[1,192,768]{2,1,0:T(8,128)(2,1)}, bf16[1,192,768]{2,1,0:T(8,128)(2,1)}, u32[]{:S(2)}, u32[]{:S(2)}) collective-permute-start(bf16[1,192,768]{2,1,0:T(8,128)(2,1)} %collective-permute-done.16.refs_16_), channel_id=1, source_target_pairs={{0,2},{2,0},{4,6},{6,4},{8,10},{10,8},{12,14},{14,12},{16,18},{18,... | collective-permute-start | bytes 884744 | tf_op jit(solution)/shard_map/ppermute | solution.py:17
  174.3 29.4 %collective-permute-start.29 = (bf16[1,192,768]{2,1,0:T(8,128)(2,1)}, bf16[1,192,768]{2,1,0:T(8,128)(2,1)}, u32[]{:S(2)}, u32[]{:S(2)}) collective-permute-start(bf16[1,192,768]{2,1,0:T(8,128)(2,1)} %copy-done.22), channel_id=1, source_target_pairs={{0,2},{2,0},{4,6},{6,4},{8,10},{10,8},{12,14},{14,12},{16,18},{18,... | collective-permute-start | bytes 884744 | tf_op jit(solution)/shard_map/ppermute | solution.py:17
  180.2 23.7 %collective-permute-start.33 = (bf16[1,192,768]{2,1,0:T(8,128)(2,1)}, bf16[1,192,768]{2,1,0:T(8,128)(2,1)}, u32[]{:S(2)}, u32[]{:S(2)}) collective-permute-start(bf16[1,192,768]{2,1,0:T(8,128)(2,1)} %copy-done.24), channel_id=1, source_target_pairs={{0,2},{2,0},{4,6},{6,4},{8,10},{10,8},{12,14},{14,12},{16,18},{18,... | collective-permute-start | bytes 884744 | tf_op jit(solution)/shard_map/ppermute | solution.py:17
  183.3 21.0 %collective-permute-start.37 = (bf16[1,192,768]{2,1,0:T(8,128)(2,1)}, bf16[1,192,768]{2,1,0:T(8,128)(2,1)}, u32[]{:S(2)}, u32[]{:S(2)}) collective-permute-start(bf16[1,192,768]{2,1,0:T(8,128)(2,1)} %copy-done.26), channel_id=1, source_target_pairs={{0,2},{2,0},{4,6},{6,4},{8,10},{10,8},{12,14},{14,12},{16,18},{18,... | collective-permute-start | bytes 884744 | tf_op jit(solution)/shard_map/ppermute | solution.py:17
  203.3 33.7 %collective-permute-start.9 = (bf16[1,192,768]{2,1,0:T(8,128)(2,1)}, bf16[1,192,768]{2,1,0:T(8,128)(2,1)S(1)}, u32[]{:S(2)}, u32[]{:S(2)}) collective-permute-start(bf16[1,192,768]{2,1,0:T(8,128)(2,1)} %collective-permute-done.8.refs_8_), channel_id=1, source_target_pairs={{0,2},{2,0},{4,6},{6,4},{8,10},{10,8},{12,14},{14,12},{16,18},{18,... | collective-permute-start | bytes 884744 | tf_op jit(solution)/shard_map/ppermute | solution.py:17
  203.3 36.5 %collective-permute-start.7 = (bf16[1,192,768]{2,1,0:T(8,128)(2,1)}, bf16[1,192,768]{2,1,0:T(8,128)(2,1)S(1)}, u32[]{:S(2)}, u32[]{:S(2)}) collective-permute-start(bf16[1,192,768]{2,1,0:T(8,128)(2,1)} %copy-done.14), channel_id=1, source_target_pairs={{0,2},{2,0},{4,6},{6,4},{8,10},{10,8},{12,14},{14,12},{16,18},{18,... | collective-permute-start | bytes 884744 | tf_op jit(solution)/shard_map/ppermute | solution.py:17
  203.8 36.6 %collective-permute-start.11 = (bf16[1,192,768]{2,1,0:T(8,128)(2,1)}, bf16[1,192,768]{2,1,0:T(8,128)(2,1)S(1)}, u32[]{:S(2)}, u32[]{:S(2)}) collective-permute-start(bf16[1,192,768]{2,1,0:T(8,128)(2,1)} %collective-permute-done.10.refs_10_), channel_id=1, source_target_pairs={{0,2},{2,0},{4,6},{6,4},{8,10},{10,8},{12,14},{14,12},{16,18},{18,... | collective-permute-start | bytes 884744 | tf_op jit(solution)/shard_map/ppermute | solution.py:17
  203.9 38.4 %collective-permute-start.15 = (bf16[1,192,768]{2,1,0:T(8,128)(2,1)}, bf16[1,192,768]{2,1,0:T(8,128)(2,1)S(1)}, u32[]{:S(2)}, u32[]{:S(2)}) collective-permute-start(bf16[1,192,768]{2,1,0:T(8,128)(2,1)} %collective-permute-done.14.refs_14_), channel_id=1, source_target_pairs={{0,2},{2,0},{4,6},{6,4},{8,10},{10,8},{12,14},{14,12},{16,18},{18,... | collective-permute-start | bytes 884744 | tf_op jit(solution)/shard_map/ppermute | solution.py:17
  204.3 38.0 %collective-permute-start.19 = (bf16[1,192,768]{2,1,0:T(8,128)(2,1)}, bf16[1,192,768]{2,1,0:T(8,128)(2,1)S(1)}, u32[]{:S(2)}, u32[]{:S(2)}) collective-permute-start(bf16[1,192,768]{2,1,0:T(8,128)(2,1)} %collective-permute-done.18.refs_18_), channel_id=1, source_target_pairs={{0,2},{2,0},{4,6},{6,4},{8,10},{10,8},{12,14},{14,12},{16,18},{18,... | collective-permute-start | bytes 884744 | tf_op jit(solution)/shard_map/ppermute | solution.py:17
  209.9 33.1 %copy-start.15 = (bf16[1,192,768]{2,1,0:T(8,128)(2,1)S(1)}, bf16[1,192,768]{2,1,0:T(8,128)(2,1)}, u32[]{:S(2)}) copy-start(bf16[1,192,768]{2,1,0:T(8,128)(2,1)} %copy-done.14) | copy-start | bytes 884740
  209.9 33.0 %copy-start.19 = (bf16[1,192,768]{2,1,0:T(8,128)(2,1)S(1)}, bf16[1,192,768]{2,1,0:T(8,128)(2,1)}, u32[]{:S(2)}) copy-start(bf16[1,192,768]{2,1,0:T(8,128)(2,1)} %copy-done.18) | copy-start | bytes 884740
  237.0 29.2 %collective-permute-start.38 = (bf16[192,384]{1,0:T(8,128)(2,1)S(1)}, bf16[192,384]{1,0:T(8,128)(2,1)S(1)}, u32[]{:S(2)}, u32[]{:S(2)}) collective-permute-start(bf16[192,384]{1,0:T(8,128)(2,1)S(1)} %get-tuple-element.18), channel_id=1, source_target_pairs={{0,8},{2,10},{4,12},{6,14},{8,0},{10,2},{12,4},{14,6},{16,24},{18,... | collective-permute-start | bytes 442376 | tf_op jit(solution)/shard_map/ppermute | solution.py:17
  239.8 28.3 %collective-permute-start.39 = (bf16[192,384]{1,0:T(8,128)(2,1)S(1)}, bf16[192,384]{1,0:T(8,128)(2,1)S(1)}, u32[]{:S(2)}, u32[]{:S(2)}) collective-permute-start(bf16[192,384]{1,0:T(8,128)(2,1)S(1)} %get-tuple-element.19), channel_id=1, source_target_pairs={{0,16},{2,18},{4,20},{6,22},{8,24},{10,26},{12,28},{14,30},{16,0},... | collective-permute-start | bytes 442376 | tf_op jit(solution)/shard_map/ppermute | solution.py:17
  240.4 27.7 %collective-permute-start.40 = (bf16[192,384]{1,0:T(8,128)(2,1)S(1)}, bf16[192,384]{1,0:T(8,128)(2,1)S(1)}, u32[]{:S(2)}, u32[]{:S(2)}) collective-permute-start(bf16[192,384]{1,0:T(8,128)(2,1)S(1)} %get-tuple-element.20), channel_id=1, source_target_pairs={{0,24},{2,26},{4,28},{6,30},{8,16},{10,18},{12,20},{14,22},{16,8},... | collective-permute-start | bytes 442376 | tf_op jit(solution)/shard_map/ppermute | solution.py:17
  263.6 8.2 %collective-permute-start.20 = (bf16[192,384]{1,0:T(8,128)(2,1)S(1)}, bf16[192,384]{1,0:T(8,128)(2,1)S(1)}, u32[]{:S(2)}, u32[]{:S(2)}) collective-permute-start(bf16[192,384]{1,0:T(8,128)(2,1)S(1)} %get-tuple-element.14), channel_id=1, source_target_pairs={{0,8},{2,10},{4,12},{6,14},{8,0},{10,2},{12,4},{14,6},{16,24},{18,... | collective-permute-start | bytes 442376 | tf_op jit(solution)/shard_map/ppermute | solution.py:17
  264.7 13.8 %collective-permute-start.21 = (bf16[192,384]{1,0:T(8,128)(2,1)S(1)}, bf16[192,384]{1,0:T(8,128)(2,1)S(1)}, u32[]{:S(2)}, u32[]{:S(2)}) collective-permute-start(bf16[192,384]{1,0:T(8,128)(2,1)S(1)} %get-tuple-element.15), channel_id=1, source_target_pairs={{0,16},{2,18},{4,20},{6,22},{8,24},{10,26},{12,28},{14,30},{16,0},... | collective-permute-start | bytes 442376 | tf_op jit(solution)/shard_map/ppermute | solution.py:17
  266.2 12.3 %collective-permute-start.22 = (bf16[192,384]{1,0:T(8,128)(2,1)S(1)}, bf16[192,384]{1,0:T(8,128)(2,1)S(1)}, u32[]{:S(2)}, u32[]{:S(2)}) collective-permute-start(bf16[192,384]{1,0:T(8,128)(2,1)S(1)} %get-tuple-element.16), channel_id=1, source_target_pairs={{0,24},{2,26},{4,28},{6,30},{8,16},{10,18},{12,20},{14,22},{16,8},... | collective-permute-start | bytes 442376 | tf_op jit(solution)/shard_map/ppermute | solution.py:17
  (28 other events, 102.6 us)

commit v2 on v1

v2 whole, which is shorter than its diff:
```python
import functools
import math

import jax
import jax.numpy as jnp
from jax import lax
from jax.experimental import pallas as pl
from jax.experimental.pallas import tpu as pltpu
from jax.sharding import PartitionSpec as P

HD = 128
LOG2_E = 1.4426950408889634
HIDDEN = -1e30
VMEM_LIMIT = 56 * 2**20


def exchange(value, axis, size, bit):
    return lax.ppermute(value, axis, [(i, i ^ bit) for i in range(size)])


def own_body(weights, *refs):
    hidden_ref = refs[0]
    sequences, rows, feats = hidden_ref.shape
    flat = hidden_ref[...].reshape(sequences * rows, feats)
    for weight_ref, out_ref in zip(refs[1 : 1 + weights], refs[1 + weights :]):
        result = jnp.dot(flat, weight_ref[...], preferred_element_type=jnp.float32)
        out_ref[0] = result.reshape(sequences, rows, -1)


def own_products(hidden_in, weights, place, ways):
    sequences, rows, feats = hidden_in.shape
    width = weights[0].shape[1] // ways

    def body(place, *refs):
        own_body(len(weights), *refs)

    return pl.pallas_call(
        body,
        out_shape=[jax.ShapeDtypeStruct((ways, sequences, rows, width), jnp.float32)] * len(weights),
        grid_spec=pltpu.PrefetchScalarGridSpec(
            num_scalar_prefetch=1,
            grid=(ways,),
            in_specs=[pl.BlockSpec((sequences, rows, feats), lambda g, place: (0, 0, 0))]
            + [pl.BlockSpec((feats, width), lambda g, place: (place[0], g))] * len(weights),
            out_specs=[pl.BlockSpec((1, sequences, rows, width), lambda g, place: (g, 0, 0, 0))]
            * len(weights),
        ),
        compiler_params=pltpu.CompilerParams(vmem_limit_bytes=VMEM_LIMIT),
        cost_estimate=pl.CostEstimate(
            flops=2 * sequences * rows * feats * width * ways * len(weights),
            bytes_accessed=2 * feats * width * ways * len(weights),
            transcendentals=0,
        ),
    )(place, hidden_in, *weights)


def rest_body(shares, weights, sequences, place, *refs):
    inputs = refs[: shares * sequences]
    weight_refs = refs[shares * sequences : shares * sequences + weights]
    start_refs = refs[shares * sequences + weights : shares * sequences + 2 * weights]
    out_ref = refs[shares * sequences + 2 * weights]
    totals = refs[shares * sequences + 2 * weights + 1 :]
    rows, width = out_ref.shape[2:]
    width //= weights
    step = pl.program_id(1)
    for share in range(shares):

        @pl.when(step == share)
        def _():
            flat = [inputs[s * shares + share][...] for s in range(sequences)]
            flat = flat[0] if sequences == 1 else jnp.concatenate(flat, axis=0)
            for n in range(weights):
                before = start_refs[n][0].reshape(sequences * rows, width) if share == 0 else totals[n][...]
                after = before + jnp.dot(flat, weight_refs[n][...], preferred_element_type=jnp.float32)
                if share < shares - 1:
                    totals[n][...] = after
                else:
                    after = after.astype(out_ref.dtype).reshape(sequences, rows, width)
                    out_ref[0, :, :, n * width : (n + 1) * width] = after


def rest_products(received, chosen, weights, starts, place, ways):
    shares = len(received[0])
    rows, feats = received[0][0].shape
    width = weights[0].shape[1] // ways
    sequences = len(chosen)
    first = chosen[0]
    in_specs = [pl.BlockSpec((rows, feats), lambda g, p, place: (0, 0))] * (shares * sequences)
    in_specs += [pl.BlockSpec((feats, width), lambda g, p, place: (place[0] ^ (p + 1), g))] * len(weights)
    in_specs += [
        pl.BlockSpec((1, sequences, rows, width), lambda g, p, place: (g, first // sequences, 0, 0))
    ] * len(weights)
    columns = width * len(weights)
    return pl.pallas_call(
        functools.partial(rest_body, shares, len(weights), sequences),
        out_shape=jax.ShapeDtypeStruct((ways, sequences, rows, columns), jnp.bfloat16),
        grid_spec=pltpu.PrefetchScalarGridSpec(
            num_scalar_prefetch=1,
            grid=(ways, shares),
            in_specs=in_specs,
            out_specs=pl.BlockSpec((1, sequences, rows, columns), lambda g, p, place: (g, 0, 0, 0)),
            scratch_shapes=[pltpu.VMEM((sequences * rows, width), jnp.float32)] * len(weights),
        ),
        compiler_params=pltpu.CompilerParams(vmem_limit_bytes=VMEM_LIMIT),
        cost_estimate=pl.CostEstimate(
            flops=2 * sequences * rows * feats * shares * columns * ways,
            bytes_accessed=2 * feats * shares * columns * ways,
            transcendentals=0,
        ),
    )(place, *[share for s in chosen for share in received[s]], *weights, *starts)


def attend_body(seq, ways, blocks, spans, tile, table, place, *refs):
    query_ref, blocks_ref, out_ref = refs[:3]
    ordered, scores, highest, sums, total, offsets, sems = refs[3:]
    rows, width = out_ref.shape[1:]
    half = rows // 2
    heads = width // HD
    rest = blocks // ways
    me = place[0]

    def span_of(device):
        return table[me ^ device, seq]

    copies = []
    for slot in range(blocks):
        low = span_of(slot % ways * rest + slot // ways)
        for part, span in ((0, low), (1, spans - 1 - low)):
            copies.append(
                pltpu.make_async_copy(
                    blocks_ref.at[slot, pl.ds(part * half, half)],
                    ordered.at[pl.ds(pl.multiple_of(span * half, 16), half)],
                    sems.at[2 * slot + part],
                )
            )
    for copy in copies:
        copy.start()
    for copy in copies:
        copy.wait()

    per_tile = tile // half
    slope = LOG2_E / math.sqrt(HD)
    row = lax.broadcasted_iota(jnp.int32, (rows, tile), 0)
    lane = lax.broadcasted_iota(jnp.int32, (rows, tile), 1)

    def score_step(first, a, t, carry):
        start = pl.multiple_of(t * tile, 128)
        visible = offsets[first:] >= start
        for h in range(heads):
            part = lax.dot_general(
                query_ref[a, 0, first:, h * HD : (h + 1) * HD],
                ordered[pl.ds(start, tile), h * HD : (h + 1) * HD],
                (((1,), (1,)), ((), ())),
                preferred_element_type=jnp.float32,
            )
            part = jnp.where(visible, part, HIDDEN)
            scores[h, first:, pl.ds(start, tile)] = part
            top = highest[h, first:]
            for j in range(tile // 128):
                top = jnp.maximum(top, part[:, j * 128 : (j + 1) * 128])
            highest[h, first:] = top
        return carry

    def value_step(first, tops, t, carry):
        start = pl.multiple_of(t * tile, 128)
        for h in range(heads):
            part = scores[h, first:, pl.ds(start, tile)]
            weight = jnp.exp2((part - tops[h][first:]) * slope)
            added = sums[h, first:]
            for j in range(tile // 128):
                added = added + weight[:, j * 128 : (j + 1) * 128]
            sums[h, first:] = added
            total[h, first:] += jnp.dot(
                weight.astype(jnp.bfloat16),
                ordered[pl.ds(start, tile), width + h * HD : width + (h + 1) * HD],
                preferred_element_type=jnp.float32,
            )
        return carry

    for a in range(ways):
        low = span_of(a * rest + me % rest)
        high = spans - 1 - low
        offsets[...] = jnp.where(row < half, low * half + row, high * half + row - half) - lane
        highest[...] = jnp.full_like(highest, HIDDEN)
        sums[...] = jnp.zeros_like(sums)
        total[...] = jnp.zeros_like(total)
        both = (low + per_tile) // per_tile
        upto = (high + per_tile) // per_tile
        lax.fori_loop(0, both, functools.partial(score_step, 0, a), 0)
        lax.fori_loop(both, upto, functools.partial(score_step, half, a), 0)
        tops = [jnp.max(highest[h], axis=1, keepdims=True) for h in range(heads)]
        lax.fori_loop(0, both, functools.partial(value_step, 0, tops), 0)
        lax.fori_loop(both, upto, functools.partial(value_step, half, tops), 0)
        for h in range(heads):
            denom = jnp.sum(sums[h], axis=1, keepdims=True)
            out_ref[a, :, h * HD : (h + 1) * HD] = (total[h] / denom).astype(jnp.bfloat16)


def attend(seq, queries, blocks, table, me):
    ways, _, rows, width = queries.shape
    count = blocks.shape[0]
    spans = 2 * count
    half = rows // 2
    length = count * rows
    tile = 4 * half
    heads = width // HD
    smem = pl.BlockSpec(memory_space=pltpu.SMEM)
    flops = ways * heads * (spans + 3) * half * half * HD * 4
    return pl.pallas_call(
        functools.partial(attend_body, seq, ways, count, spans, tile),
        out_shape=jax.ShapeDtypeStruct((ways, rows, width), jnp.bfloat16),
        grid=(1,),
        in_specs=[
            smem,
            smem,
            pl.BlockSpec((ways, 1, rows, width), lambda i: (0, seq, 0, 0)),
            pl.BlockSpec(memory_space=pl.ANY),
        ],
        out_specs=pl.BlockSpec((ways, rows, width), lambda i: (0, 0, 0)),
        scratch_shapes=[
            pltpu.VMEM((length, 2 * width), jnp.bfloat16),
            pltpu.VMEM((heads, rows, length), jnp.float32),
            pltpu.VMEM((heads, rows, 128), jnp.float32),
            pltpu.VMEM((heads, rows, 128), jnp.float32),
            pltpu.VMEM((heads, rows, HD), jnp.float32),
            pltpu.VMEM((rows, tile), jnp.int32),
            pltpu.SemaphoreType.DMA((2 * count,)),
        ],
        compiler_params=pltpu.CompilerParams(vmem_limit_bytes=VMEM_LIMIT),
        cost_estimate=pl.CostEstimate(
            flops=flops,
            bytes_accessed=4 * length * width + 4 * ways * rows * width,
            transcendentals=flops // (4 * HD),
        ),
    )(table, me, queries, blocks)


def assemble_body(*refs):
    out_ref = refs[-1]
    for s, ref in enumerate(refs[:-1]):
        out_ref[s] = ref[0]


def assemble(pieces):
    ways, rows, width = pieces[0].shape
    sequences = len(pieces)
    return pl.pallas_call(
        assemble_body,
        out_shape=jax.ShapeDtypeStruct((sequences, rows, ways * width), jnp.bfloat16),
        grid=(ways,),
        in_specs=[pl.BlockSpec((1, rows, width), lambda g: (g, 0, 0))] * sequences,
        out_specs=pl.BlockSpec((sequences, rows, width), lambda g: (0, 0, g)),
        compiler_params=pltpu.CompilerParams(vmem_limit_bytes=VMEM_LIMIT),
    )(*pieces)


def on_device(ctx_size, tp_size, hidden_in, w_q, w_k, w_v, event_pos):
    sequences, rows, _ = hidden_in.shape
    features = w_q.shape[1]
    ways = math.gcd(features // HD, ctx_size)
    rest = ctx_size // ways
    ctx_me = lax.axis_index("ctx").astype(jnp.int32)
    tp_me = lax.axis_index("tp").astype(jnp.int32)
    across = [[a * rest + j for a in range(ways)] for j in range(rest)]
    along = [[a * rest + j for j in range(rest)] for a in range(ways)]

    received = []
    for s in range(sequences):
        shares = [hidden_in[s]]
        bit = 1
        while bit < tp_size:
            shares += [exchange(share, "tp", tp_size, bit) for share in shares]
            bit *= 2
        received.append(shares[1:])

    table = event_pos[None, :, 0] // (rows // 2)
    bit = 1
    while bit < ctx_size:
        table = jnp.concatenate([table, exchange(table, "ctx", ctx_size, bit)], axis=0)
        bit *= 2

    def swap_groups(value):
        if ways == 1:
            return value
        return lax.all_to_all(value, "ctx", 0, 0, axis_index_groups=across, tiled=True)

    place = tp_me.reshape(1)
    start_k, start_v, start_q = own_products(hidden_in, [w_k, w_v, w_q], place, ways)
    place = jnp.concatenate([place, table.reshape(-1)])
    blocks = []
    for s in range(sequences):
        made = rest_products(received, [s], [w_k, w_v], [start_k, start_v], place, ways)
        blocks.append(swap_groups(made.reshape(ways, rows, -1)))
    made = rest_products(received, list(range(sequences)), [w_q], [start_q], place, ways)
    queries = swap_groups(made)
    pieces = []
    for s in range(sequences):
        gathered = lax.all_gather(blocks[s], "ctx", axis=0, axis_index_groups=along, tiled=True)
        outs = attend(s, queries, gathered, table, ctx_me.reshape(1))
        pieces.append(swap_groups(outs))
    return assemble(pieces)


def solution(mesh):
    sizes = dict(mesh.shape)
    placed = (P(None, "ctx", "tp"), P(None, "tp"), P(None, "tp"), P(None, "tp"), P(None, "ctx"))
    return jax.shard_map(
        functools.partial(on_device, sizes["ctx"], sizes["tp"]),
        mesh=mesh,
        in_specs=placed,
        out_specs=P(None, "ctx", "tp"),
        check_vma=False,
    )
```

time: 282 us -> 266 us (0.943)
  blocking collectives: 19.7 us -> 80.9 us
  local copies, waits for them, and re-layouts: 33.3 us -> 4.65 us
  waiting for transfers between devices: 77.5 us -> 53.3 us
  starting transfers between devices: 37.3 us -> 16.3 us
  Pallas kernels: 111 us -> 94.1 us
  between operations: 1.06 us -> 13.5 us
    all_to_all x0 -> x3, blocking collectives: none -> 80.9 us  [swap_groups(): lax.all_to_all(value, 'ctx', 0, 0, axis_index_groups=across, tiled=True)]
    ppermute x41 -> x6, waiting for transfers between devices: 77.5 us -> 25.9 us  [exchange(): return lax.ppermute(value, axis, [(i, i ^ bit) for i in range(size)])]
    ppermute x41 -> x6, starting transfers between devices: 37.3 us -> 9.27 us  [exchange(): return lax.ppermute(value, axis, [(i, i ^ bit) for i in range(size)])]
    unnamed x72 -> x10, local copies, waits for them, and re-layouts: 30.7 us -> 2.92 us
    all_to_all x0 -> x2, waiting for transfers between devices: none -> 27.3 us  [swap_groups(): lax.all_to_all(value, 'ctx', 0, 0, axis_index_groups=across, tiled=True)]
    unnamed x1 -> x0, blocking collectives: 19.7 us -> none
    pallas_call x13 -> x5, Pallas kernels: 68.6 us -> 52.7 us  [the longest x3 31.6 us: rest_products(): pl.pallas_call(functools.partial(rest_body, shares, len(weights), sequenc...]
    all_to_all x0 -> x2, starting transfers between devices: none -> 7.02 us  [swap_groups(): lax.all_to_all(value, 'ctx', 0, 0, axis_index_groups=across, tiled=True)]
  transfers between devices with their start and end apart: 41 -> 10, of which waited for: 12 -> 4; matrix products, arithmetic and copies ran while one was open for 0% -> 1% of each run, Pallas kernels for 39% -> 30%
where the time goes in v2:
time: 266 us; the launch traced here: 265 us
  Pallas kernels  94.1 us (35%)
  blocking collectives  80.9 us (30%)
  waiting for transfers between devices  53.3 us (20%)
  starting transfers between devices  16.3 us (6%)
  between operations  13.5 us (5%)
  local copies, waits for them, and re-layouts  4.65 us (2%)
    all_to_all x3, blocking collectives, swap_groups(): lax.all_to_all(value, 'ctx', 0, 0, axis_index_groups=across, tiled=True)  80.9 us
    pallas_call x2, Pallas kernels, attend(): pl.pallas_call(functools.partial(attend_body, seq, ways, count, spans, ti...  41.3 us
    pallas_call x3, Pallas kernels, rest_products(): pl.pallas_call(functools.partial(rest_body, shares, len(weights), sequenc...  31.6 us
    all_to_all x2, waiting for transfers between devices, swap_groups(): lax.all_to_all(value, 'ctx', 0, 0, axis_index_groups=across, tiled=True)  27.3 us
    ppermute x6, waiting for transfers between devices, exchange(): return lax.ppermute(value, axis, [(i, i ^ bit) for i in range(size)])  25.9 us
    pallas_call x1, Pallas kernels, own_products(): pl.pallas_call(body, out_shape=[jax.ShapeDtypeStruct((ways, sequences, ro...  17.7 us
    ppermute x6, starting transfers between devices, exchange(): return lax.ppermute(value, axis, [(i, i ^ bit) for i in range(size)])  9.27 us
    all_to_all x2, starting transfers between devices, swap_groups(): lax.all_to_all(value, 'ctx', 0, 0, axis_index_groups=across, tiled=True)  7.02 us
  transfers between devices with their start and end apart: 10, of which 4 were waited for; matrix products, arithmetic and copies ran while one was open for 1% of the time, Pallas kernels for 30%

profile of v2, /device:TPU:0, one launch (start us, length us, event | category | flops | bytes accessed | tf_op | source)
XLA Modules:
  0.0 265.0 jit_solution(3756794076424536506)
XLA Ops:
  6.5 0.0 all-gather.5.cloned.1.call-start
  6.5 0.8 and_reduce_fusion
  7.3 0.8 divide_reduce_fusion
  8.1 0.5 collective-permute-start
  8.7 1.6 slice_bitcast_fusion
  10.3 2.6 collective-permute-start.5
  12.9 0.0 collective-permute-done
  12.9 1.6 collective-permute-start.1
  14.5 2.0 collective-permute-done.1
  16.5 1.6 collective-permute-start.2
  18.2 2.0 collective-permute-done.2
  20.2 2.7 %collective-permute-start.3 = (s32[8,2]{1,0:T(8,128)S(1)}, s32[8,2]{1,0:T(8,128)S(1)}, u32[]{:S(2)}, u32[]{:S(2)}) collective-permute-start(s32[8,2]{1,0:T(8,128)S(1)} %pad_add_fusion), channel_id=1, source_target_pairs={{0,16},{2,18},{4,20},{6,22},{8,24},{10,26},{12,28},{14,30},{16,0},... | collective-permute-start | bytes 200 | tf_op jit(solution)/shard_map/ppermute | solution.py:18
  22.8 17.7 %shard_map.55 = (f32[4,2,192,384]{3,2,1,0:T(8,128)}, f32[4,2,192,384]{3,2,1,0:T(8,128)}, f32[4,2,192,384]{3,2,1,0:T(8,128)}) custom-call(s32[1]{0:T(128)} %bitcast.1.place, bf16[2,192,2560]{2,1,0:T(8,128)(2,1)} %refs_0_.1, bf16[5120,1536]{1,0:T(8,128)(2,1)} %refs_1_.5, bf16[5120,1536]{1,0:T(8,128)(2,1)} %refs_2_.7, bf16[5120,1536]{1,0:T(8,128)(2,1)} %refs_2_.5), custom_call_target="tpu_custom_call" | custom-call | flops 9059696640 | bytes 23592960 | tf_op jit(solution)/shard_map/pallas_call | solution.py:37
  40.5 0.0 collective-permute-done.3
  40.6 0.0 copy-start.4
  40.6 0.1 reshape.84
  40.6 0.6 pad_add_fusion.3.place
  41.3 0.0 collective-permute-done.5.refs_1_.refs_0_
  41.3 0.0 copy-start
  41.3 0.9 copy-done
  42.2 11.0 %shard_map.59 = bf16[4,1,192,768]{3,2,1,0:T(8,128)(2,1)} custom-call(s32[33]{0:T(128)} %pad_add_fusion.3.place, bf16[192,2560]{1,0:T(8,128)(2,1)} %copy-done, bf16[5120,1536]{1,0:T(8,128)(2,1)} %refs_1_.5, bf16[5120,1536]{1,0:T(8,128)(2,1)} %refs_2_.7, f32[4,2,192,384]{3,2,1,0:T(8,128)} %get-tuple-element.9.refs_3_, f32[4,2,192,384]{3,2,1,0:T(8,128)} %get-tuple-element.10.refs_4_), custom_call_target="tpu_custom_call" | custom-call | flops 3019898880 | bytes 15728640 | tf_op jit(solution)/shard_map/pallas_call | solution.py:94
  53.2 0.0 copy-done.4
  53.2 31.5 %all_to_all.25 = bf16[4,192,768]{2,1,0:T(8,128)(2,1)} all-to-all(bf16[4,192,768]{2,1,0:T(8,128)(2,1)} %bitcast.13), channel_id=1, replica_groups={{0,8,16,24},{2,10,18,26},{4,12,20,28},{6,14,22,30},{1,9,17,25},{3,11,19..., dimensions={0} | all-to-all | bytes 2359296 | tf_op jit(solution)/shard_map/all_to_all | solution.py:285
  84.7 0.0 all-gather.5.cloned.1.call-update
  84.7 0.0 all-gather.3.cloned.1.call-start
  84.8 0.3 collective-permute-start.4
  85.1 21.9 %collective-permute-done.4.refs_0_ = bf16[192,2560]{1,0:T(8,128)(2,1)S(1)} collective-permute-done((bf16[192,2560]{1,0:T(8,128)(2,1)S(1)}, bf16[192,2560]{1,0:T(8,128)(2,1)S(1)}, u32[]{:S(2)}, u32[]{:S(2)}) %collective-permute-start.4) | collective-permute-done | bytes 983072 | tf_op jit(solution)/shard_map/ppermute | solution.py:18
  106.9 0.0 copy-start.1
  106.9 1.0 copy-done.1
  107.9 11.1 %shard_map.57 = bf16[4,1,192,768]{3,2,1,0:T(8,128)(2,1)} custom-call(s32[33]{0:T(128)} %pad_add_fusion.3.place, bf16[192,2560]{1,0:T(8,128)(2,1)} %copy-done.1, bf16[5120,1536]{1,0:T(8,128)(2,1)} %refs_1_.5, bf16[5120,1536]{1,0:T(8,128)(2,1)} %refs_2_.7, f32[4,2,192,384]{3,2,1,0:T(8,128)} %get-tuple-element.9.refs_3_, ...), custom_call_target="tpu_custom_call" | custom-call | flops 3019898880 | bytes 15728640 | tf_op jit(solution)/shard_map/pallas_call | solution.py:94
  119.0 30.9 %all_to_all.26 = bf16[4,192,768]{2,1,0:T(8,128)(2,1)} all-to-all(bf16[4,192,768]{2,1,0:T(8,128)(2,1)} %bitcast.12), channel_id=1, replica_groups={{0,8,16,24},{2,10,18,26},{4,12,20,28},{6,14,22,30},{1,9,17,25},{3,11,19..., dimensions={0} | all-to-all | bytes 2359296 | tf_op jit(solution)/shard_map/all_to_all | solution.py:285
  149.9 0.0 all-gather.3.cloned.1.call-update
  150.0 9.5 %shard_map.56 = bf16[4,2,192,384]{3,2,1,0:T(8,128)(2,1)} custom-call(s32[33]{0:T(128)} %pad_add_fusion.3.place, bf16[192,2560]{1,0:T(8,128)(2,1)} %copy-done.1, bf16[192,2560]{1,0:T(8,128)(2,1)} %copy-done, bf16[5120,1536]{1,0:T(8,128)(2,1)} %refs_2_.5, f32[4,2,192,384]{3,2,1,0:T(8,128)} %get-tuple-element.8.refs_3_), custom_call_target="tpu_custom_call" | custom-call | flops 3019898880 | bytes 7864320 | tf_op jit(solution)/shard_map/pallas_call | solution.py:94
  159.5 3.5 %all-to-all-start = ((bf16[4,2,192,384]{3,2,1,0:T(8,128)(2,1)}), bf16[4,2,192,384]{3,2,1,0:T(8,128)(2,1)S(1)}, u32[]{:S(2)}, u32[]{:S(2)}) async-start(bf16[4,2,192,384]{3,2,1,0:T(8,128)(2,1)} %shard_map.56), calls=%async_computation | async-start | bytes 2359296 | tf_op jit(solution)/shard_map/all_to_all | solution.py:285
  163.0 27.3 %all-to-all-done.refs_0_ = bf16[4,2,192,384]{3,2,1,0:T(8,128)(2,1)S(1)} async-done(((bf16[4,2,192,384]{3,2,1,0:T(8,128)(2,1)}), bf16[4,2,192,384]{3,2,1,0:T(8,128)(2,1)S(1)}, u32[]{:S(2)}, u32[]{:S(2)}) %all-to-all-start) | async-done | bytes 1179680 | tf_op jit(solution)/shard_map/all_to_all | solution.py:285
  190.3 0.0 copy-start.3
  190.3 0.0 all-gather.5.cloned.1.call-done.refs_1_
  190.3 1.0 copy-done.3
  191.3 20.9 %shard_map.60 = bf16[4,192,384]{2,1,0:T(8,128)(2,1)} custom-call(s32[16,2]{1,0:T(8,128)} %copy-done.4, s32[1]{0:T(128)} %bitcast.place, bf16[4,2,192,384]{3,2,1,0:T(8,128)(2,1)} %copy-done.3, bf16[16,192,768]{2,1,0:T(8,128)(2,1)} %all-gather.5.cloned.1.call-done.refs_1_), custom_call_target="tpu_custom_call" | custom-call | flops 1981808640 | bytes 5898240 | tf_op jit(solution)/shard_map/pallas_call | solution.py:209
  212.3 3.5 %all-to-all-start.4 = ((bf16[4,192,384]{2,1,0:T(8,128)(2,1)}), bf16[4,192,384]{2,1,0:T(8,128)(2,1)S(1)}, u32[]{:S(2)}, u32[]{:S(2)}) async-start(bf16[4,192,384]{2,1,0:T(8,128)(2,1)} %shard_map.60), calls=%async_computation.4 | async-start | bytes 1179648 | tf_op jit(solution)/shard_map/all_to_all | solution.py:285
  215.8 0.0 all-gather.3.cloned.1.call-done.refs_1_
  215.8 20.4 %shard_map.58 = bf16[4,192,384]{2,1,0:T(8,128)(2,1)} custom-call(s32[16,2]{1,0:T(8,128)} %copy-done.4, s32[1]{0:T(128)} %bitcast.place, bf16[4,2,192,384]{3,2,1,0:T(8,128)(2,1)} %copy-done.3, bf16[16,192,768]{2,1,0:T(8,128)(2,1)} %all-gather.3.cloned.1.call-done.refs_1_), custom_call_target="tpu_custom_call" | custom-call | flops 1981808640 | bytes 5898240 | tf_op jit(solution)/shard_map/pallas_call | solution.py:209
  236.2 0.0 all-to-all-done.4.refs_1_
  236.2 0.0 copy-start.2
  236.2 18.5 %all_to_all.27.refs_0_ = bf16[4,192,384]{2,1,0:T(8,128)(2,1)} all-to-all(bf16[4,192,384]{2,1,0:T(8,128)(2,1)} %shard_map.58), channel_id=1, replica_groups={{0,8,16,24},{2,10,18,26},{4,12,20,28},{6,14,22,30},{1,9,17,25},{3,11,19..., dimensions={0} | all-to-all | bytes 1179648 | tf_op jit(solution)/shard_map/all_to_all | solution.py:285
  254.7 0.0 copy-done.2
  254.7 3.5 %shard_map.61 = bf16[2,192,1536]{2,1,0:T(8,128)(2,1)} custom-call(bf16[4,192,384]{2,1,0:T(8,128)(2,1)} %all_to_all.27.refs_0_, bf16[4,192,384]{2,1,0:T(8,128)(2,1)} %copy-done.2), custom_call_target="tpu_custom_call" | custom-call | tf_op jit(solution)/shard_map/pallas_call | solution.py:247
  (5 shorter events, 0.1 us)
Async XLA Ops:
  6.5 183.8 %all-gather.5.cloned.1.call-start = ((), (), s32[]{:S(2)}) async-start(), calls=%async_computation.6 | async-start | bytes 5898240 | tf_op jit(solution)/shard_map/all_gather | solution.py:298
  8.1 4.7 %collective-permute-start = (s32[1,2]{1,0:T(1,128)S(1)}, s32[1,2]{1,0:T(1,128)S(1)}, u32[]{:S(2)}, u32[]{:S(2)}) collective-permute-start(s32[1,2]{1,0:T(1,128)S(1)} %bitcast_select_fusion), channel_id=1, source_target_pairs={{0,2},{2,0},{4,6},{6,4},{8,10},{10,8},{12,14},{14,12},{16,18},{18,... | collective-permute-start | bytes 32 | tf_op jit(solution)/shard_map/ppermute | solution.py:18
  10.3 31.0 %collective-permute-start.5 = (bf16[192,2560]{1,0:T(8,128)(2,1)S(1)}, bf16[192,2560]{1,0:T(8,128)(2,1)S(1)}, u32[]{:S(2)}, u32[]{:S(2)}) collective-permute-start(bf16[192,2560]{1,0:T(8,128)(2,1)S(1)} %get-tuple-element.11), channel_id=1, source_target_pairs={{0,1},{1,0},{2,3},{3,2},{4,5},{5,4},{6,7},{7,6},{8,9},{9,8},{10,11... | collective-permute-start | bytes 2949128 | tf_op jit(solution)/shard_map/ppermute | solution.py:18
  12.9 3.6 %collective-permute-start.1 = (s32[2,2]{1,0:T(2,128)S(1)}, s32[2,2]{1,0:T(2,128)S(1)}, u32[]{:S(2)}, u32[]{:S(2)}) collective-permute-start(s32[2,2]{1,0:T(2,128)S(1)} %pad_add_fusion.2), channel_id=1, source_target_pairs={{0,4},{2,6},{4,0},{6,2},{8,12},{10,14},{12,8},{14,10},{16,20},{18,... | collective-permute-start | bytes 56 | tf_op jit(solution)/shard_map/ppermute | solution.py:18
  16.5 3.7 %collective-permute-start.2 = (s32[4,2]{1,0:T(4,128)S(1)}, s32[4,2]{1,0:T(4,128)S(1)}, u32[]{:S(2)}, u32[]{:S(2)}) collective-permute-start(s32[4,2]{1,0:T(4,128)S(1)} %pad_add_fusion.1), channel_id=1, source_target_pairs={{0,8},{2,10},{4,12},{6,14},{8,0},{10,2},{12,4},{14,6},{16,24},{18,... | collective-permute-start | bytes 104 | tf_op jit(solution)/shard_map/ppermute | solution.py:18
  20.2 20.4 %collective-permute-start.3 = (s32[8,2]{1,0:T(8,128)S(1)}, s32[8,2]{1,0:T(8,128)S(1)}, u32[]{:S(2)}, u32[]{:S(2)}) collective-permute-start(s32[8,2]{1,0:T(8,128)S(1)} %pad_add_fusion), channel_id=1, source_target_pairs={{0,16},{2,18},{4,20},{6,22},{8,24},{10,26},{12,28},{14,30},{16,0},... | collective-permute-start | bytes 200 | tf_op jit(solution)/shard_map/ppermute | solution.py:18
  40.6 12.6 %copy-start.4 = (s32[16,2]{1,0:T(8,128)}, s32[16,2]{1,0:T(8,128)S(1)}, u32[]{:S(2)}) copy-start(s32[16,2]{1,0:T(8,128)S(1)} %concatenate.21.table) | copy-start | bytes 388
  41.3 0.9 copy-start
  84.7 131.1 %all-gather.3.cloned.1.call-start = ((), (), s32[]{:S(2)}) async-start(), calls=%async_computation.5 | async-start | bytes 5898240 | tf_op jit(solution)/shard_map/all_gather | solution.py:298
  84.8 22.2 %collective-permute-start.4 = (bf16[192,2560]{1,0:T(8,128)(2,1)S(1)}, bf16[192,2560]{1,0:T(8,128)(2,1)S(1)}, u32[]{:S(2)}, u32[]{:S(2)}) collective-permute-start(bf16[192,2560]{1,0:T(8,128)(2,1)S(1)} %get-tuple-element.12), channel_id=1, source_target_pairs={{0,1},{1,0},{2,3},{3,2},{4,5},{5,4},{6,7},{7,6},{8,9},{9,8},{10,11... | collective-permute-start | bytes 2949128 | tf_op jit(solution)/shard_map/ppermute | solution.py:18
  106.9 1.0 copy-start.1
  159.5 30.9 %all-to-all-start = ((bf16[4,2,192,384]{3,2,1,0:T(8,128)(2,1)}), bf16[4,2,192,384]{3,2,1,0:T(8,128)(2,1)S(1)}, u32[]{:S(2)}, u32[]{:S(2)}) async-start(bf16[4,2,192,384]{3,2,1,0:T(8,128)(2,1)} %shard_map.56), calls=%async_computation | async-start | bytes 2359296 | tf_op jit(solution)/shard_map/all_to_all | solution.py:285
  190.3 1.0 copy-start.3
  212.3 23.9 %all-to-all-start.4 = ((bf16[4,192,384]{2,1,0:T(8,128)(2,1)}), bf16[4,192,384]{2,1,0:T(8,128)(2,1)S(1)}, u32[]{:S(2)}, u32[]{:S(2)}) async-start(bf16[4,192,384]{2,1,0:T(8,128)(2,1)} %shard_map.60), calls=%async_computation.4 | async-start | bytes 1179648 | tf_op jit(solution)/shard_map/all_to_all | solution.py:285
  236.2 18.5 %copy-start.2 = (bf16[4,192,384]{2,1,0:T(8,128)(2,1)}, bf16[4,192,384]{2,1,0:T(8,128)(2,1)S(1)}, u32[]{:S(2)}) copy-start(bf16[4,192,384]{2,1,0:T(8,128)(2,1)S(1)} %all-to-all-done.4.refs_1_) | copy-start | bytes 1769476
Sparse Core Ops, SparseCore 0:
  84.9 35.6 all-gather.4
  150.1 35.5 all-gather.2

commit v3 on v0

v3 whole, which is shorter than its diff:
```python
import functools
import math

import jax
import jax.numpy as jnp
from jax import lax
from jax.experimental import pallas as pl
from jax.experimental.pallas import tpu as pltpu
from jax.sharding import PartitionSpec as P

HD = 128
LOG2_E = 1.4426950408889634
HIDDEN = -1e30
VMEM_LIMIT = 56 * 2**20


def exchange(value, axis, size, bit):
    return lax.ppermute(value, axis, [(i, i ^ bit) for i in range(size)])


def own_body(weights, place, mine_ref, other_ref, *refs):
    flat_ref = refs[-1]
    rows = other_ref.shape[0]

    @pl.when(pl.program_id(0) == 0)
    def _():
        flat_ref[:rows] = mine_ref[0]
        flat_ref[rows:] = other_ref[...]

    for weight_ref, out_ref in zip(refs[:weights], refs[weights:-1]):
        result = jnp.dot(flat_ref[...], weight_ref[...], preferred_element_type=jnp.float32)
        out_ref[0] = result.reshape(2, rows, -1)


def own_products(hidden_in, other, weights, place, ways):
    rows, feats = other.shape
    width = weights[0].shape[1] // ways
    return pl.pallas_call(
        functools.partial(own_body, len(weights)),
        out_shape=[jax.ShapeDtypeStruct((ways, 2, rows, width), jnp.float32)] * len(weights),
        grid_spec=pltpu.PrefetchScalarGridSpec(
            num_scalar_prefetch=1,
            grid=(ways,),
            in_specs=[
                pl.BlockSpec((1, rows, feats), lambda g, place: (place[2], 0, 0)),
                pl.BlockSpec((rows, feats), lambda g, place: (0, 0)),
            ]
            + [pl.BlockSpec((feats, width), lambda g, place: (place[0], place[1] ^ g))] * len(weights),
            out_specs=[pl.BlockSpec((1, 2, rows, width), lambda g, place: (g, 0, 0, 0))] * len(weights),
            scratch_shapes=[pltpu.VMEM((2 * rows, feats), jnp.bfloat16)],
        ),
        compiler_params=pltpu.CompilerParams(vmem_limit_bytes=VMEM_LIMIT),
        cost_estimate=pl.CostEstimate(
            flops=4 * rows * feats * width * ways * len(weights),
            bytes_accessed=2 * feats * width * ways * len(weights),
            transcendentals=0,
        ),
    )(place, hidden_in, other, *weights)


def rest_body(shares, steps, weights, chunks, place, *refs):
    inputs = refs[: shares * chunks]
    weight_refs = refs[shares * chunks : shares * chunks + weights]
    start_refs = refs[shares * chunks + weights : shares * chunks + 2 * weights]
    out_refs = refs[shares * chunks + 2 * weights : shares * chunks + 2 * weights + chunks]
    totals = refs[shares * chunks + 2 * weights + chunks :]
    rows = out_refs[0].shape[0]
    width = out_refs[0].shape[1] // weights
    step = pl.program_id(0)

    @pl.when(step == 0)
    def _():
        for total, start in zip(totals, start_refs):
            total[...] = start[...].reshape(chunks * rows, width)

    for share in range(shares):

        @pl.when(step // steps == share)
        def _():
            flat = [inputs[c * shares + share][...] for c in range(chunks)]
            flat = flat[0] if chunks == 1 else jnp.concatenate(flat, axis=0)
            for total, weight in zip(totals, weight_refs):
                total[...] += jnp.dot(flat, weight[...], preferred_element_type=jnp.float32)

    @pl.when(step == shares * steps - 1)
    def _():
        for n, total in enumerate(totals):
            for c, out_ref in enumerate(out_refs):
                out_ref[:, n * width : (n + 1) * width] = total[c * rows : (c + 1) * rows].astype(
                    out_ref.dtype
                )


def rest_products(received, chosen, weights, starts, place, a, ways):
    shares = len(received[0])
    rows, feats = received[0][0].shape
    width = weights[0].shape[1] // ways
    chunks = len(chosen)
    steps = max(1, feats // 640)
    depth = feats // steps

    def share_map(share, i, place):
        return (0, jnp.clip(i - share * steps, 0, steps - 1))

    in_specs = []
    operands = []
    for c in chosen:
        for share in range(shares):
            in_specs.append(pl.BlockSpec((rows, depth), functools.partial(share_map, share)))
            operands.append(received[c][share])
    in_specs += [
        pl.BlockSpec(
            (depth, width),
            lambda i, place: ((place[0] ^ (i // steps + 1)) * steps + i % steps, place[1] ^ a),
        )
    ] * len(weights)
    in_specs += [
        pl.BlockSpec((1, chunks, rows, width), lambda i, place: (a, chosen[0] // chunks, 0, 0))
    ] * len(weights)
    columns = width * len(weights)
    return pl.pallas_call(
        functools.partial(rest_body, shares, steps, len(weights), chunks),
        out_shape=[jax.ShapeDtypeStruct((rows, columns), jnp.bfloat16)] * chunks,
        grid_spec=pltpu.PrefetchScalarGridSpec(
            num_scalar_prefetch=1,
            grid=(shares * steps,),
            in_specs=in_specs,
            out_specs=[pl.BlockSpec((rows, columns), lambda i, place: (0, 0))] * chunks,
            scratch_shapes=[pltpu.VMEM((chunks * rows, width), jnp.float32)] * len(weights),
        ),
        compiler_params=pltpu.CompilerParams(vmem_limit_bytes=VMEM_LIMIT),
        cost_estimate=pl.CostEstimate(
            flops=2 * chunks * rows * feats * shares * columns,
            bytes_accessed=2 * feats * shares * columns,
            transcendentals=0,
        ),
    )(place, *operands, *weights, *starts)


def attend_body(block, ways, offsets, spans, tile, table, place, *refs):
    count = len(offsets)
    query_refs = refs[:ways]
    block_refs = refs[ways : ways + count]
    out_refs = refs[ways + count : 2 * ways + count]
    ordered, asked, scores, highest, sums, total, position, sems = refs[2 * ways + count :]
    rows, width = out_refs[0].shape
    half = rows // 2
    heads = width // HD
    rest = count // ways
    seq = place[2]

    copies = []
    for slot, offset in enumerate(offsets):
        low = table[offset, seq]
        for part, span in ((0, low), (1, spans - 1 - low)):
            copies.append(
                pltpu.make_async_copy(
                    block_refs[slot].at[pl.ds(part * half, half)],
                    ordered.at[pl.ds(pl.multiple_of(span * half, 16), half)],
                    sems.at[2 * slot + part],
                )
            )
    for copy in copies:
        copy.start()

    from_lane = lax.broadcasted_iota(jnp.int32, (half, 128), 0) - lax.broadcasted_iota(
        jnp.int32, (half, 128), 1
    )
    for a in range(ways):
        low = table[a * rest + block, seq]
        here = slice(a * half, (a + 1) * half)
        for part, span in ((0, low), (1, spans - 1 - low)):
            asked[part, here] = query_refs[a][part * half : (part + 1) * half]
            position[part, here] = from_lane + span * half
    highest[...] = jnp.full_like(highest, HIDDEN)
    sums[...] = jnp.zeros_like(sums)
    total[...] = jnp.zeros_like(total)
    for copy in copies:
        copy.wait()

    slope = LOG2_E / math.sqrt(HD)
    middle = spans * half // 2
    for part in range(2):
        starts = range(0, middle * (part + 1), tile)
        for start in starts:
            for h in range(heads):
                found = lax.dot_general(
                    asked[part, :, h * HD : (h + 1) * HD],
                    ordered[start : start + tile, h * HD : (h + 1) * HD],
                    (((1,), (1,)), ((), ())),
                    preferred_element_type=jnp.float32,
                )
                top = highest[h]
                for j in range(tile // 128):
                    piece = found[:, j * 128 : (j + 1) * 128]
                    if start >= middle * part:
                        piece = jnp.where(position[part] >= start + j * 128, piece, HIDDEN)
                    scores[h, :, start + j * 128 : start + (j + 1) * 128] = piece
                    top = jnp.maximum(top, piece)
                highest[h] = top
        for h in range(heads):
            highest[h] = jnp.broadcast_to(
                jnp.max(highest[h], axis=1, keepdims=True), highest.shape[1:]
            )
        for start in starts:
            for h in range(heads):
                top = highest[h]
                added = sums[h]
                weights = []
                for j in range(tile // 128):
                    piece = scores[h, :, start + j * 128 : start + (j + 1) * 128]
                    piece = jnp.exp2((piece - top) * slope)
                    added = added + piece
                    weights.append(piece.astype(jnp.bfloat16))
                sums[h] = added
                total[h] += jnp.dot(
                    jnp.concatenate(weights, axis=1),
                    ordered[start : start + tile, width + h * HD : width + (h + 1) * HD],
                    preferred_element_type=jnp.float32,
                )
        for h in range(heads):
            result = total[h] / jnp.sum(sums[h], axis=1, keepdims=True)
            for a in range(ways):
                out_refs[a][part * half : (part + 1) * half, h * HD : (h + 1) * HD] = result[
                    a * half : (a + 1) * half
                ].astype(jnp.bfloat16)
        if part == 0:
            highest[...] = jnp.full_like(highest, HIDDEN)
            sums[...] = jnp.zeros_like(sums)
            total[...] = jnp.zeros_like(total)


def attend(block, queries, blocks, table, place):
    rows, width = queries[0].shape
    ways, count = len(queries), len(blocks)
    offsets = sorted(blocks)
    spans = 2 * count
    half = rows // 2
    length = count * rows
    tile = 8 * half
    heads = width // HD
    many = ways * half
    smem = pl.BlockSpec(memory_space=pltpu.SMEM)
    flops = 6 * many * heads * length * HD
    return pl.pallas_call(
        functools.partial(attend_body, block, ways, offsets, spans, tile),
        out_shape=[jax.ShapeDtypeStruct((rows, width), jnp.bfloat16)] * ways,
        grid=(1,),
        in_specs=[smem, smem]
        + [pl.BlockSpec((rows, width), lambda i: (0, 0))] * ways
        + [pl.BlockSpec(memory_space=pl.ANY)] * count,
        out_specs=[pl.BlockSpec((rows, width), lambda i: (0, 0))] * ways,
        scratch_shapes=[
            pltpu.VMEM((length, 2 * width), jnp.bfloat16),
            pltpu.VMEM((2, many, width), jnp.bfloat16),
            pltpu.VMEM((heads, many, length), jnp.float32),
            pltpu.VMEM((heads, many, 128), jnp.float32),
            pltpu.VMEM((heads, many, 128), jnp.float32),
            pltpu.VMEM((heads, many, HD), jnp.float32),
            pltpu.VMEM((2, many, 128), jnp.int32),
            pltpu.SemaphoreType.DMA((2 * count,)),
        ],
        compiler_params=pltpu.CompilerParams(vmem_limit_bytes=VMEM_LIMIT),
        cost_estimate=pl.CostEstimate(
            flops=flops,
            bytes_accessed=4 * length * width + 4 * ways * rows * width,
            transcendentals=flops // (4 * HD),
        ),
    )(table, place, *queries, *[blocks[i] for i in offsets])


def assemble_body(slots, place, *refs):
    for n in range(slots):

        @pl.when(pl.program_id(0) == n)
        def _():
            refs[-1][0] = refs[n][...]


def assemble(pieces, place):
    ways, sequences = len(pieces), len(pieces[0])
    rows, width = pieces[0][0].shape
    return pl.pallas_call(
        functools.partial(assemble_body, ways * sequences),
        out_shape=jax.ShapeDtypeStruct((sequences, rows, ways * width), jnp.bfloat16),
        grid_spec=pltpu.PrefetchScalarGridSpec(
            num_scalar_prefetch=1,
            grid=(ways * sequences,),
            in_specs=[pl.BlockSpec((rows, width), lambda n, place: (0, 0))] * (ways * sequences),
            out_specs=pl.BlockSpec(
                (1, rows, width),
                lambda n, place: (place[2] ^ (n % sequences), 0, place[1] ^ (n // sequences)),
            ),
        ),
        compiler_params=pltpu.CompilerParams(vmem_limit_bytes=VMEM_LIMIT),
    )(place, *[piece for row in pieces for piece in row])


def on_device(ctx_size, tp_size, hidden_in, w_q, w_k, w_v, event_pos):
    _, rows, _ = hidden_in.shape
    features = w_q.shape[1]
    ways = math.gcd(features // HD, ctx_size // 2)
    rest = ctx_size // ways
    ctx_me = lax.axis_index("ctx").astype(jnp.int32)
    tp_me = lax.axis_index("tp").astype(jnp.int32)
    core = ctx_me % 2
    place = jnp.stack([tp_me, ctx_me // rest, core, ctx_me])
    away = list(range(ways - 1, -1, -1))

    def over_ctx(value, offset):
        return exchange(value, "ctx", ctx_size, offset) if offset else value

    def other_shares(own):
        shares = [own]
        bit = 1
        while bit < tp_size:
            shares += [exchange(share, "tp", tp_size, bit) for share in shares]
            bit *= 2
        return shares[1:]

    mine = lax.dynamic_index_in_dim(hidden_in, core, 0, keepdims=False)
    other = over_ctx(lax.dynamic_index_in_dim(hidden_in, 1 - core, 0, keepdims=False), 1)
    received = [other_shares(mine), other_shares(other)]

    table = event_pos[None, :, 0] // (rows // 2)
    bit = 1
    while bit < ctx_size:
        table = jnp.concatenate([table, over_ctx(table, bit)], axis=0)
        bit *= 2

    start_k, start_v, start_q = own_products(hidden_in, other, [w_k, w_v, w_q], place, ways)
    place_later = jnp.concatenate([place, table.reshape(-1)])

    blocks = {}
    for b in range(2):
        for a in away:
            (made,) = rest_products(received, [b], [w_k, w_v], [start_k, start_v], place_later, a, ways)
            blocks[a * rest + b] = over_ctx(made, a * rest)
    bit = rest // 2
    while bit > 1:
        for i in list(blocks):
            blocks[i ^ bit] = over_ctx(blocks[i], bit)
        bit //= 2
    queries = [[None] * ways, [None] * ways]
    for a in away:
        made = rest_products(received, [0, 1], [w_q], [start_q], place_later, a, ways)
        for b in range(2):
            queries[b][a] = over_ctx(made[b], a * rest)
    pieces = [[None] * 2 for _ in range(ways)]
    for b in range(2):
        outs = attend(b, queries[b], blocks, table, place)
        for a in away:
            pieces[a][b] = over_ctx(outs[a], a * rest + b)
    return assemble(pieces, place)


def solution(mesh):
    sizes = dict(mesh.shape)
    placed = (P(None, "ctx", "tp"), P(None, "tp"), P(None, "tp"), P(None, "tp"), P(None, "ctx"))
    return jax.shard_map(
        functools.partial(on_device, sizes["ctx"], sizes["tp"]),
        mesh=mesh,
        in_specs=placed,
        out_specs=P(None, "ctx", "tp"),
        check_vma=False,
    )
```

time: 516 us -> 220 us (0.43)
  waiting for transfers between devices: 210 us -> 26.6 us
  local copies, waits for them, and re-layouts: 171 us -> 7.5 us
  Pallas kernels: 0 us -> 122 us
  matrix products: 69.9 us -> 0 us
  starting transfers between devices: 0.08 us -> 61 us
  blocking collectives: 21.8 us -> 0 us
  other arithmetic: 22.3 us -> 0.9 us
  between operations: 13.2 us -> 0.32 us
    all_gather x3 -> x0, waiting for transfers between devices: 210 us -> none  [the longest x1 101 us: on_device(): lax.all_gather(keys, 'ctx', axis=1, tiled=True)]
    dynamic_slice x30 -> x0, local copies, waits for them, and re-layouts: 156 us -> none  [the longest x24 153 us: scan_step(): lax.dynamic_slice_in_dim(member, offset, block_len, 1)]
    pallas_call x0 -> x16, Pallas kernels: none -> 122 us  [the longest x12 70.6 us: rest_products(): pl.pallas_call(functools.partial(rest_body, shares, steps, len(weights),...]
    dot_general x15 -> x0, matrix products: 69.9 us -> none  [the longest x3 32.7 us: on_device(): jnp.dot(flat_rows, matrix, preferred_element_type=jnp.float32)]
    ppermute x0 -> x34, starting transfers between devices: none -> 61 us  [exchange(): return lax.ppermute(value, axis, [(i, i ^ bit) for i in range(size)])]
    ppermute x0 -> x34, waiting for transfers between devices: none -> 26.6 us  [exchange(): return lax.ppermute(value, axis, [(i, i ^ bit) for i in range(size)])]
    all_gather x1 -> x0, blocking collectives: 21.8 us -> none  [on_device(): lax.all_gather(event_pos, 'ctx', axis=1, tiled=True)]
    reduce_sum x6 -> x0, other arithmetic: 18.2 us -> none  [update(): new_sum = run_sum * shrink + jnp.sum(weights, axis=3)]
  transfers between devices with their start and end apart: 3 -> 34, of which waited for: 3 -> 8; matrix products, arithmetic and copies ran while one was open for 5% -> 1% of each run, Pallas kernels for 0% -> 54%
where the time goes in v3:
time: 220 us; the launch traced here: 219 us
  Pallas kernels  122 us (55%)
  starting transfers between devices  61 us (28%)
  waiting for transfers between devices  26.6 us (12%)
  local copies, waits for them, and re-layouts  7.5 us (3%)
    pallas_call x12, Pallas kernels, rest_products(): pl.pallas_call(functools.partial(rest_body, shares, steps, len(weights),...  70.6 us
    ppermute x34, starting transfers between devices, exchange(): return lax.ppermute(value, axis, [(i, i ^ bit) for i in range(size)])  61 us
    pallas_call x2, Pallas kernels, attend(): pl.pallas_call(functools.partial(attend_body, block, ways, offsets, spans...  28 us
    ppermute x34, waiting for transfers between devices, exchange(): return lax.ppermute(value, axis, [(i, i ^ bit) for i in range(size)])  26.6 us
    pallas_call x1, Pallas kernels, own_products(): pl.pallas_call(functools.partial(own_body, len(weights)), out_shape=[jax....  18.7 us
    pallas_call x1, Pallas kernels, assemble(): pl.pallas_call(functools.partial(assemble_body, ways * sequences), out_sh...  4.96 us
  transfers between devices with their start and end apart: 34, of which 8 were waited for; matrix products, arithmetic and copies ran while one was open for 1% of the time, Pallas kernels for 54%

profile of v3, /device:TPU:0, one launch (start us, length us, event | category | flops | bytes accessed | tf_op | source)
XLA Modules:
  0.0 218.6 jit_solution(9786945326802904420)
XLA Ops:
  0.0 2.6 %dynamic-slice_bitcast_fusion = (bf16[192,2560]{1,0:T(8,128)(2,1)}, bf16[192,2560]{1,0:T(8,128)(2,1)S(1)}) fusion(bf16[2,192,2560]{2,1,0:T(8,128)(2,1)} %mine_ref.1, s32[]{:T(128)S(6)} %select_n.35, s32[]{:T(128)S(6)} %select_n.34), kind=kLoop, calls=%fused_computation | loop fusion | bytes 3932168 | tf_op jit(solution)/shard_map/jit(dynamic_index_in_dim)/squeeze | solution.py:322
  3.4 2.9 %collective-permute-start.4 = (bf16[192,2560]{1,0:T(8,128)(2,1)S(1)}, bf16[192,2560]{1,0:T(8,128)(2,1)S(1)}, u32[]{:S(2)}, u32[]{:S(2)}) collective-permute-start(bf16[192,2560]{1,0:T(8,128)(2,1)S(1)} %get-tuple-element.44), channel_id=1, source_target_pairs={{0,1},{1,0},{2,3},{3,2},{4,5},{5,4},{6,7},{7,6},{8,9},{9,8},{10,11... | collective-permute-start | bytes 2949128 | tf_op jit(solution)/shard_map/ppermute | solution.py:18
  6.4 1.8 collective-permute-start.1
  8.1 1.9 collective-permute-done.1
  10.0 1.8 collective-permute-start.2
  11.8 1.8 collective-permute-done.2
  13.7 2.8 %collective-permute-start.3 = (s32[8,2]{1,0:T(8,128)S(1)}, s32[8,2]{1,0:T(8,128)S(1)}, u32[]{:S(2)}, u32[]{:S(2)}) collective-permute-start(s32[8,2]{1,0:T(8,128)S(1)} %pad_add_fusion), channel_id=1, source_target_pairs={{0,16},{2,18},{4,20},{6,22},{8,24},{10,26},{12,28},{14,30},{16,0},... | collective-permute-start | bytes 200 | tf_op jit(solution)/shard_map/ppermute | solution.py:18
  17.1 1.1 collective-permute-done.3
  19.0 1.7 collective-permute-start.6
  20.7 18.7 %shard_map.55 = (f32[4,2,192,384]{3,2,1,0:T(8,128)}, f32[4,2,192,384]{3,2,1,0:T(8,128)}, f32[4,2,192,384]{3,2,1,0:T(8,128)}) custom-call(s32[4]{0:T(128)} %pad_add_fusion.3.place, bf16[2,192,2560]{2,1,0:T(8,128)(2,1)} %mine_ref.1, bf16[192,2560]{1,0:T(8,128)(2,1)} %copy-done.2, bf16[5120,1536]{1,0:T(8,128)(2,1)} %refs_1_.17, bf16[5120,1536]{1,0:T(8,128)(2,1)} %refs_2_.25, ...), custom_call_target="tpu_custom_call" | custom-call | flops 9059696640 | bytes 23592960 | tf_op jit(solution)/shard_map/pallas_call | solution.py:38
  40.3 5.9 %shard_map.62 = bf16[192,768]{1,0:T(8,128)(2,1)} custom-call(s32[36]{0:T(128)} %concatenate.23.place, bf16[192,2560]{1,0:T(8,128)(2,1)} %copy-done, bf16[5120,1536]{1,0:T(8,128)(2,1)} %refs_1_.17, bf16[5120,1536]{1,0:T(8,128)(2,1)} %refs_2_.25, f32[4,2,192,384]{3,2,1,0:T(8,128)} %get-tuple-element.29.refs_3_, f32[4,2,192,384]{3,2,1,0:T(8,128)} %get-tuple-element.30.refs_4_), custom_call_target="tpu_custom_call" | custom-call | flops 754974720 | bytes 3932160 | tf_op jit(solution)/shard_map/pallas_call | solution.py:121
  46.2 1.4 collective-permute-start.12
  47.6 6.0 %shard_map.64 = bf16[192,768]{1,0:T(8,128)(2,1)} custom-call(s32[36]{0:T(128)} %concatenate.23.place, bf16[192,2560]{1,0:T(8,128)(2,1)} %copy-done, bf16[5120,1536]{1,0:T(8,128)(2,1)} %refs_1_.17, bf16[5120,1536]{1,0:T(8,128)(2,1)} %refs_2_.25, f32[4,2,192,384]{3,2,1,0:T(8,128)} %get-tuple-element.29.refs_3_, f32[4,2,192,384]{3,2,1,0:T(8,128)} %get-tuple-element.30.refs_4_), custom_call_target="tpu_custom_call" | custom-call | flops 754974720 | bytes 3932160 | tf_op jit(solution)/shard_map/pallas_call | solution.py:121
  53.6 2.6 %collective-permute-start.16 = (bf16[192,768]{1,0:T(8,128)(2,1)}, bf16[192,768]{1,0:T(8,128)(2,1)S(1)}, u32[]{:S(2)}, u32[]{:S(2)}) collective-permute-start(bf16[192,768]{1,0:T(8,128)(2,1)} %shard_map.64), channel_id=1, source_target_pairs={{0,16},{2,18},{4,20},{6,22},{8,24},{10,26},{12,28},{14,30},{16,0},... | collective-permute-start | bytes 884744 | tf_op jit(solution)/shard_map/ppermute | solution.py:18
  56.2 6.0 %shard_map.66 = bf16[192,768]{1,0:T(8,128)(2,1)} custom-call(s32[36]{0:T(128)} %concatenate.23.place, bf16[192,2560]{1,0:T(8,128)(2,1)} %copy-done, bf16[5120,1536]{1,0:T(8,128)(2,1)} %refs_1_.17, bf16[5120,1536]{1,0:T(8,128)(2,1)} %refs_2_.25, f32[4,2,192,384]{3,2,1,0:T(8,128)} %get-tuple-element.29.refs_3_, f32[4,2,192,384]{3,2,1,0:T(8,128)} %get-tuple-element.30.refs_4_), custom_call_target="tpu_custom_call" | custom-call | flops 754974720 | bytes 3932160 | tf_op jit(solution)/shard_map/pallas_call | solution.py:121
  62.5 5.9 %shard_map.60.refs_4_ = bf16[192,768]{1,0:T(8,128)(2,1)} custom-call(s32[36]{0:T(128)} %concatenate.23.place, bf16[192,2560]{1,0:T(8,128)(2,1)} %copy-done, bf16[5120,1536]{1,0:T(8,128)(2,1)} %refs_1_.17, bf16[5120,1536]{1,0:T(8,128)(2,1)} %refs_2_.25, f32[4,2,192,384]{3,2,1,0:T(8,128)} %get-tuple-element.29.refs_3_, ...), custom_call_target="tpu_custom_call" | custom-call | flops 754974720 | bytes 3932160 | tf_op jit(solution)/shard_map/pallas_call | solution.py:121
  68.5 1.5 collective-permute-start.10
  70.5 3.6 %collective-permute-done.16.refs_12_ = bf16[192,768]{1,0:T(8,128)(2,1)S(1)} collective-permute-done((bf16[192,768]{1,0:T(8,128)(2,1)}, bf16[192,768]{1,0:T(8,128)(2,1)S(1)}, u32[]{:S(2)}, u32[]{:S(2)}) %collective-permute-start.16) | collective-permute-done | bytes 294944 | tf_op jit(solution)/shard_map/ppermute | solution.py:18
  74.1 1.5 collective-permute-start.18
  77.2 5.9 %shard_map.63 = bf16[192,768]{1,0:T(8,128)(2,1)} custom-call(s32[36]{0:T(128)} %concatenate.23.place, bf16[192,2560]{1,0:T(8,128)(2,1)} %copy-done.1, bf16[5120,1536]{1,0:T(8,128)(2,1)} %refs_1_.17, bf16[5120,1536]{1,0:T(8,128)(2,1)} %refs_2_.25, f32[4,2,192,384]{3,2,1,0:T(8,128)} %get-tuple-element.29.refs_3_, f32[4,2,192,384]{3,2,1,0:T(8,128)} %get-tuple-element.30.refs_4_), custom_call_target="tpu_custom_call" | custom-call | flops 754974720 | bytes 3932160 | tf_op jit(solution)/shard_map/pallas_call | solution.py:121
  83.1 5.3 %collective-permute-start.13 = (bf16[192,768]{1,0:T(8,128)(2,1)}, bf16[192,768]{1,0:T(8,128)(2,1)S(1)}, u32[]{:S(2)}, u32[]{:S(2)}) collective-permute-start(bf16[192,768]{1,0:T(8,128)(2,1)} %shard_map.63), channel_id=1, source_target_pairs={{0,8},{2,10},{4,12},{6,14},{8,0},{10,2},{12,4},{14,6},{16,24},{18,... | collective-permute-start | bytes 884744 | tf_op jit(solution)/shard_map/ppermute | solution.py:18
  88.4 5.9 %shard_map.67 = bf16[192,768]{1,0:T(8,128)(2,1)} custom-call(s32[36]{0:T(128)} %concatenate.23.place, bf16[192,2560]{1,0:T(8,128)(2,1)} %copy-done.1, bf16[5120,1536]{1,0:T(8,128)(2,1)} %refs_1_.17, bf16[5120,1536]{1,0:T(8,128)(2,1)} %refs_2_.25, f32[4,2,192,384]{3,2,1,0:T(8,128)} %get-tuple-element.29.refs_3_, f32[4,2,192,384]{3,2,1,0:T(8,128)} %get-tuple-element.30.refs_4_), custom_call_target="tpu_custom_call" | custom-call | flops 754974720 | bytes 3932160 | tf_op jit(solution)/shard_map/pallas_call | solution.py:121
  94.3 6.0 %shard_map.65 = bf16[192,768]{1,0:T(8,128)(2,1)} custom-call(s32[36]{0:T(128)} %concatenate.23.place, bf16[192,2560]{1,0:T(8,128)(2,1)} %copy-done.1, bf16[5120,1536]{1,0:T(8,128)(2,1)} %refs_1_.17, bf16[5120,1536]{1,0:T(8,128)(2,1)} %refs_2_.25, f32[4,2,192,384]{3,2,1,0:T(8,128)} %get-tuple-element.29.refs_3_, f32[4,2,192,384]{3,2,1,0:T(8,128)} %get-tuple-element.30.refs_4_), custom_call_target="tpu_custom_call" | custom-call | flops 754974720 | bytes 3932160 | tf_op jit(solution)/shard_map/pallas_call | solution.py:121
  100.4 1.1 collective-permute-start.17
  101.5 1.5 collective-permute-start.21
  103.0 5.8 %shard_map.59 = (bf16[192,384]{1,0:T(8,128)(2,1)}, bf16[192,384]{1,0:T(8,128)(2,1)}) custom-call(s32[36]{0:T(128)} %concatenate.23.place, bf16[192,2560]{1,0:T(8,128)(2,1)} %copy-done, bf16[192,2560]{1,0:T(8,128)(2,1)} %copy-done.1, bf16[5120,1536]{1,0:T(8,128)(2,1)} %refs_2_.17, f32[4,2,192,384]{3,2,1,0:T(8,128)} %get-tuple-element.24.refs_3_), custom_call_target="tpu_custom_call" | custom-call | flops 754974720 | bytes 1966080 | tf_op jit(solution)/shard_map/pallas_call | solution.py:121
  108.8 2.4 %collective-permute-start.26 = (bf16[192,384]{1,0:T(8,128)(2,1)}, bf16[192,384]{1,0:T(8,128)(2,1)S(1)}, u32[]{:S(2)}, u32[]{:S(2)}) collective-permute-start(bf16[192,384]{1,0:T(8,128)(2,1)} %get-tuple-element.35), channel_id=1, source_target_pairs={{0,24},{2,26},{4,28},{6,30},{8,16},{10,18},{12,20},{14,22},{16,8},... | collective-permute-start | bytes 442376 | tf_op jit(solution)/shard_map/ppermute | solution.py:18
  111.2 5.8 %shard_map.58 = (bf16[192,384]{1,0:T(8,128)(2,1)}, bf16[192,384]{1,0:T(8,128)(2,1)}) custom-call(s32[36]{0:T(128)} %concatenate.23.place, bf16[192,2560]{1,0:T(8,128)(2,1)} %copy-done, bf16[192,2560]{1,0:T(8,128)(2,1)} %copy-done.1, bf16[5120,1536]{1,0:T(8,128)(2,1)} %refs_2_.17, f32[4,2,192,384]{3,2,1,0:T(8,128)} %get-tuple-element.24.refs_3_), custom_call_target="tpu_custom_call" | custom-call | flops 754974720 | bytes 1966080 | tf_op jit(solution)/shard_map/pallas_call | solution.py:121
  117.1 5.9 %shard_map.61.refs_5_ = bf16[192,768]{1,0:T(8,128)(2,1)} custom-call(s32[36]{0:T(128)} %concatenate.23.place, bf16[192,2560]{1,0:T(8,128)(2,1)} %copy-done.1, bf16[5120,1536]{1,0:T(8,128)(2,1)} %refs_1_.17, bf16[5120,1536]{1,0:T(8,128)(2,1)} %refs_2_.25, f32[4,2,192,384]{3,2,1,0:T(8,128)} %get-tuple-element.29.refs_3_, ...), custom_call_target="tpu_custom_call" | custom-call | flops 754974720 | bytes 3932160 | tf_op jit(solution)/shard_map/pallas_call | solution.py:121
  123.6 1.5 collective-permute-start.15
  125.2 2.6 %collective-permute-done.17.refs_13_ = bf16[192,768]{1,0:T(8,128)(2,1)S(1)} collective-permute-done((bf16[192,768]{1,0:T(8,128)(2,1)}, bf16[192,768]{1,0:T(8,128)(2,1)S(1)}, u32[]{:S(2)}, u32[]{:S(2)}) %collective-permute-start.17) | collective-permute-done | bytes 294944 | tf_op jit(solution)/shard_map/ppermute | solution.py:18
  128.3 1.5 collective-permute-start.23
  129.8 5.7 %shard_map.57 = (bf16[192,384]{1,0:T(8,128)(2,1)}, bf16[192,384]{1,0:T(8,128)(2,1)}) custom-call(s32[36]{0:T(128)} %concatenate.23.place, bf16[192,2560]{1,0:T(8,128)(2,1)} %copy-done, bf16[192,2560]{1,0:T(8,128)(2,1)} %copy-done.1, bf16[5120,1536]{1,0:T(8,128)(2,1)} %refs_2_.17, f32[4,2,192,384]{3,2,1,0:T(8,128)} %get-tuple-element.24.refs_3_), custom_call_target="tpu_custom_call" | custom-call | flops 754974720 | bytes 1966080 | tf_op jit(solution)/shard_map/pallas_call | solution.py:121
  135.6 4.7 %collective-permute-done.25.refs_2_ = bf16[192,384]{1,0:T(8,128)(2,1)S(1)} collective-permute-done((bf16[192,384]{1,0:T(8,128)(2,1)}, bf16[192,384]{1,0:T(8,128)(2,1)S(1)}, u32[]{:S(2)}, u32[]{:S(2)}) %collective-permute-start.25) | collective-permute-done | bytes 147488 | tf_op jit(solution)/shard_map/ppermute | solution.py:18
  140.3 7.5 %collective-permute-start.24 = (bf16[192,384]{1,0:T(8,128)(2,1)}, bf16[192,384]{1,0:T(8,128)(2,1)S(1)}, u32[]{:S(2)}, u32[]{:S(2)}) collective-permute-start(bf16[192,384]{1,0:T(8,128)(2,1)} %get-tuple-element.33), channel_id=1, source_target_pairs={{0,8},{2,10},{4,12},{6,14},{8,0},{10,2},{12,4},{14,6},{16,24},{18,... | collective-permute-start | bytes 442376 | tf_op jit(solution)/shard_map/ppermute | solution.py:18
  147.8 5.8 %shard_map.56 = (bf16[192,384]{1,0:T(8,128)(2,1)}, bf16[192,384]{1,0:T(8,128)(2,1)}) custom-call(s32[36]{0:T(128)} %concatenate.23.place, bf16[192,2560]{1,0:T(8,128)(2,1)} %copy-done, bf16[192,2560]{1,0:T(8,128)(2,1)} %copy-done.1, bf16[5120,1536]{1,0:T(8,128)(2,1)} %refs_2_.17, f32[4,2,192,384]{3,2,1,0:T(8,128)} %get-tuple-element.24.refs_3_), custom_call_target="tpu_custom_call" | custom-call | flops 754974720 | bytes 1966080 | tf_op jit(solution)/shard_map/pallas_call | solution.py:121
  153.6 2.4 %collective-permute-start.9 = (bf16[192,384]{1,0:T(8,128)(2,1)S(1)}, bf16[192,384]{1,0:T(8,128)(2,1)S(1)}, u32[]{:S(2)}, u32[]{:S(2)}) collective-permute-start(bf16[192,384]{1,0:T(8,128)(2,1)S(1)} %copy-done.26), channel_id=1, source_target_pairs={{0,24},{2,26},{4,28},{6,30},{8,16},{10,18},{12,20},{14,22},{16,8},... | collective-permute-start | bytes 442376 | tf_op jit(solution)/shard_map/ppermute | solution.py:18
  156.1 2.0 collective-permute-start.7
  159.0 13.9 %shard_map.69 = (bf16[192,384]{1,0:T(8,128)(2,1)}, bf16[192,384]{1,0:T(8,128)(2,1)}, bf16[192,384]{1,0:T(8,128)(2,1)}, bf16[192,384]{1,0:T(8,128)(2,1)}) custom-call(s32[16,2]{1,0:T(8,128)} %copy-done.11, s32[4]{0:T(128)} %pad_add_fusion.3.place, bf16[192,384]{1,0:T(8,128)(2,1)} %get-tuple-element.32.refs_0_, bf16[192,384]{1,0:T(8,128)(2,1)} %copy-done.34, ...), custom_call_target="tpu_custom_call" | custom-call | flops 2717908992 | bytes 5898240 | tf_op jit(solution)/shard_map/pallas_call | solution.py:245
  173.0 7.7 %collective-permute-start.29 = (bf16[192,384]{1,0:T(8,128)(2,1)}, bf16[192,384]{1,0:T(8,128)(2,1)S(1)}, u32[]{:S(2)}, u32[]{:S(2)}) collective-permute-start(bf16[192,384]{1,0:T(8,128)(2,1)} %get-tuple-element.38), channel_id=1, source_target_pairs={{0,10},{2,8},{4,14},{6,12},{8,2},{10,0},{12,6},{14,4},{16,26},{18,... | collective-permute-start | bytes 442376 | tf_op jit(solution)/shard_map/ppermute | solution.py:18
  181.6 1.1 collective-permute-start.33
  183.5 14.1 %shard_map.68 = (bf16[192,384]{1,0:T(8,128)(2,1)}, bf16[192,384]{1,0:T(8,128)(2,1)}, bf16[192,384]{1,0:T(8,128)(2,1)}, bf16[192,384]{1,0:T(8,128)(2,1)}) custom-call(s32[16,2]{1,0:T(8,128)} %copy-done.11, s32[4]{0:T(128)} %pad_add_fusion.3.place, bf16[192,384]{1,0:T(8,128)(2,1)} %get-tuple-element.25.refs_0_, bf16[192,384]{1,0:T(8,128)(2,1)} %copy-done.33, ...), custom_call_target="tpu_custom_call" | custom-call | flops 2717908992 | bytes 5898240 | tf_op jit(solution)/shard_map/pallas_call | solution.py:245
  197.6 1.1 collective-permute-start.28
  198.7 1.9 collective-permute-start.30
  200.6 1.5 collective-permute-start.32
  202.1 4.4 %collective-permute-done.28.refs_2_ = bf16[192,384]{1,0:T(8,128)(2,1)S(1)} collective-permute-done((bf16[192,384]{1,0:T(8,128)(2,1)}, bf16[192,384]{1,0:T(8,128)(2,1)S(1)}, u32[]{:S(2)}, u32[]{:S(2)}) %collective-permute-start.28) | collective-permute-done | bytes 147488 | tf_op jit(solution)/shard_map/ppermute | solution.py:18
  206.5 6.4 %collective-permute-done.30.refs_4_ = bf16[192,384]{1,0:T(8,128)(2,1)S(1)} collective-permute-done((bf16[192,384]{1,0:T(8,128)(2,1)}, bf16[192,384]{1,0:T(8,128)(2,1)S(1)}, u32[]{:S(2)}, u32[]{:S(2)}) %collective-permute-start.30) | collective-permute-done | bytes 147488 | tf_op jit(solution)/shard_map/ppermute | solution.py:18
  213.6 5.0 %shard_map.70 = bf16[2,192,1536]{2,1,0:T(8,128)(2,1)} custom-call(s32[4]{0:T(128)} %pad_add_fusion.3.place, bf16[192,384]{1,0:T(8,128)(2,1)} %get-tuple-element.31.refs_0_, bf16[192,384]{1,0:T(8,128)(2,1)} %copy-done.4, bf16[192,384]{1,0:T(8,128)(2,1)} %copy-done.8, bf16[192,384]{1,0:T(8,128)(2,1)} %copy-done.5, bf16[192,384]{1,0:T(8,128)(2,1)} %copy-done.9, ...), custom_call_target="tpu_custom_call" | custom-call | tf_op jit(solution)/shard_map/pallas_call | solution.py:283
  (119 shorter events, 10.2 us)
Async XLA Ops:
  2.6 16.4 %collective-permute-start.5 = (bf16[192,2560]{1,0:T(8,128)(2,1)}, bf16[192,2560]{1,0:T(8,128)(2,1)S(1)}, u32[]{:S(2)}, u32[]{:S(2)}) collective-permute-start(bf16[192,2560]{1,0:T(8,128)(2,1)} %get-tuple-element.43), channel_id=1, source_target_pairs={{0,2},{2,0},{4,6},{6,4},{8,10},{10,8},{12,14},{14,12},{16,18},{18,... | collective-permute-start | bytes 2949128 | tf_op jit(solution)/shard_map/ppermute | solution.py:18
  3.3 3.1 %collective-permute-start = (s32[1,2]{1,0:T(1,128)S(1)}, s32[1,2]{1,0:T(1,128)S(1)}, u32[]{:S(2)}, u32[]{:S(2)}) collective-permute-start(s32[1,2]{1,0:T(1,128)S(1)} %bitcast_select_fusion), channel_id=1, source_target_pairs={{0,2},{2,0},{4,6},{6,4},{8,10},{10,8},{12,14},{14,12},{16,18},{18,... | collective-permute-start | bytes 32 | tf_op jit(solution)/shard_map/ppermute | solution.py:18
  3.4 35.9 %collective-permute-start.4 = (bf16[192,2560]{1,0:T(8,128)(2,1)S(1)}, bf16[192,2560]{1,0:T(8,128)(2,1)S(1)}, u32[]{:S(2)}, u32[]{:S(2)}) collective-permute-start(bf16[192,2560]{1,0:T(8,128)(2,1)S(1)} %get-tuple-element.44), channel_id=1, source_target_pairs={{0,1},{1,0},{2,3},{3,2},{4,5},{5,4},{6,7},{7,6},{8,9},{9,8},{10,11... | collective-permute-start | bytes 2949128 | tf_op jit(solution)/shard_map/ppermute | solution.py:18
  6.4 3.6 %collective-permute-start.1 = (s32[2,2]{1,0:T(2,128)S(1)}, s32[2,2]{1,0:T(2,128)S(1)}, u32[]{:S(2)}, u32[]{:S(2)}) collective-permute-start(s32[2,2]{1,0:T(2,128)S(1)} %pad_add_fusion.2), channel_id=1, source_target_pairs={{0,4},{2,6},{4,0},{6,2},{8,12},{10,14},{12,8},{14,10},{16,20},{18,... | collective-permute-start | bytes 56 | tf_op jit(solution)/shard_map/ppermute | solution.py:18
  10.0 3.7 %collective-permute-start.2 = (s32[4,2]{1,0:T(4,128)S(1)}, s32[4,2]{1,0:T(4,128)S(1)}, u32[]{:S(2)}, u32[]{:S(2)}) collective-permute-start(s32[4,2]{1,0:T(4,128)S(1)} %pad_add_fusion.1), channel_id=1, source_target_pairs={{0,8},{2,10},{4,12},{6,14},{8,0},{10,2},{12,4},{14,6},{16,24},{18,... | collective-permute-start | bytes 104 | tf_op jit(solution)/shard_map/ppermute | solution.py:18
  13.7 4.6 %collective-permute-start.3 = (s32[8,2]{1,0:T(8,128)S(1)}, s32[8,2]{1,0:T(8,128)S(1)}, u32[]{:S(2)}, u32[]{:S(2)}) collective-permute-start(s32[8,2]{1,0:T(8,128)S(1)} %pad_add_fusion), channel_id=1, source_target_pairs={{0,16},{2,18},{4,20},{6,22},{8,24},{10,26},{12,28},{14,30},{16,0},... | collective-permute-start | bytes 200 | tf_op jit(solution)/shard_map/ppermute | solution.py:18
  18.3 21.0 %copy-start.11 = (s32[16,2]{1,0:T(8,128)}, s32[16,2]{1,0:T(8,128)S(1)}, u32[]{:S(2)}) copy-start(s32[16,2]{1,0:T(8,128)S(1)} %concatenate.22.table) | copy-start | bytes 388
  19.0 57.2 %collective-permute-start.6 = (bf16[192,2560]{1,0:T(8,128)(2,1)S(1)}, bf16[192,2560]{1,0:T(8,128)(2,1)S(1)}, u32[]{:S(2)}, u32[]{:S(2)}) collective-permute-start(bf16[192,2560]{1,0:T(8,128)(2,1)S(1)} %collective-permute-done.5.other_ref), channel_id=1, source_target_pairs={{0,1},{1,0},{2,3},{3,2},{4,5},{5,4},{6,7},{7,6},{8,9},{9,8},{10,11... | collective-permute-start | bytes 2949128 | tf_op jit(solution)/shard_map/ppermute | solution.py:18
  46.2 23.8 %collective-permute-start.12 = (bf16[192,768]{1,0:T(8,128)(2,1)}, bf16[192,768]{1,0:T(8,128)(2,1)S(1)}, u32[]{:S(2)}, u32[]{:S(2)}) collective-permute-start(bf16[192,768]{1,0:T(8,128)(2,1)} %shard_map.62), channel_id=1, source_target_pairs={{0,8},{2,10},{4,12},{6,14},{8,0},{10,2},{12,4},{14,6},{16,24},{18,... | collective-permute-start | bytes 884744 | tf_op jit(solution)/shard_map/ppermute | solution.py:18
  53.6 20.5 %collective-permute-start.16 = (bf16[192,768]{1,0:T(8,128)(2,1)}, bf16[192,768]{1,0:T(8,128)(2,1)S(1)}, u32[]{:S(2)}, u32[]{:S(2)}) collective-permute-start(bf16[192,768]{1,0:T(8,128)(2,1)} %shard_map.64), channel_id=1, source_target_pairs={{0,16},{2,18},{4,20},{6,22},{8,24},{10,26},{12,28},{14,30},{16,0},... | collective-permute-start | bytes 884744 | tf_op jit(solution)/shard_map/ppermute | solution.py:18
  62.1 13.5 %collective-permute-start.20 = (bf16[192,768]{1,0:T(8,128)(2,1)}, bf16[192,768]{1,0:T(8,128)(2,1)S(1)}, u32[]{:S(2)}, u32[]{:S(2)}) collective-permute-start(bf16[192,768]{1,0:T(8,128)(2,1)} %shard_map.66), channel_id=1, source_target_pairs={{0,24},{2,26},{4,28},{6,30},{8,16},{10,18},{12,20},{14,22},{16,8},... | collective-permute-start | bytes 884744 | tf_op jit(solution)/shard_map/ppermute | solution.py:18
  68.5 31.9 %collective-permute-start.10 = (bf16[192,768]{1,0:T(8,128)(2,1)}, bf16[192,768]{1,0:T(8,128)(2,1)S(1)}, u32[]{:S(2)}, u32[]{:S(2)}) collective-permute-start(bf16[192,768]{1,0:T(8,128)(2,1)} %shard_map.60.refs_4_), channel_id=1, source_target_pairs={{0,4},{2,6},{4,0},{6,2},{8,12},{10,14},{12,8},{14,10},{16,20},{18,... | collective-permute-start | bytes 884744 | tf_op jit(solution)/shard_map/ppermute | solution.py:18
  70.0 13.1 %copy-start.12 = (bf16[192,768]{1,0:T(8,128)(2,1)}, bf16[192,768]{1,0:T(8,128)(2,1)S(1)}, u32[]{:S(2)}) copy-start(bf16[192,768]{1,0:T(8,128)(2,1)S(1)} %collective-permute-done.12.refs_8_) | copy-start | bytes 884740
  70.0 31.5 %collective-permute-start.14 = (bf16[192,768]{1,0:T(8,128)(2,1)S(1)}, bf16[192,768]{1,0:T(8,128)(2,1)S(1)}, u32[]{:S(2)}, u32[]{:S(2)}) collective-permute-start(bf16[192,768]{1,0:T(8,128)(2,1)S(1)} %collective-permute-done.12.refs_8_), channel_id=1, source_target_pairs={{0,4},{2,6},{4,0},{6,2},{8,12},{10,14},{12,8},{14,10},{16,20},{18,... | collective-permute-start | bytes 884744 | tf_op jit(solution)/shard_map/ppermute | solution.py:18
  74.1 9.0 %copy-start.13 = (bf16[192,768]{1,0:T(8,128)(2,1)}, bf16[192,768]{1,0:T(8,128)(2,1)S(1)}, u32[]{:S(2)}) copy-start(bf16[192,768]{1,0:T(8,128)(2,1)S(1)} %collective-permute-done.16.refs_12_) | copy-start | bytes 884740
  74.1 34.7 %collective-permute-start.18 = (bf16[192,768]{1,0:T(8,128)(2,1)S(1)}, bf16[192,768]{1,0:T(8,128)(2,1)S(1)}, u32[]{:S(2)}, u32[]{:S(2)}) collective-permute-start(bf16[192,768]{1,0:T(8,128)(2,1)S(1)} %collective-permute-done.16.refs_12_), channel_id=1, source_target_pairs={{0,4},{2,6},{4,0},{6,2},{8,12},{10,14},{12,8},{14,10},{16,20},{18,... | collective-permute-start | bytes 884744 | tf_op jit(solution)/shard_map/ppermute | solution.py:18
  75.6 41.3 %collective-permute-start.22 = (bf16[192,768]{1,0:T(8,128)(2,1)S(1)}, bf16[192,768]{1,0:T(8,128)(2,1)S(1)}, u32[]{:S(2)}, u32[]{:S(2)}) collective-permute-start(bf16[192,768]{1,0:T(8,128)(2,1)S(1)} %collective-permute-done.20.refs_16_), channel_id=1, source_target_pairs={{0,4},{2,6},{4,0},{6,2},{8,12},{10,14},{12,8},{14,10},{16,20},{18,... | collective-permute-start | bytes 884744 | tf_op jit(solution)/shard_map/ppermute | solution.py:18
  83.1 40.5 %collective-permute-start.13 = (bf16[192,768]{1,0:T(8,128)(2,1)}, bf16[192,768]{1,0:T(8,128)(2,1)S(1)}, u32[]{:S(2)}, u32[]{:S(2)}) collective-permute-start(bf16[192,768]{1,0:T(8,128)(2,1)} %shard_map.63), channel_id=1, source_target_pairs={{0,8},{2,10},{4,12},{6,14},{8,0},{10,2},{12,4},{14,6},{16,24},{18,... | collective-permute-start | bytes 884744 | tf_op jit(solution)/shard_map/ppermute | solution.py:18
  100.4 8.4 %copy-start.15 = (bf16[192,768]{1,0:T(8,128)(2,1)}, bf16[192,768]{1,0:T(8,128)(2,1)S(1)}, u32[]{:S(2)}) copy-start(bf16[192,768]{1,0:T(8,128)(2,1)S(1)} %collective-permute-done.10.refs_6_) | copy-start | bytes 884740
  100.4 27.4 %collective-permute-start.17 = (bf16[192,768]{1,0:T(8,128)(2,1)}, bf16[192,768]{1,0:T(8,128)(2,1)S(1)}, u32[]{:S(2)}, u32[]{:S(2)}) collective-permute-start(bf16[192,768]{1,0:T(8,128)(2,1)} %shard_map.65), channel_id=1, source_target_pairs={{0,16},{2,18},{4,20},{6,22},{8,24},{10,26},{12,28},{14,30},{16,0},... | collective-permute-start | bytes 884744 | tf_op jit(solution)/shard_map/ppermute | solution.py:18
  101.5 26.8 %collective-permute-start.21 = (bf16[192,768]{1,0:T(8,128)(2,1)S(1)}, bf16[192,768]{1,0:T(8,128)(2,1)S(1)}, u32[]{:S(2)}, u32[]{:S(2)}) collective-permute-start(bf16[192,768]{1,0:T(8,128)(2,1)S(1)} %copy-done.3), channel_id=1, source_target_pairs={{0,24},{2,26},{4,28},{6,30},{8,16},{10,18},{12,20},{14,22},{16,8},... | collective-permute-start | bytes 884744 | tf_op jit(solution)/shard_map/ppermute | solution.py:18
  108.8 14.2 %collective-permute-start.26 = (bf16[192,384]{1,0:T(8,128)(2,1)}, bf16[192,384]{1,0:T(8,128)(2,1)S(1)}, u32[]{:S(2)}, u32[]{:S(2)}) collective-permute-start(bf16[192,384]{1,0:T(8,128)(2,1)} %get-tuple-element.35), channel_id=1, source_target_pairs={{0,24},{2,26},{4,28},{6,30},{8,16},{10,18},{12,20},{14,22},{16,8},... | collective-permute-start | bytes 442376 | tf_op jit(solution)/shard_map/ppermute | solution.py:18
  117.0 23.3 %collective-permute-start.25 = (bf16[192,384]{1,0:T(8,128)(2,1)}, bf16[192,384]{1,0:T(8,128)(2,1)S(1)}, u32[]{:S(2)}, u32[]{:S(2)}) collective-permute-start(bf16[192,384]{1,0:T(8,128)(2,1)} %get-tuple-element.34), channel_id=1, source_target_pairs={{0,16},{2,18},{4,20},{6,22},{8,24},{10,26},{12,28},{14,30},{16,0},... | collective-permute-start | bytes 442376 | tf_op jit(solution)/shard_map/ppermute | solution.py:18
  123.1 12.5 %copy-start.28 = (bf16[192,384]{1,0:T(8,128)(2,1)}, bf16[192,384]{1,0:T(8,128)(2,1)S(1)}, u32[]{:S(2)}) copy-start(bf16[192,384]{1,0:T(8,128)(2,1)S(1)} %collective-permute-done.26.refs_3_) | copy-start | bytes 442372
  123.1 33.0 %collective-permute-start.11 = (bf16[192,768]{1,0:T(8,128)(2,1)}, bf16[192,768]{1,0:T(8,128)(2,1)S(1)}, u32[]{:S(2)}, u32[]{:S(2)}) collective-permute-start(bf16[192,768]{1,0:T(8,128)(2,1)} %shard_map.61.refs_5_), channel_id=1, source_target_pairs={{0,4},{2,6},{4,0},{6,2},{8,12},{10,14},{12,8},{14,10},{16,20},{18,... | collective-permute-start | bytes 884744 | tf_op jit(solution)/shard_map/ppermute | solution.py:18
  123.6 11.9 %copy-start.19 = (bf16[192,768]{1,0:T(8,128)(2,1)}, bf16[192,768]{1,0:T(8,128)(2,1)S(1)}, u32[]{:S(2)}) copy-start(bf16[192,768]{1,0:T(8,128)(2,1)S(1)} %collective-permute-done.13.refs_9_) | copy-start | bytes 884740
  123.6 32.5 %collective-permute-start.15 = (bf16[192,768]{1,0:T(8,128)(2,1)S(1)}, bf16[192,768]{1,0:T(8,128)(2,1)S(1)}, u32[]{:S(2)}, u32[]{:S(2)}) collective-permute-start(bf16[192,768]{1,0:T(8,128)(2,1)S(1)} %collective-permute-done.13.refs_9_), channel_id=1, source_target_pairs={{0,4},{2,6},{4,0},{6,2},{8,12},{10,14},{12,8},{14,10},{16,20},{18,... | collective-permute-start | bytes 884744 | tf_op jit(solution)/shard_map/ppermute | solution.py:18
  127.8 30.4 %collective-permute-start.19 = (bf16[192,768]{1,0:T(8,128)(2,1)S(1)}, bf16[192,768]{1,0:T(8,128)(2,1)S(1)}, u32[]{:S(2)}, u32[]{:S(2)}) collective-permute-start(bf16[192,768]{1,0:T(8,128)(2,1)S(1)} %collective-permute-done.17.refs_13_), channel_id=1, source_target_pairs={{0,4},{2,6},{4,0},{6,2},{8,12},{10,14},{12,8},{14,10},{16,20},{18,... | collective-permute-start | bytes 884744 | tf_op jit(solution)/shard_map/ppermute | solution.py:18
  128.3 29.9 %collective-permute-start.23 = (bf16[192,768]{1,0:T(8,128)(2,1)S(1)}, bf16[192,768]{1,0:T(8,128)(2,1)S(1)}, u32[]{:S(2)}, u32[]{:S(2)}) collective-permute-start(bf16[192,768]{1,0:T(8,128)(2,1)S(1)} %collective-permute-done.21.refs_17_), channel_id=1, source_target_pairs={{0,4},{2,6},{4,0},{6,2},{8,12},{10,14},{12,8},{14,10},{16,20},{18,... | collective-permute-start | bytes 884744 | tf_op jit(solution)/shard_map/ppermute | solution.py:18
  140.3 13.2 %copy-start.29 = (bf16[192,384]{1,0:T(8,128)(2,1)}, bf16[192,384]{1,0:T(8,128)(2,1)S(1)}, u32[]{:S(2)}) copy-start(bf16[192,384]{1,0:T(8,128)(2,1)S(1)} %collective-permute-done.25.refs_2_) | copy-start | bytes 442372
  140.3 13.2 %copy-start.26 = (bf16[192,384]{1,0:T(8,128)(2,1)S(1)}, bf16[192,384]{1,0:T(8,128)(2,1)}, u32[]{:S(2)}) copy-start(bf16[192,384]{1,0:T(8,128)(2,1)} %get-tuple-element.28) | copy-start | bytes 442372
  140.3 15.7 %copy-start.27 = (bf16[192,384]{1,0:T(8,128)(2,1)S(1)}, bf16[192,384]{1,0:T(8,128)(2,1)}, u32[]{:S(2)}) copy-start(bf16[192,384]{1,0:T(8,128)(2,1)} %get-tuple-element.27) | copy-start | bytes 442372
  140.3 15.8 %copy-start.31 = (bf16[192,384]{1,0:T(8,128)(2,1)S(1)}, bf16[192,384]{1,0:T(8,128)(2,1)}, u32[]{:S(2)}) copy-start(bf16[192,384]{1,0:T(8,128)(2,1)} %get-tuple-element.26) | copy-start | bytes 442372
  140.3 13.2 %collective-permute-start.24 = (bf16[192,384]{1,0:T(8,128)(2,1)}, bf16[192,384]{1,0:T(8,128)(2,1)S(1)}, u32[]{:S(2)}, u32[]{:S(2)}) collective-permute-start(bf16[192,384]{1,0:T(8,128)(2,1)} %get-tuple-element.33), channel_id=1, source_target_pairs={{0,8},{2,10},{4,12},{6,14},{8,0},{10,2},{12,4},{14,6},{16,24},{18,... | collective-permute-start | bytes 442376 | tf_op jit(solution)/shard_map/ppermute | solution.py:18
  153.6 27.1 %collective-permute-start.9 = (bf16[192,384]{1,0:T(8,128)(2,1)S(1)}, bf16[192,384]{1,0:T(8,128)(2,1)S(1)}, u32[]{:S(2)}, u32[]{:S(2)}) collective-permute-start(bf16[192,384]{1,0:T(8,128)(2,1)S(1)} %copy-done.26), channel_id=1, source_target_pairs={{0,24},{2,26},{4,28},{6,30},{8,16},{10,18},{12,20},{14,22},{16,8},... | collective-permute-start | bytes 442376 | tf_op jit(solution)/shard_map/ppermute | solution.py:18
  156.0 25.6 %collective-permute-start.8 = (bf16[192,384]{1,0:T(8,128)(2,1)S(1)}, bf16[192,384]{1,0:T(8,128)(2,1)S(1)}, u32[]{:S(2)}, u32[]{:S(2)}) collective-permute-start(bf16[192,384]{1,0:T(8,128)(2,1)S(1)} %copy-done.27), channel_id=1, source_target_pairs={{0,16},{2,18},{4,20},{6,22},{8,24},{10,26},{12,28},{14,30},{16,0},... | collective-permute-start | bytes 442376 | tf_op jit(solution)/shard_map/ppermute | solution.py:18
  156.1 26.7 %collective-permute-start.7 = (bf16[192,384]{1,0:T(8,128)(2,1)S(1)}, bf16[192,384]{1,0:T(8,128)(2,1)S(1)}, u32[]{:S(2)}, u32[]{:S(2)}) collective-permute-start(bf16[192,384]{1,0:T(8,128)(2,1)S(1)} %copy-done.31), channel_id=1, source_target_pairs={{0,8},{2,10},{4,12},{6,14},{8,0},{10,2},{12,4},{14,6},{16,24},{18,... | collective-permute-start | bytes 442376 | tf_op jit(solution)/shard_map/ppermute | solution.py:18
  172.9 25.8 %collective-permute-start.27 = (bf16[192,384]{1,0:T(8,128)(2,1)}, bf16[192,384]{1,0:T(8,128)(2,1)S(1)}, u32[]{:S(2)}, u32[]{:S(2)}) collective-permute-start(bf16[192,384]{1,0:T(8,128)(2,1)} %get-tuple-element.36), channel_id=1, source_target_pairs={{0,2},{2,0},{4,6},{6,4},{8,10},{10,8},{12,14},{14,12},{16,18},{18,... | collective-permute-start | bytes 442376 | tf_op jit(solution)/shard_map/ppermute | solution.py:18
  173.0 27.6 %collective-permute-start.29 = (bf16[192,384]{1,0:T(8,128)(2,1)}, bf16[192,384]{1,0:T(8,128)(2,1)S(1)}, u32[]{:S(2)}, u32[]{:S(2)}) collective-permute-start(bf16[192,384]{1,0:T(8,128)(2,1)} %get-tuple-element.38), channel_id=1, source_target_pairs={{0,10},{2,8},{4,14},{6,12},{8,2},{10,0},{12,6},{14,4},{16,26},{18,... | collective-permute-start | bytes 442376 | tf_op jit(solution)/shard_map/ppermute | solution.py:18
  180.7 21.4 %collective-permute-start.31 = (bf16[192,384]{1,0:T(8,128)(2,1)}, bf16[192,384]{1,0:T(8,128)(2,1)S(1)}, u32[]{:S(2)}, u32[]{:S(2)}) collective-permute-start(bf16[192,384]{1,0:T(8,128)(2,1)} %get-tuple-element.40), channel_id=1, source_target_pairs={{0,18},{2,16},{4,22},{6,20},{8,26},{10,24},{12,30},{14,28},{16,2},... | collective-permute-start | bytes 442376 | tf_op jit(solution)/shard_map/ppermute | solution.py:18
  181.6 20.4 %collective-permute-start.33 = (bf16[192,384]{1,0:T(8,128)(2,1)}, bf16[192,384]{1,0:T(8,128)(2,1)S(1)}, u32[]{:S(2)}, u32[]{:S(2)}) collective-permute-start(bf16[192,384]{1,0:T(8,128)(2,1)} %get-tuple-element.42), channel_id=1, source_target_pairs={{0,26},{2,24},{4,30},{6,28},{8,18},{10,16},{12,22},{14,20},{16,10}... | collective-permute-start | bytes 442376 | tf_op jit(solution)/shard_map/ppermute | solution.py:18
  197.6 8.9 %collective-permute-start.28 = (bf16[192,384]{1,0:T(8,128)(2,1)}, bf16[192,384]{1,0:T(8,128)(2,1)S(1)}, u32[]{:S(2)}, u32[]{:S(2)}) collective-permute-start(bf16[192,384]{1,0:T(8,128)(2,1)} %get-tuple-element.37), channel_id=1, source_target_pairs={{0,8},{2,10},{4,12},{6,14},{8,0},{10,2},{12,4},{14,6},{16,24},{18,... | collective-permute-start | bytes 442376 | tf_op jit(solution)/shard_map/ppermute | solution.py:18
  198.7 14.2 %copy-start.4 = (bf16[192,384]{1,0:T(8,128)(2,1)}, bf16[192,384]{1,0:T(8,128)(2,1)S(1)}, u32[]{:S(2)}) copy-start(bf16[192,384]{1,0:T(8,128)(2,1)S(1)} %collective-permute-done.27.refs_1_) | copy-start | bytes 442372
  198.7 14.2 %collective-permute-start.30 = (bf16[192,384]{1,0:T(8,128)(2,1)}, bf16[192,384]{1,0:T(8,128)(2,1)S(1)}, u32[]{:S(2)}, u32[]{:S(2)}) collective-permute-start(bf16[192,384]{1,0:T(8,128)(2,1)} %get-tuple-element.39), channel_id=1, source_target_pairs={{0,16},{2,18},{4,20},{6,22},{8,24},{10,26},{12,28},{14,30},{16,0},... | collective-permute-start | bytes 442376 | tf_op jit(solution)/shard_map/ppermute | solution.py:18
  200.6 12.3 %copy-start.5 = (bf16[192,384]{1,0:T(8,128)(2,1)}, bf16[192,384]{1,0:T(8,128)(2,1)S(1)}, u32[]{:S(2)}) copy-start(bf16[192,384]{1,0:T(8,128)(2,1)S(1)} %collective-permute-done.29.refs_3_) | copy-start | bytes 442372
  200.6 12.3 %collective-permute-start.32 = (bf16[192,384]{1,0:T(8,128)(2,1)}, bf16[192,384]{1,0:T(8,128)(2,1)S(1)}, u32[]{:S(2)}, u32[]{:S(2)}) collective-permute-start(bf16[192,384]{1,0:T(8,128)(2,1)} %get-tuple-element.41), channel_id=1, source_target_pairs={{0,24},{2,26},{4,28},{6,30},{8,16},{10,18},{12,20},{14,22},{16,8},... | collective-permute-start | bytes 442376 | tf_op jit(solution)/shard_map/ppermute | solution.py:18
  202.1 10.9 %copy-start.6 = (bf16[192,384]{1,0:T(8,128)(2,1)}, bf16[192,384]{1,0:T(8,128)(2,1)S(1)}, u32[]{:S(2)}) copy-start(bf16[192,384]{1,0:T(8,128)(2,1)S(1)} %collective-permute-done.31.refs_5_) | copy-start | bytes 442372
  202.1 10.9 %copy-start.7 = (bf16[192,384]{1,0:T(8,128)(2,1)}, bf16[192,384]{1,0:T(8,128)(2,1)S(1)}, u32[]{:S(2)}) copy-start(bf16[192,384]{1,0:T(8,128)(2,1)S(1)} %collective-permute-done.33.refs_7_) | copy-start | bytes 442372
  (22 other events, 80.2 us)

commit v4 on v3

--- a/solution.py
+++ b/solution.py
@@ -12,6 +12,7 @@
 LOG2_E = 1.4426950408889634
 HIDDEN = -1e30
 VMEM_LIMIT = 56 * 2**20
+PAD = 8
 
 
 def exchange(value, axis, size, bit):
@@ -19,59 +20,68 @@
 
 
 def own_body(weights, place, mine_ref, other_ref, *refs):
-    flat_ref = refs[-1]
     rows = other_ref.shape[0]
-
-    @pl.when(pl.program_id(0) == 0)
-    def _():
-        flat_ref[:rows] = mine_ref[0]
-        flat_ref[rows:] = other_ref[...]
-
-    for weight_ref, out_ref in zip(refs[:weights], refs[weights:-1]):
-        result = jnp.dot(flat_ref[...], weight_ref[...], preferred_element_type=jnp.float32)
-        out_ref[0] = result.reshape(2, rows, -1)
-
-
-def own_products(hidden_in, other, weights, place, ways):
+    flat = jnp.concatenate([mine_ref[0], other_ref[...]], axis=0)
+    step = pl.program_id(0)
+    for weight_ref, out_ref in zip(refs[:weights], refs[weights:]):
+        result = jnp.dot(flat, weight_ref[...], preferred_element_type=jnp.float32)
+        result = result.reshape(2, rows, -1)
+
+        @pl.when(step == 0)
+        def _():
+            out_ref[...] = result
+
+        @pl.when(step > 0)
+        def _():
+            out_ref[...] += result
+
+
+def own_products(hidden_in, other, weights, place):
     rows, feats = other.shape
-    width = weights[0].shape[1] // ways
+    features = weights[0].shape[1]
+    steps = max(1, feats // 512)
+    depth = feats // steps
     return pl.pallas_call(
         functools.partial(own_body, len(weights)),
-        out_shape=[jax.ShapeDtypeStruct((ways, 2, rows, width), jnp.float32)] * len(weights),
+        out_shape=[jax.ShapeDtypeStruct((2, rows, features), jnp.float32)] * len(weights),
         grid_spec=pltpu.PrefetchScalarGridSpec(
             num_scalar_prefetch=1,
-            grid=(ways,),
+            grid=(steps,),
             in_specs=[
-                pl.BlockSpec((1, rows, feats), lambda g, place: (place[2], 0, 0)),
-                pl.BlockSpec((rows, feats), lambda g, place: (0, 0)),
+                pl.BlockSpec((1, rows, depth), lambda i, place: (place[2], 0, i)),
+                pl.BlockSpec((rows, depth), lambda i, place: (0, i)),
             ]
-            + [pl.BlockSpec((feats, width), lambda g, place: (place[0], place[1] ^ g))] * len(weights),
-            out_specs=[pl.BlockSpec((1, 2, rows, width), lambda g, place: (g, 0, 0, 0))] * len(weights),
-            scratch_shapes=[pltpu.VMEM((2 * rows, feats), jnp.bfloat16)],
+            + [pl.BlockSpec((depth, features), lambda i, place: (place[0] * steps + i, 0))] * len(weights),
+            out_specs=[pl.BlockSpec((2, rows, features), lambda i, place: (0, 0, 0))] * len(weights),
         ),
         compiler_params=pltpu.CompilerParams(vmem_limit_bytes=VMEM_LIMIT),
         cost_estimate=pl.CostEstimate(
-            flops=4 * rows * feats * width * ways * len(weights),
-            bytes_accessed=2 * feats * width * ways * len(weights),
+            flops=4 * rows * feats * features * len(weights),
+            bytes_accessed=2 * feats * features * len(weights),
             transcendentals=0,
         ),
     )(place, hidden_in, other, *weights)
 
 
-def rest_body(shares, steps, weights, chunks, place, *refs):
+def rest_body(shares, steps, weights, chosen, ways, place, *refs):
+    chunks = len(chosen)
     inputs = refs[: shares * chunks]
     weight_refs = refs[shares * chunks : shares * chunks + weights]
-    start_refs = refs[shares * chunks + weights : shares * chunks + 2 * weights]
-    out_refs = refs[shares * chunks + 2 * weights : shares * chunks + 2 * weights + chunks]
-    totals = refs[shares * chunks + 2 * weights + chunks :]
+    refs = refs[shares * chunks + weights :]
+    start_refs, out_refs, refs = refs[:weights], refs[weights : weights + chunks * ways], refs[weights + chunks * ways :]
+    totals, earlier, sems = refs[:weights], refs[weights : 2 * weights], refs[2 * weights]
     rows = out_refs[0].shape[0]
     width = out_refs[0].shape[1] // weights
     step = pl.program_id(0)
+    copies = [
+        pltpu.make_async_copy(start_refs[n].at[pl.ds(chosen[0], chunks)], earlier[n], sems.at[n])
+        for n in range(weights)
+    ]
 
     @pl.when(step == 0)
     def _():
-        for total, start in zip(totals, start_refs):
-            total[...] = start[...].reshape(chunks * rows, width)
+        for copy in copies:
+            copy.start()
 
     for share in range(shares):
 
@@ -80,23 +90,36 @@
             flat = [inputs[c * shares + share][...] for c in range(chunks)]
             flat = flat[0] if chunks == 1 else jnp.concatenate(flat, axis=0)
             for total, weight in zip(totals, weight_refs):
-                total[...] += jnp.dot(flat, weight[...], preferred_element_type=jnp.float32)
+                result = jnp.dot(flat, weight[...], preferred_element_type=jnp.float32)
+                result = result.reshape(chunks, rows, -1)
+
+                @pl.when(step == 0)
+                def _():
+                    total[...] = result
+
+                @pl.when(step > 0)
+                def _():
+                    total[...] += result
 
     @pl.when(step == shares * steps - 1)
     def _():
-        for n, total in enumerate(totals):
-            for c, out_ref in enumerate(out_refs):
-                out_ref[:, n * width : (n + 1) * width] = total[c * rows : (c + 1) * rows].astype(
-                    out_ref.dtype
-                )
-
-
-def rest_products(received, chosen, weights, starts, place, a, ways):
+        for copy in copies:
+            copy.wait()
+        for a in range(ways):
+            columns = pl.ds(pl.multiple_of((place[1] ^ a) * width, HD), width)
+            for n in range(weights):
+                for c in range(chunks):
+                    done = totals[n][c, :, columns] + earlier[n][c, :, columns]
+                    out_refs[c * ways + a][:, n * width : (n + 1) * width] = done.astype(jnp.bfloat16)
+
+
+def rest_products(received, chosen, weights, starts, place, ways):
     shares = len(received[0])
     rows, feats = received[0][0].shape
-    width = weights[0].shape[1] // ways
+    features = weights[0].shape[1]
+    width = features // ways
     chunks = len(chosen)
-    steps = max(1, feats // 640)
+    steps = max(1, feats // 512)
     depth = feats // steps
 
     def share_map(share, i, place):
@@ -110,31 +133,31 @@
             operands.append(received[c][share])
     in_specs += [
         pl.BlockSpec(
-            (depth, width),
-            lambda i, place: ((place[0] ^ (i // steps + 1)) * steps + i % steps, place[1] ^ a),
+            (depth, features),
+            lambda i, place: ((place[0] ^ (i // steps + 1)) * steps + i % steps, 0),
         )
     ] * len(weights)
-    in_specs += [
-        pl.BlockSpec((1, chunks, rows, width), lambda i, place: (a, chosen[0] // chunks, 0, 0))
-    ] * len(weights)
+    in_specs += [pl.BlockSpec(memory_space=pl.ANY)] * len(weights)
     columns = width * len(weights)
-    return pl.pallas_call(
-        functools.partial(rest_body, shares, steps, len(weights), chunks),
-        out_shape=[jax.ShapeDtypeStruct((rows, columns), jnp.bfloat16)] * chunks,
+    outs = pl.pallas_call(
+        functools.partial(rest_body, shares, steps, len(weights), chosen, ways),
+        out_shape=[jax.ShapeDtypeStruct((rows, columns), jnp.bfloat16)] * (chunks * ways),
         grid_spec=pltpu.PrefetchScalarGridSpec(
             num_scalar_prefetch=1,
             grid=(shares * steps,),
             in_specs=in_specs,
-            out_specs=[pl.BlockSpec((rows, columns), lambda i, place: (0, 0))] * chunks,
-            scratch_shapes=[pltpu.VMEM((chunks * rows, width), jnp.float32)] * len(weights),
+            out_specs=[pl.BlockSpec((rows, columns), lambda i, place: (0, 0))] * (chunks * ways),
+            scratch_shapes=[pltpu.VMEM((chunks, rows, features), jnp.float32)] * (2 * len(weights))
+            + [pltpu.SemaphoreType.DMA((len(weights),))],
         ),
         compiler_params=pltpu.CompilerParams(vmem_limit_bytes=VMEM_LIMIT),
         cost_estimate=pl.CostEstimate(
-            flops=2 * chunks * rows * feats * shares * columns,
-            bytes_accessed=2 * feats * shares * columns,
+            flops=2 * chunks * rows * feats * shares * features * len(weights),
+            bytes_accessed=2 * feats * shares * features * len(weights),
             transcendentals=0,
         ),
     )(place, *operands, *weights, *starts)
+    return [outs[c * ways : (c + 1) * ways] for c in range(chunks)]
 
 
 def attend_body(block, ways, offsets, spans, tile, table, place, *refs):
@@ -151,7 +174,7 @@
 
     copies = []
     for slot, offset in enumerate(offsets):
-        low = table[offset, seq]
+        low = table[place[3] ^ offset, seq]
         for part, span in ((0, low), (1, spans - 1 - low)):
             copies.append(
                 pltpu.make_async_copy(
@@ -167,7 +190,7 @@
         jnp.int32, (half, 128), 1
     )
     for a in range(ways):
-        low = table[a * rest + block, seq]
+        low = table[place[3] ^ (a * rest + block), seq]
         here = slice(a * half, (a + 1) * half)
         for part, span in ((0, low), (1, spans - 1 - low)):
             asked[part, here] = query_refs[a][part * half : (part + 1) * half]
@@ -269,30 +292,33 @@
     )(table, place, *queries, *[blocks[i] for i in offsets])
 
 
-def assemble_body(slots, place, *refs):
-    for n in range(slots):
-
-        @pl.when(pl.program_id(0) == n)
-        def _():
-            refs[-1][0] = refs[n][...]
+def assemble_body(ways, sequences, place, *refs):
+    out_ref, sems = refs[-2:]
+    width = refs[0].shape[1]
+    copies = []
+    for a in range(ways):
+        for b in range(sequences):
+            n = a * sequences + b
+            columns = pl.ds(pl.multiple_of((place[1] ^ a) * width, HD), width)
+            copies.append(
+                pltpu.make_async_copy(refs[n], out_ref.at[place[2] ^ b, :, columns], sems.at[n])
+            )
+    for copy in copies:
+        copy.start()
+    for copy in copies:
+        copy.wait()
 
 
 def assemble(pieces, place):
     ways, sequences = len(pieces), len(pieces[0])
     rows, width = pieces[0][0].shape
     return pl.pallas_call(
-        functools.partial(assemble_body, ways * sequences),
+        functools.partial(assemble_body, ways, sequences),
         out_shape=jax.ShapeDtypeStruct((sequences, rows, ways * width), jnp.bfloat16),
-        grid_spec=pltpu.PrefetchScalarGridSpec(
-            num_scalar_prefetch=1,
-            grid=(ways * sequences,),
-            in_specs=[pl.BlockSpec((rows, width), lambda n, place: (0, 0))] * (ways * sequences),
-            out_specs=pl.BlockSpec(
-                (1, rows, width),
-                lambda n, place: (place[2] ^ (n % sequences), 0, place[1] ^ (n // sequences)),
-            ),
-        ),
-        compiler_params=pltpu.CompilerParams(vmem_limit_bytes=VMEM_LIMIT),
+        in_specs=[pl.BlockSpec(memory_space=pltpu.SMEM)]
+        + [pl.BlockSpec(memory_space=pl.ANY)] * (ways * sequences),
+        out_specs=pl.BlockSpec(memory_space=pl.ANY),
+        scratch_shapes=[pltpu.SemaphoreType.DMA((ways * sequences,))],
     )(place, *[piece for row in pieces for piece in row])
 
 
@@ -322,30 +348,27 @@
     other = over_ctx(lax.dynamic_index_in_dim(hidden_in, 1 - core, 0, keepdims=False), 1)
     received = [other_shares(mine), other_shares(other)]
 
-    table = event_pos[None, :, 0] // (rows // 2)
-    bit = 1
-    while bit < ctx_size:
-        table = jnp.concatenate([table, over_ctx(table, bit)], axis=0)
-        bit *= 2
-
-    start_k, start_v, start_q = own_products(hidden_in, other, [w_k, w_v, w_q], place, ways)
-    place_later = jnp.concatenate([place, table.reshape(-1)])
+    firsts = jnp.broadcast_to((event_pos[:, 0] // (rows // 2))[None, :, None, None], (1, 2, PAD, 128))
+    firsts = lax.optimization_barrier(lax.all_gather(lax.optimization_barrier(firsts), "ctx", axis=0, tiled=True))
+    table = firsts[:, :, 0, 0]
+
+    start_k, start_v, start_q = own_products(hidden_in, other, [w_k, w_v, w_q], place)
 
     blocks = {}
     for b in range(2):
+        (made,) = rest_products(received, [b], [w_k, w_v], [start_k, start_v], place, ways)
         for a in away:
-            (made,) = rest_products(received, [b], [w_k, w_v], [start_k, start_v], place_later, a, ways)
-            blocks[a * rest + b] = over_ctx(made, a * rest)
+            blocks[a * rest + b] = over_ctx(made[a], a * rest)
     bit = rest // 2
     while bit > 1:
         for i in list(blocks):
             blocks[i ^ bit] = over_ctx(blocks[i], bit)
         bit //= 2
     queries = [[None] * ways, [None] * ways]
-    for a in away:
-        made = rest_products(received, [0, 1], [w_q], [start_q], place_later, a, ways)
-        for b in range(2):
-            queries[b][a] = over_ctx(made[b], a * rest)
+    made = rest_products(received, [0, 1], [w_q], [start_q], place, ways)
+    for b in range(2):
+        for a in away:
+            queries[b][a] = over_ctx(made[b][a], a * rest)
     pieces = [[None] * 2 for _ in range(ways)]
     for b in range(2):
         outs = attend(b, queries[b], blocks, table, place)

time: 220 us -> 240 us (1.091)
  blocking collectives: 0 us -> 22.1 us
  waiting for transfers between devices: 26.6 us -> 41.8 us
  starting transfers between devices: 61 us -> 45.9 us
  Pallas kernels: 122 us -> 119 us
    pallas_call x12 -> x3, Pallas kernels: 70.6 us -> 32.9 us  [rest_products(): pl.pallas_call(functools.partial(rest_body, shares, steps, len(weights),...]
    pallas_call x1, Pallas kernels: 4.96 us -> 37.6 us  [assemble(): pl.pallas_call(functools.partial(assemble_body, ways, sequences), out_sha...]
    all_gather x0 -> x1, blocking collectives: none -> 22.1 us  [on_device(): lax.all_gather(lax.optimization_barrier(firsts), 'ctx', axis=0, tiled=True)]
    ppermute x34 -> x30, waiting for transfers between devices: 26.6 us -> 41.8 us  [exchange(): return lax.ppermute(value, axis, [(i, i ^ bit) for i in range(size)])]
    ppermute x34 -> x30, starting transfers between devices: 61 us -> 45.9 us  [exchange(): return lax.ppermute(value, axis, [(i, i ^ bit) for i in range(size)])]
  transfers between devices with their start and end apart: 34 -> 30, of which waited for: 8 -> 7; matrix products, arithmetic and copies ran while one was open for 1% -> 1% of each run, Pallas kernels for 54% -> 34%
where the time goes in v4:
time: 240 us; the launch traced here: 238 us
  Pallas kernels  119 us (50%)
  starting transfers between devices  45.9 us (19%)
  waiting for transfers between devices  41.8 us (17%)
  blocking collectives  22.1 us (9%)
  local copies, waits for them, and re-layouts  7.55 us (3%)
    ppermute x30, starting transfers between devices, exchange(): return lax.ppermute(value, axis, [(i, i ^ bit) for i in range(size)])  45.9 us
    ppermute x30, waiting for transfers between devices, exchange(): return lax.ppermute(value, axis, [(i, i ^ bit) for i in range(size)])  41.8 us
    pallas_call x1, Pallas kernels, assemble(): pl.pallas_call(functools.partial(assemble_body, ways, sequences), out_sha...  37.6 us
    pallas_call x3, Pallas kernels, rest_products(): pl.pallas_call(functools.partial(rest_body, shares, steps, len(weights),...  32.9 us
    pallas_call x2, Pallas kernels, attend(): pl.pallas_call(functools.partial(attend_body, block, ways, offsets, spans...  28 us
    all_gather x1, blocking collectives, on_device(): lax.all_gather(lax.optimization_barrier(firsts), 'ctx', axis=0, tiled=True)  22.1 us
    pallas_call x1, Pallas kernels, own_products(): pl.pallas_call(functools.partial(own_body, len(weights)), out_shape=[jax....  21 us
  transfers between devices with their start and end apart: 30, of which 7 were waited for; matrix products, arithmetic and copies ran while one was open for 1% of the time, Pallas kernels for 34%

profile of v4, /device:TPU:0, one launch (start us, length us, event | category | flops | bytes accessed | tf_op | source)
XLA Modules:
  0.0 238.3 jit_solution(15086219774710145493)
XLA Ops:
  0.0 2.6 %dynamic-slice_bitcast_fusion = (bf16[192,2560]{1,0:T(8,128)(2,1)}, bf16[192,2560]{1,0:T(8,128)(2,1)S(1)}) fusion(bf16[2,192,2560]{2,1,0:T(8,128)(2,1)} %mine_ref.1, s32[]{:T(128)S(6)} %select_n.31, s32[]{:T(128)S(6)} %select_n.30), kind=kLoop, calls=%fused_computation | loop fusion | bytes 3932168 | tf_op jit(solution)/shard_map/jit(dynamic_index_in_dim)/squeeze | solution.py:348
  2.6 0.5 collective-permute-start.1
  3.0 2.5 %collective-permute-start = (bf16[192,2560]{1,0:T(8,128)(2,1)S(1)}, bf16[192,2560]{1,0:T(8,128)(2,1)S(1)}, u32[]{:S(2)}, u32[]{:S(2)}) collective-permute-start(bf16[192,2560]{1,0:T(8,128)(2,1)S(1)} %get-tuple-element.60), channel_id=1, source_target_pairs={{0,1},{1,0},{2,3},{3,2},{4,5},{5,4},{6,7},{7,6},{8,9},{9,8},{10,11... | collective-permute-start | bytes 2949128 | tf_op jit(solution)/shard_map/ppermute | solution.py:19
  5.5 0.6 pad_add_fusion.place
  6.1 2.1 collective-permute-start.2
  8.3 21.0 %shard_map.55 = (f32[2,192,1536]{2,1,0:T(8,128)}, f32[2,192,1536]{2,1,0:T(8,128)}, f32[2,192,1536]{2,1,0:T(8,128)}) custom-call(s32[4]{0:T(128)} %pad_add_fusion.place, bf16[2,192,2560]{2,1,0:T(8,128)(2,1)} %mine_ref.1, bf16[192,2560]{1,0:T(8,128)(2,1)} %copy-done.2, bf16[5120,1536]{1,0:T(8,128)(2,1)} %refs_1_.5, bf16[5120,1536]{1,0:T(8,128)(2,1)} %refs_2_.7, ...), custom_call_target="tpu_custom_call" | custom-call | flops 9059696640 | bytes 23592960 | tf_op jit(solution)/shard_map/pallas_call | solution.py:44
  29.3 0.9 copy-done
  30.2 11.5 %shard_map.57 = (bf16[192,768]{1,0:T(8,128)(2,1)}, bf16[192,768]{1,0:T(8,128)(2,1)}, bf16[192,768]{1,0:T(8,128)(2,1)}, bf16[192,768]{1,0:T(8,128)(2,1)}) custom-call(s32[4]{0:T(128)} %pad_add_fusion.place, bf16[192,2560]{1,0:T(8,128)(2,1)} %copy-done, bf16[5120,1536]{1,0:T(8,128)(2,1)} %refs_1_.5, bf16[5120,1536]{1,0:T(8,128)(2,1)} %refs_2_.7, ...), custom_call_target="tpu_custom_call" | custom-call | flops 3019898880 | bytes 15728640 | tf_op jit(solution)/shard_map/pallas_call | solution.py:142
  41.7 1.6 collective-permute-start.8
  43.4 2.6 %collective-permute-start.12 = (bf16[192,768]{1,0:T(8,128)(2,1)}, bf16[192,768]{1,0:T(8,128)(2,1)S(1)}, u32[]{:S(2)}, u32[]{:S(2)}) collective-permute-start(bf16[192,768]{1,0:T(8,128)(2,1)} %get-tuple-element.43), channel_id=1, source_target_pairs={{0,16},{2,18},{4,20},{6,22},{8,24},{10,26},{12,28},{14,30},{16,0},... | collective-permute-start | bytes 884744 | tf_op jit(solution)/shard_map/ppermute | solution.py:19
  46.2 1.5 collective-permute-start.6
  47.7 8.6 %collective-permute-done.8.refs_8_ = bf16[192,768]{1,0:T(8,128)(2,1)S(1)} collective-permute-done((bf16[192,768]{1,0:T(8,128)(2,1)}, bf16[192,768]{1,0:T(8,128)(2,1)S(1)}, u32[]{:S(2)}, u32[]{:S(2)}) %collective-permute-start.8) | collective-permute-done | bytes 294944 | tf_op jit(solution)/shard_map/ppermute | solution.py:19
  56.4 1.5 collective-permute-start.10
  57.9 9.2 %collective-permute-done.12.refs_12_ = bf16[192,768]{1,0:T(8,128)(2,1)S(1)} collective-permute-done((bf16[192,768]{1,0:T(8,128)(2,1)}, bf16[192,768]{1,0:T(8,128)(2,1)S(1)}, u32[]{:S(2)}, u32[]{:S(2)}) %collective-permute-start.12) | collective-permute-done | bytes 294944 | tf_op jit(solution)/shard_map/ppermute | solution.py:19
  67.1 1.5 collective-permute-start.14
  68.6 0.5 collective-permute-start.18
  69.1 1.0 copy-done.1
  70.1 11.4 %shard_map.58 = (bf16[192,768]{1,0:T(8,128)(2,1)}, bf16[192,768]{1,0:T(8,128)(2,1)}, bf16[192,768]{1,0:T(8,128)(2,1)}, bf16[192,768]{1,0:T(8,128)(2,1)}) custom-call(s32[4]{0:T(128)} %pad_add_fusion.place, bf16[192,2560]{1,0:T(8,128)(2,1)} %copy-done.1, bf16[5120,1536]{1,0:T(8,128)(2,1)} %refs_1_.5, bf16[5120,1536]{1,0:T(8,128)(2,1)} %refs_2_.7, ...), custom_call_target="tpu_custom_call" | custom-call | flops 3019898880 | bytes 15728640 | tf_op jit(solution)/shard_map/pallas_call | solution.py:142
  81.6 5.0 %collective-permute-start.9 = (bf16[192,768]{1,0:T(8,128)(2,1)}, bf16[192,768]{1,0:T(8,128)(2,1)S(1)}, u32[]{:S(2)}, u32[]{:S(2)}) collective-permute-start(bf16[192,768]{1,0:T(8,128)(2,1)} %get-tuple-element.42), channel_id=1, source_target_pairs={{0,8},{2,10},{4,12},{6,14},{8,0},{10,2},{12,4},{14,6},{16,24},{18,... | collective-permute-start | bytes 884744 | tf_op jit(solution)/shard_map/ppermute | solution.py:19
  86.7 1.1 collective-permute-start.13
  87.8 1.5 collective-permute-start.17
  89.2 10.0 %shard_map.56 = (bf16[192,384]{1,0:T(8,128)(2,1)}, bf16[192,384]{1,0:T(8,128)(2,1)}, bf16[192,384]{1,0:T(8,128)(2,1)}, bf16[192,384]{1,0:T(8,128)(2,1)}, bf16[19...) custom-call(s32[4]{0:T(128)} %pad_add_fusion.place, ...), custom_call_target="tpu_custom_call" | custom-call | flops 3019898880 | bytes 7864320 | tf_op jit(solution)/shard_map/pallas_call | solution.py:142
  99.3 1.0 collective-permute-start.20
  100.3 2.0 collective-permute-start.21
  102.4 6.9 %collective-permute-done.20.refs_1_ = bf16[192,384]{1,0:T(8,128)(2,1)S(1)} collective-permute-done((bf16[192,384]{1,0:T(8,128)(2,1)}, bf16[192,384]{1,0:T(8,128)(2,1)S(1)}, u32[]{:S(2)}, u32[]{:S(2)}) %collective-permute-start.20) | collective-permute-done | bytes 147488 | tf_op jit(solution)/shard_map/ppermute | solution.py:19
  109.3 0.5 collective-permute-start.7
  109.8 1.5 collective-permute-start.11
  111.3 0.7 collective-permute-done.13.refs_13_
  112.0 0.5 collective-permute-start.15
  112.5 1.5 collective-permute-start.19
  114.1 6.6 %collective-permute-done.21.refs_2_ = bf16[192,384]{1,0:T(8,128)(2,1)S(1)} collective-permute-done((bf16[192,384]{1,0:T(8,128)(2,1)}, bf16[192,384]{1,0:T(8,128)(2,1)S(1)}, u32[]{:S(2)}, u32[]{:S(2)}) %collective-permute-start.21) | collective-permute-done | bytes 147488 | tf_op jit(solution)/shard_map/ppermute | solution.py:19
  120.7 3.6 %collective-permute-start.22 = (bf16[192,384]{1,0:T(8,128)(2,1)}, bf16[192,384]{1,0:T(8,128)(2,1)}, u32[]{:S(2)}, u32[]{:S(2)}) collective-permute-start(bf16[192,384]{1,0:T(8,128)(2,1)} %get-tuple-element.51), channel_id=1, source_target_pairs={{0,24},{2,26},{4,28},{6,30},{8,16},{10,18},{12,20},{14,22},{16,8},... | collective-permute-start | bytes 442376 | tf_op jit(solution)/shard_map/ppermute | solution.py:19
  124.4 22.1 %all_gather.3 = s32[16,2,8,128]{3,2,1,0:T(8,128)S(1)} all-gather(s32[1,2,8,128]{3,2,1,0:T(8,128)S(1)} %broadcast_in_dim.2), channel_id=1, replica_groups=mesh['ctx'=16,'tp'=2] {'ctx'}, dimensions={0}, use_global_device_ids=true | all-gather | bytes 139264 | tf_op jit(solution)/shard_map/all_gather | solution.py:352
  146.6 0.7 copy.9.table
  147.3 0.8 collective-permute-start.4
  148.1 3.5 %collective-permute-start.5 = (bf16[192,384]{1,0:T(8,128)(2,1)}, bf16[192,384]{1,0:T(8,128)(2,1)S(1)}, u32[]{:S(2)}, u32[]{:S(2)}) collective-permute-start(bf16[192,384]{1,0:T(8,128)(2,1)} %get-tuple-element.36), channel_id=1, source_target_pairs={{0,24},{2,26},{4,28},{6,30},{8,16},{10,18},{12,20},{14,22},{16,8},... | collective-permute-start | bytes 442376 | tf_op jit(solution)/shard_map/ppermute | solution.py:19
  151.8 0.6 copy-done.23
  152.5 13.9 %shard_map.60 = (bf16[192,384]{1,0:T(8,128)(2,1)}, bf16[192,384]{1,0:T(8,128)(2,1)}, bf16[192,384]{1,0:T(8,128)(2,1)}, bf16[192,384]{1,0:T(8,128)(2,1)}) custom-call(s32[16,2]{1,0:T(8,128)} %copy.9.table, s32[4]{0:T(128)} %pad_add_fusion.place, bf16[192,384]{1,0:T(8,128)(2,1)} %get-tuple-element.48.refs_0_, bf16[192,384]{1,0:T(8,128)(2,1)} %copy-done.25, ...), custom_call_target="tpu_custom_call" | custom-call | flops 2717908992 | bytes 5898240 | tf_op jit(solution)/shard_map/pallas_call | solution.py:268
  166.5 0.5 collective-permute-start.27
  167.1 3.6 %collective-permute-start.29 = (bf16[192,384]{1,0:T(8,128)(2,1)}, bf16[192,384]{1,0:T(8,128)(2,1)S(1)}, u32[]{:S(2)}, u32[]{:S(2)}) collective-permute-start(bf16[192,384]{1,0:T(8,128)(2,1)} %get-tuple-element.58), channel_id=1, source_target_pairs={{0,26},{2,24},{4,30},{6,28},{8,18},{10,16},{12,22},{14,20},{16,10}... | collective-permute-start | bytes 442376 | tf_op jit(solution)/shard_map/ppermute | solution.py:19
  170.7 0.7 copy-done.29
  171.4 14.1 %shard_map.59 = (bf16[192,384]{1,0:T(8,128)(2,1)}, bf16[192,384]{1,0:T(8,128)(2,1)}, bf16[192,384]{1,0:T(8,128)(2,1)}, bf16[192,384]{1,0:T(8,128)(2,1)}) custom-call(s32[16,2]{1,0:T(8,128)} %copy.9.table, s32[4]{0:T(128)} %pad_add_fusion.place, bf16[192,384]{1,0:T(8,128)(2,1)} %get-tuple-element.33.refs_0_, bf16[192,384]{1,0:T(8,128)(2,1)} %copy-done.27, ...), custom_call_target="tpu_custom_call" | custom-call | flops 2717908992 | bytes 5898240 | tf_op jit(solution)/shard_map/pallas_call | solution.py:268
  185.6 0.8 collective-permute-start.26
  186.4 3.5 %collective-permute-start.28 = (bf16[192,384]{1,0:T(8,128)(2,1)}, bf16[192,384]{1,0:T(8,128)(2,1)S(1)}, u32[]{:S(2)}, u32[]{:S(2)}) collective-permute-start(bf16[192,384]{1,0:T(8,128)(2,1)} %get-tuple-element.57), channel_id=1, source_target_pairs={{0,24},{2,26},{4,28},{6,30},{8,16},{10,18},{12,20},{14,22},{16,8},... | collective-permute-start | bytes 442376 | tf_op jit(solution)/shard_map/ppermute | solution.py:19
  190.0 2.9 %collective-permute-done.24.refs_2_ = bf16[192,384]{1,0:T(8,128)(2,1)S(1)} collective-permute-done((bf16[192,384]{1,0:T(8,128)(2,1)}, bf16[192,384]{1,0:T(8,128)(2,1)S(1)}, u32[]{:S(2)}, u32[]{:S(2)}) %collective-permute-start.24) | collective-permute-done | bytes 147488 | tf_op jit(solution)/shard_map/ppermute | solution.py:19
  192.8 7.0 %collective-permute-done.26.refs_4_ = bf16[192,384]{1,0:T(8,128)(2,1)S(1)} collective-permute-done((bf16[192,384]{1,0:T(8,128)(2,1)}, bf16[192,384]{1,0:T(8,128)(2,1)S(1)}, u32[]{:S(2)}, u32[]{:S(2)}) %collective-permute-start.26) | collective-permute-done | bytes 147488 | tf_op jit(solution)/shard_map/ppermute | solution.py:19
  199.9 0.6 copy-done.8
  200.5 37.6 %shard_map.61 = bf16[2,192,1536]{2,1,0:T(8,128)(2,1)} custom-call(s32[4]{0:T(128)} %pad_add_fusion.place, bf16[192,384]{1,0:T(8,128)(2,1)} %get-tuple-element.47.refs_0_, bf16[192,384]{1,0:T(8,128)(2,1)} %copy-done.3, bf16[192,384]{1,0:T(8,128)(2,1)} %copy-done.7, bf16[192,384]{1,0:T(8,128)(2,1)} %copy-done.4, bf16[192,384]{1,0:T(8,128)(2,1)} %copy-done.8, ...), custom_call_target="tpu_custom_call" | custom-call | tf_op jit(solution)/shard_map/pallas_call | solution.py:315
  (91 shorter events, 1.2 us)
Async XLA Ops:
  2.6 3.6 %collective-permute-start.1 = (bf16[192,2560]{1,0:T(8,128)(2,1)}, bf16[192,2560]{1,0:T(8,128)(2,1)S(1)}, u32[]{:S(2)}, u32[]{:S(2)}) collective-permute-start(bf16[192,2560]{1,0:T(8,128)(2,1)} %get-tuple-element.59), channel_id=1, source_target_pairs={{0,2},{2,0},{4,6},{6,4},{8,10},{10,8},{12,14},{14,12},{16,18},{18,... | collective-permute-start | bytes 2949128 | tf_op jit(solution)/shard_map/ppermute | solution.py:19
  3.0 26.3 %collective-permute-start = (bf16[192,2560]{1,0:T(8,128)(2,1)S(1)}, bf16[192,2560]{1,0:T(8,128)(2,1)S(1)}, u32[]{:S(2)}, u32[]{:S(2)}) collective-permute-start(bf16[192,2560]{1,0:T(8,128)(2,1)S(1)} %get-tuple-element.60), channel_id=1, source_target_pairs={{0,1},{1,0},{2,3},{3,2},{4,5},{5,4},{6,7},{7,6},{8,9},{9,8},{10,11... | collective-permute-start | bytes 2949128 | tf_op jit(solution)/shard_map/ppermute | solution.py:19
  6.1 63.0 %collective-permute-start.2 = (bf16[192,2560]{1,0:T(8,128)(2,1)S(1)}, bf16[192,2560]{1,0:T(8,128)(2,1)S(1)}, u32[]{:S(2)}, u32[]{:S(2)}) collective-permute-start(bf16[192,2560]{1,0:T(8,128)(2,1)S(1)} %collective-permute-done.1.other_ref), channel_id=1, source_target_pairs={{0,1},{1,0},{2,3},{3,2},{4,5},{5,4},{6,7},{7,6},{8,9},{9,8},{10,11... | collective-permute-start | bytes 2949128 | tf_op jit(solution)/shard_map/ppermute | solution.py:19
  41.7 14.6 %collective-permute-start.8 = (bf16[192,768]{1,0:T(8,128)(2,1)}, bf16[192,768]{1,0:T(8,128)(2,1)S(1)}, u32[]{:S(2)}, u32[]{:S(2)}) collective-permute-start(bf16[192,768]{1,0:T(8,128)(2,1)} %get-tuple-element.41), channel_id=1, source_target_pairs={{0,8},{2,10},{4,12},{6,14},{8,0},{10,2},{12,4},{14,6},{16,24},{18,... | collective-permute-start | bytes 884744 | tf_op jit(solution)/shard_map/ppermute | solution.py:19
  43.4 23.7 %collective-permute-start.12 = (bf16[192,768]{1,0:T(8,128)(2,1)}, bf16[192,768]{1,0:T(8,128)(2,1)S(1)}, u32[]{:S(2)}, u32[]{:S(2)}) collective-permute-start(bf16[192,768]{1,0:T(8,128)(2,1)} %get-tuple-element.43), channel_id=1, source_target_pairs={{0,16},{2,18},{4,20},{6,22},{8,24},{10,26},{12,28},{14,30},{16,0},... | collective-permute-start | bytes 884744 | tf_op jit(solution)/shard_map/ppermute | solution.py:19
  46.0 22.6 %collective-permute-start.16 = (bf16[192,768]{1,0:T(8,128)(2,1)}, bf16[192,768]{1,0:T(8,128)(2,1)S(1)}, u32[]{:S(2)}, u32[]{:S(2)}) collective-permute-start(bf16[192,768]{1,0:T(8,128)(2,1)} %get-tuple-element.45), channel_id=1, source_target_pairs={{0,24},{2,26},{4,28},{6,30},{8,16},{10,18},{12,20},{14,22},{16,8},... | collective-permute-start | bytes 884744 | tf_op jit(solution)/shard_map/ppermute | solution.py:19
  46.2 40.5 %collective-permute-start.6 = (bf16[192,768]{1,0:T(8,128)(2,1)}, bf16[192,768]{1,0:T(8,128)(2,1)S(1)}, u32[]{:S(2)}, u32[]{:S(2)}) collective-permute-start(bf16[192,768]{1,0:T(8,128)(2,1)} %get-tuple-element.39.refs_4_), channel_id=1, source_target_pairs={{0,4},{2,6},{4,0},{6,2},{8,12},{10,14},{12,8},{14,10},{16,20},{18,... | collective-permute-start | bytes 884744 | tf_op jit(solution)/shard_map/ppermute | solution.py:19
  56.4 25.2 %copy-start.10 = (bf16[192,768]{1,0:T(8,128)(2,1)}, bf16[192,768]{1,0:T(8,128)(2,1)S(1)}, u32[]{:S(2)}) copy-start(bf16[192,768]{1,0:T(8,128)(2,1)S(1)} %collective-permute-done.8.refs_8_) | copy-start | bytes 884740
  56.4 31.4 %collective-permute-start.10 = (bf16[192,768]{1,0:T(8,128)(2,1)S(1)}, bf16[192,768]{1,0:T(8,128)(2,1)S(1)}, u32[]{:S(2)}, u32[]{:S(2)}) collective-permute-start(bf16[192,768]{1,0:T(8,128)(2,1)S(1)} %collective-permute-done.8.refs_8_), channel_id=1, source_target_pairs={{0,4},{2,6},{4,0},{6,2},{8,12},{10,14},{12,8},{14,10},{16,20},{18,... | collective-permute-start | bytes 884744 | tf_op jit(solution)/shard_map/ppermute | solution.py:19
  67.1 14.5 %copy-start.11 = (bf16[192,768]{1,0:T(8,128)(2,1)}, bf16[192,768]{1,0:T(8,128)(2,1)S(1)}, u32[]{:S(2)}) copy-start(bf16[192,768]{1,0:T(8,128)(2,1)S(1)} %collective-permute-done.12.refs_12_) | copy-start | bytes 884740
  67.1 32.2 %collective-permute-start.14 = (bf16[192,768]{1,0:T(8,128)(2,1)S(1)}, bf16[192,768]{1,0:T(8,128)(2,1)S(1)}, u32[]{:S(2)}, u32[]{:S(2)}) collective-permute-start(bf16[192,768]{1,0:T(8,128)(2,1)S(1)} %collective-permute-done.12.refs_12_), channel_id=1, source_target_pairs={{0,4},{2,6},{4,0},{6,2},{8,12},{10,14},{12,8},{14,10},{16,20},{18,... | collective-permute-start | bytes 884744 | tf_op jit(solution)/shard_map/ppermute | solution.py:19
  68.6 13.0 %copy-start.12 = (bf16[192,768]{1,0:T(8,128)(2,1)}, bf16[192,768]{1,0:T(8,128)(2,1)S(1)}, u32[]{:S(2)}) copy-start(bf16[192,768]{1,0:T(8,128)(2,1)S(1)} %collective-permute-done.16.refs_16_) | copy-start | bytes 884740
  68.6 31.7 %collective-permute-start.18 = (bf16[192,768]{1,0:T(8,128)(2,1)S(1)}, bf16[192,768]{1,0:T(8,128)(2,1)S(1)}, u32[]{:S(2)}, u32[]{:S(2)}) collective-permute-start(bf16[192,768]{1,0:T(8,128)(2,1)S(1)} %collective-permute-done.16.refs_16_), channel_id=1, source_target_pairs={{0,4},{2,6},{4,0},{6,2},{8,12},{10,14},{12,8},{14,10},{16,20},{18,... | collective-permute-start | bytes 884744 | tf_op jit(solution)/shard_map/ppermute | solution.py:19
  81.6 28.2 %collective-permute-start.9 = (bf16[192,768]{1,0:T(8,128)(2,1)}, bf16[192,768]{1,0:T(8,128)(2,1)S(1)}, u32[]{:S(2)}, u32[]{:S(2)}) collective-permute-start(bf16[192,768]{1,0:T(8,128)(2,1)} %get-tuple-element.42), channel_id=1, source_target_pairs={{0,8},{2,10},{4,12},{6,14},{8,0},{10,2},{12,4},{14,6},{16,24},{18,... | collective-permute-start | bytes 884744 | tf_op jit(solution)/shard_map/ppermute | solution.py:19
  86.7 12.6 %copy-start.13 = (bf16[192,768]{1,0:T(8,128)(2,1)}, bf16[192,768]{1,0:T(8,128)(2,1)S(1)}, u32[]{:S(2)}) copy-start(bf16[192,768]{1,0:T(8,128)(2,1)S(1)} %collective-permute-done.6.refs_6_) | copy-start | bytes 884740
  86.7 25.3 %collective-permute-start.13 = (bf16[192,768]{1,0:T(8,128)(2,1)}, bf16[192,768]{1,0:T(8,128)(2,1)S(1)}, u32[]{:S(2)}, u32[]{:S(2)}) collective-permute-start(bf16[192,768]{1,0:T(8,128)(2,1)} %get-tuple-element.44), channel_id=1, source_target_pairs={{0,16},{2,18},{4,20},{6,22},{8,24},{10,26},{12,28},{14,30},{16,0},... | collective-permute-start | bytes 884744 | tf_op jit(solution)/shard_map/ppermute | solution.py:19
  87.8 11.5 %copy-start.14 = (bf16[192,768]{1,0:T(8,128)(2,1)}, bf16[192,768]{1,0:T(8,128)(2,1)S(1)}, u32[]{:S(2)}) copy-start(bf16[192,768]{1,0:T(8,128)(2,1)S(1)} %collective-permute-done.10.refs_10_) | copy-start | bytes 884740
  87.8 24.7 %collective-permute-start.17 = (bf16[192,768]{1,0:T(8,128)(2,1)}, bf16[192,768]{1,0:T(8,128)(2,1)S(1)}, u32[]{:S(2)}, u32[]{:S(2)}) collective-permute-start(bf16[192,768]{1,0:T(8,128)(2,1)} %get-tuple-element.46), channel_id=1, source_target_pairs={{0,24},{2,26},{4,28},{6,30},{8,16},{10,18},{12,20},{14,22},{16,8},... | collective-permute-start | bytes 884744 | tf_op jit(solution)/shard_map/ppermute | solution.py:19
  89.2 13.1 %copy-start.30 = (s32[2,192]{1,0:T(2,128)S(1)}, s32[2,192]{1,0:T(2,128)}, u32[]{:S(2)}) copy-start(s32[2,192]{1,0:T(2,128)} %param.9) | copy-start | bytes 4612
  89.2 20.1 %copy-start.17 = (bf16[192,768]{1,0:T(8,128)(2,1)S(1)}, bf16[192,768]{1,0:T(8,128)(2,1)}, u32[]{:S(2)}) copy-start(bf16[192,768]{1,0:T(8,128)(2,1)} %get-tuple-element.40.refs_5_) | copy-start | bytes 884740
  99.3 52.4 %copy-start.15 = (bf16[192,768]{1,0:T(8,128)(2,1)}, bf16[192,768]{1,0:T(8,128)(2,1)S(1)}, u32[]{:S(2)}) copy-start(bf16[192,768]{1,0:T(8,128)(2,1)S(1)} %collective-permute-done.14.refs_14_) | copy-start | bytes 884740
  99.3 10.0 %collective-permute-start.20 = (bf16[192,384]{1,0:T(8,128)(2,1)}, bf16[192,384]{1,0:T(8,128)(2,1)S(1)}, u32[]{:S(2)}, u32[]{:S(2)}) collective-permute-start(bf16[192,384]{1,0:T(8,128)(2,1)} %get-tuple-element.49), channel_id=1, source_target_pairs={{0,8},{2,10},{4,12},{6,14},{8,0},{10,2},{12,4},{14,6},{16,24},{18,... | collective-permute-start | bytes 442376 | tf_op jit(solution)/shard_map/ppermute | solution.py:19
  100.3 51.4 %copy-start.16 = (bf16[192,768]{1,0:T(8,128)(2,1)}, bf16[192,768]{1,0:T(8,128)(2,1)S(1)}, u32[]{:S(2)}) copy-start(bf16[192,768]{1,0:T(8,128)(2,1)S(1)} %collective-permute-done.18.refs_18_) | copy-start | bytes 884740
  100.3 20.4 %collective-permute-start.21 = (bf16[192,384]{1,0:T(8,128)(2,1)}, bf16[192,384]{1,0:T(8,128)(2,1)S(1)}, u32[]{:S(2)}, u32[]{:S(2)}) collective-permute-start(bf16[192,384]{1,0:T(8,128)(2,1)} %get-tuple-element.50), channel_id=1, source_target_pairs={{0,16},{2,18},{4,20},{6,22},{8,24},{10,26},{12,28},{14,30},{16,0},... | collective-permute-start | bytes 442376 | tf_op jit(solution)/shard_map/ppermute | solution.py:19
  109.3 42.4 %copy-start.25 = (bf16[192,384]{1,0:T(8,128)(2,1)}, bf16[192,384]{1,0:T(8,128)(2,1)S(1)}, u32[]{:S(2)}) copy-start(bf16[192,384]{1,0:T(8,128)(2,1)S(1)} %collective-permute-done.20.refs_1_) | copy-start | bytes 442372
  109.3 38.0 %collective-permute-start.7 = (bf16[192,768]{1,0:T(8,128)(2,1)S(1)}, bf16[192,768]{1,0:T(8,128)(2,1)S(1)}, u32[]{:S(2)}, u32[]{:S(2)}) collective-permute-start(bf16[192,768]{1,0:T(8,128)(2,1)S(1)} %copy-done.17), channel_id=1, source_target_pairs={{0,4},{2,6},{4,0},{6,2},{8,12},{10,14},{12,8},{14,10},{16,20},{18,... | collective-permute-start | bytes 884744 | tf_op jit(solution)/shard_map/ppermute | solution.py:19
  109.8 41.9 %copy-start.18 = (bf16[192,768]{1,0:T(8,128)(2,1)}, bf16[192,768]{1,0:T(8,128)(2,1)S(1)}, u32[]{:S(2)}) copy-start(bf16[192,768]{1,0:T(8,128)(2,1)S(1)} %collective-permute-done.9.refs_9_) | copy-start | bytes 884740
  109.8 38.3 %collective-permute-start.11 = (bf16[192,768]{1,0:T(8,128)(2,1)S(1)}, bf16[192,768]{1,0:T(8,128)(2,1)S(1)}, u32[]{:S(2)}, u32[]{:S(2)}) collective-permute-start(bf16[192,768]{1,0:T(8,128)(2,1)S(1)} %collective-permute-done.9.refs_9_), channel_id=1, source_target_pairs={{0,4},{2,6},{4,0},{6,2},{8,12},{10,14},{12,8},{14,10},{16,20},{18,... | collective-permute-start | bytes 884744 | tf_op jit(solution)/shard_map/ppermute | solution.py:19
  112.0 39.8 %copy-start.19 = (bf16[192,768]{1,0:T(8,128)(2,1)}, bf16[192,768]{1,0:T(8,128)(2,1)S(1)}, u32[]{:S(2)}) copy-start(bf16[192,768]{1,0:T(8,128)(2,1)S(1)} %collective-permute-done.13.refs_13_) | copy-start | bytes 884740
  112.0 39.7 %collective-permute-start.15 = (bf16[192,768]{1,0:T(8,128)(2,1)S(1)}, bf16[192,768]{1,0:T(8,128)(2,1)S(1)}, u32[]{:S(2)}, u32[]{:S(2)}) collective-permute-start(bf16[192,768]{1,0:T(8,128)(2,1)S(1)} %collective-permute-done.13.refs_13_), channel_id=1, source_target_pairs={{0,4},{2,6},{4,0},{6,2},{8,12},{10,14},{12,8},{14,10},{16,20},{18,... | collective-permute-start | bytes 884744 | tf_op jit(solution)/shard_map/ppermute | solution.py:19
  112.5 39.2 %copy-start.20 = (bf16[192,768]{1,0:T(8,128)(2,1)}, bf16[192,768]{1,0:T(8,128)(2,1)S(1)}, u32[]{:S(2)}) copy-start(bf16[192,768]{1,0:T(8,128)(2,1)S(1)} %collective-permute-done.17.refs_17_) | copy-start | bytes 884740
  112.5 39.2 %collective-permute-start.19 = (bf16[192,768]{1,0:T(8,128)(2,1)S(1)}, bf16[192,768]{1,0:T(8,128)(2,1)S(1)}, u32[]{:S(2)}, u32[]{:S(2)}) collective-permute-start(bf16[192,768]{1,0:T(8,128)(2,1)S(1)} %collective-permute-done.17.refs_17_), channel_id=1, source_target_pairs={{0,4},{2,6},{4,0},{6,2},{8,12},{10,14},{12,8},{14,10},{16,20},{18,... | collective-permute-start | bytes 884744 | tf_op jit(solution)/shard_map/ppermute | solution.py:19
  120.7 31.1 %copy-start.26 = (bf16[192,384]{1,0:T(8,128)(2,1)}, bf16[192,384]{1,0:T(8,128)(2,1)S(1)}, u32[]{:S(2)}) copy-start(bf16[192,384]{1,0:T(8,128)(2,1)S(1)} %collective-permute-done.21.refs_2_) | copy-start | bytes 442372
  120.7 26.6 %collective-permute-start.22 = (bf16[192,384]{1,0:T(8,128)(2,1)}, bf16[192,384]{1,0:T(8,128)(2,1)}, u32[]{:S(2)}, u32[]{:S(2)}) collective-permute-start(bf16[192,384]{1,0:T(8,128)(2,1)} %get-tuple-element.51), channel_id=1, source_target_pairs={{0,24},{2,26},{4,28},{6,30},{8,16},{10,18},{12,20},{14,22},{16,8},... | collective-permute-start | bytes 442376 | tf_op jit(solution)/shard_map/ppermute | solution.py:19
  147.3 19.2 %collective-permute-start.3 = (bf16[192,384]{1,0:T(8,128)(2,1)}, bf16[192,384]{1,0:T(8,128)(2,1)S(1)}, u32[]{:S(2)}, u32[]{:S(2)}) collective-permute-start(bf16[192,384]{1,0:T(8,128)(2,1)} %get-tuple-element.34), channel_id=1, source_target_pairs={{0,8},{2,10},{4,12},{6,14},{8,0},{10,2},{12,4},{14,6},{16,24},{18,... | collective-permute-start | bytes 442376 | tf_op jit(solution)/shard_map/ppermute | solution.py:19
  147.3 19.8 %collective-permute-start.4 = (bf16[192,384]{1,0:T(8,128)(2,1)}, bf16[192,384]{1,0:T(8,128)(2,1)S(1)}, u32[]{:S(2)}, u32[]{:S(2)}) collective-permute-start(bf16[192,384]{1,0:T(8,128)(2,1)} %get-tuple-element.35), channel_id=1, source_target_pairs={{0,16},{2,18},{4,20},{6,22},{8,24},{10,26},{12,28},{14,30},{16,0},... | collective-permute-start | bytes 442376 | tf_op jit(solution)/shard_map/ppermute | solution.py:19
  148.1 22.5 %collective-permute-start.5 = (bf16[192,384]{1,0:T(8,128)(2,1)}, bf16[192,384]{1,0:T(8,128)(2,1)S(1)}, u32[]{:S(2)}, u32[]{:S(2)}) collective-permute-start(bf16[192,384]{1,0:T(8,128)(2,1)} %get-tuple-element.36), channel_id=1, source_target_pairs={{0,24},{2,26},{4,28},{6,30},{8,16},{10,18},{12,20},{14,22},{16,8},... | collective-permute-start | bytes 442376 | tf_op jit(solution)/shard_map/ppermute | solution.py:19
  166.4 19.2 %collective-permute-start.23 = (bf16[192,384]{1,0:T(8,128)(2,1)}, bf16[192,384]{1,0:T(8,128)(2,1)S(1)}, u32[]{:S(2)}, u32[]{:S(2)}) collective-permute-start(bf16[192,384]{1,0:T(8,128)(2,1)} %get-tuple-element.52), channel_id=1, source_target_pairs={{0,2},{2,0},{4,6},{6,4},{8,10},{10,8},{12,14},{14,12},{16,18},{18,... | collective-permute-start | bytes 442376 | tf_op jit(solution)/shard_map/ppermute | solution.py:19
  166.4 20.0 %collective-permute-start.25 = (bf16[192,384]{1,0:T(8,128)(2,1)}, bf16[192,384]{1,0:T(8,128)(2,1)S(1)}, u32[]{:S(2)}, u32[]{:S(2)}) collective-permute-start(bf16[192,384]{1,0:T(8,128)(2,1)} %get-tuple-element.54), channel_id=1, source_target_pairs={{0,10},{2,8},{4,14},{6,12},{8,2},{10,0},{12,6},{14,4},{16,26},{18,... | collective-permute-start | bytes 442376 | tf_op jit(solution)/shard_map/ppermute | solution.py:19
  166.5 23.4 %collective-permute-start.27 = (bf16[192,384]{1,0:T(8,128)(2,1)}, bf16[192,384]{1,0:T(8,128)(2,1)S(1)}, u32[]{:S(2)}, u32[]{:S(2)}) collective-permute-start(bf16[192,384]{1,0:T(8,128)(2,1)} %get-tuple-element.56), channel_id=1, source_target_pairs={{0,18},{2,16},{4,22},{6,20},{8,26},{10,24},{12,30},{14,28},{16,2},... | collective-permute-start | bytes 442376 | tf_op jit(solution)/shard_map/ppermute | solution.py:19
  167.1 22.9 %collective-permute-start.29 = (bf16[192,384]{1,0:T(8,128)(2,1)}, bf16[192,384]{1,0:T(8,128)(2,1)S(1)}, u32[]{:S(2)}, u32[]{:S(2)}) collective-permute-start(bf16[192,384]{1,0:T(8,128)(2,1)} %get-tuple-element.58), channel_id=1, source_target_pairs={{0,26},{2,24},{4,30},{6,28},{8,18},{10,16},{12,22},{14,20},{16,10}... | collective-permute-start | bytes 442376 | tf_op jit(solution)/shard_map/ppermute | solution.py:19
  185.5 7.4 %collective-permute-start.24 = (bf16[192,384]{1,0:T(8,128)(2,1)}, bf16[192,384]{1,0:T(8,128)(2,1)S(1)}, u32[]{:S(2)}, u32[]{:S(2)}) collective-permute-start(bf16[192,384]{1,0:T(8,128)(2,1)} %get-tuple-element.53), channel_id=1, source_target_pairs={{0,8},{2,10},{4,12},{6,14},{8,0},{10,2},{12,4},{14,6},{16,24},{18,... | collective-permute-start | bytes 442376 | tf_op jit(solution)/shard_map/ppermute | solution.py:19
  185.6 14.3 %copy-start.3 = (bf16[192,384]{1,0:T(8,128)(2,1)}, bf16[192,384]{1,0:T(8,128)(2,1)S(1)}, u32[]{:S(2)}) copy-start(bf16[192,384]{1,0:T(8,128)(2,1)S(1)} %collective-permute-done.23.refs_1_) | copy-start | bytes 442372
  185.6 14.2 %collective-permute-start.26 = (bf16[192,384]{1,0:T(8,128)(2,1)}, bf16[192,384]{1,0:T(8,128)(2,1)S(1)}, u32[]{:S(2)}, u32[]{:S(2)}) collective-permute-start(bf16[192,384]{1,0:T(8,128)(2,1)} %get-tuple-element.55), channel_id=1, source_target_pairs={{0,16},{2,18},{4,20},{6,22},{8,24},{10,26},{12,28},{14,30},{16,0},... | collective-permute-start | bytes 442376 | tf_op jit(solution)/shard_map/ppermute | solution.py:19
  186.4 13.4 %copy-start.4 = (bf16[192,384]{1,0:T(8,128)(2,1)}, bf16[192,384]{1,0:T(8,128)(2,1)S(1)}, u32[]{:S(2)}) copy-start(bf16[192,384]{1,0:T(8,128)(2,1)S(1)} %collective-permute-done.25.refs_3_) | copy-start | bytes 442372
  186.4 13.4 %collective-permute-start.28 = (bf16[192,384]{1,0:T(8,128)(2,1)}, bf16[192,384]{1,0:T(8,128)(2,1)S(1)}, u32[]{:S(2)}, u32[]{:S(2)}) collective-permute-start(bf16[192,384]{1,0:T(8,128)(2,1)} %get-tuple-element.57), channel_id=1, source_target_pairs={{0,24},{2,26},{4,28},{6,30},{8,16},{10,18},{12,20},{14,22},{16,8},... | collective-permute-start | bytes 442376 | tf_op jit(solution)/shard_map/ppermute | solution.py:19
  189.9 9.9 %copy-start.5 = (bf16[192,384]{1,0:T(8,128)(2,1)}, bf16[192,384]{1,0:T(8,128)(2,1)S(1)}, u32[]{:S(2)}) copy-start(bf16[192,384]{1,0:T(8,128)(2,1)S(1)} %collective-permute-done.27.refs_5_) | copy-start | bytes 442372
  190.0 9.9 %copy-start.6 = (bf16[192,384]{1,0:T(8,128)(2,1)}, bf16[192,384]{1,0:T(8,128)(2,1)S(1)}, u32[]{:S(2)}) copy-start(bf16[192,384]{1,0:T(8,128)(2,1)S(1)} %collective-permute-done.29.refs_7_) | copy-start | bytes 442372
  (13 other events, 30.6 us)

commit v5 on v3

--- a/solution.py
+++ b/solution.py
@@ -29,15 +29,16 @@
 
     for weight_ref, out_ref in zip(refs[:weights], refs[weights:-1]):
         result = jnp.dot(flat_ref[...], weight_ref[...], preferred_element_type=jnp.float32)
-        out_ref[0] = result.reshape(2, rows, -1)
+        out_ref[...] = result.reshape(2, rows, -1)
 
 
 def own_products(hidden_in, other, weights, place, ways):
     rows, feats = other.shape
-    width = weights[0].shape[1] // ways
+    features = weights[0].shape[1]
+    width = features // ways
     return pl.pallas_call(
         functools.partial(own_body, len(weights)),
-        out_shape=[jax.ShapeDtypeStruct((ways, 2, rows, width), jnp.float32)] * len(weights),
+        out_shape=[jax.ShapeDtypeStruct((2, rows, features), jnp.float32)] * len(weights),
         grid_spec=pltpu.PrefetchScalarGridSpec(
             num_scalar_prefetch=1,
             grid=(ways,),
@@ -45,96 +46,99 @@
                 pl.BlockSpec((1, rows, feats), lambda g, place: (place[2], 0, 0)),
                 pl.BlockSpec((rows, feats), lambda g, place: (0, 0)),
             ]
-            + [pl.BlockSpec((feats, width), lambda g, place: (place[0], place[1] ^ g))] * len(weights),
-            out_specs=[pl.BlockSpec((1, 2, rows, width), lambda g, place: (g, 0, 0, 0))] * len(weights),
+            + [pl.BlockSpec((feats, width), lambda g, place: (place[0], g))] * len(weights),
+            out_specs=[pl.BlockSpec((2, rows, width), lambda g, place: (0, 0, g))] * len(weights),
             scratch_shapes=[pltpu.VMEM((2 * rows, feats), jnp.bfloat16)],
         ),
         compiler_params=pltpu.CompilerParams(vmem_limit_bytes=VMEM_LIMIT),
         cost_estimate=pl.CostEstimate(
-            flops=4 * rows * feats * width * ways * len(weights),
-            bytes_accessed=2 * feats * width * ways * len(weights),
+            flops=4 * rows * feats * features * len(weights),
+            bytes_accessed=2 * feats * features * len(weights),
             transcendentals=0,
         ),
     )(place, hidden_in, other, *weights)
 
 
-def rest_body(shares, steps, weights, chunks, place, *refs):
+def rest_body(shares, weights, chunks, away, place, *refs):
     inputs = refs[: shares * chunks]
-    weight_refs = refs[shares * chunks : shares * chunks + weights]
-    start_refs = refs[shares * chunks + weights : shares * chunks + 2 * weights]
-    out_refs = refs[shares * chunks + 2 * weights : shares * chunks + 2 * weights + chunks]
-    totals = refs[shares * chunks + 2 * weights + chunks :]
-    rows = out_refs[0].shape[0]
-    width = out_refs[0].shape[1] // weights
+    refs = refs[shares * chunks :]
+    weight_refs, refs = refs[: weights * shares], refs[weights * shares :]
+    start_refs, refs = refs[:weights], refs[weights:]
+    out_refs, flats = refs[: chunks * len(away)], refs[chunks * len(away) :]
+    rows, width = out_refs[0].shape
+    width //= weights
     step = pl.program_id(0)
-
-    @pl.when(step == 0)
-    def _():
-        for total, start in zip(totals, start_refs):
-            total[...] = start[...].reshape(chunks * rows, width)
-
-    for share in range(shares):
-
-        @pl.when(step // steps == share)
+    if chunks > 1:
+
+        @pl.when(step == 0)
         def _():
-            flat = [inputs[c * shares + share][...] for c in range(chunks)]
-            flat = flat[0] if chunks == 1 else jnp.concatenate(flat, axis=0)
-            for total, weight in zip(totals, weight_refs):
-                total[...] += jnp.dot(flat, weight[...], preferred_element_type=jnp.float32)
-
-    @pl.when(step == shares * steps - 1)
-    def _():
-        for n, total in enumerate(totals):
-            for c, out_ref in enumerate(out_refs):
-                out_ref[:, n * width : (n + 1) * width] = total[c * rows : (c + 1) * rows].astype(
-                    out_ref.dtype
-                )
-
-
-def rest_products(received, chosen, weights, starts, place, a, ways):
+            for share in range(shares):
+                for c in range(chunks):
+                    flats[share][c * rows : (c + 1) * rows] = inputs[c * shares + share][...]
+
+    else:
+        flats = inputs
+    made = []
+    for n in range(weights):
+        total = start_refs[n][...].reshape(chunks * rows, width)
+        for share in range(shares):
+            total += jnp.dot(
+                flats[share][...], weight_refs[n * shares + share][...], preferred_element_type=jnp.float32
+            )
+        made.append(total.astype(jnp.bfloat16))
+    for index in range(len(away)):
+
+        @pl.when(step == index)
+        def _():
+            for c in range(chunks):
+                for n in range(weights):
+                    out_refs[c * len(away) + index][:, n * width : (n + 1) * width] = made[n][
+                        c * rows : (c + 1) * rows
+                    ]
+
+
+def rest_products(received, chosen, weights, starts, place, ways, away):
     shares = len(received[0])
     rows, feats = received[0][0].shape
     width = weights[0].shape[1] // ways
     chunks = len(chosen)
-    steps = max(1, feats // 640)
-    depth = feats // steps
-
-    def share_map(share, i, place):
-        return (0, jnp.clip(i - share * steps, 0, steps - 1))
-
-    in_specs = []
-    operands = []
-    for c in chosen:
+    top = away[0]
+
+    def weight_map(share, i, place):
+        return (place[0] ^ (share + 1), place[1] ^ (top - i))
+
+    in_specs = [pl.BlockSpec((rows, feats), lambda i, place: (0, 0))] * (shares * chunks)
+    for _ in weights:
         for share in range(shares):
-            in_specs.append(pl.BlockSpec((rows, depth), functools.partial(share_map, share)))
-            operands.append(received[c][share])
+            in_specs.append(pl.BlockSpec((feats, width), functools.partial(weight_map, share)))
     in_specs += [
-        pl.BlockSpec(
-            (depth, width),
-            lambda i, place: ((place[0] ^ (i // steps + 1)) * steps + i % steps, place[1] ^ a),
-        )
-    ] * len(weights)
-    in_specs += [
-        pl.BlockSpec((1, chunks, rows, width), lambda i, place: (a, chosen[0] // chunks, 0, 0))
+        pl.BlockSpec((chunks, rows, width), lambda i, place: (chosen[0] // chunks, 0, place[1] ^ (top - i)))
     ] * len(weights)
     columns = width * len(weights)
-    return pl.pallas_call(
-        functools.partial(rest_body, shares, steps, len(weights), chunks),
-        out_shape=[jax.ShapeDtypeStruct((rows, columns), jnp.bfloat16)] * chunks,
+    scratch = [pltpu.VMEM((chunks * rows, feats), jnp.bfloat16)] * (shares if chunks > 1 else 0)
+    outs = pl.pallas_call(
+        functools.partial(rest_body, shares, len(weights), chunks, away),
+        out_shape=[jax.ShapeDtypeStruct((rows, columns), jnp.bfloat16)] * (chunks * len(away)),
         grid_spec=pltpu.PrefetchScalarGridSpec(
             num_scalar_prefetch=1,
-            grid=(shares * steps,),
+            grid=(len(away),),
             in_specs=in_specs,
-            out_specs=[pl.BlockSpec((rows, columns), lambda i, place: (0, 0))] * chunks,
-            scratch_shapes=[pltpu.VMEM((chunks * rows, width), jnp.float32)] * len(weights),
+            out_specs=[pl.BlockSpec((rows, columns), lambda i, place: (0, 0))] * (chunks * len(away)),
+            scratch_shapes=scratch,
         ),
         compiler_params=pltpu.CompilerParams(vmem_limit_bytes=VMEM_LIMIT),
         cost_estimate=pl.CostEstimate(
-            flops=2 * chunks * rows * feats * shares * columns,
-            bytes_accessed=2 * feats * shares * columns,
+            flops=2 * chunks * rows * feats * shares * columns * len(away),
+            bytes_accessed=2 * feats * shares * columns * len(away),
             transcendentals=0,
         ),
-    )(place, *operands, *weights, *starts)
+    )(
+        place,
+        *[share for c in chosen for share in received[c]],
+        *[weight for weight in weights for _ in range(shares)],
+        *starts,
+    )
+    return [dict(zip(away, outs[c * len(away) : (c + 1) * len(away)])) for c in range(chunks)]
 
 
 def attend_body(block, ways, offsets, spans, tile, table, place, *refs):
@@ -151,7 +155,7 @@
 
     copies = []
     for slot, offset in enumerate(offsets):
-        low = table[offset, seq]
+        low = table[place[3] ^ offset, seq]
         for part, span in ((0, low), (1, spans - 1 - low)):
             copies.append(
                 pltpu.make_async_copy(
@@ -167,7 +171,7 @@
         jnp.int32, (half, 128), 1
     )
     for a in range(ways):
-        low = table[a * rest + block, seq]
+        low = table[place[3] ^ (a * rest + block), seq]
         here = slice(a * half, (a + 1) * half)
         for part, span in ((0, low), (1, spans - 1 - low)):
             asked[part, here] = query_refs[a][part * half : (part + 1) * half]
@@ -269,28 +273,27 @@
     )(table, place, *queries, *[blocks[i] for i in offsets])
 
 
-def assemble_body(slots, place, *refs):
-    for n in range(slots):
-
-        @pl.when(pl.program_id(0) == n)
+def assemble_body(ways, sequences, place, *refs):
+    out_ref = refs[-1]
+    for a in range(ways):
+
+        @pl.when(pl.program_id(0) == a)
         def _():
-            refs[-1][0] = refs[n][...]
+            for b in range(sequences):
+                out_ref[place[2] ^ b] = refs[a * sequences + b][...]
 
 
 def assemble(pieces, place):
     ways, sequences = len(pieces), len(pieces[0])
     rows, width = pieces[0][0].shape
     return pl.pallas_call(
-        functools.partial(assemble_body, ways * sequences),
+        functools.partial(assemble_body, ways, sequences),
         out_shape=jax.ShapeDtypeStruct((sequences, rows, ways * width), jnp.bfloat16),
         grid_spec=pltpu.PrefetchScalarGridSpec(
             num_scalar_prefetch=1,
-            grid=(ways * sequences,),
-            in_specs=[pl.BlockSpec((rows, width), lambda n, place: (0, 0))] * (ways * sequences),
-            out_specs=pl.BlockSpec(
-                (1, rows, width),
-                lambda n, place: (place[2] ^ (n % sequences), 0, place[1] ^ (n // sequences)),
-            ),
+            grid=(ways,),
+            in_specs=[pl.BlockSpec((rows, width), lambda a, place: (0, 0))] * (ways * sequences),
+            out_specs=pl.BlockSpec((sequences, rows, width), lambda a, place: (0, 0, place[1] ^ a)),
         ),
         compiler_params=pltpu.CompilerParams(vmem_limit_bytes=VMEM_LIMIT),
     )(place, *[piece for row in pieces for piece in row])
@@ -322,33 +325,34 @@
     other = over_ctx(lax.dynamic_index_in_dim(hidden_in, 1 - core, 0, keepdims=False), 1)
     received = [other_shares(mine), other_shares(other)]
 
-    table = event_pos[None, :, 0] // (rows // 2)
-    bit = 1
-    while bit < ctx_size:
-        table = jnp.concatenate([table, over_ctx(table, bit)], axis=0)
-        bit *= 2
+    firsts = jnp.broadcast_to((event_pos[:, 0] // (rows // 2))[None], (ctx_size, 2))
+    table = lax.all_to_all(firsts, "ctx", 0, 0, tiled=True)
 
     start_k, start_v, start_q = own_products(hidden_in, other, [w_k, w_v, w_q], place, ways)
-    place_later = jnp.concatenate([place, table.reshape(-1)])
-
-    blocks = {}
-    for b in range(2):
-        for a in away:
-            (made,) = rest_products(received, [b], [w_k, w_v], [start_k, start_v], place_later, a, ways)
-            blocks[a * rest + b] = over_ctx(made, a * rest)
+
+    later = jnp.concatenate([place, table.reshape(-1)])
+    (made_0,) = rest_products(received, [0], [w_k, w_v], [start_k, start_v], later, ways, away)
+    (made_1,) = rest_products(received, [1], [w_k, w_v], [start_k, start_v], place, ways, away)
+    received, made_1 = lax.optimization_barrier((received, made_1))
+    asked = rest_products(received, [0, 1], [w_q], [start_q], place, ways, away)
+    first = {a: over_ctx(made_0[a], a * rest) for a in away}
+    for a in away:
+        first[a], asked[0][a] = lax.optimization_barrier((first[a], asked[0][a]))
+    blocks = {a * rest: first[a] for a in away}
+    queries = [{}, {}]
+    for a in away:
+        last = first[a]
+        for made, keep, key in ((made_1, blocks, a * rest + 1), (asked[0], queries[0], a), (asked[1], queries[1], a)):
+            value, last = lax.optimization_barrier((made[a], last))
+            last = keep[key] = over_ctx(value, a * rest)
     bit = rest // 2
     while bit > 1:
         for i in list(blocks):
             blocks[i ^ bit] = over_ctx(blocks[i], bit)
         bit //= 2
-    queries = [[None] * ways, [None] * ways]
-    for a in away:
-        made = rest_products(received, [0, 1], [w_q], [start_q], place_later, a, ways)
-        for b in range(2):
-            queries[b][a] = over_ctx(made[b], a * rest)
     pieces = [[None] * 2 for _ in range(ways)]
     for b in range(2):
-        outs = attend(b, queries[b], blocks, table, place)
+        outs = attend(b, [queries[b][a] for a in range(ways)], blocks, table, place)
         for a in away:
             pieces[a][b] = over_ctx(outs[a], a * rest + b)
     return assemble(pieces, place)

time: 220 us -> 196 us (0.89)
  Pallas kernels: 122 us -> 82.5 us
  waiting for transfers between devices: 26.6 us -> 59.6 us
  starting transfers between devices: 61 us -> 40.4 us
    pallas_call x13 -> x4, Pallas kernels: 75.6 us -> 35.9 us  [the longest x3 32.3 us: rest_products(): pl.pallas_call(functools.partial(rest_body, shares, len(weights), chunks,...]
    ppermute x34 -> x30, waiting for transfers between devices: 26.6 us -> 53.9 us  [exchange(): return lax.ppermute(value, axis, [(i, i ^ bit) for i in range(size)])]
    ppermute x34 -> x30, starting transfers between devices: 61 us -> 34.4 us  [exchange(): return lax.ppermute(value, axis, [(i, i ^ bit) for i in range(size)])]
    all_to_all x0 -> x1, starting transfers between devices: none -> 5.94 us  [on_device(): table = lax.all_to_all(firsts, 'ctx', 0, 0, tiled=True)]
    all_to_all x0 -> x1, waiting for transfers between devices: none -> 5.73 us  [on_device(): table = lax.all_to_all(firsts, 'ctx', 0, 0, tiled=True)]
    unnamed x72 -> x74, local copies, waits for them, and re-layouts: 4.21 us -> 5 us
  transfers between devices with their start and end apart: 34 -> 31, of which waited for: 8 -> 12; matrix products, arithmetic and copies ran while one was open for 1% -> 2% of each run, Pallas kernels for 54% -> 41%
where the time goes in v5:
time: 196 us; the launch traced here: 194 us
  Pallas kernels  82.5 us (42%)
  waiting for transfers between devices  59.6 us (30%)
  starting transfers between devices  40.4 us (21%)
  local copies, waits for them, and re-layouts  9.54 us (5%)
    ppermute x30, waiting for transfers between devices, exchange(): return lax.ppermute(value, axis, [(i, i ^ bit) for i in range(size)])  53.9 us
    ppermute x30, starting transfers between devices, exchange(): return lax.ppermute(value, axis, [(i, i ^ bit) for i in range(size)])  34.4 us
    pallas_call x3, Pallas kernels, rest_products(): pl.pallas_call(functools.partial(rest_body, shares, len(weights), chunks,...  32.3 us
    pallas_call x2, Pallas kernels, attend(): pl.pallas_call(functools.partial(attend_body, block, ways, offsets, spans...  28 us
    pallas_call x1, Pallas kernels, own_products(): pl.pallas_call(functools.partial(own_body, len(weights)), out_shape=[jax....  18.6 us
    all_to_all x1, starting transfers between devices, on_device(): table = lax.all_to_all(firsts, 'ctx', 0, 0, tiled=True)  5.94 us
    all_to_all x1, waiting for transfers between devices, on_device(): table = lax.all_to_all(firsts, 'ctx', 0, 0, tiled=True)  5.73 us
    unnamed x74, local copies, waits for them, and re-layouts  5 us
  transfers between devices with their start and end apart: 31, of which 12 were waited for; matrix products, arithmetic and copies ran while one was open for 2% of the time, Pallas kernels for 41%

profile of v5, /device:TPU:0, one launch (start us, length us, event | category | flops | bytes accessed | tf_op | source)
XLA Modules:
  0.0 194.0 jit_solution(17534385388983777587)
XLA Ops:
  0.0 2.6 %dynamic-slice_bitcast_fusion = (bf16[192,2560]{1,0:T(8,128)(2,1)}, bf16[192,2560]{1,0:T(8,128)(2,1)S(1)}) fusion(bf16[2,192,2560]{2,1,0:T(8,128)(2,1)} %mine_ref.1, s32[]{:T(128)S(6)} %select_n.31, s32[]{:T(128)S(6)} %select_n.30), kind=kLoop, calls=%fused_computation | loop fusion | bytes 3932168 | tf_op jit(solution)/shard_map/jit(dynamic_index_in_dim)/squeeze | solution.py:325
  3.0 2.5 %collective-permute-start = (bf16[192,2560]{1,0:T(8,128)(2,1)S(1)}, bf16[192,2560]{1,0:T(8,128)(2,1)S(1)}, u32[]{:S(2)}, u32[]{:S(2)}) collective-permute-start(bf16[192,2560]{1,0:T(8,128)(2,1)S(1)} %get-tuple-element.112), channel_id=1, source_target_pairs={{0,1},{1,0},{2,3},{3,2},{4,5},{5,4},{6,7},{7,6},{8,9},{9,8},{10,11... | collective-permute-start | bytes 2949128 | tf_op jit(solution)/shard_map/ppermute | solution.py:18
  5.8 0.6 broadcast_in_dim.2
  6.4 5.9 %all-to-all-start = ((s32[16,1,2]{2,1,0:T(1,128)}), s32[16,1,2]{2,1,0:T(1,128)S(1)}, u32[]{:S(2)}, u32[]{:S(2)}) async-start(s32[16,1,2]{2,1,0:T(1,128)} %broadcast_in_dim.2), calls=%async_computation | async-start | bytes 16384 | tf_op jit(solution)/shard_map/all_to_all | solution.py:329
  12.4 0.7 pad_add_fusion.place
  13.0 5.7 %all-to-all-done = s32[16,1,2]{2,1,0:T(1,128)S(1)} async-done(((s32[16,1,2]{2,1,0:T(1,128)}), s32[16,1,2]{2,1,0:T(1,128)S(1)}, u32[]{:S(2)}, u32[]{:S(2)}) %all-to-all-start) | async-done | bytes 160 | tf_op jit(solution)/shard_map/all_to_all | solution.py:329
  18.7 0.6 broadcast.47
  19.3 0.7 reduce.7
  20.1 0.7 concatenate.4.place
  21.8 18.6 %shard_map.55 = (f32[2,192,1536]{2,1,0:T(8,128)}, f32[2,192,1536]{2,1,0:T(8,128)}, f32[2,192,1536]{2,1,0:T(8,128)}) custom-call(s32[4]{0:T(128)} %pad_add_fusion.place, bf16[2,192,2560]{2,1,0:T(8,128)(2,1)} %mine_ref.1, bf16[192,2560]{1,0:T(8,128)(2,1)} %copy-done.2, bf16[5120,1536]{1,0:T(8,128)(2,1)} %refs_1_.5, bf16[5120,1536]{1,0:T(8,128)(2,1)} %refs_2_.6, ...), custom_call_target="tpu_custom_call" | custom-call | flops 9059696640 | bytes 23592960 | tf_op jit(solution)/shard_map/pallas_call | solution.py:39
  40.3 0.9 copy-done
  41.3 11.2 %shard_map.56 = (bf16[192,768]{1,0:T(8,128)(2,1)}, bf16[192,768]{1,0:T(8,128)(2,1)}, bf16[192,768]{1,0:T(8,128)(2,1)}, bf16[192,768]{1,0:T(8,128)(2,1)}) custom-call(s32[36]{0:T(128)} %concatenate.4.place, bf16[192,2560]{1,0:T(8,128)(2,1)} %copy-done, bf16[5120,1536]{1,0:T(8,128)(2,1)} %refs_1_.5, bf16[5120,1536]{1,0:T(8,128)(2,1)} %refs_2_.6, ...), custom_call_target="tpu_custom_call" | custom-call | flops 3019898880 | bytes 15728640 | tf_op jit(solution)/shard_map/pallas_call | solution.py:119
  52.5 0.6 collective-permute-start.9
  53.1 1.2 collective-permute-start.6
  54.3 2.6 %collective-permute-start.3 = (bf16[192,768]{1,0:T(8,128)(2,1)}, bf16[192,768]{1,0:T(8,128)(2,1)S(1)}, u32[]{:S(2)}, u32[]{:S(2)}) collective-permute-start(bf16[192,768]{1,0:T(8,128)(2,1)} %get-tuple-element.74), channel_id=1, source_target_pairs={{0,8},{2,10},{4,12},{6,14},{8,0},{10,2},{12,4},{14,6},{16,24},{18,... | collective-permute-start | bytes 884744 | tf_op jit(solution)/shard_map/ppermute | solution.py:18
  56.9 1.0 copy-done.1
  57.9 11.2 %shard_map.57 = (bf16[192,768]{1,0:T(8,128)(2,1)}, bf16[192,768]{1,0:T(8,128)(2,1)}, bf16[192,768]{1,0:T(8,128)(2,1)}, bf16[192,768]{1,0:T(8,128)(2,1)}) custom-call(s32[4]{0:T(128)} %pad_add_fusion.place, bf16[192,2560]{1,0:T(8,128)(2,1)} %copy-done.1, bf16[5120,1536]{1,0:T(8,128)(2,1)} %refs_1_.5, bf16[5120,1536]{1,0:T(8,128)(2,1)} %refs_2_.6, ...), custom_call_target="tpu_custom_call" | custom-call | flops 3019898880 | bytes 15728640 | tf_op jit(solution)/shard_map/pallas_call | solution.py:119
  69.1 9.8 %shard_map.58 = (bf16[192,384]{1,0:T(8,128)(2,1)}, bf16[192,384]{1,0:T(8,128)(2,1)}, bf16[192,384]{1,0:T(8,128)(2,1)}, bf16[192,384]{1,0:T(8,128)(2,1)}, bf16[19...) custom-call(s32[4]{0:T(128)} %pad_add_fusion.place, ...), custom_call_target="tpu_custom_call" | custom-call | flops 3019898880 | bytes 7864320 | tf_op jit(solution)/shard_map/pallas_call | solution.py:119
  79.0 0.7 collective-permute-start.10
  79.7 0.7 collective-permute-done.6.refs_12_
  80.6 3.0 %collective-permute-start.4 = (bf16[192,768]{1,0:T(8,128)(2,1)S(1)}, bf16[192,768]{1,0:T(8,128)(2,1)S(1)}, u32[]{:S(2)}, u32[]{:S(2)}) collective-permute-start(bf16[192,768]{1,0:T(8,128)(2,1)S(1)} %copy-done.27), channel_id=1, source_target_pairs={{0,8},{2,10},{4,12},{6,14},{8,0},{10,2},{12,4},{14,6},{16,24},{18,... | collective-permute-start | bytes 884744 | tf_op jit(solution)/shard_map/ppermute | solution.py:18
  84.1 1.5 collective-permute-start.16
  85.6 5.3 %collective-permute-done.10.refs_17_ = bf16[192,768]{1,0:T(8,128)(2,1)S(1)} collective-permute-done((bf16[192,768]{1,0:T(8,128)(2,1)S(1)}, bf16[192,768]{1,0:T(8,128)(2,1)S(1)}, u32[]{:S(2)}, u32[]{:S(2)}) %collective-permute-start.10) | collective-permute-done | bytes 294944 | tf_op jit(solution)/shard_map/ppermute | solution.py:18
  91.4 14.4 %collective-permute-done.7.refs_13_ = bf16[192,768]{1,0:T(8,128)(2,1)S(1)} collective-permute-done((bf16[192,768]{1,0:T(8,128)(2,1)S(1)}, bf16[192,768]{1,0:T(8,128)(2,1)S(1)}, u32[]{:S(2)}, u32[]{:S(2)}) %collective-permute-start.7) | collective-permute-done | bytes 294944 | tf_op jit(solution)/shard_map/ppermute | solution.py:18
  105.9 1.4 collective-permute-start.11
  107.3 3.0 %collective-permute-start.5 = (bf16[192,384]{1,0:T(8,128)(2,1)}, bf16[192,384]{1,0:T(8,128)(2,1)S(1)}, u32[]{:S(2)}, u32[]{:S(2)}) collective-permute-start(bf16[192,384]{1,0:T(8,128)(2,1)} %get-tuple-element.80), channel_id=1, source_target_pairs={{0,8},{2,10},{4,12},{6,14},{8,0},{10,2},{12,4},{14,6},{16,24},{18,... | collective-permute-start | bytes 442376 | tf_op jit(solution)/shard_map/ppermute | solution.py:18
  110.7 1.7 collective-permute-start.12
  112.4 2.3 %collective-permute-done.11.refs_3_ = bf16[192,384]{1,0:T(8,128)(2,1)S(1)} collective-permute-done((bf16[192,384]{1,0:T(8,128)(2,1)}, bf16[192,384]{1,0:T(8,128)(2,1)S(1)}, u32[]{:S(2)}, u32[]{:S(2)}) %collective-permute-start.11) | collective-permute-done | bytes 147488 | tf_op jit(solution)/shard_map/ppermute | solution.py:18
  115.0 3.7 %collective-permute-done.8.refs_2_ = bf16[192,384]{1,0:T(8,128)(2,1)S(1)} collective-permute-done((bf16[192,384]{1,0:T(8,128)(2,1)}, bf16[192,384]{1,0:T(8,128)(2,1)S(1)}, u32[]{:S(2)}, u32[]{:S(2)}) %collective-permute-start.8) | collective-permute-done | bytes 147488 | tf_op jit(solution)/shard_map/ppermute | solution.py:18
  118.7 1.1 collective-permute-start.17
  119.8 1.0 collective-permute-start.15
  120.8 2.4 %collective-permute-start.22 = (bf16[192,384]{1,0:T(8,128)(2,1)}, bf16[192,384]{1,0:T(8,128)(2,1)S(1)}, u32[]{:S(2)}, u32[]{:S(2)}) collective-permute-start(bf16[192,384]{1,0:T(8,128)(2,1)} %get-tuple-element.103), channel_id=1, source_target_pairs={{0,24},{2,26},{4,28},{6,30},{8,16},{10,18},{12,20},{14,22},{16,8},... | collective-permute-start | bytes 442376 | tf_op jit(solution)/shard_map/ppermute | solution.py:18
  123.2 3.4 %collective-permute-done.12.refs_6_ = bf16[192,768]{1,0:T(8,128)(2,1)S(1)} collective-permute-done((bf16[192,768]{1,0:T(8,128)(2,1)S(1)}, bf16[192,768]{1,0:T(8,128)(2,1)S(1)}, u32[]{:S(2)}, u32[]{:S(2)}) %collective-permute-start.12) | collective-permute-done | bytes 294944 | tf_op jit(solution)/shard_map/ppermute | solution.py:18
  126.7 6.2 %collective-permute-done.19.refs_19_ = bf16[192,768]{1,0:T(8,128)(2,1)S(1)} collective-permute-done((bf16[192,768]{1,0:T(8,128)(2,1)S(1)}, bf16[192,768]{1,0:T(8,128)(2,1)S(1)}, u32[]{:S(2)}, u32[]{:S(2)}) %collective-permute-start.19) | collective-permute-done | bytes 294944 | tf_op jit(solution)/shard_map/ppermute | solution.py:18
  133.0 5.7 %collective-permute-done.17.refs_15_ = bf16[192,768]{1,0:T(8,128)(2,1)S(1)} collective-permute-done((bf16[192,768]{1,0:T(8,128)(2,1)S(1)}, bf16[192,768]{1,0:T(8,128)(2,1)S(1)}, u32[]{:S(2)}, u32[]{:S(2)}) %collective-permute-start.17) | collective-permute-done | bytes 294944 | tf_op jit(solution)/shard_map/ppermute | solution.py:18
  138.6 3.2 %collective-permute-done.15.refs_11_ = bf16[192,768]{1,0:T(8,128)(2,1)S(1)} collective-permute-done((bf16[192,768]{1,0:T(8,128)(2,1)S(1)}, bf16[192,768]{1,0:T(8,128)(2,1)S(1)}, u32[]{:S(2)}, u32[]{:S(2)}) %collective-permute-start.15) | collective-permute-done | bytes 294944 | tf_op jit(solution)/shard_map/ppermute | solution.py:18
  142.5 13.9 %shard_map.59 = (bf16[192,384]{1,0:T(8,128)(2,1)}, bf16[192,384]{1,0:T(8,128)(2,1)}, bf16[192,384]{1,0:T(8,128)(2,1)}, bf16[192,384]{1,0:T(8,128)(2,1)}) custom-call(s32[16,2]{1,0:T(8,128)} %bitcast.9, s32[4]{0:T(128)} %pad_add_fusion.place, bf16[192,384]{1,0:T(8,128)(2,1)} %get-tuple-element.73.refs_0_, bf16[192,384]{1,0:T(8,128)(2,1)} %copy-done.33, ...), custom_call_target="tpu_custom_call" | custom-call | flops 2717908992 | bytes 5898240 | tf_op jit(solution)/shard_map/pallas_call | solution.py:249
  156.8 2.2 %collective-permute-start.26 = (bf16[192,384]{1,0:T(8,128)(2,1)}, bf16[192,384]{1,0:T(8,128)(2,1)S(1)}, u32[]{:S(2)}, u32[]{:S(2)}) collective-permute-start(bf16[192,384]{1,0:T(8,128)(2,1)} %get-tuple-element.107), channel_id=1, source_target_pairs={{0,16},{2,18},{4,20},{6,22},{8,24},{10,26},{12,28},{14,30},{16,0},... | collective-permute-start | bytes 442376 | tf_op jit(solution)/shard_map/ppermute | solution.py:18
  159.0 1.9 collective-permute-start.28
  160.9 0.6 copy-done.34
  161.5 0.6 copy-done.35
  162.2 14.1 %shard_map.60 = (bf16[192,384]{1,0:T(8,128)(2,1)}, bf16[192,384]{1,0:T(8,128)(2,1)}, bf16[192,384]{1,0:T(8,128)(2,1)}, bf16[192,384]{1,0:T(8,128)(2,1)}) custom-call(s32[16,2]{1,0:T(8,128)} %bitcast.10, s32[4]{0:T(128)} %pad_add_fusion.place, bf16[192,384]{1,0:T(8,128)(2,1)} %get-tuple-element.97.refs_0_, bf16[192,384]{1,0:T(8,128)(2,1)} %copy-done.35, ...), custom_call_target="tpu_custom_call" | custom-call | flops 2717908992 | bytes 5898240 | tf_op jit(solution)/shard_map/pallas_call | solution.py:249
  176.5 2.2 %collective-permute-start.27 = (bf16[192,384]{1,0:T(8,128)(2,1)}, bf16[192,384]{1,0:T(8,128)(2,1)S(1)}, u32[]{:S(2)}, u32[]{:S(2)}) collective-permute-start(bf16[192,384]{1,0:T(8,128)(2,1)} %get-tuple-element.108), channel_id=1, source_target_pairs={{0,18},{2,16},{4,22},{6,20},{8,26},{10,24},{12,30},{14,28},{16,2},... | collective-permute-start | bytes 442376 | tf_op jit(solution)/shard_map/ppermute | solution.py:18
  178.7 1.9 collective-permute-start.29
  180.6 4.0 %collective-permute-done.25.refs_3_ = bf16[192,384]{1,0:T(8,128)(2,1)S(1)} collective-permute-done((bf16[192,384]{1,0:T(8,128)(2,1)}, bf16[192,384]{1,0:T(8,128)(2,1)S(1)}, u32[]{:S(2)}, u32[]{:S(2)}) %collective-permute-start.25) | collective-permute-done | bytes 147488 | tf_op jit(solution)/shard_map/ppermute | solution.py:18
  184.7 4.9 %collective-permute-done.27.refs_5_ = bf16[192,384]{1,0:T(8,128)(2,1)S(1)} collective-permute-done((bf16[192,384]{1,0:T(8,128)(2,1)}, bf16[192,384]{1,0:T(8,128)(2,1)S(1)}, u32[]{:S(2)}, u32[]{:S(2)}) %collective-permute-start.27) | collective-permute-done | bytes 147488 | tf_op jit(solution)/shard_map/ppermute | solution.py:18
  189.7 0.6 copy-done.8
  190.3 3.6 %shard_map.61 = bf16[2,192,1536]{2,1,0:T(8,128)(2,1)} custom-call(s32[4]{0:T(128)} %pad_add_fusion.place, bf16[192,384]{1,0:T(8,128)(2,1)} %get-tuple-element.95.refs_0_, bf16[192,384]{1,0:T(8,128)(2,1)} %copy-done.6, bf16[192,384]{1,0:T(8,128)(2,1)} %copy-done.3, bf16[192,384]{1,0:T(8,128)(2,1)} %copy-done.7, bf16[192,384]{1,0:T(8,128)(2,1)} %copy-done.4, ...), custom_call_target="tpu_custom_call" | custom-call | tf_op jit(solution)/shard_map/pallas_call | solution.py:289
  (105 shorter events, 5.2 us)
Async XLA Ops:
  2.6 18.2 %collective-permute-start.1 = (bf16[192,2560]{1,0:T(8,128)(2,1)}, bf16[192,2560]{1,0:T(8,128)(2,1)S(1)}, u32[]{:S(2)}, u32[]{:S(2)}) collective-permute-start(bf16[192,2560]{1,0:T(8,128)(2,1)} %get-tuple-element.111), channel_id=1, source_target_pairs={{0,2},{2,0},{4,6},{6,4},{8,10},{10,8},{12,14},{14,12},{16,18},{18,... | collective-permute-start | bytes 2949128 | tf_op jit(solution)/shard_map/ppermute | solution.py:18
  3.0 37.3 %collective-permute-start = (bf16[192,2560]{1,0:T(8,128)(2,1)S(1)}, bf16[192,2560]{1,0:T(8,128)(2,1)S(1)}, u32[]{:S(2)}, u32[]{:S(2)}) collective-permute-start(bf16[192,2560]{1,0:T(8,128)(2,1)S(1)} %get-tuple-element.112), channel_id=1, source_target_pairs={{0,1},{1,0},{2,3},{3,2},{4,5},{5,4},{6,7},{7,6},{8,9},{9,8},{10,11... | collective-permute-start | bytes 2949128 | tf_op jit(solution)/shard_map/ppermute | solution.py:18
  6.4 12.3 %all-to-all-start = ((s32[16,1,2]{2,1,0:T(1,128)}), s32[16,1,2]{2,1,0:T(1,128)S(1)}, u32[]{:S(2)}, u32[]{:S(2)}) async-start(s32[16,1,2]{2,1,0:T(1,128)} %broadcast_in_dim.2), calls=%async_computation | async-start | bytes 16384 | tf_op jit(solution)/shard_map/all_to_all | solution.py:329
  18.7 21.6 %copy-start.10 = (s32[16,1,2]{2,1,0:T(1,128)}, s32[16,1,2]{2,1,0:T(1,128)S(1)}, u32[]{:S(2)}) copy-start(s32[16,1,2]{2,1,0:T(1,128)S(1)} %all-to-all-done) | copy-start | bytes 388
  20.8 36.1 %collective-permute-start.2 = (bf16[192,2560]{1,0:T(8,128)(2,1)S(1)}, bf16[192,2560]{1,0:T(8,128)(2,1)S(1)}, u32[]{:S(2)}, u32[]{:S(2)}) collective-permute-start(bf16[192,2560]{1,0:T(8,128)(2,1)S(1)} %collective-permute-done.1.other_ref), channel_id=1, source_target_pairs={{0,1},{1,0},{2,3},{3,2},{4,5},{5,4},{6,7},{7,6},{8,9},{9,8},{10,11... | collective-permute-start | bytes 2949128 | tf_op jit(solution)/shard_map/ppermute | solution.py:18
  52.5 26.5 %collective-permute-start.9 = (bf16[192,768]{1,0:T(8,128)(2,1)}, bf16[192,768]{1,0:T(8,128)(2,1)S(1)}, u32[]{:S(2)}, u32[]{:S(2)}) collective-permute-start(bf16[192,768]{1,0:T(8,128)(2,1)} %get-tuple-element.88), channel_id=1, source_target_pairs={{0,24},{2,26},{4,28},{6,30},{8,16},{10,18},{12,20},{14,22},{16,8},... | collective-permute-start | bytes 884744 | tf_op jit(solution)/shard_map/ppermute | solution.py:18
  53.1 27.3 %collective-permute-start.6 = (bf16[192,768]{1,0:T(8,128)(2,1)}, bf16[192,768]{1,0:T(8,128)(2,1)S(1)}, u32[]{:S(2)}, u32[]{:S(2)}) collective-permute-start(bf16[192,768]{1,0:T(8,128)(2,1)} %get-tuple-element.81), channel_id=1, source_target_pairs={{0,16},{2,18},{4,20},{6,22},{8,24},{10,26},{12,28},{14,30},{16,0},... | collective-permute-start | bytes 884744 | tf_op jit(solution)/shard_map/ppermute | solution.py:18
  54.3 26.3 %collective-permute-start.3 = (bf16[192,768]{1,0:T(8,128)(2,1)}, bf16[192,768]{1,0:T(8,128)(2,1)S(1)}, u32[]{:S(2)}, u32[]{:S(2)}) collective-permute-start(bf16[192,768]{1,0:T(8,128)(2,1)} %get-tuple-element.74), channel_id=1, source_target_pairs={{0,8},{2,10},{4,12},{6,14},{8,0},{10,2},{12,4},{14,6},{16,24},{18,... | collective-permute-start | bytes 884744 | tf_op jit(solution)/shard_map/ppermute | solution.py:18
  69.1 41.2 %copy-start.15 = (bf16[192,768]{1,0:T(8,128)(2,1)S(1)}, bf16[192,768]{1,0:T(8,128)(2,1)}, u32[]{:S(2)}) copy-start(bf16[192,768]{1,0:T(8,128)(2,1)} %get-tuple-element.72.refs_5_) | copy-start | bytes 884740
  69.1 41.6 %copy-start.11 = (bf16[192,768]{1,0:T(8,128)(2,1)S(1)}, bf16[192,768]{1,0:T(8,128)(2,1)}, u32[]{:S(2)}) copy-start(bf16[192,768]{1,0:T(8,128)(2,1)} %get-tuple-element.71.refs_4_) | copy-start | bytes 884740
  79.0 62.8 %copy-start.12 = (bf16[192,768]{1,0:T(8,128)(2,1)}, bf16[192,768]{1,0:T(8,128)(2,1)S(1)}, u32[]{:S(2)}) copy-start(bf16[192,768]{1,0:T(8,128)(2,1)S(1)} %collective-permute-done.9.refs_16_) | copy-start | bytes 884740
  79.0 11.9 %collective-permute-start.10 = (bf16[192,768]{1,0:T(8,128)(2,1)S(1)}, bf16[192,768]{1,0:T(8,128)(2,1)S(1)}, u32[]{:S(2)}, u32[]{:S(2)}) collective-permute-start(bf16[192,768]{1,0:T(8,128)(2,1)S(1)} %copy-done.29), channel_id=1, source_target_pairs={{0,24},{2,26},{4,28},{6,30},{8,16},{10,18},{12,20},{14,22},{16,8},... | collective-permute-start | bytes 884744 | tf_op jit(solution)/shard_map/ppermute | solution.py:18
  80.4 61.4 %copy-start.13 = (bf16[192,768]{1,0:T(8,128)(2,1)}, bf16[192,768]{1,0:T(8,128)(2,1)S(1)}, u32[]{:S(2)}) copy-start(bf16[192,768]{1,0:T(8,128)(2,1)S(1)} %collective-permute-done.6.refs_12_) | copy-start | bytes 884740
  80.4 25.5 %collective-permute-start.7 = (bf16[192,768]{1,0:T(8,128)(2,1)S(1)}, bf16[192,768]{1,0:T(8,128)(2,1)S(1)}, u32[]{:S(2)}, u32[]{:S(2)}) collective-permute-start(bf16[192,768]{1,0:T(8,128)(2,1)S(1)} %copy-done.28), channel_id=1, source_target_pairs={{0,16},{2,18},{4,20},{6,22},{8,24},{10,26},{12,28},{14,30},{16,0},... | collective-permute-start | bytes 884744 | tf_op jit(solution)/shard_map/ppermute | solution.py:18
  80.6 61.2 %copy-start.14 = (bf16[192,768]{1,0:T(8,128)(2,1)}, bf16[192,768]{1,0:T(8,128)(2,1)S(1)}, u32[]{:S(2)}) copy-start(bf16[192,768]{1,0:T(8,128)(2,1)S(1)} %collective-permute-done.3.refs_8_) | copy-start | bytes 884740
  80.6 26.7 %collective-permute-start.4 = (bf16[192,768]{1,0:T(8,128)(2,1)S(1)}, bf16[192,768]{1,0:T(8,128)(2,1)S(1)}, u32[]{:S(2)}, u32[]{:S(2)}) collective-permute-start(bf16[192,768]{1,0:T(8,128)(2,1)S(1)} %copy-done.27), channel_id=1, source_target_pairs={{0,8},{2,10},{4,12},{6,14},{8,0},{10,2},{12,4},{14,6},{16,24},{18,... | collective-permute-start | bytes 884744 | tf_op jit(solution)/shard_map/ppermute | solution.py:18
  83.6 23.7 %collective-permute-start.18 = (bf16[192,768]{1,0:T(8,128)(2,1)S(1)}, bf16[192,768]{1,0:T(8,128)(2,1)S(1)}, u32[]{:S(2)}, u32[]{:S(2)}) collective-permute-start(bf16[192,768]{1,0:T(8,128)(2,1)S(1)} %collective-permute-done.9.refs_16_), channel_id=1, source_target_pairs={{0,4},{2,6},{4,0},{6,2},{8,12},{10,14},{12,8},{14,10},{16,20},{18,... | collective-permute-start | bytes 884744 | tf_op jit(solution)/shard_map/ppermute | solution.py:18
  84.1 26.2 %collective-permute-start.16 = (bf16[192,768]{1,0:T(8,128)(2,1)S(1)}, bf16[192,768]{1,0:T(8,128)(2,1)S(1)}, u32[]{:S(2)}, u32[]{:S(2)}) collective-permute-start(bf16[192,768]{1,0:T(8,128)(2,1)S(1)} %collective-permute-done.6.refs_12_), channel_id=1, source_target_pairs={{0,4},{2,6},{4,0},{6,2},{8,12},{10,14},{12,8},{14,10},{16,20},{18,... | collective-permute-start | bytes 884744 | tf_op jit(solution)/shard_map/ppermute | solution.py:18
  90.9 50.9 %copy-start.16 = (bf16[192,768]{1,0:T(8,128)(2,1)}, bf16[192,768]{1,0:T(8,128)(2,1)S(1)}, u32[]{:S(2)}) copy-start(bf16[192,768]{1,0:T(8,128)(2,1)S(1)} %collective-permute-done.10.refs_17_) | copy-start | bytes 884740
  90.9 19.8 %collective-permute-start.14 = (bf16[192,768]{1,0:T(8,128)(2,1)S(1)}, bf16[192,768]{1,0:T(8,128)(2,1)S(1)}, u32[]{:S(2)}, u32[]{:S(2)}) collective-permute-start(bf16[192,768]{1,0:T(8,128)(2,1)S(1)} %collective-permute-done.3.refs_8_), channel_id=1, source_target_pairs={{0,4},{2,6},{4,0},{6,2},{8,12},{10,14},{12,8},{14,10},{16,20},{18,... | collective-permute-start | bytes 884744 | tf_op jit(solution)/shard_map/ppermute | solution.py:18
  105.9 36.0 %copy-start.17 = (bf16[192,768]{1,0:T(8,128)(2,1)}, bf16[192,768]{1,0:T(8,128)(2,1)S(1)}, u32[]{:S(2)}) copy-start(bf16[192,768]{1,0:T(8,128)(2,1)S(1)} %collective-permute-done.7.refs_13_) | copy-start | bytes 884740
  105.9 8.8 %collective-permute-start.11 = (bf16[192,384]{1,0:T(8,128)(2,1)}, bf16[192,384]{1,0:T(8,128)(2,1)S(1)}, u32[]{:S(2)}, u32[]{:S(2)}) collective-permute-start(bf16[192,384]{1,0:T(8,128)(2,1)} %get-tuple-element.94), channel_id=1, source_target_pairs={{0,24},{2,26},{4,28},{6,30},{8,16},{10,18},{12,20},{14,22},{16,8},... | collective-permute-start | bytes 442376 | tf_op jit(solution)/shard_map/ppermute | solution.py:18
  107.3 34.5 %copy-start.18 = (bf16[192,768]{1,0:T(8,128)(2,1)}, bf16[192,768]{1,0:T(8,128)(2,1)S(1)}, u32[]{:S(2)}) copy-start(bf16[192,768]{1,0:T(8,128)(2,1)S(1)} %collective-permute-done.4.refs_9_) | copy-start | bytes 884740
  107.3 11.4 %collective-permute-start.8 = (bf16[192,384]{1,0:T(8,128)(2,1)}, bf16[192,384]{1,0:T(8,128)(2,1)S(1)}, u32[]{:S(2)}, u32[]{:S(2)}) collective-permute-start(bf16[192,384]{1,0:T(8,128)(2,1)} %get-tuple-element.87), channel_id=1, source_target_pairs={{0,16},{2,18},{4,20},{6,22},{8,24},{10,26},{12,28},{14,30},{16,0},... | collective-permute-start | bytes 442376 | tf_op jit(solution)/shard_map/ppermute | solution.py:18
  107.3 34.5 %copy-start.19 = (bf16[192,768]{1,0:T(8,128)(2,1)}, bf16[192,768]{1,0:T(8,128)(2,1)S(1)}, u32[]{:S(2)}) copy-start(bf16[192,768]{1,0:T(8,128)(2,1)S(1)} %collective-permute-done.18.refs_18_) | copy-start | bytes 884740
  107.3 12.5 %collective-permute-start.5 = (bf16[192,384]{1,0:T(8,128)(2,1)}, bf16[192,384]{1,0:T(8,128)(2,1)S(1)}, u32[]{:S(2)}, u32[]{:S(2)}) collective-permute-start(bf16[192,384]{1,0:T(8,128)(2,1)} %get-tuple-element.80), channel_id=1, source_target_pairs={{0,8},{2,10},{4,12},{6,14},{8,0},{10,2},{12,4},{14,6},{16,24},{18,... | collective-permute-start | bytes 442376 | tf_op jit(solution)/shard_map/ppermute | solution.py:18
  110.3 31.6 %copy-start.20 = (bf16[192,768]{1,0:T(8,128)(2,1)}, bf16[192,768]{1,0:T(8,128)(2,1)S(1)}, u32[]{:S(2)}) copy-start(bf16[192,768]{1,0:T(8,128)(2,1)S(1)} %collective-permute-done.16.refs_14_) | copy-start | bytes 884740
  110.3 10.5 %collective-permute-start.13 = (bf16[192,768]{1,0:T(8,128)(2,1)S(1)}, bf16[192,768]{1,0:T(8,128)(2,1)S(1)}, u32[]{:S(2)}, u32[]{:S(2)}) collective-permute-start(bf16[192,768]{1,0:T(8,128)(2,1)S(1)} %copy-done.15), channel_id=1, source_target_pairs={{0,4},{2,6},{4,0},{6,2},{8,12},{10,14},{12,8},{14,10},{16,20},{18,... | collective-permute-start | bytes 884744 | tf_op jit(solution)/shard_map/ppermute | solution.py:18
  110.7 31.2 %copy-start.21 = (bf16[192,768]{1,0:T(8,128)(2,1)}, bf16[192,768]{1,0:T(8,128)(2,1)S(1)}, u32[]{:S(2)}) copy-start(bf16[192,768]{1,0:T(8,128)(2,1)S(1)} %collective-permute-done.14.refs_10_) | copy-start | bytes 884740
  110.7 15.9 %collective-permute-start.12 = (bf16[192,768]{1,0:T(8,128)(2,1)S(1)}, bf16[192,768]{1,0:T(8,128)(2,1)S(1)}, u32[]{:S(2)}, u32[]{:S(2)}) collective-permute-start(bf16[192,768]{1,0:T(8,128)(2,1)S(1)} %copy-done.11), channel_id=1, source_target_pairs={{0,4},{2,6},{4,0},{6,2},{8,12},{10,14},{12,8},{14,10},{16,20},{18,... | collective-permute-start | bytes 884744 | tf_op jit(solution)/shard_map/ppermute | solution.py:18
  114.7 27.2 %copy-start.30 = (bf16[192,384]{1,0:T(8,128)(2,1)}, bf16[192,384]{1,0:T(8,128)(2,1)S(1)}, u32[]{:S(2)}) copy-start(bf16[192,384]{1,0:T(8,128)(2,1)S(1)} %collective-permute-done.11.refs_3_) | copy-start | bytes 442372
  114.7 18.2 %collective-permute-start.19 = (bf16[192,768]{1,0:T(8,128)(2,1)S(1)}, bf16[192,768]{1,0:T(8,128)(2,1)S(1)}, u32[]{:S(2)}, u32[]{:S(2)}) collective-permute-start(bf16[192,768]{1,0:T(8,128)(2,1)S(1)} %collective-permute-done.10.refs_17_), channel_id=1, source_target_pairs={{0,4},{2,6},{4,0},{6,2},{8,12},{10,14},{12,8},{14,10},{16,20},{18,... | collective-permute-start | bytes 884744 | tf_op jit(solution)/shard_map/ppermute | solution.py:18
  118.7 23.1 %copy-start.31 = (bf16[192,384]{1,0:T(8,128)(2,1)}, bf16[192,384]{1,0:T(8,128)(2,1)S(1)}, u32[]{:S(2)}) copy-start(bf16[192,384]{1,0:T(8,128)(2,1)S(1)} %collective-permute-done.8.refs_2_) | copy-start | bytes 442372
  118.7 19.9 %collective-permute-start.17 = (bf16[192,768]{1,0:T(8,128)(2,1)S(1)}, bf16[192,768]{1,0:T(8,128)(2,1)S(1)}, u32[]{:S(2)}, u32[]{:S(2)}) collective-permute-start(bf16[192,768]{1,0:T(8,128)(2,1)S(1)} %collective-permute-done.7.refs_13_), channel_id=1, source_target_pairs={{0,4},{2,6},{4,0},{6,2},{8,12},{10,14},{12,8},{14,10},{16,20},{18,... | collective-permute-start | bytes 884744 | tf_op jit(solution)/shard_map/ppermute | solution.py:18
  119.8 22.1 %copy-start.33 = (bf16[192,384]{1,0:T(8,128)(2,1)}, bf16[192,384]{1,0:T(8,128)(2,1)S(1)}, u32[]{:S(2)}) copy-start(bf16[192,384]{1,0:T(8,128)(2,1)S(1)} %collective-permute-done.5.refs_1_) | copy-start | bytes 442372
  119.8 22.0 %collective-permute-start.15 = (bf16[192,768]{1,0:T(8,128)(2,1)S(1)}, bf16[192,768]{1,0:T(8,128)(2,1)S(1)}, u32[]{:S(2)}, u32[]{:S(2)}) collective-permute-start(bf16[192,768]{1,0:T(8,128)(2,1)S(1)} %collective-permute-done.4.refs_9_), channel_id=1, source_target_pairs={{0,4},{2,6},{4,0},{6,2},{8,12},{10,14},{12,8},{14,10},{16,20},{18,... | collective-permute-start | bytes 884744 | tf_op jit(solution)/shard_map/ppermute | solution.py:18
  120.8 21.1 %copy-start.22 = (bf16[192,768]{1,0:T(8,128)(2,1)}, bf16[192,768]{1,0:T(8,128)(2,1)S(1)}, u32[]{:S(2)}) copy-start(bf16[192,768]{1,0:T(8,128)(2,1)S(1)} %collective-permute-done.13.refs_7_) | copy-start | bytes 884740
  120.8 38.2 %collective-permute-start.22 = (bf16[192,384]{1,0:T(8,128)(2,1)}, bf16[192,384]{1,0:T(8,128)(2,1)S(1)}, u32[]{:S(2)}, u32[]{:S(2)}) collective-permute-start(bf16[192,384]{1,0:T(8,128)(2,1)} %get-tuple-element.103), channel_id=1, source_target_pairs={{0,24},{2,26},{4,28},{6,30},{8,16},{10,18},{12,20},{14,22},{16,8},... | collective-permute-start | bytes 442376 | tf_op jit(solution)/shard_map/ppermute | solution.py:18
  126.6 15.3 %copy-start.23 = (bf16[192,768]{1,0:T(8,128)(2,1)}, bf16[192,768]{1,0:T(8,128)(2,1)S(1)}, u32[]{:S(2)}) copy-start(bf16[192,768]{1,0:T(8,128)(2,1)S(1)} %collective-permute-done.12.refs_6_) | copy-start | bytes 884740
  126.6 34.3 %collective-permute-start.21 = (bf16[192,384]{1,0:T(8,128)(2,1)}, bf16[192,384]{1,0:T(8,128)(2,1)S(1)}, u32[]{:S(2)}, u32[]{:S(2)}) collective-permute-start(bf16[192,384]{1,0:T(8,128)(2,1)} %get-tuple-element.101), channel_id=1, source_target_pairs={{0,16},{2,18},{4,20},{6,22},{8,24},{10,26},{12,28},{14,30},{16,0},... | collective-permute-start | bytes 442376 | tf_op jit(solution)/shard_map/ppermute | solution.py:18
  132.9 28.0 %collective-permute-start.20 = (bf16[192,384]{1,0:T(8,128)(2,1)}, bf16[192,384]{1,0:T(8,128)(2,1)S(1)}, u32[]{:S(2)}, u32[]{:S(2)}) collective-permute-start(bf16[192,384]{1,0:T(8,128)(2,1)} %get-tuple-element.99), channel_id=1, source_target_pairs={{0,8},{2,10},{4,12},{6,14},{8,0},{10,2},{12,4},{14,6},{16,24},{18,... | collective-permute-start | bytes 442376 | tf_op jit(solution)/shard_map/ppermute | solution.py:18
  156.4 20.0 %collective-permute-start.24 = (bf16[192,384]{1,0:T(8,128)(2,1)}, bf16[192,384]{1,0:T(8,128)(2,1)S(1)}, u32[]{:S(2)}, u32[]{:S(2)}) collective-permute-start(bf16[192,384]{1,0:T(8,128)(2,1)} %get-tuple-element.105), channel_id=1, source_target_pairs={{0,8},{2,10},{4,12},{6,14},{8,0},{10,2},{12,4},{14,6},{16,24},{18,... | collective-permute-start | bytes 442376 | tf_op jit(solution)/shard_map/ppermute | solution.py:18
  156.8 21.9 %collective-permute-start.26 = (bf16[192,384]{1,0:T(8,128)(2,1)}, bf16[192,384]{1,0:T(8,128)(2,1)S(1)}, u32[]{:S(2)}, u32[]{:S(2)}) collective-permute-start(bf16[192,384]{1,0:T(8,128)(2,1)} %get-tuple-element.107), channel_id=1, source_target_pairs={{0,16},{2,18},{4,20},{6,22},{8,24},{10,26},{12,28},{14,30},{16,0},... | collective-permute-start | bytes 442376 | tf_op jit(solution)/shard_map/ppermute | solution.py:18
  159.0 21.6 %collective-permute-start.28 = (bf16[192,384]{1,0:T(8,128)(2,1)}, bf16[192,384]{1,0:T(8,128)(2,1)S(1)}, u32[]{:S(2)}, u32[]{:S(2)}) collective-permute-start(bf16[192,384]{1,0:T(8,128)(2,1)} %get-tuple-element.109), channel_id=1, source_target_pairs={{0,24},{2,26},{4,28},{6,30},{8,16},{10,18},{12,20},{14,22},{16,8},... | collective-permute-start | bytes 442376 | tf_op jit(solution)/shard_map/ppermute | solution.py:18
  176.3 4.3 %collective-permute-start.23 = (bf16[192,384]{1,0:T(8,128)(2,1)}, bf16[192,384]{1,0:T(8,128)(2,1)S(1)}, u32[]{:S(2)}, u32[]{:S(2)}) collective-permute-start(bf16[192,384]{1,0:T(8,128)(2,1)} %get-tuple-element.104), channel_id=1, source_target_pairs={{0,2},{2,0},{4,6},{6,4},{8,10},{10,8},{12,14},{14,12},{16,18},{18,... | collective-permute-start | bytes 442376 | tf_op jit(solution)/shard_map/ppermute | solution.py:18
  176.4 8.3 %collective-permute-start.25 = (bf16[192,384]{1,0:T(8,128)(2,1)}, bf16[192,384]{1,0:T(8,128)(2,1)S(1)}, u32[]{:S(2)}, u32[]{:S(2)}) collective-permute-start(bf16[192,384]{1,0:T(8,128)(2,1)} %get-tuple-element.106), channel_id=1, source_target_pairs={{0,10},{2,8},{4,14},{6,12},{8,2},{10,0},{12,6},{14,4},{16,26},{18,... | collective-permute-start | bytes 442376 | tf_op jit(solution)/shard_map/ppermute | solution.py:18
  176.5 13.1 %collective-permute-start.27 = (bf16[192,384]{1,0:T(8,128)(2,1)}, bf16[192,384]{1,0:T(8,128)(2,1)S(1)}, u32[]{:S(2)}, u32[]{:S(2)}) collective-permute-start(bf16[192,384]{1,0:T(8,128)(2,1)} %get-tuple-element.108), channel_id=1, source_target_pairs={{0,18},{2,16},{4,22},{6,20},{8,26},{10,24},{12,30},{14,28},{16,2},... | collective-permute-start | bytes 442376 | tf_op jit(solution)/shard_map/ppermute | solution.py:18
  178.7 10.9 %collective-permute-start.29 = (bf16[192,384]{1,0:T(8,128)(2,1)}, bf16[192,384]{1,0:T(8,128)(2,1)S(1)}, u32[]{:S(2)}, u32[]{:S(2)}) collective-permute-start(bf16[192,384]{1,0:T(8,128)(2,1)} %get-tuple-element.110), channel_id=1, source_target_pairs={{0,26},{2,24},{4,30},{6,28},{8,18},{10,16},{12,22},{14,20},{16,10}... | collective-permute-start | bytes 442376 | tf_op jit(solution)/shard_map/ppermute | solution.py:18
  (20 other events, 105.8 us)

commit v6 on v5

--- a/solution.py
+++ b/solution.py
@@ -16,6 +16,9 @@
 
 def exchange(value, axis, size, bit):
     return lax.ppermute(value, axis, [(i, i ^ bit) for i in range(size)])
+
+
+EXTRA = 16
 
 
 def own_body(weights, place, mine_ref, other_ref, *refs):
@@ -59,13 +62,14 @@
     )(place, hidden_in, other, *weights)
 
 
-def rest_body(shares, weights, chunks, away, place, *refs):
+def rest_body(shares, weights, chunks, away, extra, place, *refs):
     inputs = refs[: shares * chunks]
     refs = refs[shares * chunks :]
     weight_refs, refs = refs[: weights * shares], refs[weights * shares :]
     start_refs, refs = refs[:weights], refs[weights:]
     out_refs, flats = refs[: chunks * len(away)], refs[chunks * len(away) :]
     rows, width = out_refs[0].shape
+    rows -= extra
     width //= weights
     step = pl.program_id(0)
     if chunks > 1:
@@ -92,12 +96,16 @@
         def _():
             for c in range(chunks):
                 for n in range(weights):
-                    out_refs[c * len(away) + index][:, n * width : (n + 1) * width] = made[n][
+                    out_refs[c * len(away) + index][:rows, n * width : (n + 1) * width] = made[n][
                         c * rows : (c + 1) * rows
                     ]
-
-
-def rest_products(received, chosen, weights, starts, place, ways, away):
+            if extra:
+                line = lax.broadcasted_iota(jnp.int32, (extra, weights * width), 0)
+                spans = jnp.where(line < extra // 2, place[4], place[5]).astype(jnp.float32)
+                out_refs[index][rows:] = spans.astype(jnp.bfloat16)
+
+
+def rest_products(received, chosen, weights, starts, place, ways, away, extra=0):
     shares = len(received[0])
     rows, feats = received[0][0].shape
     width = weights[0].shape[1] // ways
@@ -117,13 +125,13 @@
     columns = width * len(weights)
     scratch = [pltpu.VMEM((chunks * rows, feats), jnp.bfloat16)] * (shares if chunks > 1 else 0)
     outs = pl.pallas_call(
-        functools.partial(rest_body, shares, len(weights), chunks, away),
-        out_shape=[jax.ShapeDtypeStruct((rows, columns), jnp.bfloat16)] * (chunks * len(away)),
+        functools.partial(rest_body, shares, len(weights), chunks, away, extra),
+        out_shape=[jax.ShapeDtypeStruct((rows + extra, columns), jnp.bfloat16)] * (chunks * len(away)),
         grid_spec=pltpu.PrefetchScalarGridSpec(
             num_scalar_prefetch=1,
             grid=(len(away),),
             in_specs=in_specs,
-            out_specs=[pl.BlockSpec((rows, columns), lambda i, place: (0, 0))] * (chunks * len(away)),
+            out_specs=[pl.BlockSpec((rows + extra, columns), lambda i, place: (0, 0))] * (chunks * len(away)),
             scratch_shapes=scratch,
         ),
         compiler_params=pltpu.CompilerParams(vmem_limit_bytes=VMEM_LIMIT),
@@ -141,7 +149,7 @@
     return [dict(zip(away, outs[c * len(away) : (c + 1) * len(away)])) for c in range(chunks)]
 
 
-def attend_body(block, ways, offsets, spans, tile, table, place, *refs):
+def attend_body(block, ways, offsets, spans, tile, table, *refs):
     count = len(offsets)
     query_refs = refs[:ways]
     block_refs = refs[ways : ways + count]
@@ -151,11 +159,10 @@
     half = rows // 2
     heads = width // HD
     rest = count // ways
-    seq = place[2]
 
     copies = []
     for slot, offset in enumerate(offsets):
-        low = table[place[3] ^ offset, seq]
+        low = table[offset]
         for part, span in ((0, low), (1, spans - 1 - low)):
             copies.append(
                 pltpu.make_async_copy(
@@ -171,7 +178,7 @@
         jnp.int32, (half, 128), 1
     )
     for a in range(ways):
-        low = table[place[3] ^ (a * rest + block), seq]
+        low = table[a * rest + block]
         here = slice(a * half, (a + 1) * half)
         for part, span in ((0, low), (1, spans - 1 - low)):
             asked[part, here] = query_refs[a][part * half : (part + 1) * half]
@@ -234,7 +241,7 @@
             total[...] = jnp.zeros_like(total)
 
 
-def attend(block, queries, blocks, table, place):
+def attend(block, queries, blocks, table):
     rows, width = queries[0].shape
     ways, count = len(queries), len(blocks)
     offsets = sorted(blocks)
@@ -250,7 +257,7 @@
         functools.partial(attend_body, block, ways, offsets, spans, tile),
         out_shape=[jax.ShapeDtypeStruct((rows, width), jnp.bfloat16)] * ways,
         grid=(1,),
-        in_specs=[smem, smem]
+        in_specs=[smem]
         + [pl.BlockSpec((rows, width), lambda i: (0, 0))] * ways
         + [pl.BlockSpec(memory_space=pl.ANY)] * count,
         out_specs=[pl.BlockSpec((rows, width), lambda i: (0, 0))] * ways,
@@ -270,7 +277,7 @@
             bytes_accessed=4 * length * width + 4 * ways * rows * width,
             transcendentals=flops // (4 * HD),
         ),
-    )(table, place, *queries, *[blocks[i] for i in offsets])
+    )(table, *queries, *[blocks[i] for i in offsets])
 
 
 def assemble_body(ways, sequences, place, *refs):
@@ -325,34 +332,49 @@
     other = over_ctx(lax.dynamic_index_in_dim(hidden_in, 1 - core, 0, keepdims=False), 1)
     received = [other_shares(mine), other_shares(other)]
 
-    firsts = jnp.broadcast_to((event_pos[:, 0] // (rows // 2))[None], (ctx_size, 2))
-    table = lax.all_to_all(firsts, "ctx", 0, 0, tiled=True)
-
     start_k, start_v, start_q = own_products(hidden_in, other, [w_k, w_v, w_q], place, ways)
 
-    later = jnp.concatenate([place, table.reshape(-1)])
-    (made_0,) = rest_products(received, [0], [w_k, w_v], [start_k, start_v], later, ways, away)
+    spans = event_pos[:, 0] // (rows // 2)
+    span_other = over_ctx(lax.dynamic_index_in_dim(spans, 1 - core, 0), 1)
+    later = jnp.concatenate([place, lax.dynamic_index_in_dim(spans, core, 0), span_other])
+    made_0 = {}
+    for part in (away[: ways // 2], away[ways // 2 :]):
+        if part:
+            made_0.update(
+                rest_products(received, [0], [w_k, w_v], [start_k, start_v], later, ways, part, EXTRA)[0]
+            )
+    first = {a: over_ctx(made_0[a], a * rest) for a in away}
+    ahead = over_ctx(made_0[0], rest // 2)
     (made_1,) = rest_products(received, [1], [w_k, w_v], [start_k, start_v], place, ways, away)
     received, made_1 = lax.optimization_barrier((received, made_1))
+    ahead_1 = over_ctx(made_1[0], rest // 2)
     asked = rest_products(received, [0, 1], [w_q], [start_q], place, ways, away)
-    first = {a: over_ctx(made_0[a], a * rest) for a in away}
     for a in away:
         first[a], asked[0][a] = lax.optimization_barrier((first[a], asked[0][a]))
     blocks = {a * rest: first[a] for a in away}
+    blocks[rest // 2] = ahead
+    blocks[rest // 2 + 1] = ahead_1
     queries = [{}, {}]
     for a in away:
-        last = first[a]
+        last = (first[a], ahead)
         for made, keep, key in ((made_1, blocks, a * rest + 1), (asked[0], queries[0], a), (asked[1], queries[1], a)):
             value, last = lax.optimization_barrier((made[a], last))
             last = keep[key] = over_ctx(value, a * rest)
+            if keep is blocks:
+                last = (last, ahead_1)
     bit = rest // 2
     while bit > 1:
         for i in list(blocks):
-            blocks[i ^ bit] = over_ctx(blocks[i], bit)
+            if i ^ bit not in blocks:
+                blocks[i ^ bit] = over_ctx(blocks[i], bit)
         bit //= 2
+    table = []
+    for i in range(0, ctx_size, 2):
+        table += [blocks[i][rows, :1], blocks[i][rows + EXTRA // 2, :1]]
+    table = jnp.concatenate(table).astype(jnp.int32)
     pieces = [[None] * 2 for _ in range(ways)]
     for b in range(2):
-        outs = attend(b, [queries[b][a] for a in range(ways)], blocks, table, place)
+        outs = attend(b, [queries[b][a] for a in range(ways)], blocks, table)
         for a in away:
             pieces[a][b] = over_ctx(outs[a], a * rest + b)
     return assemble(pieces, place)

time: 196 us -> 181 us (0.923)
  waiting for transfers between devices: 59.6 us -> 27.4 us
  local copies, waits for them, and re-layouts: 9.54 us -> 25.1 us
  Pallas kernels: 82.5 us -> 85.7 us
    ppermute x30 -> x31, waiting for transfers between devices: 53.9 us -> 27.4 us  [exchange(): return lax.ppermute(value, axis, [(i, i ^ bit) for i in range(size)])]
    concatenate x1 -> x2, local copies, waits for them, and re-layouts: 0.67 us -> 12.1 us  [the longest x1 10.2 us: on_device(): table = jnp.concatenate(table).astype(jnp.int32)]
    all_to_all x1 -> x0, starting transfers between devices: 5.94 us -> none  [on_device(): table = lax.all_to_all(firsts, 'ctx', 0, 0, tiled=True)]
    all_to_all x1 -> x0, waiting for transfers between devices: 5.73 us -> none  [on_device(): table = lax.all_to_all(firsts, 'ctx', 0, 0, tiled=True)]
    slice x0 -> x8, local copies, waits for them, and re-layouts: none -> 5.33 us  [on_device(): table += [blocks[i][rows, :1], blocks[i][rows + EXTRA // 2, :1]]]
    ppermute x30 -> x31, starting transfers between devices: 34.4 us -> 39.2 us  [exchange(): return lax.ppermute(value, axis, [(i, i ^ bit) for i in range(size)])]
    pallas_call x3 -> x4, Pallas kernels: 32.3 us -> 35.5 us  [rest_products(): pl.pallas_call(functools.partial(rest_body, shares, len(weights), chunks,...]
    unnamed x74 -> x58, local copies, waits for them, and re-layouts: 5 us -> 4.41 us
  transfers between devices with their start and end apart: 31 -> 31, of which waited for: 12 -> 5; matrix products, arithmetic and copies ran while one was open for 2% -> 11% of each run, Pallas kernels for 41% -> 46%
where the time goes in v6:
time: 181 us; the launch traced here: 179 us
  Pallas kernels  85.7 us (47%)
  starting transfers between devices  39.2 us (22%)
  waiting for transfers between devices  27.4 us (15%)
  local copies, waits for them, and re-layouts  25.1 us (14%)
    ppermute x31, starting transfers between devices, exchange(): return lax.ppermute(value, axis, [(i, i ^ bit) for i in range(size)])  39.2 us
    pallas_call x4, Pallas kernels, rest_products(): pl.pallas_call(functools.partial(rest_body, shares, len(weights), chunks,...  35.5 us
    pallas_call x2, Pallas kernels, attend(): pl.pallas_call(functools.partial(attend_body, block, ways, offsets, spans...  28 us
    ppermute x31, waiting for transfers between devices, exchange(): return lax.ppermute(value, axis, [(i, i ^ bit) for i in range(size)])  27.4 us
    pallas_call x1, Pallas kernels, own_products(): pl.pallas_call(functools.partial(own_body, len(weights)), out_shape=[jax....  18.5 us
    concatenate x1, local copies, waits for them, and re-layouts, on_device(): table = jnp.concatenate(table).astype(jnp.int32)  10.2 us
    slice x8, local copies, waits for them, and re-layouts, on_device(): table += [blocks[i][rows, :1], blocks[i][rows + EXTRA // 2, :1]]  5.33 us
    unnamed x58, local copies, waits for them, and re-layouts  4.41 us
  transfers between devices with their start and end apart: 31, of which 5 were waited for; matrix products, arithmetic and copies ran while one was open for 11% of the time, Pallas kernels for 46%

profile of v6, /device:TPU:0, one launch (start us, length us, event | category | flops | bytes accessed | tf_op | source)
XLA Modules:
  0.0 179.1 jit_solution(4172332523396801547)
XLA Ops:
  0.0 2.6 %dynamic-slice_bitcast_fusion = (bf16[192,2560]{1,0:T(8,128)(2,1)}, bf16[192,2560]{1,0:T(8,128)(2,1)S(1)}) fusion(bf16[2,192,2560]{2,1,0:T(8,128)(2,1)} %mine_ref.1, s32[]{:T(128)S(6)} %select_n.30, s32[]{:T(128)S(6)} %select_n.29), kind=kLoop, calls=%fused_computation | loop fusion | bytes 3932168 | tf_op jit(solution)/shard_map/jit(dynamic_index_in_dim)/squeeze | solution.py:332
  3.0 2.5 %collective-permute-start.1 = (bf16[192,2560]{1,0:T(8,128)(2,1)S(1)}, bf16[192,2560]{1,0:T(8,128)(2,1)S(1)}, u32[]{:S(2)}, u32[]{:S(2)}) collective-permute-start(bf16[192,2560]{1,0:T(8,128)(2,1)S(1)} %get-tuple-element.112), channel_id=1, source_target_pairs={{0,1},{1,0},{2,3},{3,2},{4,5},{5,4},{6,7},{7,6},{8,9},{9,8},{10,11... | collective-permute-start | bytes 2949128 | tf_op jit(solution)/shard_map/ppermute | solution.py:18
  5.8 0.6 fusion.8
  6.7 0.7 pad_add_fusion.place
  7.6 1.9 %concatenate.7.place = s32[6]{0:T(128)} concatenate(s32[1]{0:T(128)} %bitcast, s32[1]{0:T(128)} %bitcast.1, s32[1]{0:T(128)} %bitcast.2, s32[1]{0:T(128)} %bitcast.3, s32[1]{0:T(128)} %get-tuple-element.130, s32[1]{0:T(128)} %collective-permute-done), dimensions={0} | concatenate | bytes 48 | tf_op jit(solution)/shard_map/concatenate | solution.py:339
  10.4 18.5 %shard_map.55 = (f32[2,192,1536]{2,1,0:T(8,128)}, f32[2,192,1536]{2,1,0:T(8,128)}, f32[2,192,1536]{2,1,0:T(8,128)}) custom-call(s32[4]{0:T(128)} %pad_add_fusion.place, bf16[2,192,2560]{2,1,0:T(8,128)(2,1)} %mine_ref.1, bf16[192,2560]{1,0:T(8,128)(2,1)} %copy-done.2, bf16[5120,1536]{1,0:T(8,128)(2,1)} %refs_1_.7, bf16[5120,1536]{1,0:T(8,128)(2,1)} %refs_2_.9, ...), custom_call_target="tpu_custom_call" | custom-call | flops 9059696640 | bytes 23592960 | tf_op jit(solution)/shard_map/pallas_call | solution.py:42
  29.0 0.9 copy-done
  29.9 7.2 %shard_map.59 = (bf16[208,768]{1,0:T(8,128)(2,1)}, bf16[208,768]{1,0:T(8,128)(2,1)}) custom-call(s32[6]{0:T(128)} %concatenate.7.place, bf16[192,2560]{1,0:T(8,128)(2,1)} %copy-done, bf16[5120,1536]{1,0:T(8,128)(2,1)} %refs_1_.7, bf16[5120,1536]{1,0:T(8,128)(2,1)} %refs_2_.9, f32[2,192,1536]{2,1,0:T(8,128)} %get-tuple-element.58.refs_3_, ...), custom_call_target="tpu_custom_call" | custom-call | flops 1509949440 | bytes 7864320 | tf_op jit(solution)/shard_map/pallas_call | solution.py:127
  37.1 2.7 %collective-permute-start.7 = (bf16[208,768]{1,0:T(8,128)(2,1)}, bf16[208,768]{1,0:T(8,128)(2,1)S(1)}, u32[]{:S(2)}, u32[]{:S(2)}) collective-permute-start(bf16[208,768]{1,0:T(8,128)(2,1)} %get-tuple-element.73), channel_id=1, source_target_pairs={{0,16},{2,18},{4,20},{6,22},{8,24},{10,26},{12,28},{14,30},{16,0},... | collective-permute-start | bytes 958472 | tf_op jit(solution)/shard_map/ppermute | solution.py:18
  39.8 1.3 collective-permute-start.9
  41.0 7.3 %shard_map.56 = (bf16[208,768]{1,0:T(8,128)(2,1)}, bf16[208,768]{1,0:T(8,128)(2,1)}) custom-call(s32[6]{0:T(128)} %concatenate.7.place, bf16[192,2560]{1,0:T(8,128)(2,1)} %copy-done, bf16[5120,1536]{1,0:T(8,128)(2,1)} %refs_1_.7, bf16[5120,1536]{1,0:T(8,128)(2,1)} %refs_2_.9, f32[2,192,1536]{2,1,0:T(8,128)} %get-tuple-element.58.refs_3_, ...), custom_call_target="tpu_custom_call" | custom-call | flops 1509949440 | bytes 7864320 | tf_op jit(solution)/shard_map/pallas_call | solution.py:127
  48.7 1.5 collective-permute-start.4
  50.2 1.0 copy-done.1
  51.2 11.2 %shard_map.57 = (bf16[192,768]{1,0:T(8,128)(2,1)}, bf16[192,768]{1,0:T(8,128)(2,1)}, bf16[192,768]{1,0:T(8,128)(2,1)}, bf16[192,768]{1,0:T(8,128)(2,1)}) custom-call(s32[4]{0:T(128)} %pad_add_fusion.place, bf16[192,2560]{1,0:T(8,128)(2,1)} %copy-done.1, bf16[5120,1536]{1,0:T(8,128)(2,1)} %refs_1_.7, bf16[5120,1536]{1,0:T(8,128)(2,1)} %refs_2_.9, ...), custom_call_target="tpu_custom_call" | custom-call | flops 3019898880 | bytes 15728640 | tf_op jit(solution)/shard_map/pallas_call | solution.py:127
  62.4 0.6 collective-permute-start.11
  63.0 9.8 %shard_map.58 = (bf16[192,384]{1,0:T(8,128)(2,1)}, bf16[192,384]{1,0:T(8,128)(2,1)}, bf16[192,384]{1,0:T(8,128)(2,1)}, bf16[192,384]{1,0:T(8,128)(2,1)}, bf16[19...) custom-call(s32[4]{0:T(128)} %pad_add_fusion.place, ...), custom_call_target="tpu_custom_call" | custom-call | flops 3019898880 | bytes 7864320 | tf_op jit(solution)/shard_map/pallas_call | solution.py:127
  72.9 1.7 collective-permute-start.12
  74.6 0.6 fusion.6
  75.2 1.6 collective-permute-start.10
  77.3 2.6 %collective-permute-start.14 = (bf16[192,768]{1,0:T(8,128)(2,1)S(1)}, bf16[192,768]{1,0:T(8,128)(2,1)S(1)}, u32[]{:S(2)}, u32[]{:S(2)}) collective-permute-start(bf16[192,768]{1,0:T(8,128)(2,1)S(1)} %copy-done.22), channel_id=1, source_target_pairs={{0,16},{2,18},{4,20},{6,22},{8,24},{10,26},{12,28},{14,30},{16,0},... | collective-permute-start | bytes 884744 | tf_op jit(solution)/shard_map/ppermute | solution.py:18
  81.3 4.0 %collective-permute-done.12.refs_9_ = bf16[192,768]{1,0:T(8,128)(2,1)S(1)} collective-permute-done((bf16[192,768]{1,0:T(8,128)(2,1)S(1)}, bf16[192,768]{1,0:T(8,128)(2,1)S(1)}, u32[]{:S(2)}, u32[]{:S(2)}) %collective-permute-start.12) | collective-permute-done | bytes 294944 | tf_op jit(solution)/shard_map/ppermute | solution.py:18
  85.3 0.9 collective-permute-start.6
  86.2 0.6 fusion.5
  86.7 14.0 %collective-permute-done.14.refs_13_ = bf16[192,768]{1,0:T(8,128)(2,1)S(1)} collective-permute-done((bf16[192,768]{1,0:T(8,128)(2,1)S(1)}, bf16[192,768]{1,0:T(8,128)(2,1)S(1)}, u32[]{:S(2)}, u32[]{:S(2)}) %collective-permute-start.14) | collective-permute-done | bytes 294944 | tf_op jit(solution)/shard_map/ppermute | solution.py:18
  100.7 1.3 fusion.7
  102.0 1.0 collective-permute-start.18
  103.0 1.1 collective-permute-start.19
  104.1 1.0 collective-permute-start.20
  105.0 0.6 fusion
  105.6 4.2 %collective-permute-start.15 = (bf16[192,384]{1,0:T(8,128)(2,1)}, bf16[192,384]{1,0:T(8,128)(2,1)}, u32[]{:S(2)}, u32[]{:S(2)}) collective-permute-start(bf16[192,384]{1,0:T(8,128)(2,1)} %get-tuple-element.90), channel_id=1, source_target_pairs={{0,16},{2,18},{4,20},{6,22},{8,24},{10,26},{12,28},{14,30},{16,0},... | collective-permute-start | bytes 442376 | tf_op jit(solution)/shard_map/ppermute | solution.py:18
  109.8 1.4 collective-permute-start.17
  111.2 0.6 fusion.2
  112.4 10.2 %concatenate.8 = bf16[16]{0:T(256)(128)(2,1)S(1)} concatenate(bf16[1]{0:T(256)(128)(2,1)} %bitcast.6, bf16[1]{0:T(256)(128)(2,1)} %bitcast.7, bf16[1]{0:T(256)(128)(2,1)} %bitcast.8, bf16[1]{0:T(256)(128)(2,1)} %bitcast.9, bf16[1]{0:T(256)(128)(2,1)} %bitcast.10, bf16[1]{0:T(256)(128)(2,1)} %bitcast.11, bf16[1]{0:T(256)(128)(2,1)} %bitcast.12, bf16[1]{0:T(256)(128)(2,1)} %bitcast.13, ...), dimensions={0} | concatenate | bytes 64 | tf_op jit(solution)/shard_map/concatenate | solution.py:374
  122.6 0.6 convert_element_type.3.table
  123.2 3.0 %collective-permute-start.22 = (bf16[192,384]{1,0:T(8,128)(2,1)}, bf16[192,384]{1,0:T(8,128)(2,1)S(1)}, u32[]{:S(2)}, u32[]{:S(2)}) collective-permute-start(bf16[192,384]{1,0:T(8,128)(2,1)} %get-tuple-element.101), channel_id=1, source_target_pairs={{0,16},{2,18},{4,20},{6,22},{8,24},{10,26},{12,28},{14,30},{16,0},... | collective-permute-start | bytes 442376 | tf_op jit(solution)/shard_map/ppermute | solution.py:18
  126.2 1.4 collective-permute-start.23
  127.7 13.9 %shard_map.60 = (bf16[192,384]{1,0:T(8,128)(2,1)}, bf16[192,384]{1,0:T(8,128)(2,1)}, bf16[192,384]{1,0:T(8,128)(2,1)}, bf16[192,384]{1,0:T(8,128)(2,1)}) custom-call(s32[16]{0:T(128)} %convert_element_type.3.table, bf16[192,384]{1,0:T(8,128)(2,1)} %get-tuple-element.82.refs_0_, bf16[192,384]{1,0:T(8,128)(2,1)} %copy-done.24, ...), custom_call_target="tpu_custom_call" | custom-call | flops 2717908992 | bytes 5898240 | tf_op jit(solution)/shard_map/pallas_call | solution.py:256
  141.7 3.0 %collective-permute-start.27 = (bf16[192,384]{1,0:T(8,128)(2,1)}, bf16[192,384]{1,0:T(8,128)(2,1)S(1)}, u32[]{:S(2)}, u32[]{:S(2)}) collective-permute-start(bf16[192,384]{1,0:T(8,128)(2,1)} %get-tuple-element.107), channel_id=1, source_target_pairs={{0,16},{2,18},{4,20},{6,22},{8,24},{10,26},{12,28},{14,30},{16,0},... | collective-permute-start | bytes 442376 | tf_op jit(solution)/shard_map/ppermute | solution.py:18
  144.6 1.4 collective-permute-start.29
  146.1 0.7 copy-done.26
  146.7 0.7 copy-done.27
  147.4 14.1 %shard_map.61 = (bf16[192,384]{1,0:T(8,128)(2,1)}, bf16[192,384]{1,0:T(8,128)(2,1)}, bf16[192,384]{1,0:T(8,128)(2,1)}, bf16[192,384]{1,0:T(8,128)(2,1)}) custom-call(s32[16]{0:T(128)} %convert_element_type.3.table, bf16[192,384]{1,0:T(8,128)(2,1)} %get-tuple-element.97.refs_0_, bf16[192,384]{1,0:T(8,128)(2,1)} %copy-done.25, bf16[192,384]{1,0:T(8,128)(2,1)} %copy-done.26, ...), custom_call_target="tpu_custom_call" | custom-call | flops 2717908992 | bytes 5898240 | tf_op jit(solution)/shard_map/pallas_call | solution.py:256
  161.7 2.7 %collective-permute-start.28 = (bf16[192,384]{1,0:T(8,128)(2,1)}, bf16[192,384]{1,0:T(8,128)(2,1)S(1)}, u32[]{:S(2)}, u32[]{:S(2)}) collective-permute-start(bf16[192,384]{1,0:T(8,128)(2,1)} %get-tuple-element.108), channel_id=1, source_target_pairs={{0,18},{2,16},{4,22},{6,20},{8,26},{10,24},{12,30},{14,28},{16,2},... | collective-permute-start | bytes 442376 | tf_op jit(solution)/shard_map/ppermute | solution.py:18
  164.3 1.5 collective-permute-start.30
  165.8 4.4 %collective-permute-done.26.refs_3_ = bf16[192,384]{1,0:T(8,128)(2,1)S(1)} collective-permute-done((bf16[192,384]{1,0:T(8,128)(2,1)}, bf16[192,384]{1,0:T(8,128)(2,1)S(1)}, u32[]{:S(2)}, u32[]{:S(2)}) %collective-permute-start.26) | collective-permute-done | bytes 147488 | tf_op jit(solution)/shard_map/ppermute | solution.py:18
  170.2 4.7 %collective-permute-done.30.refs_7_ = bf16[192,384]{1,0:T(8,128)(2,1)S(1)} collective-permute-done((bf16[192,384]{1,0:T(8,128)(2,1)}, bf16[192,384]{1,0:T(8,128)(2,1)S(1)}, u32[]{:S(2)}, u32[]{:S(2)}) %collective-permute-start.30) | collective-permute-done | bytes 147488 | tf_op jit(solution)/shard_map/ppermute | solution.py:18
  174.9 0.6 copy-done.9
  175.5 3.6 %shard_map.62 = bf16[2,192,1536]{2,1,0:T(8,128)(2,1)} custom-call(s32[4]{0:T(128)} %pad_add_fusion.place, bf16[192,384]{1,0:T(8,128)(2,1)} %get-tuple-element.95.refs_0_, bf16[192,384]{1,0:T(8,128)(2,1)} %copy-done.6, bf16[192,384]{1,0:T(8,128)(2,1)} %copy-done.3, bf16[192,384]{1,0:T(8,128)(2,1)} %copy-done.7, bf16[192,384]{1,0:T(8,128)(2,1)} %copy-done.4, ...), custom_call_target="tpu_custom_call" | custom-call | tf_op jit(solution)/shard_map/pallas_call | solution.py:296
  (97 shorter events, 5.3 us)
Async XLA Ops:
  2.6 6.9 %collective-permute-start.2 = (bf16[192,2560]{1,0:T(8,128)(2,1)}, bf16[192,2560]{1,0:T(8,128)(2,1)S(1)}, u32[]{:S(2)}, u32[]{:S(2)}) collective-permute-start(bf16[192,2560]{1,0:T(8,128)(2,1)} %get-tuple-element.111), channel_id=1, source_target_pairs={{0,2},{2,0},{4,6},{6,4},{8,10},{10,8},{12,14},{14,12},{16,18},{18,... | collective-permute-start | bytes 2949128 | tf_op jit(solution)/shard_map/ppermute | solution.py:18
  3.0 25.9 %collective-permute-start.1 = (bf16[192,2560]{1,0:T(8,128)(2,1)S(1)}, bf16[192,2560]{1,0:T(8,128)(2,1)S(1)}, u32[]{:S(2)}, u32[]{:S(2)}) collective-permute-start(bf16[192,2560]{1,0:T(8,128)(2,1)S(1)} %get-tuple-element.112), channel_id=1, source_target_pairs={{0,1},{1,0},{2,3},{3,2},{4,5},{5,4},{6,7},{7,6},{8,9},{9,8},{10,11... | collective-permute-start | bytes 2949128 | tf_op jit(solution)/shard_map/ppermute | solution.py:18
  6.4 1.2 collective-permute-start
  9.5 40.7 %collective-permute-start.3 = (bf16[192,2560]{1,0:T(8,128)(2,1)S(1)}, bf16[192,2560]{1,0:T(8,128)(2,1)S(1)}, u32[]{:S(2)}, u32[]{:S(2)}) collective-permute-start(bf16[192,2560]{1,0:T(8,128)(2,1)S(1)} %collective-permute-done.2.other_ref), channel_id=1, source_target_pairs={{0,1},{1,0},{2,3},{3,2},{4,5},{5,4},{6,7},{7,6},{8,9},{9,8},{10,11... | collective-permute-start | bytes 2949128 | tf_op jit(solution)/shard_map/ppermute | solution.py:18
  37.1 38.0 %collective-permute-start.7 = (bf16[208,768]{1,0:T(8,128)(2,1)}, bf16[208,768]{1,0:T(8,128)(2,1)S(1)}, u32[]{:S(2)}, u32[]{:S(2)}) collective-permute-start(bf16[208,768]{1,0:T(8,128)(2,1)} %get-tuple-element.73), channel_id=1, source_target_pairs={{0,16},{2,18},{4,20},{6,22},{8,24},{10,26},{12,28},{14,30},{16,0},... | collective-permute-start | bytes 958472 | tf_op jit(solution)/shard_map/ppermute | solution.py:18
  39.8 35.4 %collective-permute-start.9 = (bf16[208,768]{1,0:T(8,128)(2,1)}, bf16[208,768]{1,0:T(8,128)(2,1)S(1)}, u32[]{:S(2)}, u32[]{:S(2)}) collective-permute-start(bf16[208,768]{1,0:T(8,128)(2,1)} %get-tuple-element.76), channel_id=1, source_target_pairs={{0,24},{2,26},{4,28},{6,30},{8,16},{10,18},{12,20},{14,22},{16,8},... | collective-permute-start | bytes 958472 | tf_op jit(solution)/shard_map/ppermute | solution.py:18
  48.4 24.5 %collective-permute-start.5 = (bf16[208,768]{1,0:T(8,128)(2,1)}, bf16[208,768]{1,0:T(8,128)(2,1)S(1)}, u32[]{:S(2)}, u32[]{:S(2)}) collective-permute-start(bf16[208,768]{1,0:T(8,128)(2,1)} %get-tuple-element.70), channel_id=1, source_target_pairs={{0,8},{2,10},{4,12},{6,14},{8,0},{10,2},{12,4},{14,6},{16,24},{18,... | collective-permute-start | bytes 958472 | tf_op jit(solution)/shard_map/ppermute | solution.py:18
  48.7 24.2 %collective-permute-start.4 = (bf16[208,768]{1,0:T(8,128)(2,1)}, bf16[208,768]{1,0:T(8,128)(2,1)S(1)}, u32[]{:S(2)}, u32[]{:S(2)}) collective-permute-start(bf16[208,768]{1,0:T(8,128)(2,1)} %get-tuple-element.69.refs_4_), channel_id=1, source_target_pairs={{0,4},{2,6},{4,0},{6,2},{8,12},{10,14},{12,8},{14,10},{16,20},{18,... | collective-permute-start | bytes 958472 | tf_op jit(solution)/shard_map/ppermute | solution.py:18
  62.4 18.0 %collective-permute-start.11 = (bf16[192,768]{1,0:T(8,128)(2,1)}, bf16[192,768]{1,0:T(8,128)(2,1)S(1)}, u32[]{:S(2)}, u32[]{:S(2)}) collective-permute-start(bf16[192,768]{1,0:T(8,128)(2,1)} %get-tuple-element.81.refs_5_), channel_id=1, source_target_pairs={{0,4},{2,6},{4,0},{6,2},{8,12},{10,14},{12,8},{14,10},{16,20},{18,... | collective-permute-start | bytes 884744 | tf_op jit(solution)/shard_map/ppermute | solution.py:18
  63.0 9.9 %copy-start.23 = (bf16[192,768]{1,0:T(8,128)(2,1)S(1)}, bf16[192,768]{1,0:T(8,128)(2,1)}, u32[]{:S(2)}) copy-start(bf16[192,768]{1,0:T(8,128)(2,1)} %get-tuple-element.85) | copy-start | bytes 884740
  63.0 14.3 %copy-start.22 = (bf16[192,768]{1,0:T(8,128)(2,1)S(1)}, bf16[192,768]{1,0:T(8,128)(2,1)}, u32[]{:S(2)}) copy-start(bf16[192,768]{1,0:T(8,128)(2,1)} %get-tuple-element.89) | copy-start | bytes 884740
  63.0 17.4 %copy-start.21 = (bf16[192,768]{1,0:T(8,128)(2,1)S(1)}, bf16[192,768]{1,0:T(8,128)(2,1)}, u32[]{:S(2)}) copy-start(bf16[192,768]{1,0:T(8,128)(2,1)} %get-tuple-element.93) | copy-start | bytes 884740
  72.8 54.7 %copy-start.12 = (bf16[208,768]{1,0:T(8,128)(2,1)}, bf16[208,768]{1,0:T(8,128)(2,1)S(1)}, u32[]{:S(2)}) copy-start(bf16[208,768]{1,0:T(8,128)(2,1)S(1)} %collective-permute-done.5.refs_8_) | copy-start | bytes 958468
  72.9 54.7 %copy-start.13 = (bf16[208,768]{1,0:T(8,128)(2,1)}, bf16[208,768]{1,0:T(8,128)(2,1)S(1)}, u32[]{:S(2)}) copy-start(bf16[208,768]{1,0:T(8,128)(2,1)S(1)} %collective-permute-done.4.refs_6_) | copy-start | bytes 958468
  72.9 12.4 %collective-permute-start.12 = (bf16[192,768]{1,0:T(8,128)(2,1)S(1)}, bf16[192,768]{1,0:T(8,128)(2,1)S(1)}, u32[]{:S(2)}, u32[]{:S(2)}) collective-permute-start(bf16[192,768]{1,0:T(8,128)(2,1)S(1)} %copy-done.23), channel_id=1, source_target_pairs={{0,8},{2,10},{4,12},{6,14},{8,0},{10,2},{12,4},{14,6},{16,24},{18,... | collective-permute-start | bytes 884744 | tf_op jit(solution)/shard_map/ppermute | solution.py:18
  75.1 52.4 %copy-start.10 = (bf16[208,768]{1,0:T(8,128)(2,1)}, bf16[208,768]{1,0:T(8,128)(2,1)S(1)}, u32[]{:S(2)}) copy-start(bf16[208,768]{1,0:T(8,128)(2,1)S(1)} %collective-permute-done.7.refs_12_) | copy-start | bytes 958468
  75.2 52.4 %copy-start.11 = (bf16[208,768]{1,0:T(8,128)(2,1)}, bf16[208,768]{1,0:T(8,128)(2,1)S(1)}, u32[]{:S(2)}) copy-start(bf16[208,768]{1,0:T(8,128)(2,1)S(1)} %collective-permute-done.9.refs_16_) | copy-start | bytes 958468
  75.2 27.8 %collective-permute-start.10 = (bf16[208,768]{1,0:T(8,128)(2,1)S(1)}, bf16[208,768]{1,0:T(8,128)(2,1)S(1)}, u32[]{:S(2)}, u32[]{:S(2)}) collective-permute-start(bf16[208,768]{1,0:T(8,128)(2,1)S(1)} %collective-permute-done.9.refs_16_), channel_id=1, source_target_pairs={{0,4},{2,6},{4,0},{6,2},{8,12},{10,14},{12,8},{14,10},{16,20},{18,... | collective-permute-start | bytes 958472 | tf_op jit(solution)/shard_map/ppermute | solution.py:18
  76.8 27.3 %collective-permute-start.8 = (bf16[208,768]{1,0:T(8,128)(2,1)S(1)}, bf16[208,768]{1,0:T(8,128)(2,1)S(1)}, u32[]{:S(2)}, u32[]{:S(2)}) collective-permute-start(bf16[208,768]{1,0:T(8,128)(2,1)S(1)} %collective-permute-done.7.refs_12_), channel_id=1, source_target_pairs={{0,4},{2,6},{4,0},{6,2},{8,12},{10,14},{12,8},{14,10},{16,20},{18,... | collective-permute-start | bytes 958472 | tf_op jit(solution)/shard_map/ppermute | solution.py:18
  77.3 23.5 %collective-permute-start.14 = (bf16[192,768]{1,0:T(8,128)(2,1)S(1)}, bf16[192,768]{1,0:T(8,128)(2,1)S(1)}, u32[]{:S(2)}, u32[]{:S(2)}) collective-permute-start(bf16[192,768]{1,0:T(8,128)(2,1)S(1)} %copy-done.22), channel_id=1, source_target_pairs={{0,16},{2,18},{4,20},{6,22},{8,24},{10,26},{12,28},{14,30},{16,0},... | collective-permute-start | bytes 884744 | tf_op jit(solution)/shard_map/ppermute | solution.py:18
  80.4 47.2 %copy-start.17 = (bf16[192,768]{1,0:T(8,128)(2,1)}, bf16[192,768]{1,0:T(8,128)(2,1)S(1)}, u32[]{:S(2)}) copy-start(bf16[192,768]{1,0:T(8,128)(2,1)S(1)} %collective-permute-done.11.refs_7_) | copy-start | bytes 884740
  80.4 21.6 %collective-permute-start.16 = (bf16[192,768]{1,0:T(8,128)(2,1)S(1)}, bf16[192,768]{1,0:T(8,128)(2,1)S(1)}, u32[]{:S(2)}, u32[]{:S(2)}) collective-permute-start(bf16[192,768]{1,0:T(8,128)(2,1)S(1)} %copy-done.21), channel_id=1, source_target_pairs={{0,24},{2,26},{4,28},{6,30},{8,16},{10,18},{12,20},{14,22},{16,8},... | collective-permute-start | bytes 884744 | tf_op jit(solution)/shard_map/ppermute | solution.py:18
  85.3 42.3 %copy-start.18 = (bf16[192,768]{1,0:T(8,128)(2,1)}, bf16[192,768]{1,0:T(8,128)(2,1)S(1)}, u32[]{:S(2)}) copy-start(bf16[192,768]{1,0:T(8,128)(2,1)S(1)} %collective-permute-done.12.refs_9_) | copy-start | bytes 884740
  85.3 20.3 %collective-permute-start.6 = (bf16[208,768]{1,0:T(8,128)(2,1)S(1)}, bf16[208,768]{1,0:T(8,128)(2,1)S(1)}, u32[]{:S(2)}, u32[]{:S(2)}) collective-permute-start(bf16[208,768]{1,0:T(8,128)(2,1)S(1)} %collective-permute-done.5.refs_8_), channel_id=1, source_target_pairs={{0,4},{2,6},{4,0},{6,2},{8,12},{10,14},{12,8},{14,10},{16,20},{18,... | collective-permute-start | bytes 958472 | tf_op jit(solution)/shard_map/ppermute | solution.py:18
  100.7 26.9 %copy-start.19 = (bf16[192,768]{1,0:T(8,128)(2,1)}, bf16[192,768]{1,0:T(8,128)(2,1)S(1)}, u32[]{:S(2)}) copy-start(bf16[192,768]{1,0:T(8,128)(2,1)S(1)} %collective-permute-done.14.refs_13_) | copy-start | bytes 884740
  100.7 9.1 %collective-permute-start.13 = (bf16[192,384]{1,0:T(8,128)(2,1)}, bf16[192,384]{1,0:T(8,128)(2,1)S(1)}, u32[]{:S(2)}, u32[]{:S(2)}) collective-permute-start(bf16[192,384]{1,0:T(8,128)(2,1)} %get-tuple-element.86), channel_id=1, source_target_pairs={{0,8},{2,10},{4,12},{6,14},{8,0},{10,2},{12,4},{14,6},{16,24},{18,... | collective-permute-start | bytes 442376 | tf_op jit(solution)/shard_map/ppermute | solution.py:18
  102.0 25.6 %copy-start.20 = (bf16[192,768]{1,0:T(8,128)(2,1)}, bf16[192,768]{1,0:T(8,128)(2,1)S(1)}, u32[]{:S(2)}) copy-start(bf16[192,768]{1,0:T(8,128)(2,1)S(1)} %collective-permute-done.16.refs_17_) | copy-start | bytes 884740
  102.0 24.2 %collective-permute-start.18 = (bf16[192,768]{1,0:T(8,128)(2,1)S(1)}, bf16[192,768]{1,0:T(8,128)(2,1)}, u32[]{:S(2)}, u32[]{:S(2)}) collective-permute-start(bf16[192,768]{1,0:T(8,128)(2,1)S(1)} %collective-permute-done.12.refs_9_), channel_id=1, source_target_pairs={{0,4},{2,6},{4,0},{6,2},{8,12},{10,14},{12,8},{14,10},{16,20},{18,... | collective-permute-start | bytes 884744 | tf_op jit(solution)/shard_map/ppermute | solution.py:18
  103.0 24.6 %copy-start.14 = (bf16[208,768]{1,0:T(8,128)(2,1)}, bf16[208,768]{1,0:T(8,128)(2,1)S(1)}, u32[]{:S(2)}) copy-start(bf16[208,768]{1,0:T(8,128)(2,1)S(1)} %collective-permute-done.10.refs_18_) | copy-start | bytes 958468
  103.0 24.6 %collective-permute-start.19 = (bf16[192,768]{1,0:T(8,128)(2,1)S(1)}, bf16[192,768]{1,0:T(8,128)(2,1)}, u32[]{:S(2)}, u32[]{:S(2)}) collective-permute-start(bf16[192,768]{1,0:T(8,128)(2,1)S(1)} %collective-permute-done.14.refs_13_), channel_id=1, source_target_pairs={{0,4},{2,6},{4,0},{6,2},{8,12},{10,14},{12,8},{14,10},{16,20},{18,... | collective-permute-start | bytes 884744 | tf_op jit(solution)/shard_map/ppermute | solution.py:18
  104.1 23.6 %copy-start.15 = (bf16[208,768]{1,0:T(8,128)(2,1)}, bf16[208,768]{1,0:T(8,128)(2,1)S(1)}, u32[]{:S(2)}) copy-start(bf16[208,768]{1,0:T(8,128)(2,1)S(1)} %collective-permute-done.8.refs_14_) | copy-start | bytes 958468
  104.1 23.5 %collective-permute-start.20 = (bf16[192,768]{1,0:T(8,128)(2,1)S(1)}, bf16[192,768]{1,0:T(8,128)(2,1)}, u32[]{:S(2)}, u32[]{:S(2)}) collective-permute-start(bf16[192,768]{1,0:T(8,128)(2,1)S(1)} %collective-permute-done.16.refs_17_), channel_id=1, source_target_pairs={{0,4},{2,6},{4,0},{6,2},{8,12},{10,14},{12,8},{14,10},{16,20},{18,... | collective-permute-start | bytes 884744 | tf_op jit(solution)/shard_map/ppermute | solution.py:18
  105.6 22.0 %copy-start.16 = (bf16[208,768]{1,0:T(8,128)(2,1)}, bf16[208,768]{1,0:T(8,128)(2,1)S(1)}, u32[]{:S(2)}) copy-start(bf16[208,768]{1,0:T(8,128)(2,1)S(1)} %collective-permute-done.6.refs_10_) | copy-start | bytes 958468
  105.6 17.5 %collective-permute-start.15 = (bf16[192,384]{1,0:T(8,128)(2,1)}, bf16[192,384]{1,0:T(8,128)(2,1)}, u32[]{:S(2)}, u32[]{:S(2)}) collective-permute-start(bf16[192,384]{1,0:T(8,128)(2,1)} %get-tuple-element.90), channel_id=1, source_target_pairs={{0,16},{2,18},{4,20},{6,22},{8,24},{10,26},{12,28},{14,30},{16,0},... | collective-permute-start | bytes 442376 | tf_op jit(solution)/shard_map/ppermute | solution.py:18
  109.8 13.4 %collective-permute-start.17 = (bf16[192,384]{1,0:T(8,128)(2,1)}, bf16[192,384]{1,0:T(8,128)(2,1)}, u32[]{:S(2)}, u32[]{:S(2)}) collective-permute-start(bf16[192,384]{1,0:T(8,128)(2,1)} %get-tuple-element.94), channel_id=1, source_target_pairs={{0,24},{2,26},{4,28},{6,30},{8,16},{10,18},{12,20},{14,22},{16,8},... | collective-permute-start | bytes 442376 | tf_op jit(solution)/shard_map/ppermute | solution.py:18
  123.2 21.5 %collective-permute-start.21 = (bf16[192,384]{1,0:T(8,128)(2,1)}, bf16[192,384]{1,0:T(8,128)(2,1)S(1)}, u32[]{:S(2)}, u32[]{:S(2)}) collective-permute-start(bf16[192,384]{1,0:T(8,128)(2,1)} %get-tuple-element.99), channel_id=1, source_target_pairs={{0,8},{2,10},{4,12},{6,14},{8,0},{10,2},{12,4},{14,6},{16,24},{18,... | collective-permute-start | bytes 442376 | tf_op jit(solution)/shard_map/ppermute | solution.py:18
  123.2 22.9 %collective-permute-start.22 = (bf16[192,384]{1,0:T(8,128)(2,1)}, bf16[192,384]{1,0:T(8,128)(2,1)S(1)}, u32[]{:S(2)}, u32[]{:S(2)}) collective-permute-start(bf16[192,384]{1,0:T(8,128)(2,1)} %get-tuple-element.101), channel_id=1, source_target_pairs={{0,16},{2,18},{4,20},{6,22},{8,24},{10,26},{12,28},{14,30},{16,0},... | collective-permute-start | bytes 442376 | tf_op jit(solution)/shard_map/ppermute | solution.py:18
  126.2 19.9 %collective-permute-start.23 = (bf16[192,384]{1,0:T(8,128)(2,1)}, bf16[192,384]{1,0:T(8,128)(2,1)S(1)}, u32[]{:S(2)}, u32[]{:S(2)}) collective-permute-start(bf16[192,384]{1,0:T(8,128)(2,1)} %get-tuple-element.103), channel_id=1, source_target_pairs={{0,24},{2,26},{4,28},{6,30},{8,16},{10,18},{12,20},{14,22},{16,8},... | collective-permute-start | bytes 442376 | tf_op jit(solution)/shard_map/ppermute | solution.py:18
  141.6 20.0 %collective-permute-start.25 = (bf16[192,384]{1,0:T(8,128)(2,1)}, bf16[192,384]{1,0:T(8,128)(2,1)S(1)}, u32[]{:S(2)}, u32[]{:S(2)}) collective-permute-start(bf16[192,384]{1,0:T(8,128)(2,1)} %get-tuple-element.105), channel_id=1, source_target_pairs={{0,8},{2,10},{4,12},{6,14},{8,0},{10,2},{12,4},{14,6},{16,24},{18,... | collective-permute-start | bytes 442376 | tf_op jit(solution)/shard_map/ppermute | solution.py:18
  141.7 22.7 %collective-permute-start.27 = (bf16[192,384]{1,0:T(8,128)(2,1)}, bf16[192,384]{1,0:T(8,128)(2,1)S(1)}, u32[]{:S(2)}, u32[]{:S(2)}) collective-permute-start(bf16[192,384]{1,0:T(8,128)(2,1)} %get-tuple-element.107), channel_id=1, source_target_pairs={{0,16},{2,18},{4,20},{6,22},{8,24},{10,26},{12,28},{14,30},{16,0},... | collective-permute-start | bytes 442376 | tf_op jit(solution)/shard_map/ppermute | solution.py:18
  144.6 21.2 %collective-permute-start.29 = (bf16[192,384]{1,0:T(8,128)(2,1)}, bf16[192,384]{1,0:T(8,128)(2,1)S(1)}, u32[]{:S(2)}, u32[]{:S(2)}) collective-permute-start(bf16[192,384]{1,0:T(8,128)(2,1)} %get-tuple-element.109), channel_id=1, source_target_pairs={{0,24},{2,26},{4,28},{6,30},{8,16},{10,18},{12,20},{14,22},{16,8},... | collective-permute-start | bytes 442376 | tf_op jit(solution)/shard_map/ppermute | solution.py:18
  161.5 4.3 %collective-permute-start.24 = (bf16[192,384]{1,0:T(8,128)(2,1)}, bf16[192,384]{1,0:T(8,128)(2,1)S(1)}, u32[]{:S(2)}, u32[]{:S(2)}) collective-permute-start(bf16[192,384]{1,0:T(8,128)(2,1)} %get-tuple-element.104), channel_id=1, source_target_pairs={{0,2},{2,0},{4,6},{6,4},{8,10},{10,8},{12,14},{14,12},{16,18},{18,... | collective-permute-start | bytes 442376 | tf_op jit(solution)/shard_map/ppermute | solution.py:18
  161.6 8.6 %collective-permute-start.26 = (bf16[192,384]{1,0:T(8,128)(2,1)}, bf16[192,384]{1,0:T(8,128)(2,1)S(1)}, u32[]{:S(2)}, u32[]{:S(2)}) collective-permute-start(bf16[192,384]{1,0:T(8,128)(2,1)} %get-tuple-element.106), channel_id=1, source_target_pairs={{0,10},{2,8},{4,14},{6,12},{8,2},{10,0},{12,6},{14,4},{16,26},{18,... | collective-permute-start | bytes 442376 | tf_op jit(solution)/shard_map/ppermute | solution.py:18
  161.6 13.2 %copy-start.3 = (bf16[192,384]{1,0:T(8,128)(2,1)}, bf16[192,384]{1,0:T(8,128)(2,1)S(1)}, u32[]{:S(2)}) copy-start(bf16[192,384]{1,0:T(8,128)(2,1)S(1)} %collective-permute-done.25.refs_2_) | copy-start | bytes 442372
  161.7 8.5 %collective-permute-start.28 = (bf16[192,384]{1,0:T(8,128)(2,1)}, bf16[192,384]{1,0:T(8,128)(2,1)S(1)}, u32[]{:S(2)}, u32[]{:S(2)}) collective-permute-start(bf16[192,384]{1,0:T(8,128)(2,1)} %get-tuple-element.108), channel_id=1, source_target_pairs={{0,18},{2,16},{4,22},{6,20},{8,26},{10,24},{12,30},{14,28},{16,2},... | collective-permute-start | bytes 442376 | tf_op jit(solution)/shard_map/ppermute | solution.py:18
  164.3 10.5 %copy-start.4 = (bf16[192,384]{1,0:T(8,128)(2,1)}, bf16[192,384]{1,0:T(8,128)(2,1)S(1)}, u32[]{:S(2)}) copy-start(bf16[192,384]{1,0:T(8,128)(2,1)S(1)} %collective-permute-done.27.refs_4_) | copy-start | bytes 442372
  164.3 10.5 %collective-permute-start.30 = (bf16[192,384]{1,0:T(8,128)(2,1)}, bf16[192,384]{1,0:T(8,128)(2,1)S(1)}, u32[]{:S(2)}, u32[]{:S(2)}) collective-permute-start(bf16[192,384]{1,0:T(8,128)(2,1)} %get-tuple-element.110), channel_id=1, source_target_pairs={{0,26},{2,24},{4,30},{6,28},{8,18},{10,16},{12,22},{14,20},{16,10}... | collective-permute-start | bytes 442376 | tf_op jit(solution)/shard_map/ppermute | solution.py:18
  165.8 9.1 %copy-start.5 = (bf16[192,384]{1,0:T(8,128)(2,1)}, bf16[192,384]{1,0:T(8,128)(2,1)S(1)}, u32[]{:S(2)}) copy-start(bf16[192,384]{1,0:T(8,128)(2,1)S(1)} %collective-permute-done.29.refs_6_) | copy-start | bytes 442372
  (12 other events, 32.9 us)

commit v7 on v6

--- a/solution.py
+++ b/solution.py
@@ -149,24 +149,24 @@
     return [dict(zip(away, outs[c * len(away) : (c + 1) * len(away)])) for c in range(chunks)]
 
 
-def attend_body(block, ways, offsets, spans, tile, table, *refs):
-    count = len(offsets)
+def attend_body(block, ways, slots, arrays, spans, tile, table, *refs):
+    count = len(slots)
     query_refs = refs[:ways]
-    block_refs = refs[ways : ways + count]
-    out_refs = refs[ways + count : 2 * ways + count]
-    ordered, asked, scores, highest, sums, total, position, sems = refs[2 * ways + count :]
+    block_refs = refs[ways : ways + arrays]
+    out_refs = refs[ways + arrays : 2 * ways + arrays]
+    ordered, asked, scores, highest, sums, total, position, sems = refs[2 * ways + arrays :]
     rows, width = out_refs[0].shape
     half = rows // 2
     heads = width // HD
     rest = count // ways
 
     copies = []
-    for slot, offset in enumerate(offsets):
+    for slot, (offset, array, row) in enumerate(slots):
         low = table[offset]
         for part, span in ((0, low), (1, spans - 1 - low)):
             copies.append(
                 pltpu.make_async_copy(
-                    block_refs[slot].at[pl.ds(part * half, half)],
+                    block_refs[array].at[pl.ds(row + part * half, half)],
                     ordered.at[pl.ds(pl.multiple_of(span * half, 16), half)],
                     sems.at[2 * slot + part],
                 )
@@ -191,23 +191,26 @@
 
     slope = LOG2_E / math.sqrt(HD)
     middle = spans * half // 2
+
+    def visible(part, h, column):
+        piece = scores[h, :, column : column + 128]
+        if column < middle * part:
+            return piece
+        return jnp.where(position[part] >= column, piece, HIDDEN)
+
     for part in range(2):
         starts = range(0, middle * (part + 1), tile)
         for start in starts:
             for h in range(heads):
-                found = lax.dot_general(
+                scores[h, :, start : start + tile] = lax.dot_general(
                     asked[part, :, h * HD : (h + 1) * HD],
                     ordered[start : start + tile, h * HD : (h + 1) * HD],
                     (((1,), (1,)), ((), ())),
                     preferred_element_type=jnp.float32,
                 )
                 top = highest[h]
-                for j in range(tile // 128):
-                    piece = found[:, j * 128 : (j + 1) * 128]
-                    if start >= middle * part:
-                        piece = jnp.where(position[part] >= start + j * 128, piece, HIDDEN)
-                    scores[h, :, start + j * 128 : start + (j + 1) * 128] = piece
-                    top = jnp.maximum(top, piece)
+                for column in range(start, start + tile, 128):
+                    top = jnp.maximum(top, visible(part, h, column))
                 highest[h] = top
         for h in range(heads):
             highest[h] = jnp.broadcast_to(
@@ -218,9 +221,8 @@
                 top = highest[h]
                 added = sums[h]
                 weights = []
-                for j in range(tile // 128):
-                    piece = scores[h, :, start + j * 128 : start + (j + 1) * 128]
-                    piece = jnp.exp2((piece - top) * slope)
+                for column in range(start, start + tile, 128):
+                    piece = jnp.exp2((visible(part, h, column) - top) * slope)
                     added = added + piece
                     weights.append(piece.astype(jnp.bfloat16))
                 sums[h] = added
@@ -244,7 +246,13 @@
 def attend(block, queries, blocks, table):
     rows, width = queries[0].shape
     ways, count = len(queries), len(blocks)
-    offsets = sorted(blocks)
+    arrays = []
+    slots = []
+    for offset in sorted(blocks):
+        array, row = blocks[offset]
+        if not any(array is other for other in arrays):
+            arrays.append(array)
+        slots.append((offset, [array is other for other in arrays].index(True), row))
     spans = 2 * count
     half = rows // 2
     length = count * rows
@@ -254,12 +262,12 @@
     smem = pl.BlockSpec(memory_space=pltpu.SMEM)
     flops = 6 * many * heads * length * HD
     return pl.pallas_call(
-        functools.partial(attend_body, block, ways, offsets, spans, tile),
+        functools.partial(attend_body, block, ways, slots, len(arrays), spans, tile),
         out_shape=[jax.ShapeDtypeStruct((rows, width), jnp.bfloat16)] * ways,
         grid=(1,),
         in_specs=[smem]
         + [pl.BlockSpec((rows, width), lambda i: (0, 0))] * ways
-        + [pl.BlockSpec(memory_space=pl.ANY)] * count,
+        + [pl.BlockSpec(memory_space=pl.ANY)] * len(arrays),
         out_specs=[pl.BlockSpec((rows, width), lambda i: (0, 0))] * ways,
         scratch_shapes=[
             pltpu.VMEM((length, 2 * width), jnp.bfloat16),
@@ -277,33 +285,84 @@
             bytes_accessed=4 * length * width + 4 * ways * rows * width,
             transcendentals=flops // (4 * HD),
         ),
-    )(table, *queries, *[blocks[i] for i in offsets])
-
-
-def assemble_body(ways, sequences, place, *refs):
-    out_ref = refs[-1]
+    )(table, *queries, *arrays)
+
+
+def table_body(offsets, *refs):
+    table = refs[-1]
+    for offset, ref in zip(offsets, refs):
+        found = ref[...].astype(jnp.float32)
+        for part in range(2):
+            table[offset + part] = jnp.max(found[part * EXTRA // 2 : (part + 1) * EXTRA // 2]).astype(jnp.int32)
+
+
+def span_table(blocks, rows):
+    offsets = sorted(blocks)
+    return pl.pallas_call(
+        functools.partial(table_body, offsets),
+        out_shape=jax.ShapeDtypeStruct((2 * len(offsets),), jnp.int32),
+        grid=(1,),
+        in_specs=[
+            pl.BlockSpec((EXTRA, 128), functools.partial(lambda row, i: (row, 0), (blocks[i][1] + rows) // EXTRA))
+            for i in offsets
+        ],
+        out_specs=pl.BlockSpec(memory_space=pltpu.SMEM),
+        compiler_params=pltpu.CompilerParams(vmem_limit_bytes=VMEM_LIMIT),
+    )(*[blocks[i][0] for i in offsets])
+
+
+def pack_body(*refs):
+    for n, ref in enumerate(refs[:-1]):
+
+        @pl.when(pl.program_id(0) == n)
+        def _():
+            refs[-1][...] = ref[...]
+
+
+def pack(pieces):
+    if len(pieces) == 1:
+        return pieces[0]
+    rows, columns = pieces[0].shape
+    return pl.pallas_call(
+        pack_body,
+        out_shape=jax.ShapeDtypeStruct((len(pieces) * rows, columns), jnp.bfloat16),
+        grid=(len(pieces),),
+        in_specs=[pl.BlockSpec((rows, columns), lambda i: (0, 0))] * len(pieces),
+        out_specs=pl.BlockSpec((rows, columns), lambda i: (i, 0)),
+        compiler_params=pltpu.CompilerParams(vmem_limit_bytes=VMEM_LIMIT),
+    )(*pieces)
+
+
+def assemble_body(ways, place, *refs):
     for a in range(ways):
 
         @pl.when(pl.program_id(0) == a)
         def _():
-            for b in range(sequences):
-                out_ref[place[2] ^ b] = refs[a * sequences + b][...]
-
-
-def assemble(pieces, place):
-    ways, sequences = len(pieces), len(pieces[0])
-    rows, width = pieces[0][0].shape
+            refs[-1][0] = refs[a][...]
+
+
+def assemble(pieces, b, before, place):
+    ways = len(pieces)
+    rows, width = pieces[0].shape
+    in_specs = [pl.BlockSpec((rows, width), lambda a, place: (0, 0))] * ways
+    operands = list(pieces)
+    aliases = {}
+    if before is not None:
+        in_specs.append(pl.BlockSpec(memory_space=pl.ANY))
+        operands.append(before)
+        aliases = {1 + ways: 0}
     return pl.pallas_call(
-        functools.partial(assemble_body, ways, sequences),
-        out_shape=jax.ShapeDtypeStruct((sequences, rows, ways * width), jnp.bfloat16),
+        functools.partial(assemble_body, ways),
+        out_shape=jax.ShapeDtypeStruct((2, rows, ways * width), jnp.bfloat16),
         grid_spec=pltpu.PrefetchScalarGridSpec(
             num_scalar_prefetch=1,
             grid=(ways,),
-            in_specs=[pl.BlockSpec((rows, width), lambda a, place: (0, 0))] * (ways * sequences),
-            out_specs=pl.BlockSpec((sequences, rows, width), lambda a, place: (0, 0, place[1] ^ a)),
-        ),
-        compiler_params=pltpu.CompilerParams(vmem_limit_bytes=VMEM_LIMIT),
-    )(place, *[piece for row in pieces for piece in row])
+            in_specs=in_specs,
+            out_specs=pl.BlockSpec((1, rows, width), lambda a, place: (place[2] ^ b, 0, place[1] ^ a)),
+        ),
+        input_output_aliases=aliases,
+        compiler_params=pltpu.CompilerParams(vmem_limit_bytes=VMEM_LIMIT),
+    )(place, *operands)
 
 
 def on_device(ctx_size, tp_size, hidden_in, w_q, w_k, w_v, event_pos):
@@ -344,40 +403,52 @@
                 rest_products(received, [0], [w_k, w_v], [start_k, start_v], later, ways, part, EXTRA)[0]
             )
     first = {a: over_ctx(made_0[a], a * rest) for a in away}
-    ahead = over_ctx(made_0[0], rest // 2)
     (made_1,) = rest_products(received, [1], [w_k, w_v], [start_k, start_v], place, ways, away)
-    received, made_1 = lax.optimization_barrier((received, made_1))
     ahead_1 = over_ctx(made_1[0], rest // 2)
+    for a in away:
+        first[a], made_1[a] = lax.optimization_barrier((first[a], made_1[a]))
+    packed = pack([first[a] for a in range(ways)])
+    received, packed, made_1[0] = lax.optimization_barrier((received, packed, made_1[0]))
     asked = rest_products(received, [0, 1], [w_q], [start_q], place, ways, away)
-    for a in away:
-        first[a], asked[0][a] = lax.optimization_barrier((first[a], asked[0][a]))
-    blocks = {a * rest: first[a] for a in away}
-    blocks[rest // 2] = ahead
-    blocks[rest // 2 + 1] = ahead_1
+
+    whole = {0: packed}
+    bit = rest // 2
+    while bit > 1:
+        for i in list(whole):
+            whole[i ^ bit] = over_ctx(whole[i], bit)
+        bit //= 2
+    blocks = {}
+    for i, array in whole.items():
+        for a in range(ways):
+            blocks[i ^ (a * rest)] = (array, a * (rows + EXTRA))
+    table = span_table(blocks, rows)
+
+    second = {}
     queries = [{}, {}]
     for a in away:
-        last = (first[a], ahead)
-        for made, keep, key in ((made_1, blocks, a * rest + 1), (asked[0], queries[0], a), (asked[1], queries[1], a)):
+        last = first[a]
+        for made, keep, key in ((made_1, second, a * rest + 1), (asked[0], queries[0], a), (asked[1], queries[1], a)):
             value, last = lax.optimization_barrier((made[a], last))
             last = keep[key] = over_ctx(value, a * rest)
-            if keep is blocks:
+            if keep is second and a:
                 last = (last, ahead_1)
+    freed = whole[rest // 2]
+    for a in away[:-1]:
+        second[a * rest + 1], freed = lax.optimization_barrier((second[a * rest + 1], freed))
+    second[rest // 2 + 1] = ahead_1
     bit = rest // 2
     while bit > 1:
-        for i in list(blocks):
-            if i ^ bit not in blocks:
-                blocks[i ^ bit] = over_ctx(blocks[i], bit)
+        for i in list(second):
+            if i ^ bit not in second:
+                second[i ^ bit] = over_ctx(second[i], bit)
         bit //= 2
-    table = []
-    for i in range(0, ctx_size, 2):
-        table += [blocks[i][rows, :1], blocks[i][rows + EXTRA // 2, :1]]
-    table = jnp.concatenate(table).astype(jnp.int32)
-    pieces = [[None] * 2 for _ in range(ways)]
+    blocks.update({i: (array, 0) for i, array in second.items()})
+    out = None
     for b in range(2):
         outs = attend(b, [queries[b][a] for a in range(ways)], blocks, table)
-        for a in away:
-            pieces[a][b] = over_ctx(outs[a], a * rest + b)
-    return assemble(pieces, place)
+        pieces = {a: over_ctx(outs[a], a * rest + b) for a in away}
+        out = assemble([pieces[a] for a in range(ways)], b, out, place)
+    return out
 
 
 def solution(mesh):

time: 181 us -> 188 us (1.039)
  local copies, waits for them, and re-layouts: 25.1 us -> 12.2 us
  waiting for transfers between devices: 27.4 us -> 37.7 us
  Pallas kernels: 85.7 us -> 92.8 us
  starting transfers between devices: 39.2 us -> 42.9 us
    ppermute x31 -> x28, waiting for transfers between devices: 27.4 us -> 37.7 us  [exchange(): return lax.ppermute(value, axis, [(i, i ^ bit) for i in range(size)])]
    concatenate x1 -> x0, local copies, waits for them, and re-layouts: 10.2 us -> none  [on_device(): table = jnp.concatenate(table).astype(jnp.int32)]
    pallas_call x3 -> x6, Pallas kernels: 31.6 us -> 38.7 us  [the longest x2 28 us: attend(): pl.pallas_call(functools.partial(attend_body, block, ways, slots, len(arr...]
    slice x8 -> x0, local copies, waits for them, and re-layouts: 5.33 us -> none  [on_device(): table += [blocks[i][rows, :1], blocks[i][rows + EXTRA // 2, :1]]]
    ppermute x31 -> x28, starting transfers between devices: 39.2 us -> 42.9 us  [exchange(): return lax.ppermute(value, axis, [(i, i ^ bit) for i in range(size)])]
    unnamed x58 -> x66, local copies, waits for them, and re-layouts: 4.41 us -> 7.31 us
  transfers between devices with their start and end apart: 31 -> 28, of which waited for: 5 -> 9; matrix products, arithmetic and copies ran while one was open for 11% -> 2% of each run, Pallas kernels for 46% -> 46%
where the time goes in v7:
time: 188 us; the launch traced here: 187 us
  Pallas kernels  92.8 us (49%)
  starting transfers between devices  42.9 us (23%)
  waiting for transfers between devices  37.7 us (20%)
  local copies, waits for them, and re-layouts  12.2 us (6%)
    ppermute x28, starting transfers between devices, exchange(): return lax.ppermute(value, axis, [(i, i ^ bit) for i in range(size)])  42.9 us
    ppermute x28, waiting for transfers between devices, exchange(): return lax.ppermute(value, axis, [(i, i ^ bit) for i in range(size)])  37.7 us
    pallas_call x4, Pallas kernels, rest_products(): pl.pallas_call(functools.partial(rest_body, shares, len(weights), chunks,...  35.5 us
    pallas_call x2, Pallas kernels, attend(): pl.pallas_call(functools.partial(attend_body, block, ways, slots, len(arr...  28 us
    pallas_call x1, Pallas kernels, own_products(): pl.pallas_call(functools.partial(own_body, len(weights)), out_shape=[jax....  18.5 us
    unnamed x66, local copies, waits for them, and re-layouts  7.31 us
    pallas_call x2, Pallas kernels, assemble(): pl.pallas_call(functools.partial(assemble_body, ways), out_shape=jax.Shap...  6.49 us
  transfers between devices with their start and end apart: 28, of which 9 were waited for; matrix products, arithmetic and copies ran while one was open for 2% of the time, Pallas kernels for 46%

profile of v7, /device:TPU:0, one launch (start us, length us, event | category | flops | bytes accessed | tf_op | source)
XLA Modules:
  0.0 186.6 jit_solution(9153409319119613280)
XLA Ops:
  0.0 2.6 %dynamic-slice_bitcast_fusion = (bf16[192,2560]{1,0:T(8,128)(2,1)}, bf16[192,2560]{1,0:T(8,128)(2,1)S(1)}) fusion(bf16[2,192,2560]{2,1,0:T(8,128)(2,1)} %mine_ref.1, s32[]{:T(128)S(6)} %select_n.29, s32[]{:T(128)S(6)} %select_n.28), kind=kLoop, calls=%fused_computation | loop fusion | bytes 3932168 | tf_op jit(solution)/shard_map/jit(dynamic_index_in_dim)/squeeze | solution.py:391
  3.0 2.5 %collective-permute-start = (bf16[192,2560]{1,0:T(8,128)(2,1)S(1)}, bf16[192,2560]{1,0:T(8,128)(2,1)S(1)}, u32[]{:S(2)}, u32[]{:S(2)}) collective-permute-start(bf16[192,2560]{1,0:T(8,128)(2,1)S(1)} %get-tuple-element.110), channel_id=1, source_target_pairs={{0,1},{1,0},{2,3},{3,2},{4,5},{5,4},{6,7},{7,6},{8,9},{9,8},{10,11... | collective-permute-start | bytes 2949128 | tf_op jit(solution)/shard_map/ppermute | solution.py:18
  5.8 0.6 fusion
  6.6 0.6 pad_add_fusion.place
  7.2 0.7 collective-permute-done.3
  7.8 1.7 concatenate.4.place
  9.6 0.5 collective-permute-start.2
  10.5 18.5 %shard_map.55 = (f32[2,192,1536]{2,1,0:T(8,128)}, f32[2,192,1536]{2,1,0:T(8,128)}, f32[2,192,1536]{2,1,0:T(8,128)}) custom-call(s32[4]{0:T(128)} %pad_add_fusion.place, bf16[2,192,2560]{2,1,0:T(8,128)(2,1)} %mine_ref.1, bf16[192,2560]{1,0:T(8,128)(2,1)} %copy-done.3, bf16[5120,1536]{1,0:T(8,128)(2,1)} %refs_1_.7, bf16[5120,1536]{1,0:T(8,128)(2,1)} %refs_2_.8, ...), custom_call_target="tpu_custom_call" | custom-call | flops 9059696640 | bytes 23592960 | tf_op jit(solution)/shard_map/pallas_call | solution.py:42
  29.1 0.9 copy-done.1
  30.0 7.2 %shard_map.58 = (bf16[208,768]{1,0:T(8,128)(2,1)}, bf16[208,768]{1,0:T(8,128)(2,1)}) custom-call(s32[6]{0:T(128)} %concatenate.4.place, bf16[192,2560]{1,0:T(8,128)(2,1)} %copy-done.1, bf16[5120,1536]{1,0:T(8,128)(2,1)} %refs_1_.7, bf16[5120,1536]{1,0:T(8,128)(2,1)} %refs_2_.8, f32[2,192,1536]{2,1,0:T(8,128)} %get-tuple-element.57.refs_3_, ...), custom_call_target="tpu_custom_call" | custom-call | flops 1509949440 | bytes 7864320 | tf_op jit(solution)/shard_map/pallas_call | solution.py:127
  37.2 2.7 %collective-permute-start.5 = (bf16[208,768]{1,0:T(8,128)(2,1)}, bf16[208,768]{1,0:T(8,128)(2,1)S(1)}, u32[]{:S(2)}, u32[]{:S(2)}) collective-permute-start(bf16[208,768]{1,0:T(8,128)(2,1)} %get-tuple-element.65), channel_id=1, source_target_pairs={{0,16},{2,18},{4,20},{6,22},{8,24},{10,26},{12,28},{14,30},{16,0},... | collective-permute-start | bytes 958472 | tf_op jit(solution)/shard_map/ppermute | solution.py:18
  39.9 1.2 collective-permute-start.6
  41.1 7.4 %shard_map.56 = (bf16[208,768]{1,0:T(8,128)(2,1)}, bf16[208,768]{1,0:T(8,128)(2,1)}) custom-call(s32[6]{0:T(128)} %concatenate.4.place, bf16[192,2560]{1,0:T(8,128)(2,1)} %copy-done.1, bf16[5120,1536]{1,0:T(8,128)(2,1)} %refs_1_.7, bf16[5120,1536]{1,0:T(8,128)(2,1)} %refs_2_.8, f32[2,192,1536]{2,1,0:T(8,128)} %get-tuple-element.57.refs_3_, ...), custom_call_target="tpu_custom_call" | custom-call | flops 1509949440 | bytes 7864320 | tf_op jit(solution)/shard_map/pallas_call | solution.py:127
  49.0 1.0 copy-done.2
  50.0 11.2 %shard_map.57 = (bf16[192,768]{1,0:T(8,128)(2,1)}, bf16[192,768]{1,0:T(8,128)(2,1)}, bf16[192,768]{1,0:T(8,128)(2,1)}, bf16[192,768]{1,0:T(8,128)(2,1)}) custom-call(s32[4]{0:T(128)} %pad_add_fusion.place, bf16[192,2560]{1,0:T(8,128)(2,1)} %copy-done.2, bf16[5120,1536]{1,0:T(8,128)(2,1)} %refs_1_.7, bf16[5120,1536]{1,0:T(8,128)(2,1)} %refs_2_.8, ...), custom_call_target="tpu_custom_call" | custom-call | flops 3019898880 | bytes 15728640 | tf_op jit(solution)/shard_map/pallas_call | solution.py:127
  61.3 1.1 collective-permute-done.5.refs_2_
  62.4 6.2 %collective-permute-done.4.refs_1_ = bf16[208,768]{1,0:T(8,128)(2,1)S(1)} collective-permute-done((bf16[208,768]{1,0:T(8,128)(2,1)}, bf16[208,768]{1,0:T(8,128)(2,1)S(1)}, u32[]{:S(2)}, u32[]{:S(2)}) %collective-permute-start.4) | collective-permute-done | bytes 319520 | tf_op jit(solution)/shard_map/ppermute | solution.py:18
  68.6 0.7 copy-done.6
  69.3 2.9 %shard_map.59.refs_0_.refs_2_.refs_4_.refs_6_ = bf16[832,768]{1,0:T(8,128)(2,1)} custom-call(bf16[208,768]{1,0:T(8,128)(2,1)} %get-tuple-element.61.refs_0_, bf16[208,768]{1,0:T(8,128)(2,1)} %copy-done.6, bf16[208,768]{1,0:T(8,128)(2,1)} %copy-done.4, bf16[208,768]{1,0:T(8,128)(2,1)} %copy-done.5), custom_call_target="tpu_custom_call" | custom-call | tf_op jit(solution)/shard_map/pallas_call | solution.py:326
  72.2 1.5 collective-permute-start.7
  73.7 3.5 %collective-permute-start.15 = (bf16[192,768]{1,0:T(8,128)(2,1)S(1)}, bf16[192,768]{1,0:T(8,128)(2,1)S(1)}, u32[]{:S(2)}, u32[]{:S(2)}) collective-permute-start(bf16[192,768]{1,0:T(8,128)(2,1)S(1)} %copy-done.24), channel_id=1, source_target_pairs={{0,24},{2,26},{4,28},{6,30},{8,16},{10,18},{12,20},{14,22},{16,8},... | collective-permute-start | bytes 884744 | tf_op jit(solution)/shard_map/ppermute | solution.py:18
  77.8 0.8 collective-permute-start.8
  78.6 9.7 %shard_map.61 = (bf16[192,384]{1,0:T(8,128)(2,1)}, bf16[192,384]{1,0:T(8,128)(2,1)}, bf16[192,384]{1,0:T(8,128)(2,1)}, bf16[192,384]{1,0:T(8,128)(2,1)}, bf16[19...) custom-call(s32[4]{0:T(128)} %pad_add_fusion.place, ...), custom_call_target="tpu_custom_call" | custom-call | flops 3019898880 | bytes 7864320 | tf_op jit(solution)/shard_map/pallas_call | solution.py:127
  88.4 20.4 %collective-permute-done.9.refs_7_ = bf16[192,768]{1,0:T(8,128)(2,1)S(1)} collective-permute-done((bf16[192,768]{1,0:T(8,128)(2,1)S(1)}, bf16[192,768]{1,0:T(8,128)(2,1)S(1)}, u32[]{:S(2)}, u32[]{:S(2)}) %collective-permute-start.9) | collective-permute-done | bytes 294944 | tf_op jit(solution)/shard_map/ppermute | solution.py:18
  108.8 3.5 %collective-permute-start.16 = (bf16[192,384]{1,0:T(8,128)(2,1)}, bf16[192,384]{1,0:T(8,128)(2,1)S(1)}, u32[]{:S(2)}, u32[]{:S(2)}) collective-permute-start(bf16[192,384]{1,0:T(8,128)(2,1)} %get-tuple-element.98), channel_id=1, source_target_pairs={{0,24},{2,26},{4,28},{6,30},{8,16},{10,18},{12,20},{14,22},{16,8},... | collective-permute-start | bytes 442376 | tf_op jit(solution)/shard_map/ppermute | solution.py:18
  112.3 1.5 collective-permute-start.19
  114.4 1.5 collective-permute-start.20
  116.0 6.7 %collective-permute-start.10 = (bf16[192,384]{1,0:T(8,128)(2,1)}, bf16[192,384]{1,0:T(8,128)(2,1)S(1)}, u32[]{:S(2)}, u32[]{:S(2)}) collective-permute-start(bf16[192,384]{1,0:T(8,128)(2,1)} %get-tuple-element.86), channel_id=1, source_target_pairs={{0,8},{2,10},{4,12},{6,14},{8,0},{10,2},{12,4},{14,6},{16,24},{18,... | collective-permute-start | bytes 442376 | tf_op jit(solution)/shard_map/ppermute | solution.py:18
  122.6 2.0 %collective-permute-done.13.refs_2_ = bf16[192,384]{1,0:T(8,128)(2,1)S(1)} collective-permute-done((bf16[192,384]{1,0:T(8,128)(2,1)}, bf16[192,384]{1,0:T(8,128)(2,1)S(1)}, u32[]{:S(2)}, u32[]{:S(2)}) %collective-permute-start.13) | collective-permute-done | bytes 147488 | tf_op jit(solution)/shard_map/ppermute | solution.py:18
  124.6 2.5 %collective-permute-start.17 = (bf16[192,384]{1,0:T(8,128)(2,1)}, bf16[192,384]{1,0:T(8,128)(2,1)S(1)}, u32[]{:S(2)}, u32[]{:S(2)}) collective-permute-start(bf16[192,384]{1,0:T(8,128)(2,1)} %get-tuple-element.99), channel_id=1, source_target_pairs={{0,24},{2,26},{4,28},{6,30},{8,16},{10,18},{12,20},{14,22},{16,8},... | collective-permute-start | bytes 442376 | tf_op jit(solution)/shard_map/ppermute | solution.py:18
  127.1 3.5 %collective-permute-start.14 = (bf16[192,384]{1,0:T(8,128)(2,1)}, bf16[192,384]{1,0:T(8,128)(2,1)S(1)}, u32[]{:S(2)}, u32[]{:S(2)}) collective-permute-start(bf16[192,384]{1,0:T(8,128)(2,1)} %get-tuple-element.93), channel_id=1, source_target_pairs={{0,16},{2,18},{4,20},{6,22},{8,24},{10,26},{12,28},{14,30},{16,0},... | collective-permute-start | bytes 442376 | tf_op jit(solution)/shard_map/ppermute | solution.py:18
  130.6 1.4 shard_map.60.table
  132.9 0.7 copy-done.21
  133.6 13.9 %shard_map.63 = (bf16[192,384]{1,0:T(8,128)(2,1)}, bf16[192,384]{1,0:T(8,128)(2,1)}, bf16[192,384]{1,0:T(8,128)(2,1)}, bf16[192,384]{1,0:T(8,128)(2,1)}) custom-call(s32[16]{0:T(128)} %shard_map.60.table, bf16[192,384]{1,0:T(8,128)(2,1)} %get-tuple-element.80.refs_0_, bf16[192,384]{1,0:T(8,128)(2,1)} %copy-done.31, bf16[192,384]{1,0:T(8,128)(2,1)} %copy-done.30, ...), custom_call_target="tpu_custom_call" | custom-call | flops 2717908992 | bytes 5898240 | tf_op jit(solution)/shard_map/pallas_call | solution.py:264
  147.5 2.1 %collective-permute-start.25 = (bf16[192,384]{1,0:T(8,128)(2,1)}, bf16[192,384]{1,0:T(8,128)(2,1)S(1)}, u32[]{:S(2)}, u32[]{:S(2)}) collective-permute-start(bf16[192,384]{1,0:T(8,128)(2,1)} %get-tuple-element.106), channel_id=1, source_target_pairs={{0,8},{2,10},{4,12},{6,14},{8,0},{10,2},{12,4},{14,6},{16,24},{18,... | collective-permute-start | bytes 442376 | tf_op jit(solution)/shard_map/ppermute | solution.py:18
  149.7 2.4 %collective-permute-start.27 = (bf16[192,384]{1,0:T(8,128)(2,1)}, bf16[192,384]{1,0:T(8,128)(2,1)S(1)}, u32[]{:S(2)}, u32[]{:S(2)}) collective-permute-start(bf16[192,384]{1,0:T(8,128)(2,1)} %get-tuple-element.108), channel_id=1, source_target_pairs={{0,24},{2,26},{4,28},{6,30},{8,16},{10,18},{12,20},{14,22},{16,8},... | collective-permute-start | bytes 442376 | tf_op jit(solution)/shard_map/ppermute | solution.py:18
  152.1 0.6 copy-done.28
  152.7 0.7 copy-done.29
  153.4 14.1 %shard_map.62 = (bf16[192,384]{1,0:T(8,128)(2,1)}, bf16[192,384]{1,0:T(8,128)(2,1)}, bf16[192,384]{1,0:T(8,128)(2,1)}, bf16[192,384]{1,0:T(8,128)(2,1)}) custom-call(s32[16]{0:T(128)} %shard_map.60.table, bf16[192,384]{1,0:T(8,128)(2,1)} %get-tuple-element.81.refs_0_, bf16[192,384]{1,0:T(8,128)(2,1)} %copy-done.29, bf16[192,384]{1,0:T(8,128)(2,1)} %copy-done.28, ...), custom_call_target="tpu_custom_call" | custom-call | flops 2717908992 | bytes 5898240 | tf_op jit(solution)/shard_map/pallas_call | solution.py:264
  167.5 1.2 collective-permute-start.22
  168.7 0.6 collective-permute-start.23
  169.3 2.4 %collective-permute-start.24 = (bf16[192,384]{1,0:T(8,128)(2,1)}, bf16[192,384]{1,0:T(8,128)(2,1)S(1)}, u32[]{:S(2)}, u32[]{:S(2)}) collective-permute-start(bf16[192,384]{1,0:T(8,128)(2,1)} %get-tuple-element.104), channel_id=1, source_target_pairs={{0,26},{2,24},{4,30},{6,28},{8,18},{10,16},{12,22},{14,20},{16,10}... | collective-permute-start | bytes 442376 | tf_op jit(solution)/shard_map/ppermute | solution.py:18
  171.8 0.6 copy-done.13
  172.4 3.2 %shard_map.64.refs_4_ = bf16[2,192,1536]{2,1,0:T(8,128)(2,1)} custom-call(s32[4]{0:T(128)} %pad_add_fusion.place, bf16[192,384]{1,0:T(8,128)(2,1)} %get-tuple-element.105.refs_0_, bf16[192,384]{1,0:T(8,128)(2,1)} %copy-done.11, bf16[192,384]{1,0:T(8,128)(2,1)} %copy-done.12, bf16[192,384]{1,0:T(8,128)(2,1)} %copy-done.13), custom_call_target="tpu_custom_call" | custom-call | tf_op jit(solution)/shard_map/pallas_call | solution.py:354
  175.7 6.4 %collective-permute-done.23.refs_2_ = bf16[192,384]{1,0:T(8,128)(2,1)S(1)} collective-permute-done((bf16[192,384]{1,0:T(8,128)(2,1)}, bf16[192,384]{1,0:T(8,128)(2,1)S(1)}, u32[]{:S(2)}, u32[]{:S(2)}) %collective-permute-start.23) | collective-permute-done | bytes 147488 | tf_op jit(solution)/shard_map/ppermute | solution.py:18
  182.1 0.6 copy-done.9
  182.7 0.7 copy-done.10
  183.4 3.2 %shard_map.65 = bf16[2,192,1536]{2,1,0:T(8,128)(2,1)} custom-call(s32[4]{0:T(128)} %pad_add_fusion.place, bf16[192,384]{1,0:T(8,128)(2,1)} %copy-done.7, bf16[192,384]{1,0:T(8,128)(2,1)} %copy-done.8, bf16[192,384]{1,0:T(8,128)(2,1)} %copy-done.9, bf16[192,384]{1,0:T(8,128)(2,1)} %copy-done.10, ...), custom_call_target="tpu_custom_call", output_to_operand_aliasing={{}: (5, {})} | custom-call | tf_op jit(solution)/shard_map/pallas_call | solution.py:354
  (92 shorter events, 4.0 us)
Async XLA Ops:
  0.0 5.5 %copy-start.32 = (s32[2,192]{1,0:T(2,128)S(1)}, s32[2,192]{1,0:T(2,128)}, u32[]{:S(2)}) copy-start(s32[2,192]{1,0:T(2,128)} %param.9) | copy-start | bytes 4612
  2.6 7.0 %collective-permute-start.1 = (bf16[192,2560]{1,0:T(8,128)(2,1)}, bf16[192,2560]{1,0:T(8,128)(2,1)S(1)}, u32[]{:S(2)}, u32[]{:S(2)}) collective-permute-start(bf16[192,2560]{1,0:T(8,128)(2,1)} %get-tuple-element.109), channel_id=1, source_target_pairs={{0,2},{2,0},{4,6},{6,4},{8,10},{10,8},{12,14},{14,12},{16,18},{18,... | collective-permute-start | bytes 2949128 | tf_op jit(solution)/shard_map/ppermute | solution.py:18
  3.0 26.0 %collective-permute-start = (bf16[192,2560]{1,0:T(8,128)(2,1)S(1)}, bf16[192,2560]{1,0:T(8,128)(2,1)S(1)}, u32[]{:S(2)}, u32[]{:S(2)}) collective-permute-start(bf16[192,2560]{1,0:T(8,128)(2,1)S(1)} %get-tuple-element.110), channel_id=1, source_target_pairs={{0,1},{1,0},{2,3},{3,2},{4,5},{5,4},{6,7},{7,6},{8,9},{9,8},{10,11... | collective-permute-start | bytes 2949128 | tf_op jit(solution)/shard_map/ppermute | solution.py:18
  6.4 1.5 collective-permute-start.3
  9.6 39.5 %collective-permute-start.2 = (bf16[192,2560]{1,0:T(8,128)(2,1)S(1)}, bf16[192,2560]{1,0:T(8,128)(2,1)S(1)}, u32[]{:S(2)}, u32[]{:S(2)}) collective-permute-start(bf16[192,2560]{1,0:T(8,128)(2,1)S(1)} %collective-permute-done.1.other_ref), channel_id=1, source_target_pairs={{0,1},{1,0},{2,3},{3,2},{4,5},{5,4},{6,7},{7,6},{8,9},{9,8},{10,11... | collective-permute-start | bytes 2949128 | tf_op jit(solution)/shard_map/ppermute | solution.py:18
  37.2 25.2 %collective-permute-start.5 = (bf16[208,768]{1,0:T(8,128)(2,1)}, bf16[208,768]{1,0:T(8,128)(2,1)S(1)}, u32[]{:S(2)}, u32[]{:S(2)}) collective-permute-start(bf16[208,768]{1,0:T(8,128)(2,1)} %get-tuple-element.65), channel_id=1, source_target_pairs={{0,16},{2,18},{4,20},{6,22},{8,24},{10,26},{12,28},{14,30},{16,0},... | collective-permute-start | bytes 958472 | tf_op jit(solution)/shard_map/ppermute | solution.py:18
  39.9 22.5 %collective-permute-start.6 = (bf16[208,768]{1,0:T(8,128)(2,1)}, bf16[208,768]{1,0:T(8,128)(2,1)S(1)}, u32[]{:S(2)}, u32[]{:S(2)}) collective-permute-start(bf16[208,768]{1,0:T(8,128)(2,1)} %get-tuple-element.68), channel_id=1, source_target_pairs={{0,24},{2,26},{4,28},{6,30},{8,16},{10,18},{12,20},{14,22},{16,8},... | collective-permute-start | bytes 958472 | tf_op jit(solution)/shard_map/ppermute | solution.py:18
  48.5 20.1 %collective-permute-start.4 = (bf16[208,768]{1,0:T(8,128)(2,1)}, bf16[208,768]{1,0:T(8,128)(2,1)S(1)}, u32[]{:S(2)}, u32[]{:S(2)}) collective-permute-start(bf16[208,768]{1,0:T(8,128)(2,1)} %get-tuple-element.62), channel_id=1, source_target_pairs={{0,8},{2,10},{4,12},{6,14},{8,0},{10,2},{12,4},{14,6},{16,24},{18,... | collective-permute-start | bytes 958472 | tf_op jit(solution)/shard_map/ppermute | solution.py:18
  61.2 12.5 %copy-start.24 = (bf16[192,768]{1,0:T(8,128)(2,1)S(1)}, bf16[192,768]{1,0:T(8,128)(2,1)}, u32[]{:S(2)}) copy-start(bf16[192,768]{1,0:T(8,128)(2,1)} %get-tuple-element.97) | copy-start | bytes 884740
  61.2 16.0 %copy-start.14 = (bf16[192,768]{1,0:T(8,128)(2,1)S(1)}, bf16[192,768]{1,0:T(8,128)(2,1)}, u32[]{:S(2)}) copy-start(bf16[192,768]{1,0:T(8,128)(2,1)} %get-tuple-element.79.refs_5_) | copy-start | bytes 884740
  61.2 16.6 %copy-start.23 = (bf16[192,768]{1,0:T(8,128)(2,1)S(1)}, bf16[192,768]{1,0:T(8,128)(2,1)}, u32[]{:S(2)}) copy-start(bf16[192,768]{1,0:T(8,128)(2,1)} %get-tuple-element.91) | copy-start | bytes 884740
  61.3 16.5 %copy-start.22 = (bf16[192,768]{1,0:T(8,128)(2,1)S(1)}, bf16[192,768]{1,0:T(8,128)(2,1)}, u32[]{:S(2)}) copy-start(bf16[192,768]{1,0:T(8,128)(2,1)} %get-tuple-element.85) | copy-start | bytes 884740
  62.4 6.2 %copy-start.4 = (bf16[208,768]{1,0:T(8,128)(2,1)}, bf16[208,768]{1,0:T(8,128)(2,1)S(1)}, u32[]{:S(2)}) copy-start(bf16[208,768]{1,0:T(8,128)(2,1)S(1)} %collective-permute-done.5.refs_2_) | copy-start | bytes 958468
  62.4 6.2 %copy-start.5 = (bf16[208,768]{1,0:T(8,128)(2,1)}, bf16[208,768]{1,0:T(8,128)(2,1)S(1)}, u32[]{:S(2)}) copy-start(bf16[208,768]{1,0:T(8,128)(2,1)S(1)} %collective-permute-done.6.refs_3_) | copy-start | bytes 958468
  72.2 42.1 %collective-permute-start.7 = (bf16[832,768]{1,0:T(8,128)(2,1)}, bf16[832,768]{1,0:T(8,128)(2,1)S(1)}, u32[]{:S(2)}, u32[]{:S(2)}) collective-permute-start(bf16[832,768]{1,0:T(8,128)(2,1)} %shard_map.59.refs_0_.refs_2_.refs_4_.refs_6_), channel_id=1, source_target_pairs={{0,4},{2,6},{4,0},{6,2},{8,12},{10,14},{12,8},{14,10},{16,20},{18,... | collective-permute-start | bytes 3833864 | tf_op jit(solution)/shard_map/ppermute | solution.py:18
  73.7 14.6 %collective-permute-start.15 = (bf16[192,768]{1,0:T(8,128)(2,1)S(1)}, bf16[192,768]{1,0:T(8,128)(2,1)S(1)}, u32[]{:S(2)}, u32[]{:S(2)}) collective-permute-start(bf16[192,768]{1,0:T(8,128)(2,1)S(1)} %copy-done.24), channel_id=1, source_target_pairs={{0,24},{2,26},{4,28},{6,30},{8,16},{10,18},{12,20},{14,22},{16,8},... | collective-permute-start | bytes 884744 | tf_op jit(solution)/shard_map/ppermute | solution.py:18
  77.3 31.5 %collective-permute-start.9 = (bf16[192,768]{1,0:T(8,128)(2,1)S(1)}, bf16[192,768]{1,0:T(8,128)(2,1)S(1)}, u32[]{:S(2)}, u32[]{:S(2)}) collective-permute-start(bf16[192,768]{1,0:T(8,128)(2,1)S(1)} %copy-done.14), channel_id=1, source_target_pairs={{0,4},{2,6},{4,0},{6,2},{8,12},{10,14},{12,8},{14,10},{16,20},{18,... | collective-permute-start | bytes 884744 | tf_op jit(solution)/shard_map/ppermute | solution.py:18
  77.8 34.5 %collective-permute-start.12 = (bf16[192,768]{1,0:T(8,128)(2,1)S(1)}, bf16[192,768]{1,0:T(8,128)(2,1)S(1)}, u32[]{:S(2)}, u32[]{:S(2)}) collective-permute-start(bf16[192,768]{1,0:T(8,128)(2,1)S(1)} %copy-done.23), channel_id=1, source_target_pairs={{0,16},{2,18},{4,20},{6,22},{8,24},{10,26},{12,28},{14,30},{16,0},... | collective-permute-start | bytes 884744 | tf_op jit(solution)/shard_map/ppermute | solution.py:18
  77.8 36.0 %collective-permute-start.8 = (bf16[192,768]{1,0:T(8,128)(2,1)S(1)}, bf16[192,768]{1,0:T(8,128)(2,1)S(1)}, u32[]{:S(2)}, u32[]{:S(2)}) collective-permute-start(bf16[192,768]{1,0:T(8,128)(2,1)S(1)} %copy-done.22), channel_id=1, source_target_pairs={{0,8},{2,10},{4,12},{6,14},{8,0},{10,2},{12,4},{14,6},{16,24},{18,... | collective-permute-start | bytes 884744 | tf_op jit(solution)/shard_map/ppermute | solution.py:18
  88.3 44.4 %copy-start.15 = (bf16[192,768]{1,0:T(8,128)(2,1)}, bf16[192,768]{1,0:T(8,128)(2,1)S(1)}, u32[]{:S(2)}) copy-start(bf16[192,768]{1,0:T(8,128)(2,1)S(1)} %collective-permute-done.15.refs_12_) | copy-start | bytes 884740
  108.7 24.0 %copy-start.16 = (bf16[192,768]{1,0:T(8,128)(2,1)}, bf16[192,768]{1,0:T(8,128)(2,1)S(1)}, u32[]{:S(2)}) copy-start(bf16[192,768]{1,0:T(8,128)(2,1)S(1)} %collective-permute-done.9.refs_7_) | copy-start | bytes 884740
  108.8 7.2 %collective-permute-start.16 = (bf16[192,384]{1,0:T(8,128)(2,1)}, bf16[192,384]{1,0:T(8,128)(2,1)S(1)}, u32[]{:S(2)}, u32[]{:S(2)}) collective-permute-start(bf16[192,384]{1,0:T(8,128)(2,1)} %get-tuple-element.98), channel_id=1, source_target_pairs={{0,24},{2,26},{4,28},{6,30},{8,16},{10,18},{12,20},{14,22},{16,8},... | collective-permute-start | bytes 442376 | tf_op jit(solution)/shard_map/ppermute | solution.py:18
  112.3 20.5 %copy-start.17 = (bf16[192,768]{1,0:T(8,128)(2,1)}, bf16[192,768]{1,0:T(8,128)(2,1)S(1)}, u32[]{:S(2)}) copy-start(bf16[192,768]{1,0:T(8,128)(2,1)S(1)} %collective-permute-done.12.refs_10_) | copy-start | bytes 884740
  112.3 19.8 %collective-permute-start.19 = (bf16[192,768]{1,0:T(8,128)(2,1)S(1)}, bf16[192,768]{1,0:T(8,128)(2,1)S(1)}, u32[]{:S(2)}, u32[]{:S(2)}) collective-permute-start(bf16[192,768]{1,0:T(8,128)(2,1)S(1)} %collective-permute-done.12.refs_10_), channel_id=1, source_target_pairs={{0,4},{2,6},{4,0},{6,2},{8,12},{10,14},{12,8},{14,10},{16,20},{18,... | collective-permute-start | bytes 884744 | tf_op jit(solution)/shard_map/ppermute | solution.py:18
  113.8 18.9 %copy-start.18 = (bf16[192,768]{1,0:T(8,128)(2,1)}, bf16[192,768]{1,0:T(8,128)(2,1)S(1)}, u32[]{:S(2)}) copy-start(bf16[192,768]{1,0:T(8,128)(2,1)S(1)} %collective-permute-done.8.refs_8_) | copy-start | bytes 884740
  113.8 18.4 %collective-permute-start.18 = (bf16[192,768]{1,0:T(8,128)(2,1)S(1)}, bf16[192,768]{1,0:T(8,128)(2,1)S(1)}, u32[]{:S(2)}, u32[]{:S(2)}) collective-permute-start(bf16[192,768]{1,0:T(8,128)(2,1)S(1)} %collective-permute-done.8.refs_8_), channel_id=1, source_target_pairs={{0,4},{2,6},{4,0},{6,2},{8,12},{10,14},{12,8},{14,10},{16,20},{18,... | collective-permute-start | bytes 884744 | tf_op jit(solution)/shard_map/ppermute | solution.py:18
  114.3 16.3 %copy-start = (bf16[832,768]{1,0:T(8,128)(2,1)}, bf16[832,768]{1,0:T(8,128)(2,1)S(1)}, u32[]{:S(2)}) copy-start(bf16[832,768]{1,0:T(8,128)(2,1)S(1)} %collective-permute-done.7.refs_1_.refs_3_.refs_5_.refs_7_.refs_6_) | copy-start | bytes 3833860
  114.4 18.4 %collective-permute-start.20 = (bf16[192,768]{1,0:T(8,128)(2,1)S(1)}, bf16[192,768]{1,0:T(8,128)(2,1)S(1)}, u32[]{:S(2)}, u32[]{:S(2)}) collective-permute-start(bf16[192,768]{1,0:T(8,128)(2,1)S(1)} %collective-permute-done.15.refs_12_), channel_id=1, source_target_pairs={{0,4},{2,6},{4,0},{6,2},{8,12},{10,14},{12,8},{14,10},{16,20},{18,... | collective-permute-start | bytes 884744 | tf_op jit(solution)/shard_map/ppermute | solution.py:18
  115.9 8.7 %collective-permute-start.13 = (bf16[192,384]{1,0:T(8,128)(2,1)}, bf16[192,384]{1,0:T(8,128)(2,1)S(1)}, u32[]{:S(2)}, u32[]{:S(2)}) collective-permute-start(bf16[192,384]{1,0:T(8,128)(2,1)} %get-tuple-element.92), channel_id=1, source_target_pairs={{0,16},{2,18},{4,20},{6,22},{8,24},{10,26},{12,28},{14,30},{16,0},... | collective-permute-start | bytes 442376 | tf_op jit(solution)/shard_map/ppermute | solution.py:18
  116.0 16.1 %copy-start.26 = (bf16[192,384]{1,0:T(8,128)(2,1)}, bf16[192,384]{1,0:T(8,128)(2,1)S(1)}, u32[]{:S(2)}) copy-start(bf16[192,384]{1,0:T(8,128)(2,1)S(1)} %collective-permute-done.16.refs_3_) | copy-start | bytes 442372
  116.0 11.2 %collective-permute-start.10 = (bf16[192,384]{1,0:T(8,128)(2,1)}, bf16[192,384]{1,0:T(8,128)(2,1)S(1)}, u32[]{:S(2)}, u32[]{:S(2)}) collective-permute-start(bf16[192,384]{1,0:T(8,128)(2,1)} %get-tuple-element.86), channel_id=1, source_target_pairs={{0,8},{2,10},{4,12},{6,14},{8,0},{10,2},{12,4},{14,6},{16,24},{18,... | collective-permute-start | bytes 442376 | tf_op jit(solution)/shard_map/ppermute | solution.py:18
  124.6 7.5 %copy-start.30 = (bf16[192,384]{1,0:T(8,128)(2,1)}, bf16[192,384]{1,0:T(8,128)(2,1)S(1)}, u32[]{:S(2)}) copy-start(bf16[192,384]{1,0:T(8,128)(2,1)S(1)} %collective-permute-done.13.refs_2_) | copy-start | bytes 442372
  124.6 25.1 %collective-permute-start.17 = (bf16[192,384]{1,0:T(8,128)(2,1)}, bf16[192,384]{1,0:T(8,128)(2,1)S(1)}, u32[]{:S(2)}, u32[]{:S(2)}) collective-permute-start(bf16[192,384]{1,0:T(8,128)(2,1)} %get-tuple-element.99), channel_id=1, source_target_pairs={{0,24},{2,26},{4,28},{6,30},{8,16},{10,18},{12,20},{14,22},{16,8},... | collective-permute-start | bytes 442376 | tf_op jit(solution)/shard_map/ppermute | solution.py:18
  127.1 4.9 %copy-start.31 = (bf16[192,384]{1,0:T(8,128)(2,1)}, bf16[192,384]{1,0:T(8,128)(2,1)S(1)}, u32[]{:S(2)}) copy-start(bf16[192,384]{1,0:T(8,128)(2,1)S(1)} %collective-permute-done.10.refs_1_) | copy-start | bytes 442372
  127.1 24.9 %collective-permute-start.14 = (bf16[192,384]{1,0:T(8,128)(2,1)}, bf16[192,384]{1,0:T(8,128)(2,1)S(1)}, u32[]{:S(2)}, u32[]{:S(2)}) collective-permute-start(bf16[192,384]{1,0:T(8,128)(2,1)} %get-tuple-element.93), channel_id=1, source_target_pairs={{0,16},{2,18},{4,20},{6,22},{8,24},{10,26},{12,28},{14,30},{16,0},... | collective-permute-start | bytes 442376 | tf_op jit(solution)/shard_map/ppermute | solution.py:18
  132.1 19.9 %collective-permute-start.11 = (bf16[192,384]{1,0:T(8,128)(2,1)S(1)}, bf16[192,384]{1,0:T(8,128)(2,1)S(1)}, u32[]{:S(2)}, u32[]{:S(2)}) collective-permute-start(bf16[192,384]{1,0:T(8,128)(2,1)S(1)} %copy-done.25), channel_id=1, source_target_pairs={{0,8},{2,10},{4,12},{6,14},{8,0},{10,2},{12,4},{14,6},{16,24},{18,... | collective-permute-start | bytes 442376 | tf_op jit(solution)/shard_map/ppermute | solution.py:18
  147.5 21.2 %collective-permute-start.25 = (bf16[192,384]{1,0:T(8,128)(2,1)}, bf16[192,384]{1,0:T(8,128)(2,1)S(1)}, u32[]{:S(2)}, u32[]{:S(2)}) collective-permute-start(bf16[192,384]{1,0:T(8,128)(2,1)} %get-tuple-element.106), channel_id=1, source_target_pairs={{0,8},{2,10},{4,12},{6,14},{8,0},{10,2},{12,4},{14,6},{16,24},{18,... | collective-permute-start | bytes 442376 | tf_op jit(solution)/shard_map/ppermute | solution.py:18
  149.6 19.8 %collective-permute-start.26 = (bf16[192,384]{1,0:T(8,128)(2,1)}, bf16[192,384]{1,0:T(8,128)(2,1)S(1)}, u32[]{:S(2)}, u32[]{:S(2)}) collective-permute-start(bf16[192,384]{1,0:T(8,128)(2,1)} %get-tuple-element.107), channel_id=1, source_target_pairs={{0,16},{2,18},{4,20},{6,22},{8,24},{10,26},{12,28},{14,30},{16,0},... | collective-permute-start | bytes 442376 | tf_op jit(solution)/shard_map/ppermute | solution.py:18
  149.7 2.4 %copy-start.27 = (bf16[192,384]{1,0:T(8,128)(2,1)}, bf16[192,384]{1,0:T(8,128)(2,1)S(1)}, u32[]{:S(2)}) copy-start(bf16[192,384]{1,0:T(8,128)(2,1)S(1)} %collective-permute-done.17.refs_3_) | copy-start | bytes 442372
  149.7 22.1 %collective-permute-start.27 = (bf16[192,384]{1,0:T(8,128)(2,1)}, bf16[192,384]{1,0:T(8,128)(2,1)S(1)}, u32[]{:S(2)}, u32[]{:S(2)}) collective-permute-start(bf16[192,384]{1,0:T(8,128)(2,1)} %get-tuple-element.108), channel_id=1, source_target_pairs={{0,24},{2,26},{4,28},{6,30},{8,16},{10,18},{12,20},{14,22},{16,8},... | collective-permute-start | bytes 442376 | tf_op jit(solution)/shard_map/ppermute | solution.py:18
  167.5 8.2 %collective-permute-start.21 = (bf16[192,384]{1,0:T(8,128)(2,1)}, bf16[192,384]{1,0:T(8,128)(2,1)S(1)}, u32[]{:S(2)}, u32[]{:S(2)}) collective-permute-start(bf16[192,384]{1,0:T(8,128)(2,1)} %get-tuple-element.101), channel_id=1, source_target_pairs={{0,2},{2,0},{4,6},{6,4},{8,10},{10,8},{12,14},{14,12},{16,18},{18,... | collective-permute-start | bytes 442376 | tf_op jit(solution)/shard_map/ppermute | solution.py:18
  167.5 8.1 %collective-permute-start.22 = (bf16[192,384]{1,0:T(8,128)(2,1)}, bf16[192,384]{1,0:T(8,128)(2,1)S(1)}, u32[]{:S(2)}, u32[]{:S(2)}) collective-permute-start(bf16[192,384]{1,0:T(8,128)(2,1)} %get-tuple-element.102), channel_id=1, source_target_pairs={{0,10},{2,8},{4,14},{6,12},{8,2},{10,0},{12,6},{14,4},{16,26},{18,... | collective-permute-start | bytes 442376 | tf_op jit(solution)/shard_map/ppermute | solution.py:18
  168.7 3.1 %copy-start.11 = (bf16[192,384]{1,0:T(8,128)(2,1)}, bf16[192,384]{1,0:T(8,128)(2,1)S(1)}, u32[]{:S(2)}) copy-start(bf16[192,384]{1,0:T(8,128)(2,1)S(1)} %collective-permute-done.25.refs_1_) | copy-start | bytes 442372
  168.7 13.3 %collective-permute-start.23 = (bf16[192,384]{1,0:T(8,128)(2,1)}, bf16[192,384]{1,0:T(8,128)(2,1)S(1)}, u32[]{:S(2)}, u32[]{:S(2)}) collective-permute-start(bf16[192,384]{1,0:T(8,128)(2,1)} %get-tuple-element.103), channel_id=1, source_target_pairs={{0,18},{2,16},{4,22},{6,20},{8,26},{10,24},{12,30},{14,28},{16,2},... | collective-permute-start | bytes 442376 | tf_op jit(solution)/shard_map/ppermute | solution.py:18
  169.3 2.4 %copy-start.12 = (bf16[192,384]{1,0:T(8,128)(2,1)}, bf16[192,384]{1,0:T(8,128)(2,1)S(1)}, u32[]{:S(2)}) copy-start(bf16[192,384]{1,0:T(8,128)(2,1)S(1)} %collective-permute-done.26.refs_2_) | copy-start | bytes 442372
  169.3 12.7 %collective-permute-start.24 = (bf16[192,384]{1,0:T(8,128)(2,1)}, bf16[192,384]{1,0:T(8,128)(2,1)S(1)}, u32[]{:S(2)}, u32[]{:S(2)}) collective-permute-start(bf16[192,384]{1,0:T(8,128)(2,1)} %get-tuple-element.104), channel_id=1, source_target_pairs={{0,26},{2,24},{4,30},{6,28},{8,18},{10,16},{12,22},{14,20},{16,10}... | collective-permute-start | bytes 442376 | tf_op jit(solution)/shard_map/ppermute | solution.py:18
  175.7 6.4 %copy-start.7 = (bf16[192,384]{1,0:T(8,128)(2,1)}, bf16[192,384]{1,0:T(8,128)(2,1)S(1)}, u32[]{:S(2)}) copy-start(bf16[192,384]{1,0:T(8,128)(2,1)S(1)} %collective-permute-done.21.refs_0_) | copy-start | bytes 442372
  175.7 6.4 %copy-start.8 = (bf16[192,384]{1,0:T(8,128)(2,1)}, bf16[192,384]{1,0:T(8,128)(2,1)S(1)}, u32[]{:S(2)}) copy-start(bf16[192,384]{1,0:T(8,128)(2,1)S(1)} %collective-permute-done.22.refs_1_) | copy-start | bytes 442372
  (13 other events, 10.6 us)

commit v8 on v7

--- a/solution.py
+++ b/solution.py
@@ -111,16 +111,17 @@
     width = weights[0].shape[1] // ways
     chunks = len(chosen)
     top = away[0]
+    stride = away[1] - top if len(away) > 1 else 0
 
     def weight_map(share, i, place):
-        return (place[0] ^ (share + 1), place[1] ^ (top - i))
+        return (place[0] ^ (share + 1), place[1] ^ (top + stride * i))
 
     in_specs = [pl.BlockSpec((rows, feats), lambda i, place: (0, 0))] * (shares * chunks)
     for _ in weights:
         for share in range(shares):
             in_specs.append(pl.BlockSpec((feats, width), functools.partial(weight_map, share)))
     in_specs += [
-        pl.BlockSpec((chunks, rows, width), lambda i, place: (chosen[0] // chunks, 0, place[1] ^ (top - i)))
+        pl.BlockSpec((chunks, rows, width), lambda i, place: (chosen[0] // chunks, 0, place[1] ^ (top + stride * i)))
     ] * len(weights)
     columns = width * len(weights)
     scratch = [pltpu.VMEM((chunks * rows, feats), jnp.bfloat16)] * (shares if chunks > 1 else 0)
@@ -183,64 +184,75 @@
         for part, span in ((0, low), (1, spans - 1 - low)):
             asked[part, here] = query_refs[a][part * half : (part + 1) * half]
             position[part, here] = from_lane + span * half
-    highest[...] = jnp.full_like(highest, HIDDEN)
-    sums[...] = jnp.zeros_like(sums)
-    total[...] = jnp.zeros_like(total)
     for copy in copies:
         copy.wait()
 
     slope = LOG2_E / math.sqrt(HD)
     middle = spans * half // 2
 
-    def visible(part, h, column):
-        piece = scores[h, :, column : column + 128]
-        if column < middle * part:
+    def starts(part):
+        return range(0, middle * (part + 1), tile)
+
+    def visible(unit, slot, column):
+        piece = scores[slot, :, column : column + 128]
+        if column < middle * unit[0]:
             return piece
-        return jnp.where(position[part] >= column, piece, HIDDEN)
-
-    for part in range(2):
-        starts = range(0, middle * (part + 1), tile)
-        for start in starts:
-            for h in range(heads):
-                scores[h, :, start : start + tile] = lax.dot_general(
-                    asked[part, :, h * HD : (h + 1) * HD],
-                    ordered[start : start + tile, h * HD : (h + 1) * HD],
-                    (((1,), (1,)), ((), ())),
-                    preferred_element_type=jnp.float32,
-                )
-                top = highest[h]
-                for column in range(start, start + tile, 128):
-                    top = jnp.maximum(top, visible(part, h, column))
-                highest[h] = top
-        for h in range(heads):
-            highest[h] = jnp.broadcast_to(
-                jnp.max(highest[h], axis=1, keepdims=True), highest.shape[1:]
-            )
-        for start in starts:
-            for h in range(heads):
-                top = highest[h]
-                added = sums[h]
-                weights = []
-                for column in range(start, start + tile, 128):
-                    piece = jnp.exp2((visible(part, h, column) - top) * slope)
-                    added = added + piece
-                    weights.append(piece.astype(jnp.bfloat16))
-                sums[h] = added
-                total[h] += jnp.dot(
-                    jnp.concatenate(weights, axis=1),
-                    ordered[start : start + tile, width + h * HD : width + (h + 1) * HD],
-                    preferred_element_type=jnp.float32,
-                )
-        for h in range(heads):
-            result = total[h] / jnp.sum(sums[h], axis=1, keepdims=True)
+        return jnp.where(position[unit[0]] >= column, piece, HIDDEN)
+
+    def score_tile(unit, slot, start):
+        part, h = unit
+        scores[slot, :, start : start + tile] = lax.dot_general(
+            asked[part, :, h * HD : (h + 1) * HD],
+            ordered[start : start + tile, h * HD : (h + 1) * HD],
+            (((1,), (1,)), ((), ())),
+            preferred_element_type=jnp.float32,
+        )
+        top = None if start == 0 else highest[slot]
+        for column in range(start, start + tile, 128):
+            piece = visible(unit, slot, column)
+            top = piece if top is None else jnp.maximum(top, piece)
+        highest[slot] = top
+
+    def value_tile(unit, slot, start):
+        part, h = unit
+        top = highest[slot]
+        added = None if start == 0 else sums[slot]
+        weights = []
+        for column in range(start, start + tile, 128):
+            piece = jnp.exp2((visible(unit, slot, column) - top) * slope)
+            added = piece if added is None else added + piece
+            weights.append(piece.astype(jnp.bfloat16))
+        sums[slot] = added
+        product = jnp.dot(
+            jnp.concatenate(weights, axis=1),
+            ordered[start : start + tile, width + h * HD : width + (h + 1) * HD],
+            preferred_element_type=jnp.float32,
+        )
+        if start == 0:
+            total[slot] = product
+        else:
+            total[slot] += product
+
+    units = [(0, 0)] + [(1, h) for h in range(heads)] + [(0, h) for h in range(1, heads)]
+    for n in range(len(units) + 1):
+        todo = []
+        if n < len(units):
+            todo.append([functools.partial(score_tile, units[n], n % 2, start) for start in starts(units[n][0])])
+        if n > 0:
+            slot = (n - 1) % 2
+            highest[slot] = jnp.broadcast_to(jnp.max(highest[slot], axis=1, keepdims=True), highest.shape[1:])
+            todo.append([functools.partial(value_tile, units[n - 1], slot, start) for start in starts(units[n - 1][0])])
+        for index in range(max(len(steps) for steps in todo)):
+            for steps in todo:
+                if index < len(steps):
+                    steps[index]()
+        if n > 0:
+            part, h = units[n - 1]
+            result = total[slot] / jnp.sum(sums[slot], axis=1, keepdims=True)
             for a in range(ways):
                 out_refs[a][part * half : (part + 1) * half, h * HD : (h + 1) * HD] = result[
                     a * half : (a + 1) * half
                 ].astype(jnp.bfloat16)
-        if part == 0:
-            highest[...] = jnp.full_like(highest, HIDDEN)
-            sums[...] = jnp.zeros_like(sums)
-            total[...] = jnp.zeros_like(total)
 
 
 def attend(block, queries, blocks, table):
@@ -272,10 +284,10 @@
         scratch_shapes=[
             pltpu.VMEM((length, 2 * width), jnp.bfloat16),
             pltpu.VMEM((2, many, width), jnp.bfloat16),
-            pltpu.VMEM((heads, many, length), jnp.float32),
-            pltpu.VMEM((heads, many, 128), jnp.float32),
-            pltpu.VMEM((heads, many, 128), jnp.float32),
-            pltpu.VMEM((heads, many, HD), jnp.float32),
+            pltpu.VMEM((2, many, length), jnp.float32),
+            pltpu.VMEM((2, many, 128), jnp.float32),
+            pltpu.VMEM((2, many, 128), jnp.float32),
+            pltpu.VMEM((2, many, HD), jnp.float32),
             pltpu.VMEM((2, many, 128), jnp.int32),
             pltpu.SemaphoreType.DMA((2 * count,)),
         ],
@@ -309,28 +321,6 @@
         out_specs=pl.BlockSpec(memory_space=pltpu.SMEM),
         compiler_params=pltpu.CompilerParams(vmem_limit_bytes=VMEM_LIMIT),
     )(*[blocks[i][0] for i in offsets])
-
-
-def pack_body(*refs):
-    for n, ref in enumerate(refs[:-1]):
-
-        @pl.when(pl.program_id(0) == n)
-        def _():
-            refs[-1][...] = ref[...]
-
-
-def pack(pieces):
-    if len(pieces) == 1:
-        return pieces[0]
-    rows, columns = pieces[0].shape
-    return pl.pallas_call(
-        pack_body,
-        out_shape=jax.ShapeDtypeStruct((len(pieces) * rows, columns), jnp.bfloat16),
-        grid=(len(pieces),),
-        in_specs=[pl.BlockSpec((rows, columns), lambda i: (0, 0))] * len(pieces),
-        out_specs=pl.BlockSpec((rows, columns), lambda i: (i, 0)),
-        compiler_params=pltpu.CompilerParams(vmem_limit_bytes=VMEM_LIMIT),
-    )(*pieces)
 
 
 def assemble_body(ways, place, *refs):
@@ -396,53 +386,44 @@
     spans = event_pos[:, 0] // (rows // 2)
     span_other = over_ctx(lax.dynamic_index_in_dim(spans, 1 - core, 0), 1)
     later = jnp.concatenate([place, lax.dynamic_index_in_dim(spans, core, 0), span_other])
-    made_0 = {}
-    for part in (away[: ways // 2], away[ways // 2 :]):
-        if part:
-            made_0.update(
-                rest_products(received, [0], [w_k, w_v], [start_k, start_v], later, ways, part, EXTRA)[0]
-            )
+    (made_0,) = rest_products(received, [0], [w_k, w_v], [start_k, start_v], later, ways, away, EXTRA)
     first = {a: over_ctx(made_0[a], a * rest) for a in away}
+    ahead = over_ctx(made_0[0], rest // 2)
+    asked = rest_products(received, [0], [w_q], [start_q], place, ways, away)
+    received, asked = lax.optimization_barrier((received, asked))
     (made_1,) = rest_products(received, [1], [w_k, w_v], [start_k, start_v], place, ways, away)
     ahead_1 = over_ctx(made_1[0], rest // 2)
+    received, made_1 = lax.optimization_barrier((received, made_1))
+    asked += rest_products(received, [1], [w_q], [start_q], place, ways, away)
     for a in away:
-        first[a], made_1[a] = lax.optimization_barrier((first[a], made_1[a]))
-    packed = pack([first[a] for a in range(ways)])
-    received, packed, made_1[0] = lax.optimization_barrier((received, packed, made_1[0]))
-    asked = rest_products(received, [0, 1], [w_q], [start_q], place, ways, away)
-
-    whole = {0: packed}
-    bit = rest // 2
-    while bit > 1:
-        for i in list(whole):
-            whole[i ^ bit] = over_ctx(whole[i], bit)
-        bit //= 2
-    blocks = {}
-    for i, array in whole.items():
-        for a in range(ways):
-            blocks[i ^ (a * rest)] = (array, a * (rows + EXTRA))
-    table = span_table(blocks, rows)
+        first[a], asked[1][a] = lax.optimization_barrier((first[a], asked[1][a]))
 
     second = {}
     queries = [{}, {}]
     for a in away:
-        last = first[a]
+        last = (first[a], ahead)
         for made, keep, key in ((made_1, second, a * rest + 1), (asked[0], queries[0], a), (asked[1], queries[1], a)):
             value, last = lax.optimization_barrier((made[a], last))
             last = keep[key] = over_ctx(value, a * rest)
             if keep is second and a:
                 last = (last, ahead_1)
-    freed = whole[rest // 2]
-    for a in away[:-1]:
-        second[a * rest + 1], freed = lax.optimization_barrier((second[a * rest + 1], freed))
+
+    def over_y(blocks):
+        bit = rest // 2
+        while bit > 1:
+            for i in list(blocks):
+                if i ^ bit not in blocks:
+                    blocks[i ^ bit] = over_ctx(blocks[i], bit)
+            bit //= 2
+        return blocks
+
+    blocks = {a * rest: first[a] for a in away}
+    blocks[rest // 2] = ahead
+    blocks = over_y(blocks)
+    table = span_table({i: (array, 0) for i, array in blocks.items()}, rows)
     second[rest // 2 + 1] = ahead_1
-    bit = rest // 2
-    while bit > 1:
-        for i in list(second):
-            if i ^ bit not in second:
-                second[i ^ bit] = over_ctx(second[i], bit)
-        bit //= 2
-    blocks.update({i: (array, 0) for i, array in second.items()})
+    blocks.update(over_y(second))
+    blocks = {i: (array, 0) for i, array in blocks.items()}
     out = None
     for b in range(2):
         outs = attend(b, [queries[b][a] for a in range(ways)], blocks, table)

time: 188 us -> 177 us (0.941)
  waiting for transfers between devices: 37.7 us -> 31.1 us
  Pallas kernels: 92.8 us -> 88.6 us
    ppermute x28 -> x31, waiting for transfers between devices: 37.7 us -> 31.1 us  [exchange(): return lax.ppermute(value, axis, [(i, i ^ bit) for i in range(size)])]
    pallas_call x2, Pallas kernels: 28 us -> 24.9 us  [attend(): pl.pallas_call(functools.partial(attend_body, block, ways, slots, len(arr...]
    pallas_call x1 -> x0, Pallas kernels: 2.88 us -> none  [pack(): pl.pallas_call(pack_body, out_shape=jax.ShapeDtypeStruct((len(pieces) * r...]
    unnamed x66 -> x82, local copies, waits for them, and re-layouts: 7.31 us -> 7 us
    ppermute x28 -> x31, starting transfers between devices: 42.9 us -> 42.7 us  [exchange(): return lax.ppermute(value, axis, [(i, i ^ bit) for i in range(size)])]
  transfers between devices with their start and end apart: 28 -> 31, of which waited for: 9 -> 6; matrix products, arithmetic and copies ran while one was open for 2% -> 2% of each run, Pallas kernels for 46% -> 49%
where the time goes in v8:
time: 177 us; the launch traced here: 176 us
  Pallas kernels  88.6 us (50%)
  starting transfers between devices  42.7 us (24%)
  waiting for transfers between devices  31.1 us (18%)
  local copies, waits for them, and re-layouts  12.1 us (7%)
    ppermute x31, starting transfers between devices, exchange(): return lax.ppermute(value, axis, [(i, i ^ bit) for i in range(size)])  42.7 us
    pallas_call x4, Pallas kernels, rest_products(): pl.pallas_call(functools.partial(rest_body, shares, len(weights), chunks,...  37.3 us
    ppermute x31, waiting for transfers between devices, exchange(): return lax.ppermute(value, axis, [(i, i ^ bit) for i in range(size)])  31.1 us
    pallas_call x2, Pallas kernels, attend(): pl.pallas_call(functools.partial(attend_body, block, ways, slots, len(arr...  24.9 us
    pallas_call x1, Pallas kernels, own_products(): pl.pallas_call(functools.partial(own_body, len(weights)), out_shape=[jax....  18.6 us
    unnamed x82, local copies, waits for them, and re-layouts  7 us
    pallas_call x2, Pallas kernels, assemble(): pl.pallas_call(functools.partial(assemble_body, ways), out_shape=jax.Shap...  6.49 us
  transfers between devices with their start and end apart: 31, of which 6 were waited for; matrix products, arithmetic and copies ran while one was open for 2% of the time, Pallas kernels for 49%

profile of v8, /device:TPU:0, one launch (start us, length us, event | category | flops | bytes accessed | tf_op | source)
XLA Modules:
  0.0 175.9 jit_solution(14992634928242732471)
XLA Ops:
  0.0 2.6 %dynamic-slice_bitcast_fusion = (bf16[192,2560]{1,0:T(8,128)(2,1)}, bf16[192,2560]{1,0:T(8,128)(2,1)S(1)}) fusion(bf16[2,192,2560]{2,1,0:T(8,128)(2,1)} %mine_ref.1, s32[]{:T(128)S(6)} %select_n.30, s32[]{:T(128)S(6)} %select_n.29), kind=kLoop, calls=%fused_computation | loop fusion | bytes 3932168 | tf_op jit(solution)/shard_map/jit(dynamic_index_in_dim)/squeeze | solution.py:381
  3.0 2.5 %collective-permute-start.1 = (bf16[192,2560]{1,0:T(8,128)(2,1)S(1)}, bf16[192,2560]{1,0:T(8,128)(2,1)S(1)}, u32[]{:S(2)}, u32[]{:S(2)}) collective-permute-start(bf16[192,2560]{1,0:T(8,128)(2,1)S(1)} %get-tuple-element.120), channel_id=1, source_target_pairs={{0,1},{1,0},{2,3},{3,2},{4,5},{5,4},{6,7},{7,6},{8,9},{9,8},{10,11... | collective-permute-start | bytes 2949128 | tf_op jit(solution)/shard_map/ppermute | solution.py:18
  5.8 0.6 fusion
  6.7 0.7 pad_add_fusion.place
  7.3 0.6 collective-permute-done
  7.9 1.8 %concatenate.4.place = s32[6]{0:T(128)} concatenate(s32[1]{0:T(128)} %bitcast, s32[1]{0:T(128)} %bitcast.1, s32[1]{0:T(128)} %bitcast.2, s32[1]{0:T(128)} %bitcast.3, s32[1]{0:T(128)} %get-tuple-element.122, s32[1]{0:T(128)} %collective-permute-done), dimensions={0} | concatenate | bytes 48 | tf_op jit(solution)/shard_map/concatenate | solution.py:388
  10.7 18.6 %shard_map.55 = (f32[2,192,1536]{2,1,0:T(8,128)}, f32[2,192,1536]{2,1,0:T(8,128)}, f32[2,192,1536]{2,1,0:T(8,128)}) custom-call(s32[4]{0:T(128)} %pad_add_fusion.place, bf16[2,192,2560]{2,1,0:T(8,128)(2,1)} %mine_ref.1, bf16[192,2560]{1,0:T(8,128)(2,1)} %copy-done.2, bf16[5120,1536]{1,0:T(8,128)(2,1)} %refs_1_.8, bf16[5120,1536]{1,0:T(8,128)(2,1)} %refs_2_.5, ...), custom_call_target="tpu_custom_call" | custom-call | flops 9059696640 | bytes 23592960 | tf_op jit(solution)/shard_map/pallas_call | solution.py:42
  29.2 0.9 copy-done
  30.2 11.3 %shard_map.56 = (bf16[208,768]{1,0:T(8,128)(2,1)}, bf16[208,768]{1,0:T(8,128)(2,1)}, bf16[208,768]{1,0:T(8,128)(2,1)}, bf16[208,768]{1,0:T(8,128)(2,1)}) custom-call(s32[6]{0:T(128)} %concatenate.4.place, bf16[192,2560]{1,0:T(8,128)(2,1)} %copy-done, bf16[5120,1536]{1,0:T(8,128)(2,1)} %refs_1_.8, bf16[5120,1536]{1,0:T(8,128)(2,1)} %refs_2_.5, ...), custom_call_target="tpu_custom_call" | custom-call | flops 3019898880 | bytes 15728640 | tf_op jit(solution)/shard_map/pallas_call | solution.py:128
  41.5 1.5 collective-permute-start.4
  43.1 1.6 collective-permute-start.5
  44.6 2.7 %collective-permute-start.7 = (bf16[208,768]{1,0:T(8,128)(2,1)}, bf16[208,768]{1,0:T(8,128)(2,1)S(1)}, u32[]{:S(2)}, u32[]{:S(2)}) collective-permute-start(bf16[208,768]{1,0:T(8,128)(2,1)} %get-tuple-element.81), channel_id=1, source_target_pairs={{0,16},{2,18},{4,20},{6,22},{8,24},{10,26},{12,28},{14,30},{16,0},... | collective-permute-start | bytes 958472 | tf_op jit(solution)/shard_map/ppermute | solution.py:18
  47.4 7.3 %shard_map.57 = (bf16[192,384]{1,0:T(8,128)(2,1)}, bf16[192,384]{1,0:T(8,128)(2,1)}, bf16[192,384]{1,0:T(8,128)(2,1)}, bf16[192,384]{1,0:T(8,128)(2,1)}) custom-call(s32[4]{0:T(128)} %pad_add_fusion.place, bf16[192,2560]{1,0:T(8,128)(2,1)} %copy-done, bf16[5120,1536]{1,0:T(8,128)(2,1)} %refs_1_.9, f32[2,192,1536]{2,1,0:T(8,128)} %get-tuple-element.65.refs_2_), custom_call_target="tpu_custom_call" | custom-call | flops 1509949440 | bytes 7864320 | tf_op jit(solution)/shard_map/pallas_call | solution.py:128
  54.7 0.9 copy-done.1
  55.7 11.2 %shard_map.58 = (bf16[192,768]{1,0:T(8,128)(2,1)}, bf16[192,768]{1,0:T(8,128)(2,1)}, bf16[192,768]{1,0:T(8,128)(2,1)}, bf16[192,768]{1,0:T(8,128)(2,1)}) custom-call(s32[4]{0:T(128)} %pad_add_fusion.place, bf16[192,2560]{1,0:T(8,128)(2,1)} %copy-done.1, bf16[5120,1536]{1,0:T(8,128)(2,1)} %refs_1_.8, bf16[5120,1536]{1,0:T(8,128)(2,1)} %refs_2_.5, ...), custom_call_target="tpu_custom_call" | custom-call | flops 3019898880 | bytes 15728640 | tf_op jit(solution)/shard_map/pallas_call | solution.py:128
  66.9 7.4 %shard_map.59 = (bf16[192,384]{1,0:T(8,128)(2,1)}, bf16[192,384]{1,0:T(8,128)(2,1)}, bf16[192,384]{1,0:T(8,128)(2,1)}, bf16[192,384]{1,0:T(8,128)(2,1)}) custom-call(s32[4]{0:T(128)} %pad_add_fusion.place, bf16[192,2560]{1,0:T(8,128)(2,1)} %copy-done.1, bf16[5120,1536]{1,0:T(8,128)(2,1)} %refs_1_.9, f32[2,192,1536]{2,1,0:T(8,128)} %get-tuple-element.65.refs_2_), custom_call_target="tpu_custom_call" | custom-call | flops 1509949440 | bytes 7864320 | tf_op jit(solution)/shard_map/pallas_call | solution.py:128
  74.5 0.7 collective-permute-start.11
  75.7 1.5 collective-permute-start.6
  77.2 0.5 collective-permute-start.8
  77.7 3.7 %collective-permute-start.15 = (bf16[192,768]{1,0:T(8,128)(2,1)S(1)}, bf16[192,768]{1,0:T(8,128)(2,1)S(1)}, u32[]{:S(2)}, u32[]{:S(2)}) collective-permute-start(bf16[192,768]{1,0:T(8,128)(2,1)S(1)} %copy-done.26), channel_id=1, source_target_pairs={{0,16},{2,18},{4,20},{6,22},{8,24},{10,26},{12,28},{14,30},{16,0},... | collective-permute-start | bytes 884744 | tf_op jit(solution)/shard_map/ppermute | solution.py:18
  81.5 5.4 %collective-permute-done.11.refs_9_ = bf16[192,768]{1,0:T(8,128)(2,1)S(1)} collective-permute-done((bf16[192,768]{1,0:T(8,128)(2,1)S(1)}, bf16[192,768]{1,0:T(8,128)(2,1)S(1)}, u32[]{:S(2)}, u32[]{:S(2)}) %collective-permute-start.11) | collective-permute-done | bytes 294944 | tf_op jit(solution)/shard_map/ppermute | solution.py:18
  86.9 1.8 %collective-permute-start.18 = (bf16[192,768]{1,0:T(8,128)(2,1)S(1)}, bf16[192,768]{1,0:T(8,128)(2,1)S(1)}, u32[]{:S(2)}, u32[]{:S(2)}) collective-permute-start(bf16[192,768]{1,0:T(8,128)(2,1)S(1)} %copy-done.25), channel_id=1, source_target_pairs={{0,24},{2,26},{4,28},{6,30},{8,16},{10,18},{12,20},{14,22},{16,8},... | collective-permute-start | bytes 884744 | tf_op jit(solution)/shard_map/ppermute | solution.py:18
  88.7 12.9 %collective-permute-done.15.refs_13_ = bf16[192,768]{1,0:T(8,128)(2,1)S(1)} collective-permute-done((bf16[192,768]{1,0:T(8,128)(2,1)S(1)}, bf16[192,768]{1,0:T(8,128)(2,1)S(1)}, u32[]{:S(2)}, u32[]{:S(2)}) %collective-permute-start.15) | collective-permute-done | bytes 294944 | tf_op jit(solution)/shard_map/ppermute | solution.py:18
  101.7 1.5 collective-permute-start.21
  103.1 0.6 collective-permute-start.22
  103.8 1.4 collective-permute-start.23
  105.7 5.2 %collective-permute-start.16 = (bf16[192,384]{1,0:T(8,128)(2,1)S(1)}, bf16[192,384]{1,0:T(8,128)(2,1)S(1)}, u32[]{:S(2)}, u32[]{:S(2)}) collective-permute-start(bf16[192,384]{1,0:T(8,128)(2,1)S(1)} %copy-done.32), channel_id=1, source_target_pairs={{0,16},{2,18},{4,20},{6,22},{8,24},{10,26},{12,28},{14,30},{16,0},... | collective-permute-start | bytes 442376 | tf_op jit(solution)/shard_map/ppermute | solution.py:18
  110.8 1.4 collective-permute-start.19
  112.3 1.4 shard_map.60.table
  113.7 6.6 %collective-permute-done.16.refs_2_ = bf16[192,384]{1,0:T(8,128)(2,1)S(1)} collective-permute-done((bf16[192,384]{1,0:T(8,128)(2,1)S(1)}, bf16[192,384]{1,0:T(8,128)(2,1)S(1)}, u32[]{:S(2)}, u32[]{:S(2)}) %collective-permute-start.16) | collective-permute-done | bytes 147488 | tf_op jit(solution)/shard_map/ppermute | solution.py:18
  120.4 2.1 %collective-permute-start.17 = (bf16[192,384]{1,0:T(8,128)(2,1)S(1)}, bf16[192,384]{1,0:T(8,128)(2,1)S(1)}, u32[]{:S(2)}, u32[]{:S(2)}) collective-permute-start(bf16[192,384]{1,0:T(8,128)(2,1)S(1)} %copy-done.29), channel_id=1, source_target_pairs={{0,16},{2,18},{4,20},{6,22},{8,24},{10,26},{12,28},{14,30},{16,0},... | collective-permute-start | bytes 442376 | tf_op jit(solution)/shard_map/ppermute | solution.py:18
  122.5 3.4 %collective-permute-start.20 = (bf16[192,384]{1,0:T(8,128)(2,1)S(1)}, bf16[192,384]{1,0:T(8,128)(2,1)S(1)}, u32[]{:S(2)}, u32[]{:S(2)}) collective-permute-start(bf16[192,384]{1,0:T(8,128)(2,1)S(1)} %copy-done.28), channel_id=1, source_target_pairs={{0,24},{2,26},{4,28},{6,30},{8,16},{10,18},{12,20},{14,22},{16,8},... | collective-permute-start | bytes 442376 | tf_op jit(solution)/shard_map/ppermute | solution.py:18
  126.0 0.6 copy-done.23
  126.6 0.7 copy-done.24
  127.3 12.3 %shard_map.62 = (bf16[192,384]{1,0:T(8,128)(2,1)}, bf16[192,384]{1,0:T(8,128)(2,1)}, bf16[192,384]{1,0:T(8,128)(2,1)}, bf16[192,384]{1,0:T(8,128)(2,1)}) custom-call(s32[16]{0:T(128)} %shard_map.60.table, bf16[192,384]{1,0:T(8,128)(2,1)} %get-tuple-element.91.refs_0_, bf16[192,384]{1,0:T(8,128)(2,1)} %copy-done.35, bf16[192,384]{1,0:T(8,128)(2,1)} %copy-done.38, ...), custom_call_target="tpu_custom_call" | custom-call | flops 2717908992 | bytes 5898240 | tf_op jit(solution)/shard_map/pallas_call | solution.py:276
  139.7 1.0 collective-permute-start.29
  140.7 3.4 %collective-permute-start.30 = (bf16[192,384]{1,0:T(8,128)(2,1)}, bf16[192,384]{1,0:T(8,128)(2,1)S(1)}, u32[]{:S(2)}, u32[]{:S(2)}) collective-permute-start(bf16[192,384]{1,0:T(8,128)(2,1)} %get-tuple-element.118), channel_id=1, source_target_pairs={{0,24},{2,26},{4,28},{6,30},{8,16},{10,18},{12,20},{14,22},{16,8},... | collective-permute-start | bytes 442376 | tf_op jit(solution)/shard_map/ppermute | solution.py:18
  144.1 0.6 copy-done.36
  144.8 0.7 copy-done.37
  145.4 12.6 %shard_map.61 = (bf16[192,384]{1,0:T(8,128)(2,1)}, bf16[192,384]{1,0:T(8,128)(2,1)}, bf16[192,384]{1,0:T(8,128)(2,1)}, bf16[192,384]{1,0:T(8,128)(2,1)}) custom-call(s32[16]{0:T(128)} %shard_map.60.table, bf16[192,384]{1,0:T(8,128)(2,1)} %get-tuple-element.92.refs_0_, bf16[192,384]{1,0:T(8,128)(2,1)} %copy-done.34, bf16[192,384]{1,0:T(8,128)(2,1)} %copy-done.36, ...), custom_call_target="tpu_custom_call" | custom-call | flops 2717908992 | bytes 5898240 | tf_op jit(solution)/shard_map/pallas_call | solution.py:276
  158.2 0.7 collective-permute-start.26
  158.9 3.4 %collective-permute-start.27 = (bf16[192,384]{1,0:T(8,128)(2,1)}, bf16[192,384]{1,0:T(8,128)(2,1)S(1)}, u32[]{:S(2)}, u32[]{:S(2)}) collective-permute-start(bf16[192,384]{1,0:T(8,128)(2,1)} %get-tuple-element.114), channel_id=1, source_target_pairs={{0,26},{2,24},{4,30},{6,28},{8,18},{10,16},{12,22},{14,20},{16,10}... | collective-permute-start | bytes 442376 | tf_op jit(solution)/shard_map/ppermute | solution.py:18
  162.3 0.6 copy-done.16
  163.0 3.2 %shard_map.63.refs_4_ = bf16[2,192,1536]{2,1,0:T(8,128)(2,1)} custom-call(s32[4]{0:T(128)} %pad_add_fusion.place, bf16[192,384]{1,0:T(8,128)(2,1)} %get-tuple-element.115.refs_0_, bf16[192,384]{1,0:T(8,128)(2,1)} %copy-done.14, bf16[192,384]{1,0:T(8,128)(2,1)} %copy-done.15, bf16[192,384]{1,0:T(8,128)(2,1)} %copy-done.16), custom_call_target="tpu_custom_call" | custom-call | tf_op jit(solution)/shard_map/pallas_call | solution.py:344
  166.3 5.1 %collective-permute-done.26.refs_2_ = bf16[192,384]{1,0:T(8,128)(2,1)S(1)} collective-permute-done((bf16[192,384]{1,0:T(8,128)(2,1)}, bf16[192,384]{1,0:T(8,128)(2,1)S(1)}, u32[]{:S(2)}, u32[]{:S(2)}) %collective-permute-start.26) | collective-permute-done | bytes 147488 | tf_op jit(solution)/shard_map/ppermute | solution.py:18
  171.3 0.6 copy-done.12
  172.0 0.7 copy-done.13
  172.6 3.2 %shard_map.64 = bf16[2,192,1536]{2,1,0:T(8,128)(2,1)} custom-call(s32[4]{0:T(128)} %pad_add_fusion.place, bf16[192,384]{1,0:T(8,128)(2,1)} %copy-done.10, bf16[192,384]{1,0:T(8,128)(2,1)} %copy-done.11, bf16[192,384]{1,0:T(8,128)(2,1)} %copy-done.12, bf16[192,384]{1,0:T(8,128)(2,1)} %copy-done.13, ...), custom_call_target="tpu_custom_call", output_to_operand_aliasing={{}: (5, {})} | custom-call | tf_op jit(solution)/shard_map/pallas_call | solution.py:344
  (113 shorter events, 3.4 us)
Async XLA Ops:
  2.6 7.1 %collective-permute-start.2 = (bf16[192,2560]{1,0:T(8,128)(2,1)}, bf16[192,2560]{1,0:T(8,128)(2,1)S(1)}, u32[]{:S(2)}, u32[]{:S(2)}) collective-permute-start(bf16[192,2560]{1,0:T(8,128)(2,1)} %get-tuple-element.119), channel_id=1, source_target_pairs={{0,2},{2,0},{4,6},{6,4},{8,10},{10,8},{12,14},{14,12},{16,18},{18,... | collective-permute-start | bytes 2949128 | tf_op jit(solution)/shard_map/ppermute | solution.py:18
  3.0 26.2 %collective-permute-start.1 = (bf16[192,2560]{1,0:T(8,128)(2,1)S(1)}, bf16[192,2560]{1,0:T(8,128)(2,1)S(1)}, u32[]{:S(2)}, u32[]{:S(2)}) collective-permute-start(bf16[192,2560]{1,0:T(8,128)(2,1)S(1)} %get-tuple-element.120), channel_id=1, source_target_pairs={{0,1},{1,0},{2,3},{3,2},{4,5},{5,4},{6,7},{7,6},{8,9},{9,8},{10,11... | collective-permute-start | bytes 2949128 | tf_op jit(solution)/shard_map/ppermute | solution.py:18
  6.4 1.5 collective-permute-start
  9.7 45.0 %collective-permute-start.3 = (bf16[192,2560]{1,0:T(8,128)(2,1)S(1)}, bf16[192,2560]{1,0:T(8,128)(2,1)S(1)}, u32[]{:S(2)}, u32[]{:S(2)}) collective-permute-start(bf16[192,2560]{1,0:T(8,128)(2,1)S(1)} %collective-permute-done.2.other_ref), channel_id=1, source_target_pairs={{0,1},{1,0},{2,3},{3,2},{4,5},{5,4},{6,7},{7,6},{8,9},{9,8},{10,11... | collective-permute-start | bytes 2949128 | tf_op jit(solution)/shard_map/ppermute | solution.py:18
  41.5 32.9 %collective-permute-start.4 = (bf16[208,768]{1,0:T(8,128)(2,1)}, bf16[208,768]{1,0:T(8,128)(2,1)S(1)}, u32[]{:S(2)}, u32[]{:S(2)}) collective-permute-start(bf16[208,768]{1,0:T(8,128)(2,1)} %get-tuple-element.77.refs_0_.refs_4_), channel_id=1, source_target_pairs={{0,4},{2,6},{4,0},{6,2},{8,12},{10,14},{12,8},{14,10},{16,20},{18,... | collective-permute-start | bytes 958472 | tf_op jit(solution)/shard_map/ppermute | solution.py:18
  43.1 31.4 %collective-permute-start.5 = (bf16[208,768]{1,0:T(8,128)(2,1)}, bf16[208,768]{1,0:T(8,128)(2,1)S(1)}, u32[]{:S(2)}, u32[]{:S(2)}) collective-permute-start(bf16[208,768]{1,0:T(8,128)(2,1)} %get-tuple-element.78), channel_id=1, source_target_pairs={{0,8},{2,10},{4,12},{6,14},{8,0},{10,2},{12,4},{14,6},{16,24},{18,... | collective-permute-start | bytes 958472 | tf_op jit(solution)/shard_map/ppermute | solution.py:18
  44.6 32.6 %collective-permute-start.7 = (bf16[208,768]{1,0:T(8,128)(2,1)}, bf16[208,768]{1,0:T(8,128)(2,1)S(1)}, u32[]{:S(2)}, u32[]{:S(2)}) collective-permute-start(bf16[208,768]{1,0:T(8,128)(2,1)} %get-tuple-element.81), channel_id=1, source_target_pairs={{0,16},{2,18},{4,20},{6,22},{8,24},{10,26},{12,28},{14,30},{16,0},... | collective-permute-start | bytes 958472 | tf_op jit(solution)/shard_map/ppermute | solution.py:18
  47.4 30.4 %collective-permute-start.9 = (bf16[208,768]{1,0:T(8,128)(2,1)}, bf16[208,768]{1,0:T(8,128)(2,1)S(1)}, u32[]{:S(2)}, u32[]{:S(2)}) collective-permute-start(bf16[208,768]{1,0:T(8,128)(2,1)} %get-tuple-element.84), channel_id=1, source_target_pairs={{0,24},{2,26},{4,28},{6,30},{8,16},{10,18},{12,20},{14,22},{16,8},... | collective-permute-start | bytes 958472 | tf_op jit(solution)/shard_map/ppermute | solution.py:18
  66.9 10.8 %copy-start.26 = (bf16[192,768]{1,0:T(8,128)(2,1)S(1)}, bf16[192,768]{1,0:T(8,128)(2,1)}, u32[]{:S(2)}) copy-start(bf16[192,768]{1,0:T(8,128)(2,1)} %get-tuple-element.102) | copy-start | bytes 884740
  66.9 20.0 %copy-start.25 = (bf16[192,768]{1,0:T(8,128)(2,1)S(1)}, bf16[192,768]{1,0:T(8,128)(2,1)}, u32[]{:S(2)}) copy-start(bf16[192,768]{1,0:T(8,128)(2,1)} %get-tuple-element.108) | copy-start | bytes 884740
  66.9 34.7 %copy-start.33 = (bf16[192,384]{1,0:T(8,128)(2,1)S(1)}, bf16[192,384]{1,0:T(8,128)(2,1)}, u32[]{:S(2)}) copy-start(bf16[192,384]{1,0:T(8,128)(2,1)} %get-tuple-element.97) | copy-start | bytes 442372
  66.9 38.7 %copy-start.32 = (bf16[192,384]{1,0:T(8,128)(2,1)S(1)}, bf16[192,384]{1,0:T(8,128)(2,1)}, u32[]{:S(2)}) copy-start(bf16[192,384]{1,0:T(8,128)(2,1)} %get-tuple-element.103) | copy-start | bytes 442372
  66.9 43.9 %copy-start.31 = (bf16[192,384]{1,0:T(8,128)(2,1)S(1)}, bf16[192,384]{1,0:T(8,128)(2,1)}, u32[]{:S(2)}) copy-start(bf16[192,384]{1,0:T(8,128)(2,1)} %get-tuple-element.109) | copy-start | bytes 442372
  74.4 45.9 %copy-start.30 = (bf16[192,384]{1,0:T(8,128)(2,1)S(1)}, bf16[192,384]{1,0:T(8,128)(2,1)}, u32[]{:S(2)}) copy-start(bf16[192,384]{1,0:T(8,128)(2,1)} %get-tuple-element.98) | copy-start | bytes 442372
  74.4 46.0 %copy-start.29 = (bf16[192,384]{1,0:T(8,128)(2,1)S(1)}, bf16[192,384]{1,0:T(8,128)(2,1)}, u32[]{:S(2)}) copy-start(bf16[192,384]{1,0:T(8,128)(2,1)} %get-tuple-element.104) | copy-start | bytes 442372
  74.4 48.1 %copy-start.28 = (bf16[192,384]{1,0:T(8,128)(2,1)S(1)}, bf16[192,384]{1,0:T(8,128)(2,1)}, u32[]{:S(2)}) copy-start(bf16[192,384]{1,0:T(8,128)(2,1)} %get-tuple-element.110) | copy-start | bytes 442372
  74.4 37.9 %copy-start.4 = (bf16[208,768]{1,0:T(8,128)(2,1)}, bf16[208,768]{1,0:T(8,128)(2,1)S(1)}, u32[]{:S(2)}) copy-start(bf16[208,768]{1,0:T(8,128)(2,1)S(1)} %collective-permute-done.5.refs_2_.refs_8_) | copy-start | bytes 958468
  74.4 37.8 %copy-start.3 = (bf16[208,768]{1,0:T(8,128)(2,1)}, bf16[208,768]{1,0:T(8,128)(2,1)S(1)}, u32[]{:S(2)}) copy-start(bf16[208,768]{1,0:T(8,128)(2,1)S(1)} %collective-permute-done.4.refs_1_.refs_6_) | copy-start | bytes 958468
  74.5 12.5 %collective-permute-start.11 = (bf16[192,768]{1,0:T(8,128)(2,1)S(1)}, bf16[192,768]{1,0:T(8,128)(2,1)S(1)}, u32[]{:S(2)}, u32[]{:S(2)}) collective-permute-start(bf16[192,768]{1,0:T(8,128)(2,1)S(1)} %copy-done.27), channel_id=1, source_target_pairs={{0,8},{2,10},{4,12},{6,14},{8,0},{10,2},{12,4},{14,6},{16,24},{18,... | collective-permute-start | bytes 884744 | tf_op jit(solution)/shard_map/ppermute | solution.py:18
  75.2 13.6 %collective-permute-start.12 = (bf16[192,768]{1,0:T(8,128)(2,1)S(1)}, bf16[192,768]{1,0:T(8,128)(2,1)S(1)}, u32[]{:S(2)}, u32[]{:S(2)}) collective-permute-start(bf16[192,768]{1,0:T(8,128)(2,1)S(1)} %copy-done.17), channel_id=1, source_target_pairs={{0,4},{2,6},{4,0},{6,2},{8,12},{10,14},{12,8},{14,10},{16,20},{18,... | collective-permute-start | bytes 884744 | tf_op jit(solution)/shard_map/ppermute | solution.py:18
  75.7 27.4 %collective-permute-start.6 = (bf16[208,768]{1,0:T(8,128)(2,1)S(1)}, bf16[208,768]{1,0:T(8,128)(2,1)S(1)}, u32[]{:S(2)}, u32[]{:S(2)}) collective-permute-start(bf16[208,768]{1,0:T(8,128)(2,1)S(1)} %collective-permute-done.5.refs_2_.refs_8_), channel_id=1, source_target_pairs={{0,4},{2,6},{4,0},{6,2},{8,12},{10,14},{12,8},{14,10},{16,20},{18,... | collective-permute-start | bytes 958472 | tf_op jit(solution)/shard_map/ppermute | solution.py:18
  77.2 35.1 %copy-start.5 = (bf16[208,768]{1,0:T(8,128)(2,1)}, bf16[208,768]{1,0:T(8,128)(2,1)S(1)}, u32[]{:S(2)}) copy-start(bf16[208,768]{1,0:T(8,128)(2,1)S(1)} %collective-permute-done.7.refs_4_.refs_12_) | copy-start | bytes 958468
  77.2 26.6 %collective-permute-start.8 = (bf16[208,768]{1,0:T(8,128)(2,1)S(1)}, bf16[208,768]{1,0:T(8,128)(2,1)S(1)}, u32[]{:S(2)}, u32[]{:S(2)}) collective-permute-start(bf16[208,768]{1,0:T(8,128)(2,1)S(1)} %collective-permute-done.7.refs_4_.refs_12_), channel_id=1, source_target_pairs={{0,4},{2,6},{4,0},{6,2},{8,12},{10,14},{12,8},{14,10},{16,20},{18,... | collective-permute-start | bytes 958472 | tf_op jit(solution)/shard_map/ppermute | solution.py:18
  77.7 34.6 %copy-start.6 = (bf16[208,768]{1,0:T(8,128)(2,1)}, bf16[208,768]{1,0:T(8,128)(2,1)S(1)}, u32[]{:S(2)}) copy-start(bf16[208,768]{1,0:T(8,128)(2,1)S(1)} %collective-permute-done.9.refs_6_.refs_16_) | copy-start | bytes 958468
  77.7 23.9 %collective-permute-start.15 = (bf16[192,768]{1,0:T(8,128)(2,1)S(1)}, bf16[192,768]{1,0:T(8,128)(2,1)S(1)}, u32[]{:S(2)}, u32[]{:S(2)}) collective-permute-start(bf16[192,768]{1,0:T(8,128)(2,1)S(1)} %copy-done.26), channel_id=1, source_target_pairs={{0,16},{2,18},{4,20},{6,22},{8,24},{10,26},{12,28},{14,30},{16,0},... | collective-permute-start | bytes 884744 | tf_op jit(solution)/shard_map/ppermute | solution.py:18
  86.9 39.0 %copy-start.18 = (bf16[192,768]{1,0:T(8,128)(2,1)}, bf16[192,768]{1,0:T(8,128)(2,1)S(1)}, u32[]{:S(2)}) copy-start(bf16[192,768]{1,0:T(8,128)(2,1)S(1)} %collective-permute-done.11.refs_9_) | copy-start | bytes 884740
  86.9 14.7 %collective-permute-start.18 = (bf16[192,768]{1,0:T(8,128)(2,1)S(1)}, bf16[192,768]{1,0:T(8,128)(2,1)S(1)}, u32[]{:S(2)}, u32[]{:S(2)}) collective-permute-start(bf16[192,768]{1,0:T(8,128)(2,1)S(1)} %copy-done.25), channel_id=1, source_target_pairs={{0,24},{2,26},{4,28},{6,30},{8,16},{10,18},{12,20},{14,22},{16,8},... | collective-permute-start | bytes 884744 | tf_op jit(solution)/shard_map/ppermute | solution.py:18
  88.7 37.2 %copy-start.19 = (bf16[192,768]{1,0:T(8,128)(2,1)}, bf16[192,768]{1,0:T(8,128)(2,1)S(1)}, u32[]{:S(2)}) copy-start(bf16[192,768]{1,0:T(8,128)(2,1)S(1)} %collective-permute-done.12.refs_7_) | copy-start | bytes 884740
  88.7 16.9 %collective-permute-start.10 = (bf16[208,768]{1,0:T(8,128)(2,1)S(1)}, bf16[208,768]{1,0:T(8,128)(2,1)S(1)}, u32[]{:S(2)}, u32[]{:S(2)}) collective-permute-start(bf16[208,768]{1,0:T(8,128)(2,1)S(1)} %collective-permute-done.9.refs_6_.refs_16_), channel_id=1, source_target_pairs={{0,4},{2,6},{4,0},{6,2},{8,12},{10,14},{12,8},{14,10},{16,20},{18,... | collective-permute-start | bytes 958472 | tf_op jit(solution)/shard_map/ppermute | solution.py:18
  101.6 24.3 %copy-start.20 = (bf16[192,768]{1,0:T(8,128)(2,1)}, bf16[192,768]{1,0:T(8,128)(2,1)S(1)}, u32[]{:S(2)}) copy-start(bf16[192,768]{1,0:T(8,128)(2,1)S(1)} %collective-permute-done.15.refs_13_) | copy-start | bytes 884740
  101.6 9.2 %collective-permute-start.13 = (bf16[192,384]{1,0:T(8,128)(2,1)S(1)}, bf16[192,384]{1,0:T(8,128)(2,1)S(1)}, u32[]{:S(2)}, u32[]{:S(2)}) collective-permute-start(bf16[192,384]{1,0:T(8,128)(2,1)S(1)} %copy-done.33), channel_id=1, source_target_pairs={{0,8},{2,10},{4,12},{6,14},{8,0},{10,2},{12,4},{14,6},{16,24},{18,... | collective-permute-start | bytes 442376 | tf_op jit(solution)/shard_map/ppermute | solution.py:18
  101.6 24.3 %copy-start.21 = (bf16[192,768]{1,0:T(8,128)(2,1)}, bf16[192,768]{1,0:T(8,128)(2,1)S(1)}, u32[]{:S(2)}) copy-start(bf16[192,768]{1,0:T(8,128)(2,1)S(1)} %collective-permute-done.18.refs_17_) | copy-start | bytes 884740
  101.7 20.8 %collective-permute-start.21 = (bf16[192,768]{1,0:T(8,128)(2,1)S(1)}, bf16[192,768]{1,0:T(8,128)(2,1)S(1)}, u32[]{:S(2)}, u32[]{:S(2)}) collective-permute-start(bf16[192,768]{1,0:T(8,128)(2,1)S(1)} %collective-permute-done.11.refs_9_), channel_id=1, source_target_pairs={{0,4},{2,6},{4,0},{6,2},{8,12},{10,14},{12,8},{14,10},{16,20},{18,... | collective-permute-start | bytes 884744 | tf_op jit(solution)/shard_map/ppermute | solution.py:18
  103.1 22.8 %collective-permute-start.22 = (bf16[192,768]{1,0:T(8,128)(2,1)S(1)}, bf16[192,768]{1,0:T(8,128)(2,1)S(1)}, u32[]{:S(2)}, u32[]{:S(2)}) collective-permute-start(bf16[192,768]{1,0:T(8,128)(2,1)S(1)} %collective-permute-done.15.refs_13_), channel_id=1, source_target_pairs={{0,4},{2,6},{4,0},{6,2},{8,12},{10,14},{12,8},{14,10},{16,20},{18,... | collective-permute-start | bytes 884744 | tf_op jit(solution)/shard_map/ppermute | solution.py:18
  103.8 22.1 %collective-permute-start.23 = (bf16[192,768]{1,0:T(8,128)(2,1)S(1)}, bf16[192,768]{1,0:T(8,128)(2,1)S(1)}, u32[]{:S(2)}, u32[]{:S(2)}) collective-permute-start(bf16[192,768]{1,0:T(8,128)(2,1)S(1)} %collective-permute-done.18.refs_17_), channel_id=1, source_target_pairs={{0,4},{2,6},{4,0},{6,2},{8,12},{10,14},{12,8},{14,10},{16,20},{18,... | collective-permute-start | bytes 884744 | tf_op jit(solution)/shard_map/ppermute | solution.py:18
  105.7 14.7 %collective-permute-start.16 = (bf16[192,384]{1,0:T(8,128)(2,1)S(1)}, bf16[192,384]{1,0:T(8,128)(2,1)S(1)}, u32[]{:S(2)}, u32[]{:S(2)}) collective-permute-start(bf16[192,384]{1,0:T(8,128)(2,1)S(1)} %copy-done.32), channel_id=1, source_target_pairs={{0,16},{2,18},{4,20},{6,22},{8,24},{10,26},{12,28},{14,30},{16,0},... | collective-permute-start | bytes 442376 | tf_op jit(solution)/shard_map/ppermute | solution.py:18
  110.8 15.1 %copy-start.35 = (bf16[192,384]{1,0:T(8,128)(2,1)}, bf16[192,384]{1,0:T(8,128)(2,1)S(1)}, u32[]{:S(2)}) copy-start(bf16[192,384]{1,0:T(8,128)(2,1)S(1)} %collective-permute-done.13.refs_1_) | copy-start | bytes 442372
  110.8 9.5 %collective-permute-start.19 = (bf16[192,384]{1,0:T(8,128)(2,1)S(1)}, bf16[192,384]{1,0:T(8,128)(2,1)S(1)}, u32[]{:S(2)}, u32[]{:S(2)}) collective-permute-start(bf16[192,384]{1,0:T(8,128)(2,1)S(1)} %copy-done.31), channel_id=1, source_target_pairs={{0,24},{2,26},{4,28},{6,30},{8,16},{10,18},{12,20},{14,22},{16,8},... | collective-permute-start | bytes 442376 | tf_op jit(solution)/shard_map/ppermute | solution.py:18
  120.3 20.4 %collective-permute-start.14 = (bf16[192,384]{1,0:T(8,128)(2,1)S(1)}, bf16[192,384]{1,0:T(8,128)(2,1)S(1)}, u32[]{:S(2)}, u32[]{:S(2)}) collective-permute-start(bf16[192,384]{1,0:T(8,128)(2,1)S(1)} %copy-done.30), channel_id=1, source_target_pairs={{0,8},{2,10},{4,12},{6,14},{8,0},{10,2},{12,4},{14,6},{16,24},{18,... | collective-permute-start | bytes 442376 | tf_op jit(solution)/shard_map/ppermute | solution.py:18
  120.4 23.8 %collective-permute-start.17 = (bf16[192,384]{1,0:T(8,128)(2,1)S(1)}, bf16[192,384]{1,0:T(8,128)(2,1)S(1)}, u32[]{:S(2)}, u32[]{:S(2)}) collective-permute-start(bf16[192,384]{1,0:T(8,128)(2,1)S(1)} %copy-done.29), channel_id=1, source_target_pairs={{0,16},{2,18},{4,20},{6,22},{8,24},{10,26},{12,28},{14,30},{16,0},... | collective-permute-start | bytes 442376 | tf_op jit(solution)/shard_map/ppermute | solution.py:18
  122.5 21.7 %collective-permute-start.20 = (bf16[192,384]{1,0:T(8,128)(2,1)S(1)}, bf16[192,384]{1,0:T(8,128)(2,1)S(1)}, u32[]{:S(2)}, u32[]{:S(2)}) collective-permute-start(bf16[192,384]{1,0:T(8,128)(2,1)S(1)} %copy-done.28), channel_id=1, source_target_pairs={{0,24},{2,26},{4,28},{6,30},{8,16},{10,18},{12,20},{14,22},{16,8},... | collective-permute-start | bytes 442376 | tf_op jit(solution)/shard_map/ppermute | solution.py:18
  139.7 18.5 %collective-permute-start.28 = (bf16[192,384]{1,0:T(8,128)(2,1)}, bf16[192,384]{1,0:T(8,128)(2,1)S(1)}, u32[]{:S(2)}, u32[]{:S(2)}) collective-permute-start(bf16[192,384]{1,0:T(8,128)(2,1)} %get-tuple-element.116), channel_id=1, source_target_pairs={{0,8},{2,10},{4,12},{6,14},{8,0},{10,2},{12,4},{14,6},{16,24},{18,... | collective-permute-start | bytes 442376 | tf_op jit(solution)/shard_map/ppermute | solution.py:18
  139.7 19.2 %collective-permute-start.29 = (bf16[192,384]{1,0:T(8,128)(2,1)}, bf16[192,384]{1,0:T(8,128)(2,1)S(1)}, u32[]{:S(2)}, u32[]{:S(2)}) collective-permute-start(bf16[192,384]{1,0:T(8,128)(2,1)} %get-tuple-element.117), channel_id=1, source_target_pairs={{0,16},{2,18},{4,20},{6,22},{8,24},{10,26},{12,28},{14,30},{16,0},... | collective-permute-start | bytes 442376 | tf_op jit(solution)/shard_map/ppermute | solution.py:18
  140.7 21.6 %collective-permute-start.30 = (bf16[192,384]{1,0:T(8,128)(2,1)}, bf16[192,384]{1,0:T(8,128)(2,1)S(1)}, u32[]{:S(2)}, u32[]{:S(2)}) collective-permute-start(bf16[192,384]{1,0:T(8,128)(2,1)} %get-tuple-element.118), channel_id=1, source_target_pairs={{0,24},{2,26},{4,28},{6,30},{8,16},{10,18},{12,20},{14,22},{16,8},... | collective-permute-start | bytes 442376 | tf_op jit(solution)/shard_map/ppermute | solution.py:18
  158.0 8.2 %collective-permute-start.24 = (bf16[192,384]{1,0:T(8,128)(2,1)}, bf16[192,384]{1,0:T(8,128)(2,1)S(1)}, u32[]{:S(2)}, u32[]{:S(2)}) collective-permute-start(bf16[192,384]{1,0:T(8,128)(2,1)} %get-tuple-element.111), channel_id=1, source_target_pairs={{0,2},{2,0},{4,6},{6,4},{8,10},{10,8},{12,14},{14,12},{16,18},{18,... | collective-permute-start | bytes 442376 | tf_op jit(solution)/shard_map/ppermute | solution.py:18
  158.1 8.1 %collective-permute-start.25 = (bf16[192,384]{1,0:T(8,128)(2,1)}, bf16[192,384]{1,0:T(8,128)(2,1)S(1)}, u32[]{:S(2)}, u32[]{:S(2)}) collective-permute-start(bf16[192,384]{1,0:T(8,128)(2,1)} %get-tuple-element.112), channel_id=1, source_target_pairs={{0,10},{2,8},{4,14},{6,12},{8,2},{10,0},{12,6},{14,4},{16,26},{18,... | collective-permute-start | bytes 442376 | tf_op jit(solution)/shard_map/ppermute | solution.py:18
  158.2 13.1 %collective-permute-start.26 = (bf16[192,384]{1,0:T(8,128)(2,1)}, bf16[192,384]{1,0:T(8,128)(2,1)S(1)}, u32[]{:S(2)}, u32[]{:S(2)}) collective-permute-start(bf16[192,384]{1,0:T(8,128)(2,1)} %get-tuple-element.113), channel_id=1, source_target_pairs={{0,18},{2,16},{4,22},{6,20},{8,26},{10,24},{12,30},{14,28},{16,2},... | collective-permute-start | bytes 442376 | tf_op jit(solution)/shard_map/ppermute | solution.py:18
  158.9 12.4 %collective-permute-start.27 = (bf16[192,384]{1,0:T(8,128)(2,1)}, bf16[192,384]{1,0:T(8,128)(2,1)S(1)}, u32[]{:S(2)}, u32[]{:S(2)}) collective-permute-start(bf16[192,384]{1,0:T(8,128)(2,1)} %get-tuple-element.114), channel_id=1, source_target_pairs={{0,26},{2,24},{4,30},{6,28},{8,18},{10,16},{12,22},{14,20},{16,10}... | collective-permute-start | bytes 442376 | tf_op jit(solution)/shard_map/ppermute | solution.py:18
  (24 other events, 89.2 us)

commit v9 on v8

--- a/solution.py
+++ b/solution.py
@@ -11,7 +11,7 @@
 HD = 128
 LOG2_E = 1.4426950408889634
 HIDDEN = -1e30
-VMEM_LIMIT = 56 * 2**20
+VMEM_LIMIT = 44 * 2**20
 
 
 def exchange(value, axis, size, bit):

time: 177 us -> 171 us (0.966)
  local copies, waits for them, and re-layouts: 12.1 us -> 5 us
  Pallas kernels: 88.6 us -> 85 us
  waiting for transfers between devices: 31.1 us -> 33.6 us
  starting transfers between devices: 42.7 us -> 44.9 us
    pallas_call x2, Pallas kernels: 24.9 us -> 32.6 us  [attend(): pl.pallas_call(functools.partial(attend_body, block, ways, slots, len(arr...]
    pallas_call x4, Pallas kernels: 37.3 us -> 30 us  [rest_products(): pl.pallas_call(functools.partial(rest_body, shares, len(weights), chunks,...]
    unnamed x82 -> x4, local copies, waits for them, and re-layouts: 7 us -> 0.01 us
    pallas_call x2, Pallas kernels: 6.49 us -> 3.98 us  [assemble(): pl.pallas_call(functools.partial(assemble_body, ways), out_shape=jax.Shap...]
    ppermute x31, waiting for transfers between devices: 31.1 us -> 33.6 us  [exchange(): return lax.ppermute(value, axis, [(i, i ^ bit) for i in range(size)])]
    ppermute x31, starting transfers between devices: 42.7 us -> 44.9 us  [exchange(): return lax.ppermute(value, axis, [(i, i ^ bit) for i in range(size)])]
  transfers between devices with their start and end apart: 31 -> 31, of which waited for: 6 -> 8; matrix products, arithmetic and copies ran while one was open for 2% -> 1% of each run, Pallas kernels for 49% -> 49%
where the time goes in v9:
time: 171 us; the launch traced here: 169 us
  Pallas kernels  85 us (50%)
  starting transfers between devices  44.9 us (26%)
  waiting for transfers between devices  33.6 us (20%)
  local copies, waits for them, and re-layouts  5 us (3%)
    ppermute x31, starting transfers between devices, exchange(): return lax.ppermute(value, axis, [(i, i ^ bit) for i in range(size)])  44.9 us
    ppermute x31, waiting for transfers between devices, exchange(): return lax.ppermute(value, axis, [(i, i ^ bit) for i in range(size)])  33.6 us
    pallas_call x2, Pallas kernels, attend(): pl.pallas_call(functools.partial(attend_body, block, ways, slots, len(arr...  32.6 us
    pallas_call x4, Pallas kernels, rest_products(): pl.pallas_call(functools.partial(rest_body, shares, len(weights), chunks,...  30 us
    pallas_call x1, Pallas kernels, own_products(): pl.pallas_call(functools.partial(own_body, len(weights)), out_shape=[jax....  17.7 us
    pallas_call x2, Pallas kernels, assemble(): pl.pallas_call(functools.partial(assemble_body, ways), out_shape=jax.Shap...  3.98 us
  transfers between devices with their start and end apart: 31, of which 8 were waited for; matrix products, arithmetic and copies ran while one was open for 1% of the time, Pallas kernels for 49%

profile of v9, /device:TPU:0, one launch (start us, length us, event | category | flops | bytes accessed | tf_op | source)
XLA Modules:
  0.0 169.1 jit_solution(7332565256303472870)
XLA Ops:
  0.0 3.1 %dynamic-slice_bitcast_fusion = (bf16[192,2560]{1,0:T(8,128)(2,1)}, bf16[192,2560]{1,0:T(8,128)(2,1)}) fusion(bf16[2,192,2560]{2,1,0:T(8,128)(2,1)} %mine_ref.1, s32[]{:T(128)S(6)} %select_n.30, s32[]{:T(128)S(6)} %select_n.29), kind=kLoop, calls=%fused_computation | loop fusion | bytes 3932168 | tf_op jit(solution)/shard_map/jit(dynamic_index_in_dim)/squeeze | solution.py:381
  3.1 0.5 collective-permute-start.2
  3.5 2.5 %collective-permute-start.1 = (bf16[192,2560]{1,0:T(8,128)(2,1)}, bf16[192,2560]{1,0:T(8,128)(2,1)S(1)}, u32[]{:S(2)}, u32[]{:S(2)}) collective-permute-start(bf16[192,2560]{1,0:T(8,128)(2,1)} %get-tuple-element.120), channel_id=1, source_target_pairs={{0,1},{1,0},{2,3},{3,2},{4,5},{5,4},{6,7},{7,6},{8,9},{9,8},{10,11... | collective-permute-start | bytes 2949128 | tf_op jit(solution)/shard_map/ppermute | solution.py:18
  6.0 0.1 and_reduce_fusion
  6.3 0.7 fusion
  6.9 0.2 collective-permute-start
  7.2 1.0 collective-permute-done
  8.2 1.3 concatenate.4.place
  9.5 0.7 collective-permute-start.3
  10.2 17.7 %shard_map.55 = (f32[2,192,1536]{2,1,0:T(8,128)S(1)}, f32[2,192,1536]{2,1,0:T(8,128)S(1)}, f32[2,192,1536]{2,1,0:T(8,128)S(1)}) custom-call(s32[4]{0:T(128)S(1)} %pad_add_fusion.place, bf16[2,192,2560]{2,1,0:T(8,128)(2,1)S(1)} %copy-done, bf16[192,2560]{1,0:T(8,128)(2,1)} %collective-permute-done.2.other_ref, bf16[5120,1536]{1,0:T(8,128)(2,1)} %refs_1_.8, ...), custom_call_target="tpu_custom_call" | custom-call | flops 9059696640 | bytes 23592960 | tf_op jit(solution)/shard_map/pallas_call | solution.py:42
  27.9 0.9 collective-permute-done.1.refs_0_
  28.8 8.9 %shard_map.56 = (bf16[208,768]{1,0:T(8,128)(2,1)S(1)}, bf16[208,768]{1,0:T(8,128)(2,1)S(1)}, bf16[208,768]{1,0:T(8,128)(2,1)S(1)}, bf16[208,768]{1,0:T(8,128)(2,1)S(1)}) custom-call(s32[6]{0:T(128)S(1)} %concatenate.4.place, bf16[192,2560]{1,0:T(8,128)(2,1)S(1)} %collective-permute-done.1.refs_0_, bf16[5120,1536]{1,0:T(8,128)(2,1)} %refs_1_.8, ...), custom_call_target="tpu_custom_call" | custom-call | flops 3019898880 | bytes 15728640 | tf_op jit(solution)/shard_map/pallas_call | solution.py:128
  37.8 2.0 %collective-permute-start.4 = (bf16[208,768]{1,0:T(8,128)(2,1)S(1)}, bf16[208,768]{1,0:T(8,128)(2,1)S(1)}, u32[]{:S(2)}, u32[]{:S(2)}) collective-permute-start(bf16[208,768]{1,0:T(8,128)(2,1)S(1)} %get-tuple-element.77.refs_0_.refs_4_), channel_id=1, source_target_pairs={{0,4},{2,6},{4,0},{6,2},{8,12},{10,14},{12,8},{14,10},{16,20},{18,... | collective-permute-start | bytes 958472 | tf_op jit(solution)/shard_map/ppermute | solution.py:18
  39.8 1.6 collective-permute-start.5
  41.4 2.6 %collective-permute-start.7 = (bf16[208,768]{1,0:T(8,128)(2,1)S(1)}, bf16[208,768]{1,0:T(8,128)(2,1)S(1)}, u32[]{:S(2)}, u32[]{:S(2)}) collective-permute-start(bf16[208,768]{1,0:T(8,128)(2,1)S(1)} %get-tuple-element.81), channel_id=1, source_target_pairs={{0,16},{2,18},{4,20},{6,22},{8,24},{10,26},{12,28},{14,30},{16,0},... | collective-permute-start | bytes 958472 | tf_op jit(solution)/shard_map/ppermute | solution.py:18
  44.0 0.2 collective-permute-start.9
  44.2 6.0 %shard_map.57 = (bf16[192,384]{1,0:T(8,128)(2,1)S(1)}, bf16[192,384]{1,0:T(8,128)(2,1)S(1)}, bf16[192,384]{1,0:T(8,128)(2,1)S(1)}, bf16[192,384]{1,0:T(8,128)(2,1)S(1)}) custom-call(s32[4]{0:T(128)S(1)} %pad_add_fusion.place, bf16[192,2560]{1,0:T(8,128)(2,1)S(1)} %collective-permute-done.1.refs_0_, bf16[5120,1536]{1,0:T(8,128)(2,1)} %refs_1_.9, ...), custom_call_target="tpu_custom_call" | custom-call | flops 1509949440 | bytes 7864320 | tf_op jit(solution)/shard_map/pallas_call | solution.py:128
  50.2 9.1 %shard_map.58 = (bf16[192,768]{1,0:T(8,128)(2,1)S(1)}, bf16[192,768]{1,0:T(8,128)(2,1)S(1)}, bf16[192,768]{1,0:T(8,128)(2,1)S(1)}, bf16[192,768]{1,0:T(8,128)(2,1)S(1)}) custom-call(s32[4]{0:T(128)S(1)} %pad_add_fusion.place, bf16[192,2560]{1,0:T(8,128)(2,1)S(1)} %collective-permute-done.3.refs_0_, bf16[5120,1536]{1,0:T(8,128)(2,1)} %refs_1_.8, ...), custom_call_target="tpu_custom_call" | custom-call | flops 3019898880 | bytes 15728640 | tf_op jit(solution)/shard_map/pallas_call | solution.py:128
  59.3 6.0 %shard_map.59 = (bf16[192,384]{1,0:T(8,128)(2,1)S(1)}, bf16[192,384]{1,0:T(8,128)(2,1)S(1)}, bf16[192,384]{1,0:T(8,128)(2,1)S(1)}, bf16[192,384]{1,0:T(8,128)(2,1)S(1)}) custom-call(s32[4]{0:T(128)S(1)} %pad_add_fusion.place, bf16[192,2560]{1,0:T(8,128)(2,1)S(1)} %collective-permute-done.3.refs_0_, bf16[5120,1536]{1,0:T(8,128)(2,1)} %refs_1_.9, ...), custom_call_target="tpu_custom_call" | custom-call | flops 1509949440 | bytes 7864320 | tf_op jit(solution)/shard_map/pallas_call | solution.py:128
  65.3 1.4 collective-permute-start.11
  66.7 1.5 collective-permute-start.12
  68.2 0.5 collective-permute-start.6
  68.8 1.5 collective-permute-start.8
  70.3 2.6 %collective-permute-start.15 = (bf16[192,768]{1,0:T(8,128)(2,1)S(1)}, bf16[192,768]{1,0:T(8,128)(2,1)S(1)}, u32[]{:S(2)}, u32[]{:S(2)}) collective-permute-start(bf16[192,768]{1,0:T(8,128)(2,1)S(1)} %get-tuple-element.102), channel_id=1, source_target_pairs={{0,16},{2,18},{4,20},{6,22},{8,24},{10,26},{12,28},{14,30},{16,0},... | collective-permute-start | bytes 884744 | tf_op jit(solution)/shard_map/ppermute | solution.py:18
  72.9 4.3 %collective-permute-done.11.refs_9_ = bf16[192,768]{1,0:T(8,128)(2,1)S(1)} collective-permute-done((bf16[192,768]{1,0:T(8,128)(2,1)S(1)}, bf16[192,768]{1,0:T(8,128)(2,1)S(1)}, u32[]{:S(2)}, u32[]{:S(2)}) %collective-permute-start.11) | collective-permute-done | bytes 294944 | tf_op jit(solution)/shard_map/ppermute | solution.py:18
  77.2 2.4 %collective-permute-start.18 = (bf16[192,768]{1,0:T(8,128)(2,1)S(1)}, bf16[192,768]{1,0:T(8,128)(2,1)S(1)}, u32[]{:S(2)}, u32[]{:S(2)}) collective-permute-start(bf16[192,768]{1,0:T(8,128)(2,1)S(1)} %get-tuple-element.108), channel_id=1, source_target_pairs={{0,24},{2,26},{4,28},{6,30},{8,16},{10,18},{12,20},{14,22},{16,8},... | collective-permute-start | bytes 884744 | tf_op jit(solution)/shard_map/ppermute | solution.py:18
  79.6 2.7 %collective-permute-start.10 = (bf16[208,768]{1,0:T(8,128)(2,1)S(1)}, bf16[208,768]{1,0:T(8,128)(2,1)S(1)}, u32[]{:S(2)}, u32[]{:S(2)}) collective-permute-start(bf16[208,768]{1,0:T(8,128)(2,1)S(1)} %collective-permute-done.9.refs_6_.refs_16_), channel_id=1, source_target_pairs={{0,4},{2,6},{4,0},{6,2},{8,12},{10,14},{12,8},{14,10},{16,20},{18,... | collective-permute-start | bytes 958472 | tf_op jit(solution)/shard_map/ppermute | solution.py:18
  82.3 11.4 %collective-permute-done.15.refs_13_ = bf16[192,768]{1,0:T(8,128)(2,1)S(1)} collective-permute-done((bf16[192,768]{1,0:T(8,128)(2,1)S(1)}, bf16[192,768]{1,0:T(8,128)(2,1)S(1)}, u32[]{:S(2)}, u32[]{:S(2)}) %collective-permute-start.15) | collective-permute-done | bytes 294944 | tf_op jit(solution)/shard_map/ppermute | solution.py:18
  93.8 1.9 %collective-permute-start.22 = (bf16[192,768]{1,0:T(8,128)(2,1)S(1)}, bf16[192,768]{1,0:T(8,128)(2,1)S(1)}, u32[]{:S(2)}, u32[]{:S(2)}) collective-permute-start(bf16[192,768]{1,0:T(8,128)(2,1)S(1)} %collective-permute-done.15.refs_13_), channel_id=1, source_target_pairs={{0,4},{2,6},{4,0},{6,2},{8,12},{10,14},{12,8},{14,10},{16,20},{18,... | collective-permute-start | bytes 884744 | tf_op jit(solution)/shard_map/ppermute | solution.py:18
  95.8 1.4 collective-permute-done.10.refs_7_.refs_18_
  97.2 4.6 %collective-permute-start.16 = (bf16[192,384]{1,0:T(8,128)(2,1)S(1)}, bf16[192,384]{1,0:T(8,128)(2,1)S(1)}, u32[]{:S(2)}, u32[]{:S(2)}) collective-permute-start(bf16[192,384]{1,0:T(8,128)(2,1)S(1)} %get-tuple-element.103), channel_id=1, source_target_pairs={{0,16},{2,18},{4,20},{6,22},{8,24},{10,26},{12,28},{14,30},{16,0},... | collective-permute-start | bytes 442376 | tf_op jit(solution)/shard_map/ppermute | solution.py:18
  101.8 1.4 collective-permute-start.19
  103.2 0.7 shard_map.60.table
  104.0 7.2 %collective-permute-done.16.refs_2_ = bf16[192,384]{1,0:T(8,128)(2,1)S(1)} collective-permute-done((bf16[192,384]{1,0:T(8,128)(2,1)S(1)}, bf16[192,384]{1,0:T(8,128)(2,1)S(1)}, u32[]{:S(2)}, u32[]{:S(2)}) %collective-permute-start.16) | collective-permute-done | bytes 147488 | tf_op jit(solution)/shard_map/ppermute | solution.py:18
  111.2 2.2 %collective-permute-start.17 = (bf16[192,384]{1,0:T(8,128)(2,1)S(1)}, bf16[192,384]{1,0:T(8,128)(2,1)S(1)}, u32[]{:S(2)}, u32[]{:S(2)}) collective-permute-start(bf16[192,384]{1,0:T(8,128)(2,1)S(1)} %get-tuple-element.104), channel_id=1, source_target_pairs={{0,16},{2,18},{4,20},{6,22},{8,24},{10,26},{12,28},{14,30},{16,0},... | collective-permute-start | bytes 442376 | tf_op jit(solution)/shard_map/ppermute | solution.py:18
  113.3 3.0 %collective-permute-start.20 = (bf16[192,384]{1,0:T(8,128)(2,1)S(1)}, bf16[192,384]{1,0:T(8,128)(2,1)S(1)}, u32[]{:S(2)}, u32[]{:S(2)}) collective-permute-start(bf16[192,384]{1,0:T(8,128)(2,1)S(1)} %get-tuple-element.110), channel_id=1, source_target_pairs={{0,24},{2,26},{4,28},{6,30},{8,16},{10,18},{12,20},{14,22},{16,8},... | collective-permute-start | bytes 442376 | tf_op jit(solution)/shard_map/ppermute | solution.py:18
  116.3 16.3 %shard_map.62 = (bf16[192,384]{1,0:T(8,128)(2,1)S(1)}, bf16[192,384]{1,0:T(8,128)(2,1)S(1)}, bf16[192,384]{1,0:T(8,128)(2,1)S(1)}, bf16[192,384]{1,0:T(8,128)(2,1)S(1)}) custom-call(s32[16]{0:T(128)S(1)} %shard_map.60.table, bf16[192,384]{1,0:T(8,128)(2,1)S(1)} %get-tuple-element.91.refs_0_, bf16[192,384]{1,0:T(8,128)(2,1)S(1)} %collective-permute-done.13.refs_1_, ...), custom_call_target="tpu_custom_call" | custom-call | flops 2717908992 | bytes 5898240 | tf_op jit(solution)/shard_map/pallas_call | solution.py:276
  132.6 1.5 collective-permute-start.28
  134.1 1.6 collective-permute-start.29
  135.7 1.4 collective-permute-start.30
  137.1 16.3 %shard_map.61 = (bf16[192,384]{1,0:T(8,128)(2,1)S(1)}, bf16[192,384]{1,0:T(8,128)(2,1)S(1)}, bf16[192,384]{1,0:T(8,128)(2,1)S(1)}, bf16[192,384]{1,0:T(8,128)(2,1)S(1)}) custom-call(s32[16]{0:T(128)S(1)} %shard_map.60.table, bf16[192,384]{1,0:T(8,128)(2,1)S(1)} %get-tuple-element.92.refs_0_, bf16[192,384]{1,0:T(8,128)(2,1)S(1)} %collective-permute-done.14.refs_1_, ...), custom_call_target="tpu_custom_call" | custom-call | flops 2717908992 | bytes 5898240 | tf_op jit(solution)/shard_map/pallas_call | solution.py:276
  153.5 0.7 collective-permute-start.25
  154.2 2.1 %collective-permute-start.26 = (bf16[192,384]{1,0:T(8,128)(2,1)S(1)}, bf16[192,384]{1,0:T(8,128)(2,1)S(1)}, u32[]{:S(2)}, u32[]{:S(2)}) collective-permute-start(bf16[192,384]{1,0:T(8,128)(2,1)S(1)} %get-tuple-element.113), channel_id=1, source_target_pairs={{0,18},{2,16},{4,22},{6,20},{8,26},{10,24},{12,30},{14,28},{16,2},... | collective-permute-start | bytes 442376 | tf_op jit(solution)/shard_map/ppermute | solution.py:18
  156.3 1.4 collective-permute-start.27
  157.8 2.0 %shard_map.63.refs_4_ = bf16[2,192,1536]{2,1,0:T(8,128)(2,1)} custom-call(s32[4]{0:T(128)S(1)} %pad_add_fusion.place, bf16[192,384]{1,0:T(8,128)(2,1)S(1)} %get-tuple-element.115.refs_0_, bf16[192,384]{1,0:T(8,128)(2,1)S(1)} %collective-permute-done.28.refs_1_, bf16[192,384]{1,0:T(8,128)(2,1)S(1)} %collective-permute-done.29.refs_2_, ...), custom_call_target="tpu_custom_call" | custom-call | tf_op jit(solution)/shard_map/pallas_call | solution.py:344
  159.8 2.4 %collective-permute-done.25.refs_1_ = bf16[192,384]{1,0:T(8,128)(2,1)S(1)} collective-permute-done((bf16[192,384]{1,0:T(8,128)(2,1)S(1)}, bf16[192,384]{1,0:T(8,128)(2,1)S(1)}, u32[]{:S(2)}, u32[]{:S(2)}) %collective-permute-start.25) | collective-permute-done | bytes 147488 | tf_op jit(solution)/shard_map/ppermute | solution.py:18
  162.2 4.9 %collective-permute-done.27.refs_3_ = bf16[192,384]{1,0:T(8,128)(2,1)S(1)} collective-permute-done((bf16[192,384]{1,0:T(8,128)(2,1)S(1)}, bf16[192,384]{1,0:T(8,128)(2,1)S(1)}, u32[]{:S(2)}, u32[]{:S(2)}) %collective-permute-start.27) | collective-permute-done | bytes 147488 | tf_op jit(solution)/shard_map/ppermute | solution.py:18
  167.1 2.0 %shard_map.64 = bf16[2,192,1536]{2,1,0:T(8,128)(2,1)} custom-call(s32[4]{0:T(128)S(1)} %pad_add_fusion.place, bf16[192,384]{1,0:T(8,128)(2,1)S(1)} %collective-permute-done.24.refs_0_, bf16[192,384]{1,0:T(8,128)(2,1)S(1)} %collective-permute-done.25.refs_1_, bf16[192,384]{1,0:T(8,128)(2,1)S(1)} %collective-permute-done.26.refs_2_, ...), custom_call_target="tpu_custom_call", output_to_operand_aliasing={{}: (5, {})} | custom-call | tf_op jit(solution)/shard_map/pallas_call | solution.py:344
  (35 shorter events, 0.5 us)
Async XLA Ops:
  0.0 10.2 %copy-start = (bf16[2,192,2560]{2,1,0:T(8,128)(2,1)S(1)}, bf16[2,192,2560]{2,1,0:T(8,128)(2,1)}, u32[]{:S(2)}) copy-start(bf16[2,192,2560]{2,1,0:T(8,128)(2,1)} %mine_ref.1) | copy-start | bytes 5898244
  0.0 6.0 %copy-start.1 = (s32[2,192]{1,0:T(2,128)S(1)}, s32[2,192]{1,0:T(2,128)}, u32[]{:S(2)}) copy-start(s32[2,192]{1,0:T(2,128)} %param.9) | copy-start | bytes 4612
  3.1 6.4 %collective-permute-start.2 = (bf16[192,2560]{1,0:T(8,128)(2,1)}, bf16[192,2560]{1,0:T(8,128)(2,1)}, u32[]{:S(2)}, u32[]{:S(2)}) collective-permute-start(bf16[192,2560]{1,0:T(8,128)(2,1)} %get-tuple-element.119), channel_id=1, source_target_pairs={{0,2},{2,0},{4,6},{6,4},{8,10},{10,8},{12,14},{14,12},{16,18},{18,... | collective-permute-start | bytes 2949128 | tf_op jit(solution)/shard_map/ppermute | solution.py:18
  3.5 25.3 %collective-permute-start.1 = (bf16[192,2560]{1,0:T(8,128)(2,1)}, bf16[192,2560]{1,0:T(8,128)(2,1)S(1)}, u32[]{:S(2)}, u32[]{:S(2)}) collective-permute-start(bf16[192,2560]{1,0:T(8,128)(2,1)} %get-tuple-element.120), channel_id=1, source_target_pairs={{0,1},{1,0},{2,3},{3,2},{4,5},{5,4},{6,7},{7,6},{8,9},{9,8},{10,11... | collective-permute-start | bytes 2949128 | tf_op jit(solution)/shard_map/ppermute | solution.py:18
  6.9 1.3 collective-permute-start
  9.5 40.7 %collective-permute-start.3 = (bf16[192,2560]{1,0:T(8,128)(2,1)}, bf16[192,2560]{1,0:T(8,128)(2,1)S(1)}, u32[]{:S(2)}, u32[]{:S(2)}) collective-permute-start(bf16[192,2560]{1,0:T(8,128)(2,1)} %collective-permute-done.2.other_ref), channel_id=1, source_target_pairs={{0,1},{1,0},{2,3},{3,2},{4,5},{5,4},{6,7},{7,6},{8,9},{9,8},{10,11... | collective-permute-start | bytes 2949128 | tf_op jit(solution)/shard_map/ppermute | solution.py:18
  37.8 27.5 %collective-permute-start.4 = (bf16[208,768]{1,0:T(8,128)(2,1)S(1)}, bf16[208,768]{1,0:T(8,128)(2,1)S(1)}, u32[]{:S(2)}, u32[]{:S(2)}) collective-permute-start(bf16[208,768]{1,0:T(8,128)(2,1)S(1)} %get-tuple-element.77.refs_0_.refs_4_), channel_id=1, source_target_pairs={{0,4},{2,6},{4,0},{6,2},{8,12},{10,14},{12,8},{14,10},{16,20},{18,... | collective-permute-start | bytes 958472 | tf_op jit(solution)/shard_map/ppermute | solution.py:18
  39.8 25.5 %collective-permute-start.5 = (bf16[208,768]{1,0:T(8,128)(2,1)S(1)}, bf16[208,768]{1,0:T(8,128)(2,1)S(1)}, u32[]{:S(2)}, u32[]{:S(2)}) collective-permute-start(bf16[208,768]{1,0:T(8,128)(2,1)S(1)} %get-tuple-element.78), channel_id=1, source_target_pairs={{0,8},{2,10},{4,12},{6,14},{8,0},{10,2},{12,4},{14,6},{16,24},{18,... | collective-permute-start | bytes 958472 | tf_op jit(solution)/shard_map/ppermute | solution.py:18
  41.4 27.4 %collective-permute-start.7 = (bf16[208,768]{1,0:T(8,128)(2,1)S(1)}, bf16[208,768]{1,0:T(8,128)(2,1)S(1)}, u32[]{:S(2)}, u32[]{:S(2)}) collective-permute-start(bf16[208,768]{1,0:T(8,128)(2,1)S(1)} %get-tuple-element.81), channel_id=1, source_target_pairs={{0,16},{2,18},{4,20},{6,22},{8,24},{10,26},{12,28},{14,30},{16,0},... | collective-permute-start | bytes 958472 | tf_op jit(solution)/shard_map/ppermute | solution.py:18
  44.0 26.3 %collective-permute-start.9 = (bf16[208,768]{1,0:T(8,128)(2,1)S(1)}, bf16[208,768]{1,0:T(8,128)(2,1)S(1)}, u32[]{:S(2)}, u32[]{:S(2)}) collective-permute-start(bf16[208,768]{1,0:T(8,128)(2,1)S(1)} %get-tuple-element.84), channel_id=1, source_target_pairs={{0,24},{2,26},{4,28},{6,30},{8,16},{10,18},{12,20},{14,22},{16,8},... | collective-permute-start | bytes 958472 | tf_op jit(solution)/shard_map/ppermute | solution.py:18
  65.3 11.9 %collective-permute-start.11 = (bf16[192,768]{1,0:T(8,128)(2,1)S(1)}, bf16[192,768]{1,0:T(8,128)(2,1)S(1)}, u32[]{:S(2)}, u32[]{:S(2)}) collective-permute-start(bf16[192,768]{1,0:T(8,128)(2,1)S(1)} %get-tuple-element.96), channel_id=1, source_target_pairs={{0,8},{2,10},{4,12},{6,14},{8,0},{10,2},{12,4},{14,6},{16,24},{18,... | collective-permute-start | bytes 884744 | tf_op jit(solution)/shard_map/ppermute | solution.py:18
  66.7 12.9 %collective-permute-start.12 = (bf16[192,768]{1,0:T(8,128)(2,1)S(1)}, bf16[192,768]{1,0:T(8,128)(2,1)S(1)}, u32[]{:S(2)}, u32[]{:S(2)}) collective-permute-start(bf16[192,768]{1,0:T(8,128)(2,1)S(1)} %get-tuple-element.90.refs_5_), channel_id=1, source_target_pairs={{0,4},{2,6},{4,0},{6,2},{8,12},{10,14},{12,8},{14,10},{16,20},{18,... | collective-permute-start | bytes 884744 | tf_op jit(solution)/shard_map/ppermute | solution.py:18
  68.2 25.5 %collective-permute-start.6 = (bf16[208,768]{1,0:T(8,128)(2,1)S(1)}, bf16[208,768]{1,0:T(8,128)(2,1)S(1)}, u32[]{:S(2)}, u32[]{:S(2)}) collective-permute-start(bf16[208,768]{1,0:T(8,128)(2,1)S(1)} %collective-permute-done.5.refs_2_.refs_8_), channel_id=1, source_target_pairs={{0,4},{2,6},{4,0},{6,2},{8,12},{10,14},{12,8},{14,10},{16,20},{18,... | collective-permute-start | bytes 958472 | tf_op jit(solution)/shard_map/ppermute | solution.py:18
  68.8 27.0 %collective-permute-start.8 = (bf16[208,768]{1,0:T(8,128)(2,1)S(1)}, bf16[208,768]{1,0:T(8,128)(2,1)S(1)}, u32[]{:S(2)}, u32[]{:S(2)}) collective-permute-start(bf16[208,768]{1,0:T(8,128)(2,1)S(1)} %collective-permute-done.7.refs_4_.refs_12_), channel_id=1, source_target_pairs={{0,4},{2,6},{4,0},{6,2},{8,12},{10,14},{12,8},{14,10},{16,20},{18,... | collective-permute-start | bytes 958472 | tf_op jit(solution)/shard_map/ppermute | solution.py:18
  70.3 23.4 %collective-permute-start.15 = (bf16[192,768]{1,0:T(8,128)(2,1)S(1)}, bf16[192,768]{1,0:T(8,128)(2,1)S(1)}, u32[]{:S(2)}, u32[]{:S(2)}) collective-permute-start(bf16[192,768]{1,0:T(8,128)(2,1)S(1)} %get-tuple-element.102), channel_id=1, source_target_pairs={{0,16},{2,18},{4,20},{6,22},{8,24},{10,26},{12,28},{14,30},{16,0},... | collective-permute-start | bytes 884744 | tf_op jit(solution)/shard_map/ppermute | solution.py:18
  77.2 16.5 %collective-permute-start.18 = (bf16[192,768]{1,0:T(8,128)(2,1)S(1)}, bf16[192,768]{1,0:T(8,128)(2,1)S(1)}, u32[]{:S(2)}, u32[]{:S(2)}) collective-permute-start(bf16[192,768]{1,0:T(8,128)(2,1)S(1)} %get-tuple-element.108), channel_id=1, source_target_pairs={{0,24},{2,26},{4,28},{6,30},{8,16},{10,18},{12,20},{14,22},{16,8},... | collective-permute-start | bytes 884744 | tf_op jit(solution)/shard_map/ppermute | solution.py:18
  79.6 17.6 %collective-permute-start.10 = (bf16[208,768]{1,0:T(8,128)(2,1)S(1)}, bf16[208,768]{1,0:T(8,128)(2,1)S(1)}, u32[]{:S(2)}, u32[]{:S(2)}) collective-permute-start(bf16[208,768]{1,0:T(8,128)(2,1)S(1)} %collective-permute-done.9.refs_6_.refs_16_), channel_id=1, source_target_pairs={{0,4},{2,6},{4,0},{6,2},{8,12},{10,14},{12,8},{14,10},{16,20},{18,... | collective-permute-start | bytes 958472 | tf_op jit(solution)/shard_map/ppermute | solution.py:18
  93.7 8.2 %collective-permute-start.13 = (bf16[192,384]{1,0:T(8,128)(2,1)S(1)}, bf16[192,384]{1,0:T(8,128)(2,1)S(1)}, u32[]{:S(2)}, u32[]{:S(2)}) collective-permute-start(bf16[192,384]{1,0:T(8,128)(2,1)S(1)} %get-tuple-element.97), channel_id=1, source_target_pairs={{0,8},{2,10},{4,12},{6,14},{8,0},{10,2},{12,4},{14,6},{16,24},{18,... | collective-permute-start | bytes 442376 | tf_op jit(solution)/shard_map/ppermute | solution.py:18
  93.7 19.7 %collective-permute-start.21 = (bf16[192,768]{1,0:T(8,128)(2,1)S(1)}, bf16[192,768]{1,0:T(8,128)(2,1)S(1)}, u32[]{:S(2)}, u32[]{:S(2)}) collective-permute-start(bf16[192,768]{1,0:T(8,128)(2,1)S(1)} %collective-permute-done.11.refs_9_), channel_id=1, source_target_pairs={{0,4},{2,6},{4,0},{6,2},{8,12},{10,14},{12,8},{14,10},{16,20},{18,... | collective-permute-start | bytes 884744 | tf_op jit(solution)/shard_map/ppermute | solution.py:18
  93.8 22.5 %collective-permute-start.22 = (bf16[192,768]{1,0:T(8,128)(2,1)S(1)}, bf16[192,768]{1,0:T(8,128)(2,1)S(1)}, u32[]{:S(2)}, u32[]{:S(2)}) collective-permute-start(bf16[192,768]{1,0:T(8,128)(2,1)S(1)} %collective-permute-done.15.refs_13_), channel_id=1, source_target_pairs={{0,4},{2,6},{4,0},{6,2},{8,12},{10,14},{12,8},{14,10},{16,20},{18,... | collective-permute-start | bytes 884744 | tf_op jit(solution)/shard_map/ppermute | solution.py:18
  95.7 20.6 %collective-permute-start.23 = (bf16[192,768]{1,0:T(8,128)(2,1)S(1)}, bf16[192,768]{1,0:T(8,128)(2,1)S(1)}, u32[]{:S(2)}, u32[]{:S(2)}) collective-permute-start(bf16[192,768]{1,0:T(8,128)(2,1)S(1)} %collective-permute-done.18.refs_17_), channel_id=1, source_target_pairs={{0,4},{2,6},{4,0},{6,2},{8,12},{10,14},{12,8},{14,10},{16,20},{18,... | collective-permute-start | bytes 884744 | tf_op jit(solution)/shard_map/ppermute | solution.py:18
  97.2 14.0 %collective-permute-start.16 = (bf16[192,384]{1,0:T(8,128)(2,1)S(1)}, bf16[192,384]{1,0:T(8,128)(2,1)S(1)}, u32[]{:S(2)}, u32[]{:S(2)}) collective-permute-start(bf16[192,384]{1,0:T(8,128)(2,1)S(1)} %get-tuple-element.103), channel_id=1, source_target_pairs={{0,16},{2,18},{4,20},{6,22},{8,24},{10,26},{12,28},{14,30},{16,0},... | collective-permute-start | bytes 442376 | tf_op jit(solution)/shard_map/ppermute | solution.py:18
  101.8 9.4 %collective-permute-start.19 = (bf16[192,384]{1,0:T(8,128)(2,1)S(1)}, bf16[192,384]{1,0:T(8,128)(2,1)S(1)}, u32[]{:S(2)}, u32[]{:S(2)}) collective-permute-start(bf16[192,384]{1,0:T(8,128)(2,1)S(1)} %get-tuple-element.109), channel_id=1, source_target_pairs={{0,24},{2,26},{4,28},{6,30},{8,16},{10,18},{12,20},{14,22},{16,8},... | collective-permute-start | bytes 442376 | tf_op jit(solution)/shard_map/ppermute | solution.py:18
  111.2 24.5 %collective-permute-start.14 = (bf16[192,384]{1,0:T(8,128)(2,1)S(1)}, bf16[192,384]{1,0:T(8,128)(2,1)S(1)}, u32[]{:S(2)}, u32[]{:S(2)}) collective-permute-start(bf16[192,384]{1,0:T(8,128)(2,1)S(1)} %get-tuple-element.98), channel_id=1, source_target_pairs={{0,8},{2,10},{4,12},{6,14},{8,0},{10,2},{12,4},{14,6},{16,24},{18,... | collective-permute-start | bytes 442376 | tf_op jit(solution)/shard_map/ppermute | solution.py:18
  111.2 25.9 %collective-permute-start.17 = (bf16[192,384]{1,0:T(8,128)(2,1)S(1)}, bf16[192,384]{1,0:T(8,128)(2,1)S(1)}, u32[]{:S(2)}, u32[]{:S(2)}) collective-permute-start(bf16[192,384]{1,0:T(8,128)(2,1)S(1)} %get-tuple-element.104), channel_id=1, source_target_pairs={{0,16},{2,18},{4,20},{6,22},{8,24},{10,26},{12,28},{14,30},{16,0},... | collective-permute-start | bytes 442376 | tf_op jit(solution)/shard_map/ppermute | solution.py:18
  113.3 23.8 %collective-permute-start.20 = (bf16[192,384]{1,0:T(8,128)(2,1)S(1)}, bf16[192,384]{1,0:T(8,128)(2,1)S(1)}, u32[]{:S(2)}, u32[]{:S(2)}) collective-permute-start(bf16[192,384]{1,0:T(8,128)(2,1)S(1)} %get-tuple-element.110), channel_id=1, source_target_pairs={{0,24},{2,26},{4,28},{6,30},{8,16},{10,18},{12,20},{14,22},{16,8},... | collective-permute-start | bytes 442376 | tf_op jit(solution)/shard_map/ppermute | solution.py:18
  132.6 21.6 %collective-permute-start.28 = (bf16[192,384]{1,0:T(8,128)(2,1)S(1)}, bf16[192,384]{1,0:T(8,128)(2,1)S(1)}, u32[]{:S(2)}, u32[]{:S(2)}) collective-permute-start(bf16[192,384]{1,0:T(8,128)(2,1)S(1)} %get-tuple-element.116), channel_id=1, source_target_pairs={{0,8},{2,10},{4,12},{6,14},{8,0},{10,2},{12,4},{14,6},{16,24},{18,... | collective-permute-start | bytes 442376 | tf_op jit(solution)/shard_map/ppermute | solution.py:18
  134.1 22.3 %collective-permute-start.29 = (bf16[192,384]{1,0:T(8,128)(2,1)S(1)}, bf16[192,384]{1,0:T(8,128)(2,1)S(1)}, u32[]{:S(2)}, u32[]{:S(2)}) collective-permute-start(bf16[192,384]{1,0:T(8,128)(2,1)S(1)} %get-tuple-element.117), channel_id=1, source_target_pairs={{0,16},{2,18},{4,20},{6,22},{8,24},{10,26},{12,28},{14,30},{16,0},... | collective-permute-start | bytes 442376 | tf_op jit(solution)/shard_map/ppermute | solution.py:18
  135.7 22.1 %collective-permute-start.30 = (bf16[192,384]{1,0:T(8,128)(2,1)S(1)}, bf16[192,384]{1,0:T(8,128)(2,1)S(1)}, u32[]{:S(2)}, u32[]{:S(2)}) collective-permute-start(bf16[192,384]{1,0:T(8,128)(2,1)S(1)} %get-tuple-element.118), channel_id=1, source_target_pairs={{0,24},{2,26},{4,28},{6,30},{8,16},{10,18},{12,20},{14,22},{16,8},... | collective-permute-start | bytes 442376 | tf_op jit(solution)/shard_map/ppermute | solution.py:18
  153.5 6.3 %collective-permute-start.24 = (bf16[192,384]{1,0:T(8,128)(2,1)S(1)}, bf16[192,384]{1,0:T(8,128)(2,1)S(1)}, u32[]{:S(2)}, u32[]{:S(2)}) collective-permute-start(bf16[192,384]{1,0:T(8,128)(2,1)S(1)} %get-tuple-element.111), channel_id=1, source_target_pairs={{0,2},{2,0},{4,6},{6,4},{8,10},{10,8},{12,14},{14,12},{16,18},{18,... | collective-permute-start | bytes 442376 | tf_op jit(solution)/shard_map/ppermute | solution.py:18
  153.5 8.7 %collective-permute-start.25 = (bf16[192,384]{1,0:T(8,128)(2,1)S(1)}, bf16[192,384]{1,0:T(8,128)(2,1)S(1)}, u32[]{:S(2)}, u32[]{:S(2)}) collective-permute-start(bf16[192,384]{1,0:T(8,128)(2,1)S(1)} %get-tuple-element.112), channel_id=1, source_target_pairs={{0,10},{2,8},{4,14},{6,12},{8,2},{10,0},{12,6},{14,4},{16,26},{18,... | collective-permute-start | bytes 442376 | tf_op jit(solution)/shard_map/ppermute | solution.py:18
  154.2 8.0 %collective-permute-start.26 = (bf16[192,384]{1,0:T(8,128)(2,1)S(1)}, bf16[192,384]{1,0:T(8,128)(2,1)S(1)}, u32[]{:S(2)}, u32[]{:S(2)}) collective-permute-start(bf16[192,384]{1,0:T(8,128)(2,1)S(1)} %get-tuple-element.113), channel_id=1, source_target_pairs={{0,18},{2,16},{4,22},{6,20},{8,26},{10,24},{12,30},{14,28},{16,2},... | collective-permute-start | bytes 442376 | tf_op jit(solution)/shard_map/ppermute | solution.py:18
  156.3 10.7 %collective-permute-start.27 = (bf16[192,384]{1,0:T(8,128)(2,1)S(1)}, bf16[192,384]{1,0:T(8,128)(2,1)S(1)}, u32[]{:S(2)}, u32[]{:S(2)}) collective-permute-start(bf16[192,384]{1,0:T(8,128)(2,1)S(1)} %get-tuple-element.114), channel_id=1, source_target_pairs={{0,26},{2,24},{4,30},{6,28},{8,18},{10,16},{12,22},{14,20},{16,10}... | collective-permute-start | bytes 442376 | tf_op jit(solution)/shard_map/ppermute | solution.py:18

commit v10 on v9

--- a/solution.py
+++ b/solution.py
@@ -12,6 +12,7 @@
 LOG2_E = 1.4426950408889634
 HIDDEN = -1e30
 VMEM_LIMIT = 44 * 2**20
+ATTEND_LIMIT = 56 * 2**20
 
 
 def exchange(value, axis, size, bit):
@@ -161,68 +162,71 @@
     heads = width // HD
     rest = count // ways
 
-    copies = []
+    copies = [[], []]
     for slot, (offset, array, row) in enumerate(slots):
         low = table[offset]
         for part, span in ((0, low), (1, spans - 1 - low)):
-            copies.append(
+            copies[part].append(
                 pltpu.make_async_copy(
                     block_refs[array].at[pl.ds(row + part * half, half)],
                     ordered.at[pl.ds(pl.multiple_of(span * half, 16), half)],
                     sems.at[2 * slot + part],
                 )
             )
-    for copy in copies:
+    for copy in copies[0] + copies[1]:
         copy.start()
 
+    many = ways * half
     from_lane = lax.broadcasted_iota(jnp.int32, (half, 128), 0) - lax.broadcasted_iota(
         jnp.int32, (half, 128), 1
     )
     for a in range(ways):
         low = table[a * rest + block]
-        here = slice(a * half, (a + 1) * half)
         for part, span in ((0, low), (1, spans - 1 - low)):
-            asked[part, here] = query_refs[a][part * half : (part + 1) * half]
-            position[part, here] = from_lane + span * half
-    for copy in copies:
+            here = slice(part * many + a * half, part * many + (a + 1) * half)
+            asked[here] = query_refs[a][part * half : (part + 1) * half]
+            position[here] = from_lane + span * half
+    for copy in copies[0]:
         copy.wait()
 
     slope = LOG2_E / math.sqrt(HD)
     middle = spans * half // 2
-
-    def starts(part):
-        return range(0, middle * (part + 1), tile)
-
-    def visible(unit, slot, column):
-        piece = scores[slot, :, column : column + 128]
-        if column < middle * unit[0]:
-            return piece
-        return jnp.where(position[unit[0]] >= column, piece, HIDDEN)
-
-    def score_tile(unit, slot, start):
-        part, h = unit
-        scores[slot, :, start : start + tile] = lax.dot_general(
-            asked[part, :, h * HD : (h + 1) * HD],
+    starts = range(0, 2 * middle, tile)
+
+    def first_row(start):
+        return 0 if start < middle else many
+
+    def visible(slot, column):
+        piece = scores[slot, first_row(column) :, column : column + 128]
+        if column >= middle:
+            return jnp.where(position[many:] >= column, piece, HIDDEN)
+        masked = jnp.where(position[:many] >= column, piece[:many], HIDDEN)
+        return jnp.concatenate([masked, piece[many:]], axis=0)
+
+    def score_tile(h, slot, start):
+        first = first_row(start)
+        scores[slot, first:, start : start + tile] = lax.dot_general(
+            asked[first:, h * HD : (h + 1) * HD],
             ordered[start : start + tile, h * HD : (h + 1) * HD],
             (((1,), (1,)), ((), ())),
             preferred_element_type=jnp.float32,
         )
-        top = None if start == 0 else highest[slot]
+        top = None if start == 0 else highest[slot, first:]
         for column in range(start, start + tile, 128):
-            piece = visible(unit, slot, column)
+            piece = visible(slot, column)
             top = piece if top is None else jnp.maximum(top, piece)
-        highest[slot] = top
-
-    def value_tile(unit, slot, start):
-        part, h = unit
-        top = highest[slot]
-        added = None if start == 0 else sums[slot]
+        highest[slot, first:] = top
+
+    def value_tile(h, slot, start):
+        first = first_row(start)
+        top = highest[slot, first:]
+        added = None if start == 0 else sums[slot, first:]
         weights = []
         for column in range(start, start + tile, 128):
-            piece = jnp.exp2((visible(unit, slot, column) - top) * slope)
+            piece = jnp.exp2((visible(slot, column) - top) * slope)
             added = piece if added is None else added + piece
             weights.append(piece.astype(jnp.bfloat16))
-        sums[slot] = added
+        sums[slot, first:] = added
         product = jnp.dot(
             jnp.concatenate(weights, axis=1),
             ordered[start : start + tile, width + h * HD : width + (h + 1) * HD],
@@ -231,28 +235,28 @@
         if start == 0:
             total[slot] = product
         else:
-            total[slot] += product
-
-    units = [(0, 0)] + [(1, h) for h in range(heads)] + [(0, h) for h in range(1, heads)]
-    for n in range(len(units) + 1):
-        todo = []
-        if n < len(units):
-            todo.append([functools.partial(score_tile, units[n], n % 2, start) for start in starts(units[n][0])])
+            total[slot, first:] += product
+
+    for n in range(heads + 1):
+        slot = (n - 1) % 2
         if n > 0:
-            slot = (n - 1) % 2
             highest[slot] = jnp.broadcast_to(jnp.max(highest[slot], axis=1, keepdims=True), highest.shape[1:])
-            todo.append([functools.partial(value_tile, units[n - 1], slot, start) for start in starts(units[n - 1][0])])
-        for index in range(max(len(steps) for steps in todo)):
-            for steps in todo:
-                if index < len(steps):
-                    steps[index]()
+        for start in starts:
+            if n == 0 and start == middle:
+                for copy in copies[1]:
+                    copy.wait()
+            if n < heads:
+                score_tile(n, n % 2, start)
+            if n > 0:
+                value_tile(n - 1, slot, start)
         if n > 0:
-            part, h = units[n - 1]
             result = total[slot] / jnp.sum(sums[slot], axis=1, keepdims=True)
+            result = result.astype(jnp.bfloat16)
             for a in range(ways):
-                out_refs[a][part * half : (part + 1) * half, h * HD : (h + 1) * HD] = result[
-                    a * half : (a + 1) * half
-                ].astype(jnp.bfloat16)
+                for part in range(2):
+                    out_refs[a][part * half : (part + 1) * half, (n - 1) * HD : n * HD] = result[
+                        part * many + a * half : part * many + (a + 1) * half
+                    ]
 
 
 def attend(block, queries, blocks, table):
@@ -283,15 +287,15 @@
         out_specs=[pl.BlockSpec((rows, width), lambda i: (0, 0))] * ways,
         scratch_shapes=[
             pltpu.VMEM((length, 2 * width), jnp.bfloat16),
-            pltpu.VMEM((2, many, width), jnp.bfloat16),
-            pltpu.VMEM((2, many, length), jnp.float32),
-            pltpu.VMEM((2, many, 128), jnp.float32),
-            pltpu.VMEM((2, many, 128), jnp.float32),
-            pltpu.VMEM((2, many, HD), jnp.float32),
-            pltpu.VMEM((2, many, 128), jnp.int32),
+            pltpu.VMEM((2 * many, width), jnp.bfloat16),
+            pltpu.VMEM((2, 2 * many, length), jnp.float32),
+            pltpu.VMEM((2, 2 * many, 128), jnp.float32),
+            pltpu.VMEM((2, 2 * many, 128), jnp.float32),
+            pltpu.VMEM((2, 2 * many, HD), jnp.float32),
+            pltpu.VMEM((2 * many, 128), jnp.int32),
             pltpu.SemaphoreType.DMA((2 * count,)),
         ],
-        compiler_params=pltpu.CompilerParams(vmem_limit_bytes=VMEM_LIMIT),
+        compiler_params=pltpu.CompilerParams(vmem_limit_bytes=ATTEND_LIMIT),
         cost_estimate=pl.CostEstimate(
             flops=flops,
             bytes_accessed=4 * length * width + 4 * ways * rows * width,

time: 171 us -> 168 us (0.982)
  Pallas kernels: 85 us -> 79.8 us
  local copies, waits for them, and re-layouts: 5 us -> 8.31 us
    pallas_call x2, Pallas kernels: 32.6 us -> 27.2 us  [attend(): pl.pallas_call(functools.partial(attend_body, block, ways, slots, len(arr...]
    unnamed x4 -> x56, local copies, waits for them, and re-layouts: 0.01 us -> 3.24 us
  transfers between devices with their start and end apart: 31 -> 31, of which waited for: 8 -> 8; matrix products, arithmetic and copies ran while one was open for 1% -> 1% of each run, Pallas kernels for 49% -> 47%
where the time goes in v10:
time: 168 us; the launch traced here: 166 us
  Pallas kernels  79.8 us (48%)
  starting transfers between devices  44.9 us (27%)
  waiting for transfers between devices  32.5 us (19%)
  local copies, waits for them, and re-layouts  8.31 us (5%)
    ppermute x31, starting transfers between devices, exchange(): return lax.ppermute(value, axis, [(i, i ^ bit) for i in range(size)])  44.9 us
    ppermute x31, waiting for transfers between devices, exchange(): return lax.ppermute(value, axis, [(i, i ^ bit) for i in range(size)])  32.5 us
    pallas_call x4, Pallas kernels, rest_products(): pl.pallas_call(functools.partial(rest_body, shares, len(weights), chunks,...  30.2 us
    pallas_call x2, Pallas kernels, attend(): pl.pallas_call(functools.partial(attend_body, block, ways, slots, len(arr...  27.2 us
    pallas_call x1, Pallas kernels, own_products(): pl.pallas_call(functools.partial(own_body, len(weights)), out_shape=[jax....  17.7 us
    pallas_call x2, Pallas kernels, assemble(): pl.pallas_call(functools.partial(assemble_body, ways), out_shape=jax.Shap...  3.98 us
  transfers between devices with their start and end apart: 31, of which 8 were waited for; matrix products, arithmetic and copies ran while one was open for 1% of the time, Pallas kernels for 47%

profile of v10, /device:TPU:0, one launch (start us, length us, event | category | flops | bytes accessed | tf_op | source)
XLA Modules:
  0.0 166.2 jit_solution(301665600180813269)
XLA Ops:
  0.0 3.1 %dynamic-slice_bitcast_fusion = (bf16[192,2560]{1,0:T(8,128)(2,1)}, bf16[192,2560]{1,0:T(8,128)(2,1)}) fusion(bf16[2,192,2560]{2,1,0:T(8,128)(2,1)} %mine_ref.1, s32[]{:T(128)S(6)} %select_n.30, s32[]{:T(128)S(6)} %select_n.29), kind=kLoop, calls=%fused_computation | loop fusion | bytes 3932168 | tf_op jit(solution)/shard_map/jit(dynamic_index_in_dim)/squeeze | solution.py:385
  3.5 2.5 %collective-permute-start.1 = (bf16[192,2560]{1,0:T(8,128)(2,1)}, bf16[192,2560]{1,0:T(8,128)(2,1)S(1)}, u32[]{:S(2)}, u32[]{:S(2)}) collective-permute-start(bf16[192,2560]{1,0:T(8,128)(2,1)} %get-tuple-element.120), channel_id=1, source_target_pairs={{0,1},{1,0},{2,3},{3,2},{4,5},{5,4},{6,7},{7,6},{8,9},{9,8},{10,11... | collective-permute-start | bytes 2949128 | tf_op jit(solution)/shard_map/ppermute | solution.py:19
  6.3 0.7 fusion
  7.2 1.0 collective-permute-done
  8.2 1.3 concatenate.4.place
  9.6 0.7 collective-permute-start.3
  10.3 17.7 %shard_map.55 = (f32[2,192,1536]{2,1,0:T(8,128)S(1)}, f32[2,192,1536]{2,1,0:T(8,128)S(1)}, f32[2,192,1536]{2,1,0:T(8,128)S(1)}) custom-call(s32[4]{0:T(128)S(1)} %pad_add_fusion.place, bf16[2,192,2560]{2,1,0:T(8,128)(2,1)S(1)} %copy-done, bf16[192,2560]{1,0:T(8,128)(2,1)} %collective-permute-done.2.other_ref, bf16[5120,1536]{1,0:T(8,128)(2,1)} %refs_1_.8, ...), custom_call_target="tpu_custom_call" | custom-call | flops 9059696640 | bytes 23592960 | tf_op jit(solution)/shard_map/pallas_call | solution.py:43
  28.0 0.9 collective-permute-done.1.refs_0_
  28.8 8.9 %shard_map.56 = (bf16[208,768]{1,0:T(8,128)(2,1)S(1)}, bf16[208,768]{1,0:T(8,128)(2,1)S(1)}, bf16[208,768]{1,0:T(8,128)(2,1)S(1)}, bf16[208,768]{1,0:T(8,128)(2,1)S(1)}) custom-call(s32[6]{0:T(128)S(1)} %concatenate.4.place, bf16[192,2560]{1,0:T(8,128)(2,1)S(1)} %collective-permute-done.1.refs_0_, bf16[5120,1536]{1,0:T(8,128)(2,1)} %refs_1_.8, ...), custom_call_target="tpu_custom_call" | custom-call | flops 3019898880 | bytes 15728640 | tf_op jit(solution)/shard_map/pallas_call | solution.py:129
  37.8 2.0 %collective-permute-start.4 = (bf16[208,768]{1,0:T(8,128)(2,1)S(1)}, bf16[208,768]{1,0:T(8,128)(2,1)S(1)}, u32[]{:S(2)}, u32[]{:S(2)}) collective-permute-start(bf16[208,768]{1,0:T(8,128)(2,1)S(1)} %get-tuple-element.77.refs_0_.refs_4_), channel_id=1, source_target_pairs={{0,4},{2,6},{4,0},{6,2},{8,12},{10,14},{12,8},{14,10},{16,20},{18,... | collective-permute-start | bytes 958472 | tf_op jit(solution)/shard_map/ppermute | solution.py:19
  39.8 1.6 collective-permute-start.5
  41.4 2.6 %collective-permute-start.7 = (bf16[208,768]{1,0:T(8,128)(2,1)S(1)}, bf16[208,768]{1,0:T(8,128)(2,1)S(1)}, u32[]{:S(2)}, u32[]{:S(2)}) collective-permute-start(bf16[208,768]{1,0:T(8,128)(2,1)S(1)} %get-tuple-element.81), channel_id=1, source_target_pairs={{0,16},{2,18},{4,20},{6,22},{8,24},{10,26},{12,28},{14,30},{16,0},... | collective-permute-start | bytes 958472 | tf_op jit(solution)/shard_map/ppermute | solution.py:19
  44.2 6.0 %shard_map.57 = (bf16[192,384]{1,0:T(8,128)(2,1)S(1)}, bf16[192,384]{1,0:T(8,128)(2,1)S(1)}, bf16[192,384]{1,0:T(8,128)(2,1)S(1)}, bf16[192,384]{1,0:T(8,128)(2,1)S(1)}) custom-call(s32[4]{0:T(128)S(1)} %pad_add_fusion.place, bf16[192,2560]{1,0:T(8,128)(2,1)S(1)} %collective-permute-done.1.refs_0_, bf16[5120,1536]{1,0:T(8,128)(2,1)} %refs_1_.9, ...), custom_call_target="tpu_custom_call" | custom-call | flops 1509949440 | bytes 7864320 | tf_op jit(solution)/shard_map/pallas_call | solution.py:129
  50.2 9.1 %shard_map.58 = (bf16[192,768]{1,0:T(8,128)(2,1)S(1)}, bf16[192,768]{1,0:T(8,128)(2,1)S(1)}, bf16[192,768]{1,0:T(8,128)(2,1)S(1)}, bf16[192,768]{1,0:T(8,128)(2,1)S(1)}) custom-call(s32[4]{0:T(128)S(1)} %pad_add_fusion.place, bf16[192,2560]{1,0:T(8,128)(2,1)S(1)} %collective-permute-done.3.refs_0_, bf16[5120,1536]{1,0:T(8,128)(2,1)} %refs_1_.8, ...), custom_call_target="tpu_custom_call" | custom-call | flops 3019898880 | bytes 15728640 | tf_op jit(solution)/shard_map/pallas_call | solution.py:129
  59.3 6.2 %shard_map.59 = (bf16[192,384]{1,0:T(8,128)(2,1)S(1)}, bf16[192,384]{1,0:T(8,128)(2,1)S(1)}, bf16[192,384]{1,0:T(8,128)(2,1)S(1)}, bf16[192,384]{1,0:T(8,128)(2,1)S(1)}) custom-call(s32[4]{0:T(128)S(1)} %pad_add_fusion.place, bf16[192,2560]{1,0:T(8,128)(2,1)S(1)} %collective-permute-done.3.refs_0_, bf16[5120,1536]{1,0:T(8,128)(2,1)} %refs_1_.9, ...), custom_call_target="tpu_custom_call" | custom-call | flops 1509949440 | bytes 7864320 | tf_op jit(solution)/shard_map/pallas_call | solution.py:129
  65.6 1.4 collective-permute-start.11
  66.9 1.5 collective-permute-start.12
  68.5 0.5 collective-permute-start.6
  69.0 1.5 collective-permute-start.8
  70.5 2.6 %collective-permute-start.15 = (bf16[192,768]{1,0:T(8,128)(2,1)S(1)}, bf16[192,768]{1,0:T(8,128)(2,1)S(1)}, u32[]{:S(2)}, u32[]{:S(2)}) collective-permute-start(bf16[192,768]{1,0:T(8,128)(2,1)S(1)} %get-tuple-element.102), channel_id=1, source_target_pairs={{0,16},{2,18},{4,20},{6,22},{8,24},{10,26},{12,28},{14,30},{16,0},... | collective-permute-start | bytes 884744 | tf_op jit(solution)/shard_map/ppermute | solution.py:19
  73.1 4.3 %collective-permute-done.11.refs_9_ = bf16[192,768]{1,0:T(8,128)(2,1)S(1)} collective-permute-done((bf16[192,768]{1,0:T(8,128)(2,1)S(1)}, bf16[192,768]{1,0:T(8,128)(2,1)S(1)}, u32[]{:S(2)}, u32[]{:S(2)}) %collective-permute-start.11) | collective-permute-done | bytes 294944 | tf_op jit(solution)/shard_map/ppermute | solution.py:19
  77.4 2.5 %collective-permute-start.18 = (bf16[192,768]{1,0:T(8,128)(2,1)S(1)}, bf16[192,768]{1,0:T(8,128)(2,1)S(1)}, u32[]{:S(2)}, u32[]{:S(2)}) collective-permute-start(bf16[192,768]{1,0:T(8,128)(2,1)S(1)} %get-tuple-element.108), channel_id=1, source_target_pairs={{0,24},{2,26},{4,28},{6,30},{8,16},{10,18},{12,20},{14,22},{16,8},... | collective-permute-start | bytes 884744 | tf_op jit(solution)/shard_map/ppermute | solution.py:19
  80.0 2.5 %collective-permute-start.10 = (bf16[208,768]{1,0:T(8,128)(2,1)S(1)}, bf16[208,768]{1,0:T(8,128)(2,1)S(1)}, u32[]{:S(2)}, u32[]{:S(2)}) collective-permute-start(bf16[208,768]{1,0:T(8,128)(2,1)S(1)} %collective-permute-done.9.refs_6_.refs_16_), channel_id=1, source_target_pairs={{0,4},{2,6},{4,0},{6,2},{8,12},{10,14},{12,8},{14,10},{16,20},{18,... | collective-permute-start | bytes 958472 | tf_op jit(solution)/shard_map/ppermute | solution.py:19
  82.5 11.4 %collective-permute-done.15.refs_13_ = bf16[192,768]{1,0:T(8,128)(2,1)S(1)} collective-permute-done((bf16[192,768]{1,0:T(8,128)(2,1)S(1)}, bf16[192,768]{1,0:T(8,128)(2,1)S(1)}, u32[]{:S(2)}, u32[]{:S(2)}) %collective-permute-start.15) | collective-permute-done | bytes 294944 | tf_op jit(solution)/shard_map/ppermute | solution.py:19
  94.0 2.0 %collective-permute-start.22 = (bf16[192,768]{1,0:T(8,128)(2,1)S(1)}, bf16[192,768]{1,0:T(8,128)(2,1)S(1)}, u32[]{:S(2)}, u32[]{:S(2)}) collective-permute-start(bf16[192,768]{1,0:T(8,128)(2,1)S(1)} %collective-permute-done.15.refs_13_), channel_id=1, source_target_pairs={{0,4},{2,6},{4,0},{6,2},{8,12},{10,14},{12,8},{14,10},{16,20},{18,... | collective-permute-start | bytes 884744 | tf_op jit(solution)/shard_map/ppermute | solution.py:19
  96.1 1.3 collective-permute-done.10.refs_7_.refs_18_
  97.4 4.6 %collective-permute-start.16 = (bf16[192,384]{1,0:T(8,128)(2,1)S(1)}, bf16[192,384]{1,0:T(8,128)(2,1)S(1)}, u32[]{:S(2)}, u32[]{:S(2)}) collective-permute-start(bf16[192,384]{1,0:T(8,128)(2,1)S(1)} %get-tuple-element.103), channel_id=1, source_target_pairs={{0,16},{2,18},{4,20},{6,22},{8,24},{10,26},{12,28},{14,30},{16,0},... | collective-permute-start | bytes 442376 | tf_op jit(solution)/shard_map/ppermute | solution.py:19
  102.1 1.4 collective-permute-start.19
  103.5 0.7 shard_map.60.table
  104.2 0.6 copy-done.10
  104.8 6.6 %collective-permute-done.16.refs_2_ = bf16[192,384]{1,0:T(8,128)(2,1)S(1)} collective-permute-done((bf16[192,384]{1,0:T(8,128)(2,1)S(1)}, bf16[192,384]{1,0:T(8,128)(2,1)S(1)}, u32[]{:S(2)}, u32[]{:S(2)}) %collective-permute-start.16) | collective-permute-done | bytes 147488 | tf_op jit(solution)/shard_map/ppermute | solution.py:19
  111.4 2.2 %collective-permute-start.17 = (bf16[192,384]{1,0:T(8,128)(2,1)S(1)}, bf16[192,384]{1,0:T(8,128)(2,1)S(1)}, u32[]{:S(2)}, u32[]{:S(2)}) collective-permute-start(bf16[192,384]{1,0:T(8,128)(2,1)S(1)} %get-tuple-element.104), channel_id=1, source_target_pairs={{0,16},{2,18},{4,20},{6,22},{8,24},{10,26},{12,28},{14,30},{16,0},... | collective-permute-start | bytes 442376 | tf_op jit(solution)/shard_map/ppermute | solution.py:19
  113.6 2.9 %collective-permute-start.20 = (bf16[192,384]{1,0:T(8,128)(2,1)S(1)}, bf16[192,384]{1,0:T(8,128)(2,1)S(1)}, u32[]{:S(2)}, u32[]{:S(2)}) collective-permute-start(bf16[192,384]{1,0:T(8,128)(2,1)S(1)} %get-tuple-element.110), channel_id=1, source_target_pairs={{0,24},{2,26},{4,28},{6,30},{8,16},{10,18},{12,20},{14,22},{16,8},... | collective-permute-start | bytes 442376 | tf_op jit(solution)/shard_map/ppermute | solution.py:19
  116.6 0.6 copy-done.19
  117.2 0.7 copy-done.20
  117.9 13.5 %shard_map.62 = (bf16[192,384]{1,0:T(8,128)(2,1)}, bf16[192,384]{1,0:T(8,128)(2,1)}, bf16[192,384]{1,0:T(8,128)(2,1)}, bf16[192,384]{1,0:T(8,128)(2,1)}) custom-call(s32[16]{0:T(128)} %copy-done.10, bf16[192,384]{1,0:T(8,128)(2,1)} %copy-done.13, bf16[192,384]{1,0:T(8,128)(2,1)} %copy-done.22, bf16[192,384]{1,0:T(8,128)(2,1)} %copy-done.25, ...), custom_call_target="tpu_custom_call" | custom-call | flops 2717908992 | bytes 5898240 | tf_op jit(solution)/shard_map/pallas_call | solution.py:280
  131.4 0.9 collective-permute-start.28
  132.3 1.6 collective-permute-start.29
  133.9 1.9 %collective-permute-start.30 = (bf16[192,384]{1,0:T(8,128)(2,1)}, bf16[192,384]{1,0:T(8,128)(2,1)S(1)}, u32[]{:S(2)}, u32[]{:S(2)}) collective-permute-start(bf16[192,384]{1,0:T(8,128)(2,1)} %get-tuple-element.118), channel_id=1, source_target_pairs={{0,24},{2,26},{4,28},{6,30},{8,16},{10,18},{12,20},{14,22},{16,8},... | collective-permute-start | bytes 442376 | tf_op jit(solution)/shard_map/ppermute | solution.py:19
  135.9 0.6 copy-done.23
  136.5 0.7 copy-done.24
  137.2 13.7 %shard_map.61 = (bf16[192,384]{1,0:T(8,128)(2,1)}, bf16[192,384]{1,0:T(8,128)(2,1)}, bf16[192,384]{1,0:T(8,128)(2,1)}, bf16[192,384]{1,0:T(8,128)(2,1)}) custom-call(s32[16]{0:T(128)} %copy-done.10, bf16[192,384]{1,0:T(8,128)(2,1)} %copy-done.12, bf16[192,384]{1,0:T(8,128)(2,1)} %copy-done.21, bf16[192,384]{1,0:T(8,128)(2,1)} %copy-done.23, ...), custom_call_target="tpu_custom_call" | custom-call | flops 2717908992 | bytes 5898240 | tf_op jit(solution)/shard_map/pallas_call | solution.py:280
  151.2 2.1 %collective-permute-start.26 = (bf16[192,384]{1,0:T(8,128)(2,1)}, bf16[192,384]{1,0:T(8,128)(2,1)S(1)}, u32[]{:S(2)}, u32[]{:S(2)}) collective-permute-start(bf16[192,384]{1,0:T(8,128)(2,1)} %get-tuple-element.113), channel_id=1, source_target_pairs={{0,18},{2,16},{4,22},{6,20},{8,26},{10,24},{12,30},{14,28},{16,2},... | collective-permute-start | bytes 442376 | tf_op jit(solution)/shard_map/ppermute | solution.py:19
  153.2 2.0 %collective-permute-start.27 = (bf16[192,384]{1,0:T(8,128)(2,1)}, bf16[192,384]{1,0:T(8,128)(2,1)S(1)}, u32[]{:S(2)}, u32[]{:S(2)}) collective-permute-start(bf16[192,384]{1,0:T(8,128)(2,1)} %get-tuple-element.114), channel_id=1, source_target_pairs={{0,26},{2,24},{4,30},{6,28},{8,18},{10,16},{12,22},{14,20},{16,10}... | collective-permute-start | bytes 442376 | tf_op jit(solution)/shard_map/ppermute | solution.py:19
  155.2 2.0 %shard_map.63.refs_4_ = bf16[2,192,1536]{2,1,0:T(8,128)(2,1)} custom-call(s32[4]{0:T(128)S(1)} %pad_add_fusion.place, bf16[192,384]{1,0:T(8,128)(2,1)S(1)} %copy-done.9, bf16[192,384]{1,0:T(8,128)(2,1)S(1)} %collective-permute-done.28.refs_1_, bf16[192,384]{1,0:T(8,128)(2,1)S(1)} %collective-permute-done.29.refs_2_, ...), custom_call_target="tpu_custom_call" | custom-call | tf_op jit(solution)/shard_map/pallas_call | solution.py:348
  157.2 2.5 %collective-permute-done.25.refs_1_ = bf16[192,384]{1,0:T(8,128)(2,1)S(1)} collective-permute-done((bf16[192,384]{1,0:T(8,128)(2,1)}, bf16[192,384]{1,0:T(8,128)(2,1)S(1)}, u32[]{:S(2)}, u32[]{:S(2)}) %collective-permute-start.25) | collective-permute-done | bytes 147488 | tf_op jit(solution)/shard_map/ppermute | solution.py:19
  159.8 4.4 %collective-permute-done.27.refs_3_ = bf16[192,384]{1,0:T(8,128)(2,1)S(1)} collective-permute-done((bf16[192,384]{1,0:T(8,128)(2,1)}, bf16[192,384]{1,0:T(8,128)(2,1)S(1)}, u32[]{:S(2)}, u32[]{:S(2)}) %collective-permute-start.27) | collective-permute-done | bytes 147488 | tf_op jit(solution)/shard_map/ppermute | solution.py:19
  164.2 2.0 %shard_map.64 = bf16[2,192,1536]{2,1,0:T(8,128)(2,1)} custom-call(s32[4]{0:T(128)S(1)} %pad_add_fusion.place, bf16[192,384]{1,0:T(8,128)(2,1)S(1)} %collective-permute-done.24.refs_0_, bf16[192,384]{1,0:T(8,128)(2,1)S(1)} %collective-permute-done.25.refs_1_, bf16[192,384]{1,0:T(8,128)(2,1)S(1)} %collective-permute-done.26.refs_2_, ...), custom_call_target="tpu_custom_call", output_to_operand_aliasing={{}: (5, {})} | custom-call | tf_op jit(solution)/shard_map/pallas_call | solution.py:348
  (87 shorter events, 1.8 us)
Async XLA Ops:
  0.0 10.3 %copy-start = (bf16[2,192,2560]{2,1,0:T(8,128)(2,1)S(1)}, bf16[2,192,2560]{2,1,0:T(8,128)(2,1)}, u32[]{:S(2)}) copy-start(bf16[2,192,2560]{2,1,0:T(8,128)(2,1)} %mine_ref.1) | copy-start | bytes 5898244
  3.1 6.5 %collective-permute-start.2 = (bf16[192,2560]{1,0:T(8,128)(2,1)}, bf16[192,2560]{1,0:T(8,128)(2,1)}, u32[]{:S(2)}, u32[]{:S(2)}) collective-permute-start(bf16[192,2560]{1,0:T(8,128)(2,1)} %get-tuple-element.119), channel_id=1, source_target_pairs={{0,2},{2,0},{4,6},{6,4},{8,10},{10,8},{12,14},{14,12},{16,18},{18,... | collective-permute-start | bytes 2949128 | tf_op jit(solution)/shard_map/ppermute | solution.py:19
  3.5 25.3 %collective-permute-start.1 = (bf16[192,2560]{1,0:T(8,128)(2,1)}, bf16[192,2560]{1,0:T(8,128)(2,1)S(1)}, u32[]{:S(2)}, u32[]{:S(2)}) collective-permute-start(bf16[192,2560]{1,0:T(8,128)(2,1)} %get-tuple-element.120), channel_id=1, source_target_pairs={{0,1},{1,0},{2,3},{3,2},{4,5},{5,4},{6,7},{7,6},{8,9},{9,8},{10,11... | collective-permute-start | bytes 2949128 | tf_op jit(solution)/shard_map/ppermute | solution.py:19
  6.9 1.3 collective-permute-start
  9.6 40.6 %collective-permute-start.3 = (bf16[192,2560]{1,0:T(8,128)(2,1)}, bf16[192,2560]{1,0:T(8,128)(2,1)S(1)}, u32[]{:S(2)}, u32[]{:S(2)}) collective-permute-start(bf16[192,2560]{1,0:T(8,128)(2,1)} %collective-permute-done.2.other_ref), channel_id=1, source_target_pairs={{0,1},{1,0},{2,3},{3,2},{4,5},{5,4},{6,7},{7,6},{8,9},{9,8},{10,11... | collective-permute-start | bytes 2949128 | tf_op jit(solution)/shard_map/ppermute | solution.py:19
  37.8 65.7 %copy-start.1 = (bf16[208,768]{1,0:T(8,128)(2,1)}, bf16[208,768]{1,0:T(8,128)(2,1)S(1)}, u32[]{:S(2)}) copy-start(bf16[208,768]{1,0:T(8,128)(2,1)S(1)} %get-tuple-element.77.refs_0_.refs_4_) | copy-start | bytes 958468
  37.8 27.8 %collective-permute-start.4 = (bf16[208,768]{1,0:T(8,128)(2,1)S(1)}, bf16[208,768]{1,0:T(8,128)(2,1)S(1)}, u32[]{:S(2)}, u32[]{:S(2)}) collective-permute-start(bf16[208,768]{1,0:T(8,128)(2,1)S(1)} %get-tuple-element.77.refs_0_.refs_4_), channel_id=1, source_target_pairs={{0,4},{2,6},{4,0},{6,2},{8,12},{10,14},{12,8},{14,10},{16,20},{18,... | collective-permute-start | bytes 958472 | tf_op jit(solution)/shard_map/ppermute | solution.py:19
  39.8 25.7 %collective-permute-start.5 = (bf16[208,768]{1,0:T(8,128)(2,1)S(1)}, bf16[208,768]{1,0:T(8,128)(2,1)S(1)}, u32[]{:S(2)}, u32[]{:S(2)}) collective-permute-start(bf16[208,768]{1,0:T(8,128)(2,1)S(1)} %get-tuple-element.78), channel_id=1, source_target_pairs={{0,8},{2,10},{4,12},{6,14},{8,0},{10,2},{12,4},{14,6},{16,24},{18,... | collective-permute-start | bytes 958472 | tf_op jit(solution)/shard_map/ppermute | solution.py:19
  41.4 27.6 %collective-permute-start.7 = (bf16[208,768]{1,0:T(8,128)(2,1)S(1)}, bf16[208,768]{1,0:T(8,128)(2,1)S(1)}, u32[]{:S(2)}, u32[]{:S(2)}) collective-permute-start(bf16[208,768]{1,0:T(8,128)(2,1)S(1)} %get-tuple-element.81), channel_id=1, source_target_pairs={{0,16},{2,18},{4,20},{6,22},{8,24},{10,26},{12,28},{14,30},{16,0},... | collective-permute-start | bytes 958472 | tf_op jit(solution)/shard_map/ppermute | solution.py:19
  44.0 26.5 %collective-permute-start.9 = (bf16[208,768]{1,0:T(8,128)(2,1)S(1)}, bf16[208,768]{1,0:T(8,128)(2,1)S(1)}, u32[]{:S(2)}, u32[]{:S(2)}) collective-permute-start(bf16[208,768]{1,0:T(8,128)(2,1)S(1)} %get-tuple-element.84), channel_id=1, source_target_pairs={{0,24},{2,26},{4,28},{6,30},{8,16},{10,18},{12,20},{14,22},{16,8},... | collective-permute-start | bytes 958472 | tf_op jit(solution)/shard_map/ppermute | solution.py:19
  50.2 9.1 %copy-start.13 = (bf16[192,384]{1,0:T(8,128)(2,1)}, bf16[192,384]{1,0:T(8,128)(2,1)S(1)}, u32[]{:S(2)}) copy-start(bf16[192,384]{1,0:T(8,128)(2,1)S(1)} %get-tuple-element.91.refs_0_) | copy-start | bytes 442372
  65.5 38.7 %copy-start.12 = (bf16[192,384]{1,0:T(8,128)(2,1)}, bf16[192,384]{1,0:T(8,128)(2,1)S(1)}, u32[]{:S(2)}) copy-start(bf16[192,384]{1,0:T(8,128)(2,1)S(1)} %get-tuple-element.92.refs_0_) | copy-start | bytes 442372
  65.5 51.0 %copy-start.3 = (bf16[208,768]{1,0:T(8,128)(2,1)}, bf16[208,768]{1,0:T(8,128)(2,1)S(1)}, u32[]{:S(2)}) copy-start(bf16[208,768]{1,0:T(8,128)(2,1)S(1)} %collective-permute-done.5.refs_2_.refs_8_) | copy-start | bytes 958468
  65.6 50.9 %copy-start.2 = (bf16[208,768]{1,0:T(8,128)(2,1)}, bf16[208,768]{1,0:T(8,128)(2,1)S(1)}, u32[]{:S(2)}) copy-start(bf16[208,768]{1,0:T(8,128)(2,1)S(1)} %collective-permute-done.4.refs_1_.refs_6_) | copy-start | bytes 958468
  65.6 11.9 %collective-permute-start.11 = (bf16[192,768]{1,0:T(8,128)(2,1)S(1)}, bf16[192,768]{1,0:T(8,128)(2,1)S(1)}, u32[]{:S(2)}, u32[]{:S(2)}) collective-permute-start(bf16[192,768]{1,0:T(8,128)(2,1)S(1)} %get-tuple-element.96), channel_id=1, source_target_pairs={{0,8},{2,10},{4,12},{6,14},{8,0},{10,2},{12,4},{14,6},{16,24},{18,... | collective-permute-start | bytes 884744 | tf_op jit(solution)/shard_map/ppermute | solution.py:19
  66.9 13.0 %collective-permute-start.12 = (bf16[192,768]{1,0:T(8,128)(2,1)S(1)}, bf16[192,768]{1,0:T(8,128)(2,1)S(1)}, u32[]{:S(2)}, u32[]{:S(2)}) collective-permute-start(bf16[192,768]{1,0:T(8,128)(2,1)S(1)} %get-tuple-element.90.refs_5_), channel_id=1, source_target_pairs={{0,4},{2,6},{4,0},{6,2},{8,12},{10,14},{12,8},{14,10},{16,20},{18,... | collective-permute-start | bytes 884744 | tf_op jit(solution)/shard_map/ppermute | solution.py:19
  68.5 25.5 %collective-permute-start.6 = (bf16[208,768]{1,0:T(8,128)(2,1)S(1)}, bf16[208,768]{1,0:T(8,128)(2,1)S(1)}, u32[]{:S(2)}, u32[]{:S(2)}) collective-permute-start(bf16[208,768]{1,0:T(8,128)(2,1)S(1)} %collective-permute-done.5.refs_2_.refs_8_), channel_id=1, source_target_pairs={{0,4},{2,6},{4,0},{6,2},{8,12},{10,14},{12,8},{14,10},{16,20},{18,... | collective-permute-start | bytes 958472 | tf_op jit(solution)/shard_map/ppermute | solution.py:19
  69.0 47.5 %copy-start.4 = (bf16[208,768]{1,0:T(8,128)(2,1)}, bf16[208,768]{1,0:T(8,128)(2,1)S(1)}, u32[]{:S(2)}) copy-start(bf16[208,768]{1,0:T(8,128)(2,1)S(1)} %collective-permute-done.7.refs_4_.refs_12_) | copy-start | bytes 958468
  69.0 27.0 %collective-permute-start.8 = (bf16[208,768]{1,0:T(8,128)(2,1)S(1)}, bf16[208,768]{1,0:T(8,128)(2,1)S(1)}, u32[]{:S(2)}, u32[]{:S(2)}) collective-permute-start(bf16[208,768]{1,0:T(8,128)(2,1)S(1)} %collective-permute-done.7.refs_4_.refs_12_), channel_id=1, source_target_pairs={{0,4},{2,6},{4,0},{6,2},{8,12},{10,14},{12,8},{14,10},{16,20},{18,... | collective-permute-start | bytes 958472 | tf_op jit(solution)/shard_map/ppermute | solution.py:19
  70.5 46.0 %copy-start.5 = (bf16[208,768]{1,0:T(8,128)(2,1)}, bf16[208,768]{1,0:T(8,128)(2,1)S(1)}, u32[]{:S(2)}) copy-start(bf16[208,768]{1,0:T(8,128)(2,1)S(1)} %collective-permute-done.9.refs_6_.refs_16_) | copy-start | bytes 958468
  70.5 23.4 %collective-permute-start.15 = (bf16[192,768]{1,0:T(8,128)(2,1)S(1)}, bf16[192,768]{1,0:T(8,128)(2,1)S(1)}, u32[]{:S(2)}, u32[]{:S(2)}) collective-permute-start(bf16[192,768]{1,0:T(8,128)(2,1)S(1)} %get-tuple-element.102), channel_id=1, source_target_pairs={{0,16},{2,18},{4,20},{6,22},{8,24},{10,26},{12,28},{14,30},{16,0},... | collective-permute-start | bytes 884744 | tf_op jit(solution)/shard_map/ppermute | solution.py:19
  77.4 39.1 %copy-start.14 = (bf16[192,768]{1,0:T(8,128)(2,1)}, bf16[192,768]{1,0:T(8,128)(2,1)S(1)}, u32[]{:S(2)}) copy-start(bf16[192,768]{1,0:T(8,128)(2,1)S(1)} %collective-permute-done.11.refs_9_) | copy-start | bytes 884740
  77.4 16.5 %collective-permute-start.18 = (bf16[192,768]{1,0:T(8,128)(2,1)S(1)}, bf16[192,768]{1,0:T(8,128)(2,1)S(1)}, u32[]{:S(2)}, u32[]{:S(2)}) collective-permute-start(bf16[192,768]{1,0:T(8,128)(2,1)S(1)} %get-tuple-element.108), channel_id=1, source_target_pairs={{0,24},{2,26},{4,28},{6,30},{8,16},{10,18},{12,20},{14,22},{16,8},... | collective-permute-start | bytes 884744 | tf_op jit(solution)/shard_map/ppermute | solution.py:19
  80.0 36.6 %copy-start.15 = (bf16[192,768]{1,0:T(8,128)(2,1)}, bf16[192,768]{1,0:T(8,128)(2,1)S(1)}, u32[]{:S(2)}) copy-start(bf16[192,768]{1,0:T(8,128)(2,1)S(1)} %collective-permute-done.12.refs_7_) | copy-start | bytes 884740
  80.0 17.5 %collective-permute-start.10 = (bf16[208,768]{1,0:T(8,128)(2,1)S(1)}, bf16[208,768]{1,0:T(8,128)(2,1)S(1)}, u32[]{:S(2)}, u32[]{:S(2)}) collective-permute-start(bf16[208,768]{1,0:T(8,128)(2,1)S(1)} %collective-permute-done.9.refs_6_.refs_16_), channel_id=1, source_target_pairs={{0,4},{2,6},{4,0},{6,2},{8,12},{10,14},{12,8},{14,10},{16,20},{18,... | collective-permute-start | bytes 958472 | tf_op jit(solution)/shard_map/ppermute | solution.py:19
  93.9 22.7 %copy-start.16 = (bf16[192,768]{1,0:T(8,128)(2,1)}, bf16[192,768]{1,0:T(8,128)(2,1)S(1)}, u32[]{:S(2)}) copy-start(bf16[192,768]{1,0:T(8,128)(2,1)S(1)} %collective-permute-done.15.refs_13_) | copy-start | bytes 884740
  93.9 8.2 %collective-permute-start.13 = (bf16[192,384]{1,0:T(8,128)(2,1)S(1)}, bf16[192,384]{1,0:T(8,128)(2,1)S(1)}, u32[]{:S(2)}, u32[]{:S(2)}) collective-permute-start(bf16[192,384]{1,0:T(8,128)(2,1)S(1)} %get-tuple-element.97), channel_id=1, source_target_pairs={{0,8},{2,10},{4,12},{6,14},{8,0},{10,2},{12,4},{14,6},{16,24},{18,... | collective-permute-start | bytes 442376 | tf_op jit(solution)/shard_map/ppermute | solution.py:19
  93.9 22.7 %copy-start.17 = (bf16[192,768]{1,0:T(8,128)(2,1)}, bf16[192,768]{1,0:T(8,128)(2,1)S(1)}, u32[]{:S(2)}) copy-start(bf16[192,768]{1,0:T(8,128)(2,1)S(1)} %collective-permute-done.18.refs_17_) | copy-start | bytes 884740
  93.9 19.6 %collective-permute-start.21 = (bf16[192,768]{1,0:T(8,128)(2,1)S(1)}, bf16[192,768]{1,0:T(8,128)(2,1)S(1)}, u32[]{:S(2)}, u32[]{:S(2)}) collective-permute-start(bf16[192,768]{1,0:T(8,128)(2,1)S(1)} %collective-permute-done.11.refs_9_), channel_id=1, source_target_pairs={{0,4},{2,6},{4,0},{6,2},{8,12},{10,14},{12,8},{14,10},{16,20},{18,... | collective-permute-start | bytes 884744 | tf_op jit(solution)/shard_map/ppermute | solution.py:19
  94.0 22.6 %copy-start.6 = (bf16[208,768]{1,0:T(8,128)(2,1)}, bf16[208,768]{1,0:T(8,128)(2,1)S(1)}, u32[]{:S(2)}) copy-start(bf16[208,768]{1,0:T(8,128)(2,1)S(1)} %collective-permute-done.6.refs_3_.refs_10_) | copy-start | bytes 958468
  94.0 22.5 %collective-permute-start.22 = (bf16[192,768]{1,0:T(8,128)(2,1)S(1)}, bf16[192,768]{1,0:T(8,128)(2,1)S(1)}, u32[]{:S(2)}, u32[]{:S(2)}) collective-permute-start(bf16[192,768]{1,0:T(8,128)(2,1)S(1)} %collective-permute-done.15.refs_13_), channel_id=1, source_target_pairs={{0,4},{2,6},{4,0},{6,2},{8,12},{10,14},{12,8},{14,10},{16,20},{18,... | collective-permute-start | bytes 884744 | tf_op jit(solution)/shard_map/ppermute | solution.py:19
  96.0 20.6 %copy-start.7 = (bf16[208,768]{1,0:T(8,128)(2,1)}, bf16[208,768]{1,0:T(8,128)(2,1)S(1)}, u32[]{:S(2)}) copy-start(bf16[208,768]{1,0:T(8,128)(2,1)S(1)} %collective-permute-done.8.refs_5_.refs_14_) | copy-start | bytes 958468
  96.0 20.5 %collective-permute-start.23 = (bf16[192,768]{1,0:T(8,128)(2,1)S(1)}, bf16[192,768]{1,0:T(8,128)(2,1)S(1)}, u32[]{:S(2)}, u32[]{:S(2)}) collective-permute-start(bf16[192,768]{1,0:T(8,128)(2,1)S(1)} %collective-permute-done.18.refs_17_), channel_id=1, source_target_pairs={{0,4},{2,6},{4,0},{6,2},{8,12},{10,14},{12,8},{14,10},{16,20},{18,... | collective-permute-start | bytes 884744 | tf_op jit(solution)/shard_map/ppermute | solution.py:19
  97.4 19.2 %copy-start.8 = (bf16[208,768]{1,0:T(8,128)(2,1)}, bf16[208,768]{1,0:T(8,128)(2,1)S(1)}, u32[]{:S(2)}) copy-start(bf16[208,768]{1,0:T(8,128)(2,1)S(1)} %collective-permute-done.10.refs_7_.refs_18_) | copy-start | bytes 958468
  97.4 13.9 %collective-permute-start.16 = (bf16[192,384]{1,0:T(8,128)(2,1)S(1)}, bf16[192,384]{1,0:T(8,128)(2,1)S(1)}, u32[]{:S(2)}, u32[]{:S(2)}) collective-permute-start(bf16[192,384]{1,0:T(8,128)(2,1)S(1)} %get-tuple-element.103), channel_id=1, source_target_pairs={{0,16},{2,18},{4,20},{6,22},{8,24},{10,26},{12,28},{14,30},{16,0},... | collective-permute-start | bytes 442376 | tf_op jit(solution)/shard_map/ppermute | solution.py:19
  102.1 14.5 %copy-start.22 = (bf16[192,384]{1,0:T(8,128)(2,1)}, bf16[192,384]{1,0:T(8,128)(2,1)S(1)}, u32[]{:S(2)}) copy-start(bf16[192,384]{1,0:T(8,128)(2,1)S(1)} %collective-permute-done.13.refs_1_) | copy-start | bytes 442372
  102.1 9.3 %collective-permute-start.19 = (bf16[192,384]{1,0:T(8,128)(2,1)S(1)}, bf16[192,384]{1,0:T(8,128)(2,1)S(1)}, u32[]{:S(2)}, u32[]{:S(2)}) collective-permute-start(bf16[192,384]{1,0:T(8,128)(2,1)S(1)} %get-tuple-element.109), channel_id=1, source_target_pairs={{0,24},{2,26},{4,28},{6,30},{8,16},{10,18},{12,20},{14,22},{16,8},... | collective-permute-start | bytes 442376 | tf_op jit(solution)/shard_map/ppermute | solution.py:19
  111.4 22.6 %collective-permute-start.14 = (bf16[192,384]{1,0:T(8,128)(2,1)S(1)}, bf16[192,384]{1,0:T(8,128)(2,1)S(1)}, u32[]{:S(2)}, u32[]{:S(2)}) collective-permute-start(bf16[192,384]{1,0:T(8,128)(2,1)S(1)} %get-tuple-element.98), channel_id=1, source_target_pairs={{0,8},{2,10},{4,12},{6,14},{8,0},{10,2},{12,4},{14,6},{16,24},{18,... | collective-permute-start | bytes 442376 | tf_op jit(solution)/shard_map/ppermute | solution.py:19
  111.4 24.5 %collective-permute-start.17 = (bf16[192,384]{1,0:T(8,128)(2,1)S(1)}, bf16[192,384]{1,0:T(8,128)(2,1)S(1)}, u32[]{:S(2)}, u32[]{:S(2)}) collective-permute-start(bf16[192,384]{1,0:T(8,128)(2,1)S(1)} %get-tuple-element.104), channel_id=1, source_target_pairs={{0,16},{2,18},{4,20},{6,22},{8,24},{10,26},{12,28},{14,30},{16,0},... | collective-permute-start | bytes 442376 | tf_op jit(solution)/shard_map/ppermute | solution.py:19
  113.6 22.3 %collective-permute-start.20 = (bf16[192,384]{1,0:T(8,128)(2,1)S(1)}, bf16[192,384]{1,0:T(8,128)(2,1)S(1)}, u32[]{:S(2)}, u32[]{:S(2)}) collective-permute-start(bf16[192,384]{1,0:T(8,128)(2,1)S(1)} %get-tuple-element.110), channel_id=1, source_target_pairs={{0,24},{2,26},{4,28},{6,30},{8,16},{10,18},{12,20},{14,22},{16,8},... | collective-permute-start | bytes 442376 | tf_op jit(solution)/shard_map/ppermute | solution.py:19
  131.4 19.8 %collective-permute-start.28 = (bf16[192,384]{1,0:T(8,128)(2,1)}, bf16[192,384]{1,0:T(8,128)(2,1)S(1)}, u32[]{:S(2)}, u32[]{:S(2)}) collective-permute-start(bf16[192,384]{1,0:T(8,128)(2,1)} %get-tuple-element.116), channel_id=1, source_target_pairs={{0,8},{2,10},{4,12},{6,14},{8,0},{10,2},{12,4},{14,6},{16,24},{18,... | collective-permute-start | bytes 442376 | tf_op jit(solution)/shard_map/ppermute | solution.py:19
  132.3 20.9 %collective-permute-start.29 = (bf16[192,384]{1,0:T(8,128)(2,1)}, bf16[192,384]{1,0:T(8,128)(2,1)S(1)}, u32[]{:S(2)}, u32[]{:S(2)}) collective-permute-start(bf16[192,384]{1,0:T(8,128)(2,1)} %get-tuple-element.117), channel_id=1, source_target_pairs={{0,16},{2,18},{4,20},{6,22},{8,24},{10,26},{12,28},{14,30},{16,0},... | collective-permute-start | bytes 442376 | tf_op jit(solution)/shard_map/ppermute | solution.py:19
  133.9 21.3 %copy-start.9 = (bf16[192,384]{1,0:T(8,128)(2,1)S(1)}, bf16[192,384]{1,0:T(8,128)(2,1)}, u32[]{:S(2)}) copy-start(bf16[192,384]{1,0:T(8,128)(2,1)} %get-tuple-element.115.refs_0_) | copy-start | bytes 442372
  133.9 21.3 %collective-permute-start.30 = (bf16[192,384]{1,0:T(8,128)(2,1)}, bf16[192,384]{1,0:T(8,128)(2,1)S(1)}, u32[]{:S(2)}, u32[]{:S(2)}) collective-permute-start(bf16[192,384]{1,0:T(8,128)(2,1)} %get-tuple-element.118), channel_id=1, source_target_pairs={{0,24},{2,26},{4,28},{6,30},{8,16},{10,18},{12,20},{14,22},{16,8},... | collective-permute-start | bytes 442376 | tf_op jit(solution)/shard_map/ppermute | solution.py:19
  150.9 6.3 %collective-permute-start.24 = (bf16[192,384]{1,0:T(8,128)(2,1)}, bf16[192,384]{1,0:T(8,128)(2,1)S(1)}, u32[]{:S(2)}, u32[]{:S(2)}) collective-permute-start(bf16[192,384]{1,0:T(8,128)(2,1)} %get-tuple-element.111), channel_id=1, source_target_pairs={{0,2},{2,0},{4,6},{6,4},{8,10},{10,8},{12,14},{14,12},{16,18},{18,... | collective-permute-start | bytes 442376 | tf_op jit(solution)/shard_map/ppermute | solution.py:19
  151.0 8.8 %collective-permute-start.25 = (bf16[192,384]{1,0:T(8,128)(2,1)}, bf16[192,384]{1,0:T(8,128)(2,1)S(1)}, u32[]{:S(2)}, u32[]{:S(2)}) collective-permute-start(bf16[192,384]{1,0:T(8,128)(2,1)} %get-tuple-element.112), channel_id=1, source_target_pairs={{0,10},{2,8},{4,14},{6,12},{8,2},{10,0},{12,6},{14,4},{16,26},{18,... | collective-permute-start | bytes 442376 | tf_op jit(solution)/shard_map/ppermute | solution.py:19
  151.2 8.6 %collective-permute-start.26 = (bf16[192,384]{1,0:T(8,128)(2,1)}, bf16[192,384]{1,0:T(8,128)(2,1)S(1)}, u32[]{:S(2)}, u32[]{:S(2)}) collective-permute-start(bf16[192,384]{1,0:T(8,128)(2,1)} %get-tuple-element.113), channel_id=1, source_target_pairs={{0,18},{2,16},{4,22},{6,20},{8,26},{10,24},{12,30},{14,28},{16,2},... | collective-permute-start | bytes 442376 | tf_op jit(solution)/shard_map/ppermute | solution.py:19
  153.2 10.9 %collective-permute-start.27 = (bf16[192,384]{1,0:T(8,128)(2,1)}, bf16[192,384]{1,0:T(8,128)(2,1)S(1)}, u32[]{:S(2)}, u32[]{:S(2)}) collective-permute-start(bf16[192,384]{1,0:T(8,128)(2,1)} %get-tuple-element.114), channel_id=1, source_target_pairs={{0,26},{2,24},{4,30},{6,28},{8,18},{10,16},{12,22},{14,20},{16,10}... | collective-permute-start | bytes 442376 | tf_op jit(solution)/shard_map/ppermute | solution.py:19
  (11 other events, 32.5 us)

commit v11 on v9

--- a/solution.py
+++ b/solution.py
@@ -12,6 +12,7 @@
 LOG2_E = 1.4426950408889634
 HIDDEN = -1e30
 VMEM_LIMIT = 44 * 2**20
+ATTEND_LIMIT = 56 * 2**20
 
 
 def exchange(value, axis, size, bit):
@@ -152,7 +153,7 @@
 
 def attend_body(block, ways, slots, arrays, spans, tile, table, *refs):
     count = len(slots)
-    query_refs = refs[:ways]
+    query_refs = refs[:ways][::-1]
     block_refs = refs[ways : ways + arrays]
     out_refs = refs[ways + arrays : 2 * ways + arrays]
     ordered, asked, scores, highest, sums, total, position, sems = refs[2 * ways + arrays :]
@@ -161,18 +162,18 @@
     heads = width // HD
     rest = count // ways
 
-    copies = []
+    copies = [[], []]
     for slot, (offset, array, row) in enumerate(slots):
         low = table[offset]
         for part, span in ((0, low), (1, spans - 1 - low)):
-            copies.append(
+            copies[part].append(
                 pltpu.make_async_copy(
                     block_refs[array].at[pl.ds(row + part * half, half)],
                     ordered.at[pl.ds(pl.multiple_of(span * half, 16), half)],
                     sems.at[2 * slot + part],
                 )
             )
-    for copy in copies:
+    for copy in copies[0] + copies[1]:
         copy.start()
 
     from_lane = lax.broadcasted_iota(jnp.int32, (half, 128), 0) - lax.broadcasted_iota(
@@ -184,7 +185,7 @@
         for part, span in ((0, low), (1, spans - 1 - low)):
             asked[part, here] = query_refs[a][part * half : (part + 1) * half]
             position[part, here] = from_lane + span * half
-    for copy in copies:
+    for copy in copies[0]:
         copy.wait()
 
     slope = LOG2_E / math.sqrt(HD)
@@ -201,6 +202,9 @@
 
     def score_tile(unit, slot, start):
         part, h = unit
+        if unit == (1, 0) and start == middle:
+            for copy in copies[1]:
+                copy.wait()
         scores[slot, :, start : start + tile] = lax.dot_general(
             asked[part, :, h * HD : (h + 1) * HD],
             ordered[start : start + tile, h * HD : (h + 1) * HD],
@@ -260,7 +264,7 @@
     ways, count = len(queries), len(blocks)
     arrays = []
     slots = []
-    for offset in sorted(blocks):
+    for offset in sorted(blocks, reverse=True):
         array, row = blocks[offset]
         if not any(array is other for other in arrays):
             arrays.append(array)
@@ -291,13 +295,13 @@
             pltpu.VMEM((2, many, 128), jnp.int32),
             pltpu.SemaphoreType.DMA((2 * count,)),
         ],
-        compiler_params=pltpu.CompilerParams(vmem_limit_bytes=VMEM_LIMIT),
+        compiler_params=pltpu.CompilerParams(vmem_limit_bytes=ATTEND_LIMIT),
         cost_estimate=pl.CostEstimate(
             flops=flops,
             bytes_accessed=4 * length * width + 4 * ways * rows * width,
             transcendentals=flops // (4 * HD),
         ),
-    )(table, *queries, *arrays)
+    )(table, *queries[::-1], *arrays)
 
 
 def table_body(offsets, *refs):
@@ -309,7 +313,7 @@
 
 
 def span_table(blocks, rows):
-    offsets = sorted(blocks)
+    offsets = sorted(blocks, reverse=True)
     return pl.pallas_call(
         functools.partial(table_body, offsets),
         out_shape=jax.ShapeDtypeStruct((2 * len(offsets),), jnp.int32),
@@ -328,14 +332,14 @@
 
         @pl.when(pl.program_id(0) == a)
         def _():
-            refs[-1][0] = refs[a][...]
+            refs[-1][0] = refs[ways - 1 - a][...]
 
 
 def assemble(pieces, b, before, place):
     ways = len(pieces)
     rows, width = pieces[0].shape
     in_specs = [pl.BlockSpec((rows, width), lambda a, place: (0, 0))] * ways
-    operands = list(pieces)
+    operands = list(pieces[::-1])
     aliases = {}
     if before is not None:
         in_specs.append(pl.BlockSpec(memory_space=pl.ANY))
@@ -364,7 +368,7 @@
     tp_me = lax.axis_index("tp").astype(jnp.int32)
     core = ctx_me % 2
     place = jnp.stack([tp_me, ctx_me // rest, core, ctx_me])
-    away = list(range(ways - 1, -1, -1))
+    away = list(range(ways))
 
     def over_ctx(value, offset):
         return exchange(value, "ctx", ctx_size, offset) if offset else value
@@ -393,10 +397,10 @@
     received, asked = lax.optimization_barrier((received, asked))
     (made_1,) = rest_products(received, [1], [w_k, w_v], [start_k, start_v], place, ways, away)
     ahead_1 = over_ctx(made_1[0], rest // 2)
-    received, made_1 = lax.optimization_barrier((received, made_1))
+    for a in away:
+        first[a], made_1[a] = lax.optimization_barrier((first[a], made_1[a]))
+    received, ahead_1 = lax.optimization_barrier((received, ahead_1))
     asked += rest_products(received, [1], [w_q], [start_q], place, ways, away)
-    for a in away:
-        first[a], asked[1][a] = lax.optimization_barrier((first[a], asked[1][a]))
 
     second = {}
     queries = [{}, {}]

time: 171 us -> 165 us (0.965); the launches traced: 169 us -> 165 us
  Pallas kernels: 85 us -> 76.9 us
  local copies, waits for them, and re-layouts: 5 us -> 7.86 us
  starting transfers between devices: 44.9 us -> 47.6 us
    pallas_call x2, Pallas kernels: 32.6 us -> 24.3 us  [attend(): pl.pallas_call(functools.partial(attend_body, block, ways, slots, len(arr...]
    unnamed x4 -> x56, local copies, waits for them, and re-layouts: 0.01 us -> 2.79 us
    ppermute x31, starting transfers between devices: 44.9 us -> 47.6 us  [exchange(): return lax.ppermute(value, axis, [(i, i ^ bit) for i in range(size)])]
    ppermute x31, waiting for transfers between devices: 33.6 us -> 31.9 us  [exchange(): return lax.ppermute(value, axis, [(i, i ^ bit) for i in range(size)])]
  transfers between devices with their start and end apart: 31 -> 31, of which waited for: 8 -> 7; matrix products, arithmetic and copies ran while one was open for 1% -> 1% of each run, Pallas kernels for 49% -> 45%
where the time goes in v11:
time: 165 us
  Pallas kernels  76.9 us (47%)
  starting transfers between devices  47.6 us (29%)
  waiting for transfers between devices  31.9 us (19%)
  local copies, waits for them, and re-layouts  7.86 us (5%)
    ppermute x31, starting transfers between devices, exchange(): return lax.ppermute(value, axis, [(i, i ^ bit) for i in range(size)])  47.6 us
    ppermute x31, waiting for transfers between devices, exchange(): return lax.ppermute(value, axis, [(i, i ^ bit) for i in range(size)])  31.9 us
    pallas_call x4, Pallas kernels, rest_products(): pl.pallas_call(functools.partial(rest_body, shares, len(weights), chunks,...  30.2 us
    pallas_call x2, Pallas kernels, attend(): pl.pallas_call(functools.partial(attend_body, block, ways, slots, len(arr...  24.3 us
    pallas_call x1, Pallas kernels, own_products(): pl.pallas_call(functools.partial(own_body, len(weights)), out_shape=[jax....  17.7 us
    pallas_call x2, Pallas kernels, assemble(): pl.pallas_call(functools.partial(assemble_body, ways), out_shape=jax.Shap...  3.99 us
  transfers between devices with their start and end apart: 31, of which 7 were waited for; matrix products, arithmetic and copies ran while one was open for 1% of the time, Pallas kernels for 45%

profile of v11, /device:TPU:0, one launch (start us, length us, event | category | flops | bytes accessed | tf_op | source)
XLA Modules:
  0.0 164.9 jit_solution(16748043917239519753)
XLA Ops:
  0.0 3.1 %dynamic-slice_bitcast_fusion = (bf16[192,2560]{1,0:T(8,128)(2,1)}, bf16[192,2560]{1,0:T(8,128)(2,1)}) fusion(bf16[2,192,2560]{2,1,0:T(8,128)(2,1)} %mine_ref.1, s32[]{:T(128)S(6)} %select_n.30, s32[]{:T(128)S(6)} %select_n.29), kind=kLoop, calls=%fused_computation | loop fusion | bytes 3932168 | tf_op jit(solution)/shard_map/jit(dynamic_index_in_dim)/squeeze | solution.py:385
  3.1 0.5 collective-permute-start.2
  3.5 2.5 %collective-permute-start.1 = (bf16[192,2560]{1,0:T(8,128)(2,1)}, bf16[192,2560]{1,0:T(8,128)(2,1)S(1)}, u32[]{:S(2)}, u32[]{:S(2)}) collective-permute-start(bf16[192,2560]{1,0:T(8,128)(2,1)} %get-tuple-element.114), channel_id=1, source_target_pairs={{0,1},{1,0},{2,3},{3,2},{4,5},{5,4},{6,7},{7,6},{8,9},{9,8},{10,11... | collective-permute-start | bytes 2949128 | tf_op jit(solution)/shard_map/ppermute | solution.py:19
  6.3 0.7 fusion
  7.2 1.0 collective-permute-done
  8.2 1.3 concatenate.4.place
  9.6 0.7 collective-permute-start.4
  10.3 17.7 %shard_map.55 = (f32[2,192,1536]{2,1,0:T(8,128)S(1)}, f32[2,192,1536]{2,1,0:T(8,128)S(1)}, f32[2,192,1536]{2,1,0:T(8,128)S(1)}) custom-call(s32[4]{0:T(128)S(1)} %pad_add_fusion.place, bf16[2,192,2560]{2,1,0:T(8,128)(2,1)S(1)} %copy-done, bf16[192,2560]{1,0:T(8,128)(2,1)} %collective-permute-done.2.other_ref, bf16[5120,1536]{1,0:T(8,128)(2,1)} %refs_1_.8, ...), custom_call_target="tpu_custom_call" | custom-call | flops 9059696640 | bytes 23592960 | tf_op jit(solution)/shard_map/pallas_call | solution.py:43
  28.0 0.9 collective-permute-done.1.refs_0_
  28.8 8.9 %shard_map.56 = (bf16[208,768]{1,0:T(8,128)(2,1)S(1)}, bf16[208,768]{1,0:T(8,128)(2,1)S(1)}, bf16[208,768]{1,0:T(8,128)(2,1)S(1)}, bf16[208,768]{1,0:T(8,128)(2,1)S(1)}) custom-call(s32[6]{0:T(128)S(1)} %concatenate.4.place, bf16[192,2560]{1,0:T(8,128)(2,1)S(1)} %collective-permute-done.1.refs_0_, bf16[5120,1536]{1,0:T(8,128)(2,1)} %refs_1_.8, ...), custom_call_target="tpu_custom_call" | custom-call | flops 3019898880 | bytes 15728640 | tf_op jit(solution)/shard_map/pallas_call | solution.py:129
  37.8 4.1 %collective-permute-start.3 = (bf16[208,768]{1,0:T(8,128)(2,1)S(1)}, bf16[208,768]{1,0:T(8,128)(2,1)S(1)}, u32[]{:S(2)}, u32[]{:S(2)}) collective-permute-start(bf16[208,768]{1,0:T(8,128)(2,1)S(1)} %get-tuple-element.61), channel_id=1, source_target_pairs={{0,24},{2,26},{4,28},{6,30},{8,16},{10,18},{12,20},{14,22},{16,8},... | collective-permute-start | bytes 958472 | tf_op jit(solution)/shard_map/ppermute | solution.py:19
  41.9 0.6 collective-permute-start.8
  42.5 1.7 %collective-permute-start.10 = (bf16[208,768]{1,0:T(8,128)(2,1)S(1)}, bf16[208,768]{1,0:T(8,128)(2,1)S(1)}, u32[]{:S(2)}, u32[]{:S(2)}) collective-permute-start(bf16[208,768]{1,0:T(8,128)(2,1)S(1)} %get-tuple-element.78.refs_7_.refs_19_), channel_id=1, source_target_pairs={{0,4},{2,6},{4,0},{6,2},{8,12},{10,14},{12,8},{14,10},{16,20},{18,... | collective-permute-start | bytes 958472 | tf_op jit(solution)/shard_map/ppermute | solution.py:19
  44.2 6.0 %shard_map.57 = (bf16[192,384]{1,0:T(8,128)(2,1)S(1)}, bf16[192,384]{1,0:T(8,128)(2,1)S(1)}, bf16[192,384]{1,0:T(8,128)(2,1)S(1)}, bf16[192,384]{1,0:T(8,128)(2,1)S(1)}) custom-call(s32[4]{0:T(128)S(1)} %pad_add_fusion.place, bf16[192,2560]{1,0:T(8,128)(2,1)S(1)} %collective-permute-done.1.refs_0_, bf16[5120,1536]{1,0:T(8,128)(2,1)} %refs_1_.9, ...), custom_call_target="tpu_custom_call" | custom-call | flops 1509949440 | bytes 7864320 | tf_op jit(solution)/shard_map/pallas_call | solution.py:129
  50.2 9.1 %shard_map.58 = (bf16[192,768]{1,0:T(8,128)(2,1)S(1)}, bf16[192,768]{1,0:T(8,128)(2,1)S(1)}, bf16[192,768]{1,0:T(8,128)(2,1)S(1)}, bf16[192,768]{1,0:T(8,128)(2,1)S(1)}) custom-call(s32[4]{0:T(128)S(1)} %pad_add_fusion.place, bf16[192,2560]{1,0:T(8,128)(2,1)S(1)} %collective-permute-done.4.refs_0_, bf16[5120,1536]{1,0:T(8,128)(2,1)} %refs_1_.8, ...), custom_call_target="tpu_custom_call" | custom-call | flops 3019898880 | bytes 15728640 | tf_op jit(solution)/shard_map/pallas_call | solution.py:129
  59.3 1.3 collective-permute-start.11
  60.6 3.7 %collective-permute-start.12 = (bf16[192,768]{1,0:T(8,128)(2,1)S(1)}, bf16[192,768]{1,0:T(8,128)(2,1)S(1)}, u32[]{:S(2)}, u32[]{:S(2)}) collective-permute-start(bf16[192,768]{1,0:T(8,128)(2,1)S(1)} %get-tuple-element.83), channel_id=1, source_target_pairs={{0,24},{2,26},{4,28},{6,30},{8,16},{10,18},{12,20},{14,22},{16,8},... | collective-permute-start | bytes 884744 | tf_op jit(solution)/shard_map/ppermute | solution.py:19
  64.3 0.8 collective-permute-start.5
  65.1 10.9 %collective-permute-done.6.refs_3_.refs_11_ = bf16[208,768]{1,0:T(8,128)(2,1)S(1)} collective-permute-done((bf16[208,768]{1,0:T(8,128)(2,1)S(1)}, bf16[208,768]{1,0:T(8,128)(2,1)S(1)}, u32[]{:S(2)}, u32[]{:S(2)}) %collective-permute-start.6) | collective-permute-done | bytes 319520 | tf_op jit(solution)/shard_map/ppermute | solution.py:19
  75.9 1.5 collective-permute-start.7
  77.5 7.2 %collective-permute-start.18 = (bf16[192,768]{1,0:T(8,128)(2,1)S(1)}, bf16[192,768]{1,0:T(8,128)(2,1)S(1)}, u32[]{:S(2)}, u32[]{:S(2)}) collective-permute-start(bf16[192,768]{1,0:T(8,128)(2,1)S(1)} %get-tuple-element.96), channel_id=1, source_target_pairs={{0,8},{2,10},{4,12},{6,14},{8,0},{10,2},{12,4},{14,6},{16,24},{18,... | collective-permute-start | bytes 884744 | tf_op jit(solution)/shard_map/ppermute | solution.py:19
  84.8 9.2 %collective-permute-done.15.refs_10_ = bf16[192,768]{1,0:T(8,128)(2,1)S(1)} collective-permute-done((bf16[192,768]{1,0:T(8,128)(2,1)S(1)}, bf16[192,768]{1,0:T(8,128)(2,1)S(1)}, u32[]{:S(2)}, u32[]{:S(2)}) %collective-permute-start.15) | collective-permute-done | bytes 294944 | tf_op jit(solution)/shard_map/ppermute | solution.py:19
  94.0 2.7 %collective-permute-start.13 = (bf16[192,384]{1,0:T(8,128)(2,1)S(1)}, bf16[192,384]{1,0:T(8,128)(2,1)S(1)}, u32[]{:S(2)}, u32[]{:S(2)}) collective-permute-start(bf16[192,384]{1,0:T(8,128)(2,1)S(1)} %get-tuple-element.85), channel_id=1, source_target_pairs={{0,24},{2,26},{4,28},{6,30},{8,16},{10,18},{12,20},{14,22},{16,8},... | collective-permute-start | bytes 442376 | tf_op jit(solution)/shard_map/ppermute | solution.py:19
  96.7 1.5 collective-permute-start.21
  98.2 0.6 collective-permute-start.22
  98.7 1.5 collective-permute-start.23
  100.2 1.6 collective-permute-done.13.refs_0_
  101.8 3.2 %collective-permute-start.19 = (bf16[192,384]{1,0:T(8,128)(2,1)S(1)}, bf16[192,384]{1,0:T(8,128)(2,1)S(1)}, u32[]{:S(2)}, u32[]{:S(2)}) collective-permute-start(bf16[192,384]{1,0:T(8,128)(2,1)S(1)} %get-tuple-element.97), channel_id=1, source_target_pairs={{0,8},{2,10},{4,12},{6,14},{8,0},{10,2},{12,4},{14,6},{16,24},{18,... | collective-permute-start | bytes 442376 | tf_op jit(solution)/shard_map/ppermute | solution.py:19
  105.1 6.2 %shard_map.60 = (bf16[192,384]{1,0:T(8,128)(2,1)S(1)}, bf16[192,384]{1,0:T(8,128)(2,1)S(1)}, bf16[192,384]{1,0:T(8,128)(2,1)S(1)}, bf16[192,384]{1,0:T(8,128)(2,1)S(1)}) custom-call(s32[4]{0:T(128)S(1)} %pad_add_fusion.place, bf16[192,2560]{1,0:T(8,128)(2,1)S(1)} %collective-permute-done.4.refs_0_, bf16[5120,1536]{1,0:T(8,128)(2,1)} %refs_1_.9, ...), custom_call_target="tpu_custom_call" | custom-call | flops 1509949440 | bytes 7864320 | tf_op jit(solution)/shard_map/pallas_call | solution.py:129
  111.5 0.8 shard_map.59.table
  112.2 0.2 collective-permute-start.14
  112.5 1.4 collective-permute-start.17
  113.8 2.9 %collective-permute-start.20 = (bf16[192,384]{1,0:T(8,128)(2,1)S(1)}, bf16[192,384]{1,0:T(8,128)(2,1)S(1)}, u32[]{:S(2)}, u32[]{:S(2)}) collective-permute-start(bf16[192,384]{1,0:T(8,128)(2,1)S(1)} %get-tuple-element.98), channel_id=1, source_target_pairs={{0,8},{2,10},{4,12},{6,14},{8,0},{10,2},{12,4},{14,6},{16,24},{18,... | collective-permute-start | bytes 442376 | tf_op jit(solution)/shard_map/ppermute | solution.py:19
  116.8 0.7 copy-done.19
  117.5 0.7 copy-done.20
  118.2 12.0 %shard_map.62 = (bf16[192,384]{1,0:T(8,128)(2,1)}, bf16[192,384]{1,0:T(8,128)(2,1)}, bf16[192,384]{1,0:T(8,128)(2,1)}, bf16[192,384]{1,0:T(8,128)(2,1)}) custom-call(s32[16]{0:T(128)} %copy-done.10, bf16[192,384]{1,0:T(8,128)(2,1)} %copy-done.21, bf16[192,384]{1,0:T(8,128)(2,1)} %copy-done.25, bf16[192,384]{1,0:T(8,128)(2,1)} %copy-done.26, ...), custom_call_target="tpu_custom_call" | custom-call | flops 2717908992 | bytes 5898240 | tf_op jit(solution)/shard_map/pallas_call | solution.py:280
  130.3 0.8 collective-permute-start.28
  131.0 0.9 collective-permute-start.29
  131.9 2.8 %collective-permute-start.30 = (bf16[192,384]{1,0:T(8,128)(2,1)}, bf16[192,384]{1,0:T(8,128)(2,1)S(1)}, u32[]{:S(2)}, u32[]{:S(2)}) collective-permute-start(bf16[192,384]{1,0:T(8,128)(2,1)} %get-tuple-element.111), channel_id=1, source_target_pairs={{0,8},{2,10},{4,12},{6,14},{8,0},{10,2},{12,4},{14,6},{16,24},{18,... | collective-permute-start | bytes 442376 | tf_op jit(solution)/shard_map/ppermute | solution.py:19
  134.7 0.6 copy-done.23
  135.4 0.7 copy-done.24
  136.0 12.3 %shard_map.61 = (bf16[192,384]{1,0:T(8,128)(2,1)}, bf16[192,384]{1,0:T(8,128)(2,1)}, bf16[192,384]{1,0:T(8,128)(2,1)}, bf16[192,384]{1,0:T(8,128)(2,1)}) custom-call(s32[16]{0:T(128)} %copy-done.10, bf16[192,384]{1,0:T(8,128)(2,1)} %copy-done.22, bf16[192,384]{1,0:T(8,128)(2,1)} %copy-done.23, bf16[192,384]{1,0:T(8,128)(2,1)} %copy-done.24, ...), custom_call_target="tpu_custom_call" | custom-call | flops 2717908992 | bytes 5898240 | tf_op jit(solution)/shard_map/pallas_call | solution.py:280
  148.4 1.2 collective-permute-start.25
  149.6 3.0 %collective-permute-start.27 = (bf16[192,384]{1,0:T(8,128)(2,1)}, bf16[192,384]{1,0:T(8,128)(2,1)S(1)}, u32[]{:S(2)}, u32[]{:S(2)}) collective-permute-start(bf16[192,384]{1,0:T(8,128)(2,1)} %get-tuple-element.108), channel_id=1, source_target_pairs={{0,2},{2,0},{4,6},{6,4},{8,10},{10,8},{12,14},{14,12},{16,18},{18,... | collective-permute-start | bytes 442376 | tf_op jit(solution)/shard_map/ppermute | solution.py:19
  152.6 2.0 %shard_map.63.refs_4_ = bf16[2,192,1536]{2,1,0:T(8,128)(2,1)} custom-call(s32[4]{0:T(128)S(1)} %pad_add_fusion.place, bf16[192,384]{1,0:T(8,128)(2,1)S(1)} %collective-permute-done.28.refs_0_, bf16[192,384]{1,0:T(8,128)(2,1)S(1)} %collective-permute-done.29.refs_1_, bf16[192,384]{1,0:T(8,128)(2,1)S(1)} %collective-permute-done.30.refs_2_, ...), custom_call_target="tpu_custom_call" | custom-call | tf_op jit(solution)/shard_map/pallas_call | solution.py:348
  154.6 1.9 %collective-permute-done.24.refs_0_ = bf16[192,384]{1,0:T(8,128)(2,1)S(1)} collective-permute-done((bf16[192,384]{1,0:T(8,128)(2,1)}, bf16[192,384]{1,0:T(8,128)(2,1)S(1)}, u32[]{:S(2)}, u32[]{:S(2)}) %collective-permute-start.24) | collective-permute-done | bytes 147488 | tf_op jit(solution)/shard_map/ppermute | solution.py:19
  156.5 6.4 %collective-permute-done.25.refs_1_ = bf16[192,384]{1,0:T(8,128)(2,1)S(1)} collective-permute-done((bf16[192,384]{1,0:T(8,128)(2,1)}, bf16[192,384]{1,0:T(8,128)(2,1)S(1)}, u32[]{:S(2)}, u32[]{:S(2)}) %collective-permute-start.25) | collective-permute-done | bytes 147488 | tf_op jit(solution)/shard_map/ppermute | solution.py:19
  162.9 2.0 %shard_map.64 = bf16[2,192,1536]{2,1,0:T(8,128)(2,1)} custom-call(s32[4]{0:T(128)S(1)} %pad_add_fusion.place, bf16[192,384]{1,0:T(8,128)(2,1)S(1)} %collective-permute-done.24.refs_0_, bf16[192,384]{1,0:T(8,128)(2,1)S(1)} %collective-permute-done.25.refs_1_, bf16[192,384]{1,0:T(8,128)(2,1)S(1)} %collective-permute-done.26.refs_2_, ...), custom_call_target="tpu_custom_call", output_to_operand_aliasing={{}: (5, {})} | custom-call | tf_op jit(solution)/shard_map/pallas_call | solution.py:348
  (87 shorter events, 0.9 us)
Async XLA Ops:
  0.0 10.3 %copy-start = (bf16[2,192,2560]{2,1,0:T(8,128)(2,1)S(1)}, bf16[2,192,2560]{2,1,0:T(8,128)(2,1)}, u32[]{:S(2)}) copy-start(bf16[2,192,2560]{2,1,0:T(8,128)(2,1)} %mine_ref.1) | copy-start | bytes 5898244
  3.1 6.5 %collective-permute-start.2 = (bf16[192,2560]{1,0:T(8,128)(2,1)}, bf16[192,2560]{1,0:T(8,128)(2,1)}, u32[]{:S(2)}, u32[]{:S(2)}) collective-permute-start(bf16[192,2560]{1,0:T(8,128)(2,1)} %get-tuple-element.113), channel_id=1, source_target_pairs={{0,2},{2,0},{4,6},{6,4},{8,10},{10,8},{12,14},{14,12},{16,18},{18,... | collective-permute-start | bytes 2949128 | tf_op jit(solution)/shard_map/ppermute | solution.py:19
  3.5 25.3 %collective-permute-start.1 = (bf16[192,2560]{1,0:T(8,128)(2,1)}, bf16[192,2560]{1,0:T(8,128)(2,1)S(1)}, u32[]{:S(2)}, u32[]{:S(2)}) collective-permute-start(bf16[192,2560]{1,0:T(8,128)(2,1)} %get-tuple-element.114), channel_id=1, source_target_pairs={{0,1},{1,0},{2,3},{3,2},{4,5},{5,4},{6,7},{7,6},{8,9},{9,8},{10,11... | collective-permute-start | bytes 2949128 | tf_op jit(solution)/shard_map/ppermute | solution.py:19
  6.9 1.3 collective-permute-start
  9.6 40.6 %collective-permute-start.4 = (bf16[192,2560]{1,0:T(8,128)(2,1)}, bf16[192,2560]{1,0:T(8,128)(2,1)S(1)}, u32[]{:S(2)}, u32[]{:S(2)}) collective-permute-start(bf16[192,2560]{1,0:T(8,128)(2,1)} %collective-permute-done.2.other_ref), channel_id=1, source_target_pairs={{0,1},{1,0},{2,3},{3,2},{4,5},{5,4},{6,7},{7,6},{8,9},{9,8},{10,11... | collective-permute-start | bytes 2949128 | tf_op jit(solution)/shard_map/ppermute | solution.py:19
  37.7 73.6 %copy-start.1 = (bf16[208,768]{1,0:T(8,128)(2,1)}, bf16[208,768]{1,0:T(8,128)(2,1)S(1)}, u32[]{:S(2)}) copy-start(bf16[208,768]{1,0:T(8,128)(2,1)S(1)} %get-tuple-element.78.refs_7_.refs_19_) | copy-start | bytes 958468
  37.8 22.9 %collective-permute-start.3 = (bf16[208,768]{1,0:T(8,128)(2,1)S(1)}, bf16[208,768]{1,0:T(8,128)(2,1)S(1)}, u32[]{:S(2)}, u32[]{:S(2)}) collective-permute-start(bf16[208,768]{1,0:T(8,128)(2,1)S(1)} %get-tuple-element.61), channel_id=1, source_target_pairs={{0,24},{2,26},{4,28},{6,30},{8,16},{10,18},{12,20},{14,22},{16,8},... | collective-permute-start | bytes 958472 | tf_op jit(solution)/shard_map/ppermute | solution.py:19
  41.9 34.1 %collective-permute-start.6 = (bf16[208,768]{1,0:T(8,128)(2,1)S(1)}, bf16[208,768]{1,0:T(8,128)(2,1)S(1)}, u32[]{:S(2)}, u32[]{:S(2)}) collective-permute-start(bf16[208,768]{1,0:T(8,128)(2,1)S(1)} %get-tuple-element.70), channel_id=1, source_target_pairs={{0,16},{2,18},{4,20},{6,22},{8,24},{10,26},{12,28},{14,30},{16,0},... | collective-permute-start | bytes 958472 | tf_op jit(solution)/shard_map/ppermute | solution.py:19
  41.9 35.6 %collective-permute-start.8 = (bf16[208,768]{1,0:T(8,128)(2,1)S(1)}, bf16[208,768]{1,0:T(8,128)(2,1)S(1)}, u32[]{:S(2)}, u32[]{:S(2)}) collective-permute-start(bf16[208,768]{1,0:T(8,128)(2,1)S(1)} %get-tuple-element.73), channel_id=1, source_target_pairs={{0,8},{2,10},{4,12},{6,14},{8,0},{10,2},{12,4},{14,6},{16,24},{18,... | collective-permute-start | bytes 958472 | tf_op jit(solution)/shard_map/ppermute | solution.py:19
  42.5 18.1 %collective-permute-start.10 = (bf16[208,768]{1,0:T(8,128)(2,1)S(1)}, bf16[208,768]{1,0:T(8,128)(2,1)S(1)}, u32[]{:S(2)}, u32[]{:S(2)}) collective-permute-start(bf16[208,768]{1,0:T(8,128)(2,1)S(1)} %get-tuple-element.78.refs_7_.refs_19_), channel_id=1, source_target_pairs={{0,4},{2,6},{4,0},{6,2},{8,12},{10,14},{12,8},{14,10},{16,20},{18,... | collective-permute-start | bytes 958472 | tf_op jit(solution)/shard_map/ppermute | solution.py:19
  50.2 9.1 %copy-start.12 = (bf16[192,384]{1,0:T(8,128)(2,1)}, bf16[192,384]{1,0:T(8,128)(2,1)S(1)}, u32[]{:S(2)}) copy-start(bf16[192,384]{1,0:T(8,128)(2,1)S(1)} %get-tuple-element.103.refs_3_) | copy-start | bytes 442372
  59.3 52.0 %copy-start.11 = (bf16[192,768]{1,0:T(8,128)(2,1)}, bf16[192,768]{1,0:T(8,128)(2,1)S(1)}, u32[]{:S(2)}) copy-start(bf16[192,768]{1,0:T(8,128)(2,1)S(1)} %get-tuple-element.102.refs_18_) | copy-start | bytes 884740
  59.3 18.2 %collective-permute-start.11 = (bf16[192,768]{1,0:T(8,128)(2,1)S(1)}, bf16[192,768]{1,0:T(8,128)(2,1)S(1)}, u32[]{:S(2)}, u32[]{:S(2)}) collective-permute-start(bf16[192,768]{1,0:T(8,128)(2,1)S(1)} %get-tuple-element.102.refs_18_), channel_id=1, source_target_pairs={{0,4},{2,6},{4,0},{6,2},{8,12},{10,14},{12,8},{14,10},{16,20},{18,... | collective-permute-start | bytes 884744 | tf_op jit(solution)/shard_map/ppermute | solution.py:19
  60.6 50.8 %copy-start.2 = (bf16[208,768]{1,0:T(8,128)(2,1)}, bf16[208,768]{1,0:T(8,128)(2,1)S(1)}, u32[]{:S(2)}) copy-start(bf16[208,768]{1,0:T(8,128)(2,1)S(1)} %collective-permute-done.3.refs_1_.refs_7_) | copy-start | bytes 958468
  60.6 50.8 %copy-start.5 = (bf16[208,768]{1,0:T(8,128)(2,1)}, bf16[208,768]{1,0:T(8,128)(2,1)S(1)}, u32[]{:S(2)}) copy-start(bf16[208,768]{1,0:T(8,128)(2,1)S(1)} %collective-permute-done.10.refs_6_.refs_17_) | copy-start | bytes 958468
  60.6 24.1 %collective-permute-start.12 = (bf16[192,768]{1,0:T(8,128)(2,1)S(1)}, bf16[192,768]{1,0:T(8,128)(2,1)S(1)}, u32[]{:S(2)}, u32[]{:S(2)}) collective-permute-start(bf16[192,768]{1,0:T(8,128)(2,1)S(1)} %get-tuple-element.83), channel_id=1, source_target_pairs={{0,24},{2,26},{4,28},{6,30},{8,16},{10,18},{12,20},{14,22},{16,8},... | collective-permute-start | bytes 884744 | tf_op jit(solution)/shard_map/ppermute | solution.py:19
  64.3 33.9 %collective-permute-start.5 = (bf16[208,768]{1,0:T(8,128)(2,1)S(1)}, bf16[208,768]{1,0:T(8,128)(2,1)S(1)}, u32[]{:S(2)}, u32[]{:S(2)}) collective-permute-start(bf16[208,768]{1,0:T(8,128)(2,1)S(1)} %collective-permute-done.3.refs_1_.refs_7_), channel_id=1, source_target_pairs={{0,4},{2,6},{4,0},{6,2},{8,12},{10,14},{12,8},{14,10},{16,20},{18,... | collective-permute-start | bytes 958472 | tf_op jit(solution)/shard_map/ppermute | solution.py:19
  75.9 35.5 %copy-start.3 = (bf16[208,768]{1,0:T(8,128)(2,1)}, bf16[208,768]{1,0:T(8,128)(2,1)S(1)}, u32[]{:S(2)}) copy-start(bf16[208,768]{1,0:T(8,128)(2,1)S(1)} %collective-permute-done.6.refs_3_.refs_11_) | copy-start | bytes 958468
  75.9 22.8 %collective-permute-start.7 = (bf16[208,768]{1,0:T(8,128)(2,1)S(1)}, bf16[208,768]{1,0:T(8,128)(2,1)S(1)}, u32[]{:S(2)}, u32[]{:S(2)}) collective-permute-start(bf16[208,768]{1,0:T(8,128)(2,1)S(1)} %collective-permute-done.6.refs_3_.refs_11_), channel_id=1, source_target_pairs={{0,4},{2,6},{4,0},{6,2},{8,12},{10,14},{12,8},{14,10},{16,20},{18,... | collective-permute-start | bytes 958472 | tf_op jit(solution)/shard_map/ppermute | solution.py:19
  77.5 33.9 %copy-start.4 = (bf16[208,768]{1,0:T(8,128)(2,1)}, bf16[208,768]{1,0:T(8,128)(2,1)S(1)}, u32[]{:S(2)}) copy-start(bf16[208,768]{1,0:T(8,128)(2,1)S(1)} %collective-permute-done.8.refs_5_.refs_15_) | copy-start | bytes 958468
  77.5 16.5 %collective-permute-start.15 = (bf16[192,768]{1,0:T(8,128)(2,1)S(1)}, bf16[192,768]{1,0:T(8,128)(2,1)S(1)}, u32[]{:S(2)}, u32[]{:S(2)}) collective-permute-start(bf16[192,768]{1,0:T(8,128)(2,1)S(1)} %get-tuple-element.90), channel_id=1, source_target_pairs={{0,16},{2,18},{4,20},{6,22},{8,24},{10,26},{12,28},{14,30},{16,0},... | collective-permute-start | bytes 884744 | tf_op jit(solution)/shard_map/ppermute | solution.py:19
  77.5 33.8 %copy-start.14 = (bf16[192,768]{1,0:T(8,128)(2,1)}, bf16[192,768]{1,0:T(8,128)(2,1)S(1)}, u32[]{:S(2)}) copy-start(bf16[192,768]{1,0:T(8,128)(2,1)S(1)} %collective-permute-done.11.refs_16_) | copy-start | bytes 884740
  77.5 19.2 %collective-permute-start.18 = (bf16[192,768]{1,0:T(8,128)(2,1)S(1)}, bf16[192,768]{1,0:T(8,128)(2,1)S(1)}, u32[]{:S(2)}, u32[]{:S(2)}) collective-permute-start(bf16[192,768]{1,0:T(8,128)(2,1)S(1)} %get-tuple-element.96), channel_id=1, source_target_pairs={{0,8},{2,10},{4,12},{6,14},{8,0},{10,2},{12,4},{14,6},{16,24},{18,... | collective-permute-start | bytes 884744 | tf_op jit(solution)/shard_map/ppermute | solution.py:19
  84.7 26.6 %copy-start.15 = (bf16[192,768]{1,0:T(8,128)(2,1)}, bf16[192,768]{1,0:T(8,128)(2,1)S(1)}, u32[]{:S(2)}) copy-start(bf16[192,768]{1,0:T(8,128)(2,1)S(1)} %collective-permute-done.12.refs_6_) | copy-start | bytes 884740
  84.7 15.5 %collective-permute-start.9 = (bf16[208,768]{1,0:T(8,128)(2,1)S(1)}, bf16[208,768]{1,0:T(8,128)(2,1)S(1)}, u32[]{:S(2)}, u32[]{:S(2)}) collective-permute-start(bf16[208,768]{1,0:T(8,128)(2,1)S(1)} %collective-permute-done.8.refs_5_.refs_15_), channel_id=1, source_target_pairs={{0,4},{2,6},{4,0},{6,2},{8,12},{10,14},{12,8},{14,10},{16,20},{18,... | collective-permute-start | bytes 958472 | tf_op jit(solution)/shard_map/ppermute | solution.py:19
  94.0 17.3 %copy-start.16 = (bf16[192,768]{1,0:T(8,128)(2,1)}, bf16[192,768]{1,0:T(8,128)(2,1)S(1)}, u32[]{:S(2)}) copy-start(bf16[192,768]{1,0:T(8,128)(2,1)S(1)} %collective-permute-done.15.refs_10_) | copy-start | bytes 884740
  94.0 7.8 %collective-permute-start.13 = (bf16[192,384]{1,0:T(8,128)(2,1)S(1)}, bf16[192,384]{1,0:T(8,128)(2,1)S(1)}, u32[]{:S(2)}, u32[]{:S(2)}) collective-permute-start(bf16[192,384]{1,0:T(8,128)(2,1)S(1)} %get-tuple-element.85), channel_id=1, source_target_pairs={{0,24},{2,26},{4,28},{6,30},{8,16},{10,18},{12,20},{14,22},{16,8},... | collective-permute-start | bytes 442376 | tf_op jit(solution)/shard_map/ppermute | solution.py:19
  96.7 14.7 %copy-start.17 = (bf16[192,768]{1,0:T(8,128)(2,1)}, bf16[192,768]{1,0:T(8,128)(2,1)S(1)}, u32[]{:S(2)}) copy-start(bf16[192,768]{1,0:T(8,128)(2,1)S(1)} %collective-permute-done.18.refs_14_) | copy-start | bytes 884740
  96.7 17.2 %collective-permute-start.21 = (bf16[192,768]{1,0:T(8,128)(2,1)S(1)}, bf16[192,768]{1,0:T(8,128)(2,1)S(1)}, u32[]{:S(2)}, u32[]{:S(2)}) collective-permute-start(bf16[192,768]{1,0:T(8,128)(2,1)S(1)} %collective-permute-done.12.refs_6_), channel_id=1, source_target_pairs={{0,4},{2,6},{4,0},{6,2},{8,12},{10,14},{12,8},{14,10},{16,20},{18,... | collective-permute-start | bytes 884744 | tf_op jit(solution)/shard_map/ppermute | solution.py:19
  98.2 13.3 %copy-start.6 = (bf16[208,768]{1,0:T(8,128)(2,1)}, bf16[208,768]{1,0:T(8,128)(2,1)S(1)}, u32[]{:S(2)}) copy-start(bf16[208,768]{1,0:T(8,128)(2,1)S(1)} %collective-permute-done.5.refs_0_.refs_5_) | copy-start | bytes 958468
  98.2 18.6 %collective-permute-start.22 = (bf16[192,768]{1,0:T(8,128)(2,1)S(1)}, bf16[192,768]{1,0:T(8,128)(2,1)S(1)}, u32[]{:S(2)}, u32[]{:S(2)}) collective-permute-start(bf16[192,768]{1,0:T(8,128)(2,1)S(1)} %collective-permute-done.15.refs_10_), channel_id=1, source_target_pairs={{0,4},{2,6},{4,0},{6,2},{8,12},{10,14},{12,8},{14,10},{16,20},{18,... | collective-permute-start | bytes 884744 | tf_op jit(solution)/shard_map/ppermute | solution.py:19
  98.7 12.7 %copy-start.7 = (bf16[208,768]{1,0:T(8,128)(2,1)}, bf16[208,768]{1,0:T(8,128)(2,1)S(1)}, u32[]{:S(2)}) copy-start(bf16[208,768]{1,0:T(8,128)(2,1)S(1)} %collective-permute-done.7.refs_2_.refs_9_) | copy-start | bytes 958468
  98.7 18.1 %collective-permute-start.23 = (bf16[192,768]{1,0:T(8,128)(2,1)S(1)}, bf16[192,768]{1,0:T(8,128)(2,1)S(1)}, u32[]{:S(2)}, u32[]{:S(2)}) collective-permute-start(bf16[192,768]{1,0:T(8,128)(2,1)S(1)} %collective-permute-done.18.refs_14_), channel_id=1, source_target_pairs={{0,4},{2,6},{4,0},{6,2},{8,12},{10,14},{12,8},{14,10},{16,20},{18,... | collective-permute-start | bytes 884744 | tf_op jit(solution)/shard_map/ppermute | solution.py:19
  100.2 11.2 %copy-start.8 = (bf16[208,768]{1,0:T(8,128)(2,1)}, bf16[208,768]{1,0:T(8,128)(2,1)S(1)}, u32[]{:S(2)}) copy-start(bf16[208,768]{1,0:T(8,128)(2,1)S(1)} %collective-permute-done.9.refs_4_.refs_13_) | copy-start | bytes 958468
  100.2 12.0 %collective-permute-start.16 = (bf16[192,384]{1,0:T(8,128)(2,1)S(1)}, bf16[192,384]{1,0:T(8,128)(2,1)S(1)}, u32[]{:S(2)}, u32[]{:S(2)}) collective-permute-start(bf16[192,384]{1,0:T(8,128)(2,1)S(1)} %get-tuple-element.91), channel_id=1, source_target_pairs={{0,16},{2,18},{4,20},{6,22},{8,24},{10,26},{12,28},{14,30},{16,0},... | collective-permute-start | bytes 442376 | tf_op jit(solution)/shard_map/ppermute | solution.py:19
  101.8 9.5 %copy-start.21 = (bf16[192,384]{1,0:T(8,128)(2,1)}, bf16[192,384]{1,0:T(8,128)(2,1)S(1)}, u32[]{:S(2)}) copy-start(bf16[192,384]{1,0:T(8,128)(2,1)S(1)} %collective-permute-done.13.refs_0_) | copy-start | bytes 442372
  101.8 10.6 %collective-permute-start.19 = (bf16[192,384]{1,0:T(8,128)(2,1)S(1)}, bf16[192,384]{1,0:T(8,128)(2,1)S(1)}, u32[]{:S(2)}, u32[]{:S(2)}) collective-permute-start(bf16[192,384]{1,0:T(8,128)(2,1)S(1)} %get-tuple-element.97), channel_id=1, source_target_pairs={{0,8},{2,10},{4,12},{6,14},{8,0},{10,2},{12,4},{14,6},{16,24},{18,... | collective-permute-start | bytes 442376 | tf_op jit(solution)/shard_map/ppermute | solution.py:19
  112.2 19.6 %collective-permute-start.14 = (bf16[192,384]{1,0:T(8,128)(2,1)S(1)}, bf16[192,384]{1,0:T(8,128)(2,1)S(1)}, u32[]{:S(2)}, u32[]{:S(2)}) collective-permute-start(bf16[192,384]{1,0:T(8,128)(2,1)S(1)} %get-tuple-element.86), channel_id=1, source_target_pairs={{0,24},{2,26},{4,28},{6,30},{8,16},{10,18},{12,20},{14,22},{16,8},... | collective-permute-start | bytes 442376 | tf_op jit(solution)/shard_map/ppermute | solution.py:19
  112.5 22.2 %collective-permute-start.17 = (bf16[192,384]{1,0:T(8,128)(2,1)S(1)}, bf16[192,384]{1,0:T(8,128)(2,1)S(1)}, u32[]{:S(2)}, u32[]{:S(2)}) collective-permute-start(bf16[192,384]{1,0:T(8,128)(2,1)S(1)} %get-tuple-element.92), channel_id=1, source_target_pairs={{0,16},{2,18},{4,20},{6,22},{8,24},{10,26},{12,28},{14,30},{16,0},... | collective-permute-start | bytes 442376 | tf_op jit(solution)/shard_map/ppermute | solution.py:19
  113.8 20.9 %collective-permute-start.20 = (bf16[192,384]{1,0:T(8,128)(2,1)S(1)}, bf16[192,384]{1,0:T(8,128)(2,1)S(1)}, u32[]{:S(2)}, u32[]{:S(2)}) collective-permute-start(bf16[192,384]{1,0:T(8,128)(2,1)S(1)} %get-tuple-element.98), channel_id=1, source_target_pairs={{0,8},{2,10},{4,12},{6,14},{8,0},{10,2},{12,4},{14,6},{16,24},{18,... | collective-permute-start | bytes 442376 | tf_op jit(solution)/shard_map/ppermute | solution.py:19
  130.3 19.4 %collective-permute-start.28 = (bf16[192,384]{1,0:T(8,128)(2,1)}, bf16[192,384]{1,0:T(8,128)(2,1)S(1)}, u32[]{:S(2)}, u32[]{:S(2)}) collective-permute-start(bf16[192,384]{1,0:T(8,128)(2,1)} %get-tuple-element.109), channel_id=1, source_target_pairs={{0,24},{2,26},{4,28},{6,30},{8,16},{10,18},{12,20},{14,22},{16,8},... | collective-permute-start | bytes 442376 | tf_op jit(solution)/shard_map/ppermute | solution.py:19
  131.0 18.6 %collective-permute-start.29 = (bf16[192,384]{1,0:T(8,128)(2,1)}, bf16[192,384]{1,0:T(8,128)(2,1)S(1)}, u32[]{:S(2)}, u32[]{:S(2)}) collective-permute-start(bf16[192,384]{1,0:T(8,128)(2,1)} %get-tuple-element.110), channel_id=1, source_target_pairs={{0,16},{2,18},{4,20},{6,22},{8,24},{10,26},{12,28},{14,30},{16,0},... | collective-permute-start | bytes 442376 | tf_op jit(solution)/shard_map/ppermute | solution.py:19
  131.9 20.7 %copy-start.9 = (bf16[192,384]{1,0:T(8,128)(2,1)S(1)}, bf16[192,384]{1,0:T(8,128)(2,1)}, u32[]{:S(2)}) copy-start(bf16[192,384]{1,0:T(8,128)(2,1)} %get-tuple-element.112.refs_3_) | copy-start | bytes 442372
  131.9 20.7 %collective-permute-start.30 = (bf16[192,384]{1,0:T(8,128)(2,1)}, bf16[192,384]{1,0:T(8,128)(2,1)S(1)}, u32[]{:S(2)}, u32[]{:S(2)}) collective-permute-start(bf16[192,384]{1,0:T(8,128)(2,1)} %get-tuple-element.111), channel_id=1, source_target_pairs={{0,8},{2,10},{4,12},{6,14},{8,0},{10,2},{12,4},{14,6},{16,24},{18,... | collective-permute-start | bytes 442376 | tf_op jit(solution)/shard_map/ppermute | solution.py:19
  148.3 8.2 %collective-permute-start.24 = (bf16[192,384]{1,0:T(8,128)(2,1)}, bf16[192,384]{1,0:T(8,128)(2,1)S(1)}, u32[]{:S(2)}, u32[]{:S(2)}) collective-permute-start(bf16[192,384]{1,0:T(8,128)(2,1)} %get-tuple-element.105), channel_id=1, source_target_pairs={{0,26},{2,24},{4,30},{6,28},{8,18},{10,16},{12,22},{14,20},{16,10}... | collective-permute-start | bytes 442376 | tf_op jit(solution)/shard_map/ppermute | solution.py:19
  148.4 14.5 %collective-permute-start.25 = (bf16[192,384]{1,0:T(8,128)(2,1)}, bf16[192,384]{1,0:T(8,128)(2,1)S(1)}, u32[]{:S(2)}, u32[]{:S(2)}) collective-permute-start(bf16[192,384]{1,0:T(8,128)(2,1)} %get-tuple-element.106), channel_id=1, source_target_pairs={{0,18},{2,16},{4,22},{6,20},{8,26},{10,24},{12,30},{14,28},{16,2},... | collective-permute-start | bytes 442376 | tf_op jit(solution)/shard_map/ppermute | solution.py:19
  149.6 13.2 %collective-permute-start.26 = (bf16[192,384]{1,0:T(8,128)(2,1)}, bf16[192,384]{1,0:T(8,128)(2,1)S(1)}, u32[]{:S(2)}, u32[]{:S(2)}) collective-permute-start(bf16[192,384]{1,0:T(8,128)(2,1)} %get-tuple-element.107), channel_id=1, source_target_pairs={{0,10},{2,8},{4,14},{6,12},{8,2},{10,0},{12,6},{14,4},{16,26},{18,... | collective-permute-start | bytes 442376 | tf_op jit(solution)/shard_map/ppermute | solution.py:19
  149.6 13.2 %collective-permute-start.27 = (bf16[192,384]{1,0:T(8,128)(2,1)}, bf16[192,384]{1,0:T(8,128)(2,1)S(1)}, u32[]{:S(2)}, u32[]{:S(2)}) collective-permute-start(bf16[192,384]{1,0:T(8,128)(2,1)} %get-tuple-element.108), channel_id=1, source_target_pairs={{0,2},{2,0},{4,6},{6,4},{8,10},{10,8},{12,14},{14,12},{16,18},{18,... | collective-permute-start | bytes 442376 | tf_op jit(solution)/shard_map/ppermute | solution.py:19
  (11 other events, 29.2 us)

commit v12 on v11

--- a/solution.py
+++ b/solution.py
@@ -153,7 +153,7 @@
 
 def attend_body(block, ways, slots, arrays, spans, tile, table, *refs):
     count = len(slots)
-    query_refs = refs[:ways][::-1]
+    query_refs = refs[:ways]
     block_refs = refs[ways : ways + arrays]
     out_refs = refs[ways + arrays : 2 * ways + arrays]
     ordered, asked, scores, highest, sums, total, position, sems = refs[2 * ways + arrays :]
@@ -264,7 +264,7 @@
     ways, count = len(queries), len(blocks)
     arrays = []
     slots = []
-    for offset in sorted(blocks, reverse=True):
+    for offset in sorted(blocks):
         array, row = blocks[offset]
         if not any(array is other for other in arrays):
             arrays.append(array)
@@ -301,7 +301,7 @@
             bytes_accessed=4 * length * width + 4 * ways * rows * width,
             transcendentals=flops // (4 * HD),
         ),
-    )(table, *queries[::-1], *arrays)
+    )(table, *queries, *arrays)
 
 
 def table_body(offsets, *refs):
@@ -313,7 +313,7 @@
 
 
 def span_table(blocks, rows):
-    offsets = sorted(blocks, reverse=True)
+    offsets = sorted(blocks)
     return pl.pallas_call(
         functools.partial(table_body, offsets),
         out_shape=jax.ShapeDtypeStruct((2 * len(offsets),), jnp.int32),
@@ -402,6 +402,23 @@
     received, ahead_1 = lax.optimization_barrier((received, ahead_1))
     asked += rest_products(received, [1], [w_q], [start_q], place, ways, away)
 
+    def over_y(blocks):
+        bit = rest // 2
+        while bit > 1:
+            for i in list(blocks):
+                if i ^ bit not in blocks:
+                    blocks[i ^ bit] = over_ctx(blocks[i], bit)
+            bit //= 2
+        return blocks
+
+    blocks = {a * rest: first[a] for a in away}
+    blocks[rest // 2] = ahead
+    before = []
+    for a in range(1, ways):
+        value = lax.optimization_barrier((first[a], before))[0] if a == ways - 1 else first[a]
+        before.append(over_ctx(value, rest // 2))
+        blocks[a * rest + rest // 2] = before[-1]
+    blocks = over_y(blocks)
     second = {}
     queries = [{}, {}]
     for a in away:
@@ -411,19 +428,9 @@
             last = keep[key] = over_ctx(value, a * rest)
             if keep is second and a:
                 last = (last, ahead_1)
-
-    def over_y(blocks):
-        bit = rest // 2
-        while bit > 1:
-            for i in list(blocks):
-                if i ^ bit not in blocks:
-                    blocks[i ^ bit] = over_ctx(blocks[i], bit)
-            bit //= 2
-        return blocks
-
-    blocks = {a * rest: first[a] for a in away}
-    blocks[rest // 2] = ahead
-    blocks = over_y(blocks)
+            if keep is second and a == ways - 1:
+                last = (last, [blocks[i] for i in sorted(blocks)])
+
     table = span_table({i: (array, 0) for i, array in blocks.items()}, rows)
     second[rest // 2 + 1] = ahead_1
     blocks.update(over_y(second))

time: 165 us -> 162 us (0.982)
  starting transfers between devices: 47.6 us -> 43.4 us
    ppermute x31, starting transfers between devices: 47.6 us -> 43.4 us  [exchange(): return lax.ppermute(value, axis, [(i, i ^ bit) for i in range(size)])]
  transfers between devices with their start and end apart: 31 -> 31, of which waited for: 7 -> 9; matrix products, arithmetic and copies ran while one was open for 1% -> 1% of each run, Pallas kernels for 45% -> 46%
where the time goes in v12:
time: 162 us
  Pallas kernels  76.9 us (47%)
  starting transfers between devices  43.4 us (27%)
  waiting for transfers between devices  33.2 us (20%)
  local copies, waits for them, and re-layouts  7.87 us (5%)
    ppermute x31, starting transfers between devices, exchange(): return lax.ppermute(value, axis, [(i, i ^ bit) for i in range(size)])  43.4 us
    ppermute x31, waiting for transfers between devices, exchange(): return lax.ppermute(value, axis, [(i, i ^ bit) for i in range(size)])  33.2 us
    pallas_call x4, Pallas kernels, rest_products(): pl.pallas_call(functools.partial(rest_body, shares, len(weights), chunks,...  30.2 us
    pallas_call x2, Pallas kernels, attend(): pl.pallas_call(functools.partial(attend_body, block, ways, slots, len(arr...  24.3 us
    pallas_call x1, Pallas kernels, own_products(): pl.pallas_call(functools.partial(own_body, len(weights)), out_shape=[jax....  17.7 us
    pallas_call x2, Pallas kernels, assemble(): pl.pallas_call(functools.partial(assemble_body, ways), out_shape=jax.Shap...  3.99 us
  transfers between devices with their start and end apart: 31, of which 9 were waited for; matrix products, arithmetic and copies ran while one was open for 1% of the time, Pallas kernels for 46%

profile of v12, /device:TPU:0, one launch (start us, length us, event | category | flops | bytes accessed | tf_op | source)
XLA Modules:
  0.0 162.0 jit_solution(4116047752056225223)
XLA Ops:
  0.0 3.1 %dynamic-slice_bitcast_fusion = (bf16[192,2560]{1,0:T(8,128)(2,1)}, bf16[192,2560]{1,0:T(8,128)(2,1)}) fusion(bf16[2,192,2560]{2,1,0:T(8,128)(2,1)} %mine_ref.1, s32[]{:T(128)S(6)} %select_n.30, s32[]{:T(128)S(6)} %select_n.29), kind=kLoop, calls=%fused_computation | loop fusion | bytes 3932168 | tf_op jit(solution)/shard_map/jit(dynamic_index_in_dim)/squeeze | solution.py:385
  3.5 2.5 %collective-permute-start.1 = (bf16[192,2560]{1,0:T(8,128)(2,1)}, bf16[192,2560]{1,0:T(8,128)(2,1)S(1)}, u32[]{:S(2)}, u32[]{:S(2)}) collective-permute-start(bf16[192,2560]{1,0:T(8,128)(2,1)} %get-tuple-element.116), channel_id=1, source_target_pairs={{0,1},{1,0},{2,3},{3,2},{4,5},{5,4},{6,7},{7,6},{8,9},{9,8},{10,11... | collective-permute-start | bytes 2949128 | tf_op jit(solution)/shard_map/ppermute | solution.py:19
  6.3 0.7 fusion
  7.2 1.0 collective-permute-done
  8.2 1.3 concatenate.4.place
  9.6 0.7 collective-permute-start.3
  10.3 17.7 %shard_map.55 = (f32[2,192,1536]{2,1,0:T(8,128)S(1)}, f32[2,192,1536]{2,1,0:T(8,128)S(1)}, f32[2,192,1536]{2,1,0:T(8,128)S(1)}) custom-call(s32[4]{0:T(128)S(1)} %pad_add_fusion.place, bf16[2,192,2560]{2,1,0:T(8,128)(2,1)S(1)} %copy-done, bf16[192,2560]{1,0:T(8,128)(2,1)} %collective-permute-done.2.other_ref, bf16[5120,1536]{1,0:T(8,128)(2,1)} %refs_1_.8, ...), custom_call_target="tpu_custom_call" | custom-call | flops 9059696640 | bytes 23592960 | tf_op jit(solution)/shard_map/pallas_call | solution.py:43
  28.0 0.9 collective-permute-done.1.refs_0_
  28.8 8.9 %shard_map.56 = (bf16[208,768]{1,0:T(8,128)(2,1)S(1)}, bf16[208,768]{1,0:T(8,128)(2,1)S(1)}, bf16[208,768]{1,0:T(8,128)(2,1)S(1)}, bf16[208,768]{1,0:T(8,128)(2,1)S(1)}) custom-call(s32[6]{0:T(128)S(1)} %concatenate.4.place, bf16[192,2560]{1,0:T(8,128)(2,1)S(1)} %collective-permute-done.1.refs_0_, bf16[5120,1536]{1,0:T(8,128)(2,1)} %refs_1_.8, ...), custom_call_target="tpu_custom_call" | custom-call | flops 3019898880 | bytes 15728640 | tf_op jit(solution)/shard_map/pallas_call | solution.py:129
  37.8 2.0 %collective-permute-start.4 = (bf16[208,768]{1,0:T(8,128)(2,1)S(1)}, bf16[208,768]{1,0:T(8,128)(2,1)S(1)}, u32[]{:S(2)}, u32[]{:S(2)}) collective-permute-start(bf16[208,768]{1,0:T(8,128)(2,1)S(1)} %get-tuple-element.70.refs_0_.refs_4_), channel_id=1, source_target_pairs={{0,4},{2,6},{4,0},{6,2},{8,12},{10,14},{12,8},{14,10},{16,20},{18,... | collective-permute-start | bytes 958472 | tf_op jit(solution)/shard_map/ppermute | solution.py:19
  39.8 1.6 collective-permute-start.5
  41.4 2.6 %collective-permute-start.7 = (bf16[208,768]{1,0:T(8,128)(2,1)S(1)}, bf16[208,768]{1,0:T(8,128)(2,1)S(1)}, u32[]{:S(2)}, u32[]{:S(2)}) collective-permute-start(bf16[208,768]{1,0:T(8,128)(2,1)S(1)} %get-tuple-element.74), channel_id=1, source_target_pairs={{0,16},{2,18},{4,20},{6,22},{8,24},{10,26},{12,28},{14,30},{16,0},... | collective-permute-start | bytes 958472 | tf_op jit(solution)/shard_map/ppermute | solution.py:19
  44.2 6.0 %shard_map.57 = (bf16[192,384]{1,0:T(8,128)(2,1)S(1)}, bf16[192,384]{1,0:T(8,128)(2,1)S(1)}, bf16[192,384]{1,0:T(8,128)(2,1)S(1)}, bf16[192,384]{1,0:T(8,128)(2,1)S(1)}) custom-call(s32[4]{0:T(128)S(1)} %pad_add_fusion.place, bf16[192,2560]{1,0:T(8,128)(2,1)S(1)} %collective-permute-done.1.refs_0_, bf16[5120,1536]{1,0:T(8,128)(2,1)} %refs_1_.9, ...), custom_call_target="tpu_custom_call" | custom-call | flops 1509949440 | bytes 7864320 | tf_op jit(solution)/shard_map/pallas_call | solution.py:129
  50.2 9.1 %shard_map.58 = (bf16[192,768]{1,0:T(8,128)(2,1)S(1)}, bf16[192,768]{1,0:T(8,128)(2,1)S(1)}, bf16[192,768]{1,0:T(8,128)(2,1)S(1)}, bf16[192,768]{1,0:T(8,128)(2,1)S(1)}) custom-call(s32[4]{0:T(128)S(1)} %pad_add_fusion.place, bf16[192,2560]{1,0:T(8,128)(2,1)S(1)} %collective-permute-done.3.refs_0_, bf16[5120,1536]{1,0:T(8,128)(2,1)} %refs_1_.8, ...), custom_call_target="tpu_custom_call" | custom-call | flops 3019898880 | bytes 15728640 | tf_op jit(solution)/shard_map/pallas_call | solution.py:129
  59.3 1.3 collective-permute-start.6
  60.6 5.8 %collective-permute-done.7.refs_4_.refs_12_ = bf16[208,768]{1,0:T(8,128)(2,1)S(1)} collective-permute-done((bf16[208,768]{1,0:T(8,128)(2,1)S(1)}, bf16[208,768]{1,0:T(8,128)(2,1)S(1)}, u32[]{:S(2)}, u32[]{:S(2)}) %collective-permute-start.7) | collective-permute-done | bytes 319520 | tf_op jit(solution)/shard_map/ppermute | solution.py:19
  67.0 1.5 collective-permute-start.11
  68.5 4.9 %collective-permute-start.15 = (bf16[192,768]{1,0:T(8,128)(2,1)S(1)}, bf16[192,768]{1,0:T(8,128)(2,1)S(1)}, u32[]{:S(2)}, u32[]{:S(2)}) collective-permute-start(bf16[192,768]{1,0:T(8,128)(2,1)S(1)} %get-tuple-element.98), channel_id=1, source_target_pairs={{0,16},{2,18},{4,20},{6,22},{8,24},{10,26},{12,28},{14,30},{16,0},... | collective-permute-start | bytes 884744 | tf_op jit(solution)/shard_map/ppermute | solution.py:19
  73.4 0.6 collective-permute-start.18
  74.0 2.9 %collective-permute-done.8.refs_5_.refs_14_ = bf16[208,768]{1,0:T(8,128)(2,1)S(1)} collective-permute-done((bf16[208,768]{1,0:T(8,128)(2,1)S(1)}, bf16[208,768]{1,0:T(8,128)(2,1)S(1)}, u32[]{:S(2)}, u32[]{:S(2)}) %collective-permute-start.8) | collective-permute-done | bytes 319520 | tf_op jit(solution)/shard_map/ppermute | solution.py:19
  76.9 1.0 collective-permute-start.10
  77.9 5.3 %collective-permute-done.11.refs_7_ = bf16[192,768]{1,0:T(8,128)(2,1)S(1)} collective-permute-done((bf16[192,768]{1,0:T(8,128)(2,1)S(1)}, bf16[192,768]{1,0:T(8,128)(2,1)S(1)}, u32[]{:S(2)}, u32[]{:S(2)}) %collective-permute-start.11) | collective-permute-done | bytes 294944 | tf_op jit(solution)/shard_map/ppermute | solution.py:19
  83.2 1.1 collective-permute-start.13
  84.4 1.5 collective-permute-start.21
  85.9 6.8 %collective-permute-done.15.refs_13_ = bf16[192,768]{1,0:T(8,128)(2,1)S(1)} collective-permute-done((bf16[192,768]{1,0:T(8,128)(2,1)S(1)}, bf16[192,768]{1,0:T(8,128)(2,1)S(1)}, u32[]{:S(2)}, u32[]{:S(2)}) %collective-permute-start.15) | collective-permute-done | bytes 294944 | tf_op jit(solution)/shard_map/ppermute | solution.py:19
  93.2 1.5 collective-permute-start.23
  94.8 3.7 %collective-permute-start.16 = (bf16[192,384]{1,0:T(8,128)(2,1)S(1)}, bf16[192,384]{1,0:T(8,128)(2,1)S(1)}, u32[]{:S(2)}, u32[]{:S(2)}) collective-permute-start(bf16[192,384]{1,0:T(8,128)(2,1)S(1)} %get-tuple-element.99), channel_id=1, source_target_pairs={{0,16},{2,18},{4,20},{6,22},{8,24},{10,26},{12,28},{14,30},{16,0},... | collective-permute-start | bytes 442376 | tf_op jit(solution)/shard_map/ppermute | solution.py:19
  98.5 1.6 %collective-permute-start.19 = (bf16[192,384]{1,0:T(8,128)(2,1)S(1)}, bf16[192,384]{1,0:T(8,128)(2,1)S(1)}, u32[]{:S(2)}, u32[]{:S(2)}) collective-permute-start(bf16[192,384]{1,0:T(8,128)(2,1)S(1)} %get-tuple-element.105), channel_id=1, source_target_pairs={{0,24},{2,26},{4,28},{6,30},{8,16},{10,18},{12,20},{14,22},{16,8},... | collective-permute-start | bytes 442376 | tf_op jit(solution)/shard_map/ppermute | solution.py:19
  100.1 6.2 %shard_map.60 = (bf16[192,384]{1,0:T(8,128)(2,1)S(1)}, bf16[192,384]{1,0:T(8,128)(2,1)S(1)}, bf16[192,384]{1,0:T(8,128)(2,1)S(1)}, bf16[192,384]{1,0:T(8,128)(2,1)S(1)}) custom-call(s32[4]{0:T(128)S(1)} %pad_add_fusion.place, bf16[192,2560]{1,0:T(8,128)(2,1)S(1)} %collective-permute-done.3.refs_0_, bf16[5120,1536]{1,0:T(8,128)(2,1)} %refs_1_.9, ...), custom_call_target="tpu_custom_call" | custom-call | flops 1509949440 | bytes 7864320 | tf_op jit(solution)/shard_map/pallas_call | solution.py:129
  106.4 1.6 collective-permute-done.16.refs_2_
  108.1 0.8 shard_map.59.table
  108.9 2.7 %collective-permute-start.17 = (bf16[192,384]{1,0:T(8,128)(2,1)S(1)}, bf16[192,384]{1,0:T(8,128)(2,1)S(1)}, u32[]{:S(2)}, u32[]{:S(2)}) collective-permute-start(bf16[192,384]{1,0:T(8,128)(2,1)S(1)} %get-tuple-element.100), channel_id=1, source_target_pairs={{0,16},{2,18},{4,20},{6,22},{8,24},{10,26},{12,28},{14,30},{16,0},... | collective-permute-start | bytes 442376 | tf_op jit(solution)/shard_map/ppermute | solution.py:19
  111.5 1.8 %collective-permute-start.20 = (bf16[192,384]{1,0:T(8,128)(2,1)S(1)}, bf16[192,384]{1,0:T(8,128)(2,1)S(1)}, u32[]{:S(2)}, u32[]{:S(2)}) collective-permute-start(bf16[192,384]{1,0:T(8,128)(2,1)S(1)} %get-tuple-element.106), channel_id=1, source_target_pairs={{0,24},{2,26},{4,28},{6,30},{8,16},{10,18},{12,20},{14,22},{16,8},... | collective-permute-start | bytes 442376 | tf_op jit(solution)/shard_map/ppermute | solution.py:19
  113.4 0.7 copy-done.19
  114.0 0.7 copy-done.20
  114.8 12.0 %shard_map.62 = (bf16[192,384]{1,0:T(8,128)(2,1)}, bf16[192,384]{1,0:T(8,128)(2,1)}, bf16[192,384]{1,0:T(8,128)(2,1)}, bf16[192,384]{1,0:T(8,128)(2,1)}) custom-call(s32[16]{0:T(128)} %copy-done.10, bf16[192,384]{1,0:T(8,128)(2,1)} %copy-done.12, bf16[192,384]{1,0:T(8,128)(2,1)} %copy-done.21, bf16[192,384]{1,0:T(8,128)(2,1)} %copy-done.25, ...), custom_call_target="tpu_custom_call" | custom-call | flops 2717908992 | bytes 5898240 | tf_op jit(solution)/shard_map/pallas_call | solution.py:280
  126.8 2.1 %collective-permute-start.28 = (bf16[192,384]{1,0:T(8,128)(2,1)}, bf16[192,384]{1,0:T(8,128)(2,1)S(1)}, u32[]{:S(2)}, u32[]{:S(2)}) collective-permute-start(bf16[192,384]{1,0:T(8,128)(2,1)} %get-tuple-element.111), channel_id=1, source_target_pairs={{0,24},{2,26},{4,28},{6,30},{8,16},{10,18},{12,20},{14,22},{16,8},... | collective-permute-start | bytes 442376 | tf_op jit(solution)/shard_map/ppermute | solution.py:19
  128.9 2.3 %collective-permute-start.30 = (bf16[192,384]{1,0:T(8,128)(2,1)}, bf16[192,384]{1,0:T(8,128)(2,1)S(1)}, u32[]{:S(2)}, u32[]{:S(2)}) collective-permute-start(bf16[192,384]{1,0:T(8,128)(2,1)} %get-tuple-element.113), channel_id=1, source_target_pairs={{0,8},{2,10},{4,12},{6,14},{8,0},{10,2},{12,4},{14,6},{16,24},{18,... | collective-permute-start | bytes 442376 | tf_op jit(solution)/shard_map/ppermute | solution.py:19
  131.3 0.6 copy-done.23
  131.9 0.7 copy-done.24
  132.6 12.3 %shard_map.61 = (bf16[192,384]{1,0:T(8,128)(2,1)}, bf16[192,384]{1,0:T(8,128)(2,1)}, bf16[192,384]{1,0:T(8,128)(2,1)}, bf16[192,384]{1,0:T(8,128)(2,1)}) custom-call(s32[16]{0:T(128)} %copy-done.10, bf16[192,384]{1,0:T(8,128)(2,1)} %copy-done.13, bf16[192,384]{1,0:T(8,128)(2,1)} %copy-done.22, bf16[192,384]{1,0:T(8,128)(2,1)} %copy-done.23, ...), custom_call_target="tpu_custom_call" | custom-call | flops 2717908992 | bytes 5898240 | tf_op jit(solution)/shard_map/pallas_call | solution.py:280
  144.9 1.2 collective-permute-start.25
  146.2 1.2 collective-permute-start.26
  147.4 1.8 %collective-permute-start.27 = (bf16[192,384]{1,0:T(8,128)(2,1)}, bf16[192,384]{1,0:T(8,128)(2,1)S(1)}, u32[]{:S(2)}, u32[]{:S(2)}) collective-permute-start(bf16[192,384]{1,0:T(8,128)(2,1)} %get-tuple-element.110), channel_id=1, source_target_pairs={{0,2},{2,0},{4,6},{6,4},{8,10},{10,8},{12,14},{14,12},{16,18},{18,... | collective-permute-start | bytes 442376 | tf_op jit(solution)/shard_map/ppermute | solution.py:19
  149.2 2.0 %shard_map.63.refs_4_ = bf16[2,192,1536]{2,1,0:T(8,128)(2,1)} custom-call(s32[4]{0:T(128)S(1)} %pad_add_fusion.place, bf16[192,384]{1,0:T(8,128)(2,1)S(1)} %collective-permute-done.28.refs_0_, bf16[192,384]{1,0:T(8,128)(2,1)S(1)} %collective-permute-done.29.refs_1_, bf16[192,384]{1,0:T(8,128)(2,1)S(1)} %collective-permute-done.30.refs_2_, ...), custom_call_target="tpu_custom_call" | custom-call | tf_op jit(solution)/shard_map/pallas_call | solution.py:348
  151.2 2.0 %collective-permute-done.24.refs_0_ = bf16[192,384]{1,0:T(8,128)(2,1)S(1)} collective-permute-done((bf16[192,384]{1,0:T(8,128)(2,1)}, bf16[192,384]{1,0:T(8,128)(2,1)S(1)}, u32[]{:S(2)}, u32[]{:S(2)}) %collective-permute-start.24) | collective-permute-done | bytes 147488 | tf_op jit(solution)/shard_map/ppermute | solution.py:19
  153.2 6.8 %collective-permute-done.25.refs_1_ = bf16[192,384]{1,0:T(8,128)(2,1)S(1)} collective-permute-done((bf16[192,384]{1,0:T(8,128)(2,1)}, bf16[192,384]{1,0:T(8,128)(2,1)S(1)}, u32[]{:S(2)}, u32[]{:S(2)}) %collective-permute-start.25) | collective-permute-done | bytes 147488 | tf_op jit(solution)/shard_map/ppermute | solution.py:19
  160.0 2.0 %shard_map.64 = bf16[2,192,1536]{2,1,0:T(8,128)(2,1)} custom-call(s32[4]{0:T(128)S(1)} %pad_add_fusion.place, bf16[192,384]{1,0:T(8,128)(2,1)S(1)} %collective-permute-done.24.refs_0_, bf16[192,384]{1,0:T(8,128)(2,1)S(1)} %collective-permute-done.25.refs_1_, bf16[192,384]{1,0:T(8,128)(2,1)S(1)} %collective-permute-done.26.refs_2_, ...), custom_call_target="tpu_custom_call", output_to_operand_aliasing={{}: (5, {})} | custom-call | tf_op jit(solution)/shard_map/pallas_call | solution.py:348
  (87 shorter events, 2.5 us)
Async XLA Ops:
  0.0 10.3 %copy-start = (bf16[2,192,2560]{2,1,0:T(8,128)(2,1)S(1)}, bf16[2,192,2560]{2,1,0:T(8,128)(2,1)}, u32[]{:S(2)}) copy-start(bf16[2,192,2560]{2,1,0:T(8,128)(2,1)} %mine_ref.1) | copy-start | bytes 5898244
  3.1 6.5 %collective-permute-start.2 = (bf16[192,2560]{1,0:T(8,128)(2,1)}, bf16[192,2560]{1,0:T(8,128)(2,1)}, u32[]{:S(2)}, u32[]{:S(2)}) collective-permute-start(bf16[192,2560]{1,0:T(8,128)(2,1)} %get-tuple-element.115), channel_id=1, source_target_pairs={{0,2},{2,0},{4,6},{6,4},{8,10},{10,8},{12,14},{14,12},{16,18},{18,... | collective-permute-start | bytes 2949128 | tf_op jit(solution)/shard_map/ppermute | solution.py:19
  3.5 25.3 %collective-permute-start.1 = (bf16[192,2560]{1,0:T(8,128)(2,1)}, bf16[192,2560]{1,0:T(8,128)(2,1)S(1)}, u32[]{:S(2)}, u32[]{:S(2)}) collective-permute-start(bf16[192,2560]{1,0:T(8,128)(2,1)} %get-tuple-element.116), channel_id=1, source_target_pairs={{0,1},{1,0},{2,3},{3,2},{4,5},{5,4},{6,7},{7,6},{8,9},{9,8},{10,11... | collective-permute-start | bytes 2949128 | tf_op jit(solution)/shard_map/ppermute | solution.py:19
  6.9 1.3 collective-permute-start
  9.6 40.6 %collective-permute-start.3 = (bf16[192,2560]{1,0:T(8,128)(2,1)}, bf16[192,2560]{1,0:T(8,128)(2,1)S(1)}, u32[]{:S(2)}, u32[]{:S(2)}) collective-permute-start(bf16[192,2560]{1,0:T(8,128)(2,1)} %collective-permute-done.2.other_ref), channel_id=1, source_target_pairs={{0,1},{1,0},{2,3},{3,2},{4,5},{5,4},{6,7},{7,6},{8,9},{9,8},{10,11... | collective-permute-start | bytes 2949128 | tf_op jit(solution)/shard_map/ppermute | solution.py:19
  37.7 70.3 %copy-start.1 = (bf16[208,768]{1,0:T(8,128)(2,1)}, bf16[208,768]{1,0:T(8,128)(2,1)S(1)}, u32[]{:S(2)}) copy-start(bf16[208,768]{1,0:T(8,128)(2,1)S(1)} %get-tuple-element.70.refs_0_.refs_4_) | copy-start | bytes 958468
  37.8 30.7 %collective-permute-start.4 = (bf16[208,768]{1,0:T(8,128)(2,1)S(1)}, bf16[208,768]{1,0:T(8,128)(2,1)S(1)}, u32[]{:S(2)}, u32[]{:S(2)}) collective-permute-start(bf16[208,768]{1,0:T(8,128)(2,1)S(1)} %get-tuple-element.70.refs_0_.refs_4_), channel_id=1, source_target_pairs={{0,4},{2,6},{4,0},{6,2},{8,12},{10,14},{12,8},{14,10},{16,20},{18,... | collective-permute-start | bytes 958472 | tf_op jit(solution)/shard_map/ppermute | solution.py:19
  39.8 19.5 %collective-permute-start.5 = (bf16[208,768]{1,0:T(8,128)(2,1)S(1)}, bf16[208,768]{1,0:T(8,128)(2,1)S(1)}, u32[]{:S(2)}, u32[]{:S(2)}) collective-permute-start(bf16[208,768]{1,0:T(8,128)(2,1)S(1)} %get-tuple-element.71), channel_id=1, source_target_pairs={{0,8},{2,10},{4,12},{6,14},{8,0},{10,2},{12,4},{14,6},{16,24},{18,... | collective-permute-start | bytes 958472 | tf_op jit(solution)/shard_map/ppermute | solution.py:19
  41.4 25.1 %collective-permute-start.7 = (bf16[208,768]{1,0:T(8,128)(2,1)S(1)}, bf16[208,768]{1,0:T(8,128)(2,1)S(1)}, u32[]{:S(2)}, u32[]{:S(2)}) collective-permute-start(bf16[208,768]{1,0:T(8,128)(2,1)S(1)} %get-tuple-element.74), channel_id=1, source_target_pairs={{0,16},{2,18},{4,20},{6,22},{8,24},{10,26},{12,28},{14,30},{16,0},... | collective-permute-start | bytes 958472 | tf_op jit(solution)/shard_map/ppermute | solution.py:19
  44.0 24.5 %collective-permute-start.9 = (bf16[208,768]{1,0:T(8,128)(2,1)S(1)}, bf16[208,768]{1,0:T(8,128)(2,1)S(1)}, u32[]{:S(2)}, u32[]{:S(2)}) collective-permute-start(bf16[208,768]{1,0:T(8,128)(2,1)S(1)} %get-tuple-element.77), channel_id=1, source_target_pairs={{0,24},{2,26},{4,28},{6,30},{8,16},{10,18},{12,20},{14,22},{16,8},... | collective-permute-start | bytes 958472 | tf_op jit(solution)/shard_map/ppermute | solution.py:19
  50.2 9.1 %copy-start.12 = (bf16[192,384]{1,0:T(8,128)(2,1)}, bf16[192,384]{1,0:T(8,128)(2,1)S(1)}, u32[]{:S(2)}) copy-start(bf16[192,384]{1,0:T(8,128)(2,1)S(1)} %get-tuple-element.86.refs_0_) | copy-start | bytes 442372
  59.3 47.1 %copy-start.11 = (bf16[192,768]{1,0:T(8,128)(2,1)}, bf16[192,768]{1,0:T(8,128)(2,1)S(1)}, u32[]{:S(2)}) copy-start(bf16[192,768]{1,0:T(8,128)(2,1)S(1)} %get-tuple-element.85.refs_5_) | copy-start | bytes 884740
  59.3 48.7 %copy-start.3 = (bf16[208,768]{1,0:T(8,128)(2,1)}, bf16[208,768]{1,0:T(8,128)(2,1)S(1)}, u32[]{:S(2)}) copy-start(bf16[208,768]{1,0:T(8,128)(2,1)S(1)} %collective-permute-done.5.refs_2_.refs_8_) | copy-start | bytes 958468
  59.3 14.1 %collective-permute-start.6 = (bf16[208,768]{1,0:T(8,128)(2,1)S(1)}, bf16[208,768]{1,0:T(8,128)(2,1)S(1)}, u32[]{:S(2)}, u32[]{:S(2)}) collective-permute-start(bf16[208,768]{1,0:T(8,128)(2,1)S(1)} %collective-permute-done.5.refs_2_.refs_8_), channel_id=1, source_target_pairs={{0,4},{2,6},{4,0},{6,2},{8,12},{10,14},{12,8},{14,10},{16,20},{18,... | collective-permute-start | bytes 958472 | tf_op jit(solution)/shard_map/ppermute | solution.py:19
  66.4 41.6 %copy-start.4 = (bf16[208,768]{1,0:T(8,128)(2,1)}, bf16[208,768]{1,0:T(8,128)(2,1)S(1)}, u32[]{:S(2)}) copy-start(bf16[208,768]{1,0:T(8,128)(2,1)S(1)} %collective-permute-done.7.refs_4_.refs_12_) | copy-start | bytes 958468
  66.4 10.5 %collective-permute-start.8 = (bf16[208,768]{1,0:T(8,128)(2,1)S(1)}, bf16[208,768]{1,0:T(8,128)(2,1)S(1)}, u32[]{:S(2)}, u32[]{:S(2)}) collective-permute-start(bf16[208,768]{1,0:T(8,128)(2,1)S(1)} %collective-permute-done.7.refs_4_.refs_12_), channel_id=1, source_target_pairs={{0,4},{2,6},{4,0},{6,2},{8,12},{10,14},{12,8},{14,10},{16,20},{18,... | collective-permute-start | bytes 958472 | tf_op jit(solution)/shard_map/ppermute | solution.py:19
  67.0 16.3 %collective-permute-start.11 = (bf16[192,768]{1,0:T(8,128)(2,1)S(1)}, bf16[192,768]{1,0:T(8,128)(2,1)S(1)}, u32[]{:S(2)}, u32[]{:S(2)}) collective-permute-start(bf16[192,768]{1,0:T(8,128)(2,1)S(1)} %get-tuple-element.85.refs_5_), channel_id=1, source_target_pairs={{0,4},{2,6},{4,0},{6,2},{8,12},{10,14},{12,8},{14,10},{16,20},{18,... | collective-permute-start | bytes 884744 | tf_op jit(solution)/shard_map/ppermute | solution.py:19
  68.5 39.6 %copy-start.2 = (bf16[208,768]{1,0:T(8,128)(2,1)}, bf16[208,768]{1,0:T(8,128)(2,1)S(1)}, u32[]{:S(2)}) copy-start(bf16[208,768]{1,0:T(8,128)(2,1)S(1)} %collective-permute-done.4.refs_1_.refs_6_) | copy-start | bytes 958468
  68.5 14.8 %collective-permute-start.12 = (bf16[192,768]{1,0:T(8,128)(2,1)S(1)}, bf16[192,768]{1,0:T(8,128)(2,1)S(1)}, u32[]{:S(2)}, u32[]{:S(2)}) collective-permute-start(bf16[192,768]{1,0:T(8,128)(2,1)S(1)} %get-tuple-element.91), channel_id=1, source_target_pairs={{0,8},{2,10},{4,12},{6,14},{8,0},{10,2},{12,4},{14,6},{16,24},{18,... | collective-permute-start | bytes 884744 | tf_op jit(solution)/shard_map/ppermute | solution.py:19
  68.5 39.5 %copy-start.5 = (bf16[208,768]{1,0:T(8,128)(2,1)}, bf16[208,768]{1,0:T(8,128)(2,1)S(1)}, u32[]{:S(2)}) copy-start(bf16[208,768]{1,0:T(8,128)(2,1)S(1)} %collective-permute-done.9.refs_6_.refs_16_) | copy-start | bytes 958468
  68.5 24.2 %collective-permute-start.15 = (bf16[192,768]{1,0:T(8,128)(2,1)S(1)}, bf16[192,768]{1,0:T(8,128)(2,1)S(1)}, u32[]{:S(2)}, u32[]{:S(2)}) collective-permute-start(bf16[192,768]{1,0:T(8,128)(2,1)S(1)} %get-tuple-element.98), channel_id=1, source_target_pairs={{0,16},{2,18},{4,20},{6,22},{8,24},{10,26},{12,28},{14,30},{16,0},... | collective-permute-start | bytes 884744 | tf_op jit(solution)/shard_map/ppermute | solution.py:19
  73.4 34.7 %copy-start.6 = (bf16[208,768]{1,0:T(8,128)(2,1)}, bf16[208,768]{1,0:T(8,128)(2,1)S(1)}, u32[]{:S(2)}) copy-start(bf16[208,768]{1,0:T(8,128)(2,1)S(1)} %collective-permute-done.6.refs_3_.refs_10_) | copy-start | bytes 958468
  73.4 19.8 %collective-permute-start.18 = (bf16[192,768]{1,0:T(8,128)(2,1)S(1)}, bf16[192,768]{1,0:T(8,128)(2,1)S(1)}, u32[]{:S(2)}, u32[]{:S(2)}) collective-permute-start(bf16[192,768]{1,0:T(8,128)(2,1)S(1)} %get-tuple-element.104), channel_id=1, source_target_pairs={{0,24},{2,26},{4,28},{6,30},{8,16},{10,18},{12,20},{14,22},{16,8},... | collective-permute-start | bytes 884744 | tf_op jit(solution)/shard_map/ppermute | solution.py:19
  76.9 31.1 %copy-start.7 = (bf16[208,768]{1,0:T(8,128)(2,1)}, bf16[208,768]{1,0:T(8,128)(2,1)S(1)}, u32[]{:S(2)}) copy-start(bf16[208,768]{1,0:T(8,128)(2,1)S(1)} %collective-permute-done.8.refs_5_.refs_14_) | copy-start | bytes 958468
  76.9 17.8 %collective-permute-start.10 = (bf16[208,768]{1,0:T(8,128)(2,1)S(1)}, bf16[208,768]{1,0:T(8,128)(2,1)S(1)}, u32[]{:S(2)}, u32[]{:S(2)}) collective-permute-start(bf16[208,768]{1,0:T(8,128)(2,1)S(1)} %collective-permute-done.9.refs_6_.refs_16_), channel_id=1, source_target_pairs={{0,4},{2,6},{4,0},{6,2},{8,12},{10,14},{12,8},{14,10},{16,20},{18,... | collective-permute-start | bytes 958472 | tf_op jit(solution)/shard_map/ppermute | solution.py:19
  83.2 23.1 %copy-start.14 = (bf16[192,768]{1,0:T(8,128)(2,1)}, bf16[192,768]{1,0:T(8,128)(2,1)S(1)}, u32[]{:S(2)}) copy-start(bf16[192,768]{1,0:T(8,128)(2,1)S(1)} %collective-permute-done.11.refs_7_) | copy-start | bytes 884740
  83.2 23.1 %copy-start.15 = (bf16[192,768]{1,0:T(8,128)(2,1)}, bf16[192,768]{1,0:T(8,128)(2,1)S(1)}, u32[]{:S(2)}) copy-start(bf16[192,768]{1,0:T(8,128)(2,1)S(1)} %collective-permute-done.12.refs_9_) | copy-start | bytes 884740
  83.2 15.3 %collective-permute-start.13 = (bf16[192,384]{1,0:T(8,128)(2,1)S(1)}, bf16[192,384]{1,0:T(8,128)(2,1)S(1)}, u32[]{:S(2)}, u32[]{:S(2)}) collective-permute-start(bf16[192,384]{1,0:T(8,128)(2,1)S(1)} %get-tuple-element.93), channel_id=1, source_target_pairs={{0,8},{2,10},{4,12},{6,14},{8,0},{10,2},{12,4},{14,6},{16,24},{18,... | collective-permute-start | bytes 442376 | tf_op jit(solution)/shard_map/ppermute | solution.py:19
  84.4 27.2 %collective-permute-start.21 = (bf16[192,768]{1,0:T(8,128)(2,1)S(1)}, bf16[192,768]{1,0:T(8,128)(2,1)S(1)}, u32[]{:S(2)}, u32[]{:S(2)}) collective-permute-start(bf16[192,768]{1,0:T(8,128)(2,1)S(1)} %collective-permute-done.12.refs_9_), channel_id=1, source_target_pairs={{0,4},{2,6},{4,0},{6,2},{8,12},{10,14},{12,8},{14,10},{16,20},{18,... | collective-permute-start | bytes 884744 | tf_op jit(solution)/shard_map/ppermute | solution.py:19
  92.7 13.6 %copy-start.16 = (bf16[192,768]{1,0:T(8,128)(2,1)}, bf16[192,768]{1,0:T(8,128)(2,1)S(1)}, u32[]{:S(2)}) copy-start(bf16[192,768]{1,0:T(8,128)(2,1)S(1)} %collective-permute-done.15.refs_13_) | copy-start | bytes 884740
  92.7 20.6 %collective-permute-start.22 = (bf16[192,768]{1,0:T(8,128)(2,1)S(1)}, bf16[192,768]{1,0:T(8,128)(2,1)S(1)}, u32[]{:S(2)}, u32[]{:S(2)}) collective-permute-start(bf16[192,768]{1,0:T(8,128)(2,1)S(1)} %collective-permute-done.15.refs_13_), channel_id=1, source_target_pairs={{0,4},{2,6},{4,0},{6,2},{8,12},{10,14},{12,8},{14,10},{16,20},{18,... | collective-permute-start | bytes 884744 | tf_op jit(solution)/shard_map/ppermute | solution.py:19
  93.2 13.2 %copy-start.17 = (bf16[192,768]{1,0:T(8,128)(2,1)}, bf16[192,768]{1,0:T(8,128)(2,1)S(1)}, u32[]{:S(2)}) copy-start(bf16[192,768]{1,0:T(8,128)(2,1)S(1)} %collective-permute-done.18.refs_17_) | copy-start | bytes 884740
  93.2 20.1 %collective-permute-start.23 = (bf16[192,768]{1,0:T(8,128)(2,1)S(1)}, bf16[192,768]{1,0:T(8,128)(2,1)S(1)}, u32[]{:S(2)}, u32[]{:S(2)}) collective-permute-start(bf16[192,768]{1,0:T(8,128)(2,1)S(1)} %collective-permute-done.18.refs_17_), channel_id=1, source_target_pairs={{0,4},{2,6},{4,0},{6,2},{8,12},{10,14},{12,8},{14,10},{16,20},{18,... | collective-permute-start | bytes 884744 | tf_op jit(solution)/shard_map/ppermute | solution.py:19
  94.8 13.3 %copy-start.8 = (bf16[208,768]{1,0:T(8,128)(2,1)}, bf16[208,768]{1,0:T(8,128)(2,1)S(1)}, u32[]{:S(2)}) copy-start(bf16[208,768]{1,0:T(8,128)(2,1)S(1)} %collective-permute-done.10.refs_7_.refs_18_) | copy-start | bytes 958468
  94.8 13.2 %collective-permute-start.16 = (bf16[192,384]{1,0:T(8,128)(2,1)S(1)}, bf16[192,384]{1,0:T(8,128)(2,1)S(1)}, u32[]{:S(2)}, u32[]{:S(2)}) collective-permute-start(bf16[192,384]{1,0:T(8,128)(2,1)S(1)} %get-tuple-element.99), channel_id=1, source_target_pairs={{0,16},{2,18},{4,20},{6,22},{8,24},{10,26},{12,28},{14,30},{16,0},... | collective-permute-start | bytes 442376 | tf_op jit(solution)/shard_map/ppermute | solution.py:19
  98.5 7.9 %copy-start.21 = (bf16[192,384]{1,0:T(8,128)(2,1)}, bf16[192,384]{1,0:T(8,128)(2,1)S(1)}, u32[]{:S(2)}) copy-start(bf16[192,384]{1,0:T(8,128)(2,1)S(1)} %collective-permute-done.13.refs_1_) | copy-start | bytes 442372
  98.5 10.3 %collective-permute-start.19 = (bf16[192,384]{1,0:T(8,128)(2,1)S(1)}, bf16[192,384]{1,0:T(8,128)(2,1)S(1)}, u32[]{:S(2)}, u32[]{:S(2)}) collective-permute-start(bf16[192,384]{1,0:T(8,128)(2,1)S(1)} %get-tuple-element.105), channel_id=1, source_target_pairs={{0,24},{2,26},{4,28},{6,30},{8,16},{10,18},{12,20},{14,22},{16,8},... | collective-permute-start | bytes 442376 | tf_op jit(solution)/shard_map/ppermute | solution.py:19
  108.0 20.9 %collective-permute-start.14 = (bf16[192,384]{1,0:T(8,128)(2,1)S(1)}, bf16[192,384]{1,0:T(8,128)(2,1)S(1)}, u32[]{:S(2)}, u32[]{:S(2)}) collective-permute-start(bf16[192,384]{1,0:T(8,128)(2,1)S(1)} %get-tuple-element.94), channel_id=1, source_target_pairs={{0,8},{2,10},{4,12},{6,14},{8,0},{10,2},{12,4},{14,6},{16,24},{18,... | collective-permute-start | bytes 442376 | tf_op jit(solution)/shard_map/ppermute | solution.py:19
  108.9 22.4 %collective-permute-start.17 = (bf16[192,384]{1,0:T(8,128)(2,1)S(1)}, bf16[192,384]{1,0:T(8,128)(2,1)S(1)}, u32[]{:S(2)}, u32[]{:S(2)}) collective-permute-start(bf16[192,384]{1,0:T(8,128)(2,1)S(1)} %get-tuple-element.100), channel_id=1, source_target_pairs={{0,16},{2,18},{4,20},{6,22},{8,24},{10,26},{12,28},{14,30},{16,0},... | collective-permute-start | bytes 442376 | tf_op jit(solution)/shard_map/ppermute | solution.py:19
  111.5 19.7 %collective-permute-start.20 = (bf16[192,384]{1,0:T(8,128)(2,1)S(1)}, bf16[192,384]{1,0:T(8,128)(2,1)S(1)}, u32[]{:S(2)}, u32[]{:S(2)}) collective-permute-start(bf16[192,384]{1,0:T(8,128)(2,1)S(1)} %get-tuple-element.106), channel_id=1, source_target_pairs={{0,24},{2,26},{4,28},{6,30},{8,16},{10,18},{12,20},{14,22},{16,8},... | collective-permute-start | bytes 442376 | tf_op jit(solution)/shard_map/ppermute | solution.py:19
  126.8 19.4 %collective-permute-start.28 = (bf16[192,384]{1,0:T(8,128)(2,1)}, bf16[192,384]{1,0:T(8,128)(2,1)S(1)}, u32[]{:S(2)}, u32[]{:S(2)}) collective-permute-start(bf16[192,384]{1,0:T(8,128)(2,1)} %get-tuple-element.111), channel_id=1, source_target_pairs={{0,24},{2,26},{4,28},{6,30},{8,16},{10,18},{12,20},{14,22},{16,8},... | collective-permute-start | bytes 442376 | tf_op jit(solution)/shard_map/ppermute | solution.py:19
  128.9 18.4 %collective-permute-start.29 = (bf16[192,384]{1,0:T(8,128)(2,1)}, bf16[192,384]{1,0:T(8,128)(2,1)S(1)}, u32[]{:S(2)}, u32[]{:S(2)}) collective-permute-start(bf16[192,384]{1,0:T(8,128)(2,1)} %get-tuple-element.112), channel_id=1, source_target_pairs={{0,16},{2,18},{4,20},{6,22},{8,24},{10,26},{12,28},{14,30},{16,0},... | collective-permute-start | bytes 442376 | tf_op jit(solution)/shard_map/ppermute | solution.py:19
  128.9 20.2 %copy-start.9 = (bf16[192,384]{1,0:T(8,128)(2,1)S(1)}, bf16[192,384]{1,0:T(8,128)(2,1)}, u32[]{:S(2)}) copy-start(bf16[192,384]{1,0:T(8,128)(2,1)} %get-tuple-element.114.refs_3_) | copy-start | bytes 442372
  128.9 20.2 %collective-permute-start.30 = (bf16[192,384]{1,0:T(8,128)(2,1)}, bf16[192,384]{1,0:T(8,128)(2,1)S(1)}, u32[]{:S(2)}, u32[]{:S(2)}) collective-permute-start(bf16[192,384]{1,0:T(8,128)(2,1)} %get-tuple-element.113), channel_id=1, source_target_pairs={{0,8},{2,10},{4,12},{6,14},{8,0},{10,2},{12,4},{14,6},{16,24},{18,... | collective-permute-start | bytes 442376 | tf_op jit(solution)/shard_map/ppermute | solution.py:19
  144.9 8.3 %collective-permute-start.24 = (bf16[192,384]{1,0:T(8,128)(2,1)}, bf16[192,384]{1,0:T(8,128)(2,1)S(1)}, u32[]{:S(2)}, u32[]{:S(2)}) collective-permute-start(bf16[192,384]{1,0:T(8,128)(2,1)} %get-tuple-element.107), channel_id=1, source_target_pairs={{0,26},{2,24},{4,30},{6,28},{8,18},{10,16},{12,22},{14,20},{16,10}... | collective-permute-start | bytes 442376 | tf_op jit(solution)/shard_map/ppermute | solution.py:19
  144.9 15.0 %collective-permute-start.25 = (bf16[192,384]{1,0:T(8,128)(2,1)}, bf16[192,384]{1,0:T(8,128)(2,1)S(1)}, u32[]{:S(2)}, u32[]{:S(2)}) collective-permute-start(bf16[192,384]{1,0:T(8,128)(2,1)} %get-tuple-element.108), channel_id=1, source_target_pairs={{0,18},{2,16},{4,22},{6,20},{8,26},{10,24},{12,30},{14,28},{16,2},... | collective-permute-start | bytes 442376 | tf_op jit(solution)/shard_map/ppermute | solution.py:19
  146.2 13.8 %collective-permute-start.26 = (bf16[192,384]{1,0:T(8,128)(2,1)}, bf16[192,384]{1,0:T(8,128)(2,1)S(1)}, u32[]{:S(2)}, u32[]{:S(2)}) collective-permute-start(bf16[192,384]{1,0:T(8,128)(2,1)} %get-tuple-element.109), channel_id=1, source_target_pairs={{0,10},{2,8},{4,14},{6,12},{8,2},{10,0},{12,6},{14,4},{16,26},{18,... | collective-permute-start | bytes 442376 | tf_op jit(solution)/shard_map/ppermute | solution.py:19
  147.4 12.6 %collective-permute-start.27 = (bf16[192,384]{1,0:T(8,128)(2,1)}, bf16[192,384]{1,0:T(8,128)(2,1)S(1)}, u32[]{:S(2)}, u32[]{:S(2)}) collective-permute-start(bf16[192,384]{1,0:T(8,128)(2,1)} %get-tuple-element.110), channel_id=1, source_target_pairs={{0,2},{2,0},{4,6},{6,4},{8,10},{10,8},{12,14},{14,12},{16,18},{18,... | collective-permute-start | bytes 442376 | tf_op jit(solution)/shard_map/ppermute | solution.py:19
  (11 other events, 29.7 us)

commit v13 on v12

--- a/solution.py
+++ b/solution.py
@@ -390,7 +390,12 @@
     spans = event_pos[:, 0] // (rows // 2)
     span_other = over_ctx(lax.dynamic_index_in_dim(spans, 1 - core, 0), 1)
     later = jnp.concatenate([place, lax.dynamic_index_in_dim(spans, core, 0), span_other])
-    (made_0,) = rest_products(received, [0], [w_k, w_v], [start_k, start_v], later, ways, away, EXTRA)
+    made_0 = {}
+    for part in (away[::-2], away[-2::-2]):
+        if part:
+            made_0.update(
+                rest_products(received, [0], [w_k, w_v], [start_k, start_v], later, ways, part, EXTRA)[0]
+            )
     first = {a: over_ctx(made_0[a], a * rest) for a in away}
     ahead = over_ctx(made_0[0], rest // 2)
     asked = rest_products(received, [0], [w_q], [start_q], place, ways, away)
@@ -420,17 +425,19 @@
         blocks[a * rest + rest // 2] = before[-1]
     blocks = over_y(blocks)
     second = {}
+    for a in away:
+        value, _ = lax.optimization_barrier((made_1[a], (first[a], ahead)))
+        second[a * rest + 1] = over_ctx(value, a * rest)
     queries = [{}, {}]
     for a in away:
-        last = (first[a], ahead)
-        for made, keep, key in ((made_1, second, a * rest + 1), (asked[0], queries[0], a), (asked[1], queries[1], a)):
-            value, last = lax.optimization_barrier((made[a], last))
-            last = keep[key] = over_ctx(value, a * rest)
-            if keep is second and a:
-                last = (last, ahead_1)
-            if keep is second and a == ways - 1:
-                last = (last, [blocks[i] for i in sorted(blocks)])
-
+        wait = (second[a * rest + 1], ahead_1) if a else ()
+        if a == ways - 1:
+            wait = (wait, [blocks[i] for i in sorted(blocks)])
+        value, _ = lax.optimization_barrier((asked[0][a], wait))
+        queries[0][a] = over_ctx(value, a * rest)
+    for a in away:
+        value, _ = lax.optimization_barrier((asked[1][a], queries[0][min(1, ways - 1)]))
+        queries[1][a] = over_ctx(value, a * rest)
     table = span_table({i: (array, 0) for i, array in blocks.items()}, rows)
     second[rest // 2 + 1] = ahead_1
     blocks.update(over_y(second))

time: 162 us -> 162 us (level)
  waiting for transfers between devices: 33.2 us -> 30.6 us
    ppermute x31, waiting for transfers between devices: 33.2 us -> 30.6 us  [exchange(): return lax.ppermute(value, axis, [(i, i ^ bit) for i in range(size)])]
    pallas_call x4 -> x5, Pallas kernels: 30.2 us -> 31.7 us  [rest_products(): pl.pallas_call(functools.partial(rest_body, shares, len(weights), chunks,...]
    unnamed x56 -> x58, local copies, waits for them, and re-layouts: 2.8 us -> 3.3 us
  transfers between devices with their start and end apart: 31 -> 31, of which waited for: 9 -> 9; matrix products, arithmetic and copies ran while one was open for 1% -> 2% of each run, Pallas kernels for 46% -> 47%
where the time goes in v13:
time: 162 us
  Pallas kernels  78.4 us (48%)
  starting transfers between devices  43.3 us (27%)
  waiting for transfers between devices  30.6 us (19%)
  local copies, waits for them, and re-layouts  8.48 us (5%)
    ppermute x31, starting transfers between devices, exchange(): return lax.ppermute(value, axis, [(i, i ^ bit) for i in range(size)])  43.3 us
    pallas_call x5, Pallas kernels, rest_products(): pl.pallas_call(functools.partial(rest_body, shares, len(weights), chunks,...  31.7 us
    ppermute x31, waiting for transfers between devices, exchange(): return lax.ppermute(value, axis, [(i, i ^ bit) for i in range(size)])  30.6 us
    pallas_call x2, Pallas kernels, attend(): pl.pallas_call(functools.partial(attend_body, block, ways, slots, len(arr...  24.3 us
    pallas_call x1, Pallas kernels, own_products(): pl.pallas_call(functools.partial(own_body, len(weights)), out_shape=[jax....  17.7 us
    pallas_call x2, Pallas kernels, assemble(): pl.pallas_call(functools.partial(assemble_body, ways), out_shape=jax.Shap...  3.99 us
    unnamed x58, local copies, waits for them, and re-layouts  3.3 us
  transfers between devices with their start and end apart: 31, of which 9 were waited for; matrix products, arithmetic and copies ran while one was open for 2% of the time, Pallas kernels for 47%

profile of v13, /device:TPU:0, one launch (start us, length us, event | category | flops | bytes accessed | tf_op | source)
XLA Modules:
  0.0 161.6 jit_solution(7367814129039912812)
XLA Ops:
  0.0 3.1 %dynamic-slice_bitcast_fusion = (bf16[192,2560]{1,0:T(8,128)(2,1)}, bf16[192,2560]{1,0:T(8,128)(2,1)}) fusion(bf16[2,192,2560]{2,1,0:T(8,128)(2,1)} %mine_ref.1, s32[]{:T(128)S(6)} %select_n.30, s32[]{:T(128)S(6)} %select_n.29), kind=kLoop, calls=%fused_computation | loop fusion | bytes 3932168 | tf_op jit(solution)/shard_map/jit(dynamic_index_in_dim)/squeeze | solution.py:385
  3.5 2.5 %collective-permute-start.1 = (bf16[192,2560]{1,0:T(8,128)(2,1)}, bf16[192,2560]{1,0:T(8,128)(2,1)S(1)}, u32[]{:S(2)}, u32[]{:S(2)}) collective-permute-start(bf16[192,2560]{1,0:T(8,128)(2,1)} %get-tuple-element.114), channel_id=1, source_target_pairs={{0,1},{1,0},{2,3},{3,2},{4,5},{5,4},{6,7},{7,6},{8,9},{9,8},{10,11... | collective-permute-start | bytes 2949128 | tf_op jit(solution)/shard_map/ppermute | solution.py:19
  6.3 0.7 fusion
  7.2 0.9 collective-permute-done
  8.1 1.4 concatenate.4.place
  9.5 0.9 collective-permute-start.3
  10.4 17.7 %shard_map.55 = (f32[2,192,1536]{2,1,0:T(8,128)S(1)}, f32[2,192,1536]{2,1,0:T(8,128)S(1)}, f32[2,192,1536]{2,1,0:T(8,128)S(1)}) custom-call(s32[4]{0:T(128)S(1)} %pad_add_fusion.place, bf16[2,192,2560]{2,1,0:T(8,128)(2,1)S(1)} %copy-done, bf16[192,2560]{1,0:T(8,128)(2,1)} %collective-permute-done.2.other_ref, bf16[5120,1536]{1,0:T(8,128)(2,1)} %refs_1_.10, ...), custom_call_target="tpu_custom_call" | custom-call | flops 9059696640 | bytes 23592960 | tf_op jit(solution)/shard_map/pallas_call | solution.py:43
  28.1 0.8 collective-permute-done.1.refs_0_
  28.8 5.2 %shard_map.59 = (bf16[208,768]{1,0:T(8,128)(2,1)S(1)}, bf16[208,768]{1,0:T(8,128)(2,1)S(1)}) custom-call(s32[6]{0:T(128)S(1)} %concatenate.4.place, bf16[192,2560]{1,0:T(8,128)(2,1)S(1)} %collective-permute-done.1.refs_0_, bf16[5120,1536]{1,0:T(8,128)(2,1)} %refs_1_.10, bf16[5120,1536]{1,0:T(8,128)(2,1)} %refs_2_.7, ...), custom_call_target="tpu_custom_call" | custom-call | flops 1509949440 | bytes 7864320 | tf_op jit(solution)/shard_map/pallas_call | solution.py:129
  34.1 2.1 %collective-permute-start.5 = (bf16[208,768]{1,0:T(8,128)(2,1)S(1)}, bf16[208,768]{1,0:T(8,128)(2,1)S(1)}, u32[]{:S(2)}, u32[]{:S(2)}) collective-permute-start(bf16[208,768]{1,0:T(8,128)(2,1)S(1)} %get-tuple-element.70), channel_id=1, source_target_pairs={{0,8},{2,10},{4,12},{6,14},{8,0},{10,2},{12,4},{14,6},{16,24},{18,... | collective-permute-start | bytes 958472 | tf_op jit(solution)/shard_map/ppermute | solution.py:19
  36.2 2.5 %collective-permute-start.9 = (bf16[208,768]{1,0:T(8,128)(2,1)S(1)}, bf16[208,768]{1,0:T(8,128)(2,1)S(1)}, u32[]{:S(2)}, u32[]{:S(2)}) collective-permute-start(bf16[208,768]{1,0:T(8,128)(2,1)S(1)} %get-tuple-element.76), channel_id=1, source_target_pairs={{0,24},{2,26},{4,28},{6,30},{8,16},{10,18},{12,20},{14,22},{16,8},... | collective-permute-start | bytes 958472 | tf_op jit(solution)/shard_map/ppermute | solution.py:19
  38.7 5.3 %shard_map.56 = (bf16[208,768]{1,0:T(8,128)(2,1)S(1)}, bf16[208,768]{1,0:T(8,128)(2,1)S(1)}) custom-call(s32[6]{0:T(128)S(1)} %concatenate.4.place, bf16[192,2560]{1,0:T(8,128)(2,1)S(1)} %collective-permute-done.1.refs_0_, bf16[5120,1536]{1,0:T(8,128)(2,1)} %refs_1_.10, bf16[5120,1536]{1,0:T(8,128)(2,1)} %refs_2_.7, ...), custom_call_target="tpu_custom_call" | custom-call | flops 1509949440 | bytes 7864320 | tf_op jit(solution)/shard_map/pallas_call | solution.py:129
  44.1 1.5 collective-permute-start.4
  45.6 6.0 %shard_map.57 = (bf16[192,384]{1,0:T(8,128)(2,1)S(1)}, bf16[192,384]{1,0:T(8,128)(2,1)S(1)}, bf16[192,384]{1,0:T(8,128)(2,1)S(1)}, bf16[192,384]{1,0:T(8,128)(2,1)S(1)}) custom-call(s32[4]{0:T(128)S(1)} %pad_add_fusion.place, bf16[192,2560]{1,0:T(8,128)(2,1)S(1)} %collective-permute-done.1.refs_0_, bf16[5120,1536]{1,0:T(8,128)(2,1)} %refs_1_.11, ...), custom_call_target="tpu_custom_call" | custom-call | flops 1509949440 | bytes 7864320 | tf_op jit(solution)/shard_map/pallas_call | solution.py:129
  51.6 9.1 %shard_map.58 = (bf16[192,768]{1,0:T(8,128)(2,1)S(1)}, bf16[192,768]{1,0:T(8,128)(2,1)S(1)}, bf16[192,768]{1,0:T(8,128)(2,1)S(1)}, bf16[192,768]{1,0:T(8,128)(2,1)S(1)}) custom-call(s32[4]{0:T(128)S(1)} %pad_add_fusion.place, bf16[192,2560]{1,0:T(8,128)(2,1)S(1)} %collective-permute-done.3.refs_0_, bf16[5120,1536]{1,0:T(8,128)(2,1)} %refs_1_.10, ...), custom_call_target="tpu_custom_call" | custom-call | flops 3019898880 | bytes 15728640 | tf_op jit(solution)/shard_map/pallas_call | solution.py:129
  60.7 0.6 collective-permute-start.6
  61.3 4.8 %collective-permute-done.7.refs_4_.refs_12_ = bf16[208,768]{1,0:T(8,128)(2,1)S(1)} collective-permute-done((bf16[208,768]{1,0:T(8,128)(2,1)S(1)}, bf16[208,768]{1,0:T(8,128)(2,1)S(1)}, u32[]{:S(2)}, u32[]{:S(2)}) %collective-permute-start.7) | collective-permute-done | bytes 319520 | tf_op jit(solution)/shard_map/ppermute | solution.py:19
  66.1 1.5 collective-permute-start.8
  67.6 0.5 collective-permute-start.11
  68.2 3.2 %collective-permute-start.18 = (bf16[192,768]{1,0:T(8,128)(2,1)S(1)}, bf16[192,768]{1,0:T(8,128)(2,1)S(1)}, u32[]{:S(2)}, u32[]{:S(2)}) collective-permute-start(bf16[192,768]{1,0:T(8,128)(2,1)S(1)} %get-tuple-element.97), channel_id=1, source_target_pairs={{0,16},{2,18},{4,20},{6,22},{8,24},{10,26},{12,28},{14,30},{16,0},... | collective-permute-start | bytes 884744 | tf_op jit(solution)/shard_map/ppermute | solution.py:19
  71.4 2.7 %collective-permute-start.20 = (bf16[192,768]{1,0:T(8,128)(2,1)S(1)}, bf16[192,768]{1,0:T(8,128)(2,1)S(1)}, u32[]{:S(2)}, u32[]{:S(2)}) collective-permute-start(bf16[192,768]{1,0:T(8,128)(2,1)S(1)} %get-tuple-element.99), channel_id=1, source_target_pairs={{0,24},{2,26},{4,28},{6,30},{8,16},{10,18},{12,20},{14,22},{16,8},... | collective-permute-start | bytes 884744 | tf_op jit(solution)/shard_map/ppermute | solution.py:19
  74.1 2.4 %collective-permute-done.8.refs_5_.refs_14_ = bf16[208,768]{1,0:T(8,128)(2,1)S(1)} collective-permute-done((bf16[208,768]{1,0:T(8,128)(2,1)S(1)}, bf16[208,768]{1,0:T(8,128)(2,1)S(1)}, u32[]{:S(2)}, u32[]{:S(2)}) %collective-permute-start.8) | collective-permute-done | bytes 319520 | tf_op jit(solution)/shard_map/ppermute | solution.py:19
  76.5 1.5 collective-permute-start.10
  78.0 4.8 %collective-permute-done.11.refs_7_ = bf16[192,768]{1,0:T(8,128)(2,1)S(1)} collective-permute-done((bf16[192,768]{1,0:T(8,128)(2,1)S(1)}, bf16[192,768]{1,0:T(8,128)(2,1)S(1)}, u32[]{:S(2)}, u32[]{:S(2)}) %collective-permute-start.11) | collective-permute-done | bytes 294944 | tf_op jit(solution)/shard_map/ppermute | solution.py:19
  82.9 1.6 collective-permute-start.17
  84.4 7.5 %collective-permute-done.18.refs_13_ = bf16[192,768]{1,0:T(8,128)(2,1)S(1)} collective-permute-done((bf16[192,768]{1,0:T(8,128)(2,1)S(1)}, bf16[192,768]{1,0:T(8,128)(2,1)S(1)}, u32[]{:S(2)}, u32[]{:S(2)}) %collective-permute-start.18) | collective-permute-done | bytes 294944 | tf_op jit(solution)/shard_map/ppermute | solution.py:19
  91.9 1.5 collective-permute-start.19
  93.4 0.6 collective-permute-start.21
  94.0 4.4 %collective-permute-start.26 = (bf16[192,384]{1,0:T(8,128)(2,1)S(1)}, bf16[192,384]{1,0:T(8,128)(2,1)S(1)}, u32[]{:S(2)}, u32[]{:S(2)}) collective-permute-start(bf16[192,384]{1,0:T(8,128)(2,1)S(1)} %get-tuple-element.106), channel_id=1, source_target_pairs={{0,16},{2,18},{4,20},{6,22},{8,24},{10,26},{12,28},{14,30},{16,0},... | collective-permute-start | bytes 442376 | tf_op jit(solution)/shard_map/ppermute | solution.py:19
  98.5 0.9 collective-permute-done.13.refs_1_
  99.3 2.6 %collective-permute-start.27 = (bf16[192,384]{1,0:T(8,128)(2,1)S(1)}, bf16[192,384]{1,0:T(8,128)(2,1)S(1)}, u32[]{:S(2)}, u32[]{:S(2)}) collective-permute-start(bf16[192,384]{1,0:T(8,128)(2,1)S(1)} %get-tuple-element.108), channel_id=1, source_target_pairs={{0,24},{2,26},{4,28},{6,30},{8,16},{10,18},{12,20},{14,22},{16,8},... | collective-permute-start | bytes 442376 | tf_op jit(solution)/shard_map/ppermute | solution.py:19
  102.0 6.2 %shard_map.61 = (bf16[192,384]{1,0:T(8,128)(2,1)S(1)}, bf16[192,384]{1,0:T(8,128)(2,1)S(1)}, bf16[192,384]{1,0:T(8,128)(2,1)S(1)}, bf16[192,384]{1,0:T(8,128)(2,1)S(1)}) custom-call(s32[4]{0:T(128)S(1)} %pad_add_fusion.place, bf16[192,2560]{1,0:T(8,128)(2,1)S(1)} %collective-permute-done.3.refs_0_, bf16[5120,1536]{1,0:T(8,128)(2,1)} %refs_1_.11, ...), custom_call_target="tpu_custom_call" | custom-call | flops 1509949440 | bytes 7864320 | tf_op jit(solution)/shard_map/pallas_call | solution.py:129
  108.3 0.8 shard_map.60.table
  109.6 1.7 %collective-permute-start.15 = (bf16[192,384]{1,0:T(8,128)(2,1)S(1)}, bf16[192,384]{1,0:T(8,128)(2,1)S(1)}, u32[]{:S(2)}, u32[]{:S(2)}) collective-permute-start(bf16[192,384]{1,0:T(8,128)(2,1)S(1)} %get-tuple-element.91), channel_id=1, source_target_pairs={{0,16},{2,18},{4,20},{6,22},{8,24},{10,26},{12,28},{14,30},{16,0},... | collective-permute-start | bytes 442376 | tf_op jit(solution)/shard_map/ppermute | solution.py:19
  111.3 2.6 %collective-permute-start.16 = (bf16[192,384]{1,0:T(8,128)(2,1)S(1)}, bf16[192,384]{1,0:T(8,128)(2,1)S(1)}, u32[]{:S(2)}, u32[]{:S(2)}) collective-permute-start(bf16[192,384]{1,0:T(8,128)(2,1)S(1)} %get-tuple-element.93), channel_id=1, source_target_pairs={{0,24},{2,26},{4,28},{6,30},{8,16},{10,18},{12,20},{14,22},{16,8},... | collective-permute-start | bytes 442376 | tf_op jit(solution)/shard_map/ppermute | solution.py:19
  114.0 0.7 copy-done.20
  114.7 0.7 copy-done.27
  115.4 12.0 %shard_map.63 = (bf16[192,384]{1,0:T(8,128)(2,1)}, bf16[192,384]{1,0:T(8,128)(2,1)}, bf16[192,384]{1,0:T(8,128)(2,1)}, bf16[192,384]{1,0:T(8,128)(2,1)}) custom-call(s32[16]{0:T(128)} %copy-done.10, bf16[192,384]{1,0:T(8,128)(2,1)} %copy-done.12, bf16[192,384]{1,0:T(8,128)(2,1)} %copy-done.23, bf16[192,384]{1,0:T(8,128)(2,1)} %copy-done.26, ...), custom_call_target="tpu_custom_call" | custom-call | flops 2717908992 | bytes 5898240 | tf_op jit(solution)/shard_map/pallas_call | solution.py:280
  127.5 1.2 collective-permute-start.28
  128.8 0.6 copy-done.22
  129.5 0.7 copy-done.25
  130.1 12.3 %shard_map.62 = (bf16[192,384]{1,0:T(8,128)(2,1)}, bf16[192,384]{1,0:T(8,128)(2,1)}, bf16[192,384]{1,0:T(8,128)(2,1)}, bf16[192,384]{1,0:T(8,128)(2,1)}) custom-call(s32[16]{0:T(128)} %copy-done.10, bf16[192,384]{1,0:T(8,128)(2,1)} %copy-done.13, bf16[192,384]{1,0:T(8,128)(2,1)} %copy-done.22, bf16[192,384]{1,0:T(8,128)(2,1)} %copy-done.24, ...), custom_call_target="tpu_custom_call" | custom-call | flops 2717908992 | bytes 5898240 | tf_op jit(solution)/shard_map/pallas_call | solution.py:280
  142.5 4.4 %collective-permute-start.23 = (bf16[192,384]{1,0:T(8,128)(2,1)}, bf16[192,384]{1,0:T(8,128)(2,1)S(1)}, u32[]{:S(2)}, u32[]{:S(2)}) collective-permute-start(bf16[192,384]{1,0:T(8,128)(2,1)} %get-tuple-element.101), channel_id=1, source_target_pairs={{0,18},{2,16},{4,22},{6,20},{8,26},{10,24},{12,30},{14,28},{16,2},... | collective-permute-start | bytes 442376 | tf_op jit(solution)/shard_map/ppermute | solution.py:19
  146.9 2.1 %collective-permute-start.25 = (bf16[192,384]{1,0:T(8,128)(2,1)}, bf16[192,384]{1,0:T(8,128)(2,1)S(1)}, u32[]{:S(2)}, u32[]{:S(2)}) collective-permute-start(bf16[192,384]{1,0:T(8,128)(2,1)} %get-tuple-element.103), channel_id=1, source_target_pairs={{0,2},{2,0},{4,6},{6,4},{8,10},{10,8},{12,14},{14,12},{16,18},{18,... | collective-permute-start | bytes 442376 | tf_op jit(solution)/shard_map/ppermute | solution.py:19
  149.0 5.5 %collective-permute-done.30.refs_2_ = bf16[192,384]{1,0:T(8,128)(2,1)S(1)} collective-permute-done((bf16[192,384]{1,0:T(8,128)(2,1)S(1)}, bf16[192,384]{1,0:T(8,128)(2,1)S(1)}, u32[]{:S(2)}, u32[]{:S(2)}) %collective-permute-start.30) | collective-permute-done | bytes 147488 | tf_op jit(solution)/shard_map/ppermute | solution.py:19
  154.5 2.0 %shard_map.64.refs_4_ = bf16[2,192,1536]{2,1,0:T(8,128)(2,1)} custom-call(s32[4]{0:T(128)S(1)} %pad_add_fusion.place, bf16[192,384]{1,0:T(8,128)(2,1)S(1)} %collective-permute-done.28.refs_0_, bf16[192,384]{1,0:T(8,128)(2,1)S(1)} %collective-permute-done.29.refs_1_, bf16[192,384]{1,0:T(8,128)(2,1)S(1)} %collective-permute-done.30.refs_2_, ...), custom_call_target="tpu_custom_call" | custom-call | tf_op jit(solution)/shard_map/pallas_call | solution.py:348
  156.5 3.1 %collective-permute-done.23.refs_1_ = bf16[192,384]{1,0:T(8,128)(2,1)S(1)} collective-permute-done((bf16[192,384]{1,0:T(8,128)(2,1)}, bf16[192,384]{1,0:T(8,128)(2,1)S(1)}, u32[]{:S(2)}, u32[]{:S(2)}) %collective-permute-start.23) | collective-permute-done | bytes 147488 | tf_op jit(solution)/shard_map/ppermute | solution.py:19
  159.6 2.0 %shard_map.65 = bf16[2,192,1536]{2,1,0:T(8,128)(2,1)} custom-call(s32[4]{0:T(128)S(1)} %pad_add_fusion.place, bf16[192,384]{1,0:T(8,128)(2,1)S(1)} %collective-permute-done.22.refs_0_, bf16[192,384]{1,0:T(8,128)(2,1)S(1)} %collective-permute-done.23.refs_1_, bf16[192,384]{1,0:T(8,128)(2,1)S(1)} %collective-permute-done.24.refs_2_, ...), custom_call_target="tpu_custom_call", output_to_operand_aliasing={{}: (5, {})} | custom-call | tf_op jit(solution)/shard_map/pallas_call | solution.py:348
  (90 shorter events, 2.1 us)
Async XLA Ops:
  0.0 10.4 %copy-start = (bf16[2,192,2560]{2,1,0:T(8,128)(2,1)S(1)}, bf16[2,192,2560]{2,1,0:T(8,128)(2,1)}, u32[]{:S(2)}) copy-start(bf16[2,192,2560]{2,1,0:T(8,128)(2,1)} %mine_ref.1) | copy-start | bytes 5898244
  3.1 6.5 %collective-permute-start.2 = (bf16[192,2560]{1,0:T(8,128)(2,1)}, bf16[192,2560]{1,0:T(8,128)(2,1)}, u32[]{:S(2)}, u32[]{:S(2)}) collective-permute-start(bf16[192,2560]{1,0:T(8,128)(2,1)} %get-tuple-element.113), channel_id=1, source_target_pairs={{0,2},{2,0},{4,6},{6,4},{8,10},{10,8},{12,14},{14,12},{16,18},{18,... | collective-permute-start | bytes 2949128 | tf_op jit(solution)/shard_map/ppermute | solution.py:19
  3.5 25.3 %collective-permute-start.1 = (bf16[192,2560]{1,0:T(8,128)(2,1)}, bf16[192,2560]{1,0:T(8,128)(2,1)S(1)}, u32[]{:S(2)}, u32[]{:S(2)}) collective-permute-start(bf16[192,2560]{1,0:T(8,128)(2,1)} %get-tuple-element.114), channel_id=1, source_target_pairs={{0,1},{1,0},{2,3},{3,2},{4,5},{5,4},{6,7},{7,6},{8,9},{9,8},{10,11... | collective-permute-start | bytes 2949128 | tf_op jit(solution)/shard_map/ppermute | solution.py:19
  6.9 1.2 collective-permute-start
  9.5 42.1 %collective-permute-start.3 = (bf16[192,2560]{1,0:T(8,128)(2,1)}, bf16[192,2560]{1,0:T(8,128)(2,1)S(1)}, u32[]{:S(2)}, u32[]{:S(2)}) collective-permute-start(bf16[192,2560]{1,0:T(8,128)(2,1)} %collective-permute-done.2.other_ref), channel_id=1, source_target_pairs={{0,1},{1,0},{2,3},{3,2},{4,5},{5,4},{6,7},{7,6},{8,9},{9,8},{10,11... | collective-permute-start | bytes 2949128 | tf_op jit(solution)/shard_map/ppermute | solution.py:19
  34.1 26.6 %collective-permute-start.5 = (bf16[208,768]{1,0:T(8,128)(2,1)S(1)}, bf16[208,768]{1,0:T(8,128)(2,1)S(1)}, u32[]{:S(2)}, u32[]{:S(2)}) collective-permute-start(bf16[208,768]{1,0:T(8,128)(2,1)S(1)} %get-tuple-element.70), channel_id=1, source_target_pairs={{0,8},{2,10},{4,12},{6,14},{8,0},{10,2},{12,4},{14,6},{16,24},{18,... | collective-permute-start | bytes 958472 | tf_op jit(solution)/shard_map/ppermute | solution.py:19
  36.2 31.9 %collective-permute-start.9 = (bf16[208,768]{1,0:T(8,128)(2,1)S(1)}, bf16[208,768]{1,0:T(8,128)(2,1)S(1)}, u32[]{:S(2)}, u32[]{:S(2)}) collective-permute-start(bf16[208,768]{1,0:T(8,128)(2,1)S(1)} %get-tuple-element.76), channel_id=1, source_target_pairs={{0,24},{2,26},{4,28},{6,30},{8,16},{10,18},{12,20},{14,22},{16,8},... | collective-permute-start | bytes 958472 | tf_op jit(solution)/shard_map/ppermute | solution.py:19
  43.9 64.3 %copy-start.3 = (bf16[208,768]{1,0:T(8,128)(2,1)}, bf16[208,768]{1,0:T(8,128)(2,1)S(1)}, u32[]{:S(2)}) copy-start(bf16[208,768]{1,0:T(8,128)(2,1)S(1)} %get-tuple-element.69.refs_0_.refs_4_) | copy-start | bytes 958468
  43.9 22.1 %collective-permute-start.7 = (bf16[208,768]{1,0:T(8,128)(2,1)S(1)}, bf16[208,768]{1,0:T(8,128)(2,1)S(1)}, u32[]{:S(2)}, u32[]{:S(2)}) collective-permute-start(bf16[208,768]{1,0:T(8,128)(2,1)S(1)} %get-tuple-element.73), channel_id=1, source_target_pairs={{0,16},{2,18},{4,20},{6,22},{8,24},{10,26},{12,28},{14,30},{16,0},... | collective-permute-start | bytes 958472 | tf_op jit(solution)/shard_map/ppermute | solution.py:19
  44.1 24.0 %collective-permute-start.4 = (bf16[208,768]{1,0:T(8,128)(2,1)S(1)}, bf16[208,768]{1,0:T(8,128)(2,1)S(1)}, u32[]{:S(2)}, u32[]{:S(2)}) collective-permute-start(bf16[208,768]{1,0:T(8,128)(2,1)S(1)} %get-tuple-element.69.refs_0_.refs_4_), channel_id=1, source_target_pairs={{0,4},{2,6},{4,0},{6,2},{8,12},{10,14},{12,8},{14,10},{16,20},{18,... | collective-permute-start | bytes 958472 | tf_op jit(solution)/shard_map/ppermute | solution.py:19
  60.7 47.5 %copy-start.11 = (bf16[192,768]{1,0:T(8,128)(2,1)}, bf16[192,768]{1,0:T(8,128)(2,1)S(1)}, u32[]{:S(2)}) copy-start(bf16[192,768]{1,0:T(8,128)(2,1)S(1)} %get-tuple-element.95.refs_5_) | copy-start | bytes 884740
  60.7 47.5 %copy-start.1 = (bf16[208,768]{1,0:T(8,128)(2,1)}, bf16[208,768]{1,0:T(8,128)(2,1)S(1)}, u32[]{:S(2)}) copy-start(bf16[208,768]{1,0:T(8,128)(2,1)S(1)} %collective-permute-done.5.refs_2_.refs_8_) | copy-start | bytes 958468
  60.7 10.7 %collective-permute-start.6 = (bf16[208,768]{1,0:T(8,128)(2,1)S(1)}, bf16[208,768]{1,0:T(8,128)(2,1)S(1)}, u32[]{:S(2)}, u32[]{:S(2)}) collective-permute-start(bf16[208,768]{1,0:T(8,128)(2,1)S(1)} %collective-permute-done.5.refs_2_.refs_8_), channel_id=1, source_target_pairs={{0,4},{2,6},{4,0},{6,2},{8,12},{10,14},{12,8},{14,10},{16,20},{18,... | collective-permute-start | bytes 958472 | tf_op jit(solution)/shard_map/ppermute | solution.py:19
  66.1 42.2 %copy-start.4 = (bf16[208,768]{1,0:T(8,128)(2,1)}, bf16[208,768]{1,0:T(8,128)(2,1)S(1)}, u32[]{:S(2)}) copy-start(bf16[208,768]{1,0:T(8,128)(2,1)S(1)} %collective-permute-done.7.refs_4_.refs_12_) | copy-start | bytes 958468
  66.1 10.5 %collective-permute-start.8 = (bf16[208,768]{1,0:T(8,128)(2,1)S(1)}, bf16[208,768]{1,0:T(8,128)(2,1)S(1)}, u32[]{:S(2)}, u32[]{:S(2)}) collective-permute-start(bf16[208,768]{1,0:T(8,128)(2,1)S(1)} %collective-permute-done.7.refs_4_.refs_12_), channel_id=1, source_target_pairs={{0,4},{2,6},{4,0},{6,2},{8,12},{10,14},{12,8},{14,10},{16,20},{18,... | collective-permute-start | bytes 958472 | tf_op jit(solution)/shard_map/ppermute | solution.py:19
  67.6 15.3 %collective-permute-start.11 = (bf16[192,768]{1,0:T(8,128)(2,1)S(1)}, bf16[192,768]{1,0:T(8,128)(2,1)S(1)}, u32[]{:S(2)}, u32[]{:S(2)}) collective-permute-start(bf16[192,768]{1,0:T(8,128)(2,1)S(1)} %get-tuple-element.95.refs_5_), channel_id=1, source_target_pairs={{0,4},{2,6},{4,0},{6,2},{8,12},{10,14},{12,8},{14,10},{16,20},{18,... | collective-permute-start | bytes 884744 | tf_op jit(solution)/shard_map/ppermute | solution.py:19
  68.1 40.2 %copy-start.2 = (bf16[208,768]{1,0:T(8,128)(2,1)}, bf16[208,768]{1,0:T(8,128)(2,1)S(1)}, u32[]{:S(2)}) copy-start(bf16[208,768]{1,0:T(8,128)(2,1)S(1)} %collective-permute-done.9.refs_6_.refs_16_) | copy-start | bytes 958468
  68.1 40.2 %copy-start.5 = (bf16[208,768]{1,0:T(8,128)(2,1)}, bf16[208,768]{1,0:T(8,128)(2,1)S(1)}, u32[]{:S(2)}) copy-start(bf16[208,768]{1,0:T(8,128)(2,1)S(1)} %collective-permute-done.4.refs_1_.refs_6_) | copy-start | bytes 958468
  68.1 14.7 %collective-permute-start.12 = (bf16[192,768]{1,0:T(8,128)(2,1)S(1)}, bf16[192,768]{1,0:T(8,128)(2,1)S(1)}, u32[]{:S(2)}, u32[]{:S(2)}) collective-permute-start(bf16[192,768]{1,0:T(8,128)(2,1)S(1)} %get-tuple-element.84), channel_id=1, source_target_pairs={{0,8},{2,10},{4,12},{6,14},{8,0},{10,2},{12,4},{14,6},{16,24},{18,... | collective-permute-start | bytes 884744 | tf_op jit(solution)/shard_map/ppermute | solution.py:19
  68.2 23.7 %collective-permute-start.18 = (bf16[192,768]{1,0:T(8,128)(2,1)S(1)}, bf16[192,768]{1,0:T(8,128)(2,1)S(1)}, u32[]{:S(2)}, u32[]{:S(2)}) collective-permute-start(bf16[192,768]{1,0:T(8,128)(2,1)S(1)} %get-tuple-element.97), channel_id=1, source_target_pairs={{0,16},{2,18},{4,20},{6,22},{8,24},{10,26},{12,28},{14,30},{16,0},... | collective-permute-start | bytes 884744 | tf_op jit(solution)/shard_map/ppermute | solution.py:19
  71.4 36.9 %copy-start.6 = (bf16[208,768]{1,0:T(8,128)(2,1)}, bf16[208,768]{1,0:T(8,128)(2,1)S(1)}, u32[]{:S(2)}) copy-start(bf16[208,768]{1,0:T(8,128)(2,1)S(1)} %collective-permute-done.6.refs_3_.refs_10_) | copy-start | bytes 958468
  71.4 22.0 %collective-permute-start.20 = (bf16[192,768]{1,0:T(8,128)(2,1)S(1)}, bf16[192,768]{1,0:T(8,128)(2,1)S(1)}, u32[]{:S(2)}, u32[]{:S(2)}) collective-permute-start(bf16[192,768]{1,0:T(8,128)(2,1)S(1)} %get-tuple-element.99), channel_id=1, source_target_pairs={{0,24},{2,26},{4,28},{6,30},{8,16},{10,18},{12,20},{14,22},{16,8},... | collective-permute-start | bytes 884744 | tf_op jit(solution)/shard_map/ppermute | solution.py:19
  76.5 31.8 %copy-start.7 = (bf16[208,768]{1,0:T(8,128)(2,1)}, bf16[208,768]{1,0:T(8,128)(2,1)S(1)}, u32[]{:S(2)}) copy-start(bf16[208,768]{1,0:T(8,128)(2,1)S(1)} %collective-permute-done.8.refs_5_.refs_14_) | copy-start | bytes 958468
  76.5 17.5 %collective-permute-start.10 = (bf16[208,768]{1,0:T(8,128)(2,1)S(1)}, bf16[208,768]{1,0:T(8,128)(2,1)S(1)}, u32[]{:S(2)}, u32[]{:S(2)}) collective-permute-start(bf16[208,768]{1,0:T(8,128)(2,1)S(1)} %collective-permute-done.9.refs_6_.refs_16_), channel_id=1, source_target_pairs={{0,4},{2,6},{4,0},{6,2},{8,12},{10,14},{12,8},{14,10},{16,20},{18,... | collective-permute-start | bytes 958472 | tf_op jit(solution)/shard_map/ppermute | solution.py:19
  82.8 25.3 %copy-start.14 = (bf16[192,768]{1,0:T(8,128)(2,1)}, bf16[192,768]{1,0:T(8,128)(2,1)S(1)}, u32[]{:S(2)}) copy-start(bf16[192,768]{1,0:T(8,128)(2,1)S(1)} %collective-permute-done.11.refs_7_) | copy-start | bytes 884740
  82.9 25.3 %copy-start.15 = (bf16[192,768]{1,0:T(8,128)(2,1)}, bf16[192,768]{1,0:T(8,128)(2,1)S(1)}, u32[]{:S(2)}) copy-start(bf16[192,768]{1,0:T(8,128)(2,1)S(1)} %collective-permute-done.12.refs_9_) | copy-start | bytes 884740
  82.9 26.7 %collective-permute-start.17 = (bf16[192,768]{1,0:T(8,128)(2,1)S(1)}, bf16[192,768]{1,0:T(8,128)(2,1)S(1)}, u32[]{:S(2)}, u32[]{:S(2)}) collective-permute-start(bf16[192,768]{1,0:T(8,128)(2,1)S(1)} %collective-permute-done.12.refs_9_), channel_id=1, source_target_pairs={{0,4},{2,6},{4,0},{6,2},{8,12},{10,14},{12,8},{14,10},{16,20},{18,... | collective-permute-start | bytes 884744 | tf_op jit(solution)/shard_map/ppermute | solution.py:19
  91.9 16.3 %copy-start.16 = (bf16[192,768]{1,0:T(8,128)(2,1)}, bf16[192,768]{1,0:T(8,128)(2,1)S(1)}, u32[]{:S(2)}) copy-start(bf16[192,768]{1,0:T(8,128)(2,1)S(1)} %collective-permute-done.18.refs_13_) | copy-start | bytes 884740
  91.9 19.5 %collective-permute-start.19 = (bf16[192,768]{1,0:T(8,128)(2,1)S(1)}, bf16[192,768]{1,0:T(8,128)(2,1)S(1)}, u32[]{:S(2)}, u32[]{:S(2)}) collective-permute-start(bf16[192,768]{1,0:T(8,128)(2,1)S(1)} %collective-permute-done.18.refs_13_), channel_id=1, source_target_pairs={{0,4},{2,6},{4,0},{6,2},{8,12},{10,14},{12,8},{14,10},{16,20},{18,... | collective-permute-start | bytes 884744 | tf_op jit(solution)/shard_map/ppermute | solution.py:19
  93.4 5.9 %collective-permute-start.13 = (bf16[192,384]{1,0:T(8,128)(2,1)S(1)}, bf16[192,384]{1,0:T(8,128)(2,1)S(1)}, u32[]{:S(2)}, u32[]{:S(2)}) collective-permute-start(bf16[192,384]{1,0:T(8,128)(2,1)S(1)} %get-tuple-element.86), channel_id=1, source_target_pairs={{0,8},{2,10},{4,12},{6,14},{8,0},{10,2},{12,4},{14,6},{16,24},{18,... | collective-permute-start | bytes 442376 | tf_op jit(solution)/shard_map/ppermute | solution.py:19
  93.4 14.8 %copy-start.17 = (bf16[192,768]{1,0:T(8,128)(2,1)}, bf16[192,768]{1,0:T(8,128)(2,1)S(1)}, u32[]{:S(2)}) copy-start(bf16[192,768]{1,0:T(8,128)(2,1)S(1)} %collective-permute-done.20.refs_17_) | copy-start | bytes 884740
  93.4 20.6 %collective-permute-start.21 = (bf16[192,768]{1,0:T(8,128)(2,1)S(1)}, bf16[192,768]{1,0:T(8,128)(2,1)S(1)}, u32[]{:S(2)}, u32[]{:S(2)}) collective-permute-start(bf16[192,768]{1,0:T(8,128)(2,1)S(1)} %collective-permute-done.20.refs_17_), channel_id=1, source_target_pairs={{0,4},{2,6},{4,0},{6,2},{8,12},{10,14},{12,8},{14,10},{16,20},{18,... | collective-permute-start | bytes 884744 | tf_op jit(solution)/shard_map/ppermute | solution.py:19
  94.0 14.3 %copy-start.8 = (bf16[208,768]{1,0:T(8,128)(2,1)}, bf16[208,768]{1,0:T(8,128)(2,1)S(1)}, u32[]{:S(2)}) copy-start(bf16[208,768]{1,0:T(8,128)(2,1)S(1)} %collective-permute-done.10.refs_7_.refs_18_) | copy-start | bytes 958468
  94.0 15.6 %collective-permute-start.26 = (bf16[192,384]{1,0:T(8,128)(2,1)S(1)}, bf16[192,384]{1,0:T(8,128)(2,1)S(1)}, u32[]{:S(2)}, u32[]{:S(2)}) collective-permute-start(bf16[192,384]{1,0:T(8,128)(2,1)S(1)} %get-tuple-element.106), channel_id=1, source_target_pairs={{0,16},{2,18},{4,20},{6,22},{8,24},{10,26},{12,28},{14,30},{16,0},... | collective-permute-start | bytes 442376 | tf_op jit(solution)/shard_map/ppermute | solution.py:19
  99.3 14.7 %collective-permute-start.27 = (bf16[192,384]{1,0:T(8,128)(2,1)S(1)}, bf16[192,384]{1,0:T(8,128)(2,1)S(1)}, u32[]{:S(2)}, u32[]{:S(2)}) collective-permute-start(bf16[192,384]{1,0:T(8,128)(2,1)S(1)} %get-tuple-element.108), channel_id=1, source_target_pairs={{0,24},{2,26},{4,28},{6,30},{8,16},{10,18},{12,20},{14,22},{16,8},... | collective-permute-start | bytes 442376 | tf_op jit(solution)/shard_map/ppermute | solution.py:19
  108.2 19.2 %copy-start.13 = (bf16[192,384]{1,0:T(8,128)(2,1)}, bf16[192,384]{1,0:T(8,128)(2,1)S(1)}, u32[]{:S(2)}) copy-start(bf16[192,384]{1,0:T(8,128)(2,1)S(1)} %get-tuple-element.87.refs_0_) | copy-start | bytes 442372
  109.6 19.1 %collective-permute-start.14 = (bf16[192,384]{1,0:T(8,128)(2,1)S(1)}, bf16[192,384]{1,0:T(8,128)(2,1)S(1)}, u32[]{:S(2)}, u32[]{:S(2)}) collective-permute-start(bf16[192,384]{1,0:T(8,128)(2,1)S(1)} %get-tuple-element.89), channel_id=1, source_target_pairs={{0,8},{2,10},{4,12},{6,14},{8,0},{10,2},{12,4},{14,6},{16,24},{18,... | collective-permute-start | bytes 442376 | tf_op jit(solution)/shard_map/ppermute | solution.py:19
  109.6 19.1 %collective-permute-start.15 = (bf16[192,384]{1,0:T(8,128)(2,1)S(1)}, bf16[192,384]{1,0:T(8,128)(2,1)S(1)}, u32[]{:S(2)}, u32[]{:S(2)}) collective-permute-start(bf16[192,384]{1,0:T(8,128)(2,1)S(1)} %get-tuple-element.91), channel_id=1, source_target_pairs={{0,16},{2,18},{4,20},{6,22},{8,24},{10,26},{12,28},{14,30},{16,0},... | collective-permute-start | bytes 442376 | tf_op jit(solution)/shard_map/ppermute | solution.py:19
  111.3 17.4 %collective-permute-start.16 = (bf16[192,384]{1,0:T(8,128)(2,1)S(1)}, bf16[192,384]{1,0:T(8,128)(2,1)S(1)}, u32[]{:S(2)}, u32[]{:S(2)}) collective-permute-start(bf16[192,384]{1,0:T(8,128)(2,1)S(1)} %get-tuple-element.93), channel_id=1, source_target_pairs={{0,24},{2,26},{4,28},{6,30},{8,16},{10,18},{12,20},{14,22},{16,8},... | collective-permute-start | bytes 442376 | tf_op jit(solution)/shard_map/ppermute | solution.py:19
  127.5 19.4 %collective-permute-start.28 = (bf16[192,384]{1,0:T(8,128)(2,1)}, bf16[192,384]{1,0:T(8,128)(2,1)S(1)}, u32[]{:S(2)}, u32[]{:S(2)}) collective-permute-start(bf16[192,384]{1,0:T(8,128)(2,1)} %get-tuple-element.109), channel_id=1, source_target_pairs={{0,24},{2,26},{4,28},{6,30},{8,16},{10,18},{12,20},{14,22},{16,8},... | collective-permute-start | bytes 442376 | tf_op jit(solution)/shard_map/ppermute | solution.py:19
  128.7 18.1 %copy-start.21 = (bf16[192,384]{1,0:T(8,128)(2,1)S(1)}, bf16[192,384]{1,0:T(8,128)(2,1)}, u32[]{:S(2)}) copy-start(bf16[192,384]{1,0:T(8,128)(2,1)} %get-tuple-element.111) | copy-start | bytes 442372
  128.7 25.8 %copy-start.9 = (bf16[192,384]{1,0:T(8,128)(2,1)S(1)}, bf16[192,384]{1,0:T(8,128)(2,1)}, u32[]{:S(2)}) copy-start(bf16[192,384]{1,0:T(8,128)(2,1)} %get-tuple-element.112.refs_3_) | copy-start | bytes 442372
  128.7 18.2 %collective-permute-start.29 = (bf16[192,384]{1,0:T(8,128)(2,1)}, bf16[192,384]{1,0:T(8,128)(2,1)S(1)}, u32[]{:S(2)}, u32[]{:S(2)}) collective-permute-start(bf16[192,384]{1,0:T(8,128)(2,1)} %get-tuple-element.110), channel_id=1, source_target_pairs={{0,16},{2,18},{4,20},{6,22},{8,24},{10,26},{12,28},{14,30},{16,0},... | collective-permute-start | bytes 442376 | tf_op jit(solution)/shard_map/ppermute | solution.py:19
  142.4 14.1 %collective-permute-start.22 = (bf16[192,384]{1,0:T(8,128)(2,1)}, bf16[192,384]{1,0:T(8,128)(2,1)S(1)}, u32[]{:S(2)}, u32[]{:S(2)}) collective-permute-start(bf16[192,384]{1,0:T(8,128)(2,1)} %get-tuple-element.100), channel_id=1, source_target_pairs={{0,26},{2,24},{4,30},{6,28},{8,18},{10,16},{12,22},{14,20},{16,10}... | collective-permute-start | bytes 442376 | tf_op jit(solution)/shard_map/ppermute | solution.py:19
  142.5 17.1 %collective-permute-start.23 = (bf16[192,384]{1,0:T(8,128)(2,1)}, bf16[192,384]{1,0:T(8,128)(2,1)S(1)}, u32[]{:S(2)}, u32[]{:S(2)}) collective-permute-start(bf16[192,384]{1,0:T(8,128)(2,1)} %get-tuple-element.101), channel_id=1, source_target_pairs={{0,18},{2,16},{4,22},{6,20},{8,26},{10,24},{12,30},{14,28},{16,2},... | collective-permute-start | bytes 442376 | tf_op jit(solution)/shard_map/ppermute | solution.py:19
  146.8 7.7 %collective-permute-start.30 = (bf16[192,384]{1,0:T(8,128)(2,1)S(1)}, bf16[192,384]{1,0:T(8,128)(2,1)S(1)}, u32[]{:S(2)}, u32[]{:S(2)}) collective-permute-start(bf16[192,384]{1,0:T(8,128)(2,1)S(1)} %copy-done.21), channel_id=1, source_target_pairs={{0,8},{2,10},{4,12},{6,14},{8,0},{10,2},{12,4},{14,6},{16,24},{18,... | collective-permute-start | bytes 442376 | tf_op jit(solution)/shard_map/ppermute | solution.py:19
  146.8 12.7 %collective-permute-start.24 = (bf16[192,384]{1,0:T(8,128)(2,1)}, bf16[192,384]{1,0:T(8,128)(2,1)S(1)}, u32[]{:S(2)}, u32[]{:S(2)}) collective-permute-start(bf16[192,384]{1,0:T(8,128)(2,1)} %get-tuple-element.102), channel_id=1, source_target_pairs={{0,10},{2,8},{4,14},{6,12},{8,2},{10,0},{12,6},{14,4},{16,26},{18,... | collective-permute-start | bytes 442376 | tf_op jit(solution)/shard_map/ppermute | solution.py:19
  146.9 12.7 %collective-permute-start.25 = (bf16[192,384]{1,0:T(8,128)(2,1)}, bf16[192,384]{1,0:T(8,128)(2,1)S(1)}, u32[]{:S(2)}, u32[]{:S(2)}) collective-permute-start(bf16[192,384]{1,0:T(8,128)(2,1)} %get-tuple-element.103), channel_id=1, source_target_pairs={{0,2},{2,0},{4,6},{6,4},{8,10},{10,8},{12,14},{14,12},{16,18},{18,... | collective-permute-start | bytes 442376 | tf_op jit(solution)/shard_map/ppermute | solution.py:19
  (12 other events, 39.4 us)

commit v14 on v13

--- a/solution.py
+++ b/solution.py
@@ -404,8 +404,6 @@
     ahead_1 = over_ctx(made_1[0], rest // 2)
     for a in away:
         first[a], made_1[a] = lax.optimization_barrier((first[a], made_1[a]))
-    received, ahead_1 = lax.optimization_barrier((received, ahead_1))
-    asked += rest_products(received, [1], [w_q], [start_q], place, ways, away)
 
     def over_y(blocks):
         bit = rest // 2
@@ -424,6 +422,9 @@
         before.append(over_ctx(value, rest // 2))
         blocks[a * rest + rest // 2] = before[-1]
     blocks = over_y(blocks)
+    received, _ = lax.optimization_barrier((received, blocks[(min(1, ways - 1) * rest) ^ (rest // 2)]))
+    asked += rest_products(received, [1], [w_q], [start_q], place, ways, away)
+    asked = lax.optimization_barrier(asked)
     second = {}
     for a in away:
         value, _ = lax.optimization_barrier((made_1[a], (first[a], ahead)))

time: 162 us -> 166 us (1.025)
  waiting for transfers between devices: 30.6 us -> 37.8 us
  starting transfers between devices: 43.3 us -> 40.3 us
    ppermute x31, waiting for transfers between devices: 30.6 us -> 37.8 us  [exchange(): return lax.ppermute(value, axis, [(i, i ^ bit) for i in range(size)])]
    ppermute x31, starting transfers between devices: 43.3 us -> 40.3 us  [exchange(): return lax.ppermute(value, axis, [(i, i ^ bit) for i in range(size)])]
  transfers between devices with their start and end apart: 31 -> 31, of which waited for: 9 -> 10; matrix products, arithmetic and copies ran while one was open for 2% -> 1% of each run, Pallas kernels for 47% -> 46%
where the time goes in v14:
time: 166 us
  Pallas kernels  78.4 us (47%)
  starting transfers between devices  40.3 us (24%)
  waiting for transfers between devices  37.8 us (23%)
  local copies, waits for them, and re-layouts  8.44 us (5%)
    ppermute x31, starting transfers between devices, exchange(): return lax.ppermute(value, axis, [(i, i ^ bit) for i in range(size)])  40.3 us
    ppermute x31, waiting for transfers between devices, exchange(): return lax.ppermute(value, axis, [(i, i ^ bit) for i in range(size)])  37.8 us
    pallas_call x5, Pallas kernels, rest_products(): pl.pallas_call(functools.partial(rest_body, shares, len(weights), chunks,...  31.7 us
    pallas_call x2, Pallas kernels, attend(): pl.pallas_call(functools.partial(attend_body, block, ways, slots, len(arr...  24.3 us
    pallas_call x1, Pallas kernels, own_products(): pl.pallas_call(functools.partial(own_body, len(weights)), out_shape=[jax....  17.7 us
    pallas_call x2, Pallas kernels, assemble(): pl.pallas_call(functools.partial(assemble_body, ways), out_shape=jax.Shap...  3.99 us
  transfers between devices with their start and end apart: 31, of which 10 were waited for; matrix products, arithmetic and copies ran while one was open for 1% of the time, Pallas kernels for 46%

profile of v14, /device:TPU:0, one launch (start us, length us, event | category | flops | bytes accessed | tf_op | source)
XLA Modules:
  0.0 165.8 jit_solution(16682070231309279510)
XLA Ops:
  0.0 3.1 %dynamic-slice_bitcast_fusion = (bf16[192,2560]{1,0:T(8,128)(2,1)}, bf16[192,2560]{1,0:T(8,128)(2,1)}) fusion(bf16[2,192,2560]{2,1,0:T(8,128)(2,1)} %mine_ref.1, s32[]{:T(128)S(6)} %select_n.30, s32[]{:T(128)S(6)} %select_n.29), kind=kLoop, calls=%fused_computation | loop fusion | bytes 3932168 | tf_op jit(solution)/shard_map/jit(dynamic_index_in_dim)/squeeze | solution.py:385
  3.5 2.5 %collective-permute-start.1 = (bf16[192,2560]{1,0:T(8,128)(2,1)}, bf16[192,2560]{1,0:T(8,128)(2,1)S(1)}, u32[]{:S(2)}, u32[]{:S(2)}) collective-permute-start(bf16[192,2560]{1,0:T(8,128)(2,1)} %get-tuple-element.128), channel_id=1, source_target_pairs={{0,1},{1,0},{2,3},{3,2},{4,5},{5,4},{6,7},{7,6},{8,9},{9,8},{10,11... | collective-permute-start | bytes 2949128 | tf_op jit(solution)/shard_map/ppermute | solution.py:19
  6.3 0.7 fusion
  7.2 0.9 collective-permute-done
  8.1 1.4 concatenate.4.place
  9.5 0.9 collective-permute-start.3
  10.4 17.7 %shard_map.55 = (f32[2,192,1536]{2,1,0:T(8,128)S(1)}, f32[2,192,1536]{2,1,0:T(8,128)S(1)}, f32[2,192,1536]{2,1,0:T(8,128)S(1)}) custom-call(s32[4]{0:T(128)S(1)} %pad_add_fusion.place, bf16[2,192,2560]{2,1,0:T(8,128)(2,1)S(1)} %copy-done, bf16[192,2560]{1,0:T(8,128)(2,1)} %collective-permute-done.2.other_ref, bf16[5120,1536]{1,0:T(8,128)(2,1)} %refs_1_.10, ...), custom_call_target="tpu_custom_call" | custom-call | flops 9059696640 | bytes 23592960 | tf_op jit(solution)/shard_map/pallas_call | solution.py:43
  28.1 0.8 collective-permute-done.1.refs_0_
  28.8 5.2 %shard_map.59 = (bf16[208,768]{1,0:T(8,128)(2,1)S(1)}, bf16[208,768]{1,0:T(8,128)(2,1)S(1)}) custom-call(s32[6]{0:T(128)S(1)} %concatenate.4.place, bf16[192,2560]{1,0:T(8,128)(2,1)S(1)} %collective-permute-done.1.refs_0_, bf16[5120,1536]{1,0:T(8,128)(2,1)} %refs_1_.10, bf16[5120,1536]{1,0:T(8,128)(2,1)} %refs_2_.7, ...), custom_call_target="tpu_custom_call" | custom-call | flops 1509949440 | bytes 7864320 | tf_op jit(solution)/shard_map/pallas_call | solution.py:129
  34.1 2.1 %collective-permute-start.5 = (bf16[208,768]{1,0:T(8,128)(2,1)S(1)}, bf16[208,768]{1,0:T(8,128)(2,1)S(1)}, u32[]{:S(2)}, u32[]{:S(2)}) collective-permute-start(bf16[208,768]{1,0:T(8,128)(2,1)S(1)} %get-tuple-element.77), channel_id=1, source_target_pairs={{0,8},{2,10},{4,12},{6,14},{8,0},{10,2},{12,4},{14,6},{16,24},{18,... | collective-permute-start | bytes 958472 | tf_op jit(solution)/shard_map/ppermute | solution.py:19
  36.2 2.5 %collective-permute-start.9 = (bf16[208,768]{1,0:T(8,128)(2,1)S(1)}, bf16[208,768]{1,0:T(8,128)(2,1)S(1)}, u32[]{:S(2)}, u32[]{:S(2)}) collective-permute-start(bf16[208,768]{1,0:T(8,128)(2,1)S(1)} %get-tuple-element.83), channel_id=1, source_target_pairs={{0,24},{2,26},{4,28},{6,30},{8,16},{10,18},{12,20},{14,22},{16,8},... | collective-permute-start | bytes 958472 | tf_op jit(solution)/shard_map/ppermute | solution.py:19
  38.7 5.3 %shard_map.56 = (bf16[208,768]{1,0:T(8,128)(2,1)S(1)}, bf16[208,768]{1,0:T(8,128)(2,1)S(1)}) custom-call(s32[6]{0:T(128)S(1)} %concatenate.4.place, bf16[192,2560]{1,0:T(8,128)(2,1)S(1)} %collective-permute-done.1.refs_0_, bf16[5120,1536]{1,0:T(8,128)(2,1)} %refs_1_.10, bf16[5120,1536]{1,0:T(8,128)(2,1)} %refs_2_.7, ...), custom_call_target="tpu_custom_call" | custom-call | flops 1509949440 | bytes 7864320 | tf_op jit(solution)/shard_map/pallas_call | solution.py:129
  44.1 1.5 collective-permute-start.4
  45.6 6.0 %shard_map.57 = (bf16[192,384]{1,0:T(8,128)(2,1)S(1)}, bf16[192,384]{1,0:T(8,128)(2,1)S(1)}, bf16[192,384]{1,0:T(8,128)(2,1)S(1)}, bf16[192,384]{1,0:T(8,128)(2,1)S(1)}) custom-call(s32[4]{0:T(128)S(1)} %pad_add_fusion.place, bf16[192,2560]{1,0:T(8,128)(2,1)S(1)} %collective-permute-done.1.refs_0_, bf16[5120,1536]{1,0:T(8,128)(2,1)} %refs_1_.11, ...), custom_call_target="tpu_custom_call" | custom-call | flops 1509949440 | bytes 7864320 | tf_op jit(solution)/shard_map/pallas_call | solution.py:129
  51.6 9.1 %shard_map.58 = (bf16[192,768]{1,0:T(8,128)(2,1)S(1)}, bf16[192,768]{1,0:T(8,128)(2,1)S(1)}, bf16[192,768]{1,0:T(8,128)(2,1)S(1)}, bf16[192,768]{1,0:T(8,128)(2,1)S(1)}) custom-call(s32[4]{0:T(128)S(1)} %pad_add_fusion.place, bf16[192,2560]{1,0:T(8,128)(2,1)S(1)} %collective-permute-done.3.refs_0_, bf16[5120,1536]{1,0:T(8,128)(2,1)} %refs_1_.10, ...), custom_call_target="tpu_custom_call" | custom-call | flops 3019898880 | bytes 15728640 | tf_op jit(solution)/shard_map/pallas_call | solution.py:129
  60.7 0.6 collective-permute-start.6
  61.3 4.8 %collective-permute-done.7.refs_4_.refs_12_ = bf16[208,768]{1,0:T(8,128)(2,1)S(1)} collective-permute-done((bf16[208,768]{1,0:T(8,128)(2,1)S(1)}, bf16[208,768]{1,0:T(8,128)(2,1)S(1)}, u32[]{:S(2)}, u32[]{:S(2)}) %collective-permute-start.7) | collective-permute-done | bytes 319520 | tf_op jit(solution)/shard_map/ppermute | solution.py:19
  66.1 1.5 collective-permute-start.8
  67.6 3.2 %collective-permute-start.18 = (bf16[192,768]{1,0:T(8,128)(2,1)S(1)}, bf16[192,768]{1,0:T(8,128)(2,1)S(1)}, u32[]{:S(2)}, u32[]{:S(2)}) collective-permute-start(bf16[192,768]{1,0:T(8,128)(2,1)S(1)} %get-tuple-element.111), channel_id=1, source_target_pairs={{0,16},{2,18},{4,20},{6,22},{8,24},{10,26},{12,28},{14,30},{16,0},... | collective-permute-start | bytes 884744 | tf_op jit(solution)/shard_map/ppermute | solution.py:19
  71.3 2.8 %collective-permute-start.20 = (bf16[192,768]{1,0:T(8,128)(2,1)S(1)}, bf16[192,768]{1,0:T(8,128)(2,1)S(1)}, u32[]{:S(2)}, u32[]{:S(2)}) collective-permute-start(bf16[192,768]{1,0:T(8,128)(2,1)S(1)} %get-tuple-element.113), channel_id=1, source_target_pairs={{0,24},{2,26},{4,28},{6,30},{8,16},{10,18},{12,20},{14,22},{16,8},... | collective-permute-start | bytes 884744 | tf_op jit(solution)/shard_map/ppermute | solution.py:19
  74.1 2.4 %collective-permute-done.8.refs_5_.refs_14_ = bf16[208,768]{1,0:T(8,128)(2,1)S(1)} collective-permute-done((bf16[208,768]{1,0:T(8,128)(2,1)S(1)}, bf16[208,768]{1,0:T(8,128)(2,1)S(1)}, u32[]{:S(2)}, u32[]{:S(2)}) %collective-permute-start.8) | collective-permute-done | bytes 319520 | tf_op jit(solution)/shard_map/ppermute | solution.py:19
  76.5 1.5 collective-permute-start.10
  78.0 4.0 %collective-permute-done.11.refs_9_ = bf16[192,768]{1,0:T(8,128)(2,1)S(1)} collective-permute-done((bf16[192,768]{1,0:T(8,128)(2,1)S(1)}, bf16[192,768]{1,0:T(8,128)(2,1)S(1)}, u32[]{:S(2)}, u32[]{:S(2)}) %collective-permute-start.11) | collective-permute-done | bytes 294944 | tf_op jit(solution)/shard_map/ppermute | solution.py:19
  82.0 0.5 collective-permute-start.17
  82.5 8.8 %collective-permute-done.18.refs_13_ = bf16[192,768]{1,0:T(8,128)(2,1)S(1)} collective-permute-done((bf16[192,768]{1,0:T(8,128)(2,1)S(1)}, bf16[192,768]{1,0:T(8,128)(2,1)S(1)}, u32[]{:S(2)}, u32[]{:S(2)}) %collective-permute-start.18) | collective-permute-done | bytes 294944 | tf_op jit(solution)/shard_map/ppermute | solution.py:19
  91.9 6.2 %shard_map.61 = (bf16[192,384]{1,0:T(8,128)(2,1)S(1)}, bf16[192,384]{1,0:T(8,128)(2,1)S(1)}, bf16[192,384]{1,0:T(8,128)(2,1)S(1)}, bf16[192,384]{1,0:T(8,128)(2,1)S(1)}) custom-call(s32[4]{0:T(128)S(1)} %pad_add_fusion.place, bf16[192,2560]{1,0:T(8,128)(2,1)S(1)} %collective-permute-done.3.refs_0_, bf16[5120,1536]{1,0:T(8,128)(2,1)} %refs_1_.11, ...), custom_call_target="tpu_custom_call" | custom-call | flops 1509949440 | bytes 7864320 | tf_op jit(solution)/shard_map/pallas_call | solution.py:129
  98.2 1.6 collective-permute-start.21
  99.8 2.9 %collective-permute-start.26 = (bf16[192,384]{1,0:T(8,128)(2,1)S(1)}, bf16[192,384]{1,0:T(8,128)(2,1)S(1)}, u32[]{:S(2)}, u32[]{:S(2)}) collective-permute-start(bf16[192,384]{1,0:T(8,128)(2,1)S(1)} %get-tuple-element.120), channel_id=1, source_target_pairs={{0,16},{2,18},{4,20},{6,22},{8,24},{10,26},{12,28},{14,30},{16,0},... | collective-permute-start | bytes 442376 | tf_op jit(solution)/shard_map/ppermute | solution.py:19
  102.7 3.6 %collective-permute-done.13.refs_1_ = bf16[192,384]{1,0:T(8,128)(2,1)S(1)} collective-permute-done((bf16[192,384]{1,0:T(8,128)(2,1)S(1)}, bf16[192,384]{1,0:T(8,128)(2,1)S(1)}, u32[]{:S(2)}, u32[]{:S(2)}) %collective-permute-start.13) | collective-permute-done | bytes 147488 | tf_op jit(solution)/shard_map/ppermute | solution.py:19
  106.3 2.2 %collective-permute-start.27 = (bf16[192,384]{1,0:T(8,128)(2,1)S(1)}, bf16[192,384]{1,0:T(8,128)(2,1)S(1)}, u32[]{:S(2)}, u32[]{:S(2)}) collective-permute-start(bf16[192,384]{1,0:T(8,128)(2,1)S(1)} %get-tuple-element.122), channel_id=1, source_target_pairs={{0,24},{2,26},{4,28},{6,30},{8,16},{10,18},{12,20},{14,22},{16,8},... | collective-permute-start | bytes 442376 | tf_op jit(solution)/shard_map/ppermute | solution.py:19
  108.5 0.8 shard_map.60.table
  109.8 4.0 %collective-permute-done.26.refs_2_ = bf16[192,384]{1,0:T(8,128)(2,1)S(1)} collective-permute-done((bf16[192,384]{1,0:T(8,128)(2,1)S(1)}, bf16[192,384]{1,0:T(8,128)(2,1)S(1)}, u32[]{:S(2)}, u32[]{:S(2)}) %collective-permute-start.26) | collective-permute-done | bytes 147488 | tf_op jit(solution)/shard_map/ppermute | solution.py:19
  113.8 2.6 %collective-permute-start.15 = (bf16[192,384]{1,0:T(8,128)(2,1)S(1)}, bf16[192,384]{1,0:T(8,128)(2,1)S(1)}, u32[]{:S(2)}, u32[]{:S(2)}) collective-permute-start(bf16[192,384]{1,0:T(8,128)(2,1)S(1)} %get-tuple-element.105), channel_id=1, source_target_pairs={{0,16},{2,18},{4,20},{6,22},{8,24},{10,26},{12,28},{14,30},{16,0},... | collective-permute-start | bytes 442376 | tf_op jit(solution)/shard_map/ppermute | solution.py:19
  116.4 1.8 %collective-permute-start.16 = (bf16[192,384]{1,0:T(8,128)(2,1)S(1)}, bf16[192,384]{1,0:T(8,128)(2,1)S(1)}, u32[]{:S(2)}, u32[]{:S(2)}) collective-permute-start(bf16[192,384]{1,0:T(8,128)(2,1)S(1)} %get-tuple-element.107), channel_id=1, source_target_pairs={{0,24},{2,26},{4,28},{6,30},{8,16},{10,18},{12,20},{14,22},{16,8},... | collective-permute-start | bytes 442376 | tf_op jit(solution)/shard_map/ppermute | solution.py:19
  118.3 0.7 copy-done.20
  118.9 0.7 copy-done.27
  119.6 12.0 %shard_map.63 = (bf16[192,384]{1,0:T(8,128)(2,1)}, bf16[192,384]{1,0:T(8,128)(2,1)}, bf16[192,384]{1,0:T(8,128)(2,1)}, bf16[192,384]{1,0:T(8,128)(2,1)}) custom-call(s32[16]{0:T(128)} %copy-done.10, bf16[192,384]{1,0:T(8,128)(2,1)} %copy-done.12, bf16[192,384]{1,0:T(8,128)(2,1)} %copy-done.25, bf16[192,384]{1,0:T(8,128)(2,1)} %copy-done.26, ...), custom_call_target="tpu_custom_call" | custom-call | flops 2717908992 | bytes 5898240 | tf_op jit(solution)/shard_map/pallas_call | solution.py:280
  131.6 2.1 %collective-permute-start.28 = (bf16[192,384]{1,0:T(8,128)(2,1)}, bf16[192,384]{1,0:T(8,128)(2,1)S(1)}, u32[]{:S(2)}, u32[]{:S(2)}) collective-permute-start(bf16[192,384]{1,0:T(8,128)(2,1)} %get-tuple-element.123), channel_id=1, source_target_pairs={{0,24},{2,26},{4,28},{6,30},{8,16},{10,18},{12,20},{14,22},{16,8},... | collective-permute-start | bytes 442376 | tf_op jit(solution)/shard_map/ppermute | solution.py:19
  133.8 0.6 copy-done.22
  134.4 0.7 copy-done.24
  135.1 12.3 %shard_map.62 = (bf16[192,384]{1,0:T(8,128)(2,1)}, bf16[192,384]{1,0:T(8,128)(2,1)}, bf16[192,384]{1,0:T(8,128)(2,1)}, bf16[192,384]{1,0:T(8,128)(2,1)}) custom-call(s32[16]{0:T(128)} %copy-done.10, bf16[192,384]{1,0:T(8,128)(2,1)} %copy-done.13, bf16[192,384]{1,0:T(8,128)(2,1)} %copy-done.22, bf16[192,384]{1,0:T(8,128)(2,1)} %copy-done.23, ...), custom_call_target="tpu_custom_call" | custom-call | flops 2717908992 | bytes 5898240 | tf_op jit(solution)/shard_map/pallas_call | solution.py:280
  147.5 3.5 %collective-permute-start.23 = (bf16[192,384]{1,0:T(8,128)(2,1)}, bf16[192,384]{1,0:T(8,128)(2,1)S(1)}, u32[]{:S(2)}, u32[]{:S(2)}) collective-permute-start(bf16[192,384]{1,0:T(8,128)(2,1)} %get-tuple-element.115), channel_id=1, source_target_pairs={{0,18},{2,16},{4,22},{6,20},{8,26},{10,24},{12,30},{14,28},{16,2},... | collective-permute-start | bytes 442376 | tf_op jit(solution)/shard_map/ppermute | solution.py:19
  151.0 0.6 collective-permute-start.30
  151.9 1.2 collective-permute-start.25
  153.2 5.5 %collective-permute-done.30.refs_2_ = bf16[192,384]{1,0:T(8,128)(2,1)S(1)} collective-permute-done((bf16[192,384]{1,0:T(8,128)(2,1)S(1)}, bf16[192,384]{1,0:T(8,128)(2,1)S(1)}, u32[]{:S(2)}, u32[]{:S(2)}) %collective-permute-start.30) | collective-permute-done | bytes 147488 | tf_op jit(solution)/shard_map/ppermute | solution.py:19
  158.7 2.0 %shard_map.64.refs_4_ = bf16[2,192,1536]{2,1,0:T(8,128)(2,1)} custom-call(s32[4]{0:T(128)S(1)} %pad_add_fusion.place, bf16[192,384]{1,0:T(8,128)(2,1)S(1)} %collective-permute-done.28.refs_0_, bf16[192,384]{1,0:T(8,128)(2,1)S(1)} %collective-permute-done.29.refs_1_, bf16[192,384]{1,0:T(8,128)(2,1)S(1)} %collective-permute-done.30.refs_2_, ...), custom_call_target="tpu_custom_call" | custom-call | tf_op jit(solution)/shard_map/pallas_call | solution.py:348
  160.7 3.1 %collective-permute-done.23.refs_1_ = bf16[192,384]{1,0:T(8,128)(2,1)S(1)} collective-permute-done((bf16[192,384]{1,0:T(8,128)(2,1)}, bf16[192,384]{1,0:T(8,128)(2,1)S(1)}, u32[]{:S(2)}, u32[]{:S(2)}) %collective-permute-start.23) | collective-permute-done | bytes 147488 | tf_op jit(solution)/shard_map/ppermute | solution.py:19
  163.8 2.0 %shard_map.65 = bf16[2,192,1536]{2,1,0:T(8,128)(2,1)} custom-call(s32[4]{0:T(128)S(1)} %pad_add_fusion.place, bf16[192,384]{1,0:T(8,128)(2,1)S(1)} %collective-permute-done.22.refs_0_, bf16[192,384]{1,0:T(8,128)(2,1)S(1)} %collective-permute-done.23.refs_1_, bf16[192,384]{1,0:T(8,128)(2,1)S(1)} %collective-permute-done.24.refs_2_, ...), custom_call_target="tpu_custom_call", output_to_operand_aliasing={{}: (5, {})} | custom-call | tf_op jit(solution)/shard_map/pallas_call | solution.py:348
  (90 shorter events, 3.4 us)
Async XLA Ops:
  0.0 10.4 %copy-start = (bf16[2,192,2560]{2,1,0:T(8,128)(2,1)S(1)}, bf16[2,192,2560]{2,1,0:T(8,128)(2,1)}, u32[]{:S(2)}) copy-start(bf16[2,192,2560]{2,1,0:T(8,128)(2,1)} %mine_ref.1) | copy-start | bytes 5898244
  3.1 6.5 %collective-permute-start.2 = (bf16[192,2560]{1,0:T(8,128)(2,1)}, bf16[192,2560]{1,0:T(8,128)(2,1)}, u32[]{:S(2)}, u32[]{:S(2)}) collective-permute-start(bf16[192,2560]{1,0:T(8,128)(2,1)} %get-tuple-element.127), channel_id=1, source_target_pairs={{0,2},{2,0},{4,6},{6,4},{8,10},{10,8},{12,14},{14,12},{16,18},{18,... | collective-permute-start | bytes 2949128 | tf_op jit(solution)/shard_map/ppermute | solution.py:19
  3.5 25.3 %collective-permute-start.1 = (bf16[192,2560]{1,0:T(8,128)(2,1)}, bf16[192,2560]{1,0:T(8,128)(2,1)S(1)}, u32[]{:S(2)}, u32[]{:S(2)}) collective-permute-start(bf16[192,2560]{1,0:T(8,128)(2,1)} %get-tuple-element.128), channel_id=1, source_target_pairs={{0,1},{1,0},{2,3},{3,2},{4,5},{5,4},{6,7},{7,6},{8,9},{9,8},{10,11... | collective-permute-start | bytes 2949128 | tf_op jit(solution)/shard_map/ppermute | solution.py:19
  6.9 1.2 collective-permute-start
  9.5 42.1 %collective-permute-start.3 = (bf16[192,2560]{1,0:T(8,128)(2,1)}, bf16[192,2560]{1,0:T(8,128)(2,1)S(1)}, u32[]{:S(2)}, u32[]{:S(2)}) collective-permute-start(bf16[192,2560]{1,0:T(8,128)(2,1)} %collective-permute-done.2.other_ref), channel_id=1, source_target_pairs={{0,1},{1,0},{2,3},{3,2},{4,5},{5,4},{6,7},{7,6},{8,9},{9,8},{10,11... | collective-permute-start | bytes 2949128 | tf_op jit(solution)/shard_map/ppermute | solution.py:19
  34.1 26.6 %collective-permute-start.5 = (bf16[208,768]{1,0:T(8,128)(2,1)S(1)}, bf16[208,768]{1,0:T(8,128)(2,1)S(1)}, u32[]{:S(2)}, u32[]{:S(2)}) collective-permute-start(bf16[208,768]{1,0:T(8,128)(2,1)S(1)} %get-tuple-element.77), channel_id=1, source_target_pairs={{0,8},{2,10},{4,12},{6,14},{8,0},{10,2},{12,4},{14,6},{16,24},{18,... | collective-permute-start | bytes 958472 | tf_op jit(solution)/shard_map/ppermute | solution.py:19
  36.2 34.6 %collective-permute-start.9 = (bf16[208,768]{1,0:T(8,128)(2,1)S(1)}, bf16[208,768]{1,0:T(8,128)(2,1)S(1)}, u32[]{:S(2)}, u32[]{:S(2)}) collective-permute-start(bf16[208,768]{1,0:T(8,128)(2,1)S(1)} %get-tuple-element.83), channel_id=1, source_target_pairs={{0,24},{2,26},{4,28},{6,30},{8,16},{10,18},{12,20},{14,22},{16,8},... | collective-permute-start | bytes 958472 | tf_op jit(solution)/shard_map/ppermute | solution.py:19
  43.9 64.6 %copy-start.3 = (bf16[208,768]{1,0:T(8,128)(2,1)}, bf16[208,768]{1,0:T(8,128)(2,1)S(1)}, u32[]{:S(2)}) copy-start(bf16[208,768]{1,0:T(8,128)(2,1)S(1)} %get-tuple-element.76.refs_0_.refs_4_) | copy-start | bytes 958468
  43.9 22.1 %collective-permute-start.7 = (bf16[208,768]{1,0:T(8,128)(2,1)S(1)}, bf16[208,768]{1,0:T(8,128)(2,1)S(1)}, u32[]{:S(2)}, u32[]{:S(2)}) collective-permute-start(bf16[208,768]{1,0:T(8,128)(2,1)S(1)} %get-tuple-element.80), channel_id=1, source_target_pairs={{0,16},{2,18},{4,20},{6,22},{8,24},{10,26},{12,28},{14,30},{16,0},... | collective-permute-start | bytes 958472 | tf_op jit(solution)/shard_map/ppermute | solution.py:19
  44.1 23.5 %collective-permute-start.4 = (bf16[208,768]{1,0:T(8,128)(2,1)S(1)}, bf16[208,768]{1,0:T(8,128)(2,1)S(1)}, u32[]{:S(2)}, u32[]{:S(2)}) collective-permute-start(bf16[208,768]{1,0:T(8,128)(2,1)S(1)} %get-tuple-element.76.refs_0_.refs_4_), channel_id=1, source_target_pairs={{0,4},{2,6},{4,0},{6,2},{8,12},{10,14},{12,8},{14,10},{16,20},{18,... | collective-permute-start | bytes 958472 | tf_op jit(solution)/shard_map/ppermute | solution.py:19
  60.7 37.4 %copy-start.11 = (bf16[192,768]{1,0:T(8,128)(2,1)}, bf16[192,768]{1,0:T(8,128)(2,1)S(1)}, u32[]{:S(2)}) copy-start(bf16[192,768]{1,0:T(8,128)(2,1)S(1)} %get-tuple-element.109.refs_5_) | copy-start | bytes 884740
  60.7 47.7 %copy-start.1 = (bf16[208,768]{1,0:T(8,128)(2,1)}, bf16[208,768]{1,0:T(8,128)(2,1)S(1)}, u32[]{:S(2)}) copy-start(bf16[208,768]{1,0:T(8,128)(2,1)S(1)} %collective-permute-done.5.refs_2_.refs_8_) | copy-start | bytes 958468
  60.7 10.6 %collective-permute-start.6 = (bf16[208,768]{1,0:T(8,128)(2,1)S(1)}, bf16[208,768]{1,0:T(8,128)(2,1)S(1)}, u32[]{:S(2)}, u32[]{:S(2)}) collective-permute-start(bf16[208,768]{1,0:T(8,128)(2,1)S(1)} %collective-permute-done.5.refs_2_.refs_8_), channel_id=1, source_target_pairs={{0,4},{2,6},{4,0},{6,2},{8,12},{10,14},{12,8},{14,10},{16,20},{18,... | collective-permute-start | bytes 958472 | tf_op jit(solution)/shard_map/ppermute | solution.py:19
  66.1 42.4 %copy-start.4 = (bf16[208,768]{1,0:T(8,128)(2,1)}, bf16[208,768]{1,0:T(8,128)(2,1)S(1)}, u32[]{:S(2)}) copy-start(bf16[208,768]{1,0:T(8,128)(2,1)S(1)} %collective-permute-done.7.refs_4_.refs_12_) | copy-start | bytes 958468
  66.1 10.5 %collective-permute-start.8 = (bf16[208,768]{1,0:T(8,128)(2,1)S(1)}, bf16[208,768]{1,0:T(8,128)(2,1)S(1)}, u32[]{:S(2)}, u32[]{:S(2)}) collective-permute-start(bf16[208,768]{1,0:T(8,128)(2,1)S(1)} %collective-permute-done.7.refs_4_.refs_12_), channel_id=1, source_target_pairs={{0,4},{2,6},{4,0},{6,2},{8,12},{10,14},{12,8},{14,10},{16,20},{18,... | collective-permute-start | bytes 958472 | tf_op jit(solution)/shard_map/ppermute | solution.py:19
  67.6 40.9 %copy-start.5 = (bf16[208,768]{1,0:T(8,128)(2,1)}, bf16[208,768]{1,0:T(8,128)(2,1)S(1)}, u32[]{:S(2)}) copy-start(bf16[208,768]{1,0:T(8,128)(2,1)S(1)} %collective-permute-done.4.refs_1_.refs_6_) | copy-start | bytes 958468
  67.6 14.4 %collective-permute-start.11 = (bf16[192,768]{1,0:T(8,128)(2,1)S(1)}, bf16[192,768]{1,0:T(8,128)(2,1)S(1)}, u32[]{:S(2)}, u32[]{:S(2)}) collective-permute-start(bf16[192,768]{1,0:T(8,128)(2,1)S(1)} %get-tuple-element.99), channel_id=1, source_target_pairs={{0,8},{2,10},{4,12},{6,14},{8,0},{10,2},{12,4},{14,6},{16,24},{18,... | collective-permute-start | bytes 884744 | tf_op jit(solution)/shard_map/ppermute | solution.py:19
  67.6 23.8 %collective-permute-start.18 = (bf16[192,768]{1,0:T(8,128)(2,1)S(1)}, bf16[192,768]{1,0:T(8,128)(2,1)S(1)}, u32[]{:S(2)}, u32[]{:S(2)}) collective-permute-start(bf16[192,768]{1,0:T(8,128)(2,1)S(1)} %get-tuple-element.111), channel_id=1, source_target_pairs={{0,16},{2,18},{4,20},{6,22},{8,24},{10,26},{12,28},{14,30},{16,0},... | collective-permute-start | bytes 884744 | tf_op jit(solution)/shard_map/ppermute | solution.py:19
  70.8 37.7 %copy-start.2 = (bf16[208,768]{1,0:T(8,128)(2,1)}, bf16[208,768]{1,0:T(8,128)(2,1)S(1)}, u32[]{:S(2)}) copy-start(bf16[208,768]{1,0:T(8,128)(2,1)S(1)} %collective-permute-done.9.refs_6_.refs_16_) | copy-start | bytes 958468
  70.8 27.3 %collective-permute-start.12 = (bf16[192,768]{1,0:T(8,128)(2,1)S(1)}, bf16[192,768]{1,0:T(8,128)(2,1)S(1)}, u32[]{:S(2)}, u32[]{:S(2)}) collective-permute-start(bf16[192,768]{1,0:T(8,128)(2,1)S(1)} %get-tuple-element.109.refs_5_), channel_id=1, source_target_pairs={{0,4},{2,6},{4,0},{6,2},{8,12},{10,14},{12,8},{14,10},{16,20},{18,... | collective-permute-start | bytes 884744 | tf_op jit(solution)/shard_map/ppermute | solution.py:19
  71.3 37.2 %copy-start.6 = (bf16[208,768]{1,0:T(8,128)(2,1)}, bf16[208,768]{1,0:T(8,128)(2,1)S(1)}, u32[]{:S(2)}) copy-start(bf16[208,768]{1,0:T(8,128)(2,1)S(1)} %collective-permute-done.6.refs_3_.refs_10_) | copy-start | bytes 958468
  71.3 26.9 %collective-permute-start.20 = (bf16[192,768]{1,0:T(8,128)(2,1)S(1)}, bf16[192,768]{1,0:T(8,128)(2,1)S(1)}, u32[]{:S(2)}, u32[]{:S(2)}) collective-permute-start(bf16[192,768]{1,0:T(8,128)(2,1)S(1)} %get-tuple-element.113), channel_id=1, source_target_pairs={{0,24},{2,26},{4,28},{6,30},{8,16},{10,18},{12,20},{14,22},{16,8},... | collective-permute-start | bytes 884744 | tf_op jit(solution)/shard_map/ppermute | solution.py:19
  76.5 32.0 %copy-start.7 = (bf16[208,768]{1,0:T(8,128)(2,1)}, bf16[208,768]{1,0:T(8,128)(2,1)S(1)}, u32[]{:S(2)}) copy-start(bf16[208,768]{1,0:T(8,128)(2,1)S(1)} %collective-permute-done.8.refs_5_.refs_14_) | copy-start | bytes 958468
  76.5 23.3 %collective-permute-start.10 = (bf16[208,768]{1,0:T(8,128)(2,1)S(1)}, bf16[208,768]{1,0:T(8,128)(2,1)S(1)}, u32[]{:S(2)}, u32[]{:S(2)}) collective-permute-start(bf16[208,768]{1,0:T(8,128)(2,1)S(1)} %collective-permute-done.9.refs_6_.refs_16_), channel_id=1, source_target_pairs={{0,4},{2,6},{4,0},{6,2},{8,12},{10,14},{12,8},{14,10},{16,20},{18,... | collective-permute-start | bytes 958472 | tf_op jit(solution)/shard_map/ppermute | solution.py:19
  82.0 16.1 %copy-start.14 = (bf16[192,768]{1,0:T(8,128)(2,1)}, bf16[192,768]{1,0:T(8,128)(2,1)S(1)}, u32[]{:S(2)}) copy-start(bf16[192,768]{1,0:T(8,128)(2,1)S(1)} %collective-permute-done.11.refs_9_) | copy-start | bytes 884740
  82.0 31.8 %collective-permute-start.17 = (bf16[192,768]{1,0:T(8,128)(2,1)S(1)}, bf16[192,768]{1,0:T(8,128)(2,1)S(1)}, u32[]{:S(2)}, u32[]{:S(2)}) collective-permute-start(bf16[192,768]{1,0:T(8,128)(2,1)S(1)} %collective-permute-done.11.refs_9_), channel_id=1, source_target_pairs={{0,4},{2,6},{4,0},{6,2},{8,12},{10,14},{12,8},{14,10},{16,20},{18,... | collective-permute-start | bytes 884744 | tf_op jit(solution)/shard_map/ppermute | solution.py:19
  91.4 25.0 %collective-permute-start.19 = (bf16[192,768]{1,0:T(8,128)(2,1)S(1)}, bf16[192,768]{1,0:T(8,128)(2,1)S(1)}, u32[]{:S(2)}, u32[]{:S(2)}) collective-permute-start(bf16[192,768]{1,0:T(8,128)(2,1)S(1)} %collective-permute-done.18.refs_13_), channel_id=1, source_target_pairs={{0,4},{2,6},{4,0},{6,2},{8,12},{10,14},{12,8},{14,10},{16,20},{18,... | collective-permute-start | bytes 884744 | tf_op jit(solution)/shard_map/ppermute | solution.py:19
  98.1 33.5 %copy-start.13 = (bf16[192,384]{1,0:T(8,128)(2,1)}, bf16[192,384]{1,0:T(8,128)(2,1)S(1)}, u32[]{:S(2)}) copy-start(bf16[192,384]{1,0:T(8,128)(2,1)S(1)} %get-tuple-element.101.refs_0_) | copy-start | bytes 442372
  98.1 20.1 %copy-start.16 = (bf16[192,768]{1,0:T(8,128)(2,1)}, bf16[192,768]{1,0:T(8,128)(2,1)S(1)}, u32[]{:S(2)}) copy-start(bf16[192,768]{1,0:T(8,128)(2,1)S(1)} %collective-permute-done.12.refs_7_) | copy-start | bytes 884740
  98.1 8.2 %collective-permute-start.13 = (bf16[192,384]{1,0:T(8,128)(2,1)S(1)}, bf16[192,384]{1,0:T(8,128)(2,1)S(1)}, u32[]{:S(2)}, u32[]{:S(2)}) collective-permute-start(bf16[192,384]{1,0:T(8,128)(2,1)S(1)} %get-tuple-element.100), channel_id=1, source_target_pairs={{0,8},{2,10},{4,12},{6,14},{8,0},{10,2},{12,4},{14,6},{16,24},{18,... | collective-permute-start | bytes 442376 | tf_op jit(solution)/shard_map/ppermute | solution.py:19
  98.2 20.0 %copy-start.17 = (bf16[192,768]{1,0:T(8,128)(2,1)}, bf16[192,768]{1,0:T(8,128)(2,1)S(1)}, u32[]{:S(2)}) copy-start(bf16[192,768]{1,0:T(8,128)(2,1)S(1)} %collective-permute-done.20.refs_17_) | copy-start | bytes 884740
  98.2 20.0 %collective-permute-start.21 = (bf16[192,768]{1,0:T(8,128)(2,1)S(1)}, bf16[192,768]{1,0:T(8,128)(2,1)S(1)}, u32[]{:S(2)}, u32[]{:S(2)}) collective-permute-start(bf16[192,768]{1,0:T(8,128)(2,1)S(1)} %collective-permute-done.20.refs_17_), channel_id=1, source_target_pairs={{0,4},{2,6},{4,0},{6,2},{8,12},{10,14},{12,8},{14,10},{16,20},{18,... | collective-permute-start | bytes 884744 | tf_op jit(solution)/shard_map/ppermute | solution.py:19
  99.8 18.4 %copy-start.8 = (bf16[208,768]{1,0:T(8,128)(2,1)}, bf16[208,768]{1,0:T(8,128)(2,1)S(1)}, u32[]{:S(2)}) copy-start(bf16[208,768]{1,0:T(8,128)(2,1)S(1)} %collective-permute-done.10.refs_7_.refs_18_) | copy-start | bytes 958468
  99.8 14.0 %collective-permute-start.26 = (bf16[192,384]{1,0:T(8,128)(2,1)S(1)}, bf16[192,384]{1,0:T(8,128)(2,1)S(1)}, u32[]{:S(2)}, u32[]{:S(2)}) collective-permute-start(bf16[192,384]{1,0:T(8,128)(2,1)S(1)} %get-tuple-element.120), channel_id=1, source_target_pairs={{0,16},{2,18},{4,20},{6,22},{8,24},{10,26},{12,28},{14,30},{16,0},... | collective-permute-start | bytes 442376 | tf_op jit(solution)/shard_map/ppermute | solution.py:19
  106.3 11.9 %copy-start.25 = (bf16[192,384]{1,0:T(8,128)(2,1)}, bf16[192,384]{1,0:T(8,128)(2,1)S(1)}, u32[]{:S(2)}) copy-start(bf16[192,384]{1,0:T(8,128)(2,1)S(1)} %collective-permute-done.13.refs_1_) | copy-start | bytes 442372
  106.3 11.9 %collective-permute-start.27 = (bf16[192,384]{1,0:T(8,128)(2,1)S(1)}, bf16[192,384]{1,0:T(8,128)(2,1)S(1)}, u32[]{:S(2)}, u32[]{:S(2)}) collective-permute-start(bf16[192,384]{1,0:T(8,128)(2,1)S(1)} %get-tuple-element.122), channel_id=1, source_target_pairs={{0,24},{2,26},{4,28},{6,30},{8,16},{10,18},{12,20},{14,22},{16,8},... | collective-permute-start | bytes 442376 | tf_op jit(solution)/shard_map/ppermute | solution.py:19
  113.8 19.9 %collective-permute-start.14 = (bf16[192,384]{1,0:T(8,128)(2,1)S(1)}, bf16[192,384]{1,0:T(8,128)(2,1)S(1)}, u32[]{:S(2)}, u32[]{:S(2)}) collective-permute-start(bf16[192,384]{1,0:T(8,128)(2,1)S(1)} %get-tuple-element.103), channel_id=1, source_target_pairs={{0,8},{2,10},{4,12},{6,14},{8,0},{10,2},{12,4},{14,6},{16,24},{18,... | collective-permute-start | bytes 442376 | tf_op jit(solution)/shard_map/ppermute | solution.py:19
  113.8 19.9 %collective-permute-start.15 = (bf16[192,384]{1,0:T(8,128)(2,1)S(1)}, bf16[192,384]{1,0:T(8,128)(2,1)S(1)}, u32[]{:S(2)}, u32[]{:S(2)}) collective-permute-start(bf16[192,384]{1,0:T(8,128)(2,1)S(1)} %get-tuple-element.105), channel_id=1, source_target_pairs={{0,16},{2,18},{4,20},{6,22},{8,24},{10,26},{12,28},{14,30},{16,0},... | collective-permute-start | bytes 442376 | tf_op jit(solution)/shard_map/ppermute | solution.py:19
  116.4 17.4 %collective-permute-start.16 = (bf16[192,384]{1,0:T(8,128)(2,1)S(1)}, bf16[192,384]{1,0:T(8,128)(2,1)S(1)}, u32[]{:S(2)}, u32[]{:S(2)}) collective-permute-start(bf16[192,384]{1,0:T(8,128)(2,1)S(1)} %get-tuple-element.107), channel_id=1, source_target_pairs={{0,24},{2,26},{4,28},{6,30},{8,16},{10,18},{12,20},{14,22},{16,8},... | collective-permute-start | bytes 442376 | tf_op jit(solution)/shard_map/ppermute | solution.py:19
  131.6 19.9 %collective-permute-start.28 = (bf16[192,384]{1,0:T(8,128)(2,1)}, bf16[192,384]{1,0:T(8,128)(2,1)S(1)}, u32[]{:S(2)}, u32[]{:S(2)}) collective-permute-start(bf16[192,384]{1,0:T(8,128)(2,1)} %get-tuple-element.123), channel_id=1, source_target_pairs={{0,24},{2,26},{4,28},{6,30},{8,16},{10,18},{12,20},{14,22},{16,8},... | collective-permute-start | bytes 442376 | tf_op jit(solution)/shard_map/ppermute | solution.py:19
  133.7 17.3 %copy-start.21 = (bf16[192,384]{1,0:T(8,128)(2,1)S(1)}, bf16[192,384]{1,0:T(8,128)(2,1)}, u32[]{:S(2)}) copy-start(bf16[192,384]{1,0:T(8,128)(2,1)} %get-tuple-element.125) | copy-start | bytes 442372
  133.7 25.0 %copy-start.9 = (bf16[192,384]{1,0:T(8,128)(2,1)S(1)}, bf16[192,384]{1,0:T(8,128)(2,1)}, u32[]{:S(2)}) copy-start(bf16[192,384]{1,0:T(8,128)(2,1)} %get-tuple-element.126.refs_3_) | copy-start | bytes 442372
  133.7 18.2 %collective-permute-start.29 = (bf16[192,384]{1,0:T(8,128)(2,1)}, bf16[192,384]{1,0:T(8,128)(2,1)S(1)}, u32[]{:S(2)}, u32[]{:S(2)}) collective-permute-start(bf16[192,384]{1,0:T(8,128)(2,1)} %get-tuple-element.124), channel_id=1, source_target_pairs={{0,16},{2,18},{4,20},{6,22},{8,24},{10,26},{12,28},{14,30},{16,0},... | collective-permute-start | bytes 442376 | tf_op jit(solution)/shard_map/ppermute | solution.py:19
  147.4 13.3 %collective-permute-start.22 = (bf16[192,384]{1,0:T(8,128)(2,1)}, bf16[192,384]{1,0:T(8,128)(2,1)S(1)}, u32[]{:S(2)}, u32[]{:S(2)}) collective-permute-start(bf16[192,384]{1,0:T(8,128)(2,1)} %get-tuple-element.114), channel_id=1, source_target_pairs={{0,26},{2,24},{4,30},{6,28},{8,18},{10,16},{12,22},{14,20},{16,10}... | collective-permute-start | bytes 442376 | tf_op jit(solution)/shard_map/ppermute | solution.py:19
  147.5 16.3 %collective-permute-start.23 = (bf16[192,384]{1,0:T(8,128)(2,1)}, bf16[192,384]{1,0:T(8,128)(2,1)S(1)}, u32[]{:S(2)}, u32[]{:S(2)}) collective-permute-start(bf16[192,384]{1,0:T(8,128)(2,1)} %get-tuple-element.115), channel_id=1, source_target_pairs={{0,18},{2,16},{4,22},{6,20},{8,26},{10,24},{12,30},{14,28},{16,2},... | collective-permute-start | bytes 442376 | tf_op jit(solution)/shard_map/ppermute | solution.py:19
  151.0 7.7 %collective-permute-start.30 = (bf16[192,384]{1,0:T(8,128)(2,1)S(1)}, bf16[192,384]{1,0:T(8,128)(2,1)S(1)}, u32[]{:S(2)}, u32[]{:S(2)}) collective-permute-start(bf16[192,384]{1,0:T(8,128)(2,1)S(1)} %copy-done.21), channel_id=1, source_target_pairs={{0,8},{2,10},{4,12},{6,14},{8,0},{10,2},{12,4},{14,6},{16,24},{18,... | collective-permute-start | bytes 442376 | tf_op jit(solution)/shard_map/ppermute | solution.py:19
  151.6 12.2 %collective-permute-start.24 = (bf16[192,384]{1,0:T(8,128)(2,1)}, bf16[192,384]{1,0:T(8,128)(2,1)S(1)}, u32[]{:S(2)}, u32[]{:S(2)}) collective-permute-start(bf16[192,384]{1,0:T(8,128)(2,1)} %get-tuple-element.116), channel_id=1, source_target_pairs={{0,10},{2,8},{4,14},{6,12},{8,2},{10,0},{12,6},{14,4},{16,26},{18,... | collective-permute-start | bytes 442376 | tf_op jit(solution)/shard_map/ppermute | solution.py:19
  151.9 11.8 %collective-permute-start.25 = (bf16[192,384]{1,0:T(8,128)(2,1)}, bf16[192,384]{1,0:T(8,128)(2,1)S(1)}, u32[]{:S(2)}, u32[]{:S(2)}) collective-permute-start(bf16[192,384]{1,0:T(8,128)(2,1)} %get-tuple-element.117), channel_id=1, source_target_pairs={{0,2},{2,0},{4,6},{6,4},{8,10},{10,8},{12,14},{14,12},{16,18},{18,... | collective-permute-start | bytes 442376 | tf_op jit(solution)/shard_map/ppermute | solution.py:19
  (12 other events, 36.6 us)

commit v15 on v13

--- a/solution.py
+++ b/solution.py
@@ -404,8 +404,6 @@
     ahead_1 = over_ctx(made_1[0], rest // 2)
     for a in away:
         first[a], made_1[a] = lax.optimization_barrier((first[a], made_1[a]))
-    received, ahead_1 = lax.optimization_barrier((received, ahead_1))
-    asked += rest_products(received, [1], [w_q], [start_q], place, ways, away)
 
     def over_y(blocks):
         bit = rest // 2
@@ -419,10 +417,14 @@
     blocks = {a * rest: first[a] for a in away}
     blocks[rest // 2] = ahead
     before = []
-    for a in range(1, ways):
-        value = lax.optimization_barrier((first[a], before))[0] if a == ways - 1 else first[a]
-        before.append(over_ctx(value, rest // 2))
+    for a in range(1, ways - 1):
+        before.append(over_ctx(first[a], rest // 2))
         blocks[a * rest + rest // 2] = before[-1]
+    received, _ = lax.optimization_barrier((received, before[:1]))
+    asked += rest_products(received, [1], [w_q], [start_q], place, ways, away)
+    if ways > 1:
+        value, _ = lax.optimization_barrier((first[ways - 1], (before, asked[1])))
+        blocks[(ways - 1) * rest + rest // 2] = over_ctx(value, rest // 2)
     blocks = over_y(blocks)
     second = {}
     for a in away:

time: 162 us -> 164 us (1.012)
  waiting for transfers between devices: 30.6 us -> 33.3 us
    ppermute x31, waiting for transfers between devices: 30.6 us -> 33.3 us  [exchange(): return lax.ppermute(value, axis, [(i, i ^ bit) for i in range(size)])]
  transfers between devices with their start and end apart: 31 -> 31, of which waited for: 9 -> 10; matrix products, arithmetic and copies ran while one was open for 2% -> 1% of each run, Pallas kernels for 47% -> 47%
where the time goes in v15:
time: 164 us; the launch traced here: 163 us
  Pallas kernels  78.4 us (48%)
  starting transfers between devices  42.5 us (26%)
  waiting for transfers between devices  33.3 us (20%)
  local copies, waits for them, and re-layouts  8.41 us (5%)
    ppermute x31, starting transfers between devices, exchange(): return lax.ppermute(value, axis, [(i, i ^ bit) for i in range(size)])  42.5 us
    ppermute x31, waiting for transfers between devices, exchange(): return lax.ppermute(value, axis, [(i, i ^ bit) for i in range(size)])  33.3 us
    pallas_call x5, Pallas kernels, rest_products(): pl.pallas_call(functools.partial(rest_body, shares, len(weights), chunks,...  31.7 us
    pallas_call x2, Pallas kernels, attend(): pl.pallas_call(functools.partial(attend_body, block, ways, slots, len(arr...  24.3 us
    pallas_call x1, Pallas kernels, own_products(): pl.pallas_call(functools.partial(own_body, len(weights)), out_shape=[jax....  17.7 us
    pallas_call x2, Pallas kernels, assemble(): pl.pallas_call(functools.partial(assemble_body, ways), out_shape=jax.Shap...  3.98 us
  transfers between devices with their start and end apart: 31, of which 10 were waited for; matrix products, arithmetic and copies ran while one was open for 1% of the time, Pallas kernels for 47%

profile of v15, /device:TPU:0, one launch (start us, length us, event | category | flops | bytes accessed | tf_op | source)
XLA Modules:
  0.0 163.4 jit_solution(12881569979085179997)
XLA Ops:
  0.0 3.1 %dynamic-slice_bitcast_fusion = (bf16[192,2560]{1,0:T(8,128)(2,1)}, bf16[192,2560]{1,0:T(8,128)(2,1)}) fusion(bf16[2,192,2560]{2,1,0:T(8,128)(2,1)} %mine_ref.1, s32[]{:T(128)S(6)} %select_n.30, s32[]{:T(128)S(6)} %select_n.29), kind=kLoop, calls=%fused_computation | loop fusion | bytes 3932168 | tf_op jit(solution)/shard_map/jit(dynamic_index_in_dim)/squeeze | solution.py:385
  3.5 2.5 %collective-permute-start.1 = (bf16[192,2560]{1,0:T(8,128)(2,1)}, bf16[192,2560]{1,0:T(8,128)(2,1)S(1)}, u32[]{:S(2)}, u32[]{:S(2)}) collective-permute-start(bf16[192,2560]{1,0:T(8,128)(2,1)} %get-tuple-element.112), channel_id=1, source_target_pairs={{0,1},{1,0},{2,3},{3,2},{4,5},{5,4},{6,7},{7,6},{8,9},{9,8},{10,11... | collective-permute-start | bytes 2949128 | tf_op jit(solution)/shard_map/ppermute | solution.py:19
  6.3 0.7 fusion
  7.2 0.9 collective-permute-done
  8.1 1.4 concatenate.4.place
  9.5 0.9 collective-permute-start.3
  10.4 17.7 %shard_map.55 = (f32[2,192,1536]{2,1,0:T(8,128)S(1)}, f32[2,192,1536]{2,1,0:T(8,128)S(1)}, f32[2,192,1536]{2,1,0:T(8,128)S(1)}) custom-call(s32[4]{0:T(128)S(1)} %pad_add_fusion.place, bf16[2,192,2560]{2,1,0:T(8,128)(2,1)S(1)} %copy-done, bf16[192,2560]{1,0:T(8,128)(2,1)} %collective-permute-done.2.other_ref, bf16[5120,1536]{1,0:T(8,128)(2,1)} %refs_1_.10, ...), custom_call_target="tpu_custom_call" | custom-call | flops 9059696640 | bytes 23592960 | tf_op jit(solution)/shard_map/pallas_call | solution.py:43
  28.1 0.8 collective-permute-done.1.refs_0_
  28.8 5.2 %shard_map.59 = (bf16[208,768]{1,0:T(8,128)(2,1)S(1)}, bf16[208,768]{1,0:T(8,128)(2,1)S(1)}) custom-call(s32[6]{0:T(128)S(1)} %concatenate.4.place, bf16[192,2560]{1,0:T(8,128)(2,1)S(1)} %collective-permute-done.1.refs_0_, bf16[5120,1536]{1,0:T(8,128)(2,1)} %refs_1_.10, bf16[5120,1536]{1,0:T(8,128)(2,1)} %refs_2_.7, ...), custom_call_target="tpu_custom_call" | custom-call | flops 1509949440 | bytes 7864320 | tf_op jit(solution)/shard_map/pallas_call | solution.py:129
  34.1 2.1 %collective-permute-start.5 = (bf16[208,768]{1,0:T(8,128)(2,1)S(1)}, bf16[208,768]{1,0:T(8,128)(2,1)S(1)}, u32[]{:S(2)}, u32[]{:S(2)}) collective-permute-start(bf16[208,768]{1,0:T(8,128)(2,1)S(1)} %get-tuple-element.69), channel_id=1, source_target_pairs={{0,8},{2,10},{4,12},{6,14},{8,0},{10,2},{12,4},{14,6},{16,24},{18,... | collective-permute-start | bytes 958472 | tf_op jit(solution)/shard_map/ppermute | solution.py:19
  36.2 2.5 %collective-permute-start.9 = (bf16[208,768]{1,0:T(8,128)(2,1)S(1)}, bf16[208,768]{1,0:T(8,128)(2,1)S(1)}, u32[]{:S(2)}, u32[]{:S(2)}) collective-permute-start(bf16[208,768]{1,0:T(8,128)(2,1)S(1)} %get-tuple-element.75), channel_id=1, source_target_pairs={{0,24},{2,26},{4,28},{6,30},{8,16},{10,18},{12,20},{14,22},{16,8},... | collective-permute-start | bytes 958472 | tf_op jit(solution)/shard_map/ppermute | solution.py:19
  38.7 5.3 %shard_map.56 = (bf16[208,768]{1,0:T(8,128)(2,1)S(1)}, bf16[208,768]{1,0:T(8,128)(2,1)S(1)}) custom-call(s32[6]{0:T(128)S(1)} %concatenate.4.place, bf16[192,2560]{1,0:T(8,128)(2,1)S(1)} %collective-permute-done.1.refs_0_, bf16[5120,1536]{1,0:T(8,128)(2,1)} %refs_1_.10, bf16[5120,1536]{1,0:T(8,128)(2,1)} %refs_2_.7, ...), custom_call_target="tpu_custom_call" | custom-call | flops 1509949440 | bytes 7864320 | tf_op jit(solution)/shard_map/pallas_call | solution.py:129
  44.1 1.5 collective-permute-start.4
  45.6 6.0 %shard_map.57 = (bf16[192,384]{1,0:T(8,128)(2,1)S(1)}, bf16[192,384]{1,0:T(8,128)(2,1)S(1)}, bf16[192,384]{1,0:T(8,128)(2,1)S(1)}, bf16[192,384]{1,0:T(8,128)(2,1)S(1)}) custom-call(s32[4]{0:T(128)S(1)} %pad_add_fusion.place, bf16[192,2560]{1,0:T(8,128)(2,1)S(1)} %collective-permute-done.1.refs_0_, bf16[5120,1536]{1,0:T(8,128)(2,1)} %refs_1_.11, ...), custom_call_target="tpu_custom_call" | custom-call | flops 1509949440 | bytes 7864320 | tf_op jit(solution)/shard_map/pallas_call | solution.py:129
  51.6 9.1 %shard_map.58 = (bf16[192,768]{1,0:T(8,128)(2,1)S(1)}, bf16[192,768]{1,0:T(8,128)(2,1)S(1)}, bf16[192,768]{1,0:T(8,128)(2,1)S(1)}, bf16[192,768]{1,0:T(8,128)(2,1)S(1)}) custom-call(s32[4]{0:T(128)S(1)} %pad_add_fusion.place, bf16[192,2560]{1,0:T(8,128)(2,1)S(1)} %collective-permute-done.3.refs_0_, bf16[5120,1536]{1,0:T(8,128)(2,1)} %refs_1_.10, ...), custom_call_target="tpu_custom_call" | custom-call | flops 3019898880 | bytes 15728640 | tf_op jit(solution)/shard_map/pallas_call | solution.py:129
  60.7 0.6 collective-permute-start.6
  61.3 4.8 %collective-permute-done.7.refs_4_.refs_12_ = bf16[208,768]{1,0:T(8,128)(2,1)S(1)} collective-permute-done((bf16[208,768]{1,0:T(8,128)(2,1)S(1)}, bf16[208,768]{1,0:T(8,128)(2,1)S(1)}, u32[]{:S(2)}, u32[]{:S(2)}) %collective-permute-start.7) | collective-permute-done | bytes 319520 | tf_op jit(solution)/shard_map/ppermute | solution.py:19
  66.1 1.5 collective-permute-start.8
  68.2 3.2 %collective-permute-start.18 = (bf16[192,768]{1,0:T(8,128)(2,1)S(1)}, bf16[192,768]{1,0:T(8,128)(2,1)S(1)}, u32[]{:S(2)}, u32[]{:S(2)}) collective-permute-start(bf16[192,768]{1,0:T(8,128)(2,1)S(1)} %get-tuple-element.95), channel_id=1, source_target_pairs={{0,16},{2,18},{4,20},{6,22},{8,24},{10,26},{12,28},{14,30},{16,0},... | collective-permute-start | bytes 884744 | tf_op jit(solution)/shard_map/ppermute | solution.py:19
  71.4 2.7 %collective-permute-start.20 = (bf16[192,768]{1,0:T(8,128)(2,1)S(1)}, bf16[192,768]{1,0:T(8,128)(2,1)S(1)}, u32[]{:S(2)}, u32[]{:S(2)}) collective-permute-start(bf16[192,768]{1,0:T(8,128)(2,1)S(1)} %get-tuple-element.97), channel_id=1, source_target_pairs={{0,24},{2,26},{4,28},{6,30},{8,16},{10,18},{12,20},{14,22},{16,8},... | collective-permute-start | bytes 884744 | tf_op jit(solution)/shard_map/ppermute | solution.py:19
  74.1 6.2 %shard_map.60 = (bf16[192,384]{1,0:T(8,128)(2,1)S(1)}, bf16[192,384]{1,0:T(8,128)(2,1)S(1)}, bf16[192,384]{1,0:T(8,128)(2,1)S(1)}, bf16[192,384]{1,0:T(8,128)(2,1)S(1)}) custom-call(s32[4]{0:T(128)S(1)} %pad_add_fusion.place, bf16[192,2560]{1,0:T(8,128)(2,1)S(1)} %collective-permute-done.3.refs_0_, bf16[5120,1536]{1,0:T(8,128)(2,1)} %refs_1_.11, ...), custom_call_target="tpu_custom_call" | custom-call | flops 1509949440 | bytes 7864320 | tf_op jit(solution)/shard_map/pallas_call | solution.py:129
  80.3 0.7 collective-permute-start.10
  81.0 1.8 %collective-permute-done.12.refs_7_ = bf16[192,768]{1,0:T(8,128)(2,1)S(1)} collective-permute-done((bf16[192,768]{1,0:T(8,128)(2,1)S(1)}, bf16[192,768]{1,0:T(8,128)(2,1)S(1)}, u32[]{:S(2)}, u32[]{:S(2)}) %collective-permute-start.12) | collective-permute-done | bytes 294944 | tf_op jit(solution)/shard_map/ppermute | solution.py:19
  82.9 1.6 collective-permute-start.17
  84.4 7.5 %collective-permute-done.18.refs_13_ = bf16[192,768]{1,0:T(8,128)(2,1)S(1)} collective-permute-done((bf16[192,768]{1,0:T(8,128)(2,1)S(1)}, bf16[192,768]{1,0:T(8,128)(2,1)S(1)}, u32[]{:S(2)}, u32[]{:S(2)}) %collective-permute-start.18) | collective-permute-done | bytes 294944 | tf_op jit(solution)/shard_map/ppermute | solution.py:19
  91.9 1.5 collective-permute-start.19
  93.4 0.6 collective-permute-start.21
  94.0 4.4 %collective-permute-start.26 = (bf16[192,384]{1,0:T(8,128)(2,1)S(1)}, bf16[192,384]{1,0:T(8,128)(2,1)S(1)}, u32[]{:S(2)}, u32[]{:S(2)}) collective-permute-start(bf16[192,384]{1,0:T(8,128)(2,1)S(1)} %get-tuple-element.104), channel_id=1, source_target_pairs={{0,16},{2,18},{4,20},{6,22},{8,24},{10,26},{12,28},{14,30},{16,0},... | collective-permute-start | bytes 442376 | tf_op jit(solution)/shard_map/ppermute | solution.py:19
  98.5 0.9 collective-permute-done.13.refs_1_
  99.3 2.6 %collective-permute-start.27 = (bf16[192,384]{1,0:T(8,128)(2,1)S(1)}, bf16[192,384]{1,0:T(8,128)(2,1)S(1)}, u32[]{:S(2)}, u32[]{:S(2)}) collective-permute-start(bf16[192,384]{1,0:T(8,128)(2,1)S(1)} %get-tuple-element.106), channel_id=1, source_target_pairs={{0,24},{2,26},{4,28},{6,30},{8,16},{10,18},{12,20},{14,22},{16,8},... | collective-permute-start | bytes 442376 | tf_op jit(solution)/shard_map/ppermute | solution.py:19
  102.0 0.8 shard_map.61.table
  103.3 8.1 %collective-permute-done.26.refs_2_ = bf16[192,384]{1,0:T(8,128)(2,1)S(1)} collective-permute-done((bf16[192,384]{1,0:T(8,128)(2,1)S(1)}, bf16[192,384]{1,0:T(8,128)(2,1)S(1)}, u32[]{:S(2)}, u32[]{:S(2)}) %collective-permute-start.26) | collective-permute-done | bytes 147488 | tf_op jit(solution)/shard_map/ppermute | solution.py:19
  111.3 2.9 %collective-permute-start.15 = (bf16[192,384]{1,0:T(8,128)(2,1)S(1)}, bf16[192,384]{1,0:T(8,128)(2,1)S(1)}, u32[]{:S(2)}, u32[]{:S(2)}) collective-permute-start(bf16[192,384]{1,0:T(8,128)(2,1)S(1)} %get-tuple-element.90), channel_id=1, source_target_pairs={{0,16},{2,18},{4,20},{6,22},{8,24},{10,26},{12,28},{14,30},{16,0},... | collective-permute-start | bytes 442376 | tf_op jit(solution)/shard_map/ppermute | solution.py:19
  114.3 1.4 collective-permute-start.16
  115.8 0.6 copy-done.20
  116.5 0.7 copy-done.27
  117.1 12.0 %shard_map.63 = (bf16[192,384]{1,0:T(8,128)(2,1)}, bf16[192,384]{1,0:T(8,128)(2,1)}, bf16[192,384]{1,0:T(8,128)(2,1)}, bf16[192,384]{1,0:T(8,128)(2,1)}) custom-call(s32[16]{0:T(128)} %copy-done.10, bf16[192,384]{1,0:T(8,128)(2,1)} %copy-done.12, bf16[192,384]{1,0:T(8,128)(2,1)} %copy-done.25, bf16[192,384]{1,0:T(8,128)(2,1)} %copy-done.26, ...), custom_call_target="tpu_custom_call" | custom-call | flops 2717908992 | bytes 5898240 | tf_op jit(solution)/shard_map/pallas_call | solution.py:280
  129.2 2.5 %collective-permute-start.28 = (bf16[192,384]{1,0:T(8,128)(2,1)}, bf16[192,384]{1,0:T(8,128)(2,1)S(1)}, u32[]{:S(2)}, u32[]{:S(2)}) collective-permute-start(bf16[192,384]{1,0:T(8,128)(2,1)} %get-tuple-element.107), channel_id=1, source_target_pairs={{0,24},{2,26},{4,28},{6,30},{8,16},{10,18},{12,20},{14,22},{16,8},... | collective-permute-start | bytes 442376 | tf_op jit(solution)/shard_map/ppermute | solution.py:19
  131.7 0.6 copy-done.22
  132.4 0.7 copy-done.24
  133.0 12.3 %shard_map.62 = (bf16[192,384]{1,0:T(8,128)(2,1)}, bf16[192,384]{1,0:T(8,128)(2,1)}, bf16[192,384]{1,0:T(8,128)(2,1)}, bf16[192,384]{1,0:T(8,128)(2,1)}) custom-call(s32[16]{0:T(128)} %copy-done.10, bf16[192,384]{1,0:T(8,128)(2,1)} %copy-done.13, bf16[192,384]{1,0:T(8,128)(2,1)} %copy-done.22, bf16[192,384]{1,0:T(8,128)(2,1)} %copy-done.23, ...), custom_call_target="tpu_custom_call" | custom-call | flops 2717908992 | bytes 5898240 | tf_op jit(solution)/shard_map/pallas_call | solution.py:280
  145.4 3.2 %collective-permute-start.23 = (bf16[192,384]{1,0:T(8,128)(2,1)}, bf16[192,384]{1,0:T(8,128)(2,1)S(1)}, u32[]{:S(2)}, u32[]{:S(2)}) collective-permute-start(bf16[192,384]{1,0:T(8,128)(2,1)} %get-tuple-element.99), channel_id=1, source_target_pairs={{0,18},{2,16},{4,22},{6,20},{8,26},{10,24},{12,30},{14,28},{16,2},... | collective-permute-start | bytes 442376 | tf_op jit(solution)/shard_map/ppermute | solution.py:19
  148.6 0.9 collective-permute-start.30
  149.9 0.9 collective-permute-start.25
  150.7 5.5 %collective-permute-done.30.refs_2_ = bf16[192,384]{1,0:T(8,128)(2,1)S(1)} collective-permute-done((bf16[192,384]{1,0:T(8,128)(2,1)S(1)}, bf16[192,384]{1,0:T(8,128)(2,1)S(1)}, u32[]{:S(2)}, u32[]{:S(2)}) %collective-permute-start.30) | collective-permute-done | bytes 147488 | tf_op jit(solution)/shard_map/ppermute | solution.py:19
  156.3 2.0 %shard_map.64.refs_4_ = bf16[2,192,1536]{2,1,0:T(8,128)(2,1)} custom-call(s32[4]{0:T(128)S(1)} %pad_add_fusion.place, bf16[192,384]{1,0:T(8,128)(2,1)S(1)} %collective-permute-done.28.refs_0_, bf16[192,384]{1,0:T(8,128)(2,1)S(1)} %collective-permute-done.29.refs_1_, bf16[192,384]{1,0:T(8,128)(2,1)S(1)} %collective-permute-done.30.refs_2_, ...), custom_call_target="tpu_custom_call" | custom-call | tf_op jit(solution)/shard_map/pallas_call | solution.py:348
  158.2 3.1 %collective-permute-done.23.refs_1_ = bf16[192,384]{1,0:T(8,128)(2,1)S(1)} collective-permute-done((bf16[192,384]{1,0:T(8,128)(2,1)}, bf16[192,384]{1,0:T(8,128)(2,1)S(1)}, u32[]{:S(2)}, u32[]{:S(2)}) %collective-permute-start.23) | collective-permute-done | bytes 147488 | tf_op jit(solution)/shard_map/ppermute | solution.py:19
  161.4 2.0 %shard_map.65 = bf16[2,192,1536]{2,1,0:T(8,128)(2,1)} custom-call(s32[4]{0:T(128)S(1)} %pad_add_fusion.place, bf16[192,384]{1,0:T(8,128)(2,1)S(1)} %collective-permute-done.22.refs_0_, bf16[192,384]{1,0:T(8,128)(2,1)S(1)} %collective-permute-done.23.refs_1_, bf16[192,384]{1,0:T(8,128)(2,1)S(1)} %collective-permute-done.24.refs_2_, ...), custom_call_target="tpu_custom_call", output_to_operand_aliasing={{}: (5, {})} | custom-call | tf_op jit(solution)/shard_map/pallas_call | solution.py:348
  (90 shorter events, 3.0 us)
Async XLA Ops:
  3.1 6.5 %collective-permute-start.2 = (bf16[192,2560]{1,0:T(8,128)(2,1)}, bf16[192,2560]{1,0:T(8,128)(2,1)}, u32[]{:S(2)}, u32[]{:S(2)}) collective-permute-start(bf16[192,2560]{1,0:T(8,128)(2,1)} %get-tuple-element.111), channel_id=1, source_target_pairs={{0,2},{2,0},{4,6},{6,4},{8,10},{10,8},{12,14},{14,12},{16,18},{18,... | collective-permute-start | bytes 2949128 | tf_op jit(solution)/shard_map/ppermute | solution.py:19
  3.5 25.3 %collective-permute-start.1 = (bf16[192,2560]{1,0:T(8,128)(2,1)}, bf16[192,2560]{1,0:T(8,128)(2,1)S(1)}, u32[]{:S(2)}, u32[]{:S(2)}) collective-permute-start(bf16[192,2560]{1,0:T(8,128)(2,1)} %get-tuple-element.112), channel_id=1, source_target_pairs={{0,1},{1,0},{2,3},{3,2},{4,5},{5,4},{6,7},{7,6},{8,9},{9,8},{10,11... | collective-permute-start | bytes 2949128 | tf_op jit(solution)/shard_map/ppermute | solution.py:19
  6.9 1.2 collective-permute-start
  9.5 42.1 %collective-permute-start.3 = (bf16[192,2560]{1,0:T(8,128)(2,1)}, bf16[192,2560]{1,0:T(8,128)(2,1)S(1)}, u32[]{:S(2)}, u32[]{:S(2)}) collective-permute-start(bf16[192,2560]{1,0:T(8,128)(2,1)} %collective-permute-done.2.other_ref), channel_id=1, source_target_pairs={{0,1},{1,0},{2,3},{3,2},{4,5},{5,4},{6,7},{7,6},{8,9},{9,8},{10,11... | collective-permute-start | bytes 2949128 | tf_op jit(solution)/shard_map/ppermute | solution.py:19
  34.1 26.6 %collective-permute-start.5 = (bf16[208,768]{1,0:T(8,128)(2,1)S(1)}, bf16[208,768]{1,0:T(8,128)(2,1)S(1)}, u32[]{:S(2)}, u32[]{:S(2)}) collective-permute-start(bf16[208,768]{1,0:T(8,128)(2,1)S(1)} %get-tuple-element.69), channel_id=1, source_target_pairs={{0,8},{2,10},{4,12},{6,14},{8,0},{10,2},{12,4},{14,6},{16,24},{18,... | collective-permute-start | bytes 958472 | tf_op jit(solution)/shard_map/ppermute | solution.py:19
  36.2 31.9 %collective-permute-start.9 = (bf16[208,768]{1,0:T(8,128)(2,1)S(1)}, bf16[208,768]{1,0:T(8,128)(2,1)S(1)}, u32[]{:S(2)}, u32[]{:S(2)}) collective-permute-start(bf16[208,768]{1,0:T(8,128)(2,1)S(1)} %get-tuple-element.75), channel_id=1, source_target_pairs={{0,24},{2,26},{4,28},{6,30},{8,16},{10,18},{12,20},{14,22},{16,8},... | collective-permute-start | bytes 958472 | tf_op jit(solution)/shard_map/ppermute | solution.py:19
  43.9 58.1 %copy-start.3 = (bf16[208,768]{1,0:T(8,128)(2,1)}, bf16[208,768]{1,0:T(8,128)(2,1)S(1)}, u32[]{:S(2)}) copy-start(bf16[208,768]{1,0:T(8,128)(2,1)S(1)} %get-tuple-element.68.refs_0_.refs_4_) | copy-start | bytes 958468
  43.9 22.1 %collective-permute-start.7 = (bf16[208,768]{1,0:T(8,128)(2,1)S(1)}, bf16[208,768]{1,0:T(8,128)(2,1)S(1)}, u32[]{:S(2)}, u32[]{:S(2)}) collective-permute-start(bf16[208,768]{1,0:T(8,128)(2,1)S(1)} %get-tuple-element.72), channel_id=1, source_target_pairs={{0,16},{2,18},{4,20},{6,22},{8,24},{10,26},{12,28},{14,30},{16,0},... | collective-permute-start | bytes 958472 | tf_op jit(solution)/shard_map/ppermute | solution.py:19
  44.1 24.0 %collective-permute-start.4 = (bf16[208,768]{1,0:T(8,128)(2,1)S(1)}, bf16[208,768]{1,0:T(8,128)(2,1)S(1)}, u32[]{:S(2)}, u32[]{:S(2)}) collective-permute-start(bf16[208,768]{1,0:T(8,128)(2,1)S(1)} %get-tuple-element.68.refs_0_.refs_4_), channel_id=1, source_target_pairs={{0,4},{2,6},{4,0},{6,2},{8,12},{10,14},{12,8},{14,10},{16,20},{18,... | collective-permute-start | bytes 958472 | tf_op jit(solution)/shard_map/ppermute | solution.py:19
  60.7 19.6 %copy-start.11 = (bf16[192,768]{1,0:T(8,128)(2,1)}, bf16[192,768]{1,0:T(8,128)(2,1)S(1)}, u32[]{:S(2)}) copy-start(bf16[192,768]{1,0:T(8,128)(2,1)S(1)} %get-tuple-element.93.refs_5_) | copy-start | bytes 884740
  60.7 41.2 %copy-start.1 = (bf16[208,768]{1,0:T(8,128)(2,1)}, bf16[208,768]{1,0:T(8,128)(2,1)S(1)}, u32[]{:S(2)}) copy-start(bf16[208,768]{1,0:T(8,128)(2,1)S(1)} %collective-permute-done.5.refs_2_.refs_8_) | copy-start | bytes 958468
  60.7 10.7 %collective-permute-start.6 = (bf16[208,768]{1,0:T(8,128)(2,1)S(1)}, bf16[208,768]{1,0:T(8,128)(2,1)S(1)}, u32[]{:S(2)}, u32[]{:S(2)}) collective-permute-start(bf16[208,768]{1,0:T(8,128)(2,1)S(1)} %collective-permute-done.5.refs_2_.refs_8_), channel_id=1, source_target_pairs={{0,4},{2,6},{4,0},{6,2},{8,12},{10,14},{12,8},{14,10},{16,20},{18,... | collective-permute-start | bytes 958472 | tf_op jit(solution)/shard_map/ppermute | solution.py:19
  66.1 35.9 %copy-start.4 = (bf16[208,768]{1,0:T(8,128)(2,1)}, bf16[208,768]{1,0:T(8,128)(2,1)S(1)}, u32[]{:S(2)}) copy-start(bf16[208,768]{1,0:T(8,128)(2,1)S(1)} %collective-permute-done.7.refs_4_.refs_12_) | copy-start | bytes 958468
  66.1 14.2 %collective-permute-start.8 = (bf16[208,768]{1,0:T(8,128)(2,1)S(1)}, bf16[208,768]{1,0:T(8,128)(2,1)S(1)}, u32[]{:S(2)}, u32[]{:S(2)}) collective-permute-start(bf16[208,768]{1,0:T(8,128)(2,1)S(1)} %collective-permute-done.7.refs_4_.refs_12_), channel_id=1, source_target_pairs={{0,4},{2,6},{4,0},{6,2},{8,12},{10,14},{12,8},{14,10},{16,20},{18,... | collective-permute-start | bytes 958472 | tf_op jit(solution)/shard_map/ppermute | solution.py:19
  67.6 15.3 %collective-permute-start.12 = (bf16[192,768]{1,0:T(8,128)(2,1)S(1)}, bf16[192,768]{1,0:T(8,128)(2,1)S(1)}, u32[]{:S(2)}, u32[]{:S(2)}) collective-permute-start(bf16[192,768]{1,0:T(8,128)(2,1)S(1)} %get-tuple-element.93.refs_5_), channel_id=1, source_target_pairs={{0,4},{2,6},{4,0},{6,2},{8,12},{10,14},{12,8},{14,10},{16,20},{18,... | collective-permute-start | bytes 884744 | tf_op jit(solution)/shard_map/ppermute | solution.py:19
  68.1 33.9 %copy-start.2 = (bf16[208,768]{1,0:T(8,128)(2,1)}, bf16[208,768]{1,0:T(8,128)(2,1)S(1)}, u32[]{:S(2)}) copy-start(bf16[208,768]{1,0:T(8,128)(2,1)S(1)} %collective-permute-done.9.refs_6_.refs_16_) | copy-start | bytes 958468
  68.1 33.9 %copy-start.5 = (bf16[208,768]{1,0:T(8,128)(2,1)}, bf16[208,768]{1,0:T(8,128)(2,1)S(1)}, u32[]{:S(2)}) copy-start(bf16[208,768]{1,0:T(8,128)(2,1)S(1)} %collective-permute-done.4.refs_1_.refs_6_) | copy-start | bytes 958468
  68.1 14.7 %collective-permute-start.11 = (bf16[192,768]{1,0:T(8,128)(2,1)S(1)}, bf16[192,768]{1,0:T(8,128)(2,1)S(1)}, u32[]{:S(2)}, u32[]{:S(2)}) collective-permute-start(bf16[192,768]{1,0:T(8,128)(2,1)S(1)} %get-tuple-element.86), channel_id=1, source_target_pairs={{0,8},{2,10},{4,12},{6,14},{8,0},{10,2},{12,4},{14,6},{16,24},{18,... | collective-permute-start | bytes 884744 | tf_op jit(solution)/shard_map/ppermute | solution.py:19
  68.2 23.7 %collective-permute-start.18 = (bf16[192,768]{1,0:T(8,128)(2,1)S(1)}, bf16[192,768]{1,0:T(8,128)(2,1)S(1)}, u32[]{:S(2)}, u32[]{:S(2)}) collective-permute-start(bf16[192,768]{1,0:T(8,128)(2,1)S(1)} %get-tuple-element.95), channel_id=1, source_target_pairs={{0,16},{2,18},{4,20},{6,22},{8,24},{10,26},{12,28},{14,30},{16,0},... | collective-permute-start | bytes 884744 | tf_op jit(solution)/shard_map/ppermute | solution.py:19
  71.4 30.6 %copy-start.6 = (bf16[208,768]{1,0:T(8,128)(2,1)}, bf16[208,768]{1,0:T(8,128)(2,1)S(1)}, u32[]{:S(2)}) copy-start(bf16[208,768]{1,0:T(8,128)(2,1)S(1)} %collective-permute-done.6.refs_3_.refs_10_) | copy-start | bytes 958468
  71.4 22.0 %collective-permute-start.20 = (bf16[192,768]{1,0:T(8,128)(2,1)S(1)}, bf16[192,768]{1,0:T(8,128)(2,1)S(1)}, u32[]{:S(2)}, u32[]{:S(2)}) collective-permute-start(bf16[192,768]{1,0:T(8,128)(2,1)S(1)} %get-tuple-element.97), channel_id=1, source_target_pairs={{0,24},{2,26},{4,28},{6,30},{8,16},{10,18},{12,20},{14,22},{16,8},... | collective-permute-start | bytes 884744 | tf_op jit(solution)/shard_map/ppermute | solution.py:19
  80.3 48.9 %copy-start.13 = (bf16[192,384]{1,0:T(8,128)(2,1)}, bf16[192,384]{1,0:T(8,128)(2,1)S(1)}, u32[]{:S(2)}) copy-start(bf16[192,384]{1,0:T(8,128)(2,1)S(1)} %get-tuple-element.88.refs_0_) | copy-start | bytes 442372
  80.3 35.4 %copy-start.7 = (bf16[208,768]{1,0:T(8,128)(2,1)}, bf16[208,768]{1,0:T(8,128)(2,1)S(1)}, u32[]{:S(2)}) copy-start(bf16[208,768]{1,0:T(8,128)(2,1)S(1)} %collective-permute-done.8.refs_5_.refs_14_) | copy-start | bytes 958468
  80.3 13.7 %collective-permute-start.10 = (bf16[208,768]{1,0:T(8,128)(2,1)S(1)}, bf16[208,768]{1,0:T(8,128)(2,1)S(1)}, u32[]{:S(2)}, u32[]{:S(2)}) collective-permute-start(bf16[208,768]{1,0:T(8,128)(2,1)S(1)} %collective-permute-done.9.refs_6_.refs_16_), channel_id=1, source_target_pairs={{0,4},{2,6},{4,0},{6,2},{8,12},{10,14},{12,8},{14,10},{16,20},{18,... | collective-permute-start | bytes 958472 | tf_op jit(solution)/shard_map/ppermute | solution.py:19
  82.8 32.9 %copy-start.14 = (bf16[192,768]{1,0:T(8,128)(2,1)}, bf16[192,768]{1,0:T(8,128)(2,1)S(1)}, u32[]{:S(2)}) copy-start(bf16[192,768]{1,0:T(8,128)(2,1)S(1)} %collective-permute-done.12.refs_7_) | copy-start | bytes 884740
  82.9 32.9 %copy-start.15 = (bf16[192,768]{1,0:T(8,128)(2,1)}, bf16[192,768]{1,0:T(8,128)(2,1)S(1)}, u32[]{:S(2)}) copy-start(bf16[192,768]{1,0:T(8,128)(2,1)S(1)} %collective-permute-done.11.refs_9_) | copy-start | bytes 884740
  82.9 28.5 %collective-permute-start.17 = (bf16[192,768]{1,0:T(8,128)(2,1)S(1)}, bf16[192,768]{1,0:T(8,128)(2,1)S(1)}, u32[]{:S(2)}, u32[]{:S(2)}) collective-permute-start(bf16[192,768]{1,0:T(8,128)(2,1)S(1)} %collective-permute-done.11.refs_9_), channel_id=1, source_target_pairs={{0,4},{2,6},{4,0},{6,2},{8,12},{10,14},{12,8},{14,10},{16,20},{18,... | collective-permute-start | bytes 884744 | tf_op jit(solution)/shard_map/ppermute | solution.py:19
  91.9 23.9 %copy-start.16 = (bf16[192,768]{1,0:T(8,128)(2,1)}, bf16[192,768]{1,0:T(8,128)(2,1)S(1)}, u32[]{:S(2)}) copy-start(bf16[192,768]{1,0:T(8,128)(2,1)S(1)} %collective-permute-done.18.refs_13_) | copy-start | bytes 884740
  91.9 22.4 %collective-permute-start.19 = (bf16[192,768]{1,0:T(8,128)(2,1)S(1)}, bf16[192,768]{1,0:T(8,128)(2,1)S(1)}, u32[]{:S(2)}, u32[]{:S(2)}) collective-permute-start(bf16[192,768]{1,0:T(8,128)(2,1)S(1)} %collective-permute-done.18.refs_13_), channel_id=1, source_target_pairs={{0,4},{2,6},{4,0},{6,2},{8,12},{10,14},{12,8},{14,10},{16,20},{18,... | collective-permute-start | bytes 884744 | tf_op jit(solution)/shard_map/ppermute | solution.py:19
  93.4 5.9 %collective-permute-start.13 = (bf16[192,384]{1,0:T(8,128)(2,1)S(1)}, bf16[192,384]{1,0:T(8,128)(2,1)S(1)}, u32[]{:S(2)}, u32[]{:S(2)}) collective-permute-start(bf16[192,384]{1,0:T(8,128)(2,1)S(1)} %get-tuple-element.87), channel_id=1, source_target_pairs={{0,8},{2,10},{4,12},{6,14},{8,0},{10,2},{12,4},{14,6},{16,24},{18,... | collective-permute-start | bytes 442376 | tf_op jit(solution)/shard_map/ppermute | solution.py:19
  93.4 22.4 %copy-start.17 = (bf16[192,768]{1,0:T(8,128)(2,1)}, bf16[192,768]{1,0:T(8,128)(2,1)S(1)}, u32[]{:S(2)}) copy-start(bf16[192,768]{1,0:T(8,128)(2,1)S(1)} %collective-permute-done.20.refs_17_) | copy-start | bytes 884740
  93.4 22.3 %collective-permute-start.21 = (bf16[192,768]{1,0:T(8,128)(2,1)S(1)}, bf16[192,768]{1,0:T(8,128)(2,1)S(1)}, u32[]{:S(2)}, u32[]{:S(2)}) collective-permute-start(bf16[192,768]{1,0:T(8,128)(2,1)S(1)} %collective-permute-done.20.refs_17_), channel_id=1, source_target_pairs={{0,4},{2,6},{4,0},{6,2},{8,12},{10,14},{12,8},{14,10},{16,20},{18,... | collective-permute-start | bytes 884744 | tf_op jit(solution)/shard_map/ppermute | solution.py:19
  94.0 21.8 %copy-start.8 = (bf16[208,768]{1,0:T(8,128)(2,1)}, bf16[208,768]{1,0:T(8,128)(2,1)S(1)}, u32[]{:S(2)}) copy-start(bf16[208,768]{1,0:T(8,128)(2,1)S(1)} %collective-permute-done.10.refs_7_.refs_18_) | copy-start | bytes 958468
  94.0 17.3 %collective-permute-start.26 = (bf16[192,384]{1,0:T(8,128)(2,1)S(1)}, bf16[192,384]{1,0:T(8,128)(2,1)S(1)}, u32[]{:S(2)}, u32[]{:S(2)}) collective-permute-start(bf16[192,384]{1,0:T(8,128)(2,1)S(1)} %get-tuple-element.104), channel_id=1, source_target_pairs={{0,16},{2,18},{4,20},{6,22},{8,24},{10,26},{12,28},{14,30},{16,0},... | collective-permute-start | bytes 442376 | tf_op jit(solution)/shard_map/ppermute | solution.py:19
  99.3 16.5 %copy-start.25 = (bf16[192,384]{1,0:T(8,128)(2,1)}, bf16[192,384]{1,0:T(8,128)(2,1)S(1)}, u32[]{:S(2)}) copy-start(bf16[192,384]{1,0:T(8,128)(2,1)S(1)} %collective-permute-done.13.refs_1_) | copy-start | bytes 442372
  99.3 16.4 %collective-permute-start.27 = (bf16[192,384]{1,0:T(8,128)(2,1)S(1)}, bf16[192,384]{1,0:T(8,128)(2,1)S(1)}, u32[]{:S(2)}, u32[]{:S(2)}) collective-permute-start(bf16[192,384]{1,0:T(8,128)(2,1)S(1)} %get-tuple-element.106), channel_id=1, source_target_pairs={{0,24},{2,26},{4,28},{6,30},{8,16},{10,18},{12,20},{14,22},{16,8},... | collective-permute-start | bytes 442376 | tf_op jit(solution)/shard_map/ppermute | solution.py:19
  111.3 20.3 %collective-permute-start.14 = (bf16[192,384]{1,0:T(8,128)(2,1)S(1)}, bf16[192,384]{1,0:T(8,128)(2,1)S(1)}, u32[]{:S(2)}, u32[]{:S(2)}) collective-permute-start(bf16[192,384]{1,0:T(8,128)(2,1)S(1)} %get-tuple-element.89), channel_id=1, source_target_pairs={{0,8},{2,10},{4,12},{6,14},{8,0},{10,2},{12,4},{14,6},{16,24},{18,... | collective-permute-start | bytes 442376 | tf_op jit(solution)/shard_map/ppermute | solution.py:19
  111.3 20.3 %collective-permute-start.15 = (bf16[192,384]{1,0:T(8,128)(2,1)S(1)}, bf16[192,384]{1,0:T(8,128)(2,1)S(1)}, u32[]{:S(2)}, u32[]{:S(2)}) collective-permute-start(bf16[192,384]{1,0:T(8,128)(2,1)S(1)} %get-tuple-element.90), channel_id=1, source_target_pairs={{0,16},{2,18},{4,20},{6,22},{8,24},{10,26},{12,28},{14,30},{16,0},... | collective-permute-start | bytes 442376 | tf_op jit(solution)/shard_map/ppermute | solution.py:19
  114.3 17.4 %collective-permute-start.16 = (bf16[192,384]{1,0:T(8,128)(2,1)S(1)}, bf16[192,384]{1,0:T(8,128)(2,1)S(1)}, u32[]{:S(2)}, u32[]{:S(2)}) collective-permute-start(bf16[192,384]{1,0:T(8,128)(2,1)S(1)} %get-tuple-element.91), channel_id=1, source_target_pairs={{0,24},{2,26},{4,28},{6,30},{8,16},{10,18},{12,20},{14,22},{16,8},... | collective-permute-start | bytes 442376 | tf_op jit(solution)/shard_map/ppermute | solution.py:19
  129.2 20.3 %collective-permute-start.28 = (bf16[192,384]{1,0:T(8,128)(2,1)}, bf16[192,384]{1,0:T(8,128)(2,1)S(1)}, u32[]{:S(2)}, u32[]{:S(2)}) collective-permute-start(bf16[192,384]{1,0:T(8,128)(2,1)} %get-tuple-element.107), channel_id=1, source_target_pairs={{0,24},{2,26},{4,28},{6,30},{8,16},{10,18},{12,20},{14,22},{16,8},... | collective-permute-start | bytes 442376 | tf_op jit(solution)/shard_map/ppermute | solution.py:19
  131.6 16.9 %copy-start.21 = (bf16[192,384]{1,0:T(8,128)(2,1)S(1)}, bf16[192,384]{1,0:T(8,128)(2,1)}, u32[]{:S(2)}) copy-start(bf16[192,384]{1,0:T(8,128)(2,1)} %get-tuple-element.109) | copy-start | bytes 442372
  131.6 24.6 %copy-start.9 = (bf16[192,384]{1,0:T(8,128)(2,1)S(1)}, bf16[192,384]{1,0:T(8,128)(2,1)}, u32[]{:S(2)}) copy-start(bf16[192,384]{1,0:T(8,128)(2,1)} %get-tuple-element.110.refs_3_) | copy-start | bytes 442372
  131.6 18.2 %collective-permute-start.29 = (bf16[192,384]{1,0:T(8,128)(2,1)}, bf16[192,384]{1,0:T(8,128)(2,1)S(1)}, u32[]{:S(2)}, u32[]{:S(2)}) collective-permute-start(bf16[192,384]{1,0:T(8,128)(2,1)} %get-tuple-element.108), channel_id=1, source_target_pairs={{0,16},{2,18},{4,20},{6,22},{8,24},{10,26},{12,28},{14,30},{16,0},... | collective-permute-start | bytes 442376 | tf_op jit(solution)/shard_map/ppermute | solution.py:19
  145.3 12.9 %collective-permute-start.22 = (bf16[192,384]{1,0:T(8,128)(2,1)}, bf16[192,384]{1,0:T(8,128)(2,1)S(1)}, u32[]{:S(2)}, u32[]{:S(2)}) collective-permute-start(bf16[192,384]{1,0:T(8,128)(2,1)} %get-tuple-element.98), channel_id=1, source_target_pairs={{0,26},{2,24},{4,30},{6,28},{8,18},{10,16},{12,22},{14,20},{16,10}... | collective-permute-start | bytes 442376 | tf_op jit(solution)/shard_map/ppermute | solution.py:19
  145.4 15.9 %collective-permute-start.23 = (bf16[192,384]{1,0:T(8,128)(2,1)}, bf16[192,384]{1,0:T(8,128)(2,1)S(1)}, u32[]{:S(2)}, u32[]{:S(2)}) collective-permute-start(bf16[192,384]{1,0:T(8,128)(2,1)} %get-tuple-element.99), channel_id=1, source_target_pairs={{0,18},{2,16},{4,22},{6,20},{8,26},{10,24},{12,30},{14,28},{16,2},... | collective-permute-start | bytes 442376 | tf_op jit(solution)/shard_map/ppermute | solution.py:19
  148.6 7.7 %collective-permute-start.30 = (bf16[192,384]{1,0:T(8,128)(2,1)S(1)}, bf16[192,384]{1,0:T(8,128)(2,1)S(1)}, u32[]{:S(2)}, u32[]{:S(2)}) collective-permute-start(bf16[192,384]{1,0:T(8,128)(2,1)S(1)} %copy-done.21), channel_id=1, source_target_pairs={{0,8},{2,10},{4,12},{6,14},{8,0},{10,2},{12,4},{14,6},{16,24},{18,... | collective-permute-start | bytes 442376 | tf_op jit(solution)/shard_map/ppermute | solution.py:19
  149.5 11.9 %collective-permute-start.24 = (bf16[192,384]{1,0:T(8,128)(2,1)}, bf16[192,384]{1,0:T(8,128)(2,1)S(1)}, u32[]{:S(2)}, u32[]{:S(2)}) collective-permute-start(bf16[192,384]{1,0:T(8,128)(2,1)} %get-tuple-element.100), channel_id=1, source_target_pairs={{0,10},{2,8},{4,14},{6,12},{8,2},{10,0},{12,6},{14,4},{16,26},{18,... | collective-permute-start | bytes 442376 | tf_op jit(solution)/shard_map/ppermute | solution.py:19
  149.9 11.5 %collective-permute-start.25 = (bf16[192,384]{1,0:T(8,128)(2,1)}, bf16[192,384]{1,0:T(8,128)(2,1)S(1)}, u32[]{:S(2)}, u32[]{:S(2)}) collective-permute-start(bf16[192,384]{1,0:T(8,128)(2,1)} %get-tuple-element.101), channel_id=1, source_target_pairs={{0,2},{2,0},{4,6},{6,4},{8,10},{10,8},{12,14},{14,12},{16,18},{18,... | collective-permute-start | bytes 442376 | tf_op jit(solution)/shard_map/ppermute | solution.py:19
  (12 other events, 39.9 us)

commit v16 on v13

--- a/solution.py
+++ b/solution.py
@@ -391,7 +391,7 @@
     span_other = over_ctx(lax.dynamic_index_in_dim(spans, 1 - core, 0), 1)
     later = jnp.concatenate([place, lax.dynamic_index_in_dim(spans, core, 0), span_other])
     made_0 = {}
-    for part in (away[::-2], away[-2::-2]):
+    for part in (away[: ways // 2 - 1 : -1] or away, away[: ways // 2][::-1] if ways > 1 else []):
         if part:
             made_0.update(
                 rest_products(received, [0], [w_k, w_v], [start_k, start_v], later, ways, part, EXTRA)[0]
@@ -436,7 +436,7 @@
         value, _ = lax.optimization_barrier((asked[0][a], wait))
         queries[0][a] = over_ctx(value, a * rest)
     for a in away:
-        value, _ = lax.optimization_barrier((asked[1][a], queries[0][min(1, ways - 1)]))
+        value, _ = lax.optimization_barrier((asked[1][a], queries[0][a]))
         queries[1][a] = over_ctx(value, a * rest)
     table = span_table({i: (array, 0) for i, array in blocks.items()}, rows)
     second[rest // 2 + 1] = ahead_1

time: 162 us -> 161 us (level)
    unnamed x58 -> x56, local copies, waits for them, and re-layouts: 3.3 us -> 2.79 us
  transfers between devices with their start and end apart: 31 -> 31, of which waited for: 9 -> 10; matrix products, arithmetic and copies ran while one was open for 2% -> 1% of each run, Pallas kernels for 47% -> 48%
where the time goes in v16:
time: 161 us
  Pallas kernels  78.4 us (49%)
  starting transfers between devices  44.6 us (28%)
  waiting for transfers between devices  29.4 us (18%)
  local copies, waits for them, and re-layouts  7.84 us (5%)
    ppermute x31, starting transfers between devices, exchange(): return lax.ppermute(value, axis, [(i, i ^ bit) for i in range(size)])  44.6 us
    pallas_call x5, Pallas kernels, rest_products(): pl.pallas_call(functools.partial(rest_body, shares, len(weights), chunks,...  31.7 us
    ppermute x31, waiting for transfers between devices, exchange(): return lax.ppermute(value, axis, [(i, i ^ bit) for i in range(size)])  29.4 us
    pallas_call x2, Pallas kernels, attend(): pl.pallas_call(functools.partial(attend_body, block, ways, slots, len(arr...  24.3 us
    pallas_call x1, Pallas kernels, own_products(): pl.pallas_call(functools.partial(own_body, len(weights)), out_shape=[jax....  17.7 us
    pallas_call x2, Pallas kernels, assemble(): pl.pallas_call(functools.partial(assemble_body, ways), out_shape=jax.Shap...  3.99 us
  transfers between devices with their start and end apart: 31, of which 10 were waited for; matrix products, arithmetic and copies ran while one was open for 1% of the time, Pallas kernels for 48%

profile of v16, /device:TPU:0, one launch (start us, length us, event | category | flops | bytes accessed | tf_op | source)
XLA Modules:
  0.0 160.9 jit_solution(11210829157669324634)
XLA Ops:
  0.0 3.0 %dynamic-slice_bitcast_fusion = (bf16[192,2560]{1,0:T(8,128)(2,1)}, bf16[192,2560]{1,0:T(8,128)(2,1)}) fusion(bf16[2,192,2560]{2,1,0:T(8,128)(2,1)} %mine_ref.1, s32[]{:T(128)S(6)} %select_n.30, s32[]{:T(128)S(6)} %select_n.29), kind=kLoop, calls=%fused_computation | loop fusion | bytes 3932168 | tf_op jit(solution)/shard_map/jit(dynamic_index_in_dim)/squeeze | solution.py:385
  3.5 2.5 %collective-permute-start.1 = (bf16[192,2560]{1,0:T(8,128)(2,1)}, bf16[192,2560]{1,0:T(8,128)(2,1)S(1)}, u32[]{:S(2)}, u32[]{:S(2)}) collective-permute-start(bf16[192,2560]{1,0:T(8,128)(2,1)} %get-tuple-element.114), channel_id=1, source_target_pairs={{0,1},{1,0},{2,3},{3,2},{4,5},{5,4},{6,7},{7,6},{8,9},{9,8},{10,11... | collective-permute-start | bytes 2949128 | tf_op jit(solution)/shard_map/ppermute | solution.py:19
  6.3 0.7 fusion
  7.2 0.9 collective-permute-done
  8.1 1.3 concatenate.4.place
  9.4 0.9 collective-permute-start.3
  10.3 17.7 %shard_map.55 = (f32[2,192,1536]{2,1,0:T(8,128)S(1)}, f32[2,192,1536]{2,1,0:T(8,128)S(1)}, f32[2,192,1536]{2,1,0:T(8,128)S(1)}) custom-call(s32[4]{0:T(128)S(1)} %pad_add_fusion.place, bf16[2,192,2560]{2,1,0:T(8,128)(2,1)S(1)} %copy-done, bf16[192,2560]{1,0:T(8,128)(2,1)} %collective-permute-done.2.other_ref, bf16[5120,1536]{1,0:T(8,128)(2,1)} %refs_1_.10, ...), custom_call_target="tpu_custom_call" | custom-call | flops 9059696640 | bytes 23592960 | tf_op jit(solution)/shard_map/pallas_call | solution.py:43
  27.9 0.9 collective-permute-done.1.refs_0_
  28.8 5.2 %shard_map.59 = (bf16[208,768]{1,0:T(8,128)(2,1)S(1)}, bf16[208,768]{1,0:T(8,128)(2,1)S(1)}) custom-call(s32[6]{0:T(128)S(1)} %concatenate.4.place, bf16[192,2560]{1,0:T(8,128)(2,1)S(1)} %collective-permute-done.1.refs_0_, bf16[5120,1536]{1,0:T(8,128)(2,1)} %refs_1_.10, bf16[5120,1536]{1,0:T(8,128)(2,1)} %refs_2_.7, ...), custom_call_target="tpu_custom_call" | custom-call | flops 1509949440 | bytes 7864320 | tf_op jit(solution)/shard_map/pallas_call | solution.py:129
  34.1 3.1 %collective-permute-start.7 = (bf16[208,768]{1,0:T(8,128)(2,1)S(1)}, bf16[208,768]{1,0:T(8,128)(2,1)S(1)}, u32[]{:S(2)}, u32[]{:S(2)}) collective-permute-start(bf16[208,768]{1,0:T(8,128)(2,1)S(1)} %get-tuple-element.73), channel_id=1, source_target_pairs={{0,16},{2,18},{4,20},{6,22},{8,24},{10,26},{12,28},{14,30},{16,0},... | collective-permute-start | bytes 958472 | tf_op jit(solution)/shard_map/ppermute | solution.py:19
  37.2 1.3 collective-permute-start.9
  38.5 5.2 %shard_map.56 = (bf16[208,768]{1,0:T(8,128)(2,1)S(1)}, bf16[208,768]{1,0:T(8,128)(2,1)S(1)}) custom-call(s32[6]{0:T(128)S(1)} %concatenate.4.place, bf16[192,2560]{1,0:T(8,128)(2,1)S(1)} %collective-permute-done.1.refs_0_, bf16[5120,1536]{1,0:T(8,128)(2,1)} %refs_1_.10, bf16[5120,1536]{1,0:T(8,128)(2,1)} %refs_2_.7, ...), custom_call_target="tpu_custom_call" | custom-call | flops 1509949440 | bytes 7864320 | tf_op jit(solution)/shard_map/pallas_call | solution.py:129
  44.1 1.5 collective-permute-start.4
  45.6 6.0 %shard_map.57 = (bf16[192,384]{1,0:T(8,128)(2,1)S(1)}, bf16[192,384]{1,0:T(8,128)(2,1)S(1)}, bf16[192,384]{1,0:T(8,128)(2,1)S(1)}, bf16[192,384]{1,0:T(8,128)(2,1)S(1)}) custom-call(s32[4]{0:T(128)S(1)} %pad_add_fusion.place, bf16[192,2560]{1,0:T(8,128)(2,1)S(1)} %collective-permute-done.1.refs_0_, bf16[5120,1536]{1,0:T(8,128)(2,1)} %refs_1_.11, ...), custom_call_target="tpu_custom_call" | custom-call | flops 1509949440 | bytes 7864320 | tf_op jit(solution)/shard_map/pallas_call | solution.py:129
  51.6 9.1 %shard_map.58 = (bf16[192,768]{1,0:T(8,128)(2,1)S(1)}, bf16[192,768]{1,0:T(8,128)(2,1)S(1)}, bf16[192,768]{1,0:T(8,128)(2,1)S(1)}, bf16[192,768]{1,0:T(8,128)(2,1)S(1)}) custom-call(s32[4]{0:T(128)S(1)} %pad_add_fusion.place, bf16[192,2560]{1,0:T(8,128)(2,1)S(1)} %collective-permute-done.3.refs_0_, bf16[5120,1536]{1,0:T(8,128)(2,1)} %refs_1_.10, ...), custom_call_target="tpu_custom_call" | custom-call | flops 3019898880 | bytes 15728640 | tf_op jit(solution)/shard_map/pallas_call | solution.py:129
  60.7 0.6 collective-permute-start.8
  61.3 2.6 %collective-permute-done.5.refs_2_.refs_8_ = bf16[208,768]{1,0:T(8,128)(2,1)S(1)} collective-permute-done((bf16[208,768]{1,0:T(8,128)(2,1)S(1)}, bf16[208,768]{1,0:T(8,128)(2,1)S(1)}, u32[]{:S(2)}, u32[]{:S(2)}) %collective-permute-start.5) | collective-permute-done | bytes 319520 | tf_op jit(solution)/shard_map/ppermute | solution.py:19
  63.9 1.6 collective-permute-start.6
  65.9 4.0 %collective-permute-start.15 = (bf16[192,768]{1,0:T(8,128)(2,1)S(1)}, bf16[192,768]{1,0:T(8,128)(2,1)S(1)}, u32[]{:S(2)}, u32[]{:S(2)}) collective-permute-start(bf16[192,768]{1,0:T(8,128)(2,1)S(1)} %get-tuple-element.94), channel_id=1, source_target_pairs={{0,16},{2,18},{4,20},{6,22},{8,24},{10,26},{12,28},{14,30},{16,0},... | collective-permute-start | bytes 884744 | tf_op jit(solution)/shard_map/ppermute | solution.py:19
  70.0 1.3 collective-permute-done.8.refs_5_.refs_14_
  71.3 2.9 %collective-permute-start.18 = (bf16[192,768]{1,0:T(8,128)(2,1)S(1)}, bf16[192,768]{1,0:T(8,128)(2,1)S(1)}, u32[]{:S(2)}, u32[]{:S(2)}) collective-permute-start(bf16[192,768]{1,0:T(8,128)(2,1)S(1)} %get-tuple-element.100), channel_id=1, source_target_pairs={{0,24},{2,26},{4,28},{6,30},{8,16},{10,18},{12,20},{14,22},{16,8},... | collective-permute-start | bytes 884744 | tf_op jit(solution)/shard_map/ppermute | solution.py:19
  74.2 3.9 %collective-permute-done.6.refs_3_.refs_10_ = bf16[208,768]{1,0:T(8,128)(2,1)S(1)} collective-permute-done((bf16[208,768]{1,0:T(8,128)(2,1)S(1)}, bf16[208,768]{1,0:T(8,128)(2,1)S(1)}, u32[]{:S(2)}, u32[]{:S(2)}) %collective-permute-start.6) | collective-permute-done | bytes 319520 | tf_op jit(solution)/shard_map/ppermute | solution.py:19
  78.6 5.8 %collective-permute-done.11.refs_7_ = bf16[192,768]{1,0:T(8,128)(2,1)S(1)} collective-permute-done((bf16[192,768]{1,0:T(8,128)(2,1)S(1)}, bf16[192,768]{1,0:T(8,128)(2,1)S(1)}, u32[]{:S(2)}, u32[]{:S(2)}) %collective-permute-start.11) | collective-permute-done | bytes 294944 | tf_op jit(solution)/shard_map/ppermute | solution.py:19
  84.4 1.8 %collective-permute-start.13 = (bf16[192,384]{1,0:T(8,128)(2,1)S(1)}, bf16[192,384]{1,0:T(8,128)(2,1)S(1)}, u32[]{:S(2)}, u32[]{:S(2)}) collective-permute-start(bf16[192,384]{1,0:T(8,128)(2,1)S(1)} %get-tuple-element.89), channel_id=1, source_target_pairs={{0,8},{2,10},{4,12},{6,14},{8,0},{10,2},{12,4},{14,6},{16,24},{18,... | collective-permute-start | bytes 442376 | tf_op jit(solution)/shard_map/ppermute | solution.py:19
  86.3 0.5 collective-permute-start.21
  86.8 3.8 %collective-permute-done.15.refs_13_ = bf16[192,768]{1,0:T(8,128)(2,1)S(1)} collective-permute-done((bf16[192,768]{1,0:T(8,128)(2,1)S(1)}, bf16[192,768]{1,0:T(8,128)(2,1)S(1)}, u32[]{:S(2)}, u32[]{:S(2)}) %collective-permute-start.15) | collective-permute-done | bytes 294944 | tf_op jit(solution)/shard_map/ppermute | solution.py:19
  90.6 1.5 collective-permute-start.22
  92.6 5.6 %collective-permute-start.16 = (bf16[192,384]{1,0:T(8,128)(2,1)S(1)}, bf16[192,384]{1,0:T(8,128)(2,1)S(1)}, u32[]{:S(2)}, u32[]{:S(2)}) collective-permute-start(bf16[192,384]{1,0:T(8,128)(2,1)S(1)} %get-tuple-element.95), channel_id=1, source_target_pairs={{0,16},{2,18},{4,20},{6,22},{8,24},{10,26},{12,28},{14,30},{16,0},... | collective-permute-start | bytes 442376 | tf_op jit(solution)/shard_map/ppermute | solution.py:19
  98.2 0.7 collective-permute-start.19
  98.9 6.2 %shard_map.61 = (bf16[192,384]{1,0:T(8,128)(2,1)S(1)}, bf16[192,384]{1,0:T(8,128)(2,1)S(1)}, bf16[192,384]{1,0:T(8,128)(2,1)S(1)}, bf16[192,384]{1,0:T(8,128)(2,1)S(1)}) custom-call(s32[4]{0:T(128)S(1)} %pad_add_fusion.place, bf16[192,2560]{1,0:T(8,128)(2,1)S(1)} %collective-permute-done.3.refs_0_, bf16[5120,1536]{1,0:T(8,128)(2,1)} %refs_1_.11, ...), custom_call_target="tpu_custom_call" | custom-call | flops 1509949440 | bytes 7864320 | tf_op jit(solution)/shard_map/pallas_call | solution.py:129
  105.1 1.9 %collective-permute-done.16.refs_2_ = bf16[192,384]{1,0:T(8,128)(2,1)S(1)} collective-permute-done((bf16[192,384]{1,0:T(8,128)(2,1)S(1)}, bf16[192,384]{1,0:T(8,128)(2,1)S(1)}, u32[]{:S(2)}, u32[]{:S(2)}) %collective-permute-start.16) | collective-permute-done | bytes 147488 | tf_op jit(solution)/shard_map/ppermute | solution.py:19
  107.2 0.8 shard_map.60.table
  107.9 1.9 %collective-permute-start.17 = (bf16[192,384]{1,0:T(8,128)(2,1)S(1)}, bf16[192,384]{1,0:T(8,128)(2,1)S(1)}, u32[]{:S(2)}, u32[]{:S(2)}) collective-permute-start(bf16[192,384]{1,0:T(8,128)(2,1)S(1)} %get-tuple-element.96), channel_id=1, source_target_pairs={{0,16},{2,18},{4,20},{6,22},{8,24},{10,26},{12,28},{14,30},{16,0},... | collective-permute-start | bytes 442376 | tf_op jit(solution)/shard_map/ppermute | solution.py:19
  109.9 3.0 %collective-permute-start.20 = (bf16[192,384]{1,0:T(8,128)(2,1)S(1)}, bf16[192,384]{1,0:T(8,128)(2,1)S(1)}, u32[]{:S(2)}, u32[]{:S(2)}) collective-permute-start(bf16[192,384]{1,0:T(8,128)(2,1)S(1)} %get-tuple-element.102), channel_id=1, source_target_pairs={{0,24},{2,26},{4,28},{6,30},{8,16},{10,18},{12,20},{14,22},{16,8},... | collective-permute-start | bytes 442376 | tf_op jit(solution)/shard_map/ppermute | solution.py:19
  112.9 0.7 copy-done.19
  113.5 0.7 copy-done.20
  114.3 12.0 %shard_map.63 = (bf16[192,384]{1,0:T(8,128)(2,1)}, bf16[192,384]{1,0:T(8,128)(2,1)}, bf16[192,384]{1,0:T(8,128)(2,1)}, bf16[192,384]{1,0:T(8,128)(2,1)}) custom-call(s32[16]{0:T(128)} %copy-done.10, bf16[192,384]{1,0:T(8,128)(2,1)} %copy-done.12, bf16[192,384]{1,0:T(8,128)(2,1)} %copy-done.21, bf16[192,384]{1,0:T(8,128)(2,1)} %copy-done.25, ...), custom_call_target="tpu_custom_call" | custom-call | flops 2717908992 | bytes 5898240 | tf_op jit(solution)/shard_map/pallas_call | solution.py:280
  126.3 0.9 collective-permute-start.28
  127.3 3.5 %collective-permute-start.30 = (bf16[192,384]{1,0:T(8,128)(2,1)}, bf16[192,384]{1,0:T(8,128)(2,1)S(1)}, u32[]{:S(2)}, u32[]{:S(2)}) collective-permute-start(bf16[192,384]{1,0:T(8,128)(2,1)} %get-tuple-element.111), channel_id=1, source_target_pairs={{0,8},{2,10},{4,12},{6,14},{8,0},{10,2},{12,4},{14,6},{16,24},{18,... | collective-permute-start | bytes 442376 | tf_op jit(solution)/shard_map/ppermute | solution.py:19
  130.8 0.7 copy-done.23
  131.5 0.7 copy-done.24
  132.1 12.3 %shard_map.62 = (bf16[192,384]{1,0:T(8,128)(2,1)}, bf16[192,384]{1,0:T(8,128)(2,1)}, bf16[192,384]{1,0:T(8,128)(2,1)}, bf16[192,384]{1,0:T(8,128)(2,1)}) custom-call(s32[16]{0:T(128)} %copy-done.10, bf16[192,384]{1,0:T(8,128)(2,1)} %copy-done.13, bf16[192,384]{1,0:T(8,128)(2,1)} %copy-done.22, bf16[192,384]{1,0:T(8,128)(2,1)} %copy-done.23, ...), custom_call_target="tpu_custom_call" | custom-call | flops 2717908992 | bytes 5898240 | tf_op jit(solution)/shard_map/pallas_call | solution.py:280
  144.5 1.2 collective-permute-start.25
  145.7 3.0 %collective-permute-start.27 = (bf16[192,384]{1,0:T(8,128)(2,1)}, bf16[192,384]{1,0:T(8,128)(2,1)S(1)}, u32[]{:S(2)}, u32[]{:S(2)}) collective-permute-start(bf16[192,384]{1,0:T(8,128)(2,1)} %get-tuple-element.108), channel_id=1, source_target_pairs={{0,2},{2,0},{4,6},{6,4},{8,10},{10,8},{12,14},{14,12},{16,18},{18,... | collective-permute-start | bytes 442376 | tf_op jit(solution)/shard_map/ppermute | solution.py:19
  148.7 2.0 %shard_map.64.refs_4_ = bf16[2,192,1536]{2,1,0:T(8,128)(2,1)} custom-call(s32[4]{0:T(128)S(1)} %pad_add_fusion.place, bf16[192,384]{1,0:T(8,128)(2,1)S(1)} %collective-permute-done.28.refs_0_, bf16[192,384]{1,0:T(8,128)(2,1)S(1)} %collective-permute-done.29.refs_1_, bf16[192,384]{1,0:T(8,128)(2,1)S(1)} %collective-permute-done.30.refs_2_, ...), custom_call_target="tpu_custom_call" | custom-call | tf_op jit(solution)/shard_map/pallas_call | solution.py:348
  150.7 1.9 %collective-permute-done.24.refs_0_ = bf16[192,384]{1,0:T(8,128)(2,1)S(1)} collective-permute-done((bf16[192,384]{1,0:T(8,128)(2,1)}, bf16[192,384]{1,0:T(8,128)(2,1)S(1)}, u32[]{:S(2)}, u32[]{:S(2)}) %collective-permute-start.24) | collective-permute-done | bytes 147488 | tf_op jit(solution)/shard_map/ppermute | solution.py:19
  152.6 6.4 %collective-permute-done.25.refs_1_ = bf16[192,384]{1,0:T(8,128)(2,1)S(1)} collective-permute-done((bf16[192,384]{1,0:T(8,128)(2,1)}, bf16[192,384]{1,0:T(8,128)(2,1)S(1)}, u32[]{:S(2)}, u32[]{:S(2)}) %collective-permute-start.25) | collective-permute-done | bytes 147488 | tf_op jit(solution)/shard_map/ppermute | solution.py:19
  158.9 2.0 %shard_map.65 = bf16[2,192,1536]{2,1,0:T(8,128)(2,1)} custom-call(s32[4]{0:T(128)S(1)} %pad_add_fusion.place, bf16[192,384]{1,0:T(8,128)(2,1)S(1)} %collective-permute-done.24.refs_0_, bf16[192,384]{1,0:T(8,128)(2,1)S(1)} %collective-permute-done.25.refs_1_, bf16[192,384]{1,0:T(8,128)(2,1)S(1)} %collective-permute-done.26.refs_2_, ...), custom_call_target="tpu_custom_call", output_to_operand_aliasing={{}: (5, {})} | custom-call | tf_op jit(solution)/shard_map/pallas_call | solution.py:348
  (88 shorter events, 3.0 us)
Async XLA Ops:
  0.0 10.3 %copy-start = (bf16[2,192,2560]{2,1,0:T(8,128)(2,1)S(1)}, bf16[2,192,2560]{2,1,0:T(8,128)(2,1)}, u32[]{:S(2)}) copy-start(bf16[2,192,2560]{2,1,0:T(8,128)(2,1)} %mine_ref.1) | copy-start | bytes 5898244
  3.1 6.4 %collective-permute-start.2 = (bf16[192,2560]{1,0:T(8,128)(2,1)}, bf16[192,2560]{1,0:T(8,128)(2,1)}, u32[]{:S(2)}, u32[]{:S(2)}) collective-permute-start(bf16[192,2560]{1,0:T(8,128)(2,1)} %get-tuple-element.113), channel_id=1, source_target_pairs={{0,2},{2,0},{4,6},{6,4},{8,10},{10,8},{12,14},{14,12},{16,18},{18,... | collective-permute-start | bytes 2949128 | tf_op jit(solution)/shard_map/ppermute | solution.py:19
  3.5 25.3 %collective-permute-start.1 = (bf16[192,2560]{1,0:T(8,128)(2,1)}, bf16[192,2560]{1,0:T(8,128)(2,1)S(1)}, u32[]{:S(2)}, u32[]{:S(2)}) collective-permute-start(bf16[192,2560]{1,0:T(8,128)(2,1)} %get-tuple-element.114), channel_id=1, source_target_pairs={{0,1},{1,0},{2,3},{3,2},{4,5},{5,4},{6,7},{7,6},{8,9},{9,8},{10,11... | collective-permute-start | bytes 2949128 | tf_op jit(solution)/shard_map/ppermute | solution.py:19
  6.9 1.2 collective-permute-start
  9.4 42.2 %collective-permute-start.3 = (bf16[192,2560]{1,0:T(8,128)(2,1)}, bf16[192,2560]{1,0:T(8,128)(2,1)S(1)}, u32[]{:S(2)}, u32[]{:S(2)}) collective-permute-start(bf16[192,2560]{1,0:T(8,128)(2,1)} %collective-permute-done.2.other_ref), channel_id=1, source_target_pairs={{0,1},{1,0},{2,3},{3,2},{4,5},{5,4},{6,7},{7,6},{8,9},{9,8},{10,11... | collective-permute-start | bytes 2949128 | tf_op jit(solution)/shard_map/ppermute | solution.py:19
  34.1 26.6 %collective-permute-start.7 = (bf16[208,768]{1,0:T(8,128)(2,1)S(1)}, bf16[208,768]{1,0:T(8,128)(2,1)S(1)}, u32[]{:S(2)}, u32[]{:S(2)}) collective-permute-start(bf16[208,768]{1,0:T(8,128)(2,1)S(1)} %get-tuple-element.73), channel_id=1, source_target_pairs={{0,16},{2,18},{4,20},{6,22},{8,24},{10,26},{12,28},{14,30},{16,0},... | collective-permute-start | bytes 958472 | tf_op jit(solution)/shard_map/ppermute | solution.py:19
  37.2 28.7 %collective-permute-start.9 = (bf16[208,768]{1,0:T(8,128)(2,1)S(1)}, bf16[208,768]{1,0:T(8,128)(2,1)S(1)}, u32[]{:S(2)}, u32[]{:S(2)}) collective-permute-start(bf16[208,768]{1,0:T(8,128)(2,1)S(1)} %get-tuple-element.76), channel_id=1, source_target_pairs={{0,24},{2,26},{4,28},{6,30},{8,16},{10,18},{12,20},{14,22},{16,8},... | collective-permute-start | bytes 958472 | tf_op jit(solution)/shard_map/ppermute | solution.py:19
  43.8 63.3 %copy-start.3 = (bf16[208,768]{1,0:T(8,128)(2,1)}, bf16[208,768]{1,0:T(8,128)(2,1)S(1)}, u32[]{:S(2)}) copy-start(bf16[208,768]{1,0:T(8,128)(2,1)S(1)} %get-tuple-element.69.refs_0_.refs_4_) | copy-start | bytes 958468
  43.8 20.1 %collective-permute-start.5 = (bf16[208,768]{1,0:T(8,128)(2,1)S(1)}, bf16[208,768]{1,0:T(8,128)(2,1)S(1)}, u32[]{:S(2)}, u32[]{:S(2)}) collective-permute-start(bf16[208,768]{1,0:T(8,128)(2,1)S(1)} %get-tuple-element.70), channel_id=1, source_target_pairs={{0,8},{2,10},{4,12},{6,14},{8,0},{10,2},{12,4},{14,6},{16,24},{18,... | collective-permute-start | bytes 958472 | tf_op jit(solution)/shard_map/ppermute | solution.py:19
  44.1 21.8 %collective-permute-start.4 = (bf16[208,768]{1,0:T(8,128)(2,1)S(1)}, bf16[208,768]{1,0:T(8,128)(2,1)S(1)}, u32[]{:S(2)}, u32[]{:S(2)}) collective-permute-start(bf16[208,768]{1,0:T(8,128)(2,1)S(1)} %get-tuple-element.69.refs_0_.refs_4_), channel_id=1, source_target_pairs={{0,4},{2,6},{4,0},{6,2},{8,12},{10,14},{12,8},{14,10},{16,20},{18,... | collective-permute-start | bytes 958472 | tf_op jit(solution)/shard_map/ppermute | solution.py:19
  51.6 9.1 %copy-start.12 = (bf16[192,384]{1,0:T(8,128)(2,1)}, bf16[192,384]{1,0:T(8,128)(2,1)S(1)}, u32[]{:S(2)}) copy-start(bf16[192,384]{1,0:T(8,128)(2,1)S(1)} %get-tuple-element.82.refs_0_) | copy-start | bytes 442372
  60.7 44.4 %copy-start.11 = (bf16[192,768]{1,0:T(8,128)(2,1)}, bf16[192,768]{1,0:T(8,128)(2,1)S(1)}, u32[]{:S(2)}) copy-start(bf16[192,768]{1,0:T(8,128)(2,1)S(1)} %get-tuple-element.104.refs_5_) | copy-start | bytes 884740
  60.7 46.4 %copy-start.1 = (bf16[208,768]{1,0:T(8,128)(2,1)}, bf16[208,768]{1,0:T(8,128)(2,1)S(1)}, u32[]{:S(2)}) copy-start(bf16[208,768]{1,0:T(8,128)(2,1)S(1)} %collective-permute-done.7.refs_4_.refs_12_) | copy-start | bytes 958468
  60.7 10.5 %collective-permute-start.8 = (bf16[208,768]{1,0:T(8,128)(2,1)S(1)}, bf16[208,768]{1,0:T(8,128)(2,1)S(1)}, u32[]{:S(2)}, u32[]{:S(2)}) collective-permute-start(bf16[208,768]{1,0:T(8,128)(2,1)S(1)} %collective-permute-done.7.refs_4_.refs_12_), channel_id=1, source_target_pairs={{0,4},{2,6},{4,0},{6,2},{8,12},{10,14},{12,8},{14,10},{16,20},{18,... | collective-permute-start | bytes 958472 | tf_op jit(solution)/shard_map/ppermute | solution.py:19
  63.9 43.2 %copy-start.4 = (bf16[208,768]{1,0:T(8,128)(2,1)}, bf16[208,768]{1,0:T(8,128)(2,1)S(1)}, u32[]{:S(2)}) copy-start(bf16[208,768]{1,0:T(8,128)(2,1)S(1)} %collective-permute-done.5.refs_2_.refs_8_) | copy-start | bytes 958468
  63.9 14.2 %collective-permute-start.6 = (bf16[208,768]{1,0:T(8,128)(2,1)S(1)}, bf16[208,768]{1,0:T(8,128)(2,1)S(1)}, u32[]{:S(2)}, u32[]{:S(2)}) collective-permute-start(bf16[208,768]{1,0:T(8,128)(2,1)S(1)} %collective-permute-done.5.refs_2_.refs_8_), channel_id=1, source_target_pairs={{0,4},{2,6},{4,0},{6,2},{8,12},{10,14},{12,8},{14,10},{16,20},{18,... | collective-permute-start | bytes 958472 | tf_op jit(solution)/shard_map/ppermute | solution.py:19
  65.4 19.0 %collective-permute-start.11 = (bf16[192,768]{1,0:T(8,128)(2,1)S(1)}, bf16[192,768]{1,0:T(8,128)(2,1)S(1)}, u32[]{:S(2)}, u32[]{:S(2)}) collective-permute-start(bf16[192,768]{1,0:T(8,128)(2,1)S(1)} %get-tuple-element.104.refs_5_), channel_id=1, source_target_pairs={{0,4},{2,6},{4,0},{6,2},{8,12},{10,14},{12,8},{14,10},{16,20},{18,... | collective-permute-start | bytes 884744 | tf_op jit(solution)/shard_map/ppermute | solution.py:19
  65.9 41.2 %copy-start.5 = (bf16[208,768]{1,0:T(8,128)(2,1)}, bf16[208,768]{1,0:T(8,128)(2,1)S(1)}, u32[]{:S(2)}) copy-start(bf16[208,768]{1,0:T(8,128)(2,1)S(1)} %collective-permute-done.4.refs_1_.refs_6_) | copy-start | bytes 958468
  65.9 18.5 %collective-permute-start.12 = (bf16[192,768]{1,0:T(8,128)(2,1)S(1)}, bf16[192,768]{1,0:T(8,128)(2,1)S(1)}, u32[]{:S(2)}, u32[]{:S(2)}) collective-permute-start(bf16[192,768]{1,0:T(8,128)(2,1)S(1)} %get-tuple-element.87), channel_id=1, source_target_pairs={{0,8},{2,10},{4,12},{6,14},{8,0},{10,2},{12,4},{14,6},{16,24},{18,... | collective-permute-start | bytes 884744 | tf_op jit(solution)/shard_map/ppermute | solution.py:19
  65.9 41.2 %copy-start.2 = (bf16[208,768]{1,0:T(8,128)(2,1)}, bf16[208,768]{1,0:T(8,128)(2,1)S(1)}, u32[]{:S(2)}) copy-start(bf16[208,768]{1,0:T(8,128)(2,1)S(1)} %collective-permute-done.9.refs_6_.refs_16_) | copy-start | bytes 958468
  65.9 24.7 %collective-permute-start.15 = (bf16[192,768]{1,0:T(8,128)(2,1)S(1)}, bf16[192,768]{1,0:T(8,128)(2,1)S(1)}, u32[]{:S(2)}, u32[]{:S(2)}) collective-permute-start(bf16[192,768]{1,0:T(8,128)(2,1)S(1)} %get-tuple-element.94), channel_id=1, source_target_pairs={{0,16},{2,18},{4,20},{6,22},{8,24},{10,26},{12,28},{14,30},{16,0},... | collective-permute-start | bytes 884744 | tf_op jit(solution)/shard_map/ppermute | solution.py:19
  71.3 35.9 %copy-start.6 = (bf16[208,768]{1,0:T(8,128)(2,1)}, bf16[208,768]{1,0:T(8,128)(2,1)S(1)}, u32[]{:S(2)}) copy-start(bf16[208,768]{1,0:T(8,128)(2,1)S(1)} %collective-permute-done.8.refs_5_.refs_14_) | copy-start | bytes 958468
  71.3 20.8 %collective-permute-start.18 = (bf16[192,768]{1,0:T(8,128)(2,1)S(1)}, bf16[192,768]{1,0:T(8,128)(2,1)S(1)}, u32[]{:S(2)}, u32[]{:S(2)}) collective-permute-start(bf16[192,768]{1,0:T(8,128)(2,1)S(1)} %get-tuple-element.100), channel_id=1, source_target_pairs={{0,24},{2,26},{4,28},{6,30},{8,16},{10,18},{12,20},{14,22},{16,8},... | collective-permute-start | bytes 884744 | tf_op jit(solution)/shard_map/ppermute | solution.py:19
  78.1 29.0 %copy-start.7 = (bf16[208,768]{1,0:T(8,128)(2,1)}, bf16[208,768]{1,0:T(8,128)(2,1)S(1)}, u32[]{:S(2)}) copy-start(bf16[208,768]{1,0:T(8,128)(2,1)S(1)} %collective-permute-done.6.refs_3_.refs_10_) | copy-start | bytes 958468
  78.1 14.5 %collective-permute-start.10 = (bf16[208,768]{1,0:T(8,128)(2,1)S(1)}, bf16[208,768]{1,0:T(8,128)(2,1)S(1)}, u32[]{:S(2)}, u32[]{:S(2)}) collective-permute-start(bf16[208,768]{1,0:T(8,128)(2,1)S(1)} %collective-permute-done.9.refs_6_.refs_16_), channel_id=1, source_target_pairs={{0,4},{2,6},{4,0},{6,2},{8,12},{10,14},{12,8},{14,10},{16,20},{18,... | collective-permute-start | bytes 958472 | tf_op jit(solution)/shard_map/ppermute | solution.py:19
  84.4 20.6 %copy-start.14 = (bf16[192,768]{1,0:T(8,128)(2,1)}, bf16[192,768]{1,0:T(8,128)(2,1)S(1)}, u32[]{:S(2)}) copy-start(bf16[192,768]{1,0:T(8,128)(2,1)S(1)} %collective-permute-done.11.refs_7_) | copy-start | bytes 884740
  84.4 20.6 %copy-start.15 = (bf16[192,768]{1,0:T(8,128)(2,1)}, bf16[192,768]{1,0:T(8,128)(2,1)S(1)}, u32[]{:S(2)}) copy-start(bf16[192,768]{1,0:T(8,128)(2,1)S(1)} %collective-permute-done.12.refs_9_) | copy-start | bytes 884740
  84.4 13.7 %collective-permute-start.13 = (bf16[192,384]{1,0:T(8,128)(2,1)S(1)}, bf16[192,384]{1,0:T(8,128)(2,1)S(1)}, u32[]{:S(2)}, u32[]{:S(2)}) collective-permute-start(bf16[192,384]{1,0:T(8,128)(2,1)S(1)} %get-tuple-element.89), channel_id=1, source_target_pairs={{0,8},{2,10},{4,12},{6,14},{8,0},{10,2},{12,4},{14,6},{16,24},{18,... | collective-permute-start | bytes 442376 | tf_op jit(solution)/shard_map/ppermute | solution.py:19
  86.3 23.6 %collective-permute-start.21 = (bf16[192,768]{1,0:T(8,128)(2,1)S(1)}, bf16[192,768]{1,0:T(8,128)(2,1)S(1)}, u32[]{:S(2)}, u32[]{:S(2)}) collective-permute-start(bf16[192,768]{1,0:T(8,128)(2,1)S(1)} %collective-permute-done.12.refs_9_), channel_id=1, source_target_pairs={{0,4},{2,6},{4,0},{6,2},{8,12},{10,14},{12,8},{14,10},{16,20},{18,... | collective-permute-start | bytes 884744 | tf_op jit(solution)/shard_map/ppermute | solution.py:19
  90.6 14.5 %copy-start.16 = (bf16[192,768]{1,0:T(8,128)(2,1)}, bf16[192,768]{1,0:T(8,128)(2,1)S(1)}, u32[]{:S(2)}) copy-start(bf16[192,768]{1,0:T(8,128)(2,1)S(1)} %collective-permute-done.15.refs_13_) | copy-start | bytes 884740
  90.6 22.2 %collective-permute-start.22 = (bf16[192,768]{1,0:T(8,128)(2,1)S(1)}, bf16[192,768]{1,0:T(8,128)(2,1)S(1)}, u32[]{:S(2)}, u32[]{:S(2)}) collective-permute-start(bf16[192,768]{1,0:T(8,128)(2,1)S(1)} %collective-permute-done.15.refs_13_), channel_id=1, source_target_pairs={{0,4},{2,6},{4,0},{6,2},{8,12},{10,14},{12,8},{14,10},{16,20},{18,... | collective-permute-start | bytes 884744 | tf_op jit(solution)/shard_map/ppermute | solution.py:19
  92.1 13.0 %copy-start.17 = (bf16[192,768]{1,0:T(8,128)(2,1)}, bf16[192,768]{1,0:T(8,128)(2,1)S(1)}, u32[]{:S(2)}) copy-start(bf16[192,768]{1,0:T(8,128)(2,1)S(1)} %collective-permute-done.18.refs_17_) | copy-start | bytes 884740
  92.1 20.7 %collective-permute-start.23 = (bf16[192,768]{1,0:T(8,128)(2,1)S(1)}, bf16[192,768]{1,0:T(8,128)(2,1)S(1)}, u32[]{:S(2)}, u32[]{:S(2)}) collective-permute-start(bf16[192,768]{1,0:T(8,128)(2,1)S(1)} %collective-permute-done.18.refs_17_), channel_id=1, source_target_pairs={{0,4},{2,6},{4,0},{6,2},{8,12},{10,14},{12,8},{14,10},{16,20},{18,... | collective-permute-start | bytes 884744 | tf_op jit(solution)/shard_map/ppermute | solution.py:19
  92.6 14.5 %copy-start.8 = (bf16[208,768]{1,0:T(8,128)(2,1)}, bf16[208,768]{1,0:T(8,128)(2,1)S(1)}, u32[]{:S(2)}) copy-start(bf16[208,768]{1,0:T(8,128)(2,1)S(1)} %collective-permute-done.10.refs_7_.refs_18_) | copy-start | bytes 958468
  92.6 14.5 %collective-permute-start.16 = (bf16[192,384]{1,0:T(8,128)(2,1)S(1)}, bf16[192,384]{1,0:T(8,128)(2,1)S(1)}, u32[]{:S(2)}, u32[]{:S(2)}) collective-permute-start(bf16[192,384]{1,0:T(8,128)(2,1)S(1)} %get-tuple-element.95), channel_id=1, source_target_pairs={{0,16},{2,18},{4,20},{6,22},{8,24},{10,26},{12,28},{14,30},{16,0},... | collective-permute-start | bytes 442376 | tf_op jit(solution)/shard_map/ppermute | solution.py:19
  98.2 9.7 %collective-permute-start.19 = (bf16[192,384]{1,0:T(8,128)(2,1)S(1)}, bf16[192,384]{1,0:T(8,128)(2,1)S(1)}, u32[]{:S(2)}, u32[]{:S(2)}) collective-permute-start(bf16[192,384]{1,0:T(8,128)(2,1)S(1)} %get-tuple-element.101), channel_id=1, source_target_pairs={{0,24},{2,26},{4,28},{6,30},{8,16},{10,18},{12,20},{14,22},{16,8},... | collective-permute-start | bytes 442376 | tf_op jit(solution)/shard_map/ppermute | solution.py:19
  105.1 21.2 %copy-start.13 = (bf16[192,384]{1,0:T(8,128)(2,1)}, bf16[192,384]{1,0:T(8,128)(2,1)S(1)}, u32[]{:S(2)}) copy-start(bf16[192,384]{1,0:T(8,128)(2,1)S(1)} %get-tuple-element.83.refs_0_) | copy-start | bytes 442372
  107.1 20.2 %collective-permute-start.14 = (bf16[192,384]{1,0:T(8,128)(2,1)S(1)}, bf16[192,384]{1,0:T(8,128)(2,1)S(1)}, u32[]{:S(2)}, u32[]{:S(2)}) collective-permute-start(bf16[192,384]{1,0:T(8,128)(2,1)S(1)} %get-tuple-element.90), channel_id=1, source_target_pairs={{0,8},{2,10},{4,12},{6,14},{8,0},{10,2},{12,4},{14,6},{16,24},{18,... | collective-permute-start | bytes 442376 | tf_op jit(solution)/shard_map/ppermute | solution.py:19
  107.9 22.8 %collective-permute-start.17 = (bf16[192,384]{1,0:T(8,128)(2,1)S(1)}, bf16[192,384]{1,0:T(8,128)(2,1)S(1)}, u32[]{:S(2)}, u32[]{:S(2)}) collective-permute-start(bf16[192,384]{1,0:T(8,128)(2,1)S(1)} %get-tuple-element.96), channel_id=1, source_target_pairs={{0,16},{2,18},{4,20},{6,22},{8,24},{10,26},{12,28},{14,30},{16,0},... | collective-permute-start | bytes 442376 | tf_op jit(solution)/shard_map/ppermute | solution.py:19
  109.9 20.9 %collective-permute-start.20 = (bf16[192,384]{1,0:T(8,128)(2,1)S(1)}, bf16[192,384]{1,0:T(8,128)(2,1)S(1)}, u32[]{:S(2)}, u32[]{:S(2)}) collective-permute-start(bf16[192,384]{1,0:T(8,128)(2,1)S(1)} %get-tuple-element.102), channel_id=1, source_target_pairs={{0,24},{2,26},{4,28},{6,30},{8,16},{10,18},{12,20},{14,22},{16,8},... | collective-permute-start | bytes 442376 | tf_op jit(solution)/shard_map/ppermute | solution.py:19
  126.3 19.4 %collective-permute-start.28 = (bf16[192,384]{1,0:T(8,128)(2,1)}, bf16[192,384]{1,0:T(8,128)(2,1)S(1)}, u32[]{:S(2)}, u32[]{:S(2)}) collective-permute-start(bf16[192,384]{1,0:T(8,128)(2,1)} %get-tuple-element.109), channel_id=1, source_target_pairs={{0,24},{2,26},{4,28},{6,30},{8,16},{10,18},{12,20},{14,22},{16,8},... | collective-permute-start | bytes 442376 | tf_op jit(solution)/shard_map/ppermute | solution.py:19
  127.2 18.5 %collective-permute-start.29 = (bf16[192,384]{1,0:T(8,128)(2,1)}, bf16[192,384]{1,0:T(8,128)(2,1)S(1)}, u32[]{:S(2)}, u32[]{:S(2)}) collective-permute-start(bf16[192,384]{1,0:T(8,128)(2,1)} %get-tuple-element.110), channel_id=1, source_target_pairs={{0,16},{2,18},{4,20},{6,22},{8,24},{10,26},{12,28},{14,30},{16,0},... | collective-permute-start | bytes 442376 | tf_op jit(solution)/shard_map/ppermute | solution.py:19
  127.2 21.5 %copy-start.9 = (bf16[192,384]{1,0:T(8,128)(2,1)S(1)}, bf16[192,384]{1,0:T(8,128)(2,1)}, u32[]{:S(2)}) copy-start(bf16[192,384]{1,0:T(8,128)(2,1)} %get-tuple-element.112.refs_3_) | copy-start | bytes 442372
  127.3 21.4 %collective-permute-start.30 = (bf16[192,384]{1,0:T(8,128)(2,1)}, bf16[192,384]{1,0:T(8,128)(2,1)S(1)}, u32[]{:S(2)}, u32[]{:S(2)}) collective-permute-start(bf16[192,384]{1,0:T(8,128)(2,1)} %get-tuple-element.111), channel_id=1, source_target_pairs={{0,8},{2,10},{4,12},{6,14},{8,0},{10,2},{12,4},{14,6},{16,24},{18,... | collective-permute-start | bytes 442376 | tf_op jit(solution)/shard_map/ppermute | solution.py:19
  144.4 8.2 %collective-permute-start.24 = (bf16[192,384]{1,0:T(8,128)(2,1)}, bf16[192,384]{1,0:T(8,128)(2,1)S(1)}, u32[]{:S(2)}, u32[]{:S(2)}) collective-permute-start(bf16[192,384]{1,0:T(8,128)(2,1)} %get-tuple-element.105), channel_id=1, source_target_pairs={{0,26},{2,24},{4,30},{6,28},{8,18},{10,16},{12,22},{14,20},{16,10}... | collective-permute-start | bytes 442376 | tf_op jit(solution)/shard_map/ppermute | solution.py:19
  144.5 14.5 %collective-permute-start.25 = (bf16[192,384]{1,0:T(8,128)(2,1)}, bf16[192,384]{1,0:T(8,128)(2,1)S(1)}, u32[]{:S(2)}, u32[]{:S(2)}) collective-permute-start(bf16[192,384]{1,0:T(8,128)(2,1)} %get-tuple-element.106), channel_id=1, source_target_pairs={{0,18},{2,16},{4,22},{6,20},{8,26},{10,24},{12,30},{14,28},{16,2},... | collective-permute-start | bytes 442376 | tf_op jit(solution)/shard_map/ppermute | solution.py:19
  145.7 13.2 %collective-permute-start.26 = (bf16[192,384]{1,0:T(8,128)(2,1)}, bf16[192,384]{1,0:T(8,128)(2,1)S(1)}, u32[]{:S(2)}, u32[]{:S(2)}) collective-permute-start(bf16[192,384]{1,0:T(8,128)(2,1)} %get-tuple-element.107), channel_id=1, source_target_pairs={{0,10},{2,8},{4,14},{6,12},{8,2},{10,0},{12,6},{14,4},{16,26},{18,... | collective-permute-start | bytes 442376 | tf_op jit(solution)/shard_map/ppermute | solution.py:19
  145.7 13.2 %collective-permute-start.27 = (bf16[192,384]{1,0:T(8,128)(2,1)}, bf16[192,384]{1,0:T(8,128)(2,1)S(1)}, u32[]{:S(2)}, u32[]{:S(2)}) collective-permute-start(bf16[192,384]{1,0:T(8,128)(2,1)} %get-tuple-element.108), channel_id=1, source_target_pairs={{0,2},{2,0},{4,6},{6,4},{8,10},{10,8},{12,14},{14,12},{16,18},{18,... | collective-permute-start | bytes 442376 | tf_op jit(solution)/shard_map/ppermute | solution.py:19
  (11 other events, 37.9 us)

commit v17 on v15

--- a/solution.py
+++ b/solution.py
@@ -391,7 +391,7 @@
     span_other = over_ctx(lax.dynamic_index_in_dim(spans, 1 - core, 0), 1)
     later = jnp.concatenate([place, lax.dynamic_index_in_dim(spans, core, 0), span_other])
     made_0 = {}
-    for part in (away[::-2], away[-2::-2]):
+    for part in (away[: ways // 2 - 1 : -1] or away, away[: ways // 2][::-1] if ways > 1 else []):
         if part:
             made_0.update(
                 rest_products(received, [0], [w_k, w_v], [start_k, start_v], later, ways, part, EXTRA)[0]
@@ -420,7 +420,7 @@
     for a in range(1, ways - 1):
         before.append(over_ctx(first[a], rest // 2))
         blocks[a * rest + rest // 2] = before[-1]
-    received, _ = lax.optimization_barrier((received, before[:1]))
+    received, _ = lax.optimization_barrier((received, before[-1:]))
     asked += rest_products(received, [1], [w_q], [start_q], place, ways, away)
     if ways > 1:
         value, _ = lax.optimization_barrier((first[ways - 1], (before, asked[1])))
@@ -438,7 +438,7 @@
         value, _ = lax.optimization_barrier((asked[0][a], wait))
         queries[0][a] = over_ctx(value, a * rest)
     for a in away:
-        value, _ = lax.optimization_barrier((asked[1][a], queries[0][min(1, ways - 1)]))
+        value, _ = lax.optimization_barrier((asked[1][a], queries[0][a]))
         queries[1][a] = over_ctx(value, a * rest)
     table = span_table({i: (array, 0) for i, array in blocks.items()}, rows)
     second[rest // 2 + 1] = ahead_1

time: 164 us -> 162 us (0.988)
  waiting for transfers between devices: 33.3 us -> 29.5 us
  starting transfers between devices: 42.5 us -> 45 us
    ppermute x31, waiting for transfers between devices: 33.3 us -> 29.5 us  [exchange(): return lax.ppermute(value, axis, [(i, i ^ bit) for i in range(size)])]
    ppermute x31, starting transfers between devices: 42.5 us -> 45 us  [exchange(): return lax.ppermute(value, axis, [(i, i ^ bit) for i in range(size)])]
    unnamed x58 -> x56, local copies, waits for them, and re-layouts: 3.23 us -> 3.3 us
  transfers between devices with their start and end apart: 31 -> 31, of which waited for: 10 -> 9; matrix products, arithmetic and copies ran while one was open for 1% -> 1% of each run, Pallas kernels for 47% -> 47%
where the time goes in v17:
time: 162 us
  Pallas kernels  78.4 us (48%)
  starting transfers between devices  45 us (28%)
  waiting for transfers between devices  29.5 us (18%)
  local copies, waits for them, and re-layouts  8.35 us (5%)
    ppermute x31, starting transfers between devices, exchange(): return lax.ppermute(value, axis, [(i, i ^ bit) for i in range(size)])  45 us
    pallas_call x5, Pallas kernels, rest_products(): pl.pallas_call(functools.partial(rest_body, shares, len(weights), chunks,...  31.7 us
    ppermute x31, waiting for transfers between devices, exchange(): return lax.ppermute(value, axis, [(i, i ^ bit) for i in range(size)])  29.5 us
    pallas_call x2, Pallas kernels, attend(): pl.pallas_call(functools.partial(attend_body, block, ways, slots, len(arr...  24.3 us
    pallas_call x1, Pallas kernels, own_products(): pl.pallas_call(functools.partial(own_body, len(weights)), out_shape=[jax....  17.7 us
    pallas_call x2, Pallas kernels, assemble(): pl.pallas_call(functools.partial(assemble_body, ways), out_shape=jax.Shap...  3.99 us
    unnamed x56, local copies, waits for them, and re-layouts  3.3 us
  transfers between devices with their start and end apart: 31, of which 9 were waited for; matrix products, arithmetic and copies ran while one was open for 1% of the time, Pallas kernels for 47%

profile of v17, /device:TPU:0, one launch (start us, length us, event | category | flops | bytes accessed | tf_op | source)
XLA Modules:
  0.0 162.0 jit_solution(4080224729964585982)
XLA Ops:
  0.0 3.0 %dynamic-slice_bitcast_fusion = (bf16[192,2560]{1,0:T(8,128)(2,1)}, bf16[192,2560]{1,0:T(8,128)(2,1)}) fusion(bf16[2,192,2560]{2,1,0:T(8,128)(2,1)} %mine_ref.1, s32[]{:T(128)S(6)} %select_n.30, s32[]{:T(128)S(6)} %select_n.29), kind=kLoop, calls=%fused_computation | loop fusion | bytes 3932168 | tf_op jit(solution)/shard_map/jit(dynamic_index_in_dim)/squeeze | solution.py:385
  3.5 2.5 %collective-permute-start.1 = (bf16[192,2560]{1,0:T(8,128)(2,1)}, bf16[192,2560]{1,0:T(8,128)(2,1)S(1)}, u32[]{:S(2)}, u32[]{:S(2)}) collective-permute-start(bf16[192,2560]{1,0:T(8,128)(2,1)} %get-tuple-element.112), channel_id=1, source_target_pairs={{0,1},{1,0},{2,3},{3,2},{4,5},{5,4},{6,7},{7,6},{8,9},{9,8},{10,11... | collective-permute-start | bytes 2949128 | tf_op jit(solution)/shard_map/ppermute | solution.py:19
  6.3 0.7 fusion
  7.2 0.9 collective-permute-done
  8.1 1.3 concatenate.4.place
  9.4 0.9 collective-permute-start.3
  10.3 17.7 %shard_map.55 = (f32[2,192,1536]{2,1,0:T(8,128)S(1)}, f32[2,192,1536]{2,1,0:T(8,128)S(1)}, f32[2,192,1536]{2,1,0:T(8,128)S(1)}) custom-call(s32[4]{0:T(128)S(1)} %pad_add_fusion.place, bf16[2,192,2560]{2,1,0:T(8,128)(2,1)S(1)} %copy-done, bf16[192,2560]{1,0:T(8,128)(2,1)} %collective-permute-done.2.other_ref, bf16[5120,1536]{1,0:T(8,128)(2,1)} %refs_1_.10, ...), custom_call_target="tpu_custom_call" | custom-call | flops 9059696640 | bytes 23592960 | tf_op jit(solution)/shard_map/pallas_call | solution.py:43
  27.9 0.9 collective-permute-done.1.refs_0_
  28.8 5.2 %shard_map.59 = (bf16[208,768]{1,0:T(8,128)(2,1)S(1)}, bf16[208,768]{1,0:T(8,128)(2,1)S(1)}) custom-call(s32[6]{0:T(128)S(1)} %concatenate.4.place, bf16[192,2560]{1,0:T(8,128)(2,1)S(1)} %collective-permute-done.1.refs_0_, bf16[5120,1536]{1,0:T(8,128)(2,1)} %refs_1_.10, bf16[5120,1536]{1,0:T(8,128)(2,1)} %refs_2_.7, ...), custom_call_target="tpu_custom_call" | custom-call | flops 1509949440 | bytes 7864320 | tf_op jit(solution)/shard_map/pallas_call | solution.py:129
  34.1 3.1 %collective-permute-start.7 = (bf16[208,768]{1,0:T(8,128)(2,1)S(1)}, bf16[208,768]{1,0:T(8,128)(2,1)S(1)}, u32[]{:S(2)}, u32[]{:S(2)}) collective-permute-start(bf16[208,768]{1,0:T(8,128)(2,1)S(1)} %get-tuple-element.72), channel_id=1, source_target_pairs={{0,16},{2,18},{4,20},{6,22},{8,24},{10,26},{12,28},{14,30},{16,0},... | collective-permute-start | bytes 958472 | tf_op jit(solution)/shard_map/ppermute | solution.py:19
  37.2 1.3 collective-permute-start.9
  38.5 5.2 %shard_map.56 = (bf16[208,768]{1,0:T(8,128)(2,1)S(1)}, bf16[208,768]{1,0:T(8,128)(2,1)S(1)}) custom-call(s32[6]{0:T(128)S(1)} %concatenate.4.place, bf16[192,2560]{1,0:T(8,128)(2,1)S(1)} %collective-permute-done.1.refs_0_, bf16[5120,1536]{1,0:T(8,128)(2,1)} %refs_1_.10, bf16[5120,1536]{1,0:T(8,128)(2,1)} %refs_2_.7, ...), custom_call_target="tpu_custom_call" | custom-call | flops 1509949440 | bytes 7864320 | tf_op jit(solution)/shard_map/pallas_call | solution.py:129
  44.1 1.5 collective-permute-start.4
  45.6 6.0 %shard_map.57 = (bf16[192,384]{1,0:T(8,128)(2,1)S(1)}, bf16[192,384]{1,0:T(8,128)(2,1)S(1)}, bf16[192,384]{1,0:T(8,128)(2,1)S(1)}, bf16[192,384]{1,0:T(8,128)(2,1)S(1)}) custom-call(s32[4]{0:T(128)S(1)} %pad_add_fusion.place, bf16[192,2560]{1,0:T(8,128)(2,1)S(1)} %collective-permute-done.1.refs_0_, bf16[5120,1536]{1,0:T(8,128)(2,1)} %refs_1_.11, ...), custom_call_target="tpu_custom_call" | custom-call | flops 1509949440 | bytes 7864320 | tf_op jit(solution)/shard_map/pallas_call | solution.py:129
  51.6 9.1 %shard_map.58 = (bf16[192,768]{1,0:T(8,128)(2,1)S(1)}, bf16[192,768]{1,0:T(8,128)(2,1)S(1)}, bf16[192,768]{1,0:T(8,128)(2,1)S(1)}, bf16[192,768]{1,0:T(8,128)(2,1)S(1)}) custom-call(s32[4]{0:T(128)S(1)} %pad_add_fusion.place, bf16[192,2560]{1,0:T(8,128)(2,1)S(1)} %collective-permute-done.3.refs_0_, bf16[5120,1536]{1,0:T(8,128)(2,1)} %refs_1_.10, ...), custom_call_target="tpu_custom_call" | custom-call | flops 3019898880 | bytes 15728640 | tf_op jit(solution)/shard_map/pallas_call | solution.py:129
  60.7 0.6 collective-permute-start.8
  61.3 2.6 %collective-permute-done.5.refs_2_.refs_8_ = bf16[208,768]{1,0:T(8,128)(2,1)S(1)} collective-permute-done((bf16[208,768]{1,0:T(8,128)(2,1)S(1)}, bf16[208,768]{1,0:T(8,128)(2,1)S(1)}, u32[]{:S(2)}, u32[]{:S(2)}) %collective-permute-start.5) | collective-permute-done | bytes 319520 | tf_op jit(solution)/shard_map/ppermute | solution.py:19
  63.9 1.6 collective-permute-start.6
  66.0 4.1 %collective-permute-start.15 = (bf16[192,768]{1,0:T(8,128)(2,1)S(1)}, bf16[192,768]{1,0:T(8,128)(2,1)S(1)}, u32[]{:S(2)}, u32[]{:S(2)}) collective-permute-start(bf16[192,768]{1,0:T(8,128)(2,1)S(1)} %get-tuple-element.93), channel_id=1, source_target_pairs={{0,16},{2,18},{4,20},{6,22},{8,24},{10,26},{12,28},{14,30},{16,0},... | collective-permute-start | bytes 884744 | tf_op jit(solution)/shard_map/ppermute | solution.py:19
  70.1 1.2 collective-permute-done.8.refs_5_.refs_14_
  71.3 2.9 %collective-permute-start.18 = (bf16[192,768]{1,0:T(8,128)(2,1)S(1)}, bf16[192,768]{1,0:T(8,128)(2,1)S(1)}, u32[]{:S(2)}, u32[]{:S(2)}) collective-permute-start(bf16[192,768]{1,0:T(8,128)(2,1)S(1)} %get-tuple-element.98), channel_id=1, source_target_pairs={{0,24},{2,26},{4,28},{6,30},{8,16},{10,18},{12,20},{14,22},{16,8},... | collective-permute-start | bytes 884744 | tf_op jit(solution)/shard_map/ppermute | solution.py:19
  74.2 6.2 %shard_map.60 = (bf16[192,384]{1,0:T(8,128)(2,1)S(1)}, bf16[192,384]{1,0:T(8,128)(2,1)S(1)}, bf16[192,384]{1,0:T(8,128)(2,1)S(1)}, bf16[192,384]{1,0:T(8,128)(2,1)S(1)}) custom-call(s32[4]{0:T(128)S(1)} %pad_add_fusion.place, bf16[192,2560]{1,0:T(8,128)(2,1)S(1)} %collective-permute-done.3.refs_0_, bf16[5120,1536]{1,0:T(8,128)(2,1)} %refs_1_.11, ...), custom_call_target="tpu_custom_call" | custom-call | flops 1509949440 | bytes 7864320 | tf_op jit(solution)/shard_map/pallas_call | solution.py:129
  80.4 0.6 collective-permute-start.10
  81.0 3.4 %collective-permute-done.12.refs_7_ = bf16[192,768]{1,0:T(8,128)(2,1)S(1)} collective-permute-done((bf16[192,768]{1,0:T(8,128)(2,1)S(1)}, bf16[192,768]{1,0:T(8,128)(2,1)S(1)}, u32[]{:S(2)}, u32[]{:S(2)}) %collective-permute-start.12) | collective-permute-done | bytes 294944 | tf_op jit(solution)/shard_map/ppermute | solution.py:19
  84.4 1.8 %collective-permute-start.13 = (bf16[192,384]{1,0:T(8,128)(2,1)S(1)}, bf16[192,384]{1,0:T(8,128)(2,1)S(1)}, u32[]{:S(2)}, u32[]{:S(2)}) collective-permute-start(bf16[192,384]{1,0:T(8,128)(2,1)S(1)} %get-tuple-element.89), channel_id=1, source_target_pairs={{0,8},{2,10},{4,12},{6,14},{8,0},{10,2},{12,4},{14,6},{16,24},{18,... | collective-permute-start | bytes 442376 | tf_op jit(solution)/shard_map/ppermute | solution.py:19
  86.3 0.5 collective-permute-start.21
  86.8 3.9 %collective-permute-done.15.refs_13_ = bf16[192,768]{1,0:T(8,128)(2,1)S(1)} collective-permute-done((bf16[192,768]{1,0:T(8,128)(2,1)S(1)}, bf16[192,768]{1,0:T(8,128)(2,1)S(1)}, u32[]{:S(2)}, u32[]{:S(2)}) %collective-permute-start.15) | collective-permute-done | bytes 294944 | tf_op jit(solution)/shard_map/ppermute | solution.py:19
  90.7 1.5 collective-permute-start.22
  92.7 6.5 %collective-permute-start.16 = (bf16[192,384]{1,0:T(8,128)(2,1)S(1)}, bf16[192,384]{1,0:T(8,128)(2,1)S(1)}, u32[]{:S(2)}, u32[]{:S(2)}) collective-permute-start(bf16[192,384]{1,0:T(8,128)(2,1)S(1)} %get-tuple-element.94), channel_id=1, source_target_pairs={{0,16},{2,18},{4,20},{6,22},{8,24},{10,26},{12,28},{14,30},{16,0},... | collective-permute-start | bytes 442376 | tf_op jit(solution)/shard_map/ppermute | solution.py:19
  99.7 8.4 %collective-permute-done.16.refs_2_ = bf16[192,384]{1,0:T(8,128)(2,1)S(1)} collective-permute-done((bf16[192,384]{1,0:T(8,128)(2,1)S(1)}, bf16[192,384]{1,0:T(8,128)(2,1)S(1)}, u32[]{:S(2)}, u32[]{:S(2)}) %collective-permute-start.16) | collective-permute-done | bytes 147488 | tf_op jit(solution)/shard_map/ppermute | solution.py:19
  108.1 0.8 shard_map.61.table
  108.9 0.6 copy-done.10
  109.5 1.0 collective-permute-start.17
  110.5 3.4 %collective-permute-start.20 = (bf16[192,384]{1,0:T(8,128)(2,1)S(1)}, bf16[192,384]{1,0:T(8,128)(2,1)S(1)}, u32[]{:S(2)}, u32[]{:S(2)}) collective-permute-start(bf16[192,384]{1,0:T(8,128)(2,1)S(1)} %get-tuple-element.100), channel_id=1, source_target_pairs={{0,24},{2,26},{4,28},{6,30},{8,16},{10,18},{12,20},{14,22},{16,8},... | collective-permute-start | bytes 442376 | tf_op jit(solution)/shard_map/ppermute | solution.py:19
  114.0 0.6 copy-done.19
  114.6 0.7 copy-done.20
  115.3 12.0 %shard_map.63 = (bf16[192,384]{1,0:T(8,128)(2,1)}, bf16[192,384]{1,0:T(8,128)(2,1)}, bf16[192,384]{1,0:T(8,128)(2,1)}, bf16[192,384]{1,0:T(8,128)(2,1)}) custom-call(s32[16]{0:T(128)} %copy-done.10, bf16[192,384]{1,0:T(8,128)(2,1)} %copy-done.12, bf16[192,384]{1,0:T(8,128)(2,1)} %copy-done.22, bf16[192,384]{1,0:T(8,128)(2,1)} %copy-done.25, ...), custom_call_target="tpu_custom_call" | custom-call | flops 2717908992 | bytes 5898240 | tf_op jit(solution)/shard_map/pallas_call | solution.py:280
  127.3 0.5 collective-permute-start.28
  128.0 3.8 %collective-permute-start.30 = (bf16[192,384]{1,0:T(8,128)(2,1)}, bf16[192,384]{1,0:T(8,128)(2,1)S(1)}, u32[]{:S(2)}, u32[]{:S(2)}) collective-permute-start(bf16[192,384]{1,0:T(8,128)(2,1)} %get-tuple-element.109), channel_id=1, source_target_pairs={{0,8},{2,10},{4,12},{6,14},{8,0},{10,2},{12,4},{14,6},{16,24},{18,... | collective-permute-start | bytes 442376 | tf_op jit(solution)/shard_map/ppermute | solution.py:19
  131.8 0.7 copy-done.23
  132.5 0.7 copy-done.24
  133.1 12.3 %shard_map.62 = (bf16[192,384]{1,0:T(8,128)(2,1)}, bf16[192,384]{1,0:T(8,128)(2,1)}, bf16[192,384]{1,0:T(8,128)(2,1)}, bf16[192,384]{1,0:T(8,128)(2,1)}) custom-call(s32[16]{0:T(128)} %copy-done.10, bf16[192,384]{1,0:T(8,128)(2,1)} %copy-done.13, bf16[192,384]{1,0:T(8,128)(2,1)} %copy-done.21, bf16[192,384]{1,0:T(8,128)(2,1)} %copy-done.23, ...), custom_call_target="tpu_custom_call" | custom-call | flops 2717908992 | bytes 5898240 | tf_op jit(solution)/shard_map/pallas_call | solution.py:280
  145.5 1.2 collective-permute-start.25
  146.7 3.0 %collective-permute-start.27 = (bf16[192,384]{1,0:T(8,128)(2,1)}, bf16[192,384]{1,0:T(8,128)(2,1)S(1)}, u32[]{:S(2)}, u32[]{:S(2)}) collective-permute-start(bf16[192,384]{1,0:T(8,128)(2,1)} %get-tuple-element.106), channel_id=1, source_target_pairs={{0,2},{2,0},{4,6},{6,4},{8,10},{10,8},{12,14},{14,12},{16,18},{18,... | collective-permute-start | bytes 442376 | tf_op jit(solution)/shard_map/ppermute | solution.py:19
  149.7 2.0 %shard_map.64.refs_4_ = bf16[2,192,1536]{2,1,0:T(8,128)(2,1)} custom-call(s32[4]{0:T(128)S(1)} %pad_add_fusion.place, bf16[192,384]{1,0:T(8,128)(2,1)S(1)} %collective-permute-done.28.refs_0_, bf16[192,384]{1,0:T(8,128)(2,1)S(1)} %collective-permute-done.29.refs_1_, bf16[192,384]{1,0:T(8,128)(2,1)S(1)} %collective-permute-done.30.refs_2_, ...), custom_call_target="tpu_custom_call" | custom-call | tf_op jit(solution)/shard_map/pallas_call | solution.py:348
  151.7 1.9 %collective-permute-done.24.refs_0_ = bf16[192,384]{1,0:T(8,128)(2,1)S(1)} collective-permute-done((bf16[192,384]{1,0:T(8,128)(2,1)}, bf16[192,384]{1,0:T(8,128)(2,1)S(1)}, u32[]{:S(2)}, u32[]{:S(2)}) %collective-permute-start.24) | collective-permute-done | bytes 147488 | tf_op jit(solution)/shard_map/ppermute | solution.py:19
  153.6 6.3 %collective-permute-done.25.refs_1_ = bf16[192,384]{1,0:T(8,128)(2,1)S(1)} collective-permute-done((bf16[192,384]{1,0:T(8,128)(2,1)}, bf16[192,384]{1,0:T(8,128)(2,1)S(1)}, u32[]{:S(2)}, u32[]{:S(2)}) %collective-permute-start.25) | collective-permute-done | bytes 147488 | tf_op jit(solution)/shard_map/ppermute | solution.py:19
  160.0 2.0 %shard_map.65 = bf16[2,192,1536]{2,1,0:T(8,128)(2,1)} custom-call(s32[4]{0:T(128)S(1)} %pad_add_fusion.place, bf16[192,384]{1,0:T(8,128)(2,1)S(1)} %collective-permute-done.24.refs_0_, bf16[192,384]{1,0:T(8,128)(2,1)S(1)} %collective-permute-done.25.refs_1_, bf16[192,384]{1,0:T(8,128)(2,1)S(1)} %collective-permute-done.26.refs_2_, ...), custom_call_target="tpu_custom_call", output_to_operand_aliasing={{}: (5, {})} | custom-call | tf_op jit(solution)/shard_map/pallas_call | solution.py:348
  (88 shorter events, 3.2 us)
Async XLA Ops:
  0.0 10.3 %copy-start = (bf16[2,192,2560]{2,1,0:T(8,128)(2,1)S(1)}, bf16[2,192,2560]{2,1,0:T(8,128)(2,1)}, u32[]{:S(2)}) copy-start(bf16[2,192,2560]{2,1,0:T(8,128)(2,1)} %mine_ref.1) | copy-start | bytes 5898244
  3.1 6.4 %collective-permute-start.2 = (bf16[192,2560]{1,0:T(8,128)(2,1)}, bf16[192,2560]{1,0:T(8,128)(2,1)}, u32[]{:S(2)}, u32[]{:S(2)}) collective-permute-start(bf16[192,2560]{1,0:T(8,128)(2,1)} %get-tuple-element.111), channel_id=1, source_target_pairs={{0,2},{2,0},{4,6},{6,4},{8,10},{10,8},{12,14},{14,12},{16,18},{18,... | collective-permute-start | bytes 2949128 | tf_op jit(solution)/shard_map/ppermute | solution.py:19
  3.5 25.3 %collective-permute-start.1 = (bf16[192,2560]{1,0:T(8,128)(2,1)}, bf16[192,2560]{1,0:T(8,128)(2,1)S(1)}, u32[]{:S(2)}, u32[]{:S(2)}) collective-permute-start(bf16[192,2560]{1,0:T(8,128)(2,1)} %get-tuple-element.112), channel_id=1, source_target_pairs={{0,1},{1,0},{2,3},{3,2},{4,5},{5,4},{6,7},{7,6},{8,9},{9,8},{10,11... | collective-permute-start | bytes 2949128 | tf_op jit(solution)/shard_map/ppermute | solution.py:19
  6.9 1.2 collective-permute-start
  9.4 42.2 %collective-permute-start.3 = (bf16[192,2560]{1,0:T(8,128)(2,1)}, bf16[192,2560]{1,0:T(8,128)(2,1)S(1)}, u32[]{:S(2)}, u32[]{:S(2)}) collective-permute-start(bf16[192,2560]{1,0:T(8,128)(2,1)} %collective-permute-done.2.other_ref), channel_id=1, source_target_pairs={{0,1},{1,0},{2,3},{3,2},{4,5},{5,4},{6,7},{7,6},{8,9},{9,8},{10,11... | collective-permute-start | bytes 2949128 | tf_op jit(solution)/shard_map/ppermute | solution.py:19
  34.1 26.6 %collective-permute-start.7 = (bf16[208,768]{1,0:T(8,128)(2,1)S(1)}, bf16[208,768]{1,0:T(8,128)(2,1)S(1)}, u32[]{:S(2)}, u32[]{:S(2)}) collective-permute-start(bf16[208,768]{1,0:T(8,128)(2,1)S(1)} %get-tuple-element.72), channel_id=1, source_target_pairs={{0,16},{2,18},{4,20},{6,22},{8,24},{10,26},{12,28},{14,30},{16,0},... | collective-permute-start | bytes 958472 | tf_op jit(solution)/shard_map/ppermute | solution.py:19
  37.2 28.7 %collective-permute-start.9 = (bf16[208,768]{1,0:T(8,128)(2,1)S(1)}, bf16[208,768]{1,0:T(8,128)(2,1)S(1)}, u32[]{:S(2)}, u32[]{:S(2)}) collective-permute-start(bf16[208,768]{1,0:T(8,128)(2,1)S(1)} %get-tuple-element.75), channel_id=1, source_target_pairs={{0,24},{2,26},{4,28},{6,30},{8,16},{10,18},{12,20},{14,22},{16,8},... | collective-permute-start | bytes 958472 | tf_op jit(solution)/shard_map/ppermute | solution.py:19
  43.8 64.3 %copy-start.3 = (bf16[208,768]{1,0:T(8,128)(2,1)}, bf16[208,768]{1,0:T(8,128)(2,1)S(1)}, u32[]{:S(2)}) copy-start(bf16[208,768]{1,0:T(8,128)(2,1)S(1)} %get-tuple-element.68.refs_0_.refs_4_) | copy-start | bytes 958468
  43.8 20.1 %collective-permute-start.5 = (bf16[208,768]{1,0:T(8,128)(2,1)S(1)}, bf16[208,768]{1,0:T(8,128)(2,1)S(1)}, u32[]{:S(2)}, u32[]{:S(2)}) collective-permute-start(bf16[208,768]{1,0:T(8,128)(2,1)S(1)} %get-tuple-element.69), channel_id=1, source_target_pairs={{0,8},{2,10},{4,12},{6,14},{8,0},{10,2},{12,4},{14,6},{16,24},{18,... | collective-permute-start | bytes 958472 | tf_op jit(solution)/shard_map/ppermute | solution.py:19
  44.1 21.8 %collective-permute-start.4 = (bf16[208,768]{1,0:T(8,128)(2,1)S(1)}, bf16[208,768]{1,0:T(8,128)(2,1)S(1)}, u32[]{:S(2)}, u32[]{:S(2)}) collective-permute-start(bf16[208,768]{1,0:T(8,128)(2,1)S(1)} %get-tuple-element.68.refs_0_.refs_4_), channel_id=1, source_target_pairs={{0,4},{2,6},{4,0},{6,2},{8,12},{10,14},{12,8},{14,10},{16,20},{18,... | collective-permute-start | bytes 958472 | tf_op jit(solution)/shard_map/ppermute | solution.py:19
  60.7 19.7 %copy-start.11 = (bf16[192,768]{1,0:T(8,128)(2,1)}, bf16[192,768]{1,0:T(8,128)(2,1)S(1)}, u32[]{:S(2)}) copy-start(bf16[192,768]{1,0:T(8,128)(2,1)S(1)} %get-tuple-element.102.refs_5_) | copy-start | bytes 884740
  60.7 47.4 %copy-start.1 = (bf16[208,768]{1,0:T(8,128)(2,1)}, bf16[208,768]{1,0:T(8,128)(2,1)S(1)}, u32[]{:S(2)}) copy-start(bf16[208,768]{1,0:T(8,128)(2,1)S(1)} %collective-permute-done.7.refs_4_.refs_12_) | copy-start | bytes 958468
  60.7 10.5 %collective-permute-start.8 = (bf16[208,768]{1,0:T(8,128)(2,1)S(1)}, bf16[208,768]{1,0:T(8,128)(2,1)S(1)}, u32[]{:S(2)}, u32[]{:S(2)}) collective-permute-start(bf16[208,768]{1,0:T(8,128)(2,1)S(1)} %collective-permute-done.7.refs_4_.refs_12_), channel_id=1, source_target_pairs={{0,4},{2,6},{4,0},{6,2},{8,12},{10,14},{12,8},{14,10},{16,20},{18,... | collective-permute-start | bytes 958472 | tf_op jit(solution)/shard_map/ppermute | solution.py:19
  63.9 44.2 %copy-start.4 = (bf16[208,768]{1,0:T(8,128)(2,1)}, bf16[208,768]{1,0:T(8,128)(2,1)S(1)}, u32[]{:S(2)}) copy-start(bf16[208,768]{1,0:T(8,128)(2,1)S(1)} %collective-permute-done.5.refs_2_.refs_8_) | copy-start | bytes 958468
  63.9 16.5 %collective-permute-start.6 = (bf16[208,768]{1,0:T(8,128)(2,1)S(1)}, bf16[208,768]{1,0:T(8,128)(2,1)S(1)}, u32[]{:S(2)}, u32[]{:S(2)}) collective-permute-start(bf16[208,768]{1,0:T(8,128)(2,1)S(1)} %collective-permute-done.5.refs_2_.refs_8_), channel_id=1, source_target_pairs={{0,4},{2,6},{4,0},{6,2},{8,12},{10,14},{12,8},{14,10},{16,20},{18,... | collective-permute-start | bytes 958472 | tf_op jit(solution)/shard_map/ppermute | solution.py:19
  65.4 19.0 %collective-permute-start.12 = (bf16[192,768]{1,0:T(8,128)(2,1)S(1)}, bf16[192,768]{1,0:T(8,128)(2,1)S(1)}, u32[]{:S(2)}, u32[]{:S(2)}) collective-permute-start(bf16[192,768]{1,0:T(8,128)(2,1)S(1)} %get-tuple-element.102.refs_5_), channel_id=1, source_target_pairs={{0,4},{2,6},{4,0},{6,2},{8,12},{10,14},{12,8},{14,10},{16,20},{18,... | collective-permute-start | bytes 884744 | tf_op jit(solution)/shard_map/ppermute | solution.py:19
  65.9 42.2 %copy-start.2 = (bf16[208,768]{1,0:T(8,128)(2,1)}, bf16[208,768]{1,0:T(8,128)(2,1)S(1)}, u32[]{:S(2)}) copy-start(bf16[208,768]{1,0:T(8,128)(2,1)S(1)} %collective-permute-done.9.refs_6_.refs_16_) | copy-start | bytes 958468
  65.9 42.2 %copy-start.5 = (bf16[208,768]{1,0:T(8,128)(2,1)}, bf16[208,768]{1,0:T(8,128)(2,1)S(1)}, u32[]{:S(2)}) copy-start(bf16[208,768]{1,0:T(8,128)(2,1)S(1)} %collective-permute-done.4.refs_1_.refs_6_) | copy-start | bytes 958468
  65.9 18.5 %collective-permute-start.11 = (bf16[192,768]{1,0:T(8,128)(2,1)S(1)}, bf16[192,768]{1,0:T(8,128)(2,1)S(1)}, u32[]{:S(2)}, u32[]{:S(2)}) collective-permute-start(bf16[192,768]{1,0:T(8,128)(2,1)S(1)} %get-tuple-element.88), channel_id=1, source_target_pairs={{0,8},{2,10},{4,12},{6,14},{8,0},{10,2},{12,4},{14,6},{16,24},{18,... | collective-permute-start | bytes 884744 | tf_op jit(solution)/shard_map/ppermute | solution.py:19
  66.0 24.7 %collective-permute-start.15 = (bf16[192,768]{1,0:T(8,128)(2,1)S(1)}, bf16[192,768]{1,0:T(8,128)(2,1)S(1)}, u32[]{:S(2)}, u32[]{:S(2)}) collective-permute-start(bf16[192,768]{1,0:T(8,128)(2,1)S(1)} %get-tuple-element.93), channel_id=1, source_target_pairs={{0,16},{2,18},{4,20},{6,22},{8,24},{10,26},{12,28},{14,30},{16,0},... | collective-permute-start | bytes 884744 | tf_op jit(solution)/shard_map/ppermute | solution.py:19
  71.3 36.9 %copy-start.6 = (bf16[208,768]{1,0:T(8,128)(2,1)}, bf16[208,768]{1,0:T(8,128)(2,1)S(1)}, u32[]{:S(2)}) copy-start(bf16[208,768]{1,0:T(8,128)(2,1)S(1)} %collective-permute-done.8.refs_5_.refs_14_) | copy-start | bytes 958468
  71.3 20.9 %collective-permute-start.18 = (bf16[192,768]{1,0:T(8,128)(2,1)S(1)}, bf16[192,768]{1,0:T(8,128)(2,1)S(1)}, u32[]{:S(2)}, u32[]{:S(2)}) collective-permute-start(bf16[192,768]{1,0:T(8,128)(2,1)S(1)} %get-tuple-element.98), channel_id=1, source_target_pairs={{0,24},{2,26},{4,28},{6,30},{8,16},{10,18},{12,20},{14,22},{16,8},... | collective-permute-start | bytes 884744 | tf_op jit(solution)/shard_map/ppermute | solution.py:19
  80.4 46.9 %copy-start.13 = (bf16[192,384]{1,0:T(8,128)(2,1)}, bf16[192,384]{1,0:T(8,128)(2,1)S(1)}, u32[]{:S(2)}) copy-start(bf16[192,384]{1,0:T(8,128)(2,1)S(1)} %get-tuple-element.85.refs_0_) | copy-start | bytes 442372
  80.4 33.5 %copy-start.7 = (bf16[208,768]{1,0:T(8,128)(2,1)}, bf16[208,768]{1,0:T(8,128)(2,1)S(1)}, u32[]{:S(2)}) copy-start(bf16[208,768]{1,0:T(8,128)(2,1)S(1)} %collective-permute-done.6.refs_3_.refs_10_) | copy-start | bytes 958468
  80.4 12.3 %collective-permute-start.10 = (bf16[208,768]{1,0:T(8,128)(2,1)S(1)}, bf16[208,768]{1,0:T(8,128)(2,1)S(1)}, u32[]{:S(2)}, u32[]{:S(2)}) collective-permute-start(bf16[208,768]{1,0:T(8,128)(2,1)S(1)} %collective-permute-done.9.refs_6_.refs_16_), channel_id=1, source_target_pairs={{0,4},{2,6},{4,0},{6,2},{8,12},{10,14},{12,8},{14,10},{16,20},{18,... | collective-permute-start | bytes 958472 | tf_op jit(solution)/shard_map/ppermute | solution.py:19
  84.4 29.4 %copy-start.14 = (bf16[192,768]{1,0:T(8,128)(2,1)}, bf16[192,768]{1,0:T(8,128)(2,1)S(1)}, u32[]{:S(2)}) copy-start(bf16[192,768]{1,0:T(8,128)(2,1)S(1)} %collective-permute-done.12.refs_7_) | copy-start | bytes 884740
  84.4 29.5 %copy-start.15 = (bf16[192,768]{1,0:T(8,128)(2,1)}, bf16[192,768]{1,0:T(8,128)(2,1)S(1)}, u32[]{:S(2)}) copy-start(bf16[192,768]{1,0:T(8,128)(2,1)S(1)} %collective-permute-done.11.refs_9_) | copy-start | bytes 884740
  84.4 14.8 %collective-permute-start.13 = (bf16[192,384]{1,0:T(8,128)(2,1)S(1)}, bf16[192,384]{1,0:T(8,128)(2,1)S(1)}, u32[]{:S(2)}, u32[]{:S(2)}) collective-permute-start(bf16[192,384]{1,0:T(8,128)(2,1)S(1)} %get-tuple-element.89), channel_id=1, source_target_pairs={{0,8},{2,10},{4,12},{6,14},{8,0},{10,2},{12,4},{14,6},{16,24},{18,... | collective-permute-start | bytes 442376 | tf_op jit(solution)/shard_map/ppermute | solution.py:19
  86.3 24.2 %collective-permute-start.21 = (bf16[192,768]{1,0:T(8,128)(2,1)S(1)}, bf16[192,768]{1,0:T(8,128)(2,1)S(1)}, u32[]{:S(2)}, u32[]{:S(2)}) collective-permute-start(bf16[192,768]{1,0:T(8,128)(2,1)S(1)} %collective-permute-done.11.refs_9_), channel_id=1, source_target_pairs={{0,4},{2,6},{4,0},{6,2},{8,12},{10,14},{12,8},{14,10},{16,20},{18,... | collective-permute-start | bytes 884744 | tf_op jit(solution)/shard_map/ppermute | solution.py:19
  90.7 23.2 %copy-start.16 = (bf16[192,768]{1,0:T(8,128)(2,1)}, bf16[192,768]{1,0:T(8,128)(2,1)S(1)}, u32[]{:S(2)}) copy-start(bf16[192,768]{1,0:T(8,128)(2,1)S(1)} %collective-permute-done.15.refs_13_) | copy-start | bytes 884740
  90.7 23.2 %collective-permute-start.22 = (bf16[192,768]{1,0:T(8,128)(2,1)S(1)}, bf16[192,768]{1,0:T(8,128)(2,1)S(1)}, u32[]{:S(2)}, u32[]{:S(2)}) collective-permute-start(bf16[192,768]{1,0:T(8,128)(2,1)S(1)} %collective-permute-done.15.refs_13_), channel_id=1, source_target_pairs={{0,4},{2,6},{4,0},{6,2},{8,12},{10,14},{12,8},{14,10},{16,20},{18,... | collective-permute-start | bytes 884744 | tf_op jit(solution)/shard_map/ppermute | solution.py:19
  92.2 21.7 %copy-start.17 = (bf16[192,768]{1,0:T(8,128)(2,1)}, bf16[192,768]{1,0:T(8,128)(2,1)S(1)}, u32[]{:S(2)}) copy-start(bf16[192,768]{1,0:T(8,128)(2,1)S(1)} %collective-permute-done.18.refs_17_) | copy-start | bytes 884740
  92.2 21.7 %collective-permute-start.23 = (bf16[192,768]{1,0:T(8,128)(2,1)S(1)}, bf16[192,768]{1,0:T(8,128)(2,1)S(1)}, u32[]{:S(2)}, u32[]{:S(2)}) collective-permute-start(bf16[192,768]{1,0:T(8,128)(2,1)S(1)} %collective-permute-done.18.refs_17_), channel_id=1, source_target_pairs={{0,4},{2,6},{4,0},{6,2},{8,12},{10,14},{12,8},{14,10},{16,20},{18,... | collective-permute-start | bytes 884744 | tf_op jit(solution)/shard_map/ppermute | solution.py:19
  92.7 21.2 %copy-start.8 = (bf16[208,768]{1,0:T(8,128)(2,1)}, bf16[208,768]{1,0:T(8,128)(2,1)S(1)}, u32[]{:S(2)}) copy-start(bf16[208,768]{1,0:T(8,128)(2,1)S(1)} %collective-permute-done.10.refs_7_.refs_18_) | copy-start | bytes 958468
  92.7 15.4 %collective-permute-start.16 = (bf16[192,384]{1,0:T(8,128)(2,1)S(1)}, bf16[192,384]{1,0:T(8,128)(2,1)S(1)}, u32[]{:S(2)}, u32[]{:S(2)}) collective-permute-start(bf16[192,384]{1,0:T(8,128)(2,1)S(1)} %get-tuple-element.94), channel_id=1, source_target_pairs={{0,16},{2,18},{4,20},{6,22},{8,24},{10,26},{12,28},{14,30},{16,0},... | collective-permute-start | bytes 442376 | tf_op jit(solution)/shard_map/ppermute | solution.py:19
  99.2 14.7 %copy-start.22 = (bf16[192,384]{1,0:T(8,128)(2,1)}, bf16[192,384]{1,0:T(8,128)(2,1)S(1)}, u32[]{:S(2)}) copy-start(bf16[192,384]{1,0:T(8,128)(2,1)S(1)} %collective-permute-done.13.refs_1_) | copy-start | bytes 442372
  99.2 10.3 %collective-permute-start.19 = (bf16[192,384]{1,0:T(8,128)(2,1)S(1)}, bf16[192,384]{1,0:T(8,128)(2,1)S(1)}, u32[]{:S(2)}, u32[]{:S(2)}) collective-permute-start(bf16[192,384]{1,0:T(8,128)(2,1)S(1)} %get-tuple-element.99), channel_id=1, source_target_pairs={{0,24},{2,26},{4,28},{6,30},{8,16},{10,18},{12,20},{14,22},{16,8},... | collective-permute-start | bytes 442376 | tf_op jit(solution)/shard_map/ppermute | solution.py:19
  108.1 19.9 %collective-permute-start.14 = (bf16[192,384]{1,0:T(8,128)(2,1)S(1)}, bf16[192,384]{1,0:T(8,128)(2,1)S(1)}, u32[]{:S(2)}, u32[]{:S(2)}) collective-permute-start(bf16[192,384]{1,0:T(8,128)(2,1)S(1)} %get-tuple-element.90), channel_id=1, source_target_pairs={{0,8},{2,10},{4,12},{6,14},{8,0},{10,2},{12,4},{14,6},{16,24},{18,... | collective-permute-start | bytes 442376 | tf_op jit(solution)/shard_map/ppermute | solution.py:19
  109.5 22.3 %collective-permute-start.17 = (bf16[192,384]{1,0:T(8,128)(2,1)S(1)}, bf16[192,384]{1,0:T(8,128)(2,1)S(1)}, u32[]{:S(2)}, u32[]{:S(2)}) collective-permute-start(bf16[192,384]{1,0:T(8,128)(2,1)S(1)} %get-tuple-element.95), channel_id=1, source_target_pairs={{0,16},{2,18},{4,20},{6,22},{8,24},{10,26},{12,28},{14,30},{16,0},... | collective-permute-start | bytes 442376 | tf_op jit(solution)/shard_map/ppermute | solution.py:19
  110.5 21.3 %collective-permute-start.20 = (bf16[192,384]{1,0:T(8,128)(2,1)S(1)}, bf16[192,384]{1,0:T(8,128)(2,1)S(1)}, u32[]{:S(2)}, u32[]{:S(2)}) collective-permute-start(bf16[192,384]{1,0:T(8,128)(2,1)S(1)} %get-tuple-element.100), channel_id=1, source_target_pairs={{0,24},{2,26},{4,28},{6,30},{8,16},{10,18},{12,20},{14,22},{16,8},... | collective-permute-start | bytes 442376 | tf_op jit(solution)/shard_map/ppermute | solution.py:19
  127.3 19.4 %collective-permute-start.28 = (bf16[192,384]{1,0:T(8,128)(2,1)}, bf16[192,384]{1,0:T(8,128)(2,1)S(1)}, u32[]{:S(2)}, u32[]{:S(2)}) collective-permute-start(bf16[192,384]{1,0:T(8,128)(2,1)} %get-tuple-element.107), channel_id=1, source_target_pairs={{0,24},{2,26},{4,28},{6,30},{8,16},{10,18},{12,20},{14,22},{16,8},... | collective-permute-start | bytes 442376 | tf_op jit(solution)/shard_map/ppermute | solution.py:19
  127.8 18.9 %collective-permute-start.29 = (bf16[192,384]{1,0:T(8,128)(2,1)}, bf16[192,384]{1,0:T(8,128)(2,1)S(1)}, u32[]{:S(2)}, u32[]{:S(2)}) collective-permute-start(bf16[192,384]{1,0:T(8,128)(2,1)} %get-tuple-element.108), channel_id=1, source_target_pairs={{0,16},{2,18},{4,20},{6,22},{8,24},{10,26},{12,28},{14,30},{16,0},... | collective-permute-start | bytes 442376 | tf_op jit(solution)/shard_map/ppermute | solution.py:19
  128.0 21.7 %copy-start.9 = (bf16[192,384]{1,0:T(8,128)(2,1)S(1)}, bf16[192,384]{1,0:T(8,128)(2,1)}, u32[]{:S(2)}) copy-start(bf16[192,384]{1,0:T(8,128)(2,1)} %get-tuple-element.110.refs_3_) | copy-start | bytes 442372
  128.0 21.7 %collective-permute-start.30 = (bf16[192,384]{1,0:T(8,128)(2,1)}, bf16[192,384]{1,0:T(8,128)(2,1)S(1)}, u32[]{:S(2)}, u32[]{:S(2)}) collective-permute-start(bf16[192,384]{1,0:T(8,128)(2,1)} %get-tuple-element.109), channel_id=1, source_target_pairs={{0,8},{2,10},{4,12},{6,14},{8,0},{10,2},{12,4},{14,6},{16,24},{18,... | collective-permute-start | bytes 442376 | tf_op jit(solution)/shard_map/ppermute | solution.py:19
  145.4 8.2 %collective-permute-start.24 = (bf16[192,384]{1,0:T(8,128)(2,1)}, bf16[192,384]{1,0:T(8,128)(2,1)S(1)}, u32[]{:S(2)}, u32[]{:S(2)}) collective-permute-start(bf16[192,384]{1,0:T(8,128)(2,1)} %get-tuple-element.103), channel_id=1, source_target_pairs={{0,26},{2,24},{4,30},{6,28},{8,18},{10,16},{12,22},{14,20},{16,10}... | collective-permute-start | bytes 442376 | tf_op jit(solution)/shard_map/ppermute | solution.py:19
  145.5 14.5 %collective-permute-start.25 = (bf16[192,384]{1,0:T(8,128)(2,1)}, bf16[192,384]{1,0:T(8,128)(2,1)S(1)}, u32[]{:S(2)}, u32[]{:S(2)}) collective-permute-start(bf16[192,384]{1,0:T(8,128)(2,1)} %get-tuple-element.104), channel_id=1, source_target_pairs={{0,18},{2,16},{4,22},{6,20},{8,26},{10,24},{12,30},{14,28},{16,2},... | collective-permute-start | bytes 442376 | tf_op jit(solution)/shard_map/ppermute | solution.py:19
  146.7 13.2 %collective-permute-start.26 = (bf16[192,384]{1,0:T(8,128)(2,1)}, bf16[192,384]{1,0:T(8,128)(2,1)S(1)}, u32[]{:S(2)}, u32[]{:S(2)}) collective-permute-start(bf16[192,384]{1,0:T(8,128)(2,1)} %get-tuple-element.105), channel_id=1, source_target_pairs={{0,10},{2,8},{4,14},{6,12},{8,2},{10,0},{12,6},{14,4},{16,26},{18,... | collective-permute-start | bytes 442376 | tf_op jit(solution)/shard_map/ppermute | solution.py:19
  146.7 13.2 %collective-permute-start.27 = (bf16[192,384]{1,0:T(8,128)(2,1)}, bf16[192,384]{1,0:T(8,128)(2,1)S(1)}, u32[]{:S(2)}, u32[]{:S(2)}) collective-permute-start(bf16[192,384]{1,0:T(8,128)(2,1)} %get-tuple-element.106), channel_id=1, source_target_pairs={{0,2},{2,0},{4,6},{6,4},{8,10},{10,8},{12,14},{14,12},{16,18},{18,... | collective-permute-start | bytes 442376 | tf_op jit(solution)/shard_map/ppermute | solution.py:19
  (11 other events, 36.1 us)

commit v18 on v16

--- a/solution.py
+++ b/solution.py
@@ -12,7 +12,6 @@
 LOG2_E = 1.4426950408889634
 HIDDEN = -1e30
 VMEM_LIMIT = 44 * 2**20
-ATTEND_LIMIT = 56 * 2**20
 
 
 def exchange(value, axis, size, bit):
@@ -156,25 +155,18 @@
     query_refs = refs[:ways]
     block_refs = refs[ways : ways + arrays]
     out_refs = refs[ways + arrays : 2 * ways + arrays]
-    ordered, asked, scores, highest, sums, total, position, sems = refs[2 * ways + arrays :]
+    ordered, asked, scores, highest, sums, total, position = refs[2 * ways + arrays :]
     rows, width = out_refs[0].shape
     half = rows // 2
     heads = width // HD
     rest = count // ways
 
-    copies = [[], []]
     for slot, (offset, array, row) in enumerate(slots):
         low = table[offset]
         for part, span in ((0, low), (1, spans - 1 - low)):
-            copies[part].append(
-                pltpu.make_async_copy(
-                    block_refs[array].at[pl.ds(row + part * half, half)],
-                    ordered.at[pl.ds(pl.multiple_of(span * half, 16), half)],
-                    sems.at[2 * slot + part],
-                )
-            )
-    for copy in copies[0] + copies[1]:
-        copy.start()
+            ordered[pl.ds(pl.multiple_of(span * half, 16), half)] = block_refs[array][
+                row + part * half : row + (part + 1) * half
+            ]
 
     from_lane = lax.broadcasted_iota(jnp.int32, (half, 128), 0) - lax.broadcasted_iota(
         jnp.int32, (half, 128), 1
@@ -185,8 +177,6 @@
         for part, span in ((0, low), (1, spans - 1 - low)):
             asked[part, here] = query_refs[a][part * half : (part + 1) * half]
             position[part, here] = from_lane + span * half
-    for copy in copies[0]:
-        copy.wait()
 
     slope = LOG2_E / math.sqrt(HD)
     middle = spans * half // 2
@@ -202,9 +192,6 @@
 
     def score_tile(unit, slot, start):
         part, h = unit
-        if unit == (1, 0) and start == middle:
-            for copy in copies[1]:
-                copy.wait()
         scores[slot, :, start : start + tile] = lax.dot_general(
             asked[part, :, h * HD : (h + 1) * HD],
             ordered[start : start + tile, h * HD : (h + 1) * HD],
@@ -283,7 +270,7 @@
         grid=(1,),
         in_specs=[smem]
         + [pl.BlockSpec((rows, width), lambda i: (0, 0))] * ways
-        + [pl.BlockSpec(memory_space=pl.ANY)] * len(arrays),
+        + [pl.BlockSpec(array.shape, lambda i: (0, 0)) for array in arrays],
         out_specs=[pl.BlockSpec((rows, width), lambda i: (0, 0))] * ways,
         scratch_shapes=[
             pltpu.VMEM((length, 2 * width), jnp.bfloat16),
@@ -293,9 +280,8 @@
             pltpu.VMEM((2, many, 128), jnp.float32),
             pltpu.VMEM((2, many, HD), jnp.float32),
             pltpu.VMEM((2, many, 128), jnp.int32),
-            pltpu.SemaphoreType.DMA((2 * count,)),
         ],
-        compiler_params=pltpu.CompilerParams(vmem_limit_bytes=ATTEND_LIMIT),
+        compiler_params=pltpu.CompilerParams(vmem_limit_bytes=VMEM_LIMIT),
         cost_estimate=pl.CostEstimate(
             flops=flops,
             bytes_accessed=4 * length * width + 4 * ways * rows * width,

time: 161 us -> 153 us (0.950)
  Pallas kernels: 78.4 us -> 71.9 us
  local copies, waits for them, and re-layouts: 7.84 us -> 5.04 us
    pallas_call x2, Pallas kernels: 24.3 us -> 17.7 us  [attend(): pl.pallas_call(functools.partial(attend_body, block, ways, slots, len(arr...]
    unnamed x56 -> x4, local copies, waits for them, and re-layouts: 2.79 us -> 0.01 us
  transfers between devices with their start and end apart: 31 -> 31, of which waited for: 10 -> 9; matrix products, arithmetic and copies ran while one was open for 1% -> 2% of each run, Pallas kernels for 48% -> 46%
where the time goes in v18:
time: 153 us
  Pallas kernels  71.9 us (47%)
  starting transfers between devices  45.4 us (30%)
  waiting for transfers between devices  30.1 us (20%)
  local copies, waits for them, and re-layouts  5.04 us (3%)
    ppermute x31, starting transfers between devices, exchange(): return lax.ppermute(value, axis, [(i, i ^ bit) for i in range(size)])  45.4 us
    pallas_call x5, Pallas kernels, rest_products(): pl.pallas_call(functools.partial(rest_body, shares, len(weights), chunks,...  31.7 us
    ppermute x31, waiting for transfers between devices, exchange(): return lax.ppermute(value, axis, [(i, i ^ bit) for i in range(size)])  30.1 us
    pallas_call x2, Pallas kernels, attend(): pl.pallas_call(functools.partial(attend_body, block, ways, slots, len(arr...  17.7 us
    pallas_call x1, Pallas kernels, own_products(): pl.pallas_call(functools.partial(own_body, len(weights)), out_shape=[jax....  17.7 us
    pallas_call x2, Pallas kernels, assemble(): pl.pallas_call(functools.partial(assemble_body, ways), out_shape=jax.Shap...  3.99 us
  transfers between devices with their start and end apart: 31, of which 9 were waited for; matrix products, arithmetic and copies ran while one was open for 2% of the time, Pallas kernels for 46%

profile of v18, /device:TPU:0, one launch (start us, length us, event | category | flops | bytes accessed | tf_op | source)
XLA Modules:
  0.0 152.8 jit_solution(4034753898584714639)
XLA Ops:
  0.0 3.1 %dynamic-slice_bitcast_fusion = (bf16[192,2560]{1,0:T(8,128)(2,1)}, bf16[192,2560]{1,0:T(8,128)(2,1)}) fusion(bf16[2,192,2560]{2,1,0:T(8,128)(2,1)} %mine_ref.1, s32[]{:T(128)S(6)} %select_n.30, s32[]{:T(128)S(6)} %select_n.29), kind=kLoop, calls=%fused_computation | loop fusion | bytes 3932168 | tf_op jit(solution)/shard_map/jit(dynamic_index_in_dim)/squeeze | solution.py:371
  3.1 0.5 collective-permute-start.2
  3.5 2.5 %collective-permute-start.1 = (bf16[192,2560]{1,0:T(8,128)(2,1)}, bf16[192,2560]{1,0:T(8,128)(2,1)S(1)}, u32[]{:S(2)}, u32[]{:S(2)}) collective-permute-start(bf16[192,2560]{1,0:T(8,128)(2,1)} %get-tuple-element.114), channel_id=1, source_target_pairs={{0,1},{1,0},{2,3},{3,2},{4,5},{5,4},{6,7},{7,6},{8,9},{9,8},{10,11... | collective-permute-start | bytes 2949128 | tf_op jit(solution)/shard_map/ppermute | solution.py:18
  6.3 0.7 fusion
  7.2 0.9 collective-permute-done
  8.1 1.3 concatenate.4.place
  9.4 0.9 collective-permute-start.3
  10.3 17.7 %shard_map.55 = (f32[2,192,1536]{2,1,0:T(8,128)S(1)}, f32[2,192,1536]{2,1,0:T(8,128)S(1)}, f32[2,192,1536]{2,1,0:T(8,128)S(1)}) custom-call(s32[4]{0:T(128)S(1)} %pad_add_fusion.place, bf16[2,192,2560]{2,1,0:T(8,128)(2,1)S(1)} %copy-done, bf16[192,2560]{1,0:T(8,128)(2,1)} %collective-permute-done.2.other_ref, bf16[5120,1536]{1,0:T(8,128)(2,1)} %refs_1_.10, ...), custom_call_target="tpu_custom_call" | custom-call | flops 9059696640 | bytes 23592960 | tf_op jit(solution)/shard_map/pallas_call | solution.py:42
  27.9 0.9 collective-permute-done.1.refs_0_
  28.8 5.3 %shard_map.59 = (bf16[208,768]{1,0:T(8,128)(2,1)S(1)}, bf16[208,768]{1,0:T(8,128)(2,1)S(1)}) custom-call(s32[6]{0:T(128)S(1)} %concatenate.4.place, bf16[192,2560]{1,0:T(8,128)(2,1)S(1)} %collective-permute-done.1.refs_0_, bf16[5120,1536]{1,0:T(8,128)(2,1)} %refs_1_.10, bf16[5120,1536]{1,0:T(8,128)(2,1)} %refs_2_.7, ...), custom_call_target="tpu_custom_call" | custom-call | flops 1509949440 | bytes 7864320 | tf_op jit(solution)/shard_map/pallas_call | solution.py:128
  34.1 3.1 %collective-permute-start.7 = (bf16[208,768]{1,0:T(8,128)(2,1)S(1)}, bf16[208,768]{1,0:T(8,128)(2,1)S(1)}, u32[]{:S(2)}, u32[]{:S(2)}) collective-permute-start(bf16[208,768]{1,0:T(8,128)(2,1)S(1)} %get-tuple-element.73), channel_id=1, source_target_pairs={{0,16},{2,18},{4,20},{6,22},{8,24},{10,26},{12,28},{14,30},{16,0},... | collective-permute-start | bytes 958472 | tf_op jit(solution)/shard_map/ppermute | solution.py:18
  37.2 1.3 collective-permute-start.9
  38.5 5.2 %shard_map.56 = (bf16[208,768]{1,0:T(8,128)(2,1)S(1)}, bf16[208,768]{1,0:T(8,128)(2,1)S(1)}) custom-call(s32[6]{0:T(128)S(1)} %concatenate.4.place, bf16[192,2560]{1,0:T(8,128)(2,1)S(1)} %collective-permute-done.1.refs_0_, bf16[5120,1536]{1,0:T(8,128)(2,1)} %refs_1_.10, bf16[5120,1536]{1,0:T(8,128)(2,1)} %refs_2_.7, ...), custom_call_target="tpu_custom_call" | custom-call | flops 1509949440 | bytes 7864320 | tf_op jit(solution)/shard_map/pallas_call | solution.py:128
  43.8 0.3 collective-permute-start.5
  44.1 1.5 collective-permute-start.4
  45.6 6.0 %shard_map.57 = (bf16[192,384]{1,0:T(8,128)(2,1)S(1)}, bf16[192,384]{1,0:T(8,128)(2,1)S(1)}, bf16[192,384]{1,0:T(8,128)(2,1)S(1)}, bf16[192,384]{1,0:T(8,128)(2,1)S(1)}) custom-call(s32[4]{0:T(128)S(1)} %pad_add_fusion.place, bf16[192,2560]{1,0:T(8,128)(2,1)S(1)} %collective-permute-done.1.refs_0_, bf16[5120,1536]{1,0:T(8,128)(2,1)} %refs_1_.11, ...), custom_call_target="tpu_custom_call" | custom-call | flops 1509949440 | bytes 7864320 | tf_op jit(solution)/shard_map/pallas_call | solution.py:128
  51.6 9.1 %shard_map.58 = (bf16[192,768]{1,0:T(8,128)(2,1)S(1)}, bf16[192,768]{1,0:T(8,128)(2,1)S(1)}, bf16[192,768]{1,0:T(8,128)(2,1)S(1)}, bf16[192,768]{1,0:T(8,128)(2,1)S(1)}) custom-call(s32[4]{0:T(128)S(1)} %pad_add_fusion.place, bf16[192,2560]{1,0:T(8,128)(2,1)S(1)} %collective-permute-done.3.refs_0_, bf16[5120,1536]{1,0:T(8,128)(2,1)} %refs_1_.10, ...), custom_call_target="tpu_custom_call" | custom-call | flops 3019898880 | bytes 15728640 | tf_op jit(solution)/shard_map/pallas_call | solution.py:128
  60.7 0.6 collective-permute-start.8
  61.3 2.6 %collective-permute-done.5.refs_2_.refs_8_ = bf16[208,768]{1,0:T(8,128)(2,1)S(1)} collective-permute-done((bf16[208,768]{1,0:T(8,128)(2,1)S(1)}, bf16[208,768]{1,0:T(8,128)(2,1)S(1)}, u32[]{:S(2)}, u32[]{:S(2)}) %collective-permute-start.5) | collective-permute-done | bytes 319520 | tf_op jit(solution)/shard_map/ppermute | solution.py:18
  63.9 1.6 %collective-permute-start.6 = (bf16[208,768]{1,0:T(8,128)(2,1)S(1)}, bf16[208,768]{1,0:T(8,128)(2,1)S(1)}, u32[]{:S(2)}, u32[]{:S(2)}) collective-permute-start(bf16[208,768]{1,0:T(8,128)(2,1)S(1)} %collective-permute-done.5.refs_2_.refs_8_), channel_id=1, source_target_pairs={{0,4},{2,6},{4,0},{6,2},{8,12},{10,14},{12,8},{14,10},{16,20},{18,... | collective-permute-start | bytes 958472 | tf_op jit(solution)/shard_map/ppermute | solution.py:18
  65.4 0.5 collective-permute-start.11
  65.9 4.1 %collective-permute-start.15 = (bf16[192,768]{1,0:T(8,128)(2,1)S(1)}, bf16[192,768]{1,0:T(8,128)(2,1)S(1)}, u32[]{:S(2)}, u32[]{:S(2)}) collective-permute-start(bf16[192,768]{1,0:T(8,128)(2,1)S(1)} %get-tuple-element.94), channel_id=1, source_target_pairs={{0,16},{2,18},{4,20},{6,22},{8,24},{10,26},{12,28},{14,30},{16,0},... | collective-permute-start | bytes 884744 | tf_op jit(solution)/shard_map/ppermute | solution.py:18
  70.0 1.2 collective-permute-done.8.refs_5_.refs_14_
  71.2 2.9 %collective-permute-start.18 = (bf16[192,768]{1,0:T(8,128)(2,1)S(1)}, bf16[192,768]{1,0:T(8,128)(2,1)S(1)}, u32[]{:S(2)}, u32[]{:S(2)}) collective-permute-start(bf16[192,768]{1,0:T(8,128)(2,1)S(1)} %get-tuple-element.100), channel_id=1, source_target_pairs={{0,24},{2,26},{4,28},{6,30},{8,16},{10,18},{12,20},{14,22},{16,8},... | collective-permute-start | bytes 884744 | tf_op jit(solution)/shard_map/ppermute | solution.py:18
  74.1 3.9 %collective-permute-done.6.refs_3_.refs_10_ = bf16[208,768]{1,0:T(8,128)(2,1)S(1)} collective-permute-done((bf16[208,768]{1,0:T(8,128)(2,1)S(1)}, bf16[208,768]{1,0:T(8,128)(2,1)S(1)}, u32[]{:S(2)}, u32[]{:S(2)}) %collective-permute-start.6) | collective-permute-done | bytes 319520 | tf_op jit(solution)/shard_map/ppermute | solution.py:18
  78.1 0.5 collective-permute-start.10
  78.6 5.8 %collective-permute-done.11.refs_7_ = bf16[192,768]{1,0:T(8,128)(2,1)S(1)} collective-permute-done((bf16[192,768]{1,0:T(8,128)(2,1)S(1)}, bf16[192,768]{1,0:T(8,128)(2,1)S(1)}, u32[]{:S(2)}, u32[]{:S(2)}) %collective-permute-start.11) | collective-permute-done | bytes 294944 | tf_op jit(solution)/shard_map/ppermute | solution.py:18
  84.4 1.8 %collective-permute-start.13 = (bf16[192,384]{1,0:T(8,128)(2,1)S(1)}, bf16[192,384]{1,0:T(8,128)(2,1)S(1)}, u32[]{:S(2)}, u32[]{:S(2)}) collective-permute-start(bf16[192,384]{1,0:T(8,128)(2,1)S(1)} %get-tuple-element.89), channel_id=1, source_target_pairs={{0,8},{2,10},{4,12},{6,14},{8,0},{10,2},{12,4},{14,6},{16,24},{18,... | collective-permute-start | bytes 442376 | tf_op jit(solution)/shard_map/ppermute | solution.py:18
  86.2 0.5 collective-permute-start.21
  86.7 3.9 %collective-permute-done.15.refs_13_ = bf16[192,768]{1,0:T(8,128)(2,1)S(1)} collective-permute-done((bf16[192,768]{1,0:T(8,128)(2,1)S(1)}, bf16[192,768]{1,0:T(8,128)(2,1)S(1)}, u32[]{:S(2)}, u32[]{:S(2)}) %collective-permute-start.15) | collective-permute-done | bytes 294944 | tf_op jit(solution)/shard_map/ppermute | solution.py:18
  90.6 1.5 collective-permute-start.22
  92.1 0.5 collective-permute-start.23
  92.6 5.5 %collective-permute-start.16 = (bf16[192,384]{1,0:T(8,128)(2,1)S(1)}, bf16[192,384]{1,0:T(8,128)(2,1)S(1)}, u32[]{:S(2)}, u32[]{:S(2)}) collective-permute-start(bf16[192,384]{1,0:T(8,128)(2,1)S(1)} %get-tuple-element.95), channel_id=1, source_target_pairs={{0,16},{2,18},{4,20},{6,22},{8,24},{10,26},{12,28},{14,30},{16,0},... | collective-permute-start | bytes 442376 | tf_op jit(solution)/shard_map/ppermute | solution.py:18
  98.1 0.7 collective-permute-start.19
  98.8 6.2 %shard_map.61 = (bf16[192,384]{1,0:T(8,128)(2,1)S(1)}, bf16[192,384]{1,0:T(8,128)(2,1)S(1)}, bf16[192,384]{1,0:T(8,128)(2,1)S(1)}, bf16[192,384]{1,0:T(8,128)(2,1)S(1)}) custom-call(s32[4]{0:T(128)S(1)} %pad_add_fusion.place, bf16[192,2560]{1,0:T(8,128)(2,1)S(1)} %collective-permute-done.3.refs_0_, bf16[5120,1536]{1,0:T(8,128)(2,1)} %refs_1_.11, ...), custom_call_target="tpu_custom_call" | custom-call | flops 1509949440 | bytes 7864320 | tf_op jit(solution)/shard_map/pallas_call | solution.py:128
  105.0 2.0 %collective-permute-done.16.refs_2_ = bf16[192,384]{1,0:T(8,128)(2,1)S(1)} collective-permute-done((bf16[192,384]{1,0:T(8,128)(2,1)S(1)}, bf16[192,384]{1,0:T(8,128)(2,1)S(1)}, u32[]{:S(2)}, u32[]{:S(2)}) %collective-permute-start.16) | collective-permute-done | bytes 147488 | tf_op jit(solution)/shard_map/ppermute | solution.py:18
  107.0 0.7 shard_map.60.table
  107.8 1.8 %collective-permute-start.17 = (bf16[192,384]{1,0:T(8,128)(2,1)S(1)}, bf16[192,384]{1,0:T(8,128)(2,1)S(1)}, u32[]{:S(2)}, u32[]{:S(2)}) collective-permute-start(bf16[192,384]{1,0:T(8,128)(2,1)S(1)} %get-tuple-element.96), channel_id=1, source_target_pairs={{0,16},{2,18},{4,20},{6,22},{8,24},{10,26},{12,28},{14,30},{16,0},... | collective-permute-start | bytes 442376 | tf_op jit(solution)/shard_map/ppermute | solution.py:18
  109.6 3.1 %collective-permute-start.20 = (bf16[192,384]{1,0:T(8,128)(2,1)S(1)}, bf16[192,384]{1,0:T(8,128)(2,1)S(1)}, u32[]{:S(2)}, u32[]{:S(2)}) collective-permute-start(bf16[192,384]{1,0:T(8,128)(2,1)S(1)} %get-tuple-element.102), channel_id=1, source_target_pairs={{0,24},{2,26},{4,28},{6,30},{8,16},{10,18},{12,20},{14,22},{16,8},... | collective-permute-start | bytes 442376 | tf_op jit(solution)/shard_map/ppermute | solution.py:18
  112.8 8.7 %shard_map.63 = (bf16[192,384]{1,0:T(8,128)(2,1)S(1)}, bf16[192,384]{1,0:T(8,128)(2,1)S(1)}, bf16[192,384]{1,0:T(8,128)(2,1)S(1)}, bf16[192,384]{1,0:T(8,128)(2,1)S(1)}) custom-call(s32[16]{0:T(128)S(1)} %shard_map.60.table, bf16[192,384]{1,0:T(8,128)(2,1)S(1)} %get-tuple-element.82.refs_0_, bf16[192,384]{1,0:T(8,128)(2,1)S(1)} %collective-permute-done.13.refs_1_, ...), custom_call_target="tpu_custom_call" | custom-call | flops 2717908992 | bytes 5898240 | tf_op jit(solution)/shard_map/pallas_call | solution.py:267
  121.5 0.7 collective-permute-start.28
  122.3 3.7 %collective-permute-start.30 = (bf16[192,384]{1,0:T(8,128)(2,1)S(1)}, bf16[192,384]{1,0:T(8,128)(2,1)S(1)}, u32[]{:S(2)}, u32[]{:S(2)}) collective-permute-start(bf16[192,384]{1,0:T(8,128)(2,1)S(1)} %get-tuple-element.111), channel_id=1, source_target_pairs={{0,8},{2,10},{4,12},{6,14},{8,0},{10,2},{12,4},{14,6},{16,24},{18,... | collective-permute-start | bytes 442376 | tf_op jit(solution)/shard_map/ppermute | solution.py:18
  126.0 9.0 %shard_map.62 = (bf16[192,384]{1,0:T(8,128)(2,1)S(1)}, bf16[192,384]{1,0:T(8,128)(2,1)S(1)}, bf16[192,384]{1,0:T(8,128)(2,1)S(1)}, bf16[192,384]{1,0:T(8,128)(2,1)S(1)}) custom-call(s32[16]{0:T(128)S(1)} %shard_map.60.table, bf16[192,384]{1,0:T(8,128)(2,1)S(1)} %get-tuple-element.83.refs_0_, bf16[192,384]{1,0:T(8,128)(2,1)S(1)} %collective-permute-done.14.refs_1_, ...), custom_call_target="tpu_custom_call" | custom-call | flops 2717908992 | bytes 5898240 | tf_op jit(solution)/shard_map/pallas_call | solution.py:267
  135.1 3.7 %collective-permute-start.25 = (bf16[192,384]{1,0:T(8,128)(2,1)S(1)}, bf16[192,384]{1,0:T(8,128)(2,1)S(1)}, u32[]{:S(2)}, u32[]{:S(2)}) collective-permute-start(bf16[192,384]{1,0:T(8,128)(2,1)S(1)} %get-tuple-element.106), channel_id=1, source_target_pairs={{0,18},{2,16},{4,22},{6,20},{8,26},{10,24},{12,30},{14,28},{16,2},... | collective-permute-start | bytes 442376 | tf_op jit(solution)/shard_map/ppermute | solution.py:18
  138.8 1.2 collective-permute-start.26
  140.0 2.0 %shard_map.64.refs_4_ = bf16[2,192,1536]{2,1,0:T(8,128)(2,1)} custom-call(s32[4]{0:T(128)S(1)} %pad_add_fusion.place, bf16[192,384]{1,0:T(8,128)(2,1)S(1)} %collective-permute-done.28.refs_0_, bf16[192,384]{1,0:T(8,128)(2,1)S(1)} %collective-permute-done.29.refs_1_, bf16[192,384]{1,0:T(8,128)(2,1)S(1)} %collective-permute-done.30.refs_2_, ...), custom_call_target="tpu_custom_call" | custom-call | tf_op jit(solution)/shard_map/pallas_call | solution.py:334
  142.0 8.8 %collective-permute-done.25.refs_1_ = bf16[192,384]{1,0:T(8,128)(2,1)S(1)} collective-permute-done((bf16[192,384]{1,0:T(8,128)(2,1)S(1)}, bf16[192,384]{1,0:T(8,128)(2,1)S(1)}, u32[]{:S(2)}, u32[]{:S(2)}) %collective-permute-start.25) | collective-permute-done | bytes 147488 | tf_op jit(solution)/shard_map/ppermute | solution.py:18
  150.8 2.0 %shard_map.65 = bf16[2,192,1536]{2,1,0:T(8,128)(2,1)} custom-call(s32[4]{0:T(128)S(1)} %pad_add_fusion.place, bf16[192,384]{1,0:T(8,128)(2,1)S(1)} %collective-permute-done.24.refs_0_, bf16[192,384]{1,0:T(8,128)(2,1)S(1)} %collective-permute-done.25.refs_1_, bf16[192,384]{1,0:T(8,128)(2,1)S(1)} %collective-permute-done.26.refs_2_, ...), custom_call_target="tpu_custom_call", output_to_operand_aliasing={{}: (5, {})} | custom-call | tf_op jit(solution)/shard_map/pallas_call | solution.py:334
  (36 shorter events, 0.7 us)
Async XLA Ops:
  0.0 10.3 %copy-start = (bf16[2,192,2560]{2,1,0:T(8,128)(2,1)S(1)}, bf16[2,192,2560]{2,1,0:T(8,128)(2,1)}, u32[]{:S(2)}) copy-start(bf16[2,192,2560]{2,1,0:T(8,128)(2,1)} %mine_ref.1) | copy-start | bytes 5898244
  0.0 6.0 %copy-start.1 = (s32[2,192]{1,0:T(2,128)S(1)}, s32[2,192]{1,0:T(2,128)}, u32[]{:S(2)}) copy-start(s32[2,192]{1,0:T(2,128)} %param.9) | copy-start | bytes 4612
  3.1 6.3 %collective-permute-start.2 = (bf16[192,2560]{1,0:T(8,128)(2,1)}, bf16[192,2560]{1,0:T(8,128)(2,1)}, u32[]{:S(2)}, u32[]{:S(2)}) collective-permute-start(bf16[192,2560]{1,0:T(8,128)(2,1)} %get-tuple-element.113), channel_id=1, source_target_pairs={{0,2},{2,0},{4,6},{6,4},{8,10},{10,8},{12,14},{14,12},{16,18},{18,... | collective-permute-start | bytes 2949128 | tf_op jit(solution)/shard_map/ppermute | solution.py:18
  3.5 25.3 %collective-permute-start.1 = (bf16[192,2560]{1,0:T(8,128)(2,1)}, bf16[192,2560]{1,0:T(8,128)(2,1)S(1)}, u32[]{:S(2)}, u32[]{:S(2)}) collective-permute-start(bf16[192,2560]{1,0:T(8,128)(2,1)} %get-tuple-element.114), channel_id=1, source_target_pairs={{0,1},{1,0},{2,3},{3,2},{4,5},{5,4},{6,7},{7,6},{8,9},{9,8},{10,11... | collective-permute-start | bytes 2949128 | tf_op jit(solution)/shard_map/ppermute | solution.py:18
  6.9 1.2 collective-permute-start
  9.4 42.2 %collective-permute-start.3 = (bf16[192,2560]{1,0:T(8,128)(2,1)}, bf16[192,2560]{1,0:T(8,128)(2,1)S(1)}, u32[]{:S(2)}, u32[]{:S(2)}) collective-permute-start(bf16[192,2560]{1,0:T(8,128)(2,1)} %collective-permute-done.2.other_ref), channel_id=1, source_target_pairs={{0,1},{1,0},{2,3},{3,2},{4,5},{5,4},{6,7},{7,6},{8,9},{9,8},{10,11... | collective-permute-start | bytes 2949128 | tf_op jit(solution)/shard_map/ppermute | solution.py:18
  34.1 26.6 %collective-permute-start.7 = (bf16[208,768]{1,0:T(8,128)(2,1)S(1)}, bf16[208,768]{1,0:T(8,128)(2,1)S(1)}, u32[]{:S(2)}, u32[]{:S(2)}) collective-permute-start(bf16[208,768]{1,0:T(8,128)(2,1)S(1)} %get-tuple-element.73), channel_id=1, source_target_pairs={{0,16},{2,18},{4,20},{6,22},{8,24},{10,26},{12,28},{14,30},{16,0},... | collective-permute-start | bytes 958472 | tf_op jit(solution)/shard_map/ppermute | solution.py:18
  37.2 28.7 %collective-permute-start.9 = (bf16[208,768]{1,0:T(8,128)(2,1)S(1)}, bf16[208,768]{1,0:T(8,128)(2,1)S(1)}, u32[]{:S(2)}, u32[]{:S(2)}) collective-permute-start(bf16[208,768]{1,0:T(8,128)(2,1)S(1)} %get-tuple-element.76), channel_id=1, source_target_pairs={{0,24},{2,26},{4,28},{6,30},{8,16},{10,18},{12,20},{14,22},{16,8},... | collective-permute-start | bytes 958472 | tf_op jit(solution)/shard_map/ppermute | solution.py:18
  43.8 20.1 %collective-permute-start.5 = (bf16[208,768]{1,0:T(8,128)(2,1)S(1)}, bf16[208,768]{1,0:T(8,128)(2,1)S(1)}, u32[]{:S(2)}, u32[]{:S(2)}) collective-permute-start(bf16[208,768]{1,0:T(8,128)(2,1)S(1)} %get-tuple-element.70), channel_id=1, source_target_pairs={{0,8},{2,10},{4,12},{6,14},{8,0},{10,2},{12,4},{14,6},{16,24},{18,... | collective-permute-start | bytes 958472 | tf_op jit(solution)/shard_map/ppermute | solution.py:18
  44.1 21.8 %collective-permute-start.4 = (bf16[208,768]{1,0:T(8,128)(2,1)S(1)}, bf16[208,768]{1,0:T(8,128)(2,1)S(1)}, u32[]{:S(2)}, u32[]{:S(2)}) collective-permute-start(bf16[208,768]{1,0:T(8,128)(2,1)S(1)} %get-tuple-element.69.refs_0_.refs_4_), channel_id=1, source_target_pairs={{0,4},{2,6},{4,0},{6,2},{8,12},{10,14},{12,8},{14,10},{16,20},{18,... | collective-permute-start | bytes 958472 | tf_op jit(solution)/shard_map/ppermute | solution.py:18
  60.7 10.5 %collective-permute-start.8 = (bf16[208,768]{1,0:T(8,128)(2,1)S(1)}, bf16[208,768]{1,0:T(8,128)(2,1)S(1)}, u32[]{:S(2)}, u32[]{:S(2)}) collective-permute-start(bf16[208,768]{1,0:T(8,128)(2,1)S(1)} %collective-permute-done.7.refs_4_.refs_12_), channel_id=1, source_target_pairs={{0,4},{2,6},{4,0},{6,2},{8,12},{10,14},{12,8},{14,10},{16,20},{18,... | collective-permute-start | bytes 958472 | tf_op jit(solution)/shard_map/ppermute | solution.py:18
  63.9 14.2 %collective-permute-start.6 = (bf16[208,768]{1,0:T(8,128)(2,1)S(1)}, bf16[208,768]{1,0:T(8,128)(2,1)S(1)}, u32[]{:S(2)}, u32[]{:S(2)}) collective-permute-start(bf16[208,768]{1,0:T(8,128)(2,1)S(1)} %collective-permute-done.5.refs_2_.refs_8_), channel_id=1, source_target_pairs={{0,4},{2,6},{4,0},{6,2},{8,12},{10,14},{12,8},{14,10},{16,20},{18,... | collective-permute-start | bytes 958472 | tf_op jit(solution)/shard_map/ppermute | solution.py:18
  65.4 18.9 %collective-permute-start.11 = (bf16[192,768]{1,0:T(8,128)(2,1)S(1)}, bf16[192,768]{1,0:T(8,128)(2,1)S(1)}, u32[]{:S(2)}, u32[]{:S(2)}) collective-permute-start(bf16[192,768]{1,0:T(8,128)(2,1)S(1)} %get-tuple-element.104.refs_5_), channel_id=1, source_target_pairs={{0,4},{2,6},{4,0},{6,2},{8,12},{10,14},{12,8},{14,10},{16,20},{18,... | collective-permute-start | bytes 884744 | tf_op jit(solution)/shard_map/ppermute | solution.py:18
  65.9 18.5 %collective-permute-start.12 = (bf16[192,768]{1,0:T(8,128)(2,1)S(1)}, bf16[192,768]{1,0:T(8,128)(2,1)S(1)}, u32[]{:S(2)}, u32[]{:S(2)}) collective-permute-start(bf16[192,768]{1,0:T(8,128)(2,1)S(1)} %get-tuple-element.87), channel_id=1, source_target_pairs={{0,8},{2,10},{4,12},{6,14},{8,0},{10,2},{12,4},{14,6},{16,24},{18,... | collective-permute-start | bytes 884744 | tf_op jit(solution)/shard_map/ppermute | solution.py:18
  65.9 24.7 %collective-permute-start.15 = (bf16[192,768]{1,0:T(8,128)(2,1)S(1)}, bf16[192,768]{1,0:T(8,128)(2,1)S(1)}, u32[]{:S(2)}, u32[]{:S(2)}) collective-permute-start(bf16[192,768]{1,0:T(8,128)(2,1)S(1)} %get-tuple-element.94), channel_id=1, source_target_pairs={{0,16},{2,18},{4,20},{6,22},{8,24},{10,26},{12,28},{14,30},{16,0},... | collective-permute-start | bytes 884744 | tf_op jit(solution)/shard_map/ppermute | solution.py:18
  71.2 20.9 %collective-permute-start.18 = (bf16[192,768]{1,0:T(8,128)(2,1)S(1)}, bf16[192,768]{1,0:T(8,128)(2,1)S(1)}, u32[]{:S(2)}, u32[]{:S(2)}) collective-permute-start(bf16[192,768]{1,0:T(8,128)(2,1)S(1)} %get-tuple-element.100), channel_id=1, source_target_pairs={{0,24},{2,26},{4,28},{6,30},{8,16},{10,18},{12,20},{14,22},{16,8},... | collective-permute-start | bytes 884744 | tf_op jit(solution)/shard_map/ppermute | solution.py:18
  78.1 14.6 %collective-permute-start.10 = (bf16[208,768]{1,0:T(8,128)(2,1)S(1)}, bf16[208,768]{1,0:T(8,128)(2,1)S(1)}, u32[]{:S(2)}, u32[]{:S(2)}) collective-permute-start(bf16[208,768]{1,0:T(8,128)(2,1)S(1)} %collective-permute-done.9.refs_6_.refs_16_), channel_id=1, source_target_pairs={{0,4},{2,6},{4,0},{6,2},{8,12},{10,14},{12,8},{14,10},{16,20},{18,... | collective-permute-start | bytes 958472 | tf_op jit(solution)/shard_map/ppermute | solution.py:18
  84.4 13.7 %collective-permute-start.13 = (bf16[192,384]{1,0:T(8,128)(2,1)S(1)}, bf16[192,384]{1,0:T(8,128)(2,1)S(1)}, u32[]{:S(2)}, u32[]{:S(2)}) collective-permute-start(bf16[192,384]{1,0:T(8,128)(2,1)S(1)} %get-tuple-element.89), channel_id=1, source_target_pairs={{0,8},{2,10},{4,12},{6,14},{8,0},{10,2},{12,4},{14,6},{16,24},{18,... | collective-permute-start | bytes 442376 | tf_op jit(solution)/shard_map/ppermute | solution.py:18
  86.2 23.4 %collective-permute-start.21 = (bf16[192,768]{1,0:T(8,128)(2,1)S(1)}, bf16[192,768]{1,0:T(8,128)(2,1)S(1)}, u32[]{:S(2)}, u32[]{:S(2)}) collective-permute-start(bf16[192,768]{1,0:T(8,128)(2,1)S(1)} %collective-permute-done.12.refs_9_), channel_id=1, source_target_pairs={{0,4},{2,6},{4,0},{6,2},{8,12},{10,14},{12,8},{14,10},{16,20},{18,... | collective-permute-start | bytes 884744 | tf_op jit(solution)/shard_map/ppermute | solution.py:18
  90.6 22.2 %collective-permute-start.22 = (bf16[192,768]{1,0:T(8,128)(2,1)S(1)}, bf16[192,768]{1,0:T(8,128)(2,1)S(1)}, u32[]{:S(2)}, u32[]{:S(2)}) collective-permute-start(bf16[192,768]{1,0:T(8,128)(2,1)S(1)} %collective-permute-done.15.refs_13_), channel_id=1, source_target_pairs={{0,4},{2,6},{4,0},{6,2},{8,12},{10,14},{12,8},{14,10},{16,20},{18,... | collective-permute-start | bytes 884744 | tf_op jit(solution)/shard_map/ppermute | solution.py:18
  92.1 20.7 %collective-permute-start.23 = (bf16[192,768]{1,0:T(8,128)(2,1)S(1)}, bf16[192,768]{1,0:T(8,128)(2,1)S(1)}, u32[]{:S(2)}, u32[]{:S(2)}) collective-permute-start(bf16[192,768]{1,0:T(8,128)(2,1)S(1)} %collective-permute-done.18.refs_17_), channel_id=1, source_target_pairs={{0,4},{2,6},{4,0},{6,2},{8,12},{10,14},{12,8},{14,10},{16,20},{18,... | collective-permute-start | bytes 884744 | tf_op jit(solution)/shard_map/ppermute | solution.py:18
  92.6 14.4 %collective-permute-start.16 = (bf16[192,384]{1,0:T(8,128)(2,1)S(1)}, bf16[192,384]{1,0:T(8,128)(2,1)S(1)}, u32[]{:S(2)}, u32[]{:S(2)}) collective-permute-start(bf16[192,384]{1,0:T(8,128)(2,1)S(1)} %get-tuple-element.95), channel_id=1, source_target_pairs={{0,16},{2,18},{4,20},{6,22},{8,24},{10,26},{12,28},{14,30},{16,0},... | collective-permute-start | bytes 442376 | tf_op jit(solution)/shard_map/ppermute | solution.py:18
  98.1 9.7 %collective-permute-start.19 = (bf16[192,384]{1,0:T(8,128)(2,1)S(1)}, bf16[192,384]{1,0:T(8,128)(2,1)S(1)}, u32[]{:S(2)}, u32[]{:S(2)}) collective-permute-start(bf16[192,384]{1,0:T(8,128)(2,1)S(1)} %get-tuple-element.101), channel_id=1, source_target_pairs={{0,24},{2,26},{4,28},{6,30},{8,16},{10,18},{12,20},{14,22},{16,8},... | collective-permute-start | bytes 442376 | tf_op jit(solution)/shard_map/ppermute | solution.py:18
  107.0 15.3 %collective-permute-start.14 = (bf16[192,384]{1,0:T(8,128)(2,1)S(1)}, bf16[192,384]{1,0:T(8,128)(2,1)S(1)}, u32[]{:S(2)}, u32[]{:S(2)}) collective-permute-start(bf16[192,384]{1,0:T(8,128)(2,1)S(1)} %get-tuple-element.90), channel_id=1, source_target_pairs={{0,8},{2,10},{4,12},{6,14},{8,0},{10,2},{12,4},{14,6},{16,24},{18,... | collective-permute-start | bytes 442376 | tf_op jit(solution)/shard_map/ppermute | solution.py:18
  107.8 18.2 %collective-permute-start.17 = (bf16[192,384]{1,0:T(8,128)(2,1)S(1)}, bf16[192,384]{1,0:T(8,128)(2,1)S(1)}, u32[]{:S(2)}, u32[]{:S(2)}) collective-permute-start(bf16[192,384]{1,0:T(8,128)(2,1)S(1)} %get-tuple-element.96), channel_id=1, source_target_pairs={{0,16},{2,18},{4,20},{6,22},{8,24},{10,26},{12,28},{14,30},{16,0},... | collective-permute-start | bytes 442376 | tf_op jit(solution)/shard_map/ppermute | solution.py:18
  109.6 16.4 %collective-permute-start.20 = (bf16[192,384]{1,0:T(8,128)(2,1)S(1)}, bf16[192,384]{1,0:T(8,128)(2,1)S(1)}, u32[]{:S(2)}, u32[]{:S(2)}) collective-permute-start(bf16[192,384]{1,0:T(8,128)(2,1)S(1)} %get-tuple-element.102), channel_id=1, source_target_pairs={{0,24},{2,26},{4,28},{6,30},{8,16},{10,18},{12,20},{14,22},{16,8},... | collective-permute-start | bytes 442376 | tf_op jit(solution)/shard_map/ppermute | solution.py:18
  121.5 17.3 %collective-permute-start.28 = (bf16[192,384]{1,0:T(8,128)(2,1)S(1)}, bf16[192,384]{1,0:T(8,128)(2,1)S(1)}, u32[]{:S(2)}, u32[]{:S(2)}) collective-permute-start(bf16[192,384]{1,0:T(8,128)(2,1)S(1)} %get-tuple-element.109), channel_id=1, source_target_pairs={{0,24},{2,26},{4,28},{6,30},{8,16},{10,18},{12,20},{14,22},{16,8},... | collective-permute-start | bytes 442376 | tf_op jit(solution)/shard_map/ppermute | solution.py:18
  122.3 17.7 %collective-permute-start.29 = (bf16[192,384]{1,0:T(8,128)(2,1)S(1)}, bf16[192,384]{1,0:T(8,128)(2,1)S(1)}, u32[]{:S(2)}, u32[]{:S(2)}) collective-permute-start(bf16[192,384]{1,0:T(8,128)(2,1)S(1)} %get-tuple-element.110), channel_id=1, source_target_pairs={{0,16},{2,18},{4,20},{6,22},{8,24},{10,26},{12,28},{14,30},{16,0},... | collective-permute-start | bytes 442376 | tf_op jit(solution)/shard_map/ppermute | solution.py:18
  122.3 17.7 %collective-permute-start.30 = (bf16[192,384]{1,0:T(8,128)(2,1)S(1)}, bf16[192,384]{1,0:T(8,128)(2,1)S(1)}, u32[]{:S(2)}, u32[]{:S(2)}) collective-permute-start(bf16[192,384]{1,0:T(8,128)(2,1)S(1)} %get-tuple-element.111), channel_id=1, source_target_pairs={{0,8},{2,10},{4,12},{6,14},{8,0},{10,2},{12,4},{14,6},{16,24},{18,... | collective-permute-start | bytes 442376 | tf_op jit(solution)/shard_map/ppermute | solution.py:18
  135.0 7.0 %collective-permute-start.24 = (bf16[192,384]{1,0:T(8,128)(2,1)S(1)}, bf16[192,384]{1,0:T(8,128)(2,1)S(1)}, u32[]{:S(2)}, u32[]{:S(2)}) collective-permute-start(bf16[192,384]{1,0:T(8,128)(2,1)S(1)} %get-tuple-element.105), channel_id=1, source_target_pairs={{0,26},{2,24},{4,30},{6,28},{8,18},{10,16},{12,22},{14,20},{16,10}... | collective-permute-start | bytes 442376 | tf_op jit(solution)/shard_map/ppermute | solution.py:18
  135.1 15.7 %collective-permute-start.25 = (bf16[192,384]{1,0:T(8,128)(2,1)S(1)}, bf16[192,384]{1,0:T(8,128)(2,1)S(1)}, u32[]{:S(2)}, u32[]{:S(2)}) collective-permute-start(bf16[192,384]{1,0:T(8,128)(2,1)S(1)} %get-tuple-element.106), channel_id=1, source_target_pairs={{0,18},{2,16},{4,22},{6,20},{8,26},{10,24},{12,30},{14,28},{16,2},... | collective-permute-start | bytes 442376 | tf_op jit(solution)/shard_map/ppermute | solution.py:18
  138.8 12.0 %collective-permute-start.26 = (bf16[192,384]{1,0:T(8,128)(2,1)S(1)}, bf16[192,384]{1,0:T(8,128)(2,1)S(1)}, u32[]{:S(2)}, u32[]{:S(2)}) collective-permute-start(bf16[192,384]{1,0:T(8,128)(2,1)S(1)} %get-tuple-element.107), channel_id=1, source_target_pairs={{0,10},{2,8},{4,14},{6,12},{8,2},{10,0},{12,6},{14,4},{16,26},{18,... | collective-permute-start | bytes 442376 | tf_op jit(solution)/shard_map/ppermute | solution.py:18
  140.0 10.8 %collective-permute-start.27 = (bf16[192,384]{1,0:T(8,128)(2,1)S(1)}, bf16[192,384]{1,0:T(8,128)(2,1)S(1)}, u32[]{:S(2)}, u32[]{:S(2)}) collective-permute-start(bf16[192,384]{1,0:T(8,128)(2,1)S(1)} %get-tuple-element.108), channel_id=1, source_target_pairs={{0,2},{2,0},{4,6},{6,4},{8,10},{10,8},{12,14},{14,12},{16,18},{18,... | collective-permute-start | bytes 442376 | tf_op jit(solution)/shard_map/ppermute | solution.py:18
